TPU v7x, 256 devices: a whole 4x4x8 slice. The times are simulated.
256 devices in a mesh: row: 32 (over z, x_hi, core), col: 8 (over x_lo, y).
Axes of the slice: x: 4 (x_hi: 2, x_lo: 2; x = x_hi * 2 + x_lo), y: 4, z: 8, core: 2. Of those that a mesh axis runs over, the one named last changes fastest.
Arguments:
- features: bfloat16 [8, 8192, 256], P('col', 'row'), may hold values from -6 to 6
- adj_tiles: bfloat16 [32, 8, 12, 256, 256], P('row', 'col')
- tile_row: int32 [32, 8, 12], P('row', 'col'), may hold values from 0 to 7, as said below
- tile_col: int32 [32, 8, 12], P('row', 'col'), may hold values from 0 to 31
- tile_count: int32 [32, 8], P('row', 'col'), may hold values from 1 to 12, as said below
- weight: bfloat16 [256, 256], replicated, may hold values from -0.375 to 0.375
- cotangent: bfloat16 [65536, 256], P(('row', 'col')), may hold values from -6 to 6
Outputs:
- activated: bfloat16 [65536, 256], P(('row', 'col'))
- weight_grad: float32 [256, 256], replicated
- feature_grad: bfloat16 [8, 8192, 256], P('col', 'row')
Inputs may be any that keep to these rules, and one draw needn't show every extreme that they name: The pairs (tile_row, tile_col) of the 12 slots of one block pair are distinct. `tile_count`: some block pair uses all 12 slots in every draw.
All inputs are finite; a program needn't handle non-finite values.
Results may differ from a plain program's by a relative error of at most 0.015.
Values may be sent and summed in bfloat16 or wider, within the bound.
No kernel may reach another device: no remote copies, remote signals or barrier semaphores. Data moves between devices by JAX's collectives and lax.ppermute only.
A program may use at most 64 MiB of HBM per device.

v0:
```python
import math

import jax
import jax.numpy as jnp
from jax import lax
from jax.sharding import PartitionSpec as P


def per_device(features, adj_tiles, tile_row, tile_col, tile_count, weight, cotangent):
    tiles = adj_tiles[0, 0]
    row_ids = tile_row[0, 0]
    col_ids = tile_col[0, 0]
    used_slots = tile_count[0, 0]
    slot_total = tiles.shape[0]
    tile_size = tiles.shape[1]
    feat_width = features.shape[2]
    own_rows = features.shape[1]
    row_nodes = own_rows * lax.axis_size("col")
    tile_rows = row_nodes // tile_size
    node_total = row_nodes * lax.axis_size("row")
    panel = lax.all_gather(features[0], "row", axis=0, tiled=True)
    col_nodes = panel.shape[0]
    col_tiles = col_nodes // tile_size
    live_mask = (jnp.arange(slot_total) < used_slots).astype(jnp.float32)
    panel_blocks = panel.reshape(col_tiles, tile_size, feat_width)[col_ids]
    products = jnp.einsum("sab,sbf->saf", tiles, panel_blocks, preferred_element_type=jnp.float32)
    placing = (row_ids[None, :] == jnp.arange(tile_rows)[:, None]).astype(jnp.float32) * live_mask[
        None, :
    ]
    partial_value = jnp.einsum(
        "ts,saf->taf", placing, products, precision=lax.Precision.HIGHEST
    ).reshape(row_nodes, feat_width)
    weight_full = weight.astype(jnp.float32)
    summed = lax.psum_scatter(partial_value, "col", scatter_dimension=0, tiled=True)
    pre_act = jnp.dot(summed, weight_full, precision=lax.Precision.HIGHEST)
    activated, backward = jax.vjp(jax.nn.gelu, pre_act)
    grad_pre = backward(cotangent.astype(jnp.float32))[0]
    weight_part = jnp.dot(summed.T, grad_pre, precision=lax.Precision.HIGHEST)
    back_rows = jnp.dot(grad_pre, weight_full.T, precision=lax.Precision.HIGHEST).astype(
        jnp.bfloat16
    )
    back_block = lax.all_gather(back_rows, "col", axis=0, tiled=True)
    weight_grad = lax.psum(weight_part, ("row", "col")) * (1.0 / math.sqrt(node_total))
    back_blocks = back_block.reshape(tile_rows, tile_size, feat_width)[row_ids]
    back_products = jnp.einsum(
        "sab,saf->sbf", tiles, back_blocks, preferred_element_type=jnp.float32
    )
    col_placing = (col_ids[None, :] == jnp.arange(col_tiles)[:, None]).astype(
        jnp.float32
    ) * live_mask[None, :]
    back_partial = jnp.einsum(
        "ts,sbf->tbf", col_placing, back_products, precision=lax.Precision.HIGHEST
    ).reshape(col_nodes, feat_width)
    grad_rows = lax.psum_scatter(
        back_partial.astype(jnp.bfloat16), "row", scatter_dimension=0, tiled=True
    )
    feature_grad = grad_rows.reshape(1, own_rows, feat_width)
    return (activated.astype(jnp.bfloat16), weight_grad, feature_grad)


def solution(mesh):
    return jax.shard_map(
        per_device,
        mesh=mesh,
        in_specs=(
            P("col", "row", None),
            P("row", "col", None, None, None),
            P("row", "col", None),
            P("row", "col", None),
            P("row", "col"),
            P(),
            P(("row", "col"), None),
        ),
        out_specs=(P(("row", "col"), None), P(), P("col", "row", None)),
        check_vma=False,
    )
```

profile of v0, /device:TPU:1, one launch (start us, length us, event | category | flops | bytes accessed | tf_op | source)
XLA Modules:
  0.0 591.0 jit_solution(8460658954462372399)
XLA Ops:
  7.2 0.0 copy-start
  7.2 0.0 all-gather.6.cloned.1.call-start
  7.2 0.7 all-gather.6.cloned.1.call-update
  7.9 0.0 reduce-scatter.3.cloned.1.call-start
  8.6 0.7 fusion.30
  9.3 92.6 %all-gather.6.cloned.1.call-done = bf16[1,8192,256]{2,1,0:T(8,128)(2,1)} async-done(((bf16[1,256,256]{2,1,0:T(8,128)(2,1)}), bf16[1,8192,256]{2,1,0:T(8,128)(2,1)}) %all-gather.6.cloned.1.call-update) | async-done | bytes 4194320 | tf_op jit(solution)/shard_map/all_gather | solution.py:21
  101.9 2.8 gather_fusion
  104.7 2.3 fusion.9
  107.0 5.2 copy.12
  112.2 3.9 fusion.2
  116.1 2.0 copy.10
  118.1 0.0 reduce-scatter.3.cloned.1.call-update
  118.1 0.0 all-gather.4.cloned.1.call-start
  118.1 36.3 %reduce-scatter.3.cloned.1.call-done = f32[256,256]{1,0:T(8,128)} async-done(((f32[2048,256]{1,0:T(8,128)}), f32[256,256]{1,0:T(8,128)}) %reduce-scatter.3.cloned.1.call-update) | async-done | bytes 262160 | tf_op jit(solution)/shard_map/reduce_scatter | solution.py:34
  154.5 0.0 copy-done.2
  154.5 2.0 multiply_convert_fusion
  156.5 1.1 convolution_convert_fusion
  157.6 0.0 all-gather.4.cloned.1.call-update
  157.6 0.0 all-reduce.2.cloned.1.call-start
  157.7 1.4 fusion.35
  159.1 0.0 all-reduce.2.cloned.1.call-update
  159.1 0.2 reduce-scatter.5.cloned.1.call-start
  159.3 39.0 %all-gather.4.cloned.1.call-done = bf16[2048,256]{1,0:T(8,128)(2,1)} async-done(((bf16[256,256]{1,0:T(8,128)(2,1)}), bf16[2048,256]{1,0:T(8,128)(2,1)}) %all-gather.4.cloned.1.call-update) | async-done | bytes 1048592 | tf_op jit(solution)/shard_map/all_gather | solution.py:42
  198.3 1.9 gather_fusion.1
  200.2 2.3 fusion.7
  202.5 5.2 copy.13
  207.7 8.7 %fusion.4 = bf16[32,256,256]{2,0,1:T(8,128)(2,1)S(1)} fusion(f32[12,256,256]{1,0,2:T(8,128)} %copy.13, f32[12]{0:T(128)S(1)} %compare_convert_fusion, s32[12]{0:T(128)S(1)} %bitcast.46), kind=kOutput, calls=%fused_computation.6 | convolution fusion | flops 304087808 | bytes 7340128 | tf_op jit(solution)/shard_map/ts,sbf->tbf/dot_general | solution.py:51
  216.4 4.4 copy.11
  220.8 0.0 reduce-scatter.5.cloned.1.call-update
  220.8 236.3 %all-reduce.2.cloned.1.call-done = f32[256,256]{1,0:T(8,128)} async-done(((f32[256,256]{1,0:T(8,128)}), f32[256,256]{1,0:T(8,128)}) %all-reduce.2.cloned.1.call-update) | async-done | bytes 262160 | tf_op jit(solution)/shard_map/psum | solution.py:43
  457.1 1.7 broadcast_multiply_fusion
  458.7 125.7 %reduce-scatter.5.cloned.1.call-done = bf16[256,256]{1,0:T(8,128)(2,1)} async-done(((bf16[8192,256]{1,0:T(8,128)(2,1)}), bf16[256,256]{1,0:T(8,128)(2,1)}) %reduce-scatter.5.cloned.1.call-update) | async-done | bytes 131088 | tf_op jit(solution)/shard_map/reduce_scatter | solution.py:54
  (14 shorter events, 0.0 us)
Async XLA Ops:
  7.2 97.5 %copy-start = (bf16[1,1,12,256,256]{4,3,2,1,0:T(8,128)(2,1)S(1)}, bf16[1,1,12,256,256]{4,3,2,1,0:T(8,128)(2,1)}, u32[]{:S(2)}) copy-start(bf16[1,1,12,256,256]{4,3,2,1,0:T(8,128)(2,1)} %param.8) | copy-start | bytes 4718596
  7.2 94.7 %all-gather.6.cloned.1.call-start = ((), (), s32[]{:S(2)}) async-start(), calls=%async_computation.6 | async-start | bytes 4325376 | tf_op jit(solution)/shard_map/all_gather | solution.py:21
  7.9 146.5 %reduce-scatter.3.cloned.1.call-start = ((), (), s32[]{:S(2)}) async-start(), calls=%async_computation.2 | async-start | bytes 2359296 | tf_op jit(solution)/shard_map/reduce_scatter | solution.py:34
  107.0 5.2 copy-start.4
  118.0 36.4 %copy-start.2 = (bf16[256,256]{1,0:T(8,128)(2,1)S(1)}, bf16[256,256]{1,0:T(8,128)(2,1)}, u32[]{:S(2)}) copy-start(bf16[256,256]{1,0:T(8,128)(2,1)} %param.12) | copy-start | bytes 393220
  118.1 38.4 %copy-start.5 = (bf16[256,256]{1,0:T(8,128)(2,1)S(1)}, bf16[256,256]{1,0:T(8,128)(2,1)}, u32[]{:S(2)}) copy-start(bf16[256,256]{1,0:T(8,128)(2,1)} %param.13) | copy-start | bytes 393220
  118.1 80.2 %all-gather.4.cloned.1.call-start = ((), (), s32[]{:S(2)}) async-start(), calls=%async_computation.4 | async-start | bytes 1179648 | tf_op jit(solution)/shard_map/all_gather | solution.py:42
  154.5 3.2 copy-start.1
  157.6 299.5 %all-reduce.2.cloned.1.call-start = ((), (), s32[]{:S(2)}) async-start(), calls=%async_computation.3 | async-start | bytes 524288 | tf_op jit(solution)/shard_map/psum | solution.py:43
  159.1 425.4 %reduce-scatter.5.cloned.1.call-start = ((), (), s32[]{:S(2)}) async-start(), calls=%async_computation.5 | async-start | bytes 4325376 | tf_op jit(solution)/shard_map/reduce_scatter | solution.py:54
  202.5 5.2 copy-start.3
Sparse Core Ops, SparseCore 0:
  10.8 91.0 all-gather.5
  118.2 36.2 reduce-scatter.2
  157.7 40.5 all-gather.3
  204.2 252.8 all-reduce.1
  461.7 122.7 reduce-scatter.4
where the time goes:
time: 596 us; the launch traced here: 591 us
  waiting for transfers between devices  531 us (89%)
  matrix products  21.7 us (4%)
  local copies, waits for them, and re-layouts  21.4 us (4%)
  between operations  14.5 us (2%)
    psum x1, waiting for transfers between devices, per_device(): lax.psum(weight_part, ('row', 'col')) * (1.0 / math.sqrt(node_total))  236 us
    reduce_scatter x1, waiting for transfers between devices, per_device(): lax.psum_scatter(back_partial.astype(jnp.bfloat16), 'row', scatter_dimens...  126 us
    all_gather x1, waiting for transfers between devices, per_device(): panel = lax.all_gather(features[0], 'row', axis=0, tiled=True)  92.6 us
    all_gather x1, waiting for transfers between devices, per_device(): back_block = lax.all_gather(back_rows, 'col', axis=0, tiled=True)  39 us
    reduce_scatter x1, waiting for transfers between devices, per_device(): lax.psum_scatter(partial_value, 'col', scatter_dimension=0, tiled=True)  36.3 us
  transfers between devices with their start and end apart: 5, of which 5 were waited for; matrix products, arithmetic and copies ran while one was open for 4% of the time, Pallas kernels for 0%

commit v1 on v0

v1 whole, which is shorter than its diff:
```python
import functools
import math

import jax
import jax.numpy as jnp
from jax import lax
from jax.experimental import pallas as pl
from jax.experimental.pallas import tpu as pltpu
from jax.sharding import PartitionSpec as P

NZ = 8
QUAD = 4
NCOL = 8
TILE = 256
HALF = 128
SLOTS = 12
W_ROWS = 32


def row_pairs(move):
    pairs = []
    for r in range(NZ * QUAD):
        z, q = move(r // QUAD, r % QUAD)
        pairs.append((r, (z % NZ) * QUAD + q))
    return pairs


def quad_permute(x, flip):
    return lax.ppermute(x, "row", row_pairs(lambda z, q: (z, q ^ flip)))


def z_shift(x, step):
    return lax.ppermute(x, "row", row_pairs(lambda z, q: (z + step, q)))


def z_flip(x, flip):
    return lax.ppermute(x, "row", row_pairs(lambda z, q: (z ^ flip, q)))


def col_flip(x, flip):
    return lax.ppermute(x, "col", [(c, c ^ flip) for c in range(NCOL)])


def load_live_tiles(meta, adj_refs, adj_vmem, adj_sem):
    for i in range(2):

        @pl.loop(0, meta[25 * i + 24])
        def _(s, i=i):
            pltpu.make_async_copy(
                adj_refs[i].at[s], adj_vmem.at[i, s], adj_sem.at[i, s]
            ).start()


def wait_tile(adj_refs, adj_vmem, adj_sem, i, s):
    pltpu.make_async_copy(adj_refs[i].at[s], adj_vmem.at[i, s], adj_sem.at[i, s]).wait()


def panel_place(meta, tile):
    z, q = meta[50], meta[51]
    return (((tile >> 2) - z) & 7) * QUAD + ((tile & 3) ^ q)


def forward_kernel(meta, adj0, adj1, *refs):
    pieces, (out, panel, adj_vmem, acc, panel_sem, adj_sem) = refs[:9], refs[9:]
    adj_refs = (adj0, adj1)
    starts = (0, 1, 2, 3, 4, 4.5, 5, 6, 7)
    copies = [
        pltpu.make_async_copy(
            piece,
            panel.at[pl.ds(int(start * QUAD), piece.shape[0])],
            panel_sem.at[n],
        )
        for n, (start, piece) in enumerate(zip(starts, pieces))
    ]
    for copy in copies:
        copy.start()
    load_live_tiles(meta, adj_refs, adj_vmem, adj_sem)
    acc[...] = jnp.zeros_like(acc)
    for copy in copies:
        copy.wait()
    for i in range(2):

        @pl.loop(0, meta[25 * i + 24])
        def _(s, i=i):
            wait_tile(adj_refs, adj_vmem, adj_sem, i, s)
            row = meta[25 * i + s]
            place = panel_place(meta, meta[25 * i + 12 + s])
            acc[row, i] += jnp.dot(
                adj_vmem[i, s], panel[place], preferred_element_type=jnp.float32
            )

    out[...] = acc[...].astype(jnp.bfloat16)


def backward_kernel(meta, adj0, adj1, back, out, adj_vmem, acc, adj_sem):
    adj_refs = (adj0, adj1)
    load_live_tiles(meta, adj_refs, adj_vmem, adj_sem)
    acc[...] = jnp.zeros_like(acc)
    for i in range(2):

        @pl.loop(0, meta[25 * i + 24])
        def _(s, i=i):
            wait_tile(adj_refs, adj_vmem, adj_sem, i, s)
            row = meta[25 * i + s]
            place = panel_place(meta, meta[25 * i + 12 + s])
            acc[place] += lax.dot_general(
                adj_vmem[i, s],
                back[row, pl.ds(i * TILE, TILE), :],
                (((0,), (0,)), ((), ())),
                preferred_element_type=jnp.float32,
            )

    out[...] = acc[...].astype(jnp.bfloat16)


def dense_kernel(meta, agg_own, agg_other, weight, cot_own, cot_other, act_out, send_out):
    core = meta[51] & 1
    first = core == 0
    own = agg_own[...]
    other = jnp.concatenate([agg_other[TILE:, :], agg_other[:TILE, :]], axis=0)
    low = jnp.where(first, own, other)
    high = jnp.where(first, other, own)
    w = weight[...].astype(jnp.float32)
    dot = functools.partial(
        lax.dot_general,
        precision=lax.Precision.HIGHEST,
        preferred_element_type=jnp.float32,
    )
    plain = (((1,), (0,)), ((), ()))
    v = dot(low, w[:HALF], plain) + dot(high, w[HALF:], plain)
    scale = math.sqrt(2.0 / math.pi)
    square = v * v
    t = jnp.tanh(scale * (v + 0.044715 * (square * v)))
    cdf = 0.5 * (1.0 + t)
    act_out[...] = (v[:TILE] * cdf[:TILE]).astype(jnp.bfloat16)
    slope = cdf + 0.5 * v * ((1.0 - t) * (1.0 + t)) * (scale * (1.0 + 3.0 * 0.044715 * square))
    cot = jnp.concatenate([cot_own[...], cot_other[...]], axis=0).astype(jnp.float32)
    grad = cot * slope
    w_half = jnp.where(first, w[:HALF], w[HALF:])
    back = dot(grad, w_half, (((1,), (1,)), ((), ()))).astype(jnp.bfloat16)
    w_part = dot(own, grad, (((0,), (0,)), ((), ()))).astype(jnp.bfloat16)
    for c in range(NCOL):
        send_out[c, : 2 * TILE, :] = back
        piece = w_part[16 * c : 16 * c + 16]
        send_out[c, 2 * TILE : 2 * TILE + 16, :] = piece[:, :HALF]
        send_out[c, 2 * TILE + 16 :, :] = piece[:, HALF:]


SMEM = pl.BlockSpec(memory_space=pltpu.SMEM)
VMEM = pl.BlockSpec(memory_space=pltpu.VMEM)
ANY = pl.BlockSpec(memory_space=pl.ANY)


def params(mib):
    return pltpu.CompilerParams(vmem_limit_bytes=mib << 20)


def forward_tiles(meta, adj0, adj1, pieces):
    return pl.pallas_call(
        forward_kernel,
        out_shape=jax.ShapeDtypeStruct((8, 2, TILE, HALF), jnp.bfloat16),
        in_specs=[SMEM] + [ANY] * 11,
        out_specs=VMEM,
        scratch_shapes=[
            pltpu.VMEM((NZ * QUAD, TILE, HALF), jnp.bfloat16),
            pltpu.VMEM((2, SLOTS, TILE, TILE), jnp.bfloat16),
            pltpu.VMEM((8, 2, TILE, HALF), jnp.float32),
            pltpu.SemaphoreType.DMA((9,)),
            pltpu.SemaphoreType.DMA((2, SLOTS)),
        ],
        compiler_params=params(20),
        name="forward_tiles",
    )(meta, adj0, adj1, *pieces)


def backward_tiles(meta, adj0, adj1, back):
    return pl.pallas_call(
        backward_kernel,
        out_shape=jax.ShapeDtypeStruct((NZ * QUAD, TILE, HALF), jnp.bfloat16),
        in_specs=[SMEM, ANY, ANY, VMEM],
        out_specs=VMEM,
        scratch_shapes=[
            pltpu.VMEM((2, SLOTS, TILE, TILE), jnp.bfloat16),
            pltpu.VMEM((NZ * QUAD, TILE, HALF), jnp.float32),
            pltpu.SemaphoreType.DMA((2, SLOTS)),
        ],
        compiler_params=params(20),
        name="backward_tiles",
    )(meta, adj0, adj1, back)


def dense(meta, agg_own, agg_other, weight, cot_own, cot_other):
    return pl.pallas_call(
        dense_kernel,
        out_shape=(
            jax.ShapeDtypeStruct((TILE, 2 * HALF), jnp.bfloat16),
            jax.ShapeDtypeStruct((NCOL, 2 * TILE + W_ROWS, HALF), jnp.bfloat16),
        ),
        in_specs=[SMEM] + [VMEM] * 5,
        out_specs=(VMEM, VMEM),
        compiler_params=params(20),
        name="dense",
    )(meta, agg_own, agg_other, weight, cot_own, cot_other)


def weight_total(received):
    piece = received[:, 2 * TILE :, :].astype(jnp.float32).sum(axis=0)
    for flip in (1, 2, 4):
        piece = piece + z_flip(piece, flip)
    piece = piece + quad_permute(piece, 2)
    piece = jnp.concatenate([piece[:16], piece[16:]], axis=1)
    core = lax.axis_index("row") & 1
    col = lax.axis_index("col")
    whole = piece[None]
    for flip in (1, 2, 4):
        whole = jnp.concatenate([whole, col_flip(whole, flip)], axis=0)
    whole = whole[jnp.arange(NCOL) ^ col].reshape(HALF, 2 * HALF)
    partner = quad_permute(whole, 1)
    first = core == 0
    return jnp.concatenate(
        [jnp.where(first, whole, partner), jnp.where(first, partner, whole)], axis=0
    ) * (1.0 / 256.0)


def per_device(features, adj_tiles, tile_row, tile_col, tile_count, weight, cotangent):
    row = lax.axis_index("row")
    z, quad = row // QUAD, row % QUAD
    first = (quad & 1) == 0
    adj0 = adj_tiles[0, 0]
    block = features[0]

    mine = jnp.where(first, block[:, :HALF], block[:, HALF:])
    theirs = jnp.where(first, block[:, HALF:], block[:, :HALF])
    chunk = jnp.stack(
        [mine, quad_permute(theirs, 1), quad_permute(mine, 2), quad_permute(theirs, 3)]
    )

    meta0 = jnp.concatenate([tile_row[0, 0], tile_col[0, 0], tile_count[0]])
    meta1 = quad_permute(meta0, 1)
    meta = jnp.concatenate([meta0, meta1, jnp.stack([z, quad]).astype(jnp.int32)])
    adj1 = quad_permute(adj0, 1)
    cot1 = quad_permute(cotangent, 1)

    ups, downs = [chunk], [chunk]
    for _ in range(3):
        ups.append(z_shift(ups[-1], 1))
        downs.append(z_shift(downs[-1], -1))
    far_a = z_shift(ups[-1][:2], 1)
    far_b = z_shift(downs[-1][2:], -1)
    pieces = [chunk, downs[1], downs[2], downs[3], far_a, far_b, ups[3], ups[2], ups[1]]

    partial = forward_tiles(meta, adj0, adj1, pieces)
    shares = lax.all_to_all(partial, "col", 0, 0, tiled=True)
    agg = shares.reshape(NCOL, 2 * TILE, HALF).astype(jnp.float32).sum(axis=0)
    agg_other = quad_permute(agg, 1)
    activated, send = dense(meta, agg, agg_other, weight, cotangent, cot1)
    received = lax.all_to_all(send, "col", 0, 0, tiled=True)
    weight_grad = weight_total(received)
    parts = backward_tiles(meta, adj0, adj1, received).reshape(NZ, QUAD, TILE, HALF)

    def add(a, b):
        return (a.astype(jnp.float32) + b.astype(jnp.float32)).astype(jnp.bfloat16)

    up = z_shift(parts[4, :2], 1)
    down = z_shift(parts[4, 2:], -1)
    up = jnp.concatenate([add(parts[3, :2], up), parts[3, 2:]])
    down = jnp.concatenate([parts[5, :2], add(parts[5, 2:], down)])
    up, down = z_shift(up, 1), z_shift(down, -1)
    for step in (2, 1):
        up, down = add(parts[step], up), add(parts[8 - step], down)
        up, down = z_shift(up, 1), z_shift(down, -1)
    total = (
        parts[0].astype(jnp.float32) + up.astype(jnp.float32) + down.astype(jnp.float32)
    )
    to_send = total.astype(jnp.bfloat16)
    from_core = quad_permute(to_send[1], 1).astype(jnp.float32)
    from_x = quad_permute(to_send[2], 2).astype(jnp.float32)
    from_both = quad_permute(to_send[3], 3).astype(jnp.float32)
    own_half = total[0] + from_x
    other_half = from_core + from_both
    grad = jnp.concatenate(
        [jnp.where(first, own_half, other_half), jnp.where(first, other_half, own_half)],
        axis=1,
    )
    feature_grad = grad.astype(jnp.bfloat16)[None]
    return (activated, weight_grad, feature_grad)


def solution(mesh):
    return jax.shard_map(
        per_device,
        mesh=mesh,
        in_specs=(
            P("col", "row", None),
            P("row", "col", None, None, None),
            P("row", "col", None),
            P("row", "col", None),
            P("row", "col"),
            P(),
            P(("row", "col"), None),
        ),
        out_specs=(P(("row", "col"), None), P(), P("col", "row", None)),
        check_vma=False,
    )
```

time: 596 us -> 175 us (0.29)
  waiting for transfers between devices: 531 us -> 46.3 us
  starting transfers between devices: 0.38 us -> 70 us
  blocking collectives: 0 us -> 40.7 us
  matrix products: 21.7 us -> 0 us
  local copies, waits for them, and re-layouts: 21.4 us -> 4.12 us
  between operations: 14.5 us -> 1.52 us
  Pallas kernels: 0 us -> 9.31 us
    psum x1 -> x0, waiting for transfers between devices: 236 us -> none  [per_device(): lax.psum(weight_part, ('row', 'col')) * (1.0 / math.sqrt(node_total))]
    reduce_scatter x2 -> x0, waiting for transfers between devices: 162 us -> none  [the longest x1 126 us: per_device(): lax.psum_scatter(back_partial.astype(jnp.bfloat16), 'row', scatter_dimens...]
    all_gather x2 -> x0, waiting for transfers between devices: 132 us -> none  [the longest x1 92.6 us: per_device(): panel = lax.all_gather(features[0], 'row', axis=0, tiled=True)]
    ppermute x0 -> x34, starting transfers between devices: none -> 70 us  [the longest x12 29.4 us: quad_permute(): return lax.ppermute(x, 'row', row_pairs(lambda z, q: (z, q ^ flip)))]
    ppermute x0 -> x34, waiting for transfers between devices: none -> 46.3 us  [the longest x16 25.6 us: z_shift(): return lax.ppermute(x, 'row', row_pairs(lambda z, q: (z + step, q)))]
    all_to_all x0 -> x2, blocking collectives: none -> 40.7 us  [the longest x1 22.4 us: per_device(): shares = lax.all_to_all(partial, 'col', 0, 0, tiled=True)]
    dot_general x7 -> x0, matrix products: 21.7 us -> none  [the longest x1 8.74 us: per_device(): jnp.einsum('ts,sbf->tbf', col_placing, back_products, precision=lax.Preci...]
    dot_general x3 -> x0, local copies, waits for them, and re-layouts: 12.3 us -> none  [the longest x1 5.19 us: per_device(): jnp.einsum('sab,sbf->saf', tiles, panel_blocks, preferred_element_type=jn...]
  transfers between devices with their start and end apart: 5 -> 34, of which waited for: 5 -> 17; matrix products, arithmetic and copies ran while one was open for 4% -> 3% of each run, Pallas kernels for 0% -> 0%
where the time goes in v1:
time: 175 us; the launch traced here: 176 us
  starting transfers between devices  70 us (40%)
  waiting for transfers between devices  46.3 us (26%)
  blocking collectives  40.7 us (23%)
  Pallas kernels  9.31 us (5%)
  local copies, waits for them, and re-layouts  4.12 us (2%)
  other arithmetic  3.84 us (2%)
    ppermute x12, starting transfers between devices, quad_permute(): return lax.ppermute(x, 'row', row_pairs(lambda z, q: (z, q ^ flip)))  29.4 us
    ppermute x16, waiting for transfers between devices, z_shift(): return lax.ppermute(x, 'row', row_pairs(lambda z, q: (z + step, q)))  25.6 us
    ppermute x16, starting transfers between devices, z_shift(): return lax.ppermute(x, 'row', row_pairs(lambda z, q: (z + step, q)))  23.6 us
    all_to_all x1, blocking collectives, per_device(): shares = lax.all_to_all(partial, 'col', 0, 0, tiled=True)  22.4 us
    all_to_all x1, blocking collectives, per_device(): received = lax.all_to_all(send, 'col', 0, 0, tiled=True)  18.3 us
    ppermute x12, waiting for transfers between devices, quad_permute(): return lax.ppermute(x, 'row', row_pairs(lambda z, q: (z, q ^ flip)))  11.2 us
    ppermute x3, starting transfers between devices, col_flip(): return lax.ppermute(x, 'col', [(c, c ^ flip) for c in range(NCOL)])  9.67 us
    ppermute x3, starting transfers between devices, z_flip(): return lax.ppermute(x, 'row', row_pairs(lambda z, q: (z ^ flip, q)))  7.33 us
  transfers between devices with their start and end apart: 34, of which 17 were waited for; matrix products, arithmetic and copies ran while one was open for 3% of the time, Pallas kernels for 0%

profile of v1, /device:TPU:1, one launch (start us, length us, event | category | flops | bytes accessed | tf_op | source)
XLA Modules:
  0.0 175.8 jit_solution(1642203009473801440)
XLA Ops:
  0.6 3.3 %collective-permute-start.1 = (bf16[12,256,256]{2,1,0:T(8,128)(2,1)}, bf16[12,256,256]{2,1,0:T(8,128)(2,1)S(1)}, u32[]{:S(2)}, u32[]{:S(2)}) collective-permute-start(bf16[12,256,256]{2,1,0:T(8,128)(2,1)} %bitcast.64), channel_id=1, source_target_pairs={{0,8},{8,0},{16,24},{24,16},{32,40},{40,32},{48,56},{56,48},{64,72... | collective-permute-start | bytes 4718600 | tf_op jit(solution)/shard_map/ppermute | solution.py:29
  6.3 2.0 %collective-permute-start.3 = (bf16[256,128]{1,0:T(8,128)(2,1)S(1)}, bf16[256,128]{1,0:T(8,128)(2,1)S(1)}, u32[]{:S(2)}, u32[]{:S(2)}) collective-permute-start(bf16[256,128]{1,0:T(8,128)(2,1)S(1)} %get-tuple-element.24), channel_id=1, source_target_pairs={{0,16},{8,24},{16,0},{24,8},{32,48},{40,56},{48,32},{56,40},{64,80... | collective-permute-start | bytes 196616 | tf_op jit(solution)/shard_map/ppermute | solution.py:29
  8.3 1.9 %collective-permute-done.4 = bf16[256,128]{1,0:T(8,128)(2,1)S(1)} collective-permute-done((bf16[256,128]{1,0:T(8,128)(2,1)S(1)}, bf16[256,128]{1,0:T(8,128)(2,1)S(1)}, u32[]{:S(2)}, u32[]{:S(2)}) %collective-permute-start.4) | collective-permute-done | bytes 65568 | tf_op jit(solution)/shard_map/ppermute | solution.py:29
  13.3 4.0 %collective-permute-start.5 = (bf16[4,256,128]{2,1,0:T(8,128)(2,1)S(1)}, bf16[4,256,128]{2,1,0:T(8,128)(2,1)S(1)}, u32[]{:S(2)}, u32[]{:S(2)}) collective-permute-start(bf16[4,256,128]{2,1,0:T(8,128)(2,1)S(1)} %pad_maximum_fusion.refs_0_), channel_id=1, source_target_pairs={{0,224},{8,232},{16,240},{24,248},{32,0},{40,8},{48,16},{56,24},{6... | collective-permute-start | bytes 786440 | tf_op jit(solution)/shard_map/ppermute | solution.py:33
  17.3 5.8 %collective-permute-done.8.refs_8_ = bf16[4,256,128]{2,1,0:T(8,128)(2,1)S(1)} collective-permute-done((bf16[4,256,128]{2,1,0:T(8,128)(2,1)S(1)}, bf16[4,256,128]{2,1,0:T(8,128)(2,1)S(1)}, u32[]{:S(2)}, u32[]{:S(2)}) %collective-permute-start.8) | collective-permute-done | bytes 262176 | tf_op jit(solution)/shard_map/ppermute | solution.py:33
  23.1 2.7 %collective-permute-start.6 = (bf16[4,256,128]{2,1,0:T(8,128)(2,1)S(1)}, bf16[4,256,128]{2,1,0:T(8,128)(2,1)S(1)}, u32[]{:S(2)}, u32[]{:S(2)}) collective-permute-start(bf16[4,256,128]{2,1,0:T(8,128)(2,1)S(1)} %collective-permute-done.5.refs_1_), channel_id=1, source_target_pairs={{0,224},{8,232},{16,240},{24,248},{32,0},{40,8},{48,16},{56,24},{6... | collective-permute-start | bytes 786440 | tf_op jit(solution)/shard_map/ppermute | solution.py:33
  25.8 4.9 %collective-permute-done.9.refs_7_ = bf16[4,256,128]{2,1,0:T(8,128)(2,1)S(1)} collective-permute-done((bf16[4,256,128]{2,1,0:T(8,128)(2,1)S(1)}, bf16[4,256,128]{2,1,0:T(8,128)(2,1)S(1)}, u32[]{:S(2)}, u32[]{:S(2)}) %collective-permute-start.9) | collective-permute-done | bytes 262176 | tf_op jit(solution)/shard_map/ppermute | solution.py:33
  30.7 2.7 %collective-permute-start.7 = (bf16[4,256,128]{2,1,0:T(8,128)(2,1)S(1)}, bf16[4,256,128]{2,1,0:T(8,128)(2,1)S(1)}, u32[]{:S(2)}, u32[]{:S(2)}) collective-permute-start(bf16[4,256,128]{2,1,0:T(8,128)(2,1)S(1)} %collective-permute-done.6.refs_2_), channel_id=1, source_target_pairs={{0,224},{8,232},{16,240},{24,248},{32,0},{40,8},{48,16},{56,24},{6... | collective-permute-start | bytes 786440 | tf_op jit(solution)/shard_map/ppermute | solution.py:33
  33.4 3.8 %collective-permute-done.10.refs_6_ = bf16[4,256,128]{2,1,0:T(8,128)(2,1)S(1)} collective-permute-done((bf16[4,256,128]{2,1,0:T(8,128)(2,1)S(1)}, bf16[4,256,128]{2,1,0:T(8,128)(2,1)S(1)}, u32[]{:S(2)}, u32[]{:S(2)}) %collective-permute-start.10) | collective-permute-done | bytes 262176 | tf_op jit(solution)/shard_map/ppermute | solution.py:33
  38.5 2.7 %collective-permute-start.12 = (bf16[2,256,128]{2,1,0:T(8,128)(2,1)}, bf16[2,256,128]{2,1,0:T(8,128)(2,1)}, u32[]{:S(2)}, u32[]{:S(2)}) collective-permute-start(bf16[2,256,128]{2,1,0:T(8,128)(2,1)} %slice.100), channel_id=1, source_target_pairs={{0,224},{8,232},{16,240},{24,248},{32,0},{40,8},{48,16},{56,24},{6... | collective-permute-start | bytes 393224 | tf_op jit(solution)/shard_map/ppermute | solution.py:33
  42.5 4.1 %collective-permute-start = (s32[25]{0:T(128)S(1)}, s32[25]{0:T(128)S(1)}, u32[]{:S(2)}, u32[]{:S(2)}) collective-permute-start(s32[25]{0:T(128)S(1)} %pad_add_fusion), channel_id=1, source_target_pairs={{0,8},{8,0},{16,24},{24,16},{32,40},{40,32},{48,56},{56,48},{64,72... | collective-permute-start | bytes 308 | tf_op jit(solution)/shard_map/ppermute | solution.py:29
  49.6 2.8 %forward_tiles.1 = bf16[8,2,256,128]{3,2,1,0:T(8,128)(2,1)S(1)} custom-call(s32[52]{0:T(128)S(1)} %concatenate.46.meta, bf16[12,256,256]{2,1,0:T(8,128)(2,1)S(1)} %bitcast.65, bf16[12,256,256]{2,1,0:T(8,128)(2,1)S(1)} %collective-permute-done.1.adj1, bf16[4,256,128]{2,1,0:T(8,128)(2,1)S(1)} %pad_maximum_fusion.refs_0_, ...), custom_call_target="tpu_custom_call" | custom-call | tf_op jit(solution)/shard_map/forward_tiles/pallas_call | solution.py:159
  52.5 22.4 %all_to_all.10 = bf16[8,2,256,128]{3,2,1,0:T(8,128)(2,1)S(1)} all-to-all(bf16[8,2,256,128]{3,2,1,0:T(8,128)(2,1)S(1)} %forward_tiles.1), channel_id=1, replica_groups=mesh['row'=32,'col'=8] {'col'}, dimensions={0} | all-to-all | bytes 2097152 | tf_op jit(solution)/shard_map/all_to_all | solution.py:253
  75.1 2.3 %collective-permute-start.13 = (f32[512,128]{1,0:T(8,128)S(1)}, f32[512,128]{1,0:T(8,128)S(1)}, u32[]{:S(2)}, u32[]{:S(2)}) collective-permute-start(f32[512,128]{1,0:T(8,128)S(1)} %bitcast.67), channel_id=1, source_target_pairs={{0,8},{8,0},{16,24},{24,16},{32,40},{40,32},{48,56},{56,48},{64,72... | collective-permute-start | bytes 786440 | tf_op jit(solution)/shard_map/ppermute | solution.py:29
  78.7 3.6 %dense.1 = (bf16[256,256]{1,0:T(8,128)(2,1)}, bf16[8,544,128]{2,1,0:T(8,128)(2,1)S(1)}) custom-call(s32[52]{0:T(128)S(1)} %concatenate.46.meta, f32[512,128]{1,0:T(8,128)S(1)} %bitcast.68, f32[512,128]{1,0:T(8,128)S(1)} %collective-permute-done.13.agg_other, bf16[256,256]{1,0:T(8,128)(2,1)S(1)} %copy-done.4, bf16[256,256]{1,0:T(8,128)(2,1)S(1)} %copy-done.5, ...), custom_call_target="tpu_custom_call" | custom-call | tf_op jit(solution)/shard_map/dense/pallas_call | solution.py:193
  82.3 18.3 %all_to_all.11.back = bf16[8,544,128]{2,1,0:T(8,128)(2,1)S(1)} all-to-all(bf16[8,544,128]{2,1,0:T(8,128)(2,1)S(1)} %get-tuple-element.6), channel_id=1, replica_groups=mesh['row'=32,'col'=8] {'col'}, dimensions={0} | all-to-all | bytes 2228224 | tf_op jit(solution)/shard_map/all_to_all | solution.py:257
  100.6 2.9 %backward_tiles.1 = bf16[32,256,128]{2,1,0:T(8,128)(2,1)S(1)} custom-call(s32[52]{0:T(128)S(1)} %concatenate.46.meta, bf16[12,256,256]{2,1,0:T(8,128)(2,1)S(1)} %bitcast.66, bf16[12,256,256]{2,1,0:T(8,128)(2,1)S(1)} %copy-done.3, bf16[8,544,128]{2,1,0:T(8,128)(2,1)S(1)} %all_to_all.11.back), custom_call_target="tpu_custom_call" | custom-call | tf_op jit(solution)/shard_map/backward_tiles/pallas_call | solution.py:177
  103.6 2.7 %collective-permute-start.27 = (bf16[2,256,128]{2,1,0:T(8,128)(2,1)S(1)}, bf16[2,256,128]{2,1,0:T(8,128)(2,1)S(1)}, u32[]{:S(2)}, u32[]{:S(2)}) collective-permute-start(bf16[2,256,128]{2,1,0:T(8,128)(2,1)S(1)} %get-tuple-element.14), channel_id=1, source_target_pairs={{0,224},{8,232},{16,240},{24,248},{32,0},{40,8},{48,16},{56,24},{6... | collective-permute-start | bytes 393224 | tf_op jit(solution)/shard_map/ppermute | solution.py:33
  106.4 3.0 %collective-permute-done.15 = f32[32,128]{1,0:T(8,128)S(1)} collective-permute-done((f32[32,128]{1,0:T(8,128)S(1)}, f32[32,128]{1,0:T(8,128)S(1)}, u32[]{:S(2)}, u32[]{:S(2)}) %collective-permute-start.15) | collective-permute-done | bytes 16416 | tf_op jit(solution)/shard_map/ppermute | solution.py:37
  109.4 2.3 %collective-permute-start.16 = (f32[32,128]{1,0:T(8,128)S(1)}, f32[32,128]{1,0:T(8,128)S(1)}, u32[]{:S(2)}, u32[]{:S(2)}) collective-permute-start(f32[32,128]{1,0:T(8,128)S(1)} %add.58), channel_id=1, source_target_pairs={{0,64},{8,72},{16,80},{24,88},{32,96},{40,104},{48,112},{56,120},{... | collective-permute-start | bytes 49160 | tf_op jit(solution)/shard_map/ppermute | solution.py:37
  112.9 5.0 %collective-permute-start.17 = (f32[32,128]{1,0:T(8,128)S(1)}, f32[32,128]{1,0:T(8,128)S(1)}, u32[]{:S(2)}, u32[]{:S(2)}) collective-permute-start(f32[32,128]{1,0:T(8,128)S(1)} %add.59), channel_id=1, source_target_pairs={{0,128},{8,136},{16,144},{24,152},{32,160},{40,168},{48,176},{56,1... | collective-permute-start | bytes 49160 | tf_op jit(solution)/shard_map/ppermute | solution.py:37
  120.2 3.6 %collective-permute-done.18 = f32[32,128]{1,0:T(8,128)S(1)} collective-permute-done((f32[32,128]{1,0:T(8,128)S(1)}, f32[32,128]{1,0:T(8,128)S(1)}, u32[]{:S(2)}, u32[]{:S(2)}) %collective-permute-start.18) | collective-permute-done | bytes 16416 | tf_op jit(solution)/shard_map/ppermute | solution.py:29
  124.4 2.3 %collective-permute-start.28 = (bf16[4,256,128]{2,1,0:T(8,128)(2,1)S(1)}, bf16[4,256,128]{2,1,0:T(8,128)(2,1)S(1)}, u32[]{:S(2)}, u32[]{:S(2)}) collective-permute-start(bf16[4,256,128]{2,1,0:T(8,128)(2,1)S(1)} %pad_maximum_fusion.2), channel_id=1, source_target_pairs={{0,224},{8,232},{16,240},{24,248},{32,0},{40,8},{48,16},{56,24},{6... | collective-permute-start | bytes 786440 | tf_op jit(solution)/shard_map/ppermute | solution.py:33
  126.8 3.6 %collective-permute-done.24 = bf16[4,256,128]{2,1,0:T(8,128)(2,1)S(1)} collective-permute-done((bf16[4,256,128]{2,1,0:T(8,128)(2,1)S(1)}, bf16[4,256,128]{2,1,0:T(8,128)(2,1)S(1)}, u32[]{:S(2)}, u32[]{:S(2)}) %collective-permute-start.24) | collective-permute-done | bytes 262176 | tf_op jit(solution)/shard_map/ppermute | solution.py:33
  133.3 5.5 %collective-permute-start.20 = (f32[2,16,256]{2,1,0:T(8,128)S(1)}, f32[2,16,256]{2,1,0:T(8,128)S(1)}, u32[]{:S(2)}, u32[]{:S(2)}) collective-permute-start(f32[2,16,256]{2,1,0:T(8,128)S(1)} %pad_maximum_fusion.6), channel_id=1, source_target_pairs={{0,2},{1,3},{2,0},{3,1},{4,6},{5,7},{6,4},{7,5},{8,10},{9,11},{10,... | collective-permute-start | bytes 98312 | tf_op jit(solution)/shard_map/ppermute | solution.py:41
  141.5 3.4 %collective-permute-start.21 = (f32[4,16,256]{2,1,0:T(8,128)S(1)}, f32[4,16,256]{2,1,0:T(8,128)S(1)}, u32[]{:S(2)}, u32[]{:S(2)}) collective-permute-start(f32[4,16,256]{2,1,0:T(8,128)S(1)} %pad_maximum_fusion.5), channel_id=1, source_target_pairs={{0,4},{1,5},{2,6},{3,7},{4,0},{5,1},{6,2},{7,3},{8,12},{9,13},{10,... | collective-permute-start | bytes 196616 | tf_op jit(solution)/shard_map/ppermute | solution.py:41
  145.0 1.9 %collective-permute-done.21 = f32[4,16,256]{2,1,0:T(8,128)S(1)} collective-permute-done((f32[4,16,256]{2,1,0:T(8,128)S(1)}, f32[4,16,256]{2,1,0:T(8,128)S(1)}, u32[]{:S(2)}, u32[]{:S(2)}) %collective-permute-start.21) | collective-permute-done | bytes 65568 | tf_op jit(solution)/shard_map/ppermute | solution.py:41
  147.5 11.1 %collective-permute-start.22 = (f32[128,256]{1,0:T(8,128)S(1)}, f32[128,256]{1,0:T(8,128)S(1)}, u32[]{:S(2)}, u32[]{:S(2)}) collective-permute-start(f32[128,256]{1,0:T(8,128)S(1)} %bitcast.69), channel_id=1, source_target_pairs={{0,8},{8,0},{16,24},{24,16},{32,40},{40,32},{48,56},{56,48},{64,72... | collective-permute-start | bytes 393224 | tf_op jit(solution)/shard_map/ppermute | solution.py:29
  158.7 2.8 %collective-permute-start.30 = (bf16[4,256,128]{2,1,0:T(8,128)(2,1)S(1)}, bf16[4,256,128]{2,1,0:T(8,128)(2,1)S(1)}, u32[]{:S(2)}, u32[]{:S(2)}) collective-permute-start(bf16[4,256,128]{2,1,0:T(8,128)(2,1)S(1)} %add_convert_fusion), channel_id=1, source_target_pairs={{0,224},{8,232},{16,240},{24,248},{32,0},{40,8},{48,16},{56,24},{6... | collective-permute-start | bytes 786440 | tf_op jit(solution)/shard_map/ppermute | solution.py:33
  161.4 6.2 %collective-permute-done.26 = bf16[4,256,128]{2,1,0:T(8,128)(2,1)S(1)} collective-permute-done((bf16[4,256,128]{2,1,0:T(8,128)(2,1)S(1)}, bf16[4,256,128]{2,1,0:T(8,128)(2,1)S(1)}, u32[]{:S(2)}, u32[]{:S(2)}) %collective-permute-start.26) | collective-permute-done | bytes 262176 | tf_op jit(solution)/shard_map/ppermute | solution.py:33
  169.1 2.8 %collective-permute-start.33 = (bf16[256,128]{1,0:T(8,128)(2,1)S(1)}, bf16[256,128]{1,0:T(8,128)(2,1)S(1)}, u32[]{:S(2)}, u32[]{:S(2)}) collective-permute-start(bf16[256,128]{1,0:T(8,128)(2,1)S(1)} %get-tuple-element.20), channel_id=1, source_target_pairs={{0,24},{8,16},{16,8},{24,0},{32,56},{40,48},{48,40},{56,32},{64,88... | collective-permute-start | bytes 196616 | tf_op jit(solution)/shard_map/ppermute | solution.py:29
  172.6 2.4 %collective-permute-done.33 = bf16[256,128]{1,0:T(8,128)(2,1)S(1)} collective-permute-done((bf16[256,128]{1,0:T(8,128)(2,1)S(1)}, bf16[256,128]{1,0:T(8,128)(2,1)S(1)}, u32[]{:S(2)}, u32[]{:S(2)}) %collective-permute-start.33) | collective-permute-done | bytes 65568 | tf_op jit(solution)/shard_map/ppermute | solution.py:29
  (86 shorter events, 25.7 us)
Async XLA Ops:
  0.6 47.6 %collective-permute-start.1 = (bf16[12,256,256]{2,1,0:T(8,128)(2,1)}, bf16[12,256,256]{2,1,0:T(8,128)(2,1)S(1)}, u32[]{:S(2)}, u32[]{:S(2)}) collective-permute-start(bf16[12,256,256]{2,1,0:T(8,128)(2,1)} %bitcast.64), channel_id=1, source_target_pairs={{0,8},{8,0},{16,24},{24,16},{32,40},{40,32},{48,56},{56,48},{64,72... | collective-permute-start | bytes 4718600 | tf_op jit(solution)/shard_map/ppermute | solution.py:29
  4.8 5.3 %collective-permute-start.4 = (bf16[256,128]{1,0:T(8,128)(2,1)S(1)}, bf16[256,128]{1,0:T(8,128)(2,1)S(1)}, u32[]{:S(2)}, u32[]{:S(2)}) collective-permute-start(bf16[256,128]{1,0:T(8,128)(2,1)S(1)} %get-tuple-element.25), channel_id=1, source_target_pairs={{0,24},{8,16},{16,8},{24,0},{32,56},{40,48},{48,40},{56,32},{64,88... | collective-permute-start | bytes 196616 | tf_op jit(solution)/shard_map/ppermute | solution.py:29
  5.9 4.3 %collective-permute-start.2 = (bf16[256,128]{1,0:T(8,128)(2,1)S(1)}, bf16[256,128]{1,0:T(8,128)(2,1)S(1)}, u32[]{:S(2)}, u32[]{:S(2)}) collective-permute-start(bf16[256,128]{1,0:T(8,128)(2,1)S(1)} %get-tuple-element.25), channel_id=1, source_target_pairs={{0,8},{8,0},{16,24},{24,16},{32,40},{40,32},{48,56},{56,48},{64,72... | collective-permute-start | bytes 196616 | tf_op jit(solution)/shard_map/ppermute | solution.py:29
  6.3 5.2 %collective-permute-start.3 = (bf16[256,128]{1,0:T(8,128)(2,1)S(1)}, bf16[256,128]{1,0:T(8,128)(2,1)S(1)}, u32[]{:S(2)}, u32[]{:S(2)}) collective-permute-start(bf16[256,128]{1,0:T(8,128)(2,1)S(1)} %get-tuple-element.24), channel_id=1, source_target_pairs={{0,16},{8,24},{16,0},{24,8},{32,48},{40,56},{48,32},{56,40},{64,80... | collective-permute-start | bytes 196616 | tf_op jit(solution)/shard_map/ppermute | solution.py:29
  11.6 11.5 %collective-permute-start.8 = (bf16[4,256,128]{2,1,0:T(8,128)(2,1)S(1)}, bf16[4,256,128]{2,1,0:T(8,128)(2,1)S(1)}, u32[]{:S(2)}, u32[]{:S(2)}) collective-permute-start(bf16[4,256,128]{2,1,0:T(8,128)(2,1)S(1)} %pad_maximum_fusion.refs_0_), channel_id=1, source_target_pairs={{0,32},{8,40},{16,48},{24,56},{32,64},{40,72},{48,80},{56,88},{64,... | collective-permute-start | bytes 786440 | tf_op jit(solution)/shard_map/ppermute | solution.py:33
  13.3 9.8 %collective-permute-start.5 = (bf16[4,256,128]{2,1,0:T(8,128)(2,1)S(1)}, bf16[4,256,128]{2,1,0:T(8,128)(2,1)S(1)}, u32[]{:S(2)}, u32[]{:S(2)}) collective-permute-start(bf16[4,256,128]{2,1,0:T(8,128)(2,1)S(1)} %pad_maximum_fusion.refs_0_), channel_id=1, source_target_pairs={{0,224},{8,232},{16,240},{24,248},{32,0},{40,8},{48,16},{56,24},{6... | collective-permute-start | bytes 786440 | tf_op jit(solution)/shard_map/ppermute | solution.py:33
  23.1 7.6 %collective-permute-start.9 = (bf16[4,256,128]{2,1,0:T(8,128)(2,1)S(1)}, bf16[4,256,128]{2,1,0:T(8,128)(2,1)S(1)}, u32[]{:S(2)}, u32[]{:S(2)}) collective-permute-start(bf16[4,256,128]{2,1,0:T(8,128)(2,1)S(1)} %collective-permute-done.8.refs_8_), channel_id=1, source_target_pairs={{0,32},{8,40},{16,48},{24,56},{32,64},{40,72},{48,80},{56,88},{64,... | collective-permute-start | bytes 786440 | tf_op jit(solution)/shard_map/ppermute | solution.py:33
  23.1 7.6 %collective-permute-start.6 = (bf16[4,256,128]{2,1,0:T(8,128)(2,1)S(1)}, bf16[4,256,128]{2,1,0:T(8,128)(2,1)S(1)}, u32[]{:S(2)}, u32[]{:S(2)}) collective-permute-start(bf16[4,256,128]{2,1,0:T(8,128)(2,1)S(1)} %collective-permute-done.5.refs_1_), channel_id=1, source_target_pairs={{0,224},{8,232},{16,240},{24,248},{32,0},{40,8},{48,16},{56,24},{6... | collective-permute-start | bytes 786440 | tf_op jit(solution)/shard_map/ppermute | solution.py:33
  30.7 6.4 %collective-permute-start.10 = (bf16[4,256,128]{2,1,0:T(8,128)(2,1)S(1)}, bf16[4,256,128]{2,1,0:T(8,128)(2,1)S(1)}, u32[]{:S(2)}, u32[]{:S(2)}) collective-permute-start(bf16[4,256,128]{2,1,0:T(8,128)(2,1)S(1)} %collective-permute-done.9.refs_7_), channel_id=1, source_target_pairs={{0,32},{8,40},{16,48},{24,56},{32,64},{40,72},{48,80},{56,88},{64,... | collective-permute-start | bytes 786440 | tf_op jit(solution)/shard_map/ppermute | solution.py:33
  30.7 7.1 %collective-permute-start.7 = (bf16[4,256,128]{2,1,0:T(8,128)(2,1)S(1)}, bf16[4,256,128]{2,1,0:T(8,128)(2,1)S(1)}, u32[]{:S(2)}, u32[]{:S(2)}) collective-permute-start(bf16[4,256,128]{2,1,0:T(8,128)(2,1)S(1)} %collective-permute-done.6.refs_2_), channel_id=1, source_target_pairs={{0,224},{8,232},{16,240},{24,248},{32,0},{40,8},{48,16},{56,24},{6... | collective-permute-start | bytes 786440 | tf_op jit(solution)/shard_map/ppermute | solution.py:33
  37.8 10.4 %collective-permute-start.11 = (bf16[2,256,128]{2,1,0:T(8,128)(2,1)}, bf16[2,256,128]{2,1,0:T(8,128)(2,1)S(1)}, u32[]{:S(2)}, u32[]{:S(2)}) collective-permute-start(bf16[2,256,128]{2,1,0:T(8,128)(2,1)} %slice.99), channel_id=1, source_target_pairs={{0,32},{8,40},{16,48},{24,56},{32,64},{40,72},{48,80},{56,88},{64,... | collective-permute-start | bytes 393224 | tf_op jit(solution)/shard_map/ppermute | solution.py:33
  38.5 9.7 %collective-permute-start.12 = (bf16[2,256,128]{2,1,0:T(8,128)(2,1)}, bf16[2,256,128]{2,1,0:T(8,128)(2,1)}, u32[]{:S(2)}, u32[]{:S(2)}) collective-permute-start(bf16[2,256,128]{2,1,0:T(8,128)(2,1)} %slice.100), channel_id=1, source_target_pairs={{0,224},{8,232},{16,240},{24,248},{32,0},{40,8},{48,16},{56,24},{6... | collective-permute-start | bytes 393224 | tf_op jit(solution)/shard_map/ppermute | solution.py:33
  42.5 4.9 %collective-permute-start = (s32[25]{0:T(128)S(1)}, s32[25]{0:T(128)S(1)}, u32[]{:S(2)}, u32[]{:S(2)}) collective-permute-start(s32[25]{0:T(128)S(1)} %pad_add_fusion), channel_id=1, source_target_pairs={{0,8},{8,0},{16,24},{24,16},{32,40},{40,32},{48,56},{56,48},{64,72... | collective-permute-start | bytes 308 | tf_op jit(solution)/shard_map/ppermute | solution.py:29
  75.1 3.6 %collective-permute-start.13 = (f32[512,128]{1,0:T(8,128)S(1)}, f32[512,128]{1,0:T(8,128)S(1)}, u32[]{:S(2)}, u32[]{:S(2)}) collective-permute-start(f32[512,128]{1,0:T(8,128)S(1)} %bitcast.67), channel_id=1, source_target_pairs={{0,8},{8,0},{16,24},{24,16},{32,40},{40,32},{48,56},{56,48},{64,72... | collective-permute-start | bytes 786440 | tf_op jit(solution)/shard_map/ppermute | solution.py:29
  103.5 20.2 %collective-permute-start.23 = (bf16[2,256,128]{2,1,0:T(8,128)(2,1)S(1)}, bf16[2,256,128]{2,1,0:T(8,128)(2,1)S(1)}, u32[]{:S(2)}, u32[]{:S(2)}) collective-permute-start(bf16[2,256,128]{2,1,0:T(8,128)(2,1)S(1)} %get-tuple-element.13), channel_id=1, source_target_pairs={{0,32},{8,40},{16,48},{24,56},{32,64},{40,72},{48,80},{56,88},{64,... | collective-permute-start | bytes 393224 | tf_op jit(solution)/shard_map/ppermute | solution.py:33
  103.6 20.2 %collective-permute-start.27 = (bf16[2,256,128]{2,1,0:T(8,128)(2,1)S(1)}, bf16[2,256,128]{2,1,0:T(8,128)(2,1)S(1)}, u32[]{:S(2)}, u32[]{:S(2)}) collective-permute-start(bf16[2,256,128]{2,1,0:T(8,128)(2,1)S(1)} %get-tuple-element.14), channel_id=1, source_target_pairs={{0,224},{8,232},{16,240},{24,248},{32,0},{40,8},{48,16},{56,24},{6... | collective-permute-start | bytes 393224 | tf_op jit(solution)/shard_map/ppermute | solution.py:33
  106.3 3.1 %collective-permute-start.15 = (f32[32,128]{1,0:T(8,128)S(1)}, f32[32,128]{1,0:T(8,128)S(1)}, u32[]{:S(2)}, u32[]{:S(2)}) collective-permute-start(f32[32,128]{1,0:T(8,128)S(1)} %convert_reduce_fusion.1), channel_id=1, source_target_pairs={{0,32},{8,40},{16,48},{24,56},{32,0},{40,8},{48,16},{56,24},{64,96... | collective-permute-start | bytes 49160 | tf_op jit(solution)/shard_map/ppermute | solution.py:37
  109.4 3.5 %collective-permute-start.16 = (f32[32,128]{1,0:T(8,128)S(1)}, f32[32,128]{1,0:T(8,128)S(1)}, u32[]{:S(2)}, u32[]{:S(2)}) collective-permute-start(f32[32,128]{1,0:T(8,128)S(1)} %add.58), channel_id=1, source_target_pairs={{0,64},{8,72},{16,80},{24,88},{32,96},{40,104},{48,112},{56,120},{... | collective-permute-start | bytes 49160 | tf_op jit(solution)/shard_map/ppermute | solution.py:37
  112.9 6.5 %collective-permute-start.17 = (f32[32,128]{1,0:T(8,128)S(1)}, f32[32,128]{1,0:T(8,128)S(1)}, u32[]{:S(2)}, u32[]{:S(2)}) collective-permute-start(f32[32,128]{1,0:T(8,128)S(1)} %add.59), channel_id=1, source_target_pairs={{0,128},{8,136},{16,144},{24,152},{32,160},{40,168},{48,176},{56,1... | collective-permute-start | bytes 49160 | tf_op jit(solution)/shard_map/ppermute | solution.py:37
  119.4 4.4 %collective-permute-start.18 = (f32[32,128]{1,0:T(8,128)S(1)}, f32[32,128]{1,0:T(8,128)S(1)}, u32[]{:S(2)}, u32[]{:S(2)}) collective-permute-start(f32[32,128]{1,0:T(8,128)S(1)} %add.60), channel_id=1, source_target_pairs={{0,16},{8,24},{16,0},{24,8},{32,48},{40,56},{48,32},{56,40},{64,80... | collective-permute-start | bytes 49160 | tf_op jit(solution)/shard_map/ppermute | solution.py:29
  123.9 6.5 %collective-permute-start.24 = (bf16[4,256,128]{2,1,0:T(8,128)(2,1)S(1)}, bf16[4,256,128]{2,1,0:T(8,128)(2,1)S(1)}, u32[]{:S(2)}, u32[]{:S(2)}) collective-permute-start(bf16[4,256,128]{2,1,0:T(8,128)(2,1)S(1)} %pad_maximum_fusion.1), channel_id=1, source_target_pairs={{0,32},{8,40},{16,48},{24,56},{32,64},{40,72},{48,80},{56,88},{64,... | collective-permute-start | bytes 786440 | tf_op jit(solution)/shard_map/ppermute | solution.py:33
  124.4 14.3 %collective-permute-start.28 = (bf16[4,256,128]{2,1,0:T(8,128)(2,1)S(1)}, bf16[4,256,128]{2,1,0:T(8,128)(2,1)S(1)}, u32[]{:S(2)}, u32[]{:S(2)}) collective-permute-start(bf16[4,256,128]{2,1,0:T(8,128)(2,1)S(1)} %pad_maximum_fusion.2), channel_id=1, source_target_pairs={{0,224},{8,232},{16,240},{24,248},{32,0},{40,8},{48,16},{56,24},{6... | collective-permute-start | bytes 786440 | tf_op jit(solution)/shard_map/ppermute | solution.py:33
  130.5 9.5 %collective-permute-start.25 = (bf16[4,256,128]{2,1,0:T(8,128)(2,1)S(1)}, bf16[4,256,128]{2,1,0:T(8,128)(2,1)S(1)}, u32[]{:S(2)}, u32[]{:S(2)}) collective-permute-start(bf16[4,256,128]{2,1,0:T(8,128)(2,1)S(1)} %add_convert_fusion.3), channel_id=1, source_target_pairs={{0,32},{8,40},{16,48},{24,56},{32,64},{40,72},{48,80},{56,88},{64,... | collective-permute-start | bytes 786440 | tf_op jit(solution)/shard_map/ppermute | solution.py:33
  133.3 8.3 %collective-permute-start.20 = (f32[2,16,256]{2,1,0:T(8,128)S(1)}, f32[2,16,256]{2,1,0:T(8,128)S(1)}, u32[]{:S(2)}, u32[]{:S(2)}) collective-permute-start(f32[2,16,256]{2,1,0:T(8,128)S(1)} %pad_maximum_fusion.6), channel_id=1, source_target_pairs={{0,2},{1,3},{2,0},{3,1},{4,6},{5,7},{6,4},{7,5},{8,10},{9,11},{10,... | collective-permute-start | bytes 98312 | tf_op jit(solution)/shard_map/ppermute | solution.py:41
  140.1 18.4 %collective-permute-start.29 = (bf16[4,256,128]{2,1,0:T(8,128)(2,1)S(1)}, bf16[4,256,128]{2,1,0:T(8,128)(2,1)S(1)}, u32[]{:S(2)}, u32[]{:S(2)}) collective-permute-start(bf16[4,256,128]{2,1,0:T(8,128)(2,1)S(1)} %get-tuple-element.10), channel_id=1, source_target_pairs={{0,224},{8,232},{16,240},{24,248},{32,0},{40,8},{48,16},{56,24},{6... | collective-permute-start | bytes 786440 | tf_op jit(solution)/shard_map/ppermute | solution.py:33
  141.5 5.4 %collective-permute-start.21 = (f32[4,16,256]{2,1,0:T(8,128)S(1)}, f32[4,16,256]{2,1,0:T(8,128)S(1)}, u32[]{:S(2)}, u32[]{:S(2)}) collective-permute-start(f32[4,16,256]{2,1,0:T(8,128)S(1)} %pad_maximum_fusion.5), channel_id=1, source_target_pairs={{0,4},{1,5},{2,6},{3,7},{4,0},{5,1},{6,2},{7,3},{8,12},{9,13},{10,... | collective-permute-start | bytes 196616 | tf_op jit(solution)/shard_map/ppermute | solution.py:41
  147.5 13.9 %collective-permute-start.22 = (f32[128,256]{1,0:T(8,128)S(1)}, f32[128,256]{1,0:T(8,128)S(1)}, u32[]{:S(2)}, u32[]{:S(2)}) collective-permute-start(f32[128,256]{1,0:T(8,128)S(1)} %bitcast.69), channel_id=1, source_target_pairs={{0,8},{8,0},{16,24},{24,16},{32,40},{40,32},{48,56},{56,48},{64,72... | collective-permute-start | bytes 393224 | tf_op jit(solution)/shard_map/ppermute | solution.py:29
  158.6 9.1 %collective-permute-start.26 = (bf16[4,256,128]{2,1,0:T(8,128)(2,1)S(1)}, bf16[4,256,128]{2,1,0:T(8,128)(2,1)S(1)}, u32[]{:S(2)}, u32[]{:S(2)}) collective-permute-start(bf16[4,256,128]{2,1,0:T(8,128)(2,1)S(1)} %get-tuple-element.9), channel_id=1, source_target_pairs={{0,32},{8,40},{16,48},{24,56},{32,64},{40,72},{48,80},{56,88},{64,... | collective-permute-start | bytes 786440 | tf_op jit(solution)/shard_map/ppermute | solution.py:33
  158.7 9.0 %collective-permute-start.30 = (bf16[4,256,128]{2,1,0:T(8,128)(2,1)S(1)}, bf16[4,256,128]{2,1,0:T(8,128)(2,1)S(1)}, u32[]{:S(2)}, u32[]{:S(2)}) collective-permute-start(bf16[4,256,128]{2,1,0:T(8,128)(2,1)S(1)} %add_convert_fusion), channel_id=1, source_target_pairs={{0,224},{8,232},{16,240},{24,248},{32,0},{40,8},{48,16},{56,24},{6... | collective-permute-start | bytes 786440 | tf_op jit(solution)/shard_map/ppermute | solution.py:33
  167.8 4.8 %collective-permute-start.31 = (bf16[256,128]{1,0:T(8,128)(2,1)S(1)}, bf16[256,128]{1,0:T(8,128)(2,1)S(1)}, u32[]{:S(2)}, u32[]{:S(2)}) collective-permute-start(bf16[256,128]{1,0:T(8,128)(2,1)S(1)} %get-tuple-element.21), channel_id=1, source_target_pairs={{0,16},{8,24},{16,0},{24,8},{32,48},{40,56},{48,32},{56,40},{64,80... | collective-permute-start | bytes 196616 | tf_op jit(solution)/shard_map/ppermute | solution.py:29
  168.0 4.6 %collective-permute-start.32 = (bf16[256,128]{1,0:T(8,128)(2,1)S(1)}, bf16[256,128]{1,0:T(8,128)(2,1)S(1)}, u32[]{:S(2)}, u32[]{:S(2)}) collective-permute-start(bf16[256,128]{1,0:T(8,128)(2,1)S(1)} %get-tuple-element.19), channel_id=1, source_target_pairs={{0,8},{8,0},{16,24},{24,16},{32,40},{40,32},{48,56},{56,48},{64,72... | collective-permute-start | bytes 196616 | tf_op jit(solution)/shard_map/ppermute | solution.py:29
  169.1 5.9 %collective-permute-start.33 = (bf16[256,128]{1,0:T(8,128)(2,1)S(1)}, bf16[256,128]{1,0:T(8,128)(2,1)S(1)}, u32[]{:S(2)}, u32[]{:S(2)}) collective-permute-start(bf16[256,128]{1,0:T(8,128)(2,1)S(1)} %get-tuple-element.20), channel_id=1, source_target_pairs={{0,24},{8,16},{16,8},{24,0},{32,56},{40,48},{48,40},{56,32},{64,88... | collective-permute-start | bytes 196616 | tf_op jit(solution)/shard_map/ppermute | solution.py:29
  (8 other events, 110.8 us)

commit v2 on v1

--- a/solution.py
+++ b/solution.py
@@ -14,7 +14,7 @@
 TILE = 256
 HALF = 128
 SLOTS = 12
-W_ROWS = 32
+W_ROWS = 128
 
 
 def row_pairs(move):
@@ -33,14 +33,6 @@
     return lax.ppermute(x, "row", row_pairs(lambda z, q: (z + step, q)))
 
 
-def z_flip(x, flip):
-    return lax.ppermute(x, "row", row_pairs(lambda z, q: (z ^ flip, q)))
-
-
-def col_flip(x, flip):
-    return lax.ppermute(x, "col", [(c, c ^ flip) for c in range(NCOL)])
-
-
 def load_live_tiles(meta, adj_refs, adj_vmem, adj_sem):
     for i in range(2):
 
@@ -61,16 +53,15 @@
 
 
 def forward_kernel(meta, adj0, adj1, *refs):
-    pieces, (out, panel, adj_vmem, acc, panel_sem, adj_sem) = refs[:9], refs[9:]
+    pieces, (out, panel, adj_vmem, acc, panel_sem, adj_sem) = refs[:8], refs[8:]
     adj_refs = (adj0, adj1)
-    starts = (0, 1, 2, 3, 4, 4.5, 5, 6, 7)
     copies = [
         pltpu.make_async_copy(
             piece,
-            panel.at[pl.ds(int(start * QUAD), piece.shape[0])],
+            panel.at[pl.ds(n * QUAD, QUAD)],
             panel_sem.at[n],
         )
-        for n, (start, piece) in enumerate(zip(starts, pieces))
+        for n, piece in enumerate(pieces)
     ]
     for copy in copies:
         copy.start()
@@ -141,14 +132,15 @@
     w_part = dot(own, grad, (((0,), (0,)), ((), ()))).astype(jnp.bfloat16)
     for c in range(NCOL):
         send_out[c, : 2 * TILE, :] = back
-        piece = w_part[16 * c : 16 * c + 16]
-        send_out[c, 2 * TILE : 2 * TILE + 16, :] = piece[:, :HALF]
-        send_out[c, 2 * TILE + 16 :, :] = piece[:, HALF:]
+        piece = w_part[64 * (c // 4) : 64 * (c // 4) + 64]
+        send_out[c, 2 * TILE : 2 * TILE + 64, :] = piece[:, :HALF]
+        send_out[c, 2 * TILE + 64 :, :] = piece[:, HALF:]
 
 
 SMEM = pl.BlockSpec(memory_space=pltpu.SMEM)
 VMEM = pl.BlockSpec(memory_space=pltpu.VMEM)
 ANY = pl.BlockSpec(memory_space=pl.ANY)
+HBM = pl.BlockSpec(memory_space=pltpu.HBM)
 
 
 def params(mib):
@@ -159,13 +151,13 @@
     return pl.pallas_call(
         forward_kernel,
         out_shape=jax.ShapeDtypeStruct((8, 2, TILE, HALF), jnp.bfloat16),
-        in_specs=[SMEM] + [ANY] * 11,
+        in_specs=[SMEM, HBM, HBM] + [ANY] * 8,
         out_specs=VMEM,
         scratch_shapes=[
             pltpu.VMEM((NZ * QUAD, TILE, HALF), jnp.bfloat16),
             pltpu.VMEM((2, SLOTS, TILE, TILE), jnp.bfloat16),
             pltpu.VMEM((8, 2, TILE, HALF), jnp.float32),
-            pltpu.SemaphoreType.DMA((9,)),
+            pltpu.SemaphoreType.DMA((NZ,)),
             pltpu.SemaphoreType.DMA((2, SLOTS)),
         ],
         compiler_params=params(20),
@@ -177,7 +169,7 @@
     return pl.pallas_call(
         backward_kernel,
         out_shape=jax.ShapeDtypeStruct((NZ * QUAD, TILE, HALF), jnp.bfloat16),
-        in_specs=[SMEM, ANY, ANY, VMEM],
+        in_specs=[SMEM, HBM, HBM, VMEM],
         out_specs=VMEM,
         scratch_shapes=[
             pltpu.VMEM((2, SLOTS, TILE, TILE), jnp.bfloat16),
@@ -203,23 +195,14 @@
     )(meta, agg_own, agg_other, weight, cot_own, cot_other)
 
 
-def weight_total(received):
-    piece = received[:, 2 * TILE :, :].astype(jnp.float32).sum(axis=0)
-    for flip in (1, 2, 4):
-        piece = piece + z_flip(piece, flip)
-    piece = piece + quad_permute(piece, 2)
-    piece = jnp.concatenate([piece[:16], piece[16:]], axis=1)
-    core = lax.axis_index("row") & 1
-    col = lax.axis_index("col")
-    whole = piece[None]
-    for flip in (1, 2, 4):
-        whole = jnp.concatenate([whole, col_flip(whole, flip)], axis=0)
-    whole = whole[jnp.arange(NCOL) ^ col].reshape(HALF, 2 * HALF)
-    partner = quad_permute(whole, 1)
-    first = core == 0
-    return jnp.concatenate(
-        [jnp.where(first, whole, partner), jnp.where(first, partner, whole)], axis=0
-    ) * (1.0 / 256.0)
+def z_both(x):
+    return lax.ppermute(
+        x, "row", row_pairs(lambda z, q: (z + 1 - 2 * (q & 1), q))
+    )
+
+
+def add(a, b):
+    return (a.astype(jnp.float32) + b.astype(jnp.float32)).astype(jnp.bfloat16)
 
 
 def per_device(features, adj_tiles, tile_row, tile_col, tile_count, weight, cotangent):
@@ -237,17 +220,18 @@
 
     meta0 = jnp.concatenate([tile_row[0, 0], tile_col[0, 0], tile_count[0]])
     meta1 = quad_permute(meta0, 1)
-    meta = jnp.concatenate([meta0, meta1, jnp.stack([z, quad]).astype(jnp.int32)])
     adj1 = quad_permute(adj0, 1)
     cot1 = quad_permute(cotangent, 1)
 
-    ups, downs = [chunk], [chunk]
-    for _ in range(3):
-        ups.append(z_shift(ups[-1], 1))
-        downs.append(z_shift(downs[-1], -1))
-    far_a = z_shift(ups[-1][:2], 1)
-    far_b = z_shift(downs[-1][2:], -1)
-    pieces = [chunk, downs[1], downs[2], downs[3], far_a, far_b, ups[3], ups[2], ups[1]]
+    up1, down1 = z_shift(chunk, 1), z_shift(chunk, -1)
+    up1, down1, meta1 = lax.optimization_barrier((up1, down1, meta1))
+    meta = jnp.concatenate([meta0, meta1, jnp.stack([z, quad]).astype(jnp.int32)])
+    up2, down2 = z_shift(up1, 1), z_shift(down1, -1)
+    up2, down2, cot1 = lax.optimization_barrier((up2, down2, cot1))
+    up3, down3 = z_shift(up2, 1), z_shift(down2, -1)
+    up3, down3, meta, adj1 = lax.optimization_barrier((up3, down3, meta, adj1))
+    far = z_both(jnp.where(first, up3, down3))
+    pieces = [chunk, down1, down2, down3, far, up3, up2, up1]
 
     partial = forward_tiles(meta, adj0, adj1, pieces)
     shares = lax.all_to_all(partial, "col", 0, 0, tiled=True)
@@ -255,29 +239,56 @@
     agg_other = quad_permute(agg, 1)
     activated, send = dense(meta, agg, agg_other, weight, cotangent, cot1)
     received = lax.all_to_all(send, "col", 0, 0, tiled=True)
-    weight_grad = weight_total(received)
-    parts = backward_tiles(meta, adj0, adj1, received).reshape(NZ, QUAD, TILE, HALF)
-
-    def add(a, b):
-        return (a.astype(jnp.float32) + b.astype(jnp.float32)).astype(jnp.bfloat16)
-
-    up = z_shift(parts[4, :2], 1)
-    down = z_shift(parts[4, 2:], -1)
-    up = jnp.concatenate([add(parts[3, :2], up), parts[3, 2:]])
-    down = jnp.concatenate([parts[5, :2], add(parts[5, 2:], down)])
-    up, down = z_shift(up, 1), z_shift(down, -1)
+    w_piece = received[:, 2 * TILE :, :].astype(jnp.float32).sum(axis=0).astype(jnp.bfloat16)
+    parts = backward_tiles(meta, adj0, adj1, received).reshape(NZ, QUAD * TILE, HALF)
+
+    def pack(part, piece):
+        return jnp.concatenate([part, piece], axis=0)
+
+    size = QUAD * TILE
+    got1 = z_both(pack(parts[4], w_piece))
+    zero = jnp.zeros_like(got1[:size])
+    up = add(parts[3], jnp.where(first, got1[:size], zero))
+    down = add(parts[5], jnp.where(first, zero, got1[:size]))
+    up = z_shift(pack(up, jnp.where(first, got1[size:], w_piece)), 1)
+    down = z_shift(pack(down, jnp.where(first, w_piece, got1[size:])), -1)
+    ups, downs = [up[size:]], [down[size:]]
     for step in (2, 1):
-        up, down = add(parts[step], up), add(parts[8 - step], down)
-        up, down = z_shift(up, 1), z_shift(down, -1)
+        up = z_shift(pack(add(parts[step], up[:size]), up[size:]), 1)
+        down = z_shift(pack(add(parts[8 - step], down[:size]), down[size:]), -1)
+        ups.append(up[size:])
+        downs.append(down[size:])
     total = (
-        parts[0].astype(jnp.float32) + up.astype(jnp.float32) + down.astype(jnp.float32)
-    )
+        parts[0].astype(jnp.float32)
+        + up[:size].astype(jnp.float32)
+        + down[:size].astype(jnp.float32)
+    ).reshape(QUAD, TILE, HALF)
+
+    near, far_w = jnp.where(first, got1[size:], ups[0]), ups[2]
+    above = [jnp.where(first, d, e) for d, e in zip(downs, [got1[size:]] + downs[:2])]
+    below = [near, jnp.where(first, ups[0], ups[1]), jnp.where(first, ups[1], ups[2])]
+    opposite = jnp.where(first, far_w, downs[2])
+    by_step = jnp.stack([w_piece] + above + [opposite] + below[::-1])
+    w_sum = by_step[(jnp.arange(NZ) - z) & 7].astype(jnp.float32).sum(axis=0)
+
+    w_send = w_sum.astype(jnp.bfloat16)
     to_send = total.astype(jnp.bfloat16)
-    from_core = quad_permute(to_send[1], 1).astype(jnp.float32)
-    from_x = quad_permute(to_send[2], 2).astype(jnp.float32)
-    from_both = quad_permute(to_send[3], 3).astype(jnp.float32)
-    own_half = total[0] + from_x
-    other_half = from_core + from_both
+    from_core = quad_permute(pack(to_send[1], w_send), 1)
+    from_x = quad_permute(pack(to_send[2], w_send), 2)
+    from_both = quad_permute(pack(to_send[3], w_send), 3)
+    w_half = w_send.astype(jnp.float32) + from_x[TILE:].astype(jnp.float32)
+    w_other = from_core[TILE:].astype(jnp.float32) + from_both[TILE:].astype(jnp.float32)
+    w_here = jnp.stack([w_half, w_other])
+    w_there = lax.ppermute(w_here, "col", [(c, c ^ 4) for c in range(NCOL)])
+    low_x = lax.axis_index("col") < 4
+    w_all = jnp.stack([jnp.where(low_x, w_here, w_there), jnp.where(low_x, w_there, w_here)])
+    w_all = w_all.reshape(2, 2, 2, 64, HALF).transpose(1, 0, 3, 2, 4).reshape(2, HALF, 2 * HALF)
+    weight_grad = jnp.where(
+        first, w_all, w_all[::-1]
+    ).reshape(2 * HALF, 2 * HALF) * (1.0 / 256.0)
+
+    own_half = total[0] + from_x[:TILE].astype(jnp.float32)
+    other_half = from_core[:TILE].astype(jnp.float32) + from_both[:TILE].astype(jnp.float32)
     grad = jnp.concatenate(
         [jnp.where(first, own_half, other_half), jnp.where(first, other_half, own_half)],
         axis=1,

time: 175 us -> 163 us (0.931); the launches traced: 176 us -> 162 us
  starting transfers between devices: 70 us -> 59.1 us
  blocking collectives: 40.7 us -> 37.1 us
  waiting for transfers between devices: 46.3 us -> 44.3 us
    all_to_all x1, blocking collectives: 22.4 us -> 17.5 us  [per_device(): shares = lax.all_to_all(partial, 'col', 0, 0, tiled=True)]
    ppermute x6 -> x3, starting transfers between devices: 17 us -> 12.3 us  [the longest x2 9.77 us: z_both(): lax.ppermute(x, 'row', row_pairs(lambda z, q: (z + 1 - 2 * (q & 1), q)))]
    ppermute x12 -> x10, starting transfers between devices: 29.4 us -> 25.4 us  [quad_permute(): return lax.ppermute(x, 'row', row_pairs(lambda z, q: (z, q ^ flip)))]
    ppermute x16 -> x12, waiting for transfers between devices: 25.6 us -> 23.2 us  [z_shift(): return lax.ppermute(x, 'row', row_pairs(lambda z, q: (z + step, q)))]
    ppermute x16 -> x12, starting transfers between devices: 23.6 us -> 21.4 us  [z_shift(): return lax.ppermute(x, 'row', row_pairs(lambda z, q: (z + step, q)))]
    unnamed x12 -> x15, local copies, waits for them, and re-layouts: 1.43 us -> 3.32 us
    ppermute x6 -> x3, waiting for transfers between devices: 9.53 us -> 10.2 us  [the longest x2 6.97 us: z_both(): lax.ppermute(x, 'row', row_pairs(lambda z, q: (z + 1 - 2 * (q & 1), q)))]
    ppermute x12 -> x10, waiting for transfers between devices: 11.2 us -> 11 us  [quad_permute(): return lax.ppermute(x, 'row', row_pairs(lambda z, q: (z, q ^ flip)))]
  transfers between devices with their start and end apart: 34 -> 25, of which waited for: 17 -> 17; matrix products, arithmetic and copies ran while one was open for 3% -> 2% of each run, Pallas kernels for 0% -> 0%
where the time goes in v2:
time: 163 us; the launch traced here: 162 us
  starting transfers between devices  59.1 us (36%)
  waiting for transfers between devices  44.3 us (27%)
  blocking collectives  37.1 us (23%)
  Pallas kernels  8.79 us (5%)
  other arithmetic  5.51 us (3%)
  local copies, waits for them, and re-layouts  5.26 us (3%)
  between operations  1.64 us (1%)
    ppermute x10, starting transfers between devices, quad_permute(): return lax.ppermute(x, 'row', row_pairs(lambda z, q: (z, q ^ flip)))  25.4 us
    ppermute x12, waiting for transfers between devices, z_shift(): return lax.ppermute(x, 'row', row_pairs(lambda z, q: (z + step, q)))  23.2 us
    ppermute x12, starting transfers between devices, z_shift(): return lax.ppermute(x, 'row', row_pairs(lambda z, q: (z + step, q)))  21.4 us
    all_to_all x1, blocking collectives, per_device(): received = lax.all_to_all(send, 'col', 0, 0, tiled=True)  19.5 us
    all_to_all x1, blocking collectives, per_device(): shares = lax.all_to_all(partial, 'col', 0, 0, tiled=True)  17.5 us
    ppermute x10, waiting for transfers between devices, quad_permute(): return lax.ppermute(x, 'row', row_pairs(lambda z, q: (z, q ^ flip)))  11 us
    ppermute x2, starting transfers between devices, z_both(): lax.ppermute(x, 'row', row_pairs(lambda z, q: (z + 1 - 2 * (q & 1), q)))  9.77 us
    ppermute x2, waiting for transfers between devices, z_both(): lax.ppermute(x, 'row', row_pairs(lambda z, q: (z + 1 - 2 * (q & 1), q)))  6.97 us
  transfers between devices with their start and end apart: 25, of which 17 were waited for; matrix products, arithmetic and copies ran while one was open for 2% of the time, Pallas kernels for 0%

profile of v2, /device:TPU:1, one launch (start us, length us, event | category | flops | bytes accessed | tf_op | source)
XLA Modules:
  0.0 161.7 jit_solution(1633405709831429952)
XLA Ops:
  0.6 3.3 %collective-permute-start.11 = (bf16[12,256,256]{2,1,0:T(8,128)(2,1)}, bf16[12,256,256]{2,1,0:T(8,128)(2,1)S(1)}, u32[]{:S(2)}, u32[]{:S(2)}) collective-permute-start(bf16[12,256,256]{2,1,0:T(8,128)(2,1)} %bitcast.68), channel_id=1, source_target_pairs={{0,8},{8,0},{16,24},{24,16},{32,40},{40,32},{48,56},{56,48},{64,72... | collective-permute-start | bytes 4718600 | tf_op jit(solution)/shard_map/ppermute | solution.py:29
  5.9 2.3 %collective-permute-start.2 = (bf16[256,128]{1,0:T(8,128)(2,1)S(1)}, bf16[256,128]{1,0:T(8,128)(2,1)S(1)}, u32[]{:S(2)}, u32[]{:S(2)}) collective-permute-start(bf16[256,128]{1,0:T(8,128)(2,1)S(1)} %get-tuple-element.49), channel_id=1, source_target_pairs={{0,24},{8,16},{16,8},{24,0},{32,56},{40,48},{48,40},{56,32},{64,88... | collective-permute-start | bytes 196616 | tf_op jit(solution)/shard_map/ppermute | solution.py:29
  10.0 1.8 %collective-permute-done.2 = bf16[256,128]{1,0:T(8,128)(2,1)S(1)} collective-permute-done((bf16[256,128]{1,0:T(8,128)(2,1)S(1)}, bf16[256,128]{1,0:T(8,128)(2,1)S(1)}, u32[]{:S(2)}, u32[]{:S(2)}) %collective-permute-start.2) | collective-permute-done | bytes 65568 | tf_op jit(solution)/shard_map/ppermute | solution.py:29
  11.8 5.5 %collective-permute-start.4 = (bf16[4,256,128]{2,1,0:T(8,128)(2,1)S(1)}, bf16[4,256,128]{2,1,0:T(8,128)(2,1)S(1)}, u32[]{:S(2)}, u32[]{:S(2)}) collective-permute-start(bf16[4,256,128]{2,1,0:T(8,128)(2,1)S(1)} %pad_maximum_fusion.7.refs_0_), channel_id=1, source_target_pairs={{0,224},{8,232},{16,240},{24,248},{32,0},{40,8},{48,16},{56,24},{6... | collective-permute-start | bytes 786440 | tf_op jit(solution)/shard_map/ppermute | solution.py:33
  20.2 2.4 %collective-permute-done.4.refs_1_ = bf16[4,256,128]{2,1,0:T(8,128)(2,1)S(1)} collective-permute-done((bf16[4,256,128]{2,1,0:T(8,128)(2,1)S(1)}, bf16[4,256,128]{2,1,0:T(8,128)(2,1)S(1)}, u32[]{:S(2)}, u32[]{:S(2)}) %collective-permute-start.4) | collective-permute-done | bytes 262176 | tf_op jit(solution)/shard_map/ppermute | solution.py:33
  22.6 3.1 %collective-permute-done.3.refs_7_ = bf16[4,256,128]{2,1,0:T(8,128)(2,1)S(1)} collective-permute-done((bf16[4,256,128]{2,1,0:T(8,128)(2,1)S(1)}, bf16[4,256,128]{2,1,0:T(8,128)(2,1)S(1)}, u32[]{:S(2)}, u32[]{:S(2)}) %collective-permute-start.3) | collective-permute-done | bytes 262176 | tf_op jit(solution)/shard_map/ppermute | solution.py:33
  26.4 2.7 %collective-permute-start.7 = (bf16[4,256,128]{2,1,0:T(8,128)(2,1)S(1)}, bf16[4,256,128]{2,1,0:T(8,128)(2,1)}, u32[]{:S(2)}, u32[]{:S(2)}) collective-permute-start(bf16[4,256,128]{2,1,0:T(8,128)(2,1)S(1)} %collective-permute-done.4.refs_1_), channel_id=1, source_target_pairs={{0,224},{8,232},{16,240},{24,248},{32,0},{40,8},{48,16},{56,24},{6... | collective-permute-start | bytes 786440 | tf_op jit(solution)/shard_map/ppermute | solution.py:33
  29.8 2.1 %collective-permute-start.8 = (bf16[256,256]{1,0:T(8,128)(2,1)}, bf16[256,256]{1,0:T(8,128)(2,1)S(1)}, u32[]{:S(2)}, u32[]{:S(2)}) collective-permute-start(bf16[256,256]{1,0:T(8,128)(2,1)} %cot_own.1), channel_id=1, source_target_pairs={{0,8},{8,0},{16,24},{24,16},{32,40},{40,32},{48,56},{56,48},{64,72... | collective-permute-start | bytes 393224 | tf_op jit(solution)/shard_map/ppermute | solution.py:29
  33.3 3.1 %collective-permute-start.10 = (bf16[4,256,128]{2,1,0:T(8,128)(2,1)}, bf16[4,256,128]{2,1,0:T(8,128)(2,1)}, u32[]{:S(2)}, u32[]{:S(2)}) collective-permute-start(bf16[4,256,128]{2,1,0:T(8,128)(2,1)} %collective-permute-done.7.refs_2_), channel_id=1, source_target_pairs={{0,224},{8,232},{16,240},{24,248},{32,0},{40,8},{48,16},{56,24},{6... | collective-permute-start | bytes 786440 | tf_op jit(solution)/shard_map/ppermute | solution.py:33
  37.1 3.3 %collective-permute-done.9.refs_5_ = bf16[4,256,128]{2,1,0:T(8,128)(2,1)} collective-permute-done((bf16[4,256,128]{2,1,0:T(8,128)(2,1)}, bf16[4,256,128]{2,1,0:T(8,128)(2,1)}, u32[]{:S(2)}, u32[]{:S(2)}) %collective-permute-start.9) | collective-permute-done | bytes 262176 | tf_op jit(solution)/shard_map/ppermute | solution.py:33
  41.4 2.7 %collective-permute-start.12 = (bf16[4,256,128]{2,1,0:T(8,128)(2,1)S(1)}, bf16[4,256,128]{2,1,0:T(8,128)(2,1)S(1)}, u32[]{:S(2)}, u32[]{:S(2)}) collective-permute-start(bf16[4,256,128]{2,1,0:T(8,128)(2,1)S(1)} %broadcast_select_fusion), channel_id=1, source_target_pairs={{0,32},{8,232},{16,48},{24,248},{32,64},{40,8},{48,80},{56,24},{64... | collective-permute-start | bytes 786440 | tf_op jit(solution)/shard_map/ppermute | solution.py:199
  44.2 3.3 %collective-permute-done.12.refs_4_ = bf16[4,256,128]{2,1,0:T(8,128)(2,1)S(1)} collective-permute-done((bf16[4,256,128]{2,1,0:T(8,128)(2,1)S(1)}, bf16[4,256,128]{2,1,0:T(8,128)(2,1)S(1)}, u32[]{:S(2)}, u32[]{:S(2)}) %collective-permute-start.12) | collective-permute-done | bytes 262176 | tf_op jit(solution)/shard_map/ppermute | solution.py:199
  49.4 2.7 %forward_tiles.1 = bf16[8,2,256,128]{3,2,1,0:T(8,128)(2,1)S(1)} custom-call(s32[52]{0:T(128)S(1)} %concatenate.54.meta, bf16[12,256,256]{2,1,0:T(8,128)(2,1)S(1)} %bitcast.69, bf16[12,256,256]{2,1,0:T(8,128)(2,1)S(1)} %collective-permute-done.11.adj1, bf16[4,256,128]{2,1,0:T(8,128)(2,1)S(1)} %pad_maximum_fusion.7.refs_0_, ...), custom_call_target="tpu_custom_call" | custom-call | tf_op jit(solution)/shard_map/forward_tiles/pallas_call | solution.py:151
  52.1 17.5 %all_to_all.10 = bf16[8,2,256,128]{3,2,1,0:T(8,128)(2,1)S(1)} all-to-all(bf16[8,2,256,128]{3,2,1,0:T(8,128)(2,1)S(1)} %forward_tiles.1), channel_id=1, replica_groups=mesh['row'=32,'col'=8] {'col'}, dimensions={0} | all-to-all | bytes 2097152 | tf_op jit(solution)/shard_map/all_to_all | solution.py:237
  69.8 6.9 %collective-permute-start.13 = (f32[512,128]{1,0:T(8,128)S(1)}, f32[512,128]{1,0:T(8,128)S(1)}, u32[]{:S(2)}, u32[]{:S(2)}) collective-permute-start(f32[512,128]{1,0:T(8,128)S(1)} %bitcast.71), channel_id=1, source_target_pairs={{0,8},{8,0},{16,24},{24,16},{32,40},{40,32},{48,56},{56,48},{64,72... | collective-permute-start | bytes 786440 | tf_op jit(solution)/shard_map/ppermute | solution.py:29
  77.9 3.6 %dense.1 = (bf16[256,256]{1,0:T(8,128)(2,1)}, bf16[8,640,128]{2,1,0:T(8,128)(2,1)S(1)}) custom-call(s32[52]{0:T(128)S(1)} %concatenate.54.meta, f32[512,128]{1,0:T(8,128)S(1)} %bitcast.72, f32[512,128]{1,0:T(8,128)S(1)} %collective-permute-done.13.agg_other, bf16[256,256]{1,0:T(8,128)(2,1)S(1)} %copy-done.5, bf16[256,256]{1,0:T(8,128)(2,1)S(1)} %copy-done.6, ...), custom_call_target="tpu_custom_call" | custom-call | tf_op jit(solution)/shard_map/dense/pallas_call | solution.py:185
  81.5 19.5 %all_to_all.11.back = bf16[8,640,128]{2,1,0:T(8,128)(2,1)S(1)} all-to-all(bf16[8,640,128]{2,1,0:T(8,128)(2,1)S(1)} %get-tuple-element.26), channel_id=1, replica_groups=mesh['row'=32,'col'=8] {'col'}, dimensions={0} | all-to-all | bytes 2621440 | tf_op jit(solution)/shard_map/all_to_all | solution.py:241
  101.1 2.5 %backward_tiles.1 = bf16[32,256,128]{2,1,0:T(8,128)(2,1)S(1)} custom-call(s32[52]{0:T(128)S(1)} %concatenate.54.meta, bf16[12,256,256]{2,1,0:T(8,128)(2,1)S(1)} %bitcast.70, bf16[12,256,256]{2,1,0:T(8,128)(2,1)S(1)} %collective-permute-done.11.adj1, bf16[8,640,128]{2,1,0:T(8,128)(2,1)S(1)} %all_to_all.11.back), custom_call_target="tpu_custom_call" | custom-call | tf_op jit(solution)/shard_map/backward_tiles/pallas_call | solution.py:169
  103.8 7.0 %collective-permute-start.14 = (bf16[1152,128]{1,0:T(8,128)(2,1)S(1)}, bf16[1152,128]{1,0:T(8,128)(2,1)S(1)}, u32[]{:S(2)}, u32[]{:S(2)}) collective-permute-start(bf16[1152,128]{1,0:T(8,128)(2,1)S(1)} %pad_maximum_fusion), channel_id=1, source_target_pairs={{0,32},{8,232},{16,48},{24,248},{32,64},{40,8},{48,80},{56,24},{64... | collective-permute-start | bytes 884744 | tf_op jit(solution)/shard_map/ppermute | solution.py:199
  110.8 3.7 %collective-permute-done.14 = bf16[1152,128]{1,0:T(8,128)(2,1)S(1)} collective-permute-done((bf16[1152,128]{1,0:T(8,128)(2,1)S(1)}, bf16[1152,128]{1,0:T(8,128)(2,1)S(1)}, u32[]{:S(2)}, u32[]{:S(2)}) %collective-permute-start.14) | collective-permute-done | bytes 294944 | tf_op jit(solution)/shard_map/ppermute | solution.py:199
  114.7 3.2 %collective-permute-start.15 = (bf16[1152,128]{1,0:T(8,128)(2,1)S(1)}, bf16[1152,128]{1,0:T(8,128)(2,1)S(1)}, u32[]{:S(2)}, u32[]{:S(2)}) collective-permute-start(bf16[1152,128]{1,0:T(8,128)(2,1)S(1)} %pad_maximum_fusion.1), channel_id=1, source_target_pairs={{0,224},{8,232},{16,240},{24,248},{32,0},{40,8},{48,16},{56,24},{6... | collective-permute-start | bytes 884744 | tf_op jit(solution)/shard_map/ppermute | solution.py:33
  118.0 4.0 %collective-permute-done.15 = bf16[1152,128]{1,0:T(8,128)(2,1)S(1)} collective-permute-done((bf16[1152,128]{1,0:T(8,128)(2,1)S(1)}, bf16[1152,128]{1,0:T(8,128)(2,1)S(1)}, u32[]{:S(2)}, u32[]{:S(2)}) %collective-permute-start.15) | collective-permute-done | bytes 294944 | tf_op jit(solution)/shard_map/ppermute | solution.py:33
  122.1 3.5 %collective-permute-start.16 = (bf16[1152,128]{1,0:T(8,128)(2,1)S(1)}, bf16[1152,128]{1,0:T(8,128)(2,1)S(1)}, u32[]{:S(2)}, u32[]{:S(2)}) collective-permute-start(bf16[1152,128]{1,0:T(8,128)(2,1)S(1)} %pad_maximum_fusion.2), channel_id=1, source_target_pairs={{0,224},{8,232},{16,240},{24,248},{32,0},{40,8},{48,16},{56,24},{6... | collective-permute-start | bytes 884744 | tf_op jit(solution)/shard_map/ppermute | solution.py:33
  125.8 3.4 %collective-permute-done.16 = bf16[1152,128]{1,0:T(8,128)(2,1)S(1)} collective-permute-done((bf16[1152,128]{1,0:T(8,128)(2,1)S(1)}, bf16[1152,128]{1,0:T(8,128)(2,1)S(1)}, u32[]{:S(2)}, u32[]{:S(2)}) %collective-permute-start.16) | collective-permute-done | bytes 294944 | tf_op jit(solution)/shard_map/ppermute | solution.py:33
  129.4 3.2 %collective-permute-start.17 = (bf16[1152,128]{1,0:T(8,128)(2,1)S(1)}, bf16[1152,128]{1,0:T(8,128)(2,1)S(1)}, u32[]{:S(2)}, u32[]{:S(2)}) collective-permute-start(bf16[1152,128]{1,0:T(8,128)(2,1)S(1)} %pad_maximum_fusion.3), channel_id=1, source_target_pairs={{0,224},{8,232},{16,240},{24,248},{32,0},{40,8},{48,16},{56,24},{6... | collective-permute-start | bytes 884744 | tf_op jit(solution)/shard_map/ppermute | solution.py:33
  132.9 3.4 %collective-permute-done.17 = bf16[1152,128]{1,0:T(8,128)(2,1)S(1)} collective-permute-done((bf16[1152,128]{1,0:T(8,128)(2,1)S(1)}, bf16[1152,128]{1,0:T(8,128)(2,1)S(1)}, u32[]{:S(2)}, u32[]{:S(2)}) %collective-permute-start.17) | collective-permute-done | bytes 294944 | tf_op jit(solution)/shard_map/ppermute | solution.py:33
  136.3 3.4 %collective-permute-done.20 = bf16[1152,128]{1,0:T(8,128)(2,1)S(1)} collective-permute-done((bf16[1152,128]{1,0:T(8,128)(2,1)S(1)}, bf16[1152,128]{1,0:T(8,128)(2,1)S(1)}, u32[]{:S(2)}, u32[]{:S(2)}) %collective-permute-start.20) | collective-permute-done | bytes 294944 | tf_op jit(solution)/shard_map/ppermute | solution.py:33
  140.9 5.9 %collective-permute-start.22 = (bf16[384,128]{1,0:T(8,128)(2,1)S(1)}, bf16[384,128]{1,0:T(8,128)(2,1)S(1)}, u32[]{:S(2)}, u32[]{:S(2)}) collective-permute-start(bf16[384,128]{1,0:T(8,128)(2,1)S(1)} %get-tuple-element.51), channel_id=1, source_target_pairs={{0,8},{8,0},{16,24},{24,16},{32,40},{40,32},{48,56},{56,48},{64,72... | collective-permute-start | bytes 294920 | tf_op jit(solution)/shard_map/ppermute | solution.py:29
  146.9 2.6 %collective-permute-start.23 = (bf16[384,128]{1,0:T(8,128)(2,1)S(1)}, bf16[384,128]{1,0:T(8,128)(2,1)S(1)}, u32[]{:S(2)}, u32[]{:S(2)}) collective-permute-start(bf16[384,128]{1,0:T(8,128)(2,1)S(1)} %get-tuple-element.52), channel_id=1, source_target_pairs={{0,24},{8,16},{16,8},{24,0},{32,56},{40,48},{48,40},{56,32},{64,88... | collective-permute-start | bytes 294920 | tf_op jit(solution)/shard_map/ppermute | solution.py:29
  149.5 4.3 %collective-permute-done.23 = bf16[384,128]{1,0:T(8,128)(2,1)S(1)} collective-permute-done((bf16[384,128]{1,0:T(8,128)(2,1)S(1)}, bf16[384,128]{1,0:T(8,128)(2,1)S(1)}, u32[]{:S(2)}, u32[]{:S(2)}) %collective-permute-start.23) | collective-permute-done | bytes 98336 | tf_op jit(solution)/shard_map/ppermute | solution.py:29
  153.9 2.6 %collective-permute-start.24 = (f32[2,128,128]{2,1,0:T(8,128)S(1)}, f32[2,128,128]{2,1,0:T(8,128)S(1)}, u32[]{:S(2)}, u32[]{:S(2)}) collective-permute-start(f32[2,128,128]{2,1,0:T(8,128)S(1)} %pad_maximum_fusion.11), channel_id=1, source_target_pairs={{0,4},{1,5},{2,6},{3,7},{4,0},{5,1},{6,2},{7,3},{8,12},{9,13},{10,... | collective-permute-start | bytes 393224 | tf_op jit(solution)/shard_map/ppermute | solution.py:282
  157.2 3.2 %collective-permute-done.24 = f32[2,128,128]{2,1,0:T(8,128)S(1)} collective-permute-done((f32[2,128,128]{2,1,0:T(8,128)S(1)}, f32[2,128,128]{2,1,0:T(8,128)S(1)}, u32[]{:S(2)}, u32[]{:S(2)}) %collective-permute-start.24) | collective-permute-done | bytes 131104 | tf_op jit(solution)/shard_map/ppermute | solution.py:282
  (88 shorter events, 18.3 us)
Async XLA Ops:
  0.6 46.9 %copy-start = (bf16[1,1,12,256,256]{4,3,2,1,0:T(8,128)(2,1)S(1)}, bf16[1,1,12,256,256]{4,3,2,1,0:T(8,128)(2,1)}, u32[]{:S(2)}) copy-start(bf16[1,1,12,256,256]{4,3,2,1,0:T(8,128)(2,1)} %param.8) | copy-start | bytes 4718596
  0.6 39.8 %collective-permute-start.11 = (bf16[12,256,256]{2,1,0:T(8,128)(2,1)}, bf16[12,256,256]{2,1,0:T(8,128)(2,1)S(1)}, u32[]{:S(2)}, u32[]{:S(2)}) collective-permute-start(bf16[12,256,256]{2,1,0:T(8,128)(2,1)} %bitcast.68), channel_id=1, source_target_pairs={{0,8},{8,0},{16,24},{24,16},{32,40},{40,32},{48,56},{56,48},{64,72... | collective-permute-start | bytes 4718600 | tf_op jit(solution)/shard_map/ppermute | solution.py:29
  4.9 5.2 %collective-permute-start.1 = (bf16[256,128]{1,0:T(8,128)(2,1)S(1)}, bf16[256,128]{1,0:T(8,128)(2,1)S(1)}, u32[]{:S(2)}, u32[]{:S(2)}) collective-permute-start(bf16[256,128]{1,0:T(8,128)(2,1)S(1)} %get-tuple-element.48), channel_id=1, source_target_pairs={{0,16},{8,24},{16,0},{24,8},{32,48},{40,56},{48,32},{56,40},{64,80... | collective-permute-start | bytes 196616 | tf_op jit(solution)/shard_map/ppermute | solution.py:29
  5.9 5.8 %collective-permute-start.2 = (bf16[256,128]{1,0:T(8,128)(2,1)S(1)}, bf16[256,128]{1,0:T(8,128)(2,1)S(1)}, u32[]{:S(2)}, u32[]{:S(2)}) collective-permute-start(bf16[256,128]{1,0:T(8,128)(2,1)S(1)} %get-tuple-element.49), channel_id=1, source_target_pairs={{0,24},{8,16},{16,8},{24,0},{32,56},{40,48},{48,40},{56,32},{64,88... | collective-permute-start | bytes 196616 | tf_op jit(solution)/shard_map/ppermute | solution.py:29
  8.2 3.6 %collective-permute-start = (bf16[256,128]{1,0:T(8,128)(2,1)S(1)}, bf16[256,128]{1,0:T(8,128)(2,1)S(1)}, u32[]{:S(2)}, u32[]{:S(2)}) collective-permute-start(bf16[256,128]{1,0:T(8,128)(2,1)S(1)} %get-tuple-element.49), channel_id=1, source_target_pairs={{0,8},{8,0},{16,24},{24,16},{32,40},{40,32},{48,56},{56,48},{64,72... | collective-permute-start | bytes 196616 | tf_op jit(solution)/shard_map/ppermute | solution.py:29
  11.8 10.8 %collective-permute-start.4 = (bf16[4,256,128]{2,1,0:T(8,128)(2,1)S(1)}, bf16[4,256,128]{2,1,0:T(8,128)(2,1)S(1)}, u32[]{:S(2)}, u32[]{:S(2)}) collective-permute-start(bf16[4,256,128]{2,1,0:T(8,128)(2,1)S(1)} %pad_maximum_fusion.7.refs_0_), channel_id=1, source_target_pairs={{0,224},{8,232},{16,240},{24,248},{32,0},{40,8},{48,16},{56,24},{6... | collective-permute-start | bytes 786440 | tf_op jit(solution)/shard_map/ppermute | solution.py:33
  17.3 8.4 %collective-permute-start.3 = (bf16[4,256,128]{2,1,0:T(8,128)(2,1)S(1)}, bf16[4,256,128]{2,1,0:T(8,128)(2,1)S(1)}, u32[]{:S(2)}, u32[]{:S(2)}) collective-permute-start(bf16[4,256,128]{2,1,0:T(8,128)(2,1)S(1)} %pad_maximum_fusion.7.refs_0_), channel_id=1, source_target_pairs={{0,32},{8,40},{16,48},{24,56},{32,64},{40,72},{48,80},{56,88},{64,... | collective-permute-start | bytes 786440 | tf_op jit(solution)/shard_map/ppermute | solution.py:33
  18.7 1.5 collective-permute-start.5
  25.7 7.6 %collective-permute-start.6 = (bf16[4,256,128]{2,1,0:T(8,128)(2,1)S(1)}, bf16[4,256,128]{2,1,0:T(8,128)(2,1)}, u32[]{:S(2)}, u32[]{:S(2)}) collective-permute-start(bf16[4,256,128]{2,1,0:T(8,128)(2,1)S(1)} %collective-permute-done.3.refs_7_), channel_id=1, source_target_pairs={{0,32},{8,40},{16,48},{24,56},{32,64},{40,72},{48,80},{56,88},{64,... | collective-permute-start | bytes 786440 | tf_op jit(solution)/shard_map/ppermute | solution.py:33
  25.7 0.7 copy-start.3
  26.4 6.9 %collective-permute-start.7 = (bf16[4,256,128]{2,1,0:T(8,128)(2,1)S(1)}, bf16[4,256,128]{2,1,0:T(8,128)(2,1)}, u32[]{:S(2)}, u32[]{:S(2)}) collective-permute-start(bf16[4,256,128]{2,1,0:T(8,128)(2,1)S(1)} %collective-permute-done.4.refs_1_), channel_id=1, source_target_pairs={{0,224},{8,232},{16,240},{24,248},{32,0},{40,8},{48,16},{56,24},{6... | collective-permute-start | bytes 786440 | tf_op jit(solution)/shard_map/ppermute | solution.py:33
  29.1 0.7 copy-start.1
  29.8 3.3 %collective-permute-start.8 = (bf16[256,256]{1,0:T(8,128)(2,1)}, bf16[256,256]{1,0:T(8,128)(2,1)S(1)}, u32[]{:S(2)}, u32[]{:S(2)}) collective-permute-start(bf16[256,256]{1,0:T(8,128)(2,1)} %cot_own.1), channel_id=1, source_target_pairs={{0,8},{8,0},{16,24},{24,16},{32,40},{40,32},{48,56},{56,48},{64,72... | collective-permute-start | bytes 393224 | tf_op jit(solution)/shard_map/ppermute | solution.py:29
  33.3 7.2 %collective-permute-start.9 = (bf16[4,256,128]{2,1,0:T(8,128)(2,1)}, bf16[4,256,128]{2,1,0:T(8,128)(2,1)}, u32[]{:S(2)}, u32[]{:S(2)}) collective-permute-start(bf16[4,256,128]{2,1,0:T(8,128)(2,1)} %collective-permute-done.6.refs_6_), channel_id=1, source_target_pairs={{0,32},{8,40},{16,48},{24,56},{32,64},{40,72},{48,80},{56,88},{64,... | collective-permute-start | bytes 786440 | tf_op jit(solution)/shard_map/ppermute | solution.py:33
  33.3 7.2 %collective-permute-start.10 = (bf16[4,256,128]{2,1,0:T(8,128)(2,1)}, bf16[4,256,128]{2,1,0:T(8,128)(2,1)}, u32[]{:S(2)}, u32[]{:S(2)}) collective-permute-start(bf16[4,256,128]{2,1,0:T(8,128)(2,1)} %collective-permute-done.7.refs_2_), channel_id=1, source_target_pairs={{0,224},{8,232},{16,240},{24,248},{32,0},{40,8},{48,16},{56,24},{6... | collective-permute-start | bytes 786440 | tf_op jit(solution)/shard_map/ppermute | solution.py:33
  41.4 6.1 %collective-permute-start.12 = (bf16[4,256,128]{2,1,0:T(8,128)(2,1)S(1)}, bf16[4,256,128]{2,1,0:T(8,128)(2,1)S(1)}, u32[]{:S(2)}, u32[]{:S(2)}) collective-permute-start(bf16[4,256,128]{2,1,0:T(8,128)(2,1)S(1)} %broadcast_select_fusion), channel_id=1, source_target_pairs={{0,32},{8,232},{16,48},{24,248},{32,64},{40,8},{48,80},{56,24},{64... | collective-permute-start | bytes 786440 | tf_op jit(solution)/shard_map/ppermute | solution.py:199
  47.5 1.0 copy-start.2
  48.5 0.9 copy-start.4
  52.1 25.8 %copy-start.5 = (bf16[256,256]{1,0:T(8,128)(2,1)S(1)}, bf16[256,256]{1,0:T(8,128)(2,1)}, u32[]{:S(2)}) copy-start(bf16[256,256]{1,0:T(8,128)(2,1)} %weight.1) | copy-start | bytes 393220
  52.1 25.8 %copy-start.6 = (bf16[256,256]{1,0:T(8,128)(2,1)S(1)}, bf16[256,256]{1,0:T(8,128)(2,1)}, u32[]{:S(2)}) copy-start(bf16[256,256]{1,0:T(8,128)(2,1)} %cot_own.1) | copy-start | bytes 393220
  69.8 8.1 %collective-permute-start.13 = (f32[512,128]{1,0:T(8,128)S(1)}, f32[512,128]{1,0:T(8,128)S(1)}, u32[]{:S(2)}, u32[]{:S(2)}) collective-permute-start(f32[512,128]{1,0:T(8,128)S(1)} %bitcast.71), channel_id=1, source_target_pairs={{0,8},{8,0},{16,24},{24,16},{32,40},{40,32},{48,56},{56,48},{64,72... | collective-permute-start | bytes 786440 | tf_op jit(solution)/shard_map/ppermute | solution.py:29
  103.8 10.7 %collective-permute-start.14 = (bf16[1152,128]{1,0:T(8,128)(2,1)S(1)}, bf16[1152,128]{1,0:T(8,128)(2,1)S(1)}, u32[]{:S(2)}, u32[]{:S(2)}) collective-permute-start(bf16[1152,128]{1,0:T(8,128)(2,1)S(1)} %pad_maximum_fusion), channel_id=1, source_target_pairs={{0,32},{8,232},{16,48},{24,248},{32,64},{40,8},{48,80},{56,24},{64... | collective-permute-start | bytes 884744 | tf_op jit(solution)/shard_map/ppermute | solution.py:199
  114.7 7.3 %collective-permute-start.15 = (bf16[1152,128]{1,0:T(8,128)(2,1)S(1)}, bf16[1152,128]{1,0:T(8,128)(2,1)S(1)}, u32[]{:S(2)}, u32[]{:S(2)}) collective-permute-start(bf16[1152,128]{1,0:T(8,128)(2,1)S(1)} %pad_maximum_fusion.1), channel_id=1, source_target_pairs={{0,224},{8,232},{16,240},{24,248},{32,0},{40,8},{48,16},{56,24},{6... | collective-permute-start | bytes 884744 | tf_op jit(solution)/shard_map/ppermute | solution.py:33
  117.9 7.7 %collective-permute-start.18 = (bf16[1152,128]{1,0:T(8,128)(2,1)S(1)}, bf16[1152,128]{1,0:T(8,128)(2,1)S(1)}, u32[]{:S(2)}, u32[]{:S(2)}) collective-permute-start(bf16[1152,128]{1,0:T(8,128)(2,1)S(1)} %pad_maximum_fusion.4), channel_id=1, source_target_pairs={{0,32},{8,40},{16,48},{24,56},{32,64},{40,72},{48,80},{56,88},{64,... | collective-permute-start | bytes 884744 | tf_op jit(solution)/shard_map/ppermute | solution.py:33
  122.1 7.2 %collective-permute-start.16 = (bf16[1152,128]{1,0:T(8,128)(2,1)S(1)}, bf16[1152,128]{1,0:T(8,128)(2,1)S(1)}, u32[]{:S(2)}, u32[]{:S(2)}) collective-permute-start(bf16[1152,128]{1,0:T(8,128)(2,1)S(1)} %pad_maximum_fusion.2), channel_id=1, source_target_pairs={{0,224},{8,232},{16,240},{24,248},{32,0},{40,8},{48,16},{56,24},{6... | collective-permute-start | bytes 884744 | tf_op jit(solution)/shard_map/ppermute | solution.py:33
  125.7 6.9 %collective-permute-start.19 = (bf16[1152,128]{1,0:T(8,128)(2,1)S(1)}, bf16[1152,128]{1,0:T(8,128)(2,1)S(1)}, u32[]{:S(2)}, u32[]{:S(2)}) collective-permute-start(bf16[1152,128]{1,0:T(8,128)(2,1)S(1)} %pad_maximum_fusion.5), channel_id=1, source_target_pairs={{0,32},{8,40},{16,48},{24,56},{32,64},{40,72},{48,80},{56,88},{64,... | collective-permute-start | bytes 884744 | tf_op jit(solution)/shard_map/ppermute | solution.py:33
  129.4 6.9 %collective-permute-start.17 = (bf16[1152,128]{1,0:T(8,128)(2,1)S(1)}, bf16[1152,128]{1,0:T(8,128)(2,1)S(1)}, u32[]{:S(2)}, u32[]{:S(2)}) collective-permute-start(bf16[1152,128]{1,0:T(8,128)(2,1)S(1)} %pad_maximum_fusion.3), channel_id=1, source_target_pairs={{0,224},{8,232},{16,240},{24,248},{32,0},{40,8},{48,16},{56,24},{6... | collective-permute-start | bytes 884744 | tf_op jit(solution)/shard_map/ppermute | solution.py:33
  132.7 6.9 %collective-permute-start.20 = (bf16[1152,128]{1,0:T(8,128)(2,1)S(1)}, bf16[1152,128]{1,0:T(8,128)(2,1)S(1)}, u32[]{:S(2)}, u32[]{:S(2)}) collective-permute-start(bf16[1152,128]{1,0:T(8,128)(2,1)S(1)} %pad_maximum_fusion.6), channel_id=1, source_target_pairs={{0,32},{8,40},{16,48},{24,56},{32,64},{40,72},{48,80},{56,88},{64,... | collective-permute-start | bytes 884744 | tf_op jit(solution)/shard_map/ppermute | solution.py:33
  140.6 8.9 %collective-permute-start.21 = (bf16[384,128]{1,0:T(8,128)(2,1)S(1)}, bf16[384,128]{1,0:T(8,128)(2,1)S(1)}, u32[]{:S(2)}, u32[]{:S(2)}) collective-permute-start(bf16[384,128]{1,0:T(8,128)(2,1)S(1)} %get-tuple-element.50), channel_id=1, source_target_pairs={{0,16},{8,24},{16,0},{24,8},{32,48},{40,56},{48,32},{56,40},{64,80... | collective-permute-start | bytes 294920 | tf_op jit(solution)/shard_map/ppermute | solution.py:29
  140.9 8.6 %collective-permute-start.22 = (bf16[384,128]{1,0:T(8,128)(2,1)S(1)}, bf16[384,128]{1,0:T(8,128)(2,1)S(1)}, u32[]{:S(2)}, u32[]{:S(2)}) collective-permute-start(bf16[384,128]{1,0:T(8,128)(2,1)S(1)} %get-tuple-element.51), channel_id=1, source_target_pairs={{0,8},{8,0},{16,24},{24,16},{32,40},{40,32},{48,56},{56,48},{64,72... | collective-permute-start | bytes 294920 | tf_op jit(solution)/shard_map/ppermute | solution.py:29
  146.9 7.0 %collective-permute-start.23 = (bf16[384,128]{1,0:T(8,128)(2,1)S(1)}, bf16[384,128]{1,0:T(8,128)(2,1)S(1)}, u32[]{:S(2)}, u32[]{:S(2)}) collective-permute-start(bf16[384,128]{1,0:T(8,128)(2,1)S(1)} %get-tuple-element.52), channel_id=1, source_target_pairs={{0,24},{8,16},{16,8},{24,0},{32,56},{40,48},{48,40},{56,32},{64,88... | collective-permute-start | bytes 294920 | tf_op jit(solution)/shard_map/ppermute | solution.py:29
  153.9 6.5 %collective-permute-start.24 = (f32[2,128,128]{2,1,0:T(8,128)S(1)}, f32[2,128,128]{2,1,0:T(8,128)S(1)}, u32[]{:S(2)}, u32[]{:S(2)}) collective-permute-start(f32[2,128,128]{2,1,0:T(8,128)S(1)} %pad_maximum_fusion.11), channel_id=1, source_target_pairs={{0,4},{1,5},{2,6},{3,7},{4,0},{5,1},{6,2},{7,3},{8,12},{9,13},{10,... | collective-permute-start | bytes 393224 | tf_op jit(solution)/shard_map/ppermute | solution.py:282

commit v3 on v2

--- a/solution.py
+++ b/solution.py
@@ -15,6 +15,7 @@
 HALF = 128
 SLOTS = 12
 W_ROWS = 128
+UNROLL = 4
 
 
 def row_pairs(move):
@@ -33,75 +34,105 @@
     return lax.ppermute(x, "row", row_pairs(lambda z, q: (z + step, q)))
 
 
-def load_live_tiles(meta, adj_refs, adj_vmem, adj_sem):
+def list_slots(meta, adj_refs, adj_vmem, adj_sem, rows, places, far, dummy):
+    z, q = meta[50], meta[51]
+    n = jnp.int32(0)
     for i in range(2):
-
-        @pl.loop(0, meta[25 * i + 24])
-        def _(s, i=i):
-            pltpu.make_async_copy(
-                adj_refs[i].at[s], adj_vmem.at[i, s], adj_sem.at[i, s]
-            ).start()
-
-
-def wait_tile(adj_refs, adj_vmem, adj_sem, i, s):
-    pltpu.make_async_copy(adj_refs[i].at[s], adj_vmem.at[i, s], adj_sem.at[i, s]).wait()
-
-
-def panel_place(meta, tile):
-    z, q = meta[50], meta[51]
-    return (((tile >> 2) - z) & 7) * QUAD + ((tile & 3) ^ q)
-
-
-def forward_kernel(meta, adj0, adj1, *refs):
-    pieces, (out, panel, adj_vmem, acc, panel_sem, adj_sem) = refs[:8], refs[8:]
-    adj_refs = (adj0, adj1)
+        count = meta[25 * i + 24]
+        for s in range(SLOTS):
+            tile = meta[25 * i + 12 + s]
+            place = (((tile >> 2) - z) & 7) * QUAD + ((tile & 3) ^ q)
+            live = (s < count) & (((place >> 2) == 4) == far)
+            rows[n] = meta[25 * i + s] * 2 + i
+            places[n] = place
+
+            @pl.when(live)
+            def _(i=i, s=s, n=n):
+                pltpu.make_async_copy(
+                    adj_refs[i].at[s], adj_vmem.at[n], adj_sem.at[n]
+                ).start()
+
+            n = n + live.astype(jnp.int32)
+    for u in range(UNROLL - 1):
+        rows[n + u], places[n + u] = dummy
+    return n
+
+
+def slot_products(n, adj_ref, adj_vmem, adj_sem, product, add_to):
+    @pl.loop(0, (n + UNROLL - 1) >> 2)
+    def _(step):
+        slots = [step * UNROLL + u for u in range(UNROLL)]
+        for j in slots:
+
+            @pl.when(j < n)
+            def _(j=j):
+                pltpu.make_async_copy(adj_ref.at[0], adj_vmem.at[j], adj_sem.at[j]).wait()
+
+        values = [product(j) for j in slots]
+        for j, value in zip(slots, values):
+            add_to(j, value)
+
+
+def forward_near_kernel(meta, adj0, adj1, *refs):
+    pieces, (acc, panel, adj_vmem, rows, places, panel_sem, adj_sem) = refs[:7], refs[7:]
     copies = [
-        pltpu.make_async_copy(
-            piece,
-            panel.at[pl.ds(n * QUAD, QUAD)],
-            panel_sem.at[n],
-        )
-        for n, piece in enumerate(pieces)
+        pltpu.make_async_copy(piece, panel.at[pl.ds(place * QUAD, QUAD)], panel_sem.at[place])
+        for place, piece in zip((0, 1, 2, 3, 5, 6, 7), pieces)
     ]
     for copy in copies:
         copy.start()
-    load_live_tiles(meta, adj_refs, adj_vmem, adj_sem)
+    n = list_slots(meta, (adj0, adj1), adj_vmem, adj_sem, rows, places, False, (16, 0))
     acc[...] = jnp.zeros_like(acc)
     for copy in copies:
         copy.wait()
-    for i in range(2):
-
-        @pl.loop(0, meta[25 * i + 24])
-        def _(s, i=i):
-            wait_tile(adj_refs, adj_vmem, adj_sem, i, s)
-            row = meta[25 * i + s]
-            place = panel_place(meta, meta[25 * i + 12 + s])
-            acc[row, i] += jnp.dot(
-                adj_vmem[i, s], panel[place], preferred_element_type=jnp.float32
-            )
-
-    out[...] = acc[...].astype(jnp.bfloat16)
-
-
-def backward_kernel(meta, adj0, adj1, back, out, adj_vmem, acc, adj_sem):
-    adj_refs = (adj0, adj1)
-    load_live_tiles(meta, adj_refs, adj_vmem, adj_sem)
+
+    def product(j):
+        return jnp.dot(adj_vmem[j], panel[places[j]], preferred_element_type=jnp.float32)
+
+    def add_to(j, value):
+        acc[rows[j]] += value
+
+    slot_products(n, adj0, adj_vmem, adj_sem, product, add_to)
+
+
+def forward_far_kernel(meta, adj0, adj1, near, far, out, acc, adj_vmem, rows, places, adj_sem):
+    n = list_slots(meta, (adj0, adj1), adj_vmem, adj_sem, rows, places, True, (16, 16))
+    acc[...] = near[...]
+
+    def product(j):
+        return jnp.dot(adj_vmem[j], far[places[j] - 16], preferred_element_type=jnp.float32)
+
+    def add_to(j, value):
+        acc[rows[j]] += value
+
+    slot_products(n, adj0, adj_vmem, adj_sem, product, add_to)
+    for row in range(8):
+        for i in range(2):
+            out[row, i] = acc[2 * row + i].astype(jnp.bfloat16)
+
+
+def backward_kernel(far, meta, adj0, adj1, back, out, acc, adj_vmem, rows, places, adj_sem):
+    base = 16 if far else 0
+    spare = acc.shape[0] - 1
+    n = list_slots(
+        meta, (adj0, adj1), adj_vmem, adj_sem, rows, places, far, (0, base + spare)
+    )
     acc[...] = jnp.zeros_like(acc)
-    for i in range(2):
-
-        @pl.loop(0, meta[25 * i + 24])
-        def _(s, i=i):
-            wait_tile(adj_refs, adj_vmem, adj_sem, i, s)
-            row = meta[25 * i + s]
-            place = panel_place(meta, meta[25 * i + 12 + s])
-            acc[place] += lax.dot_general(
-                adj_vmem[i, s],
-                back[row, pl.ds(i * TILE, TILE), :],
-                (((0,), (0,)), ((), ())),
-                preferred_element_type=jnp.float32,
-            )
-
-    out[...] = acc[...].astype(jnp.bfloat16)
+
+    def product(j):
+        row = rows[j]
+        return lax.dot_general(
+            adj_vmem[j],
+            back[row >> 1, pl.ds((row & 1) * TILE, TILE), :],
+            (((0,), (0,)), ((), ())),
+            preferred_element_type=jnp.float32,
+        )
+
+    def add_to(j, value):
+        acc[places[j] - base] += value
+
+    slot_products(n, adj0, adj_vmem, adj_sem, product, add_to)
+    out[...] = acc[:spare].astype(jnp.bfloat16)
 
 
 def dense_kernel(meta, agg_own, agg_other, weight, cot_own, cot_other, act_out, send_out):
@@ -147,37 +178,63 @@
     return pltpu.CompilerParams(vmem_limit_bytes=mib << 20)
 
 
-def forward_tiles(meta, adj0, adj1, pieces):
+LIST = 2 * SLOTS + UNROLL
+SLOT_SCRATCH = [
+    pltpu.VMEM((LIST, TILE, TILE), jnp.bfloat16),
+    pltpu.SMEM((LIST,), jnp.int32),
+    pltpu.SMEM((LIST,), jnp.int32),
+]
+
+
+def cost(slots, size):
+    return pl.CostEstimate(
+        flops=slots * 2 * TILE * TILE * HALF, bytes_accessed=size << 20, transcendentals=0
+    )
+
+
+def forward_near(meta, adj0, adj1, pieces):
     return pl.pallas_call(
-        forward_kernel,
+        forward_near_kernel,
+        out_shape=jax.ShapeDtypeStruct((17, TILE, HALF), jnp.float32),
+        in_specs=[SMEM] + [ANY] * 9,
+        out_specs=VMEM,
+        scratch_shapes=[pltpu.VMEM((NZ * QUAD, TILE, HALF), jnp.bfloat16)]
+        + SLOT_SCRATCH
+        + [pltpu.SemaphoreType.DMA((NZ,)), pltpu.SemaphoreType.DMA((LIST,))],
+        compiler_params=params(20),
+        cost_estimate=cost(21, 6),
+        name="forward_near",
+    )(meta, adj0, adj1, *pieces)
+
+
+def forward_far(meta, adj0, adj1, near, far):
+    return pl.pallas_call(
+        forward_far_kernel,
         out_shape=jax.ShapeDtypeStruct((8, 2, TILE, HALF), jnp.bfloat16),
-        in_specs=[SMEM, HBM, HBM] + [ANY] * 8,
+        in_specs=[SMEM, ANY, ANY, VMEM, VMEM],
         out_specs=VMEM,
-        scratch_shapes=[
-            pltpu.VMEM((NZ * QUAD, TILE, HALF), jnp.bfloat16),
-            pltpu.VMEM((2, SLOTS, TILE, TILE), jnp.bfloat16),
-            pltpu.VMEM((8, 2, TILE, HALF), jnp.float32),
-            pltpu.SemaphoreType.DMA((NZ,)),
-            pltpu.SemaphoreType.DMA((2, SLOTS)),
-        ],
+        scratch_shapes=[pltpu.VMEM((17, TILE, HALF), jnp.float32)]
+        + SLOT_SCRATCH
+        + [pltpu.SemaphoreType.DMA((LIST,))],
         compiler_params=params(20),
-        name="forward_tiles",
-    )(meta, adj0, adj1, *pieces)
-
-
-def backward_tiles(meta, adj0, adj1, back):
+        cost_estimate=cost(3, 4),
+        name="forward_far",
+    )(meta, adj0, adj1, near, far)
+
+
+def backward_tiles(meta, adj0, adj1, back, far):
+    places = QUAD if far else NZ * QUAD
     return pl.pallas_call(
-        backward_kernel,
-        out_shape=jax.ShapeDtypeStruct((NZ * QUAD, TILE, HALF), jnp.bfloat16),
-        in_specs=[SMEM, HBM, HBM, VMEM],
+        functools.partial(backward_kernel, far),
+        out_shape=jax.ShapeDtypeStruct((places, TILE, HALF), jnp.bfloat16),
+        in_specs=[SMEM, ANY, ANY, VMEM],
         out_specs=VMEM,
-        scratch_shapes=[
-            pltpu.VMEM((2, SLOTS, TILE, TILE), jnp.bfloat16),
-            pltpu.VMEM((NZ * QUAD, TILE, HALF), jnp.float32),
-            pltpu.SemaphoreType.DMA((2, SLOTS)),
-        ],
+        scratch_shapes=[pltpu.VMEM((places + 1, TILE, HALF), jnp.float32)]
+        + SLOT_SCRATCH
+        + [pltpu.SemaphoreType.DMA((LIST,))],
         compiler_params=params(20),
-        name="backward_tiles",
+        cost_estimate=cost(3, 2) if far else cost(21, 6),
+        name="backward_far" if far else "backward_near",
     )(meta, adj0, adj1, back)
 
 
@@ -214,39 +271,37 @@
 
     mine = jnp.where(first, block[:, :HALF], block[:, HALF:])
     theirs = jnp.where(first, block[:, HALF:], block[:, :HALF])
+    meta0 = jnp.concatenate([tile_row[0, 0], tile_col[0, 0], tile_count[0]])
+    listed = jnp.pad(meta0.astype(jnp.bfloat16)[None], ((0, 15), (0, HALF - 25)))
+    from_core = quad_permute(jnp.concatenate([theirs, listed], axis=0), 1)
     chunk = jnp.stack(
-        [mine, quad_permute(theirs, 1), quad_permute(mine, 2), quad_permute(theirs, 3)]
-    )
-
-    meta0 = jnp.concatenate([tile_row[0, 0], tile_col[0, 0], tile_count[0]])
-    meta1 = quad_permute(meta0, 1)
+        [mine, from_core[:TILE], quad_permute(mine, 2), quad_permute(theirs, 3)]
+    )
+    meta1 = from_core[TILE, :25].astype(jnp.int32)
+    meta = jnp.concatenate([meta0, meta1, jnp.stack([z, quad]).astype(jnp.int32)])
     adj1 = quad_permute(adj0, 1)
     cot1 = quad_permute(cotangent, 1)
 
     up1, down1 = z_shift(chunk, 1), z_shift(chunk, -1)
-    up1, down1, meta1 = lax.optimization_barrier((up1, down1, meta1))
-    meta = jnp.concatenate([meta0, meta1, jnp.stack([z, quad]).astype(jnp.int32)])
     up2, down2 = z_shift(up1, 1), z_shift(down1, -1)
-    up2, down2, cot1 = lax.optimization_barrier((up2, down2, cot1))
     up3, down3 = z_shift(up2, 1), z_shift(down2, -1)
-    up3, down3, meta, adj1 = lax.optimization_barrier((up3, down3, meta, adj1))
     far = z_both(jnp.where(first, up3, down3))
-    pieces = [chunk, down1, down2, down3, far, up3, up2, up1]
-
-    partial = forward_tiles(meta, adj0, adj1, pieces)
+    near = forward_near(meta, adj0, adj1, [chunk, down1, down2, down3, up3, up2, up1])
+    partial = forward_far(meta, adj0, adj1, near, far)
     shares = lax.all_to_all(partial, "col", 0, 0, tiled=True)
     agg = shares.reshape(NCOL, 2 * TILE, HALF).astype(jnp.float32).sum(axis=0)
     agg_other = quad_permute(agg, 1)
     activated, send = dense(meta, agg, agg_other, weight, cotangent, cot1)
     received = lax.all_to_all(send, "col", 0, 0, tiled=True)
     w_piece = received[:, 2 * TILE :, :].astype(jnp.float32).sum(axis=0).astype(jnp.bfloat16)
-    parts = backward_tiles(meta, adj0, adj1, received).reshape(NZ, QUAD * TILE, HALF)
+    size = QUAD * TILE
+    far_part = backward_tiles(meta, adj0, adj1, received, True).reshape(size, HALF)
+    parts = backward_tiles(meta, adj0, adj1, received, False).reshape(NZ, size, HALF)
 
     def pack(part, piece):
         return jnp.concatenate([part, piece], axis=0)
 
-    size = QUAD * TILE
-    got1 = z_both(pack(parts[4], w_piece))
+    got1 = z_both(pack(far_part, w_piece))
     zero = jnp.zeros_like(got1[:size])
     up = add(parts[3], jnp.where(first, got1[:size], zero))
     down = add(parts[5], jnp.where(first, zero, got1[:size]))

time: 163 us -> 161 us (0.988)
  blocking collectives: 37.1 us -> 14.9 us
  waiting for transfers between devices: 44.3 us -> 59.9 us
  starting transfers between devices: 59.1 us -> 48.8 us
  Pallas kernels: 8.79 us -> 16.8 us
  local copies, waits for them, and re-layouts: 5.26 us -> 11.7 us
    all_to_all x1 -> x0, blocking collectives: 19.5 us -> none  [per_device(): received = lax.all_to_all(send, 'col', 0, 0, tiled=True)]
    all_to_all x0 -> x1, waiting for transfers between devices: none -> 17.8 us  [per_device(): received = lax.all_to_all(send, 'col', 0, 0, tiled=True)]
    pallas_call x2 -> x4, Pallas kernels: 5.16 us -> 13.1 us  [the longest x2 7.19 us: backward_tiles(): pl.pallas_call(functools.partial(backward_kernel, far), out_shape=jax.Sha...]
    ppermute x12, waiting for transfers between devices: 23.2 us -> 30.2 us  [z_shift(): return lax.ppermute(x, 'row', row_pairs(lambda z, q: (z + step, q)))]
    ppermute x2, starting transfers between devices: 9.77 us -> 2.73 us  [z_both(): lax.ppermute(x, 'row', row_pairs(lambda z, q: (z + 1 - 2 * (q & 1), q)))]
    unnamed x15 -> x37, local copies, waits for them, and re-layouts: 3.32 us -> 10.3 us
    ppermute x2, waiting for transfers between devices: 6.97 us -> 0.01 us  [z_both(): lax.ppermute(x, 'row', row_pairs(lambda z, q: (z + 1 - 2 * (q & 1), q)))]
    ppermute x10 -> x9, starting transfers between devices: 25.4 us -> 20.2 us  [quad_permute(): return lax.ppermute(x, 'row', row_pairs(lambda z, q: (z, q ^ flip)))]
  transfers between devices with their start and end apart: 25 -> 25, of which waited for: 17 -> 14; matrix products, arithmetic and copies ran while one was open for 2% -> 1% of each run, Pallas kernels for 0% -> 6%
where the time goes in v3:
time: 161 us; the launch traced here: 160 us
  waiting for transfers between devices  59.9 us (37%)
  starting transfers between devices  48.8 us (30%)
  Pallas kernels  16.8 us (10%)
  blocking collectives  14.9 us (9%)
  local copies, waits for them, and re-layouts  11.7 us (7%)
  other arithmetic  6.29 us (4%)
  between operations  1.87 us (1%)
    ppermute x12, waiting for transfers between devices, z_shift(): return lax.ppermute(x, 'row', row_pairs(lambda z, q: (z + step, q)))  30.2 us
    ppermute x12, starting transfers between devices, z_shift(): return lax.ppermute(x, 'row', row_pairs(lambda z, q: (z + step, q)))  20.5 us
    ppermute x9, starting transfers between devices, quad_permute(): return lax.ppermute(x, 'row', row_pairs(lambda z, q: (z, q ^ flip)))  20.2 us
    all_to_all x1, waiting for transfers between devices, per_device(): received = lax.all_to_all(send, 'col', 0, 0, tiled=True)  17.8 us
    all_to_all x1, blocking collectives, per_device(): shares = lax.all_to_all(partial, 'col', 0, 0, tiled=True)  14.9 us
    unnamed x37, local copies, waits for them, and re-layouts  10.3 us
    ppermute x9, waiting for transfers between devices, quad_permute(): return lax.ppermute(x, 'row', row_pairs(lambda z, q: (z, q ^ flip)))  8.92 us
    pallas_call x2, Pallas kernels, backward_tiles(): pl.pallas_call(functools.partial(backward_kernel, far), out_shape=jax.Sha...  7.19 us
  transfers between devices with their start and end apart: 25, of which 14 were waited for; matrix products, arithmetic and copies ran while one was open for 1% of the time, Pallas kernels for 6%

profile of v3, /device:TPU:1, one launch (start us, length us, event | category | flops | bytes accessed | tf_op | source)
XLA Modules:
  0.0 160.2 jit_solution(1833020820763486582)
XLA Ops:
  3.1 3.3 %collective-permute-start = (bf16[272,128]{1,0:T(8,128)(2,1)S(1)}, bf16[272,128]{1,0:T(8,128)(2,1)S(1)}, u32[]{:S(2)}, u32[]{:S(2)}) collective-permute-start(bf16[272,128]{1,0:T(8,128)(2,1)S(1)} %pad_maximum_fusion.13), channel_id=1, source_target_pairs={{0,8},{8,0},{16,24},{24,16},{32,40},{40,32},{48,56},{56,48},{64,72... | collective-permute-start | bytes 208904 | tf_op jit(solution)/shard_map/ppermute | solution.py:30
  7.9 2.0 %collective-permute-start.2 = (bf16[256,128]{1,0:T(8,128)(2,1)S(1)}, bf16[256,128]{1,0:T(8,128)(2,1)S(1)}, u32[]{:S(2)}, u32[]{:S(2)}) collective-permute-start(bf16[256,128]{1,0:T(8,128)(2,1)S(1)} %get-tuple-element.27), channel_id=1, source_target_pairs={{0,16},{8,24},{16,0},{24,8},{32,48},{40,56},{48,32},{56,40},{64,80... | collective-permute-start | bytes 196616 | tf_op jit(solution)/shard_map/ppermute | solution.py:30
  9.8 1.9 %collective-permute-done.3 = bf16[256,128]{1,0:T(8,128)(2,1)S(1)} collective-permute-done((bf16[256,128]{1,0:T(8,128)(2,1)S(1)}, bf16[256,128]{1,0:T(8,128)(2,1)S(1)}, u32[]{:S(2)}, u32[]{:S(2)}) %collective-permute-start.3) | collective-permute-done | bytes 65568 | tf_op jit(solution)/shard_map/ppermute | solution.py:30
  11.7 1.3 collective-permute-done.2
  13.1 5.7 %collective-permute-start.4 = (bf16[4,256,128]{2,1,0:T(8,128)(2,1)S(1)}, bf16[4,256,128]{2,1,0:T(8,128)(2,1)S(1)}, u32[]{:S(2)}, u32[]{:S(2)}) collective-permute-start(bf16[4,256,128]{2,1,0:T(8,128)(2,1)S(1)} %pad_maximum_fusion.7.refs_0_), channel_id=1, source_target_pairs={{0,224},{8,232},{16,240},{24,248},{32,0},{40,8},{48,16},{56,24},{6... | collective-permute-start | bytes 786440 | tf_op jit(solution)/shard_map/ppermute | solution.py:34
  18.7 4.8 %collective-permute-done.4.refs_1_ = bf16[4,256,128]{2,1,0:T(8,128)(2,1)S(1)} collective-permute-done((bf16[4,256,128]{2,1,0:T(8,128)(2,1)S(1)}, bf16[4,256,128]{2,1,0:T(8,128)(2,1)S(1)}, u32[]{:S(2)}, u32[]{:S(2)}) %collective-permute-start.4) | collective-permute-done | bytes 262176 | tf_op jit(solution)/shard_map/ppermute | solution.py:34
  23.5 3.4 %collective-permute-start.5 = (bf16[4,256,128]{2,1,0:T(8,128)(2,1)S(1)}, bf16[4,256,128]{2,1,0:T(8,128)(2,1)S(1)}, u32[]{:S(2)}, u32[]{:S(2)}) collective-permute-start(bf16[4,256,128]{2,1,0:T(8,128)(2,1)S(1)} %collective-permute-done.4.refs_1_), channel_id=1, source_target_pairs={{0,224},{8,232},{16,240},{24,248},{32,0},{40,8},{48,16},{56,24},{6... | collective-permute-start | bytes 786440 | tf_op jit(solution)/shard_map/ppermute | solution.py:34
  28.3 2.4 %collective-permute-done.5.refs_2_ = bf16[4,256,128]{2,1,0:T(8,128)(2,1)S(1)} collective-permute-done((bf16[4,256,128]{2,1,0:T(8,128)(2,1)S(1)}, bf16[4,256,128]{2,1,0:T(8,128)(2,1)S(1)}, u32[]{:S(2)}, u32[]{:S(2)}) %collective-permute-start.5) | collective-permute-done | bytes 262176 | tf_op jit(solution)/shard_map/ppermute | solution.py:34
  30.7 3.4 %collective-permute-start.6 = (bf16[4,256,128]{2,1,0:T(8,128)(2,1)S(1)}, bf16[4,256,128]{2,1,0:T(8,128)(2,1)S(1)}, u32[]{:S(2)}, u32[]{:S(2)}) collective-permute-start(bf16[4,256,128]{2,1,0:T(8,128)(2,1)S(1)} %collective-permute-done.5.refs_2_), channel_id=1, source_target_pairs={{0,224},{8,232},{16,240},{24,248},{32,0},{40,8},{48,16},{56,24},{6... | collective-permute-start | bytes 786440 | tf_op jit(solution)/shard_map/ppermute | solution.py:34
  35.6 1.9 %collective-permute-done.6.refs_3_ = bf16[4,256,128]{2,1,0:T(8,128)(2,1)S(1)} collective-permute-done((bf16[4,256,128]{2,1,0:T(8,128)(2,1)S(1)}, bf16[4,256,128]{2,1,0:T(8,128)(2,1)S(1)}, u32[]{:S(2)}, u32[]{:S(2)}) %collective-permute-start.6) | collective-permute-done | bytes 262176 | tf_op jit(solution)/shard_map/ppermute | solution.py:34
  37.5 3.8 %collective-permute-done.9.refs_4_ = bf16[4,256,128]{2,1,0:T(8,128)(2,1)S(1)} collective-permute-done((bf16[4,256,128]{2,1,0:T(8,128)(2,1)S(1)}, bf16[4,256,128]{2,1,0:T(8,128)(2,1)S(1)}, u32[]{:S(2)}, u32[]{:S(2)}) %collective-permute-start.9) | collective-permute-done | bytes 262176 | tf_op jit(solution)/shard_map/ppermute | solution.py:34
  48.6 4.2 %forward_near.1.near = f32[17,256,128]{2,1,0:T(8,128)S(1)} custom-call(s32[52]{0:T(128)S(1)} %concatenate.72.meta, bf16[12,256,256]{2,1,0:T(8,128)(2,1)S(1)} %bitcast.78, bf16[12,256,256]{2,1,0:T(8,128)(2,1)S(1)} %collective-permute-done.1.adj1, bf16[4,256,128]{2,1,0:T(8,128)(2,1)S(1)} %pad_maximum_fusion.7.refs_0_, bf16[4,256,128]{2,1,0:T(8,128)(2,1)S(1)} %copy-done.7, ...), custom_call_target="tpu_custom_call" | custom-call | flops 352321536 | bytes 6291456 | tf_op jit(solution)/shard_map/forward_near/pallas_call | solution.py:196
  52.8 1.8 %forward_far.1 = bf16[8,2,256,128]{3,2,1,0:T(8,128)(2,1)S(1)} custom-call(s32[52]{0:T(128)S(1)} %concatenate.72.meta, bf16[12,256,256]{2,1,0:T(8,128)(2,1)S(1)} %bitcast.79, bf16[12,256,256]{2,1,0:T(8,128)(2,1)S(1)} %collective-permute-done.1.adj1, f32[17,256,128]{2,1,0:T(8,128)S(1)} %forward_near.1.near, bf16[4,256,128]{2,1,0:T(8,128)(2,1)} %collective-permute-done.10.far), custom_call_target="tpu_custom_call" | custom-call | flops 50331648 | bytes 4194304 | tf_op jit(solution)/shard_map/forward_far/pallas_call | solution.py:211
  54.6 14.9 %all_to_all.10 = bf16[8,2,256,128]{3,2,1,0:T(8,128)(2,1)S(1)} all-to-all(bf16[8,2,256,128]{3,2,1,0:T(8,128)(2,1)S(1)} %forward_far.1), channel_id=1, replica_groups=mesh['row'=32,'col'=8] {'col'}, dimensions={0} | all-to-all | bytes 2097152 | tf_op jit(solution)/shard_map/all_to_all | solution.py:291
  69.7 6.0 %collective-permute-start.11 = (f32[512,128]{1,0:T(8,128)S(1)}, f32[512,128]{1,0:T(8,128)S(1)}, u32[]{:S(2)}, u32[]{:S(2)}) collective-permute-start(f32[512,128]{1,0:T(8,128)S(1)} %bitcast.82), channel_id=1, source_target_pairs={{0,8},{8,0},{16,24},{24,16},{32,40},{40,32},{48,56},{56,48},{64,72... | collective-permute-start | bytes 786440 | tf_op jit(solution)/shard_map/ppermute | solution.py:30
  77.1 3.6 %dense.1 = (bf16[256,256]{1,0:T(8,128)(2,1)}, bf16[8,640,128]{2,1,0:T(8,128)(2,1)S(1)}) custom-call(s32[52]{0:T(128)S(1)} %concatenate.72.meta, f32[512,128]{1,0:T(8,128)S(1)} %bitcast.83, f32[512,128]{1,0:T(8,128)S(1)} %collective-permute-done.11.agg_other, bf16[256,256]{1,0:T(8,128)(2,1)S(1)} %copy-done.14, bf16[256,256]{1,0:T(8,128)(2,1)S(1)} %copy-done.15, ...), custom_call_target="tpu_custom_call" | custom-call | tf_op jit(solution)/shard_map/dense/pallas_call | solution.py:242
  81.8 4.3 %all-to-all-start.1 = ((bf16[8,640,128]{2,1,0:T(8,128)(2,1)}), bf16[8,640,128]{2,1,0:T(8,128)(2,1)}, u32[]{:S(2)}, u32[]{:S(2)}) async-start(bf16[8,640,128]{2,1,0:T(8,128)(2,1)} %copy-done.1), calls=%async_computation.1 | async-start | bytes 2621440 | tf_op jit(solution)/shard_map/all_to_all | solution.py:295
  86.1 17.8 %all-to-all-done.1.back = bf16[8,640,128]{2,1,0:T(8,128)(2,1)} async-done(((bf16[8,640,128]{2,1,0:T(8,128)(2,1)}), bf16[8,640,128]{2,1,0:T(8,128)(2,1)}, u32[]{:S(2)}, u32[]{:S(2)}) %all-to-all-start.1) | async-done | bytes 1310752 | tf_op jit(solution)/shard_map/all_to_all | solution.py:295
  104.9 2.0 %backward_far.1 = bf16[4,256,128]{2,1,0:T(8,128)(2,1)S(1)} custom-call(s32[52]{0:T(128)S(1)} %concatenate.72.meta, bf16[12,256,256]{2,1,0:T(8,128)(2,1)S(1)} %bitcast.80, bf16[12,256,256]{2,1,0:T(8,128)(2,1)S(1)} %collective-permute-done.1.adj1, bf16[8,640,128]{2,1,0:T(8,128)(2,1)} %all-to-all-done.1.back), custom_call_target="tpu_custom_call" | custom-call | flops 50331648 | bytes 2097152 | tf_op jit(solution)/shard_map/backward_far/pallas_call | solution.py:227
  106.9 2.7 %collective-permute-start.13 = (bf16[1152,128]{1,0:T(8,128)(2,1)S(1)}, bf16[1152,128]{1,0:T(8,128)(2,1)S(1)}, u32[]{:S(2)}, u32[]{:S(2)}) collective-permute-start(bf16[1152,128]{1,0:T(8,128)(2,1)S(1)} %pad_maximum_fusion), channel_id=1, source_target_pairs={{0,32},{8,232},{16,48},{24,248},{32,64},{40,8},{48,80},{56,24},{64... | collective-permute-start | bytes 884744 | tf_op jit(solution)/shard_map/ppermute | solution.py:256
  109.6 5.2 %backward_near.1 = bf16[32,256,128]{2,1,0:T(8,128)(2,1)S(1)} custom-call(s32[52]{0:T(128)S(1)} %concatenate.72.meta, bf16[12,256,256]{2,1,0:T(8,128)(2,1)S(1)} %bitcast.81, bf16[12,256,256]{2,1,0:T(8,128)(2,1)S(1)} %collective-permute-done.1.adj1, bf16[8,640,128]{2,1,0:T(8,128)(2,1)} %all-to-all-done.1.back), custom_call_target="tpu_custom_call" | custom-call | flops 352321536 | bytes 6291456 | tf_op jit(solution)/shard_map/backward_near/pallas_call | solution.py:227
  115.3 1.4 collective-permute-start.14
  116.9 6.1 %collective-permute-done.14 = bf16[1152,128]{1,0:T(8,128)(2,1)S(1)} collective-permute-done((bf16[1152,128]{1,0:T(8,128)(2,1)S(1)}, bf16[1152,128]{1,0:T(8,128)(2,1)S(1)}, u32[]{:S(2)}, u32[]{:S(2)}) %collective-permute-start.14) | collective-permute-done | bytes 294944 | tf_op jit(solution)/shard_map/ppermute | solution.py:34
  123.2 2.8 %collective-permute-start.15 = (bf16[1152,128]{1,0:T(8,128)(2,1)S(1)}, bf16[1152,128]{1,0:T(8,128)(2,1)S(1)}, u32[]{:S(2)}, u32[]{:S(2)}) collective-permute-start(bf16[1152,128]{1,0:T(8,128)(2,1)S(1)} %pad_maximum_fusion.2), channel_id=1, source_target_pairs={{0,224},{8,232},{16,240},{24,248},{32,0},{40,8},{48,16},{56,24},{6... | collective-permute-start | bytes 884744 | tf_op jit(solution)/shard_map/ppermute | solution.py:34
  126.2 4.5 %collective-permute-done.15 = bf16[1152,128]{1,0:T(8,128)(2,1)S(1)} collective-permute-done((bf16[1152,128]{1,0:T(8,128)(2,1)S(1)}, bf16[1152,128]{1,0:T(8,128)(2,1)S(1)}, u32[]{:S(2)}, u32[]{:S(2)}) %collective-permute-start.15) | collective-permute-done | bytes 294944 | tf_op jit(solution)/shard_map/ppermute | solution.py:34
  130.8 3.5 %collective-permute-start.16 = (bf16[1152,128]{1,0:T(8,128)(2,1)S(1)}, bf16[1152,128]{1,0:T(8,128)(2,1)S(1)}, u32[]{:S(2)}, u32[]{:S(2)}) collective-permute-start(bf16[1152,128]{1,0:T(8,128)(2,1)S(1)} %pad_maximum_fusion.3), channel_id=1, source_target_pairs={{0,224},{8,232},{16,240},{24,248},{32,0},{40,8},{48,16},{56,24},{6... | collective-permute-start | bytes 884744 | tf_op jit(solution)/shard_map/ppermute | solution.py:34
  134.6 3.4 %collective-permute-done.16 = bf16[1152,128]{1,0:T(8,128)(2,1)S(1)} collective-permute-done((bf16[1152,128]{1,0:T(8,128)(2,1)S(1)}, bf16[1152,128]{1,0:T(8,128)(2,1)S(1)}, u32[]{:S(2)}, u32[]{:S(2)}) %collective-permute-start.16) | collective-permute-done | bytes 294944 | tf_op jit(solution)/shard_map/ppermute | solution.py:34
  138.0 3.3 %collective-permute-done.19 = bf16[1152,128]{1,0:T(8,128)(2,1)S(1)} collective-permute-done((bf16[1152,128]{1,0:T(8,128)(2,1)S(1)}, bf16[1152,128]{1,0:T(8,128)(2,1)S(1)}, u32[]{:S(2)}, u32[]{:S(2)}) %collective-permute-start.19) | collective-permute-done | bytes 294944 | tf_op jit(solution)/shard_map/ppermute | solution.py:34
  142.3 1.3 collective-permute-start.20
  143.5 5.9 %collective-permute-start.22 = (bf16[384,128]{1,0:T(8,128)(2,1)S(1)}, bf16[384,128]{1,0:T(8,128)(2,1)S(1)}, u32[]{:S(2)}, u32[]{:S(2)}) collective-permute-start(bf16[384,128]{1,0:T(8,128)(2,1)S(1)} %get-tuple-element.31), channel_id=1, source_target_pairs={{0,24},{8,16},{16,8},{24,0},{32,56},{40,48},{48,40},{56,32},{64,88... | collective-permute-start | bytes 294920 | tf_op jit(solution)/shard_map/ppermute | solution.py:30
  149.4 4.7 %collective-permute-done.22 = bf16[384,128]{1,0:T(8,128)(2,1)S(1)} collective-permute-done((bf16[384,128]{1,0:T(8,128)(2,1)S(1)}, bf16[384,128]{1,0:T(8,128)(2,1)S(1)}, u32[]{:S(2)}, u32[]{:S(2)}) %collective-permute-start.22) | collective-permute-done | bytes 98336 | tf_op jit(solution)/shard_map/ppermute | solution.py:30
  155.9 3.0 %collective-permute-done.23 = f32[2,128,128]{2,1,0:T(8,128)S(1)} collective-permute-done((f32[2,128,128]{2,1,0:T(8,128)S(1)}, f32[2,128,128]{2,1,0:T(8,128)S(1)}, u32[]{:S(2)}, u32[]{:S(2)}) %collective-permute-start.23) | collective-permute-done | bytes 131104 | tf_op jit(solution)/shard_map/ppermute | solution.py:337
  (115 shorter events, 22.2 us)
Async XLA Ops:
  0.6 42.2 %copy-start.16 = (s32[1,1,12]{2,1,0:T(1,128)S(1)}, s32[1,1,12]{2,1,0:T(1,128)}, u32[]{:S(2)}) copy-start(s32[1,1,12]{2,1,0:T(1,128)} %param.9) | copy-start | bytes 148
  0.6 42.2 %copy-start.17 = (s32[1,1,12]{2,1,0:T(1,128)S(1)}, s32[1,1,12]{2,1,0:T(1,128)}, u32[]{:S(2)}) copy-start(s32[1,1,12]{2,1,0:T(1,128)} %param.10) | copy-start | bytes 148
  0.7 42.3 %copy-start = (bf16[1,1,12,256,256]{4,3,2,1,0:T(8,128)(2,1)S(1)}, bf16[1,1,12,256,256]{4,3,2,1,0:T(8,128)(2,1)}, u32[]{:S(2)}) copy-start(bf16[1,1,12,256,256]{4,3,2,1,0:T(8,128)(2,1)} %param.8) | copy-start | bytes 4718596
  3.1 6.7 %collective-permute-start = (bf16[272,128]{1,0:T(8,128)(2,1)S(1)}, bf16[272,128]{1,0:T(8,128)(2,1)S(1)}, u32[]{:S(2)}, u32[]{:S(2)}) collective-permute-start(bf16[272,128]{1,0:T(8,128)(2,1)S(1)} %pad_maximum_fusion.13), channel_id=1, source_target_pairs={{0,8},{8,0},{16,24},{24,16},{32,40},{40,32},{48,56},{56,48},{64,72... | collective-permute-start | bytes 208904 | tf_op jit(solution)/shard_map/ppermute | solution.py:30
  6.4 5.3 %collective-permute-start.3 = (bf16[256,128]{1,0:T(8,128)(2,1)S(1)}, bf16[256,128]{1,0:T(8,128)(2,1)S(1)}, u32[]{:S(2)}, u32[]{:S(2)}) collective-permute-start(bf16[256,128]{1,0:T(8,128)(2,1)S(1)} %get-tuple-element.28), channel_id=1, source_target_pairs={{0,24},{8,16},{16,8},{24,0},{32,56},{40,48},{48,40},{56,32},{64,88... | collective-permute-start | bytes 196616 | tf_op jit(solution)/shard_map/ppermute | solution.py:30
  7.4 35.5 %collective-permute-start.1 = (bf16[12,256,256]{2,1,0:T(8,128)(2,1)}, bf16[12,256,256]{2,1,0:T(8,128)(2,1)S(1)}, u32[]{:S(2)}, u32[]{:S(2)}) collective-permute-start(bf16[12,256,256]{2,1,0:T(8,128)(2,1)} %bitcast.77), channel_id=1, source_target_pairs={{0,8},{8,0},{16,24},{24,16},{32,40},{40,32},{48,56},{56,48},{64,72... | collective-permute-start | bytes 4718600 | tf_op jit(solution)/shard_map/ppermute | solution.py:30
  7.9 5.2 %collective-permute-start.2 = (bf16[256,128]{1,0:T(8,128)(2,1)S(1)}, bf16[256,128]{1,0:T(8,128)(2,1)S(1)}, u32[]{:S(2)}, u32[]{:S(2)}) collective-permute-start(bf16[256,128]{1,0:T(8,128)(2,1)S(1)} %get-tuple-element.27), channel_id=1, source_target_pairs={{0,16},{8,24},{16,0},{24,8},{32,48},{40,56},{48,32},{56,40},{64,80... | collective-permute-start | bytes 196616 | tf_op jit(solution)/shard_map/ppermute | solution.py:30
  13.1 10.4 %collective-permute-start.4 = (bf16[4,256,128]{2,1,0:T(8,128)(2,1)S(1)}, bf16[4,256,128]{2,1,0:T(8,128)(2,1)S(1)}, u32[]{:S(2)}, u32[]{:S(2)}) collective-permute-start(bf16[4,256,128]{2,1,0:T(8,128)(2,1)S(1)} %pad_maximum_fusion.7.refs_0_), channel_id=1, source_target_pairs={{0,224},{8,232},{16,240},{24,248},{32,0},{40,8},{48,16},{56,24},{6... | collective-permute-start | bytes 786440 | tf_op jit(solution)/shard_map/ppermute | solution.py:34
  18.7 8.9 %collective-permute-start.7 = (bf16[4,256,128]{2,1,0:T(8,128)(2,1)S(1)}, bf16[4,256,128]{2,1,0:T(8,128)(2,1)S(1)}, u32[]{:S(2)}, u32[]{:S(2)}) collective-permute-start(bf16[4,256,128]{2,1,0:T(8,128)(2,1)S(1)} %pad_maximum_fusion.7.refs_0_), channel_id=1, source_target_pairs={{0,32},{8,40},{16,48},{24,56},{32,64},{40,72},{48,80},{56,88},{64,... | collective-permute-start | bytes 786440 | tf_op jit(solution)/shard_map/ppermute | solution.py:34
  23.5 7.2 %collective-permute-start.5 = (bf16[4,256,128]{2,1,0:T(8,128)(2,1)S(1)}, bf16[4,256,128]{2,1,0:T(8,128)(2,1)S(1)}, u32[]{:S(2)}, u32[]{:S(2)}) collective-permute-start(bf16[4,256,128]{2,1,0:T(8,128)(2,1)S(1)} %collective-permute-done.4.refs_1_), channel_id=1, source_target_pairs={{0,224},{8,232},{16,240},{24,248},{32,0},{40,8},{48,16},{56,24},{6... | collective-permute-start | bytes 786440 | tf_op jit(solution)/shard_map/ppermute | solution.py:34
  27.6 7.3 %collective-permute-start.8 = (bf16[4,256,128]{2,1,0:T(8,128)(2,1)S(1)}, bf16[4,256,128]{2,1,0:T(8,128)(2,1)S(1)}, u32[]{:S(2)}, u32[]{:S(2)}) collective-permute-start(bf16[4,256,128]{2,1,0:T(8,128)(2,1)S(1)} %collective-permute-done.7.refs_6_), channel_id=1, source_target_pairs={{0,32},{8,40},{16,48},{24,56},{32,64},{40,72},{48,80},{56,88},{64,... | collective-permute-start | bytes 786440 | tf_op jit(solution)/shard_map/ppermute | solution.py:34
  30.7 6.7 %collective-permute-start.6 = (bf16[4,256,128]{2,1,0:T(8,128)(2,1)S(1)}, bf16[4,256,128]{2,1,0:T(8,128)(2,1)S(1)}, u32[]{:S(2)}, u32[]{:S(2)}) collective-permute-start(bf16[4,256,128]{2,1,0:T(8,128)(2,1)S(1)} %collective-permute-done.5.refs_2_), channel_id=1, source_target_pairs={{0,224},{8,232},{16,240},{24,248},{32,0},{40,8},{48,16},{56,24},{6... | collective-permute-start | bytes 786440 | tf_op jit(solution)/shard_map/ppermute | solution.py:34
  34.9 6.4 %collective-permute-start.9 = (bf16[4,256,128]{2,1,0:T(8,128)(2,1)S(1)}, bf16[4,256,128]{2,1,0:T(8,128)(2,1)S(1)}, u32[]{:S(2)}, u32[]{:S(2)}) collective-permute-start(bf16[4,256,128]{2,1,0:T(8,128)(2,1)S(1)} %collective-permute-done.8.refs_5_), channel_id=1, source_target_pairs={{0,32},{8,40},{16,48},{24,56},{32,64},{40,72},{48,80},{56,88},{64,... | collective-permute-start | bytes 786440 | tf_op jit(solution)/shard_map/ppermute | solution.py:34
  42.8 10.0 %collective-permute-start.10 = (bf16[4,256,128]{2,1,0:T(8,128)(2,1)}, bf16[4,256,128]{2,1,0:T(8,128)(2,1)}, u32[]{:S(2)}, u32[]{:S(2)}) collective-permute-start(bf16[4,256,128]{2,1,0:T(8,128)(2,1)} %broadcast_select_fusion), channel_id=1, source_target_pairs={{0,32},{8,232},{16,48},{24,248},{32,64},{40,8},{48,80},{56,24},{64... | collective-permute-start | bytes 786440 | tf_op jit(solution)/shard_map/ppermute | solution.py:256
  42.9 1.0 copy-start.3
  54.6 21.1 %copy-start.15 = (bf16[256,256]{1,0:T(8,128)(2,1)S(1)}, bf16[256,256]{1,0:T(8,128)(2,1)}, u32[]{:S(2)}) copy-start(bf16[256,256]{1,0:T(8,128)(2,1)} %cot_own.1) | copy-start | bytes 393220
  54.6 22.5 %copy-start.14 = (bf16[256,256]{1,0:T(8,128)(2,1)S(1)}, bf16[256,256]{1,0:T(8,128)(2,1)}, u32[]{:S(2)}) copy-start(bf16[256,256]{1,0:T(8,128)(2,1)} %weight.1) | copy-start | bytes 393220
  69.7 7.4 %collective-permute-start.11 = (f32[512,128]{1,0:T(8,128)S(1)}, f32[512,128]{1,0:T(8,128)S(1)}, u32[]{:S(2)}, u32[]{:S(2)}) collective-permute-start(f32[512,128]{1,0:T(8,128)S(1)} %bitcast.82), channel_id=1, source_target_pairs={{0,8},{8,0},{16,24},{24,16},{32,40},{40,32},{48,56},{56,48},{64,72... | collective-permute-start | bytes 786440 | tf_op jit(solution)/shard_map/ppermute | solution.py:30
  75.7 1.3 collective-permute-start.12
  80.7 1.1 copy-start.1
  81.8 22.1 %all-to-all-start.1 = ((bf16[8,640,128]{2,1,0:T(8,128)(2,1)}), bf16[8,640,128]{2,1,0:T(8,128)(2,1)}, u32[]{:S(2)}, u32[]{:S(2)}) async-start(bf16[8,640,128]{2,1,0:T(8,128)(2,1)} %copy-done.1), calls=%async_computation.1 | async-start | bytes 2621440 | tf_op jit(solution)/shard_map/all_to_all | solution.py:295
  106.9 8.2 %collective-permute-start.13 = (bf16[1152,128]{1,0:T(8,128)(2,1)S(1)}, bf16[1152,128]{1,0:T(8,128)(2,1)S(1)}, u32[]{:S(2)}, u32[]{:S(2)}) collective-permute-start(bf16[1152,128]{1,0:T(8,128)(2,1)S(1)} %pad_maximum_fusion), channel_id=1, source_target_pairs={{0,32},{8,232},{16,48},{24,248},{32,64},{40,8},{48,80},{56,24},{64... | collective-permute-start | bytes 884744 | tf_op jit(solution)/shard_map/ppermute | solution.py:256
  115.3 7.8 %collective-permute-start.14 = (bf16[1152,128]{1,0:T(8,128)(2,1)S(1)}, bf16[1152,128]{1,0:T(8,128)(2,1)S(1)}, u32[]{:S(2)}, u32[]{:S(2)}) collective-permute-start(bf16[1152,128]{1,0:T(8,128)(2,1)S(1)} %pad_maximum_fusion.1), channel_id=1, source_target_pairs={{0,224},{8,232},{16,240},{24,248},{32,0},{40,8},{48,16},{56,24},{6... | collective-permute-start | bytes 884744 | tf_op jit(solution)/shard_map/ppermute | solution.py:34
  116.7 9.2 %collective-permute-start.17 = (bf16[1152,128]{1,0:T(8,128)(2,1)S(1)}, bf16[1152,128]{1,0:T(8,128)(2,1)S(1)}, u32[]{:S(2)}, u32[]{:S(2)}) collective-permute-start(bf16[1152,128]{1,0:T(8,128)(2,1)S(1)} %pad_maximum_fusion.4), channel_id=1, source_target_pairs={{0,32},{8,40},{16,48},{24,56},{32,64},{40,72},{48,80},{56,88},{64,... | collective-permute-start | bytes 884744 | tf_op jit(solution)/shard_map/ppermute | solution.py:34
  123.2 7.5 %collective-permute-start.15 = (bf16[1152,128]{1,0:T(8,128)(2,1)S(1)}, bf16[1152,128]{1,0:T(8,128)(2,1)S(1)}, u32[]{:S(2)}, u32[]{:S(2)}) collective-permute-start(bf16[1152,128]{1,0:T(8,128)(2,1)S(1)} %pad_maximum_fusion.2), channel_id=1, source_target_pairs={{0,224},{8,232},{16,240},{24,248},{32,0},{40,8},{48,16},{56,24},{6... | collective-permute-start | bytes 884744 | tf_op jit(solution)/shard_map/ppermute | solution.py:34
  126.1 8.2 %collective-permute-start.18 = (bf16[1152,128]{1,0:T(8,128)(2,1)S(1)}, bf16[1152,128]{1,0:T(8,128)(2,1)S(1)}, u32[]{:S(2)}, u32[]{:S(2)}) collective-permute-start(bf16[1152,128]{1,0:T(8,128)(2,1)S(1)} %pad_maximum_fusion.5), channel_id=1, source_target_pairs={{0,32},{8,40},{16,48},{24,56},{32,64},{40,72},{48,80},{56,88},{64,... | collective-permute-start | bytes 884744 | tf_op jit(solution)/shard_map/ppermute | solution.py:34
  130.8 7.2 %collective-permute-start.16 = (bf16[1152,128]{1,0:T(8,128)(2,1)S(1)}, bf16[1152,128]{1,0:T(8,128)(2,1)S(1)}, u32[]{:S(2)}, u32[]{:S(2)}) collective-permute-start(bf16[1152,128]{1,0:T(8,128)(2,1)S(1)} %pad_maximum_fusion.3), channel_id=1, source_target_pairs={{0,224},{8,232},{16,240},{24,248},{32,0},{40,8},{48,16},{56,24},{6... | collective-permute-start | bytes 884744 | tf_op jit(solution)/shard_map/ppermute | solution.py:34
  134.4 6.9 %collective-permute-start.19 = (bf16[1152,128]{1,0:T(8,128)(2,1)S(1)}, bf16[1152,128]{1,0:T(8,128)(2,1)S(1)}, u32[]{:S(2)}, u32[]{:S(2)}) collective-permute-start(bf16[1152,128]{1,0:T(8,128)(2,1)S(1)} %pad_maximum_fusion.6), channel_id=1, source_target_pairs={{0,32},{8,40},{16,48},{24,56},{32,64},{40,72},{48,80},{56,88},{64,... | collective-permute-start | bytes 884744 | tf_op jit(solution)/shard_map/ppermute | solution.py:34
  142.3 7.2 %collective-permute-start.20 = (bf16[384,128]{1,0:T(8,128)(2,1)S(1)}, bf16[384,128]{1,0:T(8,128)(2,1)S(1)}, u32[]{:S(2)}, u32[]{:S(2)}) collective-permute-start(bf16[384,128]{1,0:T(8,128)(2,1)S(1)} %get-tuple-element.29), channel_id=1, source_target_pairs={{0,16},{8,24},{16,0},{24,8},{32,48},{40,56},{48,32},{56,40},{64,80... | collective-permute-start | bytes 294920 | tf_op jit(solution)/shard_map/ppermute | solution.py:30
  143.5 10.6 %collective-permute-start.22 = (bf16[384,128]{1,0:T(8,128)(2,1)S(1)}, bf16[384,128]{1,0:T(8,128)(2,1)S(1)}, u32[]{:S(2)}, u32[]{:S(2)}) collective-permute-start(bf16[384,128]{1,0:T(8,128)(2,1)S(1)} %get-tuple-element.31), channel_id=1, source_target_pairs={{0,24},{8,16},{16,8},{24,0},{32,56},{40,48},{48,40},{56,32},{64,88... | collective-permute-start | bytes 294920 | tf_op jit(solution)/shard_map/ppermute | solution.py:30
  149.4 4.7 %collective-permute-start.21 = (bf16[384,128]{1,0:T(8,128)(2,1)S(1)}, bf16[384,128]{1,0:T(8,128)(2,1)S(1)}, u32[]{:S(2)}, u32[]{:S(2)}) collective-permute-start(bf16[384,128]{1,0:T(8,128)(2,1)S(1)} %get-tuple-element.30), channel_id=1, source_target_pairs={{0,8},{8,0},{16,24},{24,16},{32,40},{40,32},{48,56},{56,48},{64,72... | collective-permute-start | bytes 294920 | tf_op jit(solution)/shard_map/ppermute | solution.py:30
  154.1 4.8 %collective-permute-start.23 = (f32[2,128,128]{2,1,0:T(8,128)S(1)}, f32[2,128,128]{2,1,0:T(8,128)S(1)}, u32[]{:S(2)}, u32[]{:S(2)}) collective-permute-start(f32[2,128,128]{2,1,0:T(8,128)S(1)} %pad_maximum_fusion.11), channel_id=1, source_target_pairs={{0,4},{1,5},{2,6},{3,7},{4,0},{5,1},{6,2},{7,3},{8,12},{9,13},{10,... | collective-permute-start | bytes 393224 | tf_op jit(solution)/shard_map/ppermute | solution.py:337
  (11 other events, 9.1 us)

commit v4 on v3

v4 whole, which is shorter than its diff:
```python
import functools
import math

import jax
import jax.numpy as jnp
from jax import lax
from jax.experimental import pallas as pl
from jax.experimental.pallas import tpu as pltpu
from jax.sharding import PartitionSpec as P

NZ = 8
QUAD = 4
NCOL = 8
TILE = 256
HALF = 128
SLOTS = 12
W_ROWS = 128
UNROLL = 4


def row_pairs(move):
    pairs = []
    for r in range(NZ * QUAD):
        z, q = move(r // QUAD, r % QUAD)
        pairs.append((r, (z % NZ) * QUAD + q))
    return pairs


def quad_permute(x, flip):
    return lax.ppermute(x, "row", row_pairs(lambda z, q: (z, q ^ flip)))


def z_shift(x, step):
    return lax.ppermute(x, "row", row_pairs(lambda z, q: (z + step, q)))


def prepare_kernel(rows, cols, count, block, mine, message):
    core = lax.axis_index("row") & 1

    @pl.when(core == 0)
    def _():
        mine[...] = block[:, :HALF]
        message[:TILE, :] = block[:, HALF:]

    @pl.when(core == 1)
    def _():
        mine[...] = block[:, HALF:]
        message[:TILE, :] = block[:, :HALF]

    lane = lax.broadcasted_iota(jnp.int32, (16, HALF), 1)
    values = jnp.zeros((16, HALF), jnp.float32)
    listed = [rows[s] for s in range(SLOTS)] + [cols[s] for s in range(SLOTS)] + [count[0]]
    for n, value in enumerate(listed):
        values = jnp.where(lane == n, value.astype(jnp.float32), values)
    message[TILE:, :] = values.astype(jnp.bfloat16)


def list_slots(lists, adj_refs, adj_vmem, adj_sem, rows, places, far, dummy):
    own_rows, own_cols, own_count, partner = lists
    device = lax.axis_index("row")
    z, q = device >> 2, device & 3
    n = jnp.int32(0)
    for i in range(2):
        count = partner[24] if i else own_count[0]
        for s in range(SLOTS):
            tile = partner[12 + s] if i else own_cols[s]
            row = partner[s] if i else own_rows[s]
            place = (((tile >> 2) - z) & 7) * QUAD + ((tile & 3) ^ q)
            live = (s < count) & (((place >> 2) == 4) == far)
            rows[n] = row * 2 + i
            places[n] = place

            @pl.when(live)
            def _(i=i, s=s, n=n):
                pltpu.make_async_copy(
                    adj_refs[i].at[s], adj_vmem.at[n], adj_sem.at[n]
                ).start()

            n = n + live.astype(jnp.int32)
    for u in range(UNROLL - 1):
        rows[n + u], places[n + u] = dummy
    return n


def slot_products(n, adj_ref, adj_vmem, adj_sem, product, add_to):
    @pl.loop(0, (n + UNROLL - 1) >> 2)
    def _(step):
        slots = [step * UNROLL + u for u in range(UNROLL)]
        for j in slots:

            @pl.when(j < n)
            def _(j=j):
                pltpu.make_async_copy(adj_ref.at[0], adj_vmem.at[j], adj_sem.at[j]).wait()

        values = [product(j) for j in slots]
        for j, value in zip(slots, values):
            add_to(j, value)


def forward_near_kernel(*refs):
    lists, (adj0, adj1), refs = refs[:4], refs[4:6], refs[6:]
    pieces, (acc, panel, adj_vmem, rows, places, panel_sem, adj_sem) = refs[:7], refs[7:]
    copies = [
        pltpu.make_async_copy(piece, panel.at[pl.ds(place * QUAD, QUAD)], panel_sem.at[place])
        for place, piece in zip((0, 1, 2, 3, 5, 6, 7), pieces)
    ]
    for copy in copies:
        copy.start()
    n = list_slots(lists, (adj0, adj1), adj_vmem, adj_sem, rows, places, False, (16, 0))
    acc[...] = jnp.zeros_like(acc)
    for copy in copies:
        copy.wait()

    def product(j):
        return jnp.dot(adj_vmem[j], panel[places[j]], preferred_element_type=jnp.float32)

    def add_to(j, value):
        acc[rows[j]] += value

    slot_products(n, adj0, adj_vmem, adj_sem, product, add_to)


def forward_far_kernel(*refs):
    lists, refs = refs[:4], refs[4:]
    adj0, adj1, near, far, out, acc, adj_vmem, rows, places, adj_sem = refs
    n = list_slots(lists, (adj0, adj1), adj_vmem, adj_sem, rows, places, True, (16, 16))
    acc[...] = near[...]

    def product(j):
        return jnp.dot(adj_vmem[j], far[places[j] - 16], preferred_element_type=jnp.float32)

    def add_to(j, value):
        acc[rows[j]] += value

    slot_products(n, adj0, adj_vmem, adj_sem, product, add_to)
    for row in range(8):
        for i in range(2):
            out[row, i] = acc[2 * row + i].astype(jnp.bfloat16)


def backward_kernel(far, *refs):
    lists, refs = refs[:4], refs[4:]
    adj0, adj1, back, out, acc, adj_vmem, rows, places, adj_sem = refs
    base = 16 if far else 0
    spare = acc.shape[0] - 1
    n = list_slots(
        lists, (adj0, adj1), adj_vmem, adj_sem, rows, places, far, (0, base + spare)
    )
    acc[...] = jnp.zeros_like(acc)

    def product(j):
        row = rows[j]
        return lax.dot_general(
            adj_vmem[j],
            back[row >> 1, pl.ds((row & 1) * TILE, TILE), :],
            (((0,), (0,)), ((), ())),
            preferred_element_type=jnp.float32,
        )

    def add_to(j, value):
        acc[places[j] - base] += value

    slot_products(n, adj0, adj_vmem, adj_sem, product, add_to)
    if not far:
        out[...] = acc[:spare].astype(jnp.bfloat16)
        return
    for k in range(QUAD):
        out[k * TILE : (k + 1) * TILE, :] = acc[k].astype(jnp.bfloat16)
    piece = back[0, 2 * TILE :, :].astype(jnp.float32)
    for c in range(1, NCOL):
        piece = piece + back[c, 2 * TILE :, :].astype(jnp.float32)
    out[QUAD * TILE :, :] = piece.astype(jnp.bfloat16)


def split(x):
    high = x.astype(jnp.bfloat16)
    return high, (x - high.astype(jnp.float32)).astype(jnp.bfloat16)


def dense_kernel(agg_own, agg_other, weight, cot_own, cot_other, act_out, send_out):
    first = (lax.axis_index("row") & 1) == 0
    own = agg_own[...]
    other = jnp.concatenate([agg_other[TILE:, :], agg_other[:TILE, :]], axis=0)
    w = weight[...]
    w_other_half = jnp.where(first, w[HALF:], w[:HALF])
    w_half = jnp.where(first, w[:HALF], w[HALF:])

    def dot(a, b, dims=((1,), (0,))):
        return lax.dot_general(a, b, (dims, ((), ())), preferred_element_type=jnp.float32)

    own_hi, own_lo = split(own)
    other_hi, other_lo = split(other)
    v = (dot(own_hi, w_half) + dot(own_lo, w_half)) + (
        dot(other_hi, w_other_half) + dot(other_lo, w_other_half)
    )
    scale = math.sqrt(2.0 / math.pi)
    square = v * v
    t = jnp.tanh(scale * (v + 0.044715 * (square * v)))
    cdf = 0.5 * (1.0 + t)
    act_out[...] = (v[:TILE] * cdf[:TILE]).astype(jnp.bfloat16)
    slope = cdf + 0.5 * v * ((1.0 - t) * (1.0 + t)) * (scale * (1.0 + 3.0 * 0.044715 * square))
    cot = jnp.concatenate([cot_own[...], cot_other[...]], axis=0).astype(jnp.float32)
    grad_hi, grad_lo = split(cot * slope)
    nodes = ((1,), (1,))
    back = (dot(grad_hi, w_half, nodes) + dot(grad_lo, w_half, nodes)).astype(jnp.bfloat16)
    rows = ((0,), (0,))
    w_part = (
        dot(own_hi, grad_hi, rows) + dot(own_lo, grad_hi, rows) + dot(own_hi, grad_lo, rows)
    ).astype(jnp.bfloat16)
    for c in range(NCOL):
        send_out[c, : 2 * TILE, :] = back
        piece = w_part[64 * (c // 4) : 64 * (c // 4) + 64]
        send_out[c, 2 * TILE : 2 * TILE + 64, :] = piece[:, :HALF]
        send_out[c, 2 * TILE + 64 :, :] = piece[:, HALF:]


def sum_kernel(parts, own, got1, up2, up3, up4, down2, down3, down4, kept, *refs):
    messages, by_step = refs[:3], refs[3]
    device = lax.axis_index("row")
    z, core = device >> 2, device & 1
    size = QUAD * TILE
    by_step[0] = own[size:, :]

    @pl.when(core == 0)
    def _():
        for k, ref in enumerate((down2, down3, down4, up4, up3, up2, got1)):
            by_step[k + 1] = ref[size:, :]

    @pl.when(core == 1)
    def _():
        for k, ref in enumerate((got1, down2, down3, down4, up4, up3, up2)):
            by_step[k + 1] = ref[size:, :]

    w_sum = by_step[(0 - z) & 7].astype(jnp.float32)
    for a in range(1, NZ):
        w_sum = w_sum + by_step[(a - z) & 7].astype(jnp.float32)
    w_send = w_sum.astype(jnp.bfloat16)
    for k in range(QUAD):
        rows = pl.ds(k * TILE, TILE)
        total = (
            parts[k].astype(jnp.float32)
            + up4[rows, :].astype(jnp.float32)
            + down4[rows, :].astype(jnp.float32)
        )
        if k == 0:
            kept[...] = total
        else:
            messages[k - 1][:TILE, :] = total.astype(jnp.bfloat16)
            messages[k - 1][TILE:, :] = w_send


def last_kernel(kept, sent, from_core, from_x, from_both, grad_out, w_out):
    core = lax.axis_index("row") & 1

    def f32(ref, rows):
        return ref[rows, :].astype(jnp.float32)

    grads, pieces = pl.ds(0, TILE), pl.ds(TILE, W_ROWS)
    mine = (kept[...] + f32(from_x, grads)).astype(jnp.bfloat16)
    theirs = (f32(from_core, grads) + f32(from_both, grads)).astype(jnp.bfloat16)
    w_mine = f32(sent, pieces) + f32(from_x, pieces)
    w_theirs = f32(from_core, pieces) + f32(from_both, pieces)

    @pl.when(core == 0)
    def _():
        grad_out[:, :HALF] = mine
        grad_out[:, HALF:] = theirs

    @pl.when(core == 1)
    def _():
        grad_out[:, HALF:] = mine
        grad_out[:, :HALF] = theirs

    w_out[core] = w_mine
    w_out[1 - core] = w_theirs


def weight_kernel(here, there, out):
    x = lax.axis_index("col") >> 2
    scale = 1.0 / 256.0

    def place(ref, x_lo):
        for core in range(2):
            rows = pl.ds(core * HALF + x_lo * 64, 64)
            out[rows, :HALF] = ref[core, :64, :] * scale
            out[rows, HALF:] = ref[core, 64:, :] * scale

    @pl.when(x == 0)
    def _():
        place(here, 0)
        place(there, 1)

    @pl.when(x == 1)
    def _():
        place(there, 0)
        place(here, 1)


SMEM = pl.BlockSpec(memory_space=pltpu.SMEM)
VMEM = pl.BlockSpec(memory_space=pltpu.VMEM)
ANY = pl.BlockSpec(memory_space=pl.ANY)


def params(mib):
    return pltpu.CompilerParams(vmem_limit_bytes=mib << 20)


LIST = 2 * SLOTS + UNROLL
SLOT_SCRATCH = [
    pltpu.VMEM((LIST, TILE, TILE), jnp.bfloat16),
    pltpu.SMEM((LIST,), jnp.int32),
    pltpu.SMEM((LIST,), jnp.int32),
]


def cost(slots, size):
    return pl.CostEstimate(
        flops=slots * 2 * TILE * TILE * HALF, bytes_accessed=size << 20, transcendentals=0
    )


LISTS = [SMEM] * 4


def local(kernel, out_shape, n_in, mib=20, scratch=(), name=None, scalars=0, any_in=0, cost=None):
    n_out = len(out_shape) if isinstance(out_shape, tuple) else None
    return pl.pallas_call(
        kernel,
        out_shape=out_shape,
        in_specs=[SMEM] * scalars + [ANY] * any_in + [VMEM] * (n_in - scalars - any_in),
        out_specs=(VMEM,) * n_out if n_out else VMEM,
        scratch_shapes=scratch,
        compiler_params=params(mib),
        cost_estimate=cost,
        name=name,
    )


def shape(*dims, dtype=jnp.bfloat16):
    return jax.ShapeDtypeStruct(dims, dtype)


def prepare(rows, cols, count, block):
    return local(
        prepare_kernel,
        (shape(TILE, HALF), shape(TILE + 16, HALF)),
        4,
        scalars=3,
        name="prepare",
    )(rows, cols, count, block)


def forward_near(lists, adj0, adj1, pieces):
    return local(
        forward_near_kernel,
        shape(17, TILE, HALF, dtype=jnp.float32),
        13,
        scalars=4,
        any_in=9,
        scratch=[pltpu.VMEM((NZ * QUAD, TILE, HALF), jnp.bfloat16)]
        + SLOT_SCRATCH
        + [pltpu.SemaphoreType.DMA((NZ,)), pltpu.SemaphoreType.DMA((LIST,))],
        cost=cost(21, 6),
        name="forward_near",
    )(*lists, adj0, adj1, *pieces)


def forward_far(lists, adj0, adj1, near, far):
    return local(
        forward_far_kernel,
        shape(8, 2, TILE, HALF),
        8,
        scalars=4,
        any_in=2,
        scratch=[pltpu.VMEM((17, TILE, HALF), jnp.float32)]
        + SLOT_SCRATCH
        + [pltpu.SemaphoreType.DMA((LIST,))],
        cost=cost(3, 4),
        name="forward_far",
    )(*lists, adj0, adj1, near, far)


def backward_tiles(lists, adj0, adj1, back, far):
    places = QUAD if far else NZ * QUAD
    return local(
        functools.partial(backward_kernel, far),
        shape(QUAD * TILE + W_ROWS, HALF) if far else shape(places, TILE, HALF),
        7,
        scalars=4,
        any_in=2,
        scratch=[pltpu.VMEM((places + 1, TILE, HALF), jnp.float32)]
        + SLOT_SCRATCH
        + [pltpu.SemaphoreType.DMA((LIST,))],
        cost=cost(3, 2) if far else cost(21, 6),
        name="backward_far" if far else "backward_near",
    )(*lists, adj0, adj1, back)


def dense(agg_own, agg_other, weight, cot_own, cot_other):
    return local(
        dense_kernel,
        (shape(TILE, 2 * HALF), shape(NCOL, 2 * TILE + W_ROWS, HALF)),
        5,
        name="dense",
    )(agg_own, agg_other, weight, cot_own, cot_other)


def ring_end(parts, messages):
    message = shape(TILE + W_ROWS, HALF)
    return local(
        sum_kernel,
        (shape(TILE, HALF, dtype=jnp.float32), message, message, message),
        9,
        scratch=[pltpu.VMEM((NZ, W_ROWS, HALF), jnp.bfloat16)],
        name="ring_end",
    )(parts, *messages)


def last(kept, sent, from_core, from_x, from_both):
    return local(
        last_kernel,
        (shape(TILE, 2 * HALF), shape(2, W_ROWS, HALF, dtype=jnp.float32)),
        5,
        name="last",
    )(kept, sent, from_core, from_x, from_both)


def weight_places(here, there):
    return local(
        weight_kernel, shape(2 * HALF, 2 * HALF, dtype=jnp.float32), 2, name="weight_places"
    )(here, there)


def z_both(x):
    return lax.ppermute(
        x, "row", row_pairs(lambda z, q: (z + 1 - 2 * (q & 1), q))
    )


def add(a, b):
    return (a.astype(jnp.float32) + b.astype(jnp.float32)).astype(jnp.bfloat16)


def per_device(features, adj_tiles, tile_row, tile_col, tile_count, weight, cotangent):
    first = (lax.axis_index("row") & 1) == 0
    adj0 = adj_tiles[0, 0]
    own_lists = (tile_row[0, 0], tile_col[0, 0], tile_count[0])

    mine, theirs = prepare(*own_lists, features[0])
    from_core = quad_permute(theirs, 1)
    from_both = quad_permute(theirs, 3)
    chunk = jnp.stack([mine, from_core[:TILE], quad_permute(mine, 2), from_both[:TILE]])
    lists = own_lists + (from_core[TILE, :25].astype(jnp.int32),)
    adj1 = quad_permute(adj0, 1)
    cot1 = quad_permute(cotangent, 1)

    up1, down1 = z_shift(chunk, 1), z_shift(chunk, -1)
    up2, down2 = z_shift(up1, 1), z_shift(down1, -1)
    up3, down3 = z_shift(up2, 1), z_shift(down2, -1)
    far = z_both(jnp.where(first, up3, down3))
    near = forward_near(lists, adj0, adj1, [chunk, down1, down2, down3, up3, up2, up1])
    partial = forward_far(lists, adj0, adj1, near, far)

    shares = lax.all_to_all(partial, "col", 0, 0, tiled=True)
    agg = shares.reshape(NCOL, 2 * TILE, HALF).astype(jnp.float32).sum(axis=0)
    agg_other = quad_permute(agg, 1)
    activated, send = dense(agg, agg_other, weight, cotangent, cot1)
    received = lax.all_to_all(send, "col", 0, 0, tiled=True)

    size = QUAD * TILE
    far_part = backward_tiles(lists, adj0, adj1, received, True)
    blocks = backward_tiles(lists, adj0, adj1, received, False)
    parts = blocks.reshape(NZ, size, HALF)

    def pack(part, message, piece):
        return jnp.concatenate([add(part, message), piece], axis=0)

    w_piece = far_part[size:]
    got1 = z_both(far_part)
    zero = jnp.zeros((size, HALF), jnp.bfloat16)
    up = pack(
        parts[3], jnp.where(first, got1[:size], zero), jnp.where(first, got1[size:], w_piece)
    )
    down = pack(
        parts[5], jnp.where(first, zero, got1[:size]), jnp.where(first, w_piece, got1[size:])
    )
    up2, down2 = z_shift(up, 1), z_shift(down, -1)
    up3 = z_shift(pack(parts[2], up2[:size], up2[size:]), 1)
    down3 = z_shift(pack(parts[6], down2[:size], down2[size:]), -1)
    up4 = z_shift(pack(parts[1], up3[:size], up3[size:]), 1)
    down4 = z_shift(pack(parts[7], down3[:size], down3[size:]), -1)

    kept, to_core, to_x, to_both = ring_end(
        blocks, (far_part, got1, up2, up3, up4, down2, down3, down4)
    )
    grad, w_here = last(
        kept, to_core, quad_permute(to_core, 1), quad_permute(to_x, 2), quad_permute(to_both, 3)
    )
    w_there = lax.ppermute(w_here, "col", [(c, c ^ 4) for c in range(NCOL)])
    return (activated, weight_places(w_here, w_there), grad[None])


def solution(mesh):
    return jax.shard_map(
        per_device,
        mesh=mesh,
        in_specs=(
            P("col", "row", None),
            P("row", "col", None, None, None),
            P("row", "col", None),
            P("row", "col", None),
            P("row", "col"),
            P(),
            P(("row", "col"), None),
        ),
        out_specs=(P(("row", "col"), None), P(), P("col", "row", None)),
        check_vma=False,
    )
```

time: 161 us -> 150 us (0.932)
  blocking collectives: 14.9 us -> 35.6 us
  waiting for transfers between devices: 59.9 us -> 43.6 us
  local copies, waits for them, and re-layouts: 11.7 us -> 7 us
  other arithmetic: 6.29 us -> 1.84 us
  Pallas kernels: 16.8 us -> 13.1 us
    all_to_all x0 -> x1, blocking collectives: none -> 19.5 us  [per_device(): received = lax.all_to_all(send, 'col', 0, 0, tiled=True)]
    all_to_all x1 -> x0, waiting for transfers between devices: 17.8 us -> none  [per_device(): received = lax.all_to_all(send, 'col', 0, 0, tiled=True)]
    all_to_all x1 -> x0, starting transfers between devices: 4.28 us -> none  [per_device(): received = lax.all_to_all(send, 'col', 0, 0, tiled=True)]
    ppermute x9, starting transfers between devices: 20.2 us -> 24.3 us  [quad_permute(): return lax.ppermute(x, 'row', row_pairs(lambda z, q: (z, q ^ flip)))]
    pallas_call x5 -> x9, Pallas kernels: 16.8 us -> 13.1 us  [the longest x2 4.83 us: backward_tiles(): local(functools.partial(backward_kernel, far), shape(QUAD * TILE + W_ROWS...]
    unnamed x37 -> x28, local copies, waits for them, and re-layouts: 10.3 us -> 6.85 us
    ppermute x1, waiting for transfers between devices: 3 us -> 4.89 us  [per_device(): w_there = lax.ppermute(w_here, 'col', [(c, c ^ 4) for c in range(NCOL)])]
  transfers between devices with their start and end apart: 25 -> 24, of which waited for: 14 -> 15; matrix products, arithmetic and copies ran while one was open for 1% -> 1% of each run, Pallas kernels for 6% -> 5%
where the time goes in v4:
time: 150 us; the launch traced here: 151 us
  starting transfers between devices  47.6 us (32%)
  waiting for transfers between devices  43.6 us (29%)
  blocking collectives  35.6 us (24%)
  Pallas kernels  13.1 us (9%)
  local copies, waits for them, and re-layouts  7 us (5%)
  other arithmetic  1.84 us (1%)
  between operations  1.74 us (1%)
    ppermute x12, waiting for transfers between devices, z_shift(): return lax.ppermute(x, 'row', row_pairs(lambda z, q: (z + step, q)))  29.4 us
    ppermute x9, starting transfers between devices, quad_permute(): return lax.ppermute(x, 'row', row_pairs(lambda z, q: (z, q ^ flip)))  24.3 us
    ppermute x12, starting transfers between devices, z_shift(): return lax.ppermute(x, 'row', row_pairs(lambda z, q: (z + step, q)))  21.5 us
    all_to_all x1, blocking collectives, per_device(): received = lax.all_to_all(send, 'col', 0, 0, tiled=True)  19.5 us
    all_to_all x1, blocking collectives, per_device(): shares = lax.all_to_all(partial, 'col', 0, 0, tiled=True)  16.1 us
    ppermute x9, waiting for transfers between devices, quad_permute(): return lax.ppermute(x, 'row', row_pairs(lambda z, q: (z, q ^ flip)))  9.21 us
    unnamed x28, local copies, waits for them, and re-layouts  6.85 us
    ppermute x1, waiting for transfers between devices, per_device(): w_there = lax.ppermute(w_here, 'col', [(c, c ^ 4) for c in range(NCOL)])  4.89 us
  transfers between devices with their start and end apart: 24, of which 15 were waited for; matrix products, arithmetic and copies ran while one was open for 1% of the time, Pallas kernels for 5%

profile of v4, /device:TPU:1, one launch (start us, length us, event | category | flops | bytes accessed | tf_op | source)
XLA Modules:
  0.0 150.6 jit_solution(1320895262971706616)
XLA Ops:
  4.2 4.2 %collective-permute-start.3 = (bf16[272,128]{1,0:T(8,128)(2,1)S(1)}, bf16[272,128]{1,0:T(8,128)(2,1)S(1)}, u32[]{:S(2)}, u32[]{:S(2)}) collective-permute-start(bf16[272,128]{1,0:T(8,128)(2,1)S(1)} %get-tuple-element.13), channel_id=1, source_target_pairs={{0,24},{8,16},{16,8},{24,0},{32,56},{40,48},{48,40},{56,32},{64,88... | collective-permute-start | bytes 208904 | tf_op jit(solution)/shard_map/ppermute | solution.py:30
  9.0 2.0 %collective-permute-start.2 = (bf16[256,128]{1,0:T(8,128)(2,1)S(1)}, bf16[256,128]{1,0:T(8,128)(2,1)S(1)}, u32[]{:S(2)}, u32[]{:S(2)}) collective-permute-start(bf16[256,128]{1,0:T(8,128)(2,1)S(1)} %get-tuple-element.14), channel_id=1, source_target_pairs={{0,16},{8,24},{16,0},{24,8},{32,48},{40,56},{48,32},{56,40},{64,80... | collective-permute-start | bytes 196616 | tf_op jit(solution)/shard_map/ppermute | solution.py:30
  11.0 3.2 %collective-permute-done.2 = bf16[256,128]{1,0:T(8,128)(2,1)S(1)} collective-permute-done((bf16[256,128]{1,0:T(8,128)(2,1)S(1)}, bf16[256,128]{1,0:T(8,128)(2,1)S(1)}, u32[]{:S(2)}, u32[]{:S(2)}) %collective-permute-start.2) | collective-permute-done | bytes 65568 | tf_op jit(solution)/shard_map/ppermute | solution.py:30
  14.2 5.7 %collective-permute-start.4 = (bf16[4,256,128]{2,1,0:T(8,128)(2,1)S(1)}, bf16[4,256,128]{2,1,0:T(8,128)(2,1)S(1)}, u32[]{:S(2)}, u32[]{:S(2)}) collective-permute-start(bf16[4,256,128]{2,1,0:T(8,128)(2,1)S(1)} %pad_maximum_fusion.6.refs_6_), channel_id=1, source_target_pairs={{0,224},{8,232},{16,240},{24,248},{32,0},{40,8},{48,16},{56,24},{6... | collective-permute-start | bytes 786440 | tf_op jit(solution)/shard_map/ppermute | solution.py:34
  19.9 4.8 %collective-permute-done.4.refs_7_ = bf16[4,256,128]{2,1,0:T(8,128)(2,1)S(1)} collective-permute-done((bf16[4,256,128]{2,1,0:T(8,128)(2,1)S(1)}, bf16[4,256,128]{2,1,0:T(8,128)(2,1)S(1)}, u32[]{:S(2)}, u32[]{:S(2)}) %collective-permute-start.4) | collective-permute-done | bytes 262176 | tf_op jit(solution)/shard_map/ppermute | solution.py:34
  24.7 3.4 %collective-permute-start.5 = (bf16[4,256,128]{2,1,0:T(8,128)(2,1)S(1)}, bf16[4,256,128]{2,1,0:T(8,128)(2,1)}, u32[]{:S(2)}, u32[]{:S(2)}) collective-permute-start(bf16[4,256,128]{2,1,0:T(8,128)(2,1)S(1)} %collective-permute-done.4.refs_7_), channel_id=1, source_target_pairs={{0,224},{8,232},{16,240},{24,248},{32,0},{40,8},{48,16},{56,24},{6... | collective-permute-start | bytes 786440 | tf_op jit(solution)/shard_map/ppermute | solution.py:34
  29.6 2.5 %collective-permute-done.5.refs_8_ = bf16[4,256,128]{2,1,0:T(8,128)(2,1)} collective-permute-done((bf16[4,256,128]{2,1,0:T(8,128)(2,1)S(1)}, bf16[4,256,128]{2,1,0:T(8,128)(2,1)}, u32[]{:S(2)}, u32[]{:S(2)}) %collective-permute-start.5) | collective-permute-done | bytes 262176 | tf_op jit(solution)/shard_map/ppermute | solution.py:34
  32.1 3.5 %collective-permute-start.6 = (bf16[4,256,128]{2,1,0:T(8,128)(2,1)}, bf16[4,256,128]{2,1,0:T(8,128)(2,1)}, u32[]{:S(2)}, u32[]{:S(2)}) collective-permute-start(bf16[4,256,128]{2,1,0:T(8,128)(2,1)} %collective-permute-done.5.refs_8_), channel_id=1, source_target_pairs={{0,224},{8,232},{16,240},{24,248},{32,0},{40,8},{48,16},{56,24},{6... | collective-permute-start | bytes 786440 | tf_op jit(solution)/shard_map/ppermute | solution.py:34
  36.0 3.2 %collective-permute-done.6.refs_9_ = bf16[4,256,128]{2,1,0:T(8,128)(2,1)} collective-permute-done((bf16[4,256,128]{2,1,0:T(8,128)(2,1)}, bf16[4,256,128]{2,1,0:T(8,128)(2,1)}, u32[]{:S(2)}, u32[]{:S(2)}) %collective-permute-start.6) | collective-permute-done | bytes 262176 | tf_op jit(solution)/shard_map/ppermute | solution.py:34
  39.2 3.5 %collective-permute-done.9.refs_10_ = bf16[4,256,128]{2,1,0:T(8,128)(2,1)} collective-permute-done((bf16[4,256,128]{2,1,0:T(8,128)(2,1)}, bf16[4,256,128]{2,1,0:T(8,128)(2,1)}, u32[]{:S(2)}, u32[]{:S(2)}) %collective-permute-start.9) | collective-permute-done | bytes 262176 | tf_op jit(solution)/shard_map/ppermute | solution.py:34
  47.1 3.3 %forward_near.1.refs_6_ = f32[17,256,128]{2,1,0:T(8,128)S(1)} custom-call(s32[12]{0:T(128)S(1)} %bitcast.51, s32[12]{0:T(128)S(1)} %bitcast.56, s32[1]{0:T(128)} %bitcast.37.refs_2_, s32[25]{0:T(128)S(1)} %fusion.6.refs_3_, bf16[12,256,256]{2,1,0:T(8,128)(2,1)S(1)} %bitcast.42, bf16[12,256,256]{2,1,0:T(8,128)(2,1)S(1)} %collective-permute-done.1.refs_5_, ...), custom_call_target="tpu_custom_call" | custom-call | flops 352321536 | bytes 6291456 | tf_op jit(solution)/shard_map/forward_near/pallas_call | solution.py:354
  50.4 1.4 forward_far.1
  51.8 16.1 %all_to_all.10 = bf16[8,2,256,128]{3,2,1,0:T(8,128)(2,1)S(1)} all-to-all(bf16[8,2,256,128]{3,2,1,0:T(8,128)(2,1)S(1)} %forward_far.1), channel_id=1, replica_groups=mesh['row'=32,'col'=8] {'col'}, dimensions={0} | all-to-all | bytes 2097152 | tf_op jit(solution)/shard_map/all_to_all | solution.py:464
  68.1 6.3 %collective-permute-start.11 = (f32[512,128]{1,0:T(8,128)S(1)}, f32[512,128]{1,0:T(8,128)S(1)}, u32[]{:S(2)}, u32[]{:S(2)}) collective-permute-start(f32[512,128]{1,0:T(8,128)S(1)} %bitcast.46), channel_id=1, source_target_pairs={{0,8},{8,0},{16,24},{24,16},{32,40},{40,32},{48,56},{56,48},{64,72... | collective-permute-start | bytes 786440 | tf_op jit(solution)/shard_map/ppermute | solution.py:30
  75.8 1.4 dense.1
  77.2 19.5 %all_to_all.11.refs_6_ = bf16[8,640,128]{2,1,0:T(8,128)(2,1)S(1)} all-to-all(bf16[8,640,128]{2,1,0:T(8,128)(2,1)S(1)} %get-tuple-element.16), channel_id=1, replica_groups=mesh['row'=32,'col'=8] {'col'}, dimensions={0} | all-to-all | bytes 2621440 | tf_op jit(solution)/shard_map/all_to_all | solution.py:468
  96.7 1.2 backward_far.1.own
  98.0 1.8 %collective-permute-start.13 = (bf16[1152,128]{1,0:T(8,128)(2,1)S(1)}, bf16[1152,128]{1,0:T(8,128)(2,1)S(1)}, u32[]{:S(2)}, u32[]{:S(2)}) collective-permute-start(bf16[1152,128]{1,0:T(8,128)(2,1)S(1)} %backward_far.1.own), channel_id=1, source_target_pairs={{0,32},{8,232},{16,48},{24,248},{32,64},{40,8},{48,80},{56,24},{64... | collective-permute-start | bytes 884744 | tf_op jit(solution)/shard_map/ppermute | solution.py:435
  99.7 3.6 %backward_near.1.parts = bf16[32,256,128]{2,1,0:T(8,128)(2,1)S(1)} custom-call(s32[12]{0:T(128)S(1)} %bitcast.54, s32[12]{0:T(128)S(1)} %bitcast.59, s32[1]{0:T(128)} %bitcast.39.refs_2_, s32[25]{0:T(128)S(1)} %fusion.6.refs_3_, bf16[12,256,256]{2,1,0:T(8,128)(2,1)S(1)} %bitcast.45, bf16[12,256,256]{2,1,0:T(8,128)(2,1)S(1)} %collective-permute-done.1.refs_5_, ...), custom_call_target="tpu_custom_call" | custom-call | flops 352321536 | bytes 6291456 | tf_op jit(solution)/shard_map/backward_near/pallas_call | solution.py:385
  103.9 1.5 %collective-permute-start.14 = (bf16[1152,128]{1,0:T(8,128)(2,1)S(1)}, bf16[1152,128]{1,0:T(8,128)(2,1)S(1)}, u32[]{:S(2)}, u32[]{:S(2)}) collective-permute-start(bf16[1152,128]{1,0:T(8,128)(2,1)S(1)} %pad_maximum_fusion), channel_id=1, source_target_pairs={{0,32},{8,40},{16,48},{24,56},{32,64},{40,72},{48,80},{56,88},{64,... | collective-permute-start | bytes 884744 | tf_op jit(solution)/shard_map/ppermute | solution.py:34
  105.4 1.6 %collective-permute-start.17 = (bf16[1152,128]{1,0:T(8,128)(2,1)S(1)}, bf16[1152,128]{1,0:T(8,128)(2,1)S(1)}, u32[]{:S(2)}, u32[]{:S(2)}) collective-permute-start(bf16[1152,128]{1,0:T(8,128)(2,1)S(1)} %pad_maximum_fusion.3), channel_id=1, source_target_pairs={{0,224},{8,232},{16,240},{24,248},{32,0},{40,8},{48,16},{56,24},{6... | collective-permute-start | bytes 884744 | tf_op jit(solution)/shard_map/ppermute | solution.py:34
  107.0 4.0 %collective-permute-done.14.up2 = bf16[1152,128]{1,0:T(8,128)(2,1)S(1)} collective-permute-done((bf16[1152,128]{1,0:T(8,128)(2,1)S(1)}, bf16[1152,128]{1,0:T(8,128)(2,1)S(1)}, u32[]{:S(2)}, u32[]{:S(2)}) %collective-permute-start.14) | collective-permute-done | bytes 294944 | tf_op jit(solution)/shard_map/ppermute | solution.py:34
  111.3 2.7 %collective-permute-start.18 = (bf16[1152,128]{1,0:T(8,128)(2,1)S(1)}, bf16[1152,128]{1,0:T(8,128)(2,1)S(1)}, u32[]{:S(2)}, u32[]{:S(2)}) collective-permute-start(bf16[1152,128]{1,0:T(8,128)(2,1)S(1)} %pad_maximum_fusion.4), channel_id=1, source_target_pairs={{0,224},{8,232},{16,240},{24,248},{32,0},{40,8},{48,16},{56,24},{6... | collective-permute-start | bytes 884744 | tf_op jit(solution)/shard_map/ppermute | solution.py:34
  114.1 4.9 %collective-permute-done.15.up3 = bf16[1152,128]{1,0:T(8,128)(2,1)S(1)} collective-permute-done((bf16[1152,128]{1,0:T(8,128)(2,1)S(1)}, bf16[1152,128]{1,0:T(8,128)(2,1)S(1)}, u32[]{:S(2)}, u32[]{:S(2)}) %collective-permute-start.15) | collective-permute-done | bytes 294944 | tf_op jit(solution)/shard_map/ppermute | solution.py:34
  119.4 2.9 %collective-permute-start.19 = (bf16[1152,128]{1,0:T(8,128)(2,1)S(1)}, bf16[1152,128]{1,0:T(8,128)(2,1)S(1)}, u32[]{:S(2)}, u32[]{:S(2)}) collective-permute-start(bf16[1152,128]{1,0:T(8,128)(2,1)S(1)} %pad_maximum_fusion.5), channel_id=1, source_target_pairs={{0,224},{8,232},{16,240},{24,248},{32,0},{40,8},{48,16},{56,24},{6... | collective-permute-start | bytes 884744 | tf_op jit(solution)/shard_map/ppermute | solution.py:34
  122.2 5.8 %collective-permute-done.16.up4 = bf16[1152,128]{1,0:T(8,128)(2,1)S(1)} collective-permute-done((bf16[1152,128]{1,0:T(8,128)(2,1)S(1)}, bf16[1152,128]{1,0:T(8,128)(2,1)S(1)}, u32[]{:S(2)}, u32[]{:S(2)}) %collective-permute-start.16) | collective-permute-done | bytes 294944 | tf_op jit(solution)/shard_map/ppermute | solution.py:34
  128.4 7.8 %collective-permute-start.20 = (bf16[384,128]{1,0:T(8,128)(2,1)S(1)}, bf16[384,128]{1,0:T(8,128)(2,1)S(1)}, u32[]{:S(2)}, u32[]{:S(2)}) collective-permute-start(bf16[384,128]{1,0:T(8,128)(2,1)S(1)} %get-tuple-element.18.sent), channel_id=1, source_target_pairs={{0,8},{8,0},{16,24},{24,16},{32,40},{40,32},{48,56},{56,48},{64,72... | collective-permute-start | bytes 294920 | tf_op jit(solution)/shard_map/ppermute | solution.py:30
  136.1 1.2 collective-permute-start.21
  137.3 2.0 %collective-permute-start.22 = (bf16[384,128]{1,0:T(8,128)(2,1)S(1)}, bf16[384,128]{1,0:T(8,128)(2,1)S(1)}, u32[]{:S(2)}, u32[]{:S(2)}) collective-permute-start(bf16[384,128]{1,0:T(8,128)(2,1)S(1)} %get-tuple-element.20), channel_id=1, source_target_pairs={{0,24},{8,16},{16,8},{24,0},{32,56},{40,48},{48,40},{56,32},{64,88... | collective-permute-start | bytes 294920 | tf_op jit(solution)/shard_map/ppermute | solution.py:30
  139.4 2.6 %collective-permute-done.21.from_x = bf16[384,128]{1,0:T(8,128)(2,1)S(1)} collective-permute-done((bf16[384,128]{1,0:T(8,128)(2,1)S(1)}, bf16[384,128]{1,0:T(8,128)(2,1)S(1)}, u32[]{:S(2)}, u32[]{:S(2)}) %collective-permute-start.21) | collective-permute-done | bytes 98336 | tf_op jit(solution)/shard_map/ppermute | solution.py:30
  142.0 2.3 %collective-permute-done.22.from_both = bf16[384,128]{1,0:T(8,128)(2,1)S(1)} collective-permute-done((bf16[384,128]{1,0:T(8,128)(2,1)S(1)}, bf16[384,128]{1,0:T(8,128)(2,1)S(1)}, u32[]{:S(2)}, u32[]{:S(2)}) %collective-permute-start.22) | collective-permute-done | bytes 98336 | tf_op jit(solution)/shard_map/ppermute | solution.py:30
  145.0 4.9 %collective-permute-done.23.there = f32[2,128,128]{2,1,0:T(8,128)S(1)} collective-permute-done((f32[2,128,128]{2,1,0:T(8,128)S(1)}, f32[2,128,128]{2,1,0:T(8,128)S(1)}, u32[]{:S(2)}, u32[]{:S(2)}) %collective-permute-start.23) | collective-permute-done | bytes 131104 | tf_op jit(solution)/shard_map/ppermute | solution.py:499
  (78 shorter events, 13.8 us)
Async XLA Ops:
  0.6 43.2 %copy-start = (bf16[1,1,12,256,256]{4,3,2,1,0:T(8,128)(2,1)S(1)}, bf16[1,1,12,256,256]{4,3,2,1,0:T(8,128)(2,1)}, u32[]{:S(2)}) copy-start(bf16[1,1,12,256,256]{4,3,2,1,0:T(8,128)(2,1)} %param.8) | copy-start | bytes 4718596
  1.4 0.9 copy-start.7
  4.2 6.7 %collective-permute-start.3 = (bf16[272,128]{1,0:T(8,128)(2,1)S(1)}, bf16[272,128]{1,0:T(8,128)(2,1)S(1)}, u32[]{:S(2)}, u32[]{:S(2)}) collective-permute-start(bf16[272,128]{1,0:T(8,128)(2,1)S(1)} %get-tuple-element.13), channel_id=1, source_target_pairs={{0,24},{8,16},{16,8},{24,0},{32,56},{40,48},{48,40},{56,32},{64,88... | collective-permute-start | bytes 208904 | tf_op jit(solution)/shard_map/ppermute | solution.py:30
  8.5 2.5 %collective-permute-start = (bf16[272,128]{1,0:T(8,128)(2,1)S(1)}, bf16[272,128]{1,0:T(8,128)(2,1)S(1)}, u32[]{:S(2)}, u32[]{:S(2)}) collective-permute-start(bf16[272,128]{1,0:T(8,128)(2,1)S(1)} %get-tuple-element.13), channel_id=1, source_target_pairs={{0,8},{8,0},{16,24},{24,16},{32,40},{40,32},{48,56},{56,48},{64,72... | collective-permute-start | bytes 208904 | tf_op jit(solution)/shard_map/ppermute | solution.py:30
  8.5 35.4 %collective-permute-start.1 = (bf16[12,256,256]{2,1,0:T(8,128)(2,1)}, bf16[12,256,256]{2,1,0:T(8,128)(2,1)S(1)}, u32[]{:S(2)}, u32[]{:S(2)}) collective-permute-start(bf16[12,256,256]{2,1,0:T(8,128)(2,1)} %bitcast.41), channel_id=1, source_target_pairs={{0,8},{8,0},{16,24},{24,16},{32,40},{40,32},{48,56},{56,48},{64,72... | collective-permute-start | bytes 4718600 | tf_op jit(solution)/shard_map/ppermute | solution.py:30
  9.0 5.2 %collective-permute-start.2 = (bf16[256,128]{1,0:T(8,128)(2,1)S(1)}, bf16[256,128]{1,0:T(8,128)(2,1)S(1)}, u32[]{:S(2)}, u32[]{:S(2)}) collective-permute-start(bf16[256,128]{1,0:T(8,128)(2,1)S(1)} %get-tuple-element.14), channel_id=1, source_target_pairs={{0,16},{8,24},{16,0},{24,8},{32,48},{40,56},{48,32},{56,40},{64,80... | collective-permute-start | bytes 196616 | tf_op jit(solution)/shard_map/ppermute | solution.py:30
  14.2 10.5 %collective-permute-start.4 = (bf16[4,256,128]{2,1,0:T(8,128)(2,1)S(1)}, bf16[4,256,128]{2,1,0:T(8,128)(2,1)S(1)}, u32[]{:S(2)}, u32[]{:S(2)}) collective-permute-start(bf16[4,256,128]{2,1,0:T(8,128)(2,1)S(1)} %pad_maximum_fusion.6.refs_6_), channel_id=1, source_target_pairs={{0,224},{8,232},{16,240},{24,248},{32,0},{40,8},{48,16},{56,24},{6... | collective-permute-start | bytes 786440 | tf_op jit(solution)/shard_map/ppermute | solution.py:34
  19.9 9.0 %collective-permute-start.7 = (bf16[4,256,128]{2,1,0:T(8,128)(2,1)S(1)}, bf16[4,256,128]{2,1,0:T(8,128)(2,1)S(1)}, u32[]{:S(2)}, u32[]{:S(2)}) collective-permute-start(bf16[4,256,128]{2,1,0:T(8,128)(2,1)S(1)} %pad_maximum_fusion.6.refs_6_), channel_id=1, source_target_pairs={{0,32},{8,40},{16,48},{24,56},{32,64},{40,72},{48,80},{56,88},{64,... | collective-permute-start | bytes 786440 | tf_op jit(solution)/shard_map/ppermute | solution.py:34
  24.7 7.3 %collective-permute-start.5 = (bf16[4,256,128]{2,1,0:T(8,128)(2,1)S(1)}, bf16[4,256,128]{2,1,0:T(8,128)(2,1)}, u32[]{:S(2)}, u32[]{:S(2)}) collective-permute-start(bf16[4,256,128]{2,1,0:T(8,128)(2,1)S(1)} %collective-permute-done.4.refs_7_), channel_id=1, source_target_pairs={{0,224},{8,232},{16,240},{24,248},{32,0},{40,8},{48,16},{56,24},{6... | collective-permute-start | bytes 786440 | tf_op jit(solution)/shard_map/ppermute | solution.py:34
  28.8 7.2 %collective-permute-start.8 = (bf16[4,256,128]{2,1,0:T(8,128)(2,1)S(1)}, bf16[4,256,128]{2,1,0:T(8,128)(2,1)}, u32[]{:S(2)}, u32[]{:S(2)}) collective-permute-start(bf16[4,256,128]{2,1,0:T(8,128)(2,1)S(1)} %collective-permute-done.7.refs_12_), channel_id=1, source_target_pairs={{0,32},{8,40},{16,48},{24,56},{32,64},{40,72},{48,80},{56,88},{64,... | collective-permute-start | bytes 786440 | tf_op jit(solution)/shard_map/ppermute | solution.py:34
  32.1 7.1 %collective-permute-start.6 = (bf16[4,256,128]{2,1,0:T(8,128)(2,1)}, bf16[4,256,128]{2,1,0:T(8,128)(2,1)}, u32[]{:S(2)}, u32[]{:S(2)}) collective-permute-start(bf16[4,256,128]{2,1,0:T(8,128)(2,1)} %collective-permute-done.5.refs_8_), channel_id=1, source_target_pairs={{0,224},{8,232},{16,240},{24,248},{32,0},{40,8},{48,16},{56,24},{6... | collective-permute-start | bytes 786440 | tf_op jit(solution)/shard_map/ppermute | solution.py:34
  36.0 6.7 %collective-permute-start.9 = (bf16[4,256,128]{2,1,0:T(8,128)(2,1)}, bf16[4,256,128]{2,1,0:T(8,128)(2,1)}, u32[]{:S(2)}, u32[]{:S(2)}) collective-permute-start(bf16[4,256,128]{2,1,0:T(8,128)(2,1)} %collective-permute-done.8.refs_11_), channel_id=1, source_target_pairs={{0,32},{8,40},{16,48},{24,56},{32,64},{40,72},{48,80},{56,88},{64,... | collective-permute-start | bytes 786440 | tf_op jit(solution)/shard_map/ppermute | solution.py:34
  43.7 6.7 %collective-permute-start.10 = (bf16[4,256,128]{2,1,0:T(8,128)(2,1)S(1)}, bf16[4,256,128]{2,1,0:T(8,128)(2,1)S(1)}, u32[]{:S(2)}, u32[]{:S(2)}) collective-permute-start(bf16[4,256,128]{2,1,0:T(8,128)(2,1)S(1)} %broadcast_select_fusion), channel_id=1, source_target_pairs={{0,32},{8,232},{16,48},{24,248},{32,64},{40,8},{48,80},{56,24},{64... | collective-permute-start | bytes 786440 | tf_op jit(solution)/shard_map/ppermute | solution.py:435
  43.9 1.0 copy-start.2
  44.8 0.9 copy-start.4
  51.8 22.6 %copy-start.6 = (bf16[256,256]{1,0:T(8,128)(2,1)S(1)}, bf16[256,256]{1,0:T(8,128)(2,1)}, u32[]{:S(2)}) copy-start(bf16[256,256]{1,0:T(8,128)(2,1)} %cot_own.1) | copy-start | bytes 393220
  51.8 24.0 %copy-start.5 = (bf16[256,256]{1,0:T(8,128)(2,1)S(1)}, bf16[256,256]{1,0:T(8,128)(2,1)}, u32[]{:S(2)}) copy-start(bf16[256,256]{1,0:T(8,128)(2,1)} %weight.1) | copy-start | bytes 393220
  68.1 28.7 %copy-start.10 = (s32[1,1,12]{2,1,0:T(1,128)S(1)}, s32[1,1,12]{2,1,0:T(1,128)}, u32[]{:S(2)}) copy-start(s32[1,1,12]{2,1,0:T(1,128)} %param.9) | copy-start | bytes 148
  68.1 28.6 %copy-start.13 = (s32[1,1,12]{2,1,0:T(1,128)S(1)}, s32[1,1,12]{2,1,0:T(1,128)}, u32[]{:S(2)}) copy-start(s32[1,1,12]{2,1,0:T(1,128)} %param.10) | copy-start | bytes 148
  68.1 7.7 %collective-permute-start.11 = (f32[512,128]{1,0:T(8,128)S(1)}, f32[512,128]{1,0:T(8,128)S(1)}, u32[]{:S(2)}, u32[]{:S(2)}) collective-permute-start(f32[512,128]{1,0:T(8,128)S(1)} %bitcast.46), channel_id=1, source_target_pairs={{0,8},{8,0},{16,24},{24,16},{32,40},{40,32},{48,56},{56,48},{64,72... | collective-permute-start | bytes 786440 | tf_op jit(solution)/shard_map/ppermute | solution.py:30
  74.4 1.3 collective-permute-start.12
  98.0 5.7 %collective-permute-start.13 = (bf16[1152,128]{1,0:T(8,128)(2,1)S(1)}, bf16[1152,128]{1,0:T(8,128)(2,1)S(1)}, u32[]{:S(2)}, u32[]{:S(2)}) collective-permute-start(bf16[1152,128]{1,0:T(8,128)(2,1)S(1)} %backward_far.1.own), channel_id=1, source_target_pairs={{0,32},{8,232},{16,48},{24,248},{32,64},{40,8},{48,80},{56,24},{64... | collective-permute-start | bytes 884744 | tf_op jit(solution)/shard_map/ppermute | solution.py:435
  103.9 7.1 %collective-permute-start.14 = (bf16[1152,128]{1,0:T(8,128)(2,1)S(1)}, bf16[1152,128]{1,0:T(8,128)(2,1)S(1)}, u32[]{:S(2)}, u32[]{:S(2)}) collective-permute-start(bf16[1152,128]{1,0:T(8,128)(2,1)S(1)} %pad_maximum_fusion), channel_id=1, source_target_pairs={{0,32},{8,40},{16,48},{24,56},{32,64},{40,72},{48,80},{56,88},{64,... | collective-permute-start | bytes 884744 | tf_op jit(solution)/shard_map/ppermute | solution.py:34
  105.4 5.8 %collective-permute-start.17 = (bf16[1152,128]{1,0:T(8,128)(2,1)S(1)}, bf16[1152,128]{1,0:T(8,128)(2,1)S(1)}, u32[]{:S(2)}, u32[]{:S(2)}) collective-permute-start(bf16[1152,128]{1,0:T(8,128)(2,1)S(1)} %pad_maximum_fusion.3), channel_id=1, source_target_pairs={{0,224},{8,232},{16,240},{24,248},{32,0},{40,8},{48,16},{56,24},{6... | collective-permute-start | bytes 884744 | tf_op jit(solution)/shard_map/ppermute | solution.py:34
  111.1 7.9 %collective-permute-start.15 = (bf16[1152,128]{1,0:T(8,128)(2,1)S(1)}, bf16[1152,128]{1,0:T(8,128)(2,1)S(1)}, u32[]{:S(2)}, u32[]{:S(2)}) collective-permute-start(bf16[1152,128]{1,0:T(8,128)(2,1)S(1)} %pad_maximum_fusion.1), channel_id=1, source_target_pairs={{0,32},{8,40},{16,48},{24,56},{32,64},{40,72},{48,80},{56,88},{64,... | collective-permute-start | bytes 884744 | tf_op jit(solution)/shard_map/ppermute | solution.py:34
  111.3 7.9 %collective-permute-start.18 = (bf16[1152,128]{1,0:T(8,128)(2,1)S(1)}, bf16[1152,128]{1,0:T(8,128)(2,1)S(1)}, u32[]{:S(2)}, u32[]{:S(2)}) collective-permute-start(bf16[1152,128]{1,0:T(8,128)(2,1)S(1)} %pad_maximum_fusion.4), channel_id=1, source_target_pairs={{0,224},{8,232},{16,240},{24,248},{32,0},{40,8},{48,16},{56,24},{6... | collective-permute-start | bytes 884744 | tf_op jit(solution)/shard_map/ppermute | solution.py:34
  119.1 9.0 %collective-permute-start.16 = (bf16[1152,128]{1,0:T(8,128)(2,1)S(1)}, bf16[1152,128]{1,0:T(8,128)(2,1)S(1)}, u32[]{:S(2)}, u32[]{:S(2)}) collective-permute-start(bf16[1152,128]{1,0:T(8,128)(2,1)S(1)} %pad_maximum_fusion.2), channel_id=1, source_target_pairs={{0,32},{8,40},{16,48},{24,56},{32,64},{40,72},{48,80},{56,88},{64,... | collective-permute-start | bytes 884744 | tf_op jit(solution)/shard_map/ppermute | solution.py:34
  119.4 8.8 %collective-permute-start.19 = (bf16[1152,128]{1,0:T(8,128)(2,1)S(1)}, bf16[1152,128]{1,0:T(8,128)(2,1)S(1)}, u32[]{:S(2)}, u32[]{:S(2)}) collective-permute-start(bf16[1152,128]{1,0:T(8,128)(2,1)S(1)} %pad_maximum_fusion.5), channel_id=1, source_target_pairs={{0,224},{8,232},{16,240},{24,248},{32,0},{40,8},{48,16},{56,24},{6... | collective-permute-start | bytes 884744 | tf_op jit(solution)/shard_map/ppermute | solution.py:34
  128.4 11.0 %collective-permute-start.20 = (bf16[384,128]{1,0:T(8,128)(2,1)S(1)}, bf16[384,128]{1,0:T(8,128)(2,1)S(1)}, u32[]{:S(2)}, u32[]{:S(2)}) collective-permute-start(bf16[384,128]{1,0:T(8,128)(2,1)S(1)} %get-tuple-element.18.sent), channel_id=1, source_target_pairs={{0,8},{8,0},{16,24},{24,16},{32,40},{40,32},{48,56},{56,48},{64,72... | collective-permute-start | bytes 294920 | tf_op jit(solution)/shard_map/ppermute | solution.py:30
  136.1 5.9 %collective-permute-start.21 = (bf16[384,128]{1,0:T(8,128)(2,1)S(1)}, bf16[384,128]{1,0:T(8,128)(2,1)S(1)}, u32[]{:S(2)}, u32[]{:S(2)}) collective-permute-start(bf16[384,128]{1,0:T(8,128)(2,1)S(1)} %get-tuple-element.19), channel_id=1, source_target_pairs={{0,16},{8,24},{16,0},{24,8},{32,48},{40,56},{48,32},{56,40},{64,80... | collective-permute-start | bytes 294920 | tf_op jit(solution)/shard_map/ppermute | solution.py:30
  137.3 6.9 %collective-permute-start.22 = (bf16[384,128]{1,0:T(8,128)(2,1)S(1)}, bf16[384,128]{1,0:T(8,128)(2,1)S(1)}, u32[]{:S(2)}, u32[]{:S(2)}) collective-permute-start(bf16[384,128]{1,0:T(8,128)(2,1)S(1)} %get-tuple-element.20), channel_id=1, source_target_pairs={{0,24},{8,16},{16,8},{24,0},{32,56},{40,48},{48,40},{56,32},{64,88... | collective-permute-start | bytes 294920 | tf_op jit(solution)/shard_map/ppermute | solution.py:30
  145.0 4.9 %collective-permute-start.23 = (f32[2,128,128]{2,1,0:T(8,128)S(1)}, f32[2,128,128]{2,1,0:T(8,128)S(1)}, u32[]{:S(2)}, u32[]{:S(2)}) collective-permute-start(f32[2,128,128]{2,1,0:T(8,128)S(1)} %get-tuple-element.21.here), channel_id=1, source_target_pairs={{0,4},{1,5},{2,6},{3,7},{4,0},{5,1},{6,2},{7,3},{8,12},{9,13},{10,... | collective-permute-start | bytes 393224 | tf_op jit(solution)/shard_map/ppermute | solution.py:499
  (6 other events, 4.0 us)

commit v5 on v4

v5 whole, which is shorter than its diff:
```python
import functools
import math

import jax
import jax.numpy as jnp
from jax import lax
from jax.experimental import pallas as pl
from jax.experimental.pallas import tpu as pltpu
from jax.sharding import PartitionSpec as P

NZ = 8
QUAD = 4
NCOL = 8
TILE = 256
HALF = 128
SLOTS = 12
W_ROWS = 128
UNROLL = 4


def row_pairs(move):
    pairs = []
    for r in range(NZ * QUAD):
        z, q = move(r // QUAD, r % QUAD)
        pairs.append((r, (z % NZ) * QUAD + q))
    return pairs


def quad_permute(x, flip):
    return lax.ppermute(x, "row", row_pairs(lambda z, q: (z, q ^ flip)))


def z_shift(x, step):
    return lax.ppermute(x, "row", row_pairs(lambda z, q: (z + step, q)))


def prepare_kernel(rows, cols, count, block, keep, message, own_lists):
    core = lax.axis_index("row") & 1

    @pl.when(core == 0)
    def _():
        keep[...] = block[:, :HALF]
        message[16:, :] = block[:, HALF:]

    @pl.when(core == 1)
    def _():
        keep[...] = block[:, HALF:]
        message[16:, :] = block[:, :HALF]

    lane = lax.broadcasted_iota(jnp.int32, (16, HALF), 1)
    values = jnp.zeros((16, HALF), jnp.float32)
    listed = [rows[s] for s in range(SLOTS)] + [cols[s] for s in range(SLOTS)] + [count[0, 0]]
    for n, value in enumerate(listed):
        values = jnp.where(lane == n, value.astype(jnp.float32), values)
        own_lists[n] = value
    message[:16, :] = values.astype(jnp.bfloat16)


def join_kernel(own_keep, own_message, x_block, keep, message):
    core = lax.axis_index("row") & 1
    keep[0] = own_keep[...]
    message[: TILE + 16, :] = own_message[...]

    @pl.when(core == 0)
    def _():
        keep[1] = x_block[:, :HALF]
        message[TILE + 16 :, :] = x_block[:, HALF:]

    @pl.when(core == 1)
    def _():
        keep[1] = x_block[:, HALF:]
        message[TILE + 16 :, :] = x_block[:, :HALF]


def list_slots(lists, adj_refs, adj_vmem, adj_sem, rows, places, far, dummy):
    device = lax.axis_index("row")
    z, q = device >> 2, device & 3
    n = jnp.int32(0)
    for i in range(2):
        count = lists[i][24]
        for s in range(SLOTS):
            tile = lists[i][12 + s]
            row = lists[i][s]
            other = (tile & 3) ^ q
            place = (((tile >> 2) - z) & 7) * QUAD + ((other & 1) * 2 + (other >> 1))
            live = (s < count) & (((place >> 2) == 4) == far)
            rows[n] = row * 2 + i
            places[n] = place

            @pl.when(live)
            def _(i=i, s=s, n=n):
                pltpu.make_async_copy(
                    adj_refs[i].at[s], adj_vmem.at[n], adj_sem.at[n]
                ).start()

            n = n + live.astype(jnp.int32)
    for u in range(UNROLL - 1):
        rows[n + u], places[n + u] = dummy
    return n


def slot_products(n, adj_ref, adj_vmem, adj_sem, product, add_to):
    @pl.loop(0, (n + UNROLL - 1) >> 2)
    def _(step):
        slots = [step * UNROLL + u for u in range(UNROLL)]
        for j in slots:

            @pl.when(j < n)
            def _(j=j):
                pltpu.make_async_copy(adj_ref.at[0], adj_vmem.at[j], adj_sem.at[j]).wait()

        values = [product(j) for j in slots]
        for j, value in zip(slots, values):
            add_to(j, value)


def forward_near_kernel(*refs):
    lists, (adj0, adj1), refs = refs[:2], refs[2:4], refs[4:]
    pieces, (acc, panel, adj_vmem, rows, places, panel_sem, adj_sem) = refs[:7], refs[7:]
    copies = [
        pltpu.make_async_copy(piece, panel.at[pl.ds(place * QUAD, QUAD)], panel_sem.at[place])
        for place, piece in zip((0, 1, 2, 3, 5, 6, 7), pieces)
    ]
    for copy in copies:
        copy.start()
    n = list_slots(lists, (adj0, adj1), adj_vmem, adj_sem, rows, places, False, (16, 0))
    acc[...] = jnp.zeros_like(acc)
    for copy in copies:
        copy.wait()

    def product(j):
        return jnp.dot(adj_vmem[j], panel[places[j]], preferred_element_type=jnp.float32)

    def add_to(j, value):
        acc[rows[j]] += value

    slot_products(n, adj0, adj_vmem, adj_sem, product, add_to)


def forward_far_kernel(*refs):
    lists, refs = refs[:2], refs[2:]
    adj0, adj1, near, far_a, far_b, out, acc, far, adj_vmem, rows, places, adj_sem = refs
    n = list_slots(lists, (adj0, adj1), adj_vmem, adj_sem, rows, places, True, (16, 16))
    far[:2] = far_a[...]
    far[2:] = far_b[...]
    acc[...] = near[...]

    def product(j):
        return jnp.dot(adj_vmem[j], far[places[j] - 16], preferred_element_type=jnp.float32)

    def add_to(j, value):
        acc[rows[j]] += value

    slot_products(n, adj0, adj_vmem, adj_sem, product, add_to)
    for row in range(8):
        for i in range(2):
            out[row, i] = acc[2 * row + i].astype(jnp.bfloat16)


def backward_kernel(far, *refs):
    lists, refs = refs[:2], refs[2:]
    adj0, adj1, back = refs[:3]
    acc, adj_vmem, rows, places, adj_sem = refs[-5:]
    outs = refs[3:-5]
    base = 16 if far else 0
    spare = acc.shape[0] - 1
    n = list_slots(
        lists, (adj0, adj1), adj_vmem, adj_sem, rows, places, far, (0, base + spare)
    )
    acc[...] = jnp.zeros_like(acc)

    def product(j):
        row = rows[j]
        return lax.dot_general(
            adj_vmem[j],
            back[row >> 1, pl.ds((row & 1) * TILE, TILE), :],
            (((0,), (0,)), ((), ())),
            preferred_element_type=jnp.float32,
        )

    def add_to(j, value):
        acc[places[j] - base] += value

    slot_products(n, adj0, adj_vmem, adj_sem, product, add_to)
    if not far:
        outs[0][...] = acc[:spare].astype(jnp.bfloat16)
        return
    for k in range(QUAD):
        rows = pl.ds((k & 1) * TILE, TILE)
        outs[k >> 1][rows, :] = acc[k].astype(jnp.bfloat16)
    piece = back[0, 2 * TILE :, :].astype(jnp.float32)
    for c in range(1, NCOL):
        piece = piece + back[c, 2 * TILE :, :].astype(jnp.float32)
    for out in outs:
        out[2 * TILE :, :] = piece.astype(jnp.bfloat16)


def split(x):
    high = x.astype(jnp.bfloat16)
    return high, (x - high.astype(jnp.float32)).astype(jnp.bfloat16)


def dense_kernel(agg_own, agg_other, weight, cot_own, cot_other, act_out, send_out):
    first = (lax.axis_index("row") & 1) == 0
    own = agg_own[...]
    other = jnp.concatenate([agg_other[TILE:, :], agg_other[:TILE, :]], axis=0)
    w = weight[...]
    w_other_half = jnp.where(first, w[HALF:], w[:HALF])
    w_half = jnp.where(first, w[:HALF], w[HALF:])

    def dot(a, b, dims=((1,), (0,))):
        return lax.dot_general(a, b, (dims, ((), ())), preferred_element_type=jnp.float32)

    own_hi, own_lo = split(own)
    other_hi, other_lo = split(other)
    v = (dot(own_hi, w_half) + dot(own_lo, w_half)) + (
        dot(other_hi, w_other_half) + dot(other_lo, w_other_half)
    )
    scale = math.sqrt(2.0 / math.pi)
    square = v * v
    t = jnp.tanh(scale * (v + 0.044715 * (square * v)))
    cdf = 0.5 * (1.0 + t)
    act_out[...] = (v[:TILE] * cdf[:TILE]).astype(jnp.bfloat16)
    slope = cdf + 0.5 * v * ((1.0 - t) * (1.0 + t)) * (scale * (1.0 + 3.0 * 0.044715 * square))
    cot = jnp.concatenate([cot_own[...], cot_other[...]], axis=0).astype(jnp.float32)
    grad_hi, grad_lo = split(cot * slope)
    nodes = ((1,), (1,))
    back = (dot(grad_hi, w_half, nodes) + dot(grad_lo, w_half, nodes)).astype(jnp.bfloat16)
    rows = ((0,), (0,))
    w_part = (
        dot(own_hi, grad_hi, rows) + dot(own_lo, grad_hi, rows) + dot(own_hi, grad_lo, rows)
    ).astype(jnp.bfloat16)
    for c in range(NCOL):
        send_out[c, : 2 * TILE, :] = back
        piece = w_part[64 * (c // 4) : 64 * (c // 4) + 64]
        send_out[c, 2 * TILE : 2 * TILE + 64, :] = piece[:, :HALF]
        send_out[c, 2 * TILE + 64 :, :] = piece[:, HALF:]


def sum_kernel(parts, own, up1, up2, up3, up4, down1, down2, down3, down4, kept, message, by_step):
    z = lax.axis_index("row") >> 2
    size = QUAD * TILE
    by_step[0] = own[2 * TILE :, :]
    by_step[1] = down1[2 * TILE :, :]
    by_step[7] = up1[2 * TILE :, :]
    for k, ref in ((2, down2), (3, down3), (4, up4), (5, up3), (6, up2)):
        by_step[k] = ref[size:, :]
    w_sum = by_step[(0 - z) & 7].astype(jnp.float32)
    for a in range(1, NZ):
        w_sum = w_sum + by_step[(a - z) & 7].astype(jnp.float32)
    message[2 * TILE :, :] = w_sum.astype(jnp.bfloat16)
    for k in range(QUAD):
        rows = pl.ds(k * TILE, TILE)
        total = (
            parts[k].astype(jnp.float32)
            + up4[rows, :].astype(jnp.float32)
            + down4[rows, :].astype(jnp.float32)
        )
        if k & 1:
            message[(k >> 1) * TILE : ((k >> 1) + 1) * TILE, :] = total.astype(jnp.bfloat16)
        else:
            kept[k >> 1] = total


def middle_kernel(kept, sent, from_x, mine, message, w_mine):
    mine[...] = (kept[0] + from_x[:TILE, :].astype(jnp.float32)).astype(jnp.bfloat16)
    message[:TILE, :] = (
        kept[1] + from_x[TILE : 2 * TILE, :].astype(jnp.float32)
    ).astype(jnp.bfloat16)
    w_sum = sent[2 * TILE :, :].astype(jnp.float32) + from_x[2 * TILE :, :].astype(jnp.float32)
    high, low = split(w_sum)
    message[TILE : TILE + W_ROWS, :] = high
    message[TILE + W_ROWS :, :] = low
    w_mine[...] = high.astype(jnp.float32) + low.astype(jnp.float32)


def last_kernel(mine, from_core, w_mine, w_x, w_both, grad_out, w_out):
    core = lax.axis_index("row") & 1
    x_lo = lax.axis_index("col") >> 2
    scale = 1.0 / 256.0
    w_core = from_core[TILE : TILE + W_ROWS, :].astype(jnp.float32) + from_core[
        TILE + W_ROWS :, :
    ].astype(jnp.float32)

    def place(value, start):
        rows = pl.ds(pl.multiple_of(start, 64), 64)
        w_out[rows, :HALF] = value[:64, :] * scale
        w_out[rows, HALF:] = value[64:, :] * scale

    place(w_mine[...], core * HALF + x_lo * 64)
    place(w_x[...], core * HALF + (1 - x_lo) * 64)
    place(w_core, (1 - core) * HALF + x_lo * 64)
    place(w_both[...], (1 - core) * HALF + (1 - x_lo) * 64)

    @pl.when(core == 0)
    def _():
        grad_out[:, :HALF] = mine[...]
        grad_out[:, HALF:] = from_core[:TILE, :]

    @pl.when(core == 1)
    def _():
        grad_out[:, HALF:] = mine[...]
        grad_out[:, :HALF] = from_core[:TILE, :]


SMEM = pl.BlockSpec(memory_space=pltpu.SMEM)
VMEM = pl.BlockSpec(memory_space=pltpu.VMEM)
ANY = pl.BlockSpec(memory_space=pl.ANY)


def params(mib):
    return pltpu.CompilerParams(vmem_limit_bytes=mib << 20)


LIST = 2 * SLOTS + UNROLL
SLOT_SCRATCH = [
    pltpu.VMEM((LIST, TILE, TILE), jnp.bfloat16),
    pltpu.SMEM((LIST,), jnp.int32),
    pltpu.SMEM((LIST,), jnp.int32),
]


def cost(slots, size):
    return pl.CostEstimate(
        flops=slots * 2 * TILE * TILE * HALF, bytes_accessed=size << 20, transcendentals=0
    )


LISTS = [SMEM] * 4


def shape(*dims, dtype=jnp.bfloat16):
    return jax.ShapeDtypeStruct(dims, dtype)


def local(kernel, outs, n_in, name, scalars=0, any_in=0, scratch=(), cost=None, scalar_out=0):
    return pl.pallas_call(
        kernel,
        out_shape=outs,
        in_specs=[SMEM] * scalars + [ANY] * any_in + [VMEM] * (n_in - scalars - any_in),
        out_specs=(VMEM,) * (len(outs) - scalar_out) + (SMEM,) * scalar_out,
        scratch_shapes=scratch,
        compiler_params=params(20),
        cost_estimate=cost,
        name=name,
    )


def prepare(rows, cols, count, block):
    return local(
        prepare_kernel,
        (shape(TILE, HALF), shape(TILE + 16, HALF), shape(25, dtype=jnp.int32)),
        4,
        "prepare",
        scalars=3,
        scalar_out=1,
    )(rows, cols, count, block)


def join(own_keep, own_message, x_block):
    return local(
        join_kernel, (shape(2, TILE, HALF), shape(2 * TILE + 16, HALF)), 3, "join"
    )(own_keep, own_message, x_block)


def forward_near(lists, adj0, adj1, pieces):
    return local(
        forward_near_kernel,
        (shape(17, TILE, HALF, dtype=jnp.float32),),
        11,
        "forward_near",
        scalars=2,
        any_in=9,
        scratch=[pltpu.VMEM((NZ * QUAD, TILE, HALF), jnp.bfloat16)]
        + SLOT_SCRATCH
        + [pltpu.SemaphoreType.DMA((NZ,)), pltpu.SemaphoreType.DMA((LIST,))],
        cost=cost(21, 6),
    )(*lists, adj0, adj1, *pieces)[0]


def forward_far(lists, adj0, adj1, near, far_a, far_b):
    return local(
        forward_far_kernel,
        (shape(8, 2, TILE, HALF),),
        7,
        "forward_far",
        scalars=2,
        any_in=2,
        scratch=[
            pltpu.VMEM((17, TILE, HALF), jnp.float32),
            pltpu.VMEM((QUAD, TILE, HALF), jnp.bfloat16),
        ]
        + SLOT_SCRATCH
        + [pltpu.SemaphoreType.DMA((LIST,))],
        cost=cost(3, 4),
    )(*lists, adj0, adj1, near, far_a, far_b)[0]


def backward_tiles(lists, adj0, adj1, back, far):
    places = QUAD if far else NZ * QUAD
    message = shape(2 * TILE + W_ROWS, HALF)
    return local(
        functools.partial(backward_kernel, far),
        (message, message) if far else (shape(places, TILE, HALF),),
        5,
        "backward_far" if far else "backward_near",
        scalars=2,
        any_in=2,
        scratch=[pltpu.VMEM((places + 1, TILE, HALF), jnp.float32)]
        + SLOT_SCRATCH
        + [pltpu.SemaphoreType.DMA((LIST,))],
        cost=cost(3, 2) if far else cost(21, 6),
    )(*lists, adj0, adj1, back)


def dense(agg_own, agg_other, weight, cot_own, cot_other):
    return local(
        dense_kernel,
        (shape(TILE, 2 * HALF), shape(NCOL, 2 * TILE + W_ROWS, HALF)),
        5,
        "dense",
    )(agg_own, agg_other, weight, cot_own, cot_other)


def ring_end(parts, *messages):
    return local(
        sum_kernel,
        (shape(2, TILE, HALF, dtype=jnp.float32), shape(2 * TILE + W_ROWS, HALF)),
        10,
        "ring_end",
        scratch=[pltpu.VMEM((NZ, W_ROWS, HALF), jnp.bfloat16)],
    )(parts, *messages)


def middle(kept, sent, from_x):
    return local(
        middle_kernel,
        (
            shape(TILE, HALF),
            shape(TILE + 2 * W_ROWS, HALF),
            shape(W_ROWS, HALF, dtype=jnp.float32),
        ),
        3,
        "middle",
    )(kept, sent, from_x)


def last(mine, from_core, w_mine, w_x, w_both):
    return local(
        last_kernel,
        (shape(TILE, 2 * HALF), shape(2 * HALF, 2 * HALF, dtype=jnp.float32)),
        5,
        "last",
    )(mine, from_core, w_mine, w_x, w_both)


def add(a, b):
    return (a.astype(jnp.float32) + b.astype(jnp.float32)).astype(jnp.bfloat16)


def per_device(features, adj_tiles, tile_row, tile_col, tile_count, weight, cotangent):
    adj0 = adj_tiles[0, 0]
    block = features[0]

    x_block = quad_permute(block, 2)
    keep, message, own_lists = prepare(tile_row[0, 0], tile_col[0, 0], tile_count, block)
    keep, message = join(keep, message, x_block)
    from_core = quad_permute(message, 1)
    chunk = jnp.concatenate([keep, from_core[16:].reshape(2, TILE, HALF)], axis=0)
    lists = (own_lists, from_core[0, :25].astype(jnp.int32))
    adj1 = quad_permute(adj0, 1)
    cot1 = quad_permute(cotangent, 1)

    up1, down1 = z_shift(chunk, 1), z_shift(chunk, -1)
    up2, down2 = z_shift(up1, 1), z_shift(down1, -1)
    up3, down3 = z_shift(up2, 1), z_shift(down2, -1)
    far_a, far_b = z_shift(up3[:2], 1), z_shift(down3[2:], -1)
    near = forward_near(lists, adj0, adj1, [chunk, down1, down2, down3, up3, up2, up1])
    partial = forward_far(lists, adj0, adj1, near, far_a, far_b)

    shares = lax.all_to_all(partial, "col", 0, 0, tiled=True)
    agg = shares.reshape(NCOL, 2 * TILE, HALF).astype(jnp.float32).sum(axis=0)
    agg_other = quad_permute(agg, 1)
    activated, send = dense(agg, agg_other, weight, cotangent, cot1)
    received = lax.all_to_all(send, "col", 0, 0, tiled=True)

    half, size = 2 * TILE, QUAD * TILE
    own, own_down = backward_tiles(lists, adj0, adj1, received, True)
    (blocks,) = backward_tiles(lists, adj0, adj1, received, False)
    parts = blocks.reshape(NZ, size, HALF)
    up1, down1 = z_shift(own, 1), z_shift(own_down, -1)
    up = [add(parts[3, :half], up1[:half]), parts[3, half:], up1[half:]]
    down = [parts[5, :half], add(parts[5, half:], down1[:half]), down1[half:]]
    up2, down2 = z_shift(jnp.concatenate(up), 1), z_shift(jnp.concatenate(down), -1)
    up = [add(parts[2], up2[:size]), up2[size:]]
    down = [add(parts[6], down2[:size]), down2[size:]]
    up3, down3 = z_shift(jnp.concatenate(up), 1), z_shift(jnp.concatenate(down), -1)
    up4 = z_shift(jnp.concatenate([add(parts[1], up3[:size]), up3[size:]]), 1)
    down4 = z_shift(add(parts[7], down3[:size]), -1)

    kept, to_x = ring_end(blocks, own, up1, up2, up3, up4, down1, down2, down3, down4)
    mine, to_core, w_mine = middle(kept, to_x, quad_permute(to_x, 2))
    across = [(c, c ^ 4) for c in range(NCOL)]
    both = [
        (r * NCOL + c, (r ^ 1) * NCOL + (c ^ 4)) for r in range(NZ * QUAD) for c in range(NCOL)
    ]
    w_x = lax.ppermute(w_mine, "col", across)
    w_both = lax.ppermute(w_mine, ("row", "col"), both)
    grad, weight_grad = last(mine, quad_permute(to_core, 1), w_mine, w_x, w_both)
    return (activated, weight_grad, grad[None])


def solution(mesh):
    return jax.shard_map(
        per_device,
        mesh=mesh,
        in_specs=(
            P("col", "row", None),
            P("row", "col", None, None, None),
            P("row", "col", None),
            P("row", "col", None),
            P("row", "col"),
            P(),
            P(("row", "col"), None),
        ),
        out_specs=(P(("row", "col"), None), P(), P("col", "row", None)),
        check_vma=False,
    )
```

time: 150 us -> 142 us (0.947)
  waiting for transfers between devices: 43.6 us -> 38.6 us
  local copies, waits for them, and re-layouts: 7 us -> 2.38 us
  Pallas kernels: 13.1 us -> 15 us
  starting transfers between devices: 47.6 us -> 49.2 us
    unnamed x28 -> x12, local copies, waits for them, and re-layouts: 6.85 us -> 2.22 us
    ppermute x12 -> x16, starting transfers between devices: 21.5 us -> 25.7 us  [z_shift(): return lax.ppermute(x, 'row', row_pairs(lambda z, q: (z + step, q)))]
    ppermute x9 -> x7, starting transfers between devices: 24.3 us -> 21.8 us  [quad_permute(): return lax.ppermute(x, 'row', row_pairs(lambda z, q: (z, q ^ flip)))]
    ppermute x12 -> x16, waiting for transfers between devices: 29.4 us -> 27.1 us  [z_shift(): return lax.ppermute(x, 'row', row_pairs(lambda z, q: (z + step, q)))]
    pallas_call x8 -> x9, Pallas kernels: 11.7 us -> 13.6 us  [the longest x2 5.71 us: backward_tiles(): local(functools.partial(backward_kernel, far), (message, message) if far...]
    ppermute x3 -> x2, waiting for transfers between devices: 5 us -> 3.51 us  [the longest x1 1.92 us: per_device(): w_x = lax.ppermute(w_mine, 'col', across)]
    ppermute x9 -> x7, waiting for transfers between devices: 9.21 us -> 7.95 us  [quad_permute(): return lax.ppermute(x, 'row', row_pairs(lambda z, q: (z, q ^ flip)))]
  transfers between devices with their start and end apart: 24 -> 25, of which waited for: 15 -> 14; matrix products, arithmetic and copies ran while one was open for 1% -> 0% of each run, Pallas kernels for 5% -> 6%
where the time goes in v5:
time: 142 us
  starting transfers between devices  49.2 us (35%)
  waiting for transfers between devices  38.6 us (27%)
  blocking collectives  34.5 us (24%)
  Pallas kernels  15 us (11%)
  local copies, waits for them, and re-layouts  2.38 us (2%)
  between operations  1.64 us (1%)
    ppermute x16, waiting for transfers between devices, z_shift(): return lax.ppermute(x, 'row', row_pairs(lambda z, q: (z + step, q)))  27.1 us
    ppermute x16, starting transfers between devices, z_shift(): return lax.ppermute(x, 'row', row_pairs(lambda z, q: (z + step, q)))  25.7 us
    ppermute x7, starting transfers between devices, quad_permute(): return lax.ppermute(x, 'row', row_pairs(lambda z, q: (z, q ^ flip)))  21.8 us
    all_to_all x1, blocking collectives, per_device(): received = lax.all_to_all(send, 'col', 0, 0, tiled=True)  19.5 us
    all_to_all x1, blocking collectives, per_device(): shares = lax.all_to_all(partial, 'col', 0, 0, tiled=True)  15 us
    ppermute x7, waiting for transfers between devices, quad_permute(): return lax.ppermute(x, 'row', row_pairs(lambda z, q: (z, q ^ flip)))  7.95 us
    pallas_call x2, Pallas kernels, backward_tiles(): local(functools.partial(backward_kernel, far), (message, message) if far...  5.71 us
    pallas_call x1, Pallas kernels, forward_near(): local(forward_near_kernel, (shape(17, TILE, HALF, dtype=jnp.float32),), 1...  3.26 us
  transfers between devices with their start and end apart: 25, of which 14 were waited for; matrix products, arithmetic and copies ran while one was open for 0% of the time, Pallas kernels for 6%

profile of v5, /device:TPU:1, one launch (start us, length us, event | category | flops | bytes accessed | tf_op | source)
XLA Modules:
  0.0 142.0 jit_solution(11893688539002436167)
XLA Ops:
  0.6 3.3 %collective-permute-start.2 = (bf16[12,256,256]{2,1,0:T(8,128)(2,1)}, bf16[12,256,256]{2,1,0:T(8,128)(2,1)S(1)}, u32[]{:S(2)}, u32[]{:S(2)}) collective-permute-start(bf16[12,256,256]{2,1,0:T(8,128)(2,1)} %bitcast.39), channel_id=1, source_target_pairs={{0,8},{8,0},{16,24},{24,16},{32,40},{40,32},{48,56},{56,48},{64,72... | collective-permute-start | bytes 4718600 | tf_op jit(solution)/shard_map/ppermute | solution.py:30
  7.9 1.2 prepare.1
  9.1 1.7 %collective-permute-done.x_block = bf16[256,256]{1,0:T(8,128)(2,1)S(1)} collective-permute-done((bf16[256,256]{1,0:T(8,128)(2,1)}, bf16[256,256]{1,0:T(8,128)(2,1)S(1)}, u32[]{:S(2)}, u32[]{:S(2)}) %collective-permute-start) | collective-permute-done | bytes 131104 | tf_op jit(solution)/shard_map/ppermute | solution.py:30
  12.8 3.9 %collective-permute-start.3 = (bf16[4,256,128]{2,1,0:T(8,128)(2,1)S(1)}, bf16[4,256,128]{2,1,0:T(8,128)(2,1)S(1)}, u32[]{:S(2)}, u32[]{:S(2)}) collective-permute-start(bf16[4,256,128]{2,1,0:T(8,128)(2,1)S(1)} %pad_maximum_fusion.5.refs_4_), channel_id=1, source_target_pairs={{0,224},{8,232},{16,240},{24,248},{32,0},{40,8},{48,16},{56,24},{6... | collective-permute-start | bytes 786440 | tf_op jit(solution)/shard_map/ppermute | solution.py:34
  16.7 5.3 %collective-permute-done.3.refs_5_ = bf16[4,256,128]{2,1,0:T(8,128)(2,1)S(1)} collective-permute-done((bf16[4,256,128]{2,1,0:T(8,128)(2,1)S(1)}, bf16[4,256,128]{2,1,0:T(8,128)(2,1)S(1)}, u32[]{:S(2)}, u32[]{:S(2)}) %collective-permute-start.3) | collective-permute-done | bytes 262176 | tf_op jit(solution)/shard_map/ppermute | solution.py:34
  22.0 3.4 %collective-permute-start.4 = (bf16[4,256,128]{2,1,0:T(8,128)(2,1)S(1)}, bf16[4,256,128]{2,1,0:T(8,128)(2,1)S(1)}, u32[]{:S(2)}, u32[]{:S(2)}) collective-permute-start(bf16[4,256,128]{2,1,0:T(8,128)(2,1)S(1)} %collective-permute-done.3.refs_5_), channel_id=1, source_target_pairs={{0,224},{8,232},{16,240},{24,248},{32,0},{40,8},{48,16},{56,24},{6... | collective-permute-start | bytes 786440 | tf_op jit(solution)/shard_map/ppermute | solution.py:34
  25.4 4.4 %collective-permute-done.4.refs_6_ = bf16[4,256,128]{2,1,0:T(8,128)(2,1)S(1)} collective-permute-done((bf16[4,256,128]{2,1,0:T(8,128)(2,1)S(1)}, bf16[4,256,128]{2,1,0:T(8,128)(2,1)S(1)}, u32[]{:S(2)}, u32[]{:S(2)}) %collective-permute-start.4) | collective-permute-done | bytes 262176 | tf_op jit(solution)/shard_map/ppermute | solution.py:34
  29.9 3.4 %collective-permute-start.5 = (bf16[4,256,128]{2,1,0:T(8,128)(2,1)S(1)}, bf16[4,256,128]{2,1,0:T(8,128)(2,1)S(1)}, u32[]{:S(2)}, u32[]{:S(2)}) collective-permute-start(bf16[4,256,128]{2,1,0:T(8,128)(2,1)S(1)} %collective-permute-done.4.refs_6_), channel_id=1, source_target_pairs={{0,224},{8,232},{16,240},{24,248},{32,0},{40,8},{48,16},{56,24},{6... | collective-permute-start | bytes 786440 | tf_op jit(solution)/shard_map/ppermute | solution.py:34
  33.3 3.3 %collective-permute-done.5.refs_7_ = bf16[4,256,128]{2,1,0:T(8,128)(2,1)S(1)} collective-permute-done((bf16[4,256,128]{2,1,0:T(8,128)(2,1)S(1)}, bf16[4,256,128]{2,1,0:T(8,128)(2,1)S(1)}, u32[]{:S(2)}, u32[]{:S(2)}) %collective-permute-start.5) | collective-permute-done | bytes 262176 | tf_op jit(solution)/shard_map/ppermute | solution.py:34
  36.6 3.7 %collective-permute-start.10 = (bf16[2,256,128]{2,1,0:T(8,128)(2,1)S(1)}, bf16[2,256,128]{2,1,0:T(8,128)(2,1)S(1)}, u32[]{:S(2)}, u32[]{:S(2)}) collective-permute-start(bf16[2,256,128]{2,1,0:T(8,128)(2,1)S(1)} %slice.99), channel_id=1, source_target_pairs={{0,224},{8,232},{16,240},{24,248},{32,0},{40,8},{48,16},{56,24},{6... | collective-permute-start | bytes 393224 | tf_op jit(solution)/shard_map/ppermute | solution.py:34
  40.4 3.3 %forward_near.1.refs_4_ = f32[17,256,128]{2,1,0:T(8,128)S(1)} custom-call(s32[25]{0:T(128)S(1)} %get-tuple-element.19.refs_0_, s32[25]{0:T(128)S(1)} %fusion.6.refs_1_, bf16[12,256,256]{2,1,0:T(8,128)(2,1)S(1)} %bitcast.40, bf16[12,256,256]{2,1,0:T(8,128)(2,1)S(1)} %collective-permute-done.2.refs_3_, bf16[4,256,128]{2,1,0:T(8,128)(2,1)S(1)} %pad_maximum_fusion.5.refs_4_, ...), custom_call_target="tpu_custom_call" | custom-call | flops 352321536 | bytes 6291456 | tf_op jit(solution)/shard_map/forward_near/pallas_call | solution.py:367
  43.7 1.7 %collective-permute-done.9.refs_5_ = bf16[2,256,128]{2,1,0:T(8,128)(2,1)S(1)} collective-permute-done((bf16[2,256,128]{2,1,0:T(8,128)(2,1)S(1)}, bf16[2,256,128]{2,1,0:T(8,128)(2,1)S(1)}, u32[]{:S(2)}, u32[]{:S(2)}) %collective-permute-start.9) | collective-permute-done | bytes 131104 | tf_op jit(solution)/shard_map/ppermute | solution.py:34
  45.4 2.4 %forward_far.1 = bf16[8,2,256,128]{3,2,1,0:T(8,128)(2,1)S(1)} custom-call(s32[25]{0:T(128)S(1)} %get-tuple-element.19.refs_0_, s32[25]{0:T(128)S(1)} %fusion.6.refs_1_, bf16[12,256,256]{2,1,0:T(8,128)(2,1)S(1)} %bitcast.41, bf16[12,256,256]{2,1,0:T(8,128)(2,1)S(1)} %collective-permute-done.2.refs_3_, f32[17,256,128]{2,1,0:T(8,128)S(1)} %forward_near.1.refs_4_, ...), custom_call_target="tpu_custom_call" | custom-call | flops 50331648 | bytes 4194304 | tf_op jit(solution)/shard_map/forward_far/pallas_call | solution.py:382
  47.8 15.0 %all_to_all.10 = bf16[8,2,256,128]{3,2,1,0:T(8,128)(2,1)S(1)} all-to-all(bf16[8,2,256,128]{3,2,1,0:T(8,128)(2,1)S(1)} %forward_far.1), channel_id=1, replica_groups=mesh['row'=32,'col'=8] {'col'}, dimensions={0} | all-to-all | bytes 2097152 | tf_op jit(solution)/shard_map/all_to_all | solution.py:481
  62.9 6.3 %collective-permute-start.11 = (f32[512,128]{1,0:T(8,128)S(1)}, f32[512,128]{1,0:T(8,128)S(1)}, u32[]{:S(2)}, u32[]{:S(2)}) collective-permute-start(f32[512,128]{1,0:T(8,128)S(1)} %bitcast.46), channel_id=1, source_target_pairs={{0,8},{8,0},{16,24},{24,16},{32,40},{40,32},{48,56},{56,48},{64,72... | collective-permute-start | bytes 786440 | tf_op jit(solution)/shard_map/ppermute | solution.py:30
  70.5 1.4 dense.1
  71.9 19.5 %all_to_all.11.refs_4_ = bf16[8,640,128]{2,1,0:T(8,128)(2,1)S(1)} all-to-all(bf16[8,640,128]{2,1,0:T(8,128)(2,1)S(1)} %get-tuple-element.25), channel_id=1, replica_groups=mesh['row'=32,'col'=8] {'col'}, dimensions={0} | all-to-all | bytes 2621440 | tf_op jit(solution)/shard_map/all_to_all | solution.py:485
  91.4 2.2 %backward_far.1 = (bf16[640,128]{1,0:T(8,128)(2,1)S(1)}, bf16[640,128]{1,0:T(8,128)(2,1)S(1)}) custom-call(s32[25]{0:T(128)S(1)} %get-tuple-element.19.refs_0_, s32[25]{0:T(128)S(1)} %fusion.6.refs_1_, bf16[12,256,256]{2,1,0:T(8,128)(2,1)S(1)} %bitcast.42, bf16[12,256,256]{2,1,0:T(8,128)(2,1)S(1)} %collective-permute-done.2.refs_3_, ...), custom_call_target="tpu_custom_call" | custom-call | flops 50331648 | bytes 2097152 | tf_op jit(solution)/shard_map/backward_far/pallas_call | solution.py:402
  93.8 2.7 %collective-permute-start.17 = (bf16[640,128]{1,0:T(8,128)(2,1)S(1)}, bf16[640,128]{1,0:T(8,128)(2,1)S(1)}, u32[]{:S(2)}, u32[]{:S(2)}) collective-permute-start(bf16[640,128]{1,0:T(8,128)(2,1)S(1)} %get-tuple-element.27), channel_id=1, source_target_pairs={{0,224},{8,232},{16,240},{24,248},{32,0},{40,8},{48,16},{56,24},{6... | collective-permute-start | bytes 491528 | tf_op jit(solution)/shard_map/ppermute | solution.py:34
  96.4 3.5 %backward_near.1.parts = bf16[32,256,128]{2,1,0:T(8,128)(2,1)S(1)} custom-call(s32[25]{0:T(128)S(1)} %get-tuple-element.19.refs_0_, s32[25]{0:T(128)S(1)} %fusion.6.refs_1_, bf16[12,256,256]{2,1,0:T(8,128)(2,1)S(1)} %bitcast.43, bf16[12,256,256]{2,1,0:T(8,128)(2,1)S(1)} %collective-permute-done.2.refs_3_, bf16[8,640,128]{2,1,0:T(8,128)(2,1)S(1)} %all_to_all.11.refs_4_), custom_call_target="tpu_custom_call" | custom-call | flops 352321536 | bytes 6291456 | tf_op jit(solution)/shard_map/backward_near/pallas_call | solution.py:402
  100.3 2.7 %collective-permute-start.18 = (bf16[1152,128]{1,0:T(8,128)(2,1)S(1)}, bf16[1152,128]{1,0:T(8,128)(2,1)S(1)}, u32[]{:S(2)}, u32[]{:S(2)}) collective-permute-start(bf16[1152,128]{1,0:T(8,128)(2,1)S(1)} %pad_maximum_fusion.3), channel_id=1, source_target_pairs={{0,224},{8,232},{16,240},{24,248},{32,0},{40,8},{48,16},{56,24},{6... | collective-permute-start | bytes 884744 | tf_op jit(solution)/shard_map/ppermute | solution.py:34
  103.0 3.9 %collective-permute-done.14.up2 = bf16[1152,128]{1,0:T(8,128)(2,1)S(1)} collective-permute-done((bf16[1152,128]{1,0:T(8,128)(2,1)S(1)}, bf16[1152,128]{1,0:T(8,128)(2,1)S(1)}, u32[]{:S(2)}, u32[]{:S(2)}) %collective-permute-start.14) | collective-permute-done | bytes 294944 | tf_op jit(solution)/shard_map/ppermute | solution.py:34
  107.3 2.7 %collective-permute-start.19 = (bf16[1152,128]{1,0:T(8,128)(2,1)S(1)}, bf16[1152,128]{1,0:T(8,128)(2,1)S(1)}, u32[]{:S(2)}, u32[]{:S(2)}) collective-permute-start(bf16[1152,128]{1,0:T(8,128)(2,1)S(1)} %pad_maximum_fusion.4), channel_id=1, source_target_pairs={{0,224},{8,232},{16,240},{24,248},{32,0},{40,8},{48,16},{56,24},{6... | collective-permute-start | bytes 884744 | tf_op jit(solution)/shard_map/ppermute | solution.py:34
  110.0 3.9 %collective-permute-done.15.up3 = bf16[1152,128]{1,0:T(8,128)(2,1)S(1)} collective-permute-done((bf16[1152,128]{1,0:T(8,128)(2,1)S(1)}, bf16[1152,128]{1,0:T(8,128)(2,1)S(1)}, u32[]{:S(2)}, u32[]{:S(2)}) %collective-permute-start.15) | collective-permute-done | bytes 294944 | tf_op jit(solution)/shard_map/ppermute | solution.py:34
  114.3 2.7 %collective-permute-start.20 = (bf16[1024,128]{1,0:T(8,128)(2,1)S(1)}, bf16[1024,128]{1,0:T(8,128)(2,1)S(1)}, u32[]{:S(2)}, u32[]{:S(2)}) collective-permute-start(bf16[1024,128]{1,0:T(8,128)(2,1)S(1)} %fusion), channel_id=1, source_target_pairs={{0,224},{8,232},{16,240},{24,248},{32,0},{40,8},{48,16},{56,24},{6... | collective-permute-start | bytes 786440 | tf_op jit(solution)/shard_map/ppermute | solution.py:34
  117.0 4.3 %collective-permute-done.20.down4 = bf16[1024,128]{1,0:T(8,128)(2,1)S(1)} collective-permute-done((bf16[1024,128]{1,0:T(8,128)(2,1)S(1)}, bf16[1024,128]{1,0:T(8,128)(2,1)S(1)}, u32[]{:S(2)}, u32[]{:S(2)}) %collective-permute-start.20) | collective-permute-done | bytes 262176 | tf_op jit(solution)/shard_map/ppermute | solution.py:34
  121.7 1.5 %collective-permute-start.21 = (bf16[640,128]{1,0:T(8,128)(2,1)S(1)}, bf16[640,128]{1,0:T(8,128)(2,1)S(1)}, u32[]{:S(2)}, u32[]{:S(2)}) collective-permute-start(bf16[640,128]{1,0:T(8,128)(2,1)S(1)} %get-tuple-element.29.sent), channel_id=1, source_target_pairs={{0,16},{8,24},{16,0},{24,8},{32,48},{40,56},{48,32},{56,40},{64,80... | collective-permute-start | bytes 491528 | tf_op jit(solution)/shard_map/ppermute | solution.py:30
  123.3 4.2 %collective-permute-done.21.from_x = bf16[640,128]{1,0:T(8,128)(2,1)S(1)} collective-permute-done((bf16[640,128]{1,0:T(8,128)(2,1)S(1)}, bf16[640,128]{1,0:T(8,128)(2,1)S(1)}, u32[]{:S(2)}, u32[]{:S(2)}) %collective-permute-start.21) | collective-permute-done | bytes 163872 | tf_op jit(solution)/shard_map/ppermute | solution.py:30
  127.5 8.4 %collective-permute-start.22 = (bf16[512,128]{1,0:T(8,128)(2,1)S(1)}, bf16[512,128]{1,0:T(8,128)(2,1)S(1)}, u32[]{:S(2)}, u32[]{:S(2)}) collective-permute-start(bf16[512,128]{1,0:T(8,128)(2,1)S(1)} %get-tuple-element.31), channel_id=1, source_target_pairs={{0,8},{8,0},{16,24},{24,16},{32,40},{40,32},{48,56},{56,48},{64,72... | collective-permute-start | bytes 393224 | tf_op jit(solution)/shard_map/ppermute | solution.py:30
  135.9 1.7 %collective-permute-start.24 = (f32[128,128]{1,0:T(8,128)S(1)}, f32[128,128]{1,0:T(8,128)S(1)}, u32[]{:S(2)}, u32[]{:S(2)}) collective-permute-start(f32[128,128]{1,0:T(8,128)S(1)} %get-tuple-element.32.w_mine), channel_id=1, source_target_pairs={{0,12},{1,13},{2,14},{3,15},{4,8},{5,9},{6,10},{7,11},{8,4},{9,5},... | collective-permute-start | bytes 196616 | tf_op jit(solution)/shard_map/ppermute | solution.py:508
  137.7 1.9 %collective-permute-done.23.w_x = f32[128,128]{1,0:T(8,128)S(1)} collective-permute-done((f32[128,128]{1,0:T(8,128)S(1)}, f32[128,128]{1,0:T(8,128)S(1)}, u32[]{:S(2)}, u32[]{:S(2)}) %collective-permute-start.23) | collective-permute-done | bytes 65568 | tf_op jit(solution)/shard_map/ppermute | solution.py:507
  139.6 1.6 %collective-permute-done.24.w_both = f32[128,128]{1,0:T(8,128)S(1)} collective-permute-done((f32[128,128]{1,0:T(8,128)S(1)}, f32[128,128]{1,0:T(8,128)S(1)}, u32[]{:S(2)}, u32[]{:S(2)}) %collective-permute-start.24) | collective-permute-done | bytes 65568 | tf_op jit(solution)/shard_map/ppermute | solution.py:508
  (65 shorter events, 9.2 us)
Async XLA Ops:
  0.6 39.8 %copy-start = (bf16[1,1,12,256,256]{4,3,2,1,0:T(8,128)(2,1)S(1)}, bf16[1,1,12,256,256]{4,3,2,1,0:T(8,128)(2,1)}, u32[]{:S(2)}) copy-start(bf16[1,1,12,256,256]{4,3,2,1,0:T(8,128)(2,1)} %param.8) | copy-start | bytes 4718596
  0.6 39.7 %collective-permute-start.2 = (bf16[12,256,256]{2,1,0:T(8,128)(2,1)}, bf16[12,256,256]{2,1,0:T(8,128)(2,1)S(1)}, u32[]{:S(2)}, u32[]{:S(2)}) collective-permute-start(bf16[12,256,256]{2,1,0:T(8,128)(2,1)} %bitcast.39), channel_id=1, source_target_pairs={{0,8},{8,0},{16,24},{24,16},{32,40},{40,32},{48,56},{56,48},{64,72... | collective-permute-start | bytes 4718600 | tf_op jit(solution)/shard_map/ppermute | solution.py:30
  4.0 6.8 %collective-permute-start = (bf16[256,256]{1,0:T(8,128)(2,1)}, bf16[256,256]{1,0:T(8,128)(2,1)S(1)}, u32[]{:S(2)}, u32[]{:S(2)}) collective-permute-start(bf16[256,256]{1,0:T(8,128)(2,1)} %bitcast.48), channel_id=1, source_target_pairs={{0,16},{8,24},{16,0},{24,8},{32,48},{40,56},{48,32},{56,40},{64,80... | collective-permute-start | bytes 393224 | tf_op jit(solution)/shard_map/ppermute | solution.py:30
  5.6 0.9 copy-start.3
  6.6 0.7 copy-start.4
  7.2 0.7 copy-start.5
  10.8 2.0 %collective-permute-start.1 = (bf16[528,128]{1,0:T(8,128)(2,1)S(1)}, bf16[528,128]{1,0:T(8,128)(2,1)S(1)}, u32[]{:S(2)}, u32[]{:S(2)}) collective-permute-start(bf16[528,128]{1,0:T(8,128)(2,1)S(1)} %get-tuple-element.22), channel_id=1, source_target_pairs={{0,8},{8,0},{16,24},{24,16},{32,40},{40,32},{48,56},{56,48},{64,72... | collective-permute-start | bytes 405512 | tf_op jit(solution)/shard_map/ppermute | solution.py:30
  12.8 9.2 %collective-permute-start.3 = (bf16[4,256,128]{2,1,0:T(8,128)(2,1)S(1)}, bf16[4,256,128]{2,1,0:T(8,128)(2,1)S(1)}, u32[]{:S(2)}, u32[]{:S(2)}) collective-permute-start(bf16[4,256,128]{2,1,0:T(8,128)(2,1)S(1)} %pad_maximum_fusion.5.refs_4_), channel_id=1, source_target_pairs={{0,224},{8,232},{16,240},{24,248},{32,0},{40,8},{48,16},{56,24},{6... | collective-permute-start | bytes 786440 | tf_op jit(solution)/shard_map/ppermute | solution.py:34
  16.7 8.7 %collective-permute-start.6 = (bf16[4,256,128]{2,1,0:T(8,128)(2,1)S(1)}, bf16[4,256,128]{2,1,0:T(8,128)(2,1)S(1)}, u32[]{:S(2)}, u32[]{:S(2)}) collective-permute-start(bf16[4,256,128]{2,1,0:T(8,128)(2,1)S(1)} %pad_maximum_fusion.5.refs_4_), channel_id=1, source_target_pairs={{0,32},{8,40},{16,48},{24,56},{32,64},{40,72},{48,80},{56,88},{64,... | collective-permute-start | bytes 786440 | tf_op jit(solution)/shard_map/ppermute | solution.py:34
  22.0 7.8 %collective-permute-start.4 = (bf16[4,256,128]{2,1,0:T(8,128)(2,1)S(1)}, bf16[4,256,128]{2,1,0:T(8,128)(2,1)S(1)}, u32[]{:S(2)}, u32[]{:S(2)}) collective-permute-start(bf16[4,256,128]{2,1,0:T(8,128)(2,1)S(1)} %collective-permute-done.3.refs_5_), channel_id=1, source_target_pairs={{0,224},{8,232},{16,240},{24,248},{32,0},{40,8},{48,16},{56,24},{6... | collective-permute-start | bytes 786440 | tf_op jit(solution)/shard_map/ppermute | solution.py:34
  25.4 7.8 %collective-permute-start.7 = (bf16[4,256,128]{2,1,0:T(8,128)(2,1)S(1)}, bf16[4,256,128]{2,1,0:T(8,128)(2,1)S(1)}, u32[]{:S(2)}, u32[]{:S(2)}) collective-permute-start(bf16[4,256,128]{2,1,0:T(8,128)(2,1)S(1)} %collective-permute-done.6.refs_10_), channel_id=1, source_target_pairs={{0,32},{8,40},{16,48},{24,56},{32,64},{40,72},{48,80},{56,88},{64,... | collective-permute-start | bytes 786440 | tf_op jit(solution)/shard_map/ppermute | solution.py:34
  29.9 6.7 %collective-permute-start.5 = (bf16[4,256,128]{2,1,0:T(8,128)(2,1)S(1)}, bf16[4,256,128]{2,1,0:T(8,128)(2,1)S(1)}, u32[]{:S(2)}, u32[]{:S(2)}) collective-permute-start(bf16[4,256,128]{2,1,0:T(8,128)(2,1)S(1)} %collective-permute-done.4.refs_6_), channel_id=1, source_target_pairs={{0,224},{8,232},{16,240},{24,248},{32,0},{40,8},{48,16},{56,24},{6... | collective-permute-start | bytes 786440 | tf_op jit(solution)/shard_map/ppermute | solution.py:34
  33.3 7.0 %collective-permute-start.8 = (bf16[4,256,128]{2,1,0:T(8,128)(2,1)S(1)}, bf16[4,256,128]{2,1,0:T(8,128)(2,1)S(1)}, u32[]{:S(2)}, u32[]{:S(2)}) collective-permute-start(bf16[4,256,128]{2,1,0:T(8,128)(2,1)S(1)} %collective-permute-done.7.refs_9_), channel_id=1, source_target_pairs={{0,32},{8,40},{16,48},{24,56},{32,64},{40,72},{48,80},{56,88},{64,... | collective-permute-start | bytes 786440 | tf_op jit(solution)/shard_map/ppermute | solution.py:34
  36.6 7.1 %collective-permute-start.10 = (bf16[2,256,128]{2,1,0:T(8,128)(2,1)S(1)}, bf16[2,256,128]{2,1,0:T(8,128)(2,1)S(1)}, u32[]{:S(2)}, u32[]{:S(2)}) collective-permute-start(bf16[2,256,128]{2,1,0:T(8,128)(2,1)S(1)} %slice.99), channel_id=1, source_target_pairs={{0,224},{8,232},{16,240},{24,248},{32,0},{40,8},{48,16},{56,24},{6... | collective-permute-start | bytes 393224 | tf_op jit(solution)/shard_map/ppermute | solution.py:34
  40.3 5.1 %collective-permute-start.9 = (bf16[2,256,128]{2,1,0:T(8,128)(2,1)S(1)}, bf16[2,256,128]{2,1,0:T(8,128)(2,1)S(1)}, u32[]{:S(2)}, u32[]{:S(2)}) collective-permute-start(bf16[2,256,128]{2,1,0:T(8,128)(2,1)S(1)} %slice.98), channel_id=1, source_target_pairs={{0,32},{8,40},{16,48},{24,56},{32,64},{40,72},{48,80},{56,88},{64,... | collective-permute-start | bytes 393224 | tf_op jit(solution)/shard_map/ppermute | solution.py:34
  47.7 21.4 %copy-start.2 = (bf16[256,256]{1,0:T(8,128)(2,1)S(1)}, bf16[256,256]{1,0:T(8,128)(2,1)}, u32[]{:S(2)}) copy-start(bf16[256,256]{1,0:T(8,128)(2,1)} %cot_own.1) | copy-start | bytes 393220
  47.8 22.7 %copy-start.1 = (bf16[256,256]{1,0:T(8,128)(2,1)S(1)}, bf16[256,256]{1,0:T(8,128)(2,1)}, u32[]{:S(2)}) copy-start(bf16[256,256]{1,0:T(8,128)(2,1)} %weight.1) | copy-start | bytes 393220
  62.9 7.6 %collective-permute-start.11 = (f32[512,128]{1,0:T(8,128)S(1)}, f32[512,128]{1,0:T(8,128)S(1)}, u32[]{:S(2)}, u32[]{:S(2)}) collective-permute-start(f32[512,128]{1,0:T(8,128)S(1)} %bitcast.46), channel_id=1, source_target_pairs={{0,8},{8,0},{16,24},{24,16},{32,40},{40,32},{48,56},{56,48},{64,72... | collective-permute-start | bytes 786440 | tf_op jit(solution)/shard_map/ppermute | solution.py:30
  69.1 1.3 collective-permute-start.12
  93.7 6.3 %collective-permute-start.13 = (bf16[640,128]{1,0:T(8,128)(2,1)S(1)}, bf16[640,128]{1,0:T(8,128)(2,1)S(1)}, u32[]{:S(2)}, u32[]{:S(2)}) collective-permute-start(bf16[640,128]{1,0:T(8,128)(2,1)S(1)} %get-tuple-element.26.own), channel_id=1, source_target_pairs={{0,32},{8,40},{16,48},{24,56},{32,64},{40,72},{48,80},{56,88},{64,... | collective-permute-start | bytes 491528 | tf_op jit(solution)/shard_map/ppermute | solution.py:34
  93.8 6.2 %collective-permute-start.17 = (bf16[640,128]{1,0:T(8,128)(2,1)S(1)}, bf16[640,128]{1,0:T(8,128)(2,1)S(1)}, u32[]{:S(2)}, u32[]{:S(2)}) collective-permute-start(bf16[640,128]{1,0:T(8,128)(2,1)S(1)} %get-tuple-element.27), channel_id=1, source_target_pairs={{0,224},{8,232},{16,240},{24,248},{32,0},{40,8},{48,16},{56,24},{6... | collective-permute-start | bytes 491528 | tf_op jit(solution)/shard_map/ppermute | solution.py:34
  100.1 6.9 %collective-permute-start.14 = (bf16[1152,128]{1,0:T(8,128)(2,1)S(1)}, bf16[1152,128]{1,0:T(8,128)(2,1)S(1)}, u32[]{:S(2)}, u32[]{:S(2)}) collective-permute-start(bf16[1152,128]{1,0:T(8,128)(2,1)S(1)} %pad_maximum_fusion), channel_id=1, source_target_pairs={{0,32},{8,40},{16,48},{24,56},{32,64},{40,72},{48,80},{56,88},{64,... | collective-permute-start | bytes 884744 | tf_op jit(solution)/shard_map/ppermute | solution.py:34
  100.3 6.9 %collective-permute-start.18 = (bf16[1152,128]{1,0:T(8,128)(2,1)S(1)}, bf16[1152,128]{1,0:T(8,128)(2,1)S(1)}, u32[]{:S(2)}, u32[]{:S(2)}) collective-permute-start(bf16[1152,128]{1,0:T(8,128)(2,1)S(1)} %pad_maximum_fusion.3), channel_id=1, source_target_pairs={{0,224},{8,232},{16,240},{24,248},{32,0},{40,8},{48,16},{56,24},{6... | collective-permute-start | bytes 884744 | tf_op jit(solution)/shard_map/ppermute | solution.py:34
  107.1 6.9 %collective-permute-start.15 = (bf16[1152,128]{1,0:T(8,128)(2,1)S(1)}, bf16[1152,128]{1,0:T(8,128)(2,1)S(1)}, u32[]{:S(2)}, u32[]{:S(2)}) collective-permute-start(bf16[1152,128]{1,0:T(8,128)(2,1)S(1)} %pad_maximum_fusion.1), channel_id=1, source_target_pairs={{0,32},{8,40},{16,48},{24,56},{32,64},{40,72},{48,80},{56,88},{64,... | collective-permute-start | bytes 884744 | tf_op jit(solution)/shard_map/ppermute | solution.py:34
  107.3 6.8 %collective-permute-start.19 = (bf16[1152,128]{1,0:T(8,128)(2,1)S(1)}, bf16[1152,128]{1,0:T(8,128)(2,1)S(1)}, u32[]{:S(2)}, u32[]{:S(2)}) collective-permute-start(bf16[1152,128]{1,0:T(8,128)(2,1)S(1)} %pad_maximum_fusion.4), channel_id=1, source_target_pairs={{0,224},{8,232},{16,240},{24,248},{32,0},{40,8},{48,16},{56,24},{6... | collective-permute-start | bytes 884744 | tf_op jit(solution)/shard_map/ppermute | solution.py:34
  114.1 7.5 %collective-permute-start.16 = (bf16[1152,128]{1,0:T(8,128)(2,1)S(1)}, bf16[1152,128]{1,0:T(8,128)(2,1)S(1)}, u32[]{:S(2)}, u32[]{:S(2)}) collective-permute-start(bf16[1152,128]{1,0:T(8,128)(2,1)S(1)} %pad_maximum_fusion.2), channel_id=1, source_target_pairs={{0,32},{8,40},{16,48},{24,56},{32,64},{40,72},{48,80},{56,88},{64,... | collective-permute-start | bytes 884744 | tf_op jit(solution)/shard_map/ppermute | solution.py:34
  114.3 7.0 %collective-permute-start.20 = (bf16[1024,128]{1,0:T(8,128)(2,1)S(1)}, bf16[1024,128]{1,0:T(8,128)(2,1)S(1)}, u32[]{:S(2)}, u32[]{:S(2)}) collective-permute-start(bf16[1024,128]{1,0:T(8,128)(2,1)S(1)} %fusion), channel_id=1, source_target_pairs={{0,224},{8,232},{16,240},{24,248},{32,0},{40,8},{48,16},{56,24},{6... | collective-permute-start | bytes 786440 | tf_op jit(solution)/shard_map/ppermute | solution.py:34
  121.7 5.8 %collective-permute-start.21 = (bf16[640,128]{1,0:T(8,128)(2,1)S(1)}, bf16[640,128]{1,0:T(8,128)(2,1)S(1)}, u32[]{:S(2)}, u32[]{:S(2)}) collective-permute-start(bf16[640,128]{1,0:T(8,128)(2,1)S(1)} %get-tuple-element.29.sent), channel_id=1, source_target_pairs={{0,16},{8,24},{16,0},{24,8},{32,48},{40,56},{48,32},{56,40},{64,80... | collective-permute-start | bytes 491528 | tf_op jit(solution)/shard_map/ppermute | solution.py:30
  127.5 13.6 %collective-permute-start.22 = (bf16[512,128]{1,0:T(8,128)(2,1)S(1)}, bf16[512,128]{1,0:T(8,128)(2,1)S(1)}, u32[]{:S(2)}, u32[]{:S(2)}) collective-permute-start(bf16[512,128]{1,0:T(8,128)(2,1)S(1)} %get-tuple-element.31), channel_id=1, source_target_pairs={{0,8},{8,0},{16,24},{24,16},{32,40},{40,32},{48,56},{56,48},{64,72... | collective-permute-start | bytes 393224 | tf_op jit(solution)/shard_map/ppermute | solution.py:30
  135.9 3.7 %collective-permute-start.23 = (f32[128,128]{1,0:T(8,128)S(1)}, f32[128,128]{1,0:T(8,128)S(1)}, u32[]{:S(2)}, u32[]{:S(2)}) collective-permute-start(f32[128,128]{1,0:T(8,128)S(1)} %get-tuple-element.32.w_mine), channel_id=1, source_target_pairs={{0,4},{1,5},{2,6},{3,7},{4,0},{5,1},{6,2},{7,3},{8,12},{9,13},{10,... | collective-permute-start | bytes 196616 | tf_op jit(solution)/shard_map/ppermute | solution.py:507
  135.9 5.2 %collective-permute-start.24 = (f32[128,128]{1,0:T(8,128)S(1)}, f32[128,128]{1,0:T(8,128)S(1)}, u32[]{:S(2)}, u32[]{:S(2)}) collective-permute-start(f32[128,128]{1,0:T(8,128)S(1)} %get-tuple-element.32.w_mine), channel_id=1, source_target_pairs={{0,12},{1,13},{2,14},{3,15},{4,8},{5,9},{6,10},{7,11},{8,4},{9,5},... | collective-permute-start | bytes 196616 | tf_op jit(solution)/shard_map/ppermute | solution.py:508

commit v6 on v5

--- a/solution.py
+++ b/solution.py
@@ -81,8 +81,7 @@
         for s in range(SLOTS):
             tile = lists[i][12 + s]
             row = lists[i][s]
-            other = (tile & 3) ^ q
-            place = (((tile >> 2) - z) & 7) * QUAD + ((other & 1) * 2 + (other >> 1))
+            place = (((tile >> 2) - z) & 7) * QUAD + ((tile & 3) ^ q)
             live = (s < count) & (((place >> 2) == 4) == far)
             rows[n] = row * 2 + i
             places[n] = place
@@ -237,60 +236,68 @@
         send_out[c, 2 * TILE + 64 :, :] = piece[:, HALF:]
 
 
-def sum_kernel(parts, own, up1, up2, up3, up4, down1, down2, down3, down4, kept, message, by_step):
+def f32(ref, start, rows=TILE):
+    return ref[start : start + rows, :].astype(jnp.float32)
+
+
+def away_kernel(parts, own, up1, up2, up3, up4, down1, down2, down3, down4, message, w_z):
     z = lax.axis_index("row") >> 2
-    size = QUAD * TILE
-    by_step[0] = own[2 * TILE :, :]
-    by_step[1] = down1[2 * TILE :, :]
-    by_step[7] = up1[2 * TILE :, :]
-    for k, ref in ((2, down2), (3, down3), (4, up4), (5, up3), (6, up2)):
-        by_step[k] = ref[size:, :]
-    w_sum = by_step[(0 - z) & 7].astype(jnp.float32)
+    half, size = 2 * TILE, QUAD * TILE
+    by_step = (
+        (own, half),
+        (down1, half),
+        (down2, size),
+        (down3, size),
+        (up4, half),
+        (up3, size),
+        (up2, size),
+        (up1, half),
+    )
+    for k, (ref, start) in enumerate(by_step):
+        w_z[(k + z) & 7] = ref[start:, :]
+    w_sum = w_z[0].astype(jnp.float32)
     for a in range(1, NZ):
-        w_sum = w_sum + by_step[(a - z) & 7].astype(jnp.float32)
-    message[2 * TILE :, :] = w_sum.astype(jnp.bfloat16)
-    for k in range(QUAD):
-        rows = pl.ds(k * TILE, TILE)
-        total = (
-            parts[k].astype(jnp.float32)
-            + up4[rows, :].astype(jnp.float32)
-            + down4[rows, :].astype(jnp.float32)
-        )
-        if k & 1:
-            message[(k >> 1) * TILE : ((k >> 1) + 1) * TILE, :] = total.astype(jnp.bfloat16)
-        else:
-            kept[k >> 1] = total
-
-
-def middle_kernel(kept, sent, from_x, mine, message, w_mine):
-    mine[...] = (kept[0] + from_x[:TILE, :].astype(jnp.float32)).astype(jnp.bfloat16)
-    message[:TILE, :] = (
-        kept[1] + from_x[TILE : 2 * TILE, :].astype(jnp.float32)
-    ).astype(jnp.bfloat16)
-    w_sum = sent[2 * TILE :, :].astype(jnp.float32) + from_x[2 * TILE :, :].astype(jnp.float32)
-    high, low = split(w_sum)
-    message[TILE : TILE + W_ROWS, :] = high
-    message[TILE + W_ROWS :, :] = low
-    w_mine[...] = high.astype(jnp.float32) + low.astype(jnp.float32)
-
-
-def last_kernel(mine, from_core, w_mine, w_x, w_both, grad_out, w_out):
+        w_sum = w_sum + w_z[a].astype(jnp.float32)
+    message[half:, :] = w_sum.astype(jnp.bfloat16)
+    for k in range(2):
+        start = k * TILE
+        total = parts[2 + k].astype(jnp.float32) + f32(up4, start) + f32(down4, start)
+        message[start : start + TILE, :] = total.astype(jnp.bfloat16)
+
+
+def middle_kernel(parts, up4, down4, sent, from_x, w_lo, w_both, mine, message, w_here):
+    x_lo = lax.axis_index("col") >> 2
+    half = 2 * TILE
+    for k, ref in enumerate((mine, message)):
+        start = k * TILE
+        total = parts[k].astype(jnp.float32) + f32(up4, start) + f32(down4, start)
+        ref[:TILE, :] = (total + f32(from_x, start)).astype(jnp.bfloat16)
+    sums = (
+        f32(sent, half, W_ROWS) + f32(from_x, half, W_ROWS),
+        w_lo[...].astype(jnp.float32) + w_both[...].astype(jnp.float32),
+    )
+    for value, place in zip(sums, (x_lo, 1 - x_lo)):
+        high, low = split(value)
+        w_here[place] = high.astype(jnp.float32) + low.astype(jnp.float32)
+        start = pl.multiple_of(TILE + place * 2 * W_ROWS, W_ROWS)
+        message[pl.ds(start, W_ROWS), :] = high
+        message[pl.ds(start + W_ROWS, W_ROWS), :] = low
+
+
+def last_kernel(mine, from_core, w_here, grad_out, w_out):
     core = lax.axis_index("row") & 1
-    x_lo = lax.axis_index("col") >> 2
     scale = 1.0 / 256.0
-    w_core = from_core[TILE : TILE + W_ROWS, :].astype(jnp.float32) + from_core[
-        TILE + W_ROWS :, :
-    ].astype(jnp.float32)
 
     def place(value, start):
         rows = pl.ds(pl.multiple_of(start, 64), 64)
         w_out[rows, :HALF] = value[:64, :] * scale
         w_out[rows, HALF:] = value[64:, :] * scale
 
-    place(w_mine[...], core * HALF + x_lo * 64)
-    place(w_x[...], core * HALF + (1 - x_lo) * 64)
-    place(w_core, (1 - core) * HALF + x_lo * 64)
-    place(w_both[...], (1 - core) * HALF + (1 - x_lo) * 64)
+    for x_lo in range(2):
+        start = TILE + x_lo * 2 * W_ROWS
+        place(w_here[x_lo], core * HALF + x_lo * 64)
+        w_core = f32(from_core, start, W_ROWS) + f32(from_core, start + W_ROWS, W_ROWS)
+        place(w_core, (1 - core) * HALF + x_lo * 64)
 
     @pl.when(core == 0)
     def _():
@@ -422,36 +429,36 @@
     )(agg_own, agg_other, weight, cot_own, cot_other)
 
 
-def ring_end(parts, *messages):
-    return local(
-        sum_kernel,
-        (shape(2, TILE, HALF, dtype=jnp.float32), shape(2 * TILE + W_ROWS, HALF)),
+def away(parts, *messages):
+    return local(
+        away_kernel,
+        (shape(2 * TILE + W_ROWS, HALF),),
         10,
-        "ring_end",
+        "away",
         scratch=[pltpu.VMEM((NZ, W_ROWS, HALF), jnp.bfloat16)],
-    )(parts, *messages)
-
-
-def middle(kept, sent, from_x):
+    )(parts, *messages)[0]
+
+
+def middle(*operands):
     return local(
         middle_kernel,
         (
             shape(TILE, HALF),
-            shape(TILE + 2 * W_ROWS, HALF),
-            shape(W_ROWS, HALF, dtype=jnp.float32),
+            shape(TILE + 4 * W_ROWS, HALF),
+            shape(2, W_ROWS, HALF, dtype=jnp.float32),
         ),
-        3,
+        7,
         "middle",
-    )(kept, sent, from_x)
-
-
-def last(mine, from_core, w_mine, w_x, w_both):
+    )(*operands)
+
+
+def last(mine, from_core, w_here):
     return local(
         last_kernel,
         (shape(TILE, 2 * HALF), shape(2 * HALF, 2 * HALF, dtype=jnp.float32)),
-        5,
+        3,
         "last",
-    )(mine, from_core, w_mine, w_x, w_both)
+    )(mine, from_core, w_here)
 
 
 def add(a, b):
@@ -466,7 +473,8 @@
     keep, message, own_lists = prepare(tile_row[0, 0], tile_col[0, 0], tile_count, block)
     keep, message = join(keep, message, x_block)
     from_core = quad_permute(message, 1)
-    chunk = jnp.concatenate([keep, from_core[16:].reshape(2, TILE, HALF)], axis=0)
+    core_keep = from_core[16:].reshape(2, TILE, HALF)
+    chunk = jnp.stack([keep[0], core_keep[0], keep[1], core_keep[1]])
     lists = (own_lists, from_core[0, :25].astype(jnp.int32))
     adj1 = quad_permute(adj0, 1)
     cot1 = quad_permute(cotangent, 1)
@@ -495,18 +503,22 @@
     up = [add(parts[2], up2[:size]), up2[size:]]
     down = [add(parts[6], down2[:size]), down2[size:]]
     up3, down3 = z_shift(jnp.concatenate(up), 1), z_shift(jnp.concatenate(down), -1)
-    up4 = z_shift(jnp.concatenate([add(parts[1], up3[:size]), up3[size:]]), 1)
-    down4 = z_shift(add(parts[7], down3[:size]), -1)
-
-    kept, to_x = ring_end(blocks, own, up1, up2, up3, up4, down1, down2, down3, down4)
-    mine, to_core, w_mine = middle(kept, to_x, quad_permute(to_x, 2))
-    across = [(c, c ^ 4) for c in range(NCOL)]
+    up = add(parts[1], up3[:size])
+    down = add(parts[7], down3[:size])
+    up4_away = z_shift(jnp.concatenate([up[half:], up3[size:]]), 1)
+    down4_away = z_shift(down[half:], -1)
+    up4, down4 = z_shift(up[:half], 1), z_shift(down[:half], -1)
+
+    to_x = away(blocks, own, up1, up2, up3, up4_away, down1, down2, down3, down4_away)
+    w_send = to_x[half:]
+    from_x = quad_permute(to_x, 2)
+    w_lo = lax.ppermute(w_send, "col", [(c, c ^ 4) for c in range(NCOL)])
     both = [
-        (r * NCOL + c, (r ^ 1) * NCOL + (c ^ 4)) for r in range(NZ * QUAD) for c in range(NCOL)
+        (r * NCOL + c, (r ^ 2) * NCOL + (c ^ 4)) for r in range(NZ * QUAD) for c in range(NCOL)
     ]
-    w_x = lax.ppermute(w_mine, "col", across)
-    w_both = lax.ppermute(w_mine, ("row", "col"), both)
-    grad, weight_grad = last(mine, quad_permute(to_core, 1), w_mine, w_x, w_both)
+    w_both = lax.ppermute(w_send, ("row", "col"), both)
+    mine, to_core, w_here = middle(blocks, up4, down4, to_x, from_x, w_lo, w_both)
+    grad, weight_grad = last(mine, quad_permute(to_core, 1), w_here)
     return (activated, weight_grad, grad[None])
 
 

time: 142 us -> 142 us (level)
  starting transfers between devices: 49.2 us -> 54.8 us
  waiting for transfers between devices: 38.6 us -> 35.6 us
  Pallas kernels: 15 us -> 12.2 us
    ppermute x16 -> x18, waiting for transfers between devices: 27.1 us -> 32.4 us  [z_shift(): return lax.ppermute(x, 'row', row_pairs(lambda z, q: (z + step, q)))]
    ppermute x7, waiting for transfers between devices: 7.95 us -> 3.12 us  [quad_permute(): return lax.ppermute(x, 'row', row_pairs(lambda z, q: (z, q ^ flip)))]
    ppermute x16 -> x18, starting transfers between devices: 25.7 us -> 29.4 us  [z_shift(): return lax.ppermute(x, 'row', row_pairs(lambda z, q: (z + step, q)))]
    ppermute x2, waiting for transfers between devices: 3.51 us -> 0.01 us  [the longest x1 0.01 us: per_device(): w_lo = lax.ppermute(w_send, 'col', [(c, c ^ 4) for c in range(NCOL)])]
    ppermute x7, starting transfers between devices: 21.8 us -> 24.8 us  [quad_permute(): return lax.ppermute(x, 'row', row_pairs(lambda z, q: (z, q ^ flip)))]
  transfers between devices with their start and end apart: 25 -> 27, of which waited for: 14 -> 14; matrix products, arithmetic and copies ran while one was open for 0% -> 0% of each run, Pallas kernels for 6% -> 4%
where the time goes in v6:
time: 142 us
  starting transfers between devices  54.8 us (39%)
  waiting for transfers between devices  35.6 us (25%)
  blocking collectives  34.5 us (24%)
  Pallas kernels  12.2 us (9%)
  local copies, waits for them, and re-layouts  2.41 us (2%)
  between operations  1.65 us (1%)
    ppermute x18, waiting for transfers between devices, z_shift(): return lax.ppermute(x, 'row', row_pairs(lambda z, q: (z + step, q)))  32.4 us
    ppermute x18, starting transfers between devices, z_shift(): return lax.ppermute(x, 'row', row_pairs(lambda z, q: (z + step, q)))  29.4 us
    ppermute x7, starting transfers between devices, quad_permute(): return lax.ppermute(x, 'row', row_pairs(lambda z, q: (z, q ^ flip)))  24.8 us
    all_to_all x1, blocking collectives, per_device(): received = lax.all_to_all(send, 'col', 0, 0, tiled=True)  19.5 us
    all_to_all x1, blocking collectives, per_device(): shares = lax.all_to_all(partial, 'col', 0, 0, tiled=True)  15 us
    pallas_call x2, Pallas kernels, backward_tiles(): local(functools.partial(backward_kernel, far), (message, message) if far...  4.31 us
    ppermute x7, waiting for transfers between devices, quad_permute(): return lax.ppermute(x, 'row', row_pairs(lambda z, q: (z, q ^ flip)))  3.12 us
  transfers between devices with their start and end apart: 27, of which 14 were waited for; matrix products, arithmetic and copies ran while one was open for 0% of the time, Pallas kernels for 4%

profile of v6, /device:TPU:1, one launch (start us, length us, event | category | flops | bytes accessed | tf_op | source)
XLA Modules:
  0.0 141.9 jit_solution(15151584129624541257)
XLA Ops:
  0.6 3.7 %collective-permute-start = (bf16[256,256]{1,0:T(8,128)(2,1)}, bf16[256,256]{1,0:T(8,128)(2,1)S(1)}, u32[]{:S(2)}, u32[]{:S(2)}) collective-permute-start(bf16[256,256]{1,0:T(8,128)(2,1)} %bitcast.51), channel_id=1, source_target_pairs={{0,16},{8,24},{16,0},{24,8},{32,48},{40,56},{48,32},{56,40},{64,80... | collective-permute-start | bytes 393224 | tf_op jit(solution)/shard_map/ppermute | solution.py:30
  8.1 1.2 prepare.1
  9.4 1.4 collective-permute-start.1
  11.8 4.7 %collective-permute-start.3 = (bf16[4,256,128]{2,1,0:T(8,128)(2,1)S(1)}, bf16[4,256,128]{2,1,0:T(8,128)(2,1)S(1)}, u32[]{:S(2)}, u32[]{:S(2)}) collective-permute-start(bf16[4,256,128]{2,1,0:T(8,128)(2,1)S(1)} %pad_maximum_fusion.4.refs_4_), channel_id=1, source_target_pairs={{0,224},{8,232},{16,240},{24,248},{32,0},{40,8},{48,16},{56,24},{6... | collective-permute-start | bytes 786440 | tf_op jit(solution)/shard_map/ppermute | solution.py:34
  16.5 5.6 %collective-permute-done.3.refs_5_ = bf16[4,256,128]{2,1,0:T(8,128)(2,1)S(1)} collective-permute-done((bf16[4,256,128]{2,1,0:T(8,128)(2,1)S(1)}, bf16[4,256,128]{2,1,0:T(8,128)(2,1)S(1)}, u32[]{:S(2)}, u32[]{:S(2)}) %collective-permute-start.3) | collective-permute-done | bytes 262176 | tf_op jit(solution)/shard_map/ppermute | solution.py:34
  22.1 3.4 %collective-permute-start.4 = (bf16[4,256,128]{2,1,0:T(8,128)(2,1)S(1)}, bf16[4,256,128]{2,1,0:T(8,128)(2,1)S(1)}, u32[]{:S(2)}, u32[]{:S(2)}) collective-permute-start(bf16[4,256,128]{2,1,0:T(8,128)(2,1)S(1)} %collective-permute-done.3.refs_5_), channel_id=1, source_target_pairs={{0,224},{8,232},{16,240},{24,248},{32,0},{40,8},{48,16},{56,24},{6... | collective-permute-start | bytes 786440 | tf_op jit(solution)/shard_map/ppermute | solution.py:34
  25.5 4.6 %collective-permute-done.4.refs_6_ = bf16[4,256,128]{2,1,0:T(8,128)(2,1)S(1)} collective-permute-done((bf16[4,256,128]{2,1,0:T(8,128)(2,1)S(1)}, bf16[4,256,128]{2,1,0:T(8,128)(2,1)S(1)}, u32[]{:S(2)}, u32[]{:S(2)}) %collective-permute-start.4) | collective-permute-done | bytes 262176 | tf_op jit(solution)/shard_map/ppermute | solution.py:34
  30.1 3.4 %collective-permute-start.5 = (bf16[4,256,128]{2,1,0:T(8,128)(2,1)S(1)}, bf16[4,256,128]{2,1,0:T(8,128)(2,1)S(1)}, u32[]{:S(2)}, u32[]{:S(2)}) collective-permute-start(bf16[4,256,128]{2,1,0:T(8,128)(2,1)S(1)} %collective-permute-done.4.refs_6_), channel_id=1, source_target_pairs={{0,224},{8,232},{16,240},{24,248},{32,0},{40,8},{48,16},{56,24},{6... | collective-permute-start | bytes 786440 | tf_op jit(solution)/shard_map/ppermute | solution.py:34
  33.6 3.7 %collective-permute-done.5.refs_7_ = bf16[4,256,128]{2,1,0:T(8,128)(2,1)S(1)} collective-permute-done((bf16[4,256,128]{2,1,0:T(8,128)(2,1)S(1)}, bf16[4,256,128]{2,1,0:T(8,128)(2,1)S(1)}, u32[]{:S(2)}, u32[]{:S(2)}) %collective-permute-start.5) | collective-permute-done | bytes 262176 | tf_op jit(solution)/shard_map/ppermute | solution.py:34
  37.3 3.5 %collective-permute-start.10 = (bf16[2,256,128]{2,1,0:T(8,128)(2,1)S(1)}, bf16[2,256,128]{2,1,0:T(8,128)(2,1)S(1)}, u32[]{:S(2)}, u32[]{:S(2)}) collective-permute-start(bf16[2,256,128]{2,1,0:T(8,128)(2,1)S(1)} %slice.143), channel_id=1, source_target_pairs={{0,224},{8,232},{16,240},{24,248},{32,0},{40,8},{48,16},{56,24},{6... | collective-permute-start | bytes 393224 | tf_op jit(solution)/shard_map/ppermute | solution.py:34
  40.9 2.4 %forward_near.1.refs_4_ = f32[17,256,128]{2,1,0:T(8,128)S(1)} custom-call(s32[25]{0:T(128)S(1)} %get-tuple-element.17.refs_0_, s32[25]{0:T(128)S(1)} %fusion.6.refs_1_, bf16[12,256,256]{2,1,0:T(8,128)(2,1)S(1)} %bitcast.45, bf16[12,256,256]{2,1,0:T(8,128)(2,1)S(1)} %collective-permute-done.2.refs_3_, bf16[4,256,128]{2,1,0:T(8,128)(2,1)S(1)} %pad_maximum_fusion.4.refs_4_, ...), custom_call_target="tpu_custom_call" | custom-call | flops 352321536 | bytes 6291456 | tf_op jit(solution)/shard_map/forward_near/pallas_call | solution.py:374
  43.4 2.5 %collective-permute-done.9.refs_5_ = bf16[2,256,128]{2,1,0:T(8,128)(2,1)S(1)} collective-permute-done((bf16[2,256,128]{2,1,0:T(8,128)(2,1)S(1)}, bf16[2,256,128]{2,1,0:T(8,128)(2,1)S(1)}, u32[]{:S(2)}, u32[]{:S(2)}) %collective-permute-start.9) | collective-permute-done | bytes 131104 | tf_op jit(solution)/shard_map/ppermute | solution.py:34
  45.9 1.8 %forward_far.1 = bf16[8,2,256,128]{3,2,1,0:T(8,128)(2,1)S(1)} custom-call(s32[25]{0:T(128)S(1)} %get-tuple-element.17.refs_0_, s32[25]{0:T(128)S(1)} %fusion.6.refs_1_, bf16[12,256,256]{2,1,0:T(8,128)(2,1)S(1)} %bitcast.46, bf16[12,256,256]{2,1,0:T(8,128)(2,1)S(1)} %collective-permute-done.2.refs_3_, f32[17,256,128]{2,1,0:T(8,128)S(1)} %forward_near.1.refs_4_, ...), custom_call_target="tpu_custom_call" | custom-call | flops 50331648 | bytes 4194304 | tf_op jit(solution)/shard_map/forward_far/pallas_call | solution.py:389
  47.8 15.0 %all_to_all.10 = bf16[8,2,256,128]{3,2,1,0:T(8,128)(2,1)S(1)} all-to-all(bf16[8,2,256,128]{3,2,1,0:T(8,128)(2,1)S(1)} %forward_far.1), channel_id=1, replica_groups=mesh['row'=32,'col'=8] {'col'}, dimensions={0} | all-to-all | bytes 2097152 | tf_op jit(solution)/shard_map/all_to_all | solution.py:489
  62.9 6.0 %collective-permute-start.11 = (f32[512,128]{1,0:T(8,128)S(1)}, f32[512,128]{1,0:T(8,128)S(1)}, u32[]{:S(2)}, u32[]{:S(2)}) collective-permute-start(f32[512,128]{1,0:T(8,128)S(1)} %bitcast.49), channel_id=1, source_target_pairs={{0,8},{8,0},{16,24},{24,16},{32,40},{40,32},{48,56},{56,48},{64,72... | collective-permute-start | bytes 786440 | tf_op jit(solution)/shard_map/ppermute | solution.py:30
  70.3 1.4 dense.1
  71.7 19.5 %all_to_all.11.refs_4_ = bf16[8,640,128]{2,1,0:T(8,128)(2,1)S(1)} all-to-all(bf16[8,640,128]{2,1,0:T(8,128)(2,1)S(1)} %get-tuple-element.23), channel_id=1, replica_groups=mesh['row'=32,'col'=8] {'col'}, dimensions={0} | all-to-all | bytes 2621440 | tf_op jit(solution)/shard_map/all_to_all | solution.py:493
  91.3 1.7 %backward_far.1 = (bf16[640,128]{1,0:T(8,128)(2,1)S(1)}, bf16[640,128]{1,0:T(8,128)(2,1)S(1)}) custom-call(s32[25]{0:T(128)S(1)} %get-tuple-element.17.refs_0_, s32[25]{0:T(128)S(1)} %fusion.6.refs_1_, bf16[12,256,256]{2,1,0:T(8,128)(2,1)S(1)} %bitcast.47, bf16[12,256,256]{2,1,0:T(8,128)(2,1)S(1)} %collective-permute-done.2.refs_3_, ...), custom_call_target="tpu_custom_call" | custom-call | flops 50331648 | bytes 2097152 | tf_op jit(solution)/shard_map/backward_far/pallas_call | solution.py:409
  93.1 2.7 %collective-permute-start.17 = (bf16[640,128]{1,0:T(8,128)(2,1)S(1)}, bf16[640,128]{1,0:T(8,128)(2,1)S(1)}, u32[]{:S(2)}, u32[]{:S(2)}) collective-permute-start(bf16[640,128]{1,0:T(8,128)(2,1)S(1)} %get-tuple-element.25), channel_id=1, source_target_pairs={{0,224},{8,232},{16,240},{24,248},{32,0},{40,8},{48,16},{56,24},{6... | collective-permute-start | bytes 491528 | tf_op jit(solution)/shard_map/ppermute | solution.py:34
  95.7 2.6 %backward_near.1.parts = bf16[32,256,128]{2,1,0:T(8,128)(2,1)S(1)} custom-call(s32[25]{0:T(128)S(1)} %get-tuple-element.17.refs_0_, s32[25]{0:T(128)S(1)} %fusion.6.refs_1_, bf16[12,256,256]{2,1,0:T(8,128)(2,1)S(1)} %bitcast.48, bf16[12,256,256]{2,1,0:T(8,128)(2,1)S(1)} %collective-permute-done.2.refs_3_, bf16[8,640,128]{2,1,0:T(8,128)(2,1)S(1)} %all_to_all.11.refs_4_), custom_call_target="tpu_custom_call" | custom-call | flops 352321536 | bytes 6291456 | tf_op jit(solution)/shard_map/backward_near/pallas_call | solution.py:409
  98.8 2.7 %collective-permute-start.18 = (bf16[1152,128]{1,0:T(8,128)(2,1)S(1)}, bf16[1152,128]{1,0:T(8,128)(2,1)S(1)}, u32[]{:S(2)}, u32[]{:S(2)}) collective-permute-start(bf16[1152,128]{1,0:T(8,128)(2,1)S(1)} %pad_maximum_fusion.2), channel_id=1, source_target_pairs={{0,224},{8,232},{16,240},{24,248},{32,0},{40,8},{48,16},{56,24},{6... | collective-permute-start | bytes 884744 | tf_op jit(solution)/shard_map/ppermute | solution.py:34
  101.5 3.9 %collective-permute-done.14.up2 = bf16[1152,128]{1,0:T(8,128)(2,1)S(1)} collective-permute-done((bf16[1152,128]{1,0:T(8,128)(2,1)S(1)}, bf16[1152,128]{1,0:T(8,128)(2,1)S(1)}, u32[]{:S(2)}, u32[]{:S(2)}) %collective-permute-start.14) | collective-permute-done | bytes 294944 | tf_op jit(solution)/shard_map/ppermute | solution.py:34
  105.8 2.7 %collective-permute-start.19 = (bf16[1152,128]{1,0:T(8,128)(2,1)S(1)}, bf16[1152,128]{1,0:T(8,128)(2,1)S(1)}, u32[]{:S(2)}, u32[]{:S(2)}) collective-permute-start(bf16[1152,128]{1,0:T(8,128)(2,1)S(1)} %pad_maximum_fusion.3), channel_id=1, source_target_pairs={{0,224},{8,232},{16,240},{24,248},{32,0},{40,8},{48,16},{56,24},{6... | collective-permute-start | bytes 884744 | tf_op jit(solution)/shard_map/ppermute | solution.py:34
  108.5 4.0 %collective-permute-done.15.up3 = bf16[1152,128]{1,0:T(8,128)(2,1)S(1)} collective-permute-done((bf16[1152,128]{1,0:T(8,128)(2,1)S(1)}, bf16[1152,128]{1,0:T(8,128)(2,1)S(1)}, u32[]{:S(2)}, u32[]{:S(2)}) %collective-permute-start.15) | collective-permute-done | bytes 294944 | tf_op jit(solution)/shard_map/ppermute | solution.py:34
  112.8 3.0 %collective-permute-start.22 = (bf16[512,128]{1,0:T(8,128)(2,1)S(1)}, bf16[512,128]{1,0:T(8,128)(2,1)S(1)}, u32[]{:S(2)}, u32[]{:S(2)}) collective-permute-start(bf16[512,128]{1,0:T(8,128)(2,1)S(1)} %get-tuple-element.39), channel_id=1, source_target_pairs={{0,224},{8,232},{16,240},{24,248},{32,0},{40,8},{48,16},{56,24},{6... | collective-permute-start | bytes 393224 | tf_op jit(solution)/shard_map/ppermute | solution.py:34
  115.8 3.4 %collective-permute-done.22.down4 = bf16[512,128]{1,0:T(8,128)(2,1)S(1)} collective-permute-done((bf16[512,128]{1,0:T(8,128)(2,1)S(1)}, bf16[512,128]{1,0:T(8,128)(2,1)S(1)}, u32[]{:S(2)}, u32[]{:S(2)}) %collective-permute-start.22) | collective-permute-done | bytes 131104 | tf_op jit(solution)/shard_map/ppermute | solution.py:34
  119.6 3.0 %collective-permute-start.23 = (bf16[640,128]{1,0:T(8,128)(2,1)S(1)}, bf16[640,128]{1,0:T(8,128)(2,1)S(1)}, u32[]{:S(2)}, u32[]{:S(2)}) collective-permute-start(bf16[640,128]{1,0:T(8,128)(2,1)S(1)} %away.1.sent), channel_id=1, source_target_pairs={{0,16},{8,24},{16,0},{24,8},{32,48},{40,56},{48,32},{56,40},{64,80... | collective-permute-start | bytes 491528 | tf_op jit(solution)/shard_map/ppermute | solution.py:30
  122.6 2.8 %collective-permute-start.20 = (bf16[512,128]{1,0:T(8,128)(2,1)S(1)}, bf16[512,128]{1,0:T(8,128)(2,1)S(1)}, u32[]{:S(2)}, u32[]{:S(2)}) collective-permute-start(bf16[512,128]{1,0:T(8,128)(2,1)S(1)} %get-tuple-element.40), channel_id=1, source_target_pairs={{0,224},{8,232},{16,240},{24,248},{32,0},{40,8},{48,16},{56,24},{6... | collective-permute-start | bytes 393224 | tf_op jit(solution)/shard_map/ppermute | solution.py:34
  126.1 1.3 collective-permute-done.20.down4
  127.4 3.1 %collective-permute-done.16.up4 = bf16[512,128]{1,0:T(8,128)(2,1)S(1)} collective-permute-done((bf16[512,128]{1,0:T(8,128)(2,1)S(1)}, bf16[512,128]{1,0:T(8,128)(2,1)S(1)}, u32[]{:S(2)}, u32[]{:S(2)}) %collective-permute-start.16) | collective-permute-done | bytes 131104 | tf_op jit(solution)/shard_map/ppermute | solution.py:34
  130.6 9.5 %collective-permute-start.26 = (bf16[768,128]{1,0:T(8,128)(2,1)S(1)}, bf16[768,128]{1,0:T(8,128)(2,1)S(1)}, u32[]{:S(2)}, u32[]{:S(2)}) collective-permute-start(bf16[768,128]{1,0:T(8,128)(2,1)S(1)} %get-tuple-element.27), channel_id=1, source_target_pairs={{0,8},{8,0},{16,24},{24,16},{32,40},{40,32},{48,56},{56,48},{64,72... | collective-permute-start | bytes 589832 | tf_op jit(solution)/shard_map/ppermute | solution.py:30
  140.1 1.1 collective-permute-done.26.from_core
  (73 shorter events, 8.9 us)
Async XLA Ops:
  0.6 40.3 %copy-start = (bf16[1,1,12,256,256]{4,3,2,1,0:T(8,128)(2,1)S(1)}, bf16[1,1,12,256,256]{4,3,2,1,0:T(8,128)(2,1)}, u32[]{:S(2)}) copy-start(bf16[1,1,12,256,256]{4,3,2,1,0:T(8,128)(2,1)} %param.8) | copy-start | bytes 4718596
  0.6 8.7 %collective-permute-start = (bf16[256,256]{1,0:T(8,128)(2,1)}, bf16[256,256]{1,0:T(8,128)(2,1)S(1)}, u32[]{:S(2)}, u32[]{:S(2)}) collective-permute-start(bf16[256,256]{1,0:T(8,128)(2,1)} %bitcast.51), channel_id=1, source_target_pairs={{0,16},{8,24},{16,0},{24,8},{32,48},{40,56},{48,32},{56,40},{64,80... | collective-permute-start | bytes 393224 | tf_op jit(solution)/shard_map/ppermute | solution.py:30
  4.3 36.6 %collective-permute-start.2 = (bf16[12,256,256]{2,1,0:T(8,128)(2,1)}, bf16[12,256,256]{2,1,0:T(8,128)(2,1)S(1)}, u32[]{:S(2)}, u32[]{:S(2)}) collective-permute-start(bf16[12,256,256]{2,1,0:T(8,128)(2,1)} %bitcast.44), channel_id=1, source_target_pairs={{0,8},{8,0},{16,24},{24,16},{32,40},{40,32},{48,56},{56,48},{64,72... | collective-permute-start | bytes 4718600 | tf_op jit(solution)/shard_map/ppermute | solution.py:30
  5.9 0.9 copy-start.3
  6.8 0.7 copy-start.4
  9.4 2.4 %collective-permute-start.1 = (bf16[528,128]{1,0:T(8,128)(2,1)S(1)}, bf16[528,128]{1,0:T(8,128)(2,1)S(1)}, u32[]{:S(2)}, u32[]{:S(2)}) collective-permute-start(bf16[528,128]{1,0:T(8,128)(2,1)S(1)} %get-tuple-element.20), channel_id=1, source_target_pairs={{0,8},{8,0},{16,24},{24,16},{32,40},{40,32},{48,56},{56,48},{64,72... | collective-permute-start | bytes 405512 | tf_op jit(solution)/shard_map/ppermute | solution.py:30
  11.8 10.3 %collective-permute-start.3 = (bf16[4,256,128]{2,1,0:T(8,128)(2,1)S(1)}, bf16[4,256,128]{2,1,0:T(8,128)(2,1)S(1)}, u32[]{:S(2)}, u32[]{:S(2)}) collective-permute-start(bf16[4,256,128]{2,1,0:T(8,128)(2,1)S(1)} %pad_maximum_fusion.4.refs_4_), channel_id=1, source_target_pairs={{0,224},{8,232},{16,240},{24,248},{32,0},{40,8},{48,16},{56,24},{6... | collective-permute-start | bytes 786440 | tf_op jit(solution)/shard_map/ppermute | solution.py:34
  16.5 9.0 %collective-permute-start.6 = (bf16[4,256,128]{2,1,0:T(8,128)(2,1)S(1)}, bf16[4,256,128]{2,1,0:T(8,128)(2,1)S(1)}, u32[]{:S(2)}, u32[]{:S(2)}) collective-permute-start(bf16[4,256,128]{2,1,0:T(8,128)(2,1)S(1)} %pad_maximum_fusion.4.refs_4_), channel_id=1, source_target_pairs={{0,32},{8,40},{16,48},{24,56},{32,64},{40,72},{48,80},{56,88},{64,... | collective-permute-start | bytes 786440 | tf_op jit(solution)/shard_map/ppermute | solution.py:34
  22.1 8.1 %collective-permute-start.4 = (bf16[4,256,128]{2,1,0:T(8,128)(2,1)S(1)}, bf16[4,256,128]{2,1,0:T(8,128)(2,1)S(1)}, u32[]{:S(2)}, u32[]{:S(2)}) collective-permute-start(bf16[4,256,128]{2,1,0:T(8,128)(2,1)S(1)} %collective-permute-done.3.refs_5_), channel_id=1, source_target_pairs={{0,224},{8,232},{16,240},{24,248},{32,0},{40,8},{48,16},{56,24},{6... | collective-permute-start | bytes 786440 | tf_op jit(solution)/shard_map/ppermute | solution.py:34
  25.5 8.1 %collective-permute-start.7 = (bf16[4,256,128]{2,1,0:T(8,128)(2,1)S(1)}, bf16[4,256,128]{2,1,0:T(8,128)(2,1)S(1)}, u32[]{:S(2)}, u32[]{:S(2)}) collective-permute-start(bf16[4,256,128]{2,1,0:T(8,128)(2,1)S(1)} %collective-permute-done.6.refs_10_), channel_id=1, source_target_pairs={{0,32},{8,40},{16,48},{24,56},{32,64},{40,72},{48,80},{56,88},{64,... | collective-permute-start | bytes 786440 | tf_op jit(solution)/shard_map/ppermute | solution.py:34
  30.1 7.1 %collective-permute-start.5 = (bf16[4,256,128]{2,1,0:T(8,128)(2,1)S(1)}, bf16[4,256,128]{2,1,0:T(8,128)(2,1)S(1)}, u32[]{:S(2)}, u32[]{:S(2)}) collective-permute-start(bf16[4,256,128]{2,1,0:T(8,128)(2,1)S(1)} %collective-permute-done.4.refs_6_), channel_id=1, source_target_pairs={{0,224},{8,232},{16,240},{24,248},{32,0},{40,8},{48,16},{56,24},{6... | collective-permute-start | bytes 786440 | tf_op jit(solution)/shard_map/ppermute | solution.py:34
  33.6 7.2 %collective-permute-start.8 = (bf16[4,256,128]{2,1,0:T(8,128)(2,1)S(1)}, bf16[4,256,128]{2,1,0:T(8,128)(2,1)S(1)}, u32[]{:S(2)}, u32[]{:S(2)}) collective-permute-start(bf16[4,256,128]{2,1,0:T(8,128)(2,1)S(1)} %collective-permute-done.7.refs_9_), channel_id=1, source_target_pairs={{0,32},{8,40},{16,48},{24,56},{32,64},{40,72},{48,80},{56,88},{64,... | collective-permute-start | bytes 786440 | tf_op jit(solution)/shard_map/ppermute | solution.py:34
  37.3 6.1 %collective-permute-start.10 = (bf16[2,256,128]{2,1,0:T(8,128)(2,1)S(1)}, bf16[2,256,128]{2,1,0:T(8,128)(2,1)S(1)}, u32[]{:S(2)}, u32[]{:S(2)}) collective-permute-start(bf16[2,256,128]{2,1,0:T(8,128)(2,1)S(1)} %slice.143), channel_id=1, source_target_pairs={{0,224},{8,232},{16,240},{24,248},{32,0},{40,8},{48,16},{56,24},{6... | collective-permute-start | bytes 393224 | tf_op jit(solution)/shard_map/ppermute | solution.py:34
  40.8 5.1 %collective-permute-start.9 = (bf16[2,256,128]{2,1,0:T(8,128)(2,1)S(1)}, bf16[2,256,128]{2,1,0:T(8,128)(2,1)S(1)}, u32[]{:S(2)}, u32[]{:S(2)}) collective-permute-start(bf16[2,256,128]{2,1,0:T(8,128)(2,1)S(1)} %slice.142), channel_id=1, source_target_pairs={{0,32},{8,40},{16,48},{24,56},{32,64},{40,72},{48,80},{56,88},{64,... | collective-permute-start | bytes 393224 | tf_op jit(solution)/shard_map/ppermute | solution.py:34
  47.8 21.2 %copy-start.2 = (bf16[256,256]{1,0:T(8,128)(2,1)S(1)}, bf16[256,256]{1,0:T(8,128)(2,1)}, u32[]{:S(2)}) copy-start(bf16[256,256]{1,0:T(8,128)(2,1)} %cot_own.1) | copy-start | bytes 393220
  47.8 22.5 %copy-start.1 = (bf16[256,256]{1,0:T(8,128)(2,1)S(1)}, bf16[256,256]{1,0:T(8,128)(2,1)}, u32[]{:S(2)}) copy-start(bf16[256,256]{1,0:T(8,128)(2,1)} %weight.1) | copy-start | bytes 393220
  62.9 7.4 %collective-permute-start.11 = (f32[512,128]{1,0:T(8,128)S(1)}, f32[512,128]{1,0:T(8,128)S(1)}, u32[]{:S(2)}, u32[]{:S(2)}) collective-permute-start(f32[512,128]{1,0:T(8,128)S(1)} %bitcast.49), channel_id=1, source_target_pairs={{0,8},{8,0},{16,24},{24,16},{32,40},{40,32},{48,56},{56,48},{64,72... | collective-permute-start | bytes 786440 | tf_op jit(solution)/shard_map/ppermute | solution.py:30
  69.0 1.3 collective-permute-start.12
  93.0 5.5 %collective-permute-start.13 = (bf16[640,128]{1,0:T(8,128)(2,1)S(1)}, bf16[640,128]{1,0:T(8,128)(2,1)S(1)}, u32[]{:S(2)}, u32[]{:S(2)}) collective-permute-start(bf16[640,128]{1,0:T(8,128)(2,1)S(1)} %get-tuple-element.24.own), channel_id=1, source_target_pairs={{0,32},{8,40},{16,48},{24,56},{32,64},{40,72},{48,80},{56,88},{64,... | collective-permute-start | bytes 491528 | tf_op jit(solution)/shard_map/ppermute | solution.py:34
  93.1 5.4 %collective-permute-start.17 = (bf16[640,128]{1,0:T(8,128)(2,1)S(1)}, bf16[640,128]{1,0:T(8,128)(2,1)S(1)}, u32[]{:S(2)}, u32[]{:S(2)}) collective-permute-start(bf16[640,128]{1,0:T(8,128)(2,1)S(1)} %get-tuple-element.25), channel_id=1, source_target_pairs={{0,224},{8,232},{16,240},{24,248},{32,0},{40,8},{48,16},{56,24},{6... | collective-permute-start | bytes 491528 | tf_op jit(solution)/shard_map/ppermute | solution.py:34
  98.5 6.9 %collective-permute-start.14 = (bf16[1152,128]{1,0:T(8,128)(2,1)S(1)}, bf16[1152,128]{1,0:T(8,128)(2,1)S(1)}, u32[]{:S(2)}, u32[]{:S(2)}) collective-permute-start(bf16[1152,128]{1,0:T(8,128)(2,1)S(1)} %pad_maximum_fusion), channel_id=1, source_target_pairs={{0,32},{8,40},{16,48},{24,56},{32,64},{40,72},{48,80},{56,88},{64,... | collective-permute-start | bytes 884744 | tf_op jit(solution)/shard_map/ppermute | solution.py:34
  98.8 6.9 %collective-permute-start.18 = (bf16[1152,128]{1,0:T(8,128)(2,1)S(1)}, bf16[1152,128]{1,0:T(8,128)(2,1)S(1)}, u32[]{:S(2)}, u32[]{:S(2)}) collective-permute-start(bf16[1152,128]{1,0:T(8,128)(2,1)S(1)} %pad_maximum_fusion.2), channel_id=1, source_target_pairs={{0,224},{8,232},{16,240},{24,248},{32,0},{40,8},{48,16},{56,24},{6... | collective-permute-start | bytes 884744 | tf_op jit(solution)/shard_map/ppermute | solution.py:34
  105.5 6.9 %collective-permute-start.15 = (bf16[1152,128]{1,0:T(8,128)(2,1)S(1)}, bf16[1152,128]{1,0:T(8,128)(2,1)S(1)}, u32[]{:S(2)}, u32[]{:S(2)}) collective-permute-start(bf16[1152,128]{1,0:T(8,128)(2,1)S(1)} %pad_maximum_fusion.1), channel_id=1, source_target_pairs={{0,32},{8,40},{16,48},{24,56},{32,64},{40,72},{48,80},{56,88},{64,... | collective-permute-start | bytes 884744 | tf_op jit(solution)/shard_map/ppermute | solution.py:34
  105.8 6.9 %collective-permute-start.19 = (bf16[1152,128]{1,0:T(8,128)(2,1)S(1)}, bf16[1152,128]{1,0:T(8,128)(2,1)S(1)}, u32[]{:S(2)}, u32[]{:S(2)}) collective-permute-start(bf16[1152,128]{1,0:T(8,128)(2,1)S(1)} %pad_maximum_fusion.3), channel_id=1, source_target_pairs={{0,224},{8,232},{16,240},{24,248},{32,0},{40,8},{48,16},{56,24},{6... | collective-permute-start | bytes 884744 | tf_op jit(solution)/shard_map/ppermute | solution.py:34
  112.6 6.9 %collective-permute-start.21 = (bf16[640,128]{1,0:T(8,128)(2,1)S(1)}, bf16[640,128]{1,0:T(8,128)(2,1)S(1)}, u32[]{:S(2)}, u32[]{:S(2)}) collective-permute-start(bf16[640,128]{1,0:T(8,128)(2,1)S(1)} %pad_maximum_fusion.5), channel_id=1, source_target_pairs={{0,32},{8,40},{16,48},{24,56},{32,64},{40,72},{48,80},{56,88},{64,... | collective-permute-start | bytes 491528 | tf_op jit(solution)/shard_map/ppermute | solution.py:34
  112.8 6.4 %collective-permute-start.22 = (bf16[512,128]{1,0:T(8,128)(2,1)S(1)}, bf16[512,128]{1,0:T(8,128)(2,1)S(1)}, u32[]{:S(2)}, u32[]{:S(2)}) collective-permute-start(bf16[512,128]{1,0:T(8,128)(2,1)S(1)} %get-tuple-element.39), channel_id=1, source_target_pairs={{0,224},{8,232},{16,240},{24,248},{32,0},{40,8},{48,16},{56,24},{6... | collective-permute-start | bytes 393224 | tf_op jit(solution)/shard_map/ppermute | solution.py:34
  119.6 10.9 %collective-permute-start.23 = (bf16[640,128]{1,0:T(8,128)(2,1)S(1)}, bf16[640,128]{1,0:T(8,128)(2,1)S(1)}, u32[]{:S(2)}, u32[]{:S(2)}) collective-permute-start(bf16[640,128]{1,0:T(8,128)(2,1)S(1)} %away.1.sent), channel_id=1, source_target_pairs={{0,16},{8,24},{16,0},{24,8},{32,48},{40,56},{48,32},{56,40},{64,80... | collective-permute-start | bytes 491528 | tf_op jit(solution)/shard_map/ppermute | solution.py:30
  122.6 4.8 %collective-permute-start.20 = (bf16[512,128]{1,0:T(8,128)(2,1)S(1)}, bf16[512,128]{1,0:T(8,128)(2,1)S(1)}, u32[]{:S(2)}, u32[]{:S(2)}) collective-permute-start(bf16[512,128]{1,0:T(8,128)(2,1)S(1)} %get-tuple-element.40), channel_id=1, source_target_pairs={{0,224},{8,232},{16,240},{24,248},{32,0},{40,8},{48,16},{56,24},{6... | collective-permute-start | bytes 393224 | tf_op jit(solution)/shard_map/ppermute | solution.py:34
  125.4 5.0 %collective-permute-start.16 = (bf16[512,128]{1,0:T(8,128)(2,1)S(1)}, bf16[512,128]{1,0:T(8,128)(2,1)S(1)}, u32[]{:S(2)}, u32[]{:S(2)}) collective-permute-start(bf16[512,128]{1,0:T(8,128)(2,1)S(1)} %get-tuple-element.42), channel_id=1, source_target_pairs={{0,32},{8,40},{16,48},{24,56},{32,64},{40,72},{48,80},{56,88},{64,... | collective-permute-start | bytes 393224 | tf_op jit(solution)/shard_map/ppermute | solution.py:34
  125.4 5.0 %collective-permute-start.24 = (bf16[128,128]{1,0:T(8,128)(2,1)S(1)}, bf16[128,128]{1,0:T(8,128)(2,1)S(1)}, u32[]{:S(2)}, u32[]{:S(2)}) collective-permute-start(bf16[128,128]{1,0:T(8,128)(2,1)S(1)} %slice.167), channel_id=1, source_target_pairs={{0,4},{1,5},{2,6},{3,7},{4,0},{5,1},{6,2},{7,3},{8,12},{9,13},{10,... | collective-permute-start | bytes 98312 | tf_op jit(solution)/shard_map/ppermute | solution.py:515
  125.4 5.0 %collective-permute-start.25 = (bf16[128,128]{1,0:T(8,128)(2,1)S(1)}, bf16[128,128]{1,0:T(8,128)(2,1)S(1)}, u32[]{:S(2)}, u32[]{:S(2)}) collective-permute-start(bf16[128,128]{1,0:T(8,128)(2,1)S(1)} %slice.167), channel_id=1, source_target_pairs={{0,20},{1,21},{2,22},{3,23},{4,16},{5,17},{6,18},{7,19},{8,28},{9,... | collective-permute-start | bytes 98312 | tf_op jit(solution)/shard_map/ppermute | solution.py:519
  130.6 10.6 %collective-permute-start.26 = (bf16[768,128]{1,0:T(8,128)(2,1)S(1)}, bf16[768,128]{1,0:T(8,128)(2,1)S(1)}, u32[]{:S(2)}, u32[]{:S(2)}) collective-permute-start(bf16[768,128]{1,0:T(8,128)(2,1)S(1)} %get-tuple-element.27), channel_id=1, source_target_pairs={{0,8},{8,0},{16,24},{24,16},{32,40},{40,32},{48,56},{56,48},{64,72... | collective-permute-start | bytes 589832 | tf_op jit(solution)/shard_map/ppermute | solution.py:30
  (1 other events, 0.7 us)

commit v7 on v6

--- a/solution.py
+++ b/solution.py
@@ -56,23 +56,7 @@
     message[:16, :] = values.astype(jnp.bfloat16)
 
 
-def join_kernel(own_keep, own_message, x_block, keep, message):
-    core = lax.axis_index("row") & 1
-    keep[0] = own_keep[...]
-    message[: TILE + 16, :] = own_message[...]
-
-    @pl.when(core == 0)
-    def _():
-        keep[1] = x_block[:, :HALF]
-        message[TILE + 16 :, :] = x_block[:, HALF:]
-
-    @pl.when(core == 1)
-    def _():
-        keep[1] = x_block[:, HALF:]
-        message[TILE + 16 :, :] = x_block[:, :HALF]
-
-
-def list_slots(lists, adj_refs, adj_vmem, adj_sem, rows, places, far, dummy):
+def list_slots(lists, adj_refs, adj_vmem, adj_sem, rows, places, chosen, dummy):
     device = lax.axis_index("row")
     z, q = device >> 2, device & 3
     n = jnp.int32(0)
@@ -82,7 +66,7 @@
             tile = lists[i][12 + s]
             row = lists[i][s]
             place = (((tile >> 2) - z) & 7) * QUAD + ((tile & 3) ^ q)
-            live = (s < count) & (((place >> 2) == 4) == far)
+            live = (s < count) & chosen(place)
             rows[n] = row * 2 + i
             places[n] = place
 
@@ -113,16 +97,38 @@
             add_to(j, value)
 
 
+NEAR_PIECES = (
+    [(0, 0, 2, 0), (1, 0, 2, 2)]
+    + [(2, 0, 2, 28), (3, 0, 2, 4), (4, 0, 2, 30), (4, 2, 2, 6)]
+    + [(5, 0, 2, 24), (6, 0, 2, 8), (7, 0, 2, 26), (7, 2, 2, 10)]
+    + [(8, 0, 2, 20), (9, 0, 2, 12), (10, 0, 2, 22), (10, 2, 2, 14)]
+    + [(11, 0, 1, 16), (12, 0, 1, 17)]
+)
+
+
 def forward_near_kernel(*refs):
-    lists, (adj0, adj1), refs = refs[:2], refs[2:4], refs[4:]
-    pieces, (acc, panel, adj_vmem, rows, places, panel_sem, adj_sem) = refs[:7], refs[7:]
+    lists, (adj0, adj1), pieces, refs = refs[:2], refs[2:4], refs[4:17], refs[17:]
+    acc, panel, adj_vmem, rows, places, panel_sem, adj_sem = refs
     copies = [
-        pltpu.make_async_copy(piece, panel.at[pl.ds(place * QUAD, QUAD)], panel_sem.at[place])
-        for place, piece in zip((0, 1, 2, 3, 5, 6, 7), pieces)
+        pltpu.make_async_copy(
+            pieces[piece].at[pl.ds(start, blocks)],
+            panel.at[pl.ds(place, blocks)],
+            panel_sem.at[k],
+        )
+        for k, (piece, start, blocks, place) in enumerate(NEAR_PIECES)
     ]
     for copy in copies:
         copy.start()
-    n = list_slots(lists, (adj0, adj1), adj_vmem, adj_sem, rows, places, False, (16, 0))
+    n = list_slots(
+        lists,
+        (adj0, adj1),
+        adj_vmem,
+        adj_sem,
+        rows,
+        places,
+        lambda place: (place >> 1) != 9,
+        (16, 0),
+    )
     acc[...] = jnp.zeros_like(acc)
     for copy in copies:
         copy.wait()
@@ -138,14 +144,21 @@
 
 def forward_far_kernel(*refs):
     lists, refs = refs[:2], refs[2:]
-    adj0, adj1, near, far_a, far_b, out, acc, far, adj_vmem, rows, places, adj_sem = refs
-    n = list_slots(lists, (adj0, adj1), adj_vmem, adj_sem, rows, places, True, (16, 16))
-    far[:2] = far_a[...]
-    far[2:] = far_b[...]
+    adj0, adj1, near, far, out, acc, adj_vmem, rows, places, adj_sem = refs
+    n = list_slots(
+        lists,
+        (adj0, adj1),
+        adj_vmem,
+        adj_sem,
+        rows,
+        places,
+        lambda place: (place >> 1) == 9,
+        (16, 18),
+    )
     acc[...] = near[...]
 
     def product(j):
-        return jnp.dot(adj_vmem[j], far[places[j] - 16], preferred_element_type=jnp.float32)
+        return jnp.dot(adj_vmem[j], far[places[j] - 18], preferred_element_type=jnp.float32)
 
     def add_to(j, value):
         acc[rows[j]] += value
@@ -164,7 +177,14 @@
     base = 16 if far else 0
     spare = acc.shape[0] - 1
     n = list_slots(
-        lists, (adj0, adj1), adj_vmem, adj_sem, rows, places, far, (0, base + spare)
+        lists,
+        (adj0, adj1),
+        adj_vmem,
+        adj_sem,
+        rows,
+        places,
+        lambda place: ((place >> 2) == 4) == far,
+        (0, base + spare),
     )
     acc[...] = jnp.zeros_like(acc)
 
@@ -181,17 +201,28 @@
         acc[places[j] - base] += value
 
     slot_products(n, adj0, adj_vmem, adj_sem, product, add_to)
-    if not far:
-        outs[0][...] = acc[:spare].astype(jnp.bfloat16)
+
+    def write(out, start, place):
+        for k in range(2):
+            rows = pl.ds(start + k * TILE, TILE)
+            out[rows, :] = acc[place - base + k].astype(jnp.bfloat16)
+
+    if far:
+        own, to_x = outs
+        write(own, 0, 16)
+        write(to_x, 0, 18)
+        piece = back[0, 2 * TILE :, :].astype(jnp.float32)
+        for c in range(1, NCOL):
+            piece = piece + back[c, 2 * TILE :, :].astype(jnp.float32)
+        to_x[2 * TILE :, :] = piece.astype(jnp.bfloat16)
         return
-    for k in range(QUAD):
-        rows = pl.ds((k & 1) * TILE, TILE)
-        outs[k >> 1][rows, :] = acc[k].astype(jnp.bfloat16)
-    piece = back[0, 2 * TILE :, :].astype(jnp.float32)
-    for c in range(1, NCOL):
-        piece = piece + back[c, 2 * TILE :, :].astype(jnp.float32)
-    for out in outs:
-        out[2 * TILE :, :] = piece.astype(jnp.bfloat16)
+    own, to_x3, to_x2, to_x1, to_x0 = outs
+    for z in (0, 1, 2, 3, 5, 6, 7):
+        write(own, z * 2 * TILE, z * QUAD)
+    for step, out in ((3, to_x3), (2, to_x2), (1, to_x1)):
+        write(out, 0, step * QUAD + 2)
+        write(out, 2 * TILE, (NZ - step) * QUAD + 2)
+    write(to_x0, 0, 2)
 
 
 def split(x):
@@ -240,44 +271,47 @@
     return ref[start : start + rows, :].astype(jnp.float32)
 
 
-def away_kernel(parts, own, up1, up2, up3, up4, down1, down2, down3, down4, message, w_z):
-    z = lax.axis_index("row") >> 2
-    half, size = 2 * TILE, QUAD * TILE
-    by_step = (
-        (own, half),
-        (down1, half),
-        (down2, size),
-        (down3, size),
-        (up4, half),
-        (up3, size),
-        (up2, size),
-        (up1, half),
-    )
-    for k, (ref, start) in enumerate(by_step):
-        w_z[(k + z) & 7] = ref[start:, :]
-    w_sum = w_z[0].astype(jnp.float32)
-    for a in range(1, NZ):
-        w_sum = w_sum + w_z[a].astype(jnp.float32)
-    message[half:, :] = w_sum.astype(jnp.bfloat16)
-    for k in range(2):
-        start = k * TILE
-        total = parts[2 + k].astype(jnp.float32) + f32(up4, start) + f32(down4, start)
-        message[start : start + TILE, :] = total.astype(jnp.bfloat16)
-
-
-def middle_kernel(parts, up4, down4, sent, from_x, w_lo, w_both, mine, message, w_here):
-    x_lo = lax.axis_index("col") >> 2
+def enter_kernel(own, sent, from_x, w_lo, w_both, up, down):
     half = 2 * TILE
-    for k, ref in enumerate((mine, message)):
-        start = k * TILE
-        total = parts[k].astype(jnp.float32) + f32(up4, start) + f32(down4, start)
-        ref[:TILE, :] = (total + f32(from_x, start)).astype(jnp.bfloat16)
     sums = (
         f32(sent, half, W_ROWS) + f32(from_x, half, W_ROWS),
         w_lo[...].astype(jnp.float32) + w_both[...].astype(jnp.float32),
     )
-    for value, place in zip(sums, (x_lo, 1 - x_lo)):
-        high, low = split(value)
+    for k, out in enumerate((up, down)):
+        start = k * TILE
+        out[:TILE, :] = (f32(own, start) + f32(from_x, start)).astype(jnp.bfloat16)
+        for j, value in enumerate(sums):
+            rows = pl.ds(TILE + j * W_ROWS, W_ROWS)
+            out[rows, :] = value.astype(jnp.bfloat16)
+
+
+def leave_kernel(
+    own, from_x, up, up1, up2, up3, up4, down1, down2, down3, down4, mine, message, w_here, by_step
+):
+    z = lax.axis_index("row") >> 2
+    x_lo = lax.axis_index("col") >> 2
+    half = 2 * TILE
+    pieces = (
+        (up, TILE),
+        (down1, TILE),
+        (down2, half),
+        (down3, half),
+        (up4, half),
+        (up3, half),
+        (up2, half),
+        (up1, TILE),
+    )
+    for k, (ref, start) in enumerate(pieces):
+        by_step[(k + z) & 7] = ref[start : start + 2 * W_ROWS, :]
+    w_sum = by_step[0].astype(jnp.float32)
+    for a in range(1, NZ):
+        w_sum = w_sum + by_step[a].astype(jnp.float32)
+    for k, ref in enumerate((mine, message)):
+        start = k * TILE
+        total = f32(own, start) + f32(from_x, start) + f32(up4, start) + f32(down4, start)
+        ref[:TILE, :] = total.astype(jnp.bfloat16)
+    for k, place in enumerate((x_lo, 1 - x_lo)):
+        high, low = split(w_sum[k * W_ROWS : (k + 1) * W_ROWS])
         w_here[place] = high.astype(jnp.float32) + low.astype(jnp.float32)
         start = pl.multiple_of(TILE + place * 2 * W_ROWS, W_ROWS)
         message[pl.ds(start, W_ROWS), :] = high
@@ -364,56 +398,50 @@
     )(rows, cols, count, block)
 
 
-def join(own_keep, own_message, x_block):
-    return local(
-        join_kernel, (shape(2, TILE, HALF), shape(2 * TILE + 16, HALF)), 3, "join"
-    )(own_keep, own_message, x_block)
-
-
 def forward_near(lists, adj0, adj1, pieces):
     return local(
         forward_near_kernel,
         (shape(17, TILE, HALF, dtype=jnp.float32),),
-        11,
+        17,
         "forward_near",
         scalars=2,
-        any_in=9,
+        any_in=15,
         scratch=[pltpu.VMEM((NZ * QUAD, TILE, HALF), jnp.bfloat16)]
         + SLOT_SCRATCH
-        + [pltpu.SemaphoreType.DMA((NZ,)), pltpu.SemaphoreType.DMA((LIST,))],
-        cost=cost(21, 6),
+        + [pltpu.SemaphoreType.DMA((len(NEAR_PIECES),)), pltpu.SemaphoreType.DMA((LIST,))],
+        cost=cost(22, 6),
     )(*lists, adj0, adj1, *pieces)[0]
 
 
-def forward_far(lists, adj0, adj1, near, far_a, far_b):
+def forward_far(lists, adj0, adj1, near, far):
     return local(
         forward_far_kernel,
         (shape(8, 2, TILE, HALF),),
-        7,
+        6,
         "forward_far",
         scalars=2,
         any_in=2,
-        scratch=[
-            pltpu.VMEM((17, TILE, HALF), jnp.float32),
-            pltpu.VMEM((QUAD, TILE, HALF), jnp.bfloat16),
-        ]
+        scratch=[pltpu.VMEM((17, TILE, HALF), jnp.float32)]
         + SLOT_SCRATCH
         + [pltpu.SemaphoreType.DMA((LIST,))],
-        cost=cost(3, 4),
-    )(*lists, adj0, adj1, near, far_a, far_b)[0]
+        cost=cost(2, 4),
+    )(*lists, adj0, adj1, near, far)[0]
 
 
 def backward_tiles(lists, adj0, adj1, back, far):
-    places = QUAD if far else NZ * QUAD
-    message = shape(2 * TILE + W_ROWS, HALF)
+    half = 2 * TILE
+    if far:
+        outs = (shape(half, HALF), shape(half + W_ROWS, HALF))
+    else:
+        outs = (shape(NZ * half, HALF),) + (shape(2 * half, HALF),) * 3 + (shape(half, HALF),)
     return local(
         functools.partial(backward_kernel, far),
-        (message, message) if far else (shape(places, TILE, HALF),),
+        outs,
         5,
         "backward_far" if far else "backward_near",
         scalars=2,
         any_in=2,
-        scratch=[pltpu.VMEM((places + 1, TILE, HALF), jnp.float32)]
+        scratch=[pltpu.VMEM(((QUAD if far else NZ * QUAD) + 1, TILE, HALF), jnp.float32)]
         + SLOT_SCRATCH
         + [pltpu.SemaphoreType.DMA((LIST,))],
         cost=cost(3, 2) if far else cost(21, 6),
@@ -429,26 +457,22 @@
     )(agg_own, agg_other, weight, cot_own, cot_other)
 
 
-def away(parts, *messages):
-    return local(
-        away_kernel,
-        (shape(2 * TILE + W_ROWS, HALF),),
-        10,
-        "away",
-        scratch=[pltpu.VMEM((NZ, W_ROWS, HALF), jnp.bfloat16)],
-    )(parts, *messages)[0]
-
-
-def middle(*operands):
-    return local(
-        middle_kernel,
+def enter(*operands):
+    message = shape(TILE + 2 * W_ROWS, HALF)
+    return local(enter_kernel, (message, message), 5, "enter")(*operands)
+
+
+def leave(*operands):
+    return local(
+        leave_kernel,
         (
             shape(TILE, HALF),
             shape(TILE + 4 * W_ROWS, HALF),
             shape(2, W_ROWS, HALF, dtype=jnp.float32),
         ),
-        7,
-        "middle",
+        11,
+        "leave",
+        scratch=[pltpu.VMEM((NZ, 2 * W_ROWS, HALF), jnp.bfloat16)],
     )(*operands)
 
 
@@ -461,30 +485,35 @@
     )(mine, from_core, w_here)
 
 
-def add(a, b):
-    return (a.astype(jnp.float32) + b.astype(jnp.float32)).astype(jnp.bfloat16)
+def add(*terms):
+    return sum(term.astype(jnp.float32) for term in terms).astype(jnp.bfloat16)
 
 
 def per_device(features, adj_tiles, tile_row, tile_col, tile_count, weight, cotangent):
     adj0 = adj_tiles[0, 0]
-    block = features[0]
-
-    x_block = quad_permute(block, 2)
-    keep, message, own_lists = prepare(tile_row[0, 0], tile_col[0, 0], tile_count, block)
-    keep, message = join(keep, message, x_block)
+
+    keep, message, own_lists = prepare(tile_row[0, 0], tile_col[0, 0], tile_count, features[0])
     from_core = quad_permute(message, 1)
-    core_keep = from_core[16:].reshape(2, TILE, HALF)
-    chunk = jnp.stack([keep[0], core_keep[0], keep[1], core_keep[1]])
+    chunk = jnp.stack([keep, from_core[16:]])
     lists = (own_lists, from_core[0, :25].astype(jnp.int32))
     adj1 = quad_permute(adj0, 1)
     cot1 = quad_permute(cotangent, 1)
 
+    x0 = quad_permute(chunk, 2)
     up1, down1 = z_shift(chunk, 1), z_shift(chunk, -1)
+    x1 = quad_permute(jnp.concatenate([up1, down1]), 2)
     up2, down2 = z_shift(up1, 1), z_shift(down1, -1)
+    up2, down2, x0 = lax.optimization_barrier((up2, down2, x0))
+    x2 = quad_permute(jnp.concatenate([up2, down2]), 2)
     up3, down3 = z_shift(up2, 1), z_shift(down2, -1)
-    far_a, far_b = z_shift(up3[:2], 1), z_shift(down3[2:], -1)
-    near = forward_near(lists, adj0, adj1, [chunk, down1, down2, down3, up3, up2, up1])
-    partial = forward_far(lists, adj0, adj1, near, far_a, far_b)
+    up3, down3, x1 = lax.optimization_barrier((up3, down3, x1))
+    x3 = quad_permute(jnp.concatenate([up3, down3]), 2)
+    far_a, far_b = z_shift(up3[:1], 1), z_shift(down3[1:], -1)
+    far_a, far_b, x2 = lax.optimization_barrier((far_a, far_b, x2))
+    far = quad_permute(jnp.concatenate([far_a, far_b]), 2)
+    pieces = [chunk, x0, up1, down1, x1, up2, down2, x2, up3, down3, x3]
+    near = forward_near(lists, adj0, adj1, pieces + [far_a, far_b])
+    partial = forward_far(lists, adj0, adj1, near, far)
 
     shares = lax.all_to_all(partial, "col", 0, 0, tiled=True)
     agg = shares.reshape(NCOL, 2 * TILE, HALF).astype(jnp.float32).sum(axis=0)
@@ -492,32 +521,40 @@
     activated, send = dense(agg, agg_other, weight, cotangent, cot1)
     received = lax.all_to_all(send, "col", 0, 0, tiled=True)
 
-    half, size = 2 * TILE, QUAD * TILE
-    own, own_down = backward_tiles(lists, adj0, adj1, received, True)
-    (blocks,) = backward_tiles(lists, adj0, adj1, received, False)
-    parts = blocks.reshape(NZ, size, HALF)
-    up1, down1 = z_shift(own, 1), z_shift(own_down, -1)
-    up = [add(parts[3, :half], up1[:half]), parts[3, half:], up1[half:]]
-    down = [parts[5, :half], add(parts[5, half:], down1[:half]), down1[half:]]
-    up2, down2 = z_shift(jnp.concatenate(up), 1), z_shift(jnp.concatenate(down), -1)
-    up = [add(parts[2], up2[:size]), up2[size:]]
-    down = [add(parts[6], down2[:size]), down2[size:]]
-    up3, down3 = z_shift(jnp.concatenate(up), 1), z_shift(jnp.concatenate(down), -1)
-    up = add(parts[1], up3[:size])
-    down = add(parts[7], down3[:size])
-    up4_away = z_shift(jnp.concatenate([up[half:], up3[size:]]), 1)
-    down4_away = z_shift(down[half:], -1)
-    up4, down4 = z_shift(up[:half], 1), z_shift(down[:half], -1)
-
-    to_x = away(blocks, own, up1, up2, up3, up4_away, down1, down2, down3, down4_away)
-    w_send = to_x[half:]
-    from_x = quad_permute(to_x, 2)
-    w_lo = lax.ppermute(w_send, "col", [(c, c ^ 4) for c in range(NCOL)])
+    half = 2 * TILE
+    own4, to_x4 = backward_tiles(lists, adj0, adj1, received, True)
+    w_send = to_x4[half:]
     both = [
         (r * NCOL + c, (r ^ 2) * NCOL + (c ^ 4)) for r in range(NZ * QUAD) for c in range(NCOL)
     ]
+    x4 = quad_permute(to_x4, 2)
+    w_lo = lax.ppermute(w_send, "col", [(c, c ^ 4) for c in range(NCOL)])
     w_both = lax.ppermute(w_send, ("row", "col"), both)
-    mine, to_core, w_here = middle(blocks, up4, down4, to_x, from_x, w_lo, w_both)
+    own, to_x3, to_x2, to_x1, to_x0 = backward_tiles(lists, adj0, adj1, received, False)
+    own = own.reshape(NZ, half, HALF)
+    x3, x2, x1, x0 = (quad_permute(x, 2) for x in (to_x3, to_x2, to_x1, to_x0))
+    up_first, down_first = enter(own4, to_x4, x4, w_lo, w_both)
+    up1, down1 = z_shift(up_first, 1), z_shift(down_first, -1)
+    up = [
+        add(own[3, :TILE], x3[:TILE], up1[:TILE]),
+        add(own[3, TILE:], x3[TILE:half]),
+        up1[TILE:],
+    ]
+    down = [
+        add(own[5, :TILE], x3[half : half + TILE]),
+        add(own[5, TILE:], x3[half + TILE :], down1[:TILE]),
+        down1[TILE:],
+    ]
+    up2, down2 = z_shift(jnp.concatenate(up), 1), z_shift(jnp.concatenate(down), -1)
+    up = [add(own[2], x2[:half], up2[:half]), up2[half:]]
+    down = [add(own[6], x2[half:], down2[:half]), down2[half:]]
+    up3, down3 = z_shift(jnp.concatenate(up), 1), z_shift(jnp.concatenate(down), -1)
+    up = [add(own[1], x1[:half], up3[:half]), up3[half:]]
+    up4 = z_shift(jnp.concatenate(up), 1)
+    down4 = z_shift(add(own[7], x1[half:], down3[:half]), -1)
+    mine, to_core, w_here = leave(
+        own[0], x0, up_first, up1, up2, up3, up4, down1, down2, down3, down4
+    )
     grad, weight_grad = last(mine, quad_permute(to_core, 1), w_here)
     return (activated, weight_grad, grad[None])
 

time: 142 us -> 148 us (1.042)
  starting transfers between devices: 54.8 us -> 66.1 us
  waiting for transfers between devices: 35.6 us -> 25.8 us
  blocking collectives: 34.5 us -> 37 us
    ppermute x18 -> x16, waiting for transfers between devices: 32.4 us -> 12.4 us  [z_shift(): return lax.ppermute(x, 'row', row_pairs(lambda z, q: (z + step, q)))]
    ppermute x7 -> x15, starting transfers between devices: 24.8 us -> 39.5 us  [quad_permute(): return lax.ppermute(x, 'row', row_pairs(lambda z, q: (z, q ^ flip)))]
    ppermute x1, waiting for transfers between devices: 0.01 us -> 5 us  [per_device(): w_lo = lax.ppermute(w_send, 'col', [(c, c ^ 4) for c in range(NCOL)])]
    ppermute x18 -> x16, starting transfers between devices: 29.4 us -> 24.6 us  [z_shift(): return lax.ppermute(x, 'row', row_pairs(lambda z, q: (z + step, q)))]
    ppermute x7 -> x15, waiting for transfers between devices: 3.12 us -> 7.91 us  [quad_permute(): return lax.ppermute(x, 'row', row_pairs(lambda z, q: (z, q ^ flip)))]
    all_to_all x1, blocking collectives: 15 us -> 17.5 us  [per_device(): shares = lax.all_to_all(partial, 'col', 0, 0, tiled=True)]
    pallas_call x1, Pallas kernels: 2.43 us -> 4.58 us  [forward_near(): local(forward_near_kernel, (shape(17, TILE, HALF, dtype=jnp.float32),), 1...]
    ppermute x1, starting transfers between devices: 0.01 us -> 1.97 us  [per_device(): w_lo = lax.ppermute(w_send, 'col', [(c, c ^ 4) for c in range(NCOL)])]
  transfers between devices with their start and end apart: 27 -> 33, of which waited for: 14 -> 18; matrix products, arithmetic and copies ran while one was open for 0% -> 0% of each run, Pallas kernels for 4% -> 5%
where the time goes in v7:
time: 148 us; the launch traced here: 147 us
  starting transfers between devices  66.1 us (45%)
  blocking collectives  37 us (25%)
  waiting for transfers between devices  25.8 us (17%)
  Pallas kernels  13.6 us (9%)
  local copies, waits for them, and re-layouts  2.28 us (2%)
  between operations  1.51 us (1%)
    ppermute x15, starting transfers between devices, quad_permute(): return lax.ppermute(x, 'row', row_pairs(lambda z, q: (z, q ^ flip)))  39.5 us
    ppermute x16, starting transfers between devices, z_shift(): return lax.ppermute(x, 'row', row_pairs(lambda z, q: (z + step, q)))  24.6 us
    all_to_all x1, blocking collectives, per_device(): received = lax.all_to_all(send, 'col', 0, 0, tiled=True)  19.5 us
    all_to_all x1, blocking collectives, per_device(): shares = lax.all_to_all(partial, 'col', 0, 0, tiled=True)  17.5 us
    ppermute x16, waiting for transfers between devices, z_shift(): return lax.ppermute(x, 'row', row_pairs(lambda z, q: (z + step, q)))  12.4 us
    ppermute x15, waiting for transfers between devices, quad_permute(): return lax.ppermute(x, 'row', row_pairs(lambda z, q: (z, q ^ flip)))  7.91 us
    ppermute x1, waiting for transfers between devices, per_device(): w_lo = lax.ppermute(w_send, 'col', [(c, c ^ 4) for c in range(NCOL)])  5 us
    pallas_call x1, Pallas kernels, forward_near(): local(forward_near_kernel, (shape(17, TILE, HALF, dtype=jnp.float32),), 1...  4.58 us
  transfers between devices with their start and end apart: 33, of which 18 were waited for; matrix products, arithmetic and copies ran while one was open for 0% of the time, Pallas kernels for 5%

profile of v7, /device:TPU:1, one launch (start us, length us, event | category | flops | bytes accessed | tf_op | source)
XLA Modules:
  0.0 146.9 jit_solution(8247635866774496206)
XLA Ops:
  0.6 3.3 %collective-permute-start.1 = (bf16[12,256,256]{2,1,0:T(8,128)(2,1)}, bf16[12,256,256]{2,1,0:T(8,128)(2,1)S(1)}, u32[]{:S(2)}, u32[]{:S(2)}) collective-permute-start(bf16[12,256,256]{2,1,0:T(8,128)(2,1)} %bitcast.35), channel_id=1, source_target_pairs={{0,8},{8,0},{16,24},{24,16},{32,40},{40,32},{48,56},{56,48},{64,72... | collective-permute-start | bytes 4718600 | tf_op jit(solution)/shard_map/ppermute | solution.py:30
  9.5 3.9 %collective-permute-start.4 = (bf16[2,256,128]{2,1,0:T(8,128)(2,1)S(1)}, bf16[2,256,128]{2,1,0:T(8,128)(2,1)S(1)}, u32[]{:S(2)}, u32[]{:S(2)}) collective-permute-start(bf16[2,256,128]{2,1,0:T(8,128)(2,1)S(1)} %pad_maximum_fusion.8.refs_4_), channel_id=1, source_target_pairs={{0,224},{8,232},{16,240},{24,248},{32,0},{40,8},{48,16},{56,24},{6... | collective-permute-start | bytes 393224 | tf_op jit(solution)/shard_map/ppermute | solution.py:34
  13.4 2.7 %collective-permute-start.6 = (bf16[2,256,128]{2,1,0:T(8,128)(2,1)S(1)}, bf16[2,256,128]{2,1,0:T(8,128)(2,1)S(1)}, u32[]{:S(2)}, u32[]{:S(2)}) collective-permute-start(bf16[2,256,128]{2,1,0:T(8,128)(2,1)S(1)} %pad_maximum_fusion.8.refs_4_), channel_id=1, source_target_pairs={{0,16},{8,24},{16,0},{24,8},{32,48},{40,56},{48,32},{56,40},{64,80... | collective-permute-start | bytes 393224 | tf_op jit(solution)/shard_map/ppermute | solution.py:30
  17.0 2.7 %collective-permute-start.5 = (bf16[2,256,128]{2,1,0:T(8,128)(2,1)S(1)}, bf16[2,256,128]{2,1,0:T(8,128)(2,1)S(1)}, u32[]{:S(2)}, u32[]{:S(2)}) collective-permute-start(bf16[2,256,128]{2,1,0:T(8,128)(2,1)S(1)} %collective-permute-done.4.refs_7_), channel_id=1, source_target_pairs={{0,224},{8,232},{16,240},{24,248},{32,0},{40,8},{48,16},{56,24},{6... | collective-permute-start | bytes 393224 | tf_op jit(solution)/shard_map/ppermute | solution.py:34
  19.8 2.8 %collective-permute-start.9 = (bf16[4,256,128]{2,1,0:T(8,128)(2,1)S(1)}, bf16[4,256,128]{2,1,0:T(8,128)(2,1)S(1)}, u32[]{:S(2)}, u32[]{:S(2)}) collective-permute-start(bf16[4,256,128]{2,1,0:T(8,128)(2,1)S(1)} %pad_maximum_fusion), channel_id=1, source_target_pairs={{0,16},{8,24},{16,0},{24,8},{32,48},{40,56},{48,32},{56,40},{64,80... | collective-permute-start | bytes 786440 | tf_op jit(solution)/shard_map/ppermute | solution.py:30
  22.6 2.8 %collective-permute-start.12 = (bf16[4,256,128]{2,1,0:T(8,128)(2,1)S(1)}, bf16[4,256,128]{2,1,0:T(8,128)(2,1)S(1)}, u32[]{:S(2)}, u32[]{:S(2)}) collective-permute-start(bf16[4,256,128]{2,1,0:T(8,128)(2,1)S(1)} %pad_maximum_fusion.1), channel_id=1, source_target_pairs={{0,16},{8,24},{16,0},{24,8},{32,48},{40,56},{48,32},{56,40},{64,80... | collective-permute-start | bytes 786440 | tf_op jit(solution)/shard_map/ppermute | solution.py:30
  25.4 2.7 %collective-permute-start.8 = (bf16[2,256,128]{2,1,0:T(8,128)(2,1)S(1)}, bf16[2,256,128]{2,1,0:T(8,128)(2,1)S(1)}, u32[]{:S(2)}, u32[]{:S(2)}) collective-permute-start(bf16[2,256,128]{2,1,0:T(8,128)(2,1)S(1)} %collective-permute-done.5.refs_10_), channel_id=1, source_target_pairs={{0,224},{8,232},{16,240},{24,248},{32,0},{40,8},{48,16},{56,24},{6... | collective-permute-start | bytes 393224 | tf_op jit(solution)/shard_map/ppermute | solution.py:34
  28.1 2.6 %collective-permute-done.7.refs_12_ = bf16[2,256,128]{2,1,0:T(8,128)(2,1)S(1)} collective-permute-done((bf16[2,256,128]{2,1,0:T(8,128)(2,1)S(1)}, bf16[2,256,128]{2,1,0:T(8,128)(2,1)S(1)}, u32[]{:S(2)}, u32[]{:S(2)}) %collective-permute-start.7) | collective-permute-done | bytes 131104 | tf_op jit(solution)/shard_map/ppermute | solution.py:34
  30.7 1.5 %collective-permute-start.10 = (bf16[1,256,128]{2,1,0:T(8,128)(2,1)S(1)}, bf16[1,256,128]{2,1,0:T(8,128)(2,1)S(1)}, u32[]{:S(2)}, u32[]{:S(2)}) collective-permute-start(bf16[1,256,128]{2,1,0:T(8,128)(2,1)S(1)} %slice.106), channel_id=1, source_target_pairs={{0,32},{8,40},{16,48},{24,56},{32,64},{40,72},{48,80},{56,88},{64,... | collective-permute-start | bytes 196616 | tf_op jit(solution)/shard_map/ppermute | solution.py:34
  33.7 1.5 %collective-permute-done.10.refs_15_ = bf16[1,256,128]{2,1,0:T(8,128)(2,1)S(1)} collective-permute-done((bf16[1,256,128]{2,1,0:T(8,128)(2,1)S(1)}, bf16[1,256,128]{2,1,0:T(8,128)(2,1)S(1)}, u32[]{:S(2)}, u32[]{:S(2)}) %collective-permute-start.10) | collective-permute-done | bytes 65568 | tf_op jit(solution)/shard_map/ppermute | solution.py:34
  35.4 1.4 collective-permute-start.14
  36.7 3.6 %collective-permute-done.13.refs_14_ = bf16[4,256,128]{2,1,0:T(8,128)(2,1)S(1)} collective-permute-done((bf16[4,256,128]{2,1,0:T(8,128)(2,1)S(1)}, bf16[4,256,128]{2,1,0:T(8,128)(2,1)S(1)}, u32[]{:S(2)}, u32[]{:S(2)}) %collective-permute-start.13) | collective-permute-done | bytes 262176 | tf_op jit(solution)/shard_map/ppermute | solution.py:30
  40.4 4.6 %forward_near.1.refs_4_ = f32[17,256,128]{2,1,0:T(8,128)S(1)} custom-call(s32[25]{0:T(128)S(1)} %get-tuple-element.31.refs_0_, s32[25]{0:T(128)S(1)} %fusion.6.refs_1_, bf16[12,256,256]{2,1,0:T(8,128)(2,1)S(1)} %bitcast.36, bf16[12,256,256]{2,1,0:T(8,128)(2,1)S(1)} %collective-permute-done.1.refs_3_, bf16[2,256,128]{2,1,0:T(8,128)(2,1)S(1)} %pad_maximum_fusion.8.refs_4_, ...), custom_call_target="tpu_custom_call" | custom-call | flops 369098752 | bytes 6291456 | tf_op jit(solution)/shard_map/forward_near/pallas_call | solution.py:402
  45.0 1.5 %forward_far.1 = bf16[8,2,256,128]{3,2,1,0:T(8,128)(2,1)S(1)} custom-call(s32[25]{0:T(128)S(1)} %get-tuple-element.31.refs_0_, s32[25]{0:T(128)S(1)} %fusion.6.refs_1_, bf16[12,256,256]{2,1,0:T(8,128)(2,1)S(1)} %bitcast.37, bf16[12,256,256]{2,1,0:T(8,128)(2,1)S(1)} %collective-permute-done.1.refs_3_, f32[17,256,128]{2,1,0:T(8,128)S(1)} %forward_near.1.refs_4_, ...), custom_call_target="tpu_custom_call" | custom-call | flops 33554432 | bytes 4194304 | tf_op jit(solution)/shard_map/forward_far/pallas_call | solution.py:417
  46.5 17.5 %all_to_all.10 = bf16[8,2,256,128]{3,2,1,0:T(8,128)(2,1)S(1)} all-to-all(bf16[8,2,256,128]{3,2,1,0:T(8,128)(2,1)S(1)} %forward_far.1), channel_id=1, replica_groups=mesh['row'=32,'col'=8] {'col'}, dimensions={0} | all-to-all | bytes 2097152 | tf_op jit(solution)/shard_map/all_to_all | solution.py:518
  64.1 6.4 %collective-permute-start.15 = (f32[512,128]{1,0:T(8,128)S(1)}, f32[512,128]{1,0:T(8,128)S(1)}, u32[]{:S(2)}, u32[]{:S(2)}) collective-permute-start(f32[512,128]{1,0:T(8,128)S(1)} %bitcast.40), channel_id=1, source_target_pairs={{0,8},{8,0},{16,24},{24,16},{32,40},{40,32},{48,56},{56,48},{64,72... | collective-permute-start | bytes 786440 | tf_op jit(solution)/shard_map/ppermute | solution.py:30
  71.9 1.4 dense.1
  73.3 19.5 %all_to_all.11.refs_4_ = bf16[8,640,128]{2,1,0:T(8,128)(2,1)S(1)} all-to-all(bf16[8,640,128]{2,1,0:T(8,128)(2,1)S(1)} %get-tuple-element.44), channel_id=1, replica_groups=mesh['row'=32,'col'=8] {'col'}, dimensions={0} | all-to-all | bytes 2621440 | tf_op jit(solution)/shard_map/all_to_all | solution.py:522
  92.8 1.7 %backward_far.1 = (bf16[512,128]{1,0:T(8,128)(2,1)S(1)}, bf16[640,128]{1,0:T(8,128)(2,1)S(1)}) custom-call(s32[25]{0:T(128)S(1)} %get-tuple-element.31.refs_0_, s32[25]{0:T(128)S(1)} %fusion.6.refs_1_, bf16[12,256,256]{2,1,0:T(8,128)(2,1)S(1)} %bitcast.38, bf16[12,256,256]{2,1,0:T(8,128)(2,1)S(1)} %collective-permute-done.1.refs_3_, ...), custom_call_target="tpu_custom_call" | custom-call | flops 50331648 | bytes 2097152 | tf_op jit(solution)/shard_map/backward_far/pallas_call | solution.py:437
  94.7 2.1 %backward_near.1 = (bf16[4096,128]{1,0:T(8,128)(2,1)S(1)}, bf16[1024,128]{1,0:T(8,128)(2,1)S(1)}, bf16[1024,128]{1,0:T(8,128)(2,1)S(1)}, bf16[1024,128]{1,0:T(8,128)(2,1)S(1)}, bf16[512,128]{1,0:T(8,128)(2,1)S(1)}) custom-call(s32[25]{0:T(128)S(1)} %get-tuple-element.31.refs_0_, s32[25]{0:T(128)S(1)} %fusion.6.refs_1_, bf16[12,256,256]{2,1,0:T(8,128)(2,1)S(1)} %bitcast.39, ...), custom_call_target="tpu_custom_call" | custom-call | flops 352321536 | bytes 6291456 | tf_op jit(solution)/shard_map/backward_near/pallas_call | solution.py:437
  96.7 3.5 %collective-permute-start.22 = (bf16[1024,128]{1,0:T(8,128)(2,1)S(1)}, bf16[1024,128]{1,0:T(8,128)(2,1)S(1)}, u32[]{:S(2)}, u32[]{:S(2)}) collective-permute-start(bf16[1024,128]{1,0:T(8,128)(2,1)S(1)} %get-tuple-element.50), channel_id=1, source_target_pairs={{0,16},{8,24},{16,0},{24,8},{32,48},{40,56},{48,32},{56,40},{64,80... | collective-permute-start | bytes 786440 | tf_op jit(solution)/shard_map/ppermute | solution.py:30
  100.3 2.0 %collective-permute-start.19 = (bf16[128,128]{1,0:T(8,128)(2,1)S(1)}, bf16[128,128]{1,0:T(8,128)(2,1)S(1)}, u32[]{:S(2)}, u32[]{:S(2)}) collective-permute-start(bf16[128,128]{1,0:T(8,128)(2,1)S(1)} %slice.109), channel_id=1, source_target_pairs={{0,4},{1,5},{2,6},{3,7},{4,0},{5,1},{6,2},{7,3},{8,12},{9,13},{10,... | collective-permute-start | bytes 98312 | tf_op jit(solution)/shard_map/ppermute | solution.py:531
  102.3 5.0 %collective-permute-done.19.w_lo = bf16[128,128]{1,0:T(8,128)(2,1)S(1)} collective-permute-done((bf16[128,128]{1,0:T(8,128)(2,1)S(1)}, bf16[128,128]{1,0:T(8,128)(2,1)S(1)}, u32[]{:S(2)}, u32[]{:S(2)}) %collective-permute-start.19) | collective-permute-done | bytes 32800 | tf_op jit(solution)/shard_map/ppermute | solution.py:531
  109.1 1.5 %collective-permute-start.28 = (bf16[512,128]{1,0:T(8,128)(2,1)S(1)}, bf16[512,128]{1,0:T(8,128)(2,1)S(1)}, u32[]{:S(2)}, u32[]{:S(2)}) collective-permute-start(bf16[512,128]{1,0:T(8,128)(2,1)S(1)} %get-tuple-element.53), channel_id=1, source_target_pairs={{0,224},{8,232},{16,240},{24,248},{32,0},{40,8},{48,16},{56,24},{6... | collective-permute-start | bytes 393224 | tf_op jit(solution)/shard_map/ppermute | solution.py:34
  113.9 1.5 %collective-permute-start.23 = (bf16[768,128]{1,0:T(8,128)(2,1)S(1)}, bf16[768,128]{1,0:T(8,128)(2,1)S(1)}, u32[]{:S(2)}, u32[]{:S(2)}) collective-permute-start(bf16[768,128]{1,0:T(8,128)(2,1)S(1)} %pad_maximum_fusion.3), channel_id=1, source_target_pairs={{0,32},{8,40},{16,48},{24,56},{32,64},{40,72},{48,80},{56,88},{64,... | collective-permute-start | bytes 589832 | tf_op jit(solution)/shard_map/ppermute | solution.py:34
  116.7 3.0 %collective-permute-start.26 = (bf16[1024,128]{1,0:T(8,128)(2,1)S(1)}, bf16[1024,128]{1,0:T(8,128)(2,1)S(1)}, u32[]{:S(2)}, u32[]{:S(2)}) collective-permute-start(bf16[1024,128]{1,0:T(8,128)(2,1)S(1)} %get-tuple-element.52), channel_id=1, source_target_pairs={{0,16},{8,24},{16,0},{24,8},{32,48},{40,56},{48,32},{56,40},{64,80... | collective-permute-start | bytes 786440 | tf_op jit(solution)/shard_map/ppermute | solution.py:30
  121.4 2.1 %collective-permute-start.30 = (bf16[768,128]{1,0:T(8,128)(2,1)S(1)}, bf16[768,128]{1,0:T(8,128)(2,1)S(1)}, u32[]{:S(2)}, u32[]{:S(2)}) collective-permute-start(bf16[768,128]{1,0:T(8,128)(2,1)S(1)} %pad_maximum_fusion.7), channel_id=1, source_target_pairs={{0,224},{8,232},{16,240},{24,248},{32,0},{40,8},{48,16},{56,24},{6... | collective-permute-start | bytes 589832 | tf_op jit(solution)/shard_map/ppermute | solution.py:34
  123.6 3.2 %collective-permute-done.25.up3 = bf16[768,128]{1,0:T(8,128)(2,1)S(1)} collective-permute-done((bf16[768,128]{1,0:T(8,128)(2,1)S(1)}, bf16[768,128]{1,0:T(8,128)(2,1)S(1)}, u32[]{:S(2)}, u32[]{:S(2)}) %collective-permute-start.25) | collective-permute-done | bytes 196640 | tf_op jit(solution)/shard_map/ppermute | solution.py:34
  127.2 1.9 %collective-permute-start.27 = (bf16[768,128]{1,0:T(8,128)(2,1)S(1)}, bf16[768,128]{1,0:T(8,128)(2,1)S(1)}, u32[]{:S(2)}, u32[]{:S(2)}) collective-permute-start(bf16[768,128]{1,0:T(8,128)(2,1)S(1)} %pad_maximum_fusion.5), channel_id=1, source_target_pairs={{0,32},{8,40},{16,48},{24,56},{32,64},{40,72},{48,80},{56,88},{64,... | collective-permute-start | bytes 589832 | tf_op jit(solution)/shard_map/ppermute | solution.py:34
  129.0 2.6 %collective-permute-start.17 = (bf16[512,128]{1,0:T(8,128)(2,1)S(1)}, bf16[512,128]{1,0:T(8,128)(2,1)S(1)}, u32[]{:S(2)}, u32[]{:S(2)}) collective-permute-start(bf16[512,128]{1,0:T(8,128)(2,1)S(1)} %get-tuple-element.46), channel_id=1, source_target_pairs={{0,16},{8,24},{16,0},{24,8},{32,48},{40,56},{48,32},{56,40},{64,80... | collective-permute-start | bytes 393224 | tf_op jit(solution)/shard_map/ppermute | solution.py:30
  131.6 2.0 %collective-permute-start.31 = (bf16[512,128]{1,0:T(8,128)(2,1)S(1)}, bf16[512,128]{1,0:T(8,128)(2,1)S(1)}, u32[]{:S(2)}, u32[]{:S(2)}) collective-permute-start(bf16[512,128]{1,0:T(8,128)(2,1)S(1)} %get-tuple-element.59), channel_id=1, source_target_pairs={{0,224},{8,232},{16,240},{24,248},{32,0},{40,8},{48,16},{56,24},{6... | collective-permute-start | bytes 393224 | tf_op jit(solution)/shard_map/ppermute | solution.py:34
  135.7 9.3 %collective-permute-start.32 = (bf16[768,128]{1,0:T(8,128)(2,1)S(1)}, bf16[768,128]{1,0:T(8,128)(2,1)S(1)}, u32[]{:S(2)}, u32[]{:S(2)}) collective-permute-start(bf16[768,128]{1,0:T(8,128)(2,1)S(1)} %get-tuple-element.55), channel_id=1, source_target_pairs={{0,8},{8,0},{16,24},{24,16},{32,40},{40,32},{48,56},{56,48},{64,72... | collective-permute-start | bytes 589832 | tf_op jit(solution)/shard_map/ppermute | solution.py:30
  (82 shorter events, 21.4 us)
Async XLA Ops:
  0.6 39.7 %collective-permute-start.1 = (bf16[12,256,256]{2,1,0:T(8,128)(2,1)}, bf16[12,256,256]{2,1,0:T(8,128)(2,1)S(1)}, u32[]{:S(2)}, u32[]{:S(2)}) collective-permute-start(bf16[12,256,256]{2,1,0:T(8,128)(2,1)} %bitcast.35), channel_id=1, source_target_pairs={{0,8},{8,0},{16,24},{24,16},{32,40},{40,32},{48,56},{56,48},{64,72... | collective-permute-start | bytes 4718600 | tf_op jit(solution)/shard_map/ppermute | solution.py:30
  9.4 7.6 %collective-permute-start.2 = (bf16[2,256,128]{2,1,0:T(8,128)(2,1)S(1)}, bf16[2,256,128]{2,1,0:T(8,128)(2,1)S(1)}, u32[]{:S(2)}, u32[]{:S(2)}) collective-permute-start(bf16[2,256,128]{2,1,0:T(8,128)(2,1)S(1)} %pad_maximum_fusion.8.refs_4_), channel_id=1, source_target_pairs={{0,32},{8,40},{16,48},{24,56},{32,64},{40,72},{48,80},{56,88},{64,... | collective-permute-start | bytes 393224 | tf_op jit(solution)/shard_map/ppermute | solution.py:34
  9.5 7.5 %collective-permute-start.4 = (bf16[2,256,128]{2,1,0:T(8,128)(2,1)S(1)}, bf16[2,256,128]{2,1,0:T(8,128)(2,1)S(1)}, u32[]{:S(2)}, u32[]{:S(2)}) collective-permute-start(bf16[2,256,128]{2,1,0:T(8,128)(2,1)S(1)} %pad_maximum_fusion.8.refs_4_), channel_id=1, source_target_pairs={{0,224},{8,232},{16,240},{24,248},{32,0},{40,8},{48,16},{56,24},{6... | collective-permute-start | bytes 393224 | tf_op jit(solution)/shard_map/ppermute | solution.py:34
  13.4 9.2 %collective-permute-start.6 = (bf16[2,256,128]{2,1,0:T(8,128)(2,1)S(1)}, bf16[2,256,128]{2,1,0:T(8,128)(2,1)S(1)}, u32[]{:S(2)}, u32[]{:S(2)}) collective-permute-start(bf16[2,256,128]{2,1,0:T(8,128)(2,1)S(1)} %pad_maximum_fusion.8.refs_4_), channel_id=1, source_target_pairs={{0,16},{8,24},{16,0},{24,8},{32,48},{40,56},{48,32},{56,40},{64,80... | collective-permute-start | bytes 393224 | tf_op jit(solution)/shard_map/ppermute | solution.py:30
  17.0 5.5 %collective-permute-start.3 = (bf16[2,256,128]{2,1,0:T(8,128)(2,1)S(1)}, bf16[2,256,128]{2,1,0:T(8,128)(2,1)S(1)}, u32[]{:S(2)}, u32[]{:S(2)}) collective-permute-start(bf16[2,256,128]{2,1,0:T(8,128)(2,1)S(1)} %collective-permute-done.2.refs_6_), channel_id=1, source_target_pairs={{0,32},{8,40},{16,48},{24,56},{32,64},{40,72},{48,80},{56,88},{64,... | collective-permute-start | bytes 393224 | tf_op jit(solution)/shard_map/ppermute | solution.py:34
  17.0 5.5 %collective-permute-start.5 = (bf16[2,256,128]{2,1,0:T(8,128)(2,1)S(1)}, bf16[2,256,128]{2,1,0:T(8,128)(2,1)S(1)}, u32[]{:S(2)}, u32[]{:S(2)}) collective-permute-start(bf16[2,256,128]{2,1,0:T(8,128)(2,1)S(1)} %collective-permute-done.4.refs_7_), channel_id=1, source_target_pairs={{0,224},{8,232},{16,240},{24,248},{32,0},{40,8},{48,16},{56,24},{6... | collective-permute-start | bytes 393224 | tf_op jit(solution)/shard_map/ppermute | solution.py:34
  19.8 8.3 %collective-permute-start.9 = (bf16[4,256,128]{2,1,0:T(8,128)(2,1)S(1)}, bf16[4,256,128]{2,1,0:T(8,128)(2,1)S(1)}, u32[]{:S(2)}, u32[]{:S(2)}) collective-permute-start(bf16[4,256,128]{2,1,0:T(8,128)(2,1)S(1)} %pad_maximum_fusion), channel_id=1, source_target_pairs={{0,16},{8,24},{16,0},{24,8},{32,48},{40,56},{48,32},{56,40},{64,80... | collective-permute-start | bytes 786440 | tf_op jit(solution)/shard_map/ppermute | solution.py:30
  22.6 12.7 %collective-permute-start.12 = (bf16[4,256,128]{2,1,0:T(8,128)(2,1)S(1)}, bf16[4,256,128]{2,1,0:T(8,128)(2,1)S(1)}, u32[]{:S(2)}, u32[]{:S(2)}) collective-permute-start(bf16[4,256,128]{2,1,0:T(8,128)(2,1)S(1)} %pad_maximum_fusion.1), channel_id=1, source_target_pairs={{0,16},{8,24},{16,0},{24,8},{32,48},{40,56},{48,32},{56,40},{64,80... | collective-permute-start | bytes 786440 | tf_op jit(solution)/shard_map/ppermute | solution.py:30
  25.4 5.3 %collective-permute-start.7 = (bf16[2,256,128]{2,1,0:T(8,128)(2,1)S(1)}, bf16[2,256,128]{2,1,0:T(8,128)(2,1)S(1)}, u32[]{:S(2)}, u32[]{:S(2)}) collective-permute-start(bf16[2,256,128]{2,1,0:T(8,128)(2,1)S(1)} %collective-permute-done.3.refs_9_), channel_id=1, source_target_pairs={{0,32},{8,40},{16,48},{24,56},{32,64},{40,72},{48,80},{56,88},{64,... | collective-permute-start | bytes 393224 | tf_op jit(solution)/shard_map/ppermute | solution.py:34
  25.4 5.3 %collective-permute-start.8 = (bf16[2,256,128]{2,1,0:T(8,128)(2,1)S(1)}, bf16[2,256,128]{2,1,0:T(8,128)(2,1)S(1)}, u32[]{:S(2)}, u32[]{:S(2)}) collective-permute-start(bf16[2,256,128]{2,1,0:T(8,128)(2,1)S(1)} %collective-permute-done.5.refs_10_), channel_id=1, source_target_pairs={{0,224},{8,232},{16,240},{24,248},{32,0},{40,8},{48,16},{56,24},{6... | collective-permute-start | bytes 393224 | tf_op jit(solution)/shard_map/ppermute | solution.py:34
  30.7 4.5 %collective-permute-start.10 = (bf16[1,256,128]{2,1,0:T(8,128)(2,1)S(1)}, bf16[1,256,128]{2,1,0:T(8,128)(2,1)S(1)}, u32[]{:S(2)}, u32[]{:S(2)}) collective-permute-start(bf16[1,256,128]{2,1,0:T(8,128)(2,1)S(1)} %slice.106), channel_id=1, source_target_pairs={{0,32},{8,40},{16,48},{24,56},{32,64},{40,72},{48,80},{56,88},{64,... | collective-permute-start | bytes 196616 | tf_op jit(solution)/shard_map/ppermute | solution.py:34
  32.2 3.1 %collective-permute-start.11 = (bf16[1,256,128]{2,1,0:T(8,128)(2,1)S(1)}, bf16[1,256,128]{2,1,0:T(8,128)(2,1)S(1)}, u32[]{:S(2)}, u32[]{:S(2)}) collective-permute-start(bf16[1,256,128]{2,1,0:T(8,128)(2,1)S(1)} %slice.107), channel_id=1, source_target_pairs={{0,224},{8,232},{16,240},{24,248},{32,0},{40,8},{48,16},{56,24},{6... | collective-permute-start | bytes 196616 | tf_op jit(solution)/shard_map/ppermute | solution.py:34
  33.5 6.8 %collective-permute-start.13 = (bf16[4,256,128]{2,1,0:T(8,128)(2,1)S(1)}, bf16[4,256,128]{2,1,0:T(8,128)(2,1)S(1)}, u32[]{:S(2)}, u32[]{:S(2)}) collective-permute-start(bf16[4,256,128]{2,1,0:T(8,128)(2,1)S(1)} %pad_maximum_fusion.2), channel_id=1, source_target_pairs={{0,16},{8,24},{16,0},{24,8},{32,48},{40,56},{48,32},{56,40},{64,80... | collective-permute-start | bytes 786440 | tf_op jit(solution)/shard_map/ppermute | solution.py:30
  35.4 9.6 %collective-permute-start.14 = (bf16[2,256,128]{2,1,0:T(8,128)(2,1)S(1)}, bf16[2,256,128]{2,1,0:T(8,128)(2,1)S(1)}, u32[]{:S(2)}, u32[]{:S(2)}) collective-permute-start(bf16[2,256,128]{2,1,0:T(8,128)(2,1)S(1)} %pad_maximum_fusion.9), channel_id=1, source_target_pairs={{0,16},{8,24},{16,0},{24,8},{32,48},{40,56},{48,32},{56,40},{64,80... | collective-permute-start | bytes 393224 | tf_op jit(solution)/shard_map/ppermute | solution.py:30
  64.1 7.7 %collective-permute-start.15 = (f32[512,128]{1,0:T(8,128)S(1)}, f32[512,128]{1,0:T(8,128)S(1)}, u32[]{:S(2)}, u32[]{:S(2)}) collective-permute-start(f32[512,128]{1,0:T(8,128)S(1)} %bitcast.40), channel_id=1, source_target_pairs={{0,8},{8,0},{16,24},{24,16},{32,40},{40,32},{48,56},{56,48},{64,72... | collective-permute-start | bytes 786440 | tf_op jit(solution)/shard_map/ppermute | solution.py:30
  70.5 1.3 collective-permute-start.16
  94.6 13.2 %collective-permute-start.18 = (bf16[640,128]{1,0:T(8,128)(2,1)S(1)}, bf16[640,128]{1,0:T(8,128)(2,1)S(1)}, u32[]{:S(2)}, u32[]{:S(2)}) collective-permute-start(bf16[640,128]{1,0:T(8,128)(2,1)S(1)} %get-tuple-element.48.sent), channel_id=1, source_target_pairs={{0,16},{8,24},{16,0},{24,8},{32,48},{40,56},{48,32},{56,40},{64,80... | collective-permute-start | bytes 491528 | tf_op jit(solution)/shard_map/ppermute | solution.py:30
  96.7 16.2 %collective-permute-start.22 = (bf16[1024,128]{1,0:T(8,128)(2,1)S(1)}, bf16[1024,128]{1,0:T(8,128)(2,1)S(1)}, u32[]{:S(2)}, u32[]{:S(2)}) collective-permute-start(bf16[1024,128]{1,0:T(8,128)(2,1)S(1)} %get-tuple-element.50), channel_id=1, source_target_pairs={{0,16},{8,24},{16,0},{24,8},{32,48},{40,56},{48,32},{56,40},{64,80... | collective-permute-start | bytes 786440 | tf_op jit(solution)/shard_map/ppermute | solution.py:30
  100.3 7.0 %collective-permute-start.19 = (bf16[128,128]{1,0:T(8,128)(2,1)S(1)}, bf16[128,128]{1,0:T(8,128)(2,1)S(1)}, u32[]{:S(2)}, u32[]{:S(2)}) collective-permute-start(bf16[128,128]{1,0:T(8,128)(2,1)S(1)} %slice.109), channel_id=1, source_target_pairs={{0,4},{1,5},{2,6},{3,7},{4,0},{5,1},{6,2},{7,3},{8,12},{9,13},{10,... | collective-permute-start | bytes 98312 | tf_op jit(solution)/shard_map/ppermute | solution.py:531
  102.3 5.5 %collective-permute-start.20 = (bf16[128,128]{1,0:T(8,128)(2,1)S(1)}, bf16[128,128]{1,0:T(8,128)(2,1)S(1)}, u32[]{:S(2)}, u32[]{:S(2)}) collective-permute-start(bf16[128,128]{1,0:T(8,128)(2,1)S(1)} %slice.109), channel_id=1, source_target_pairs={{0,20},{1,21},{2,22},{3,23},{4,16},{5,17},{6,18},{7,19},{8,28},{9,... | collective-permute-start | bytes 98312 | tf_op jit(solution)/shard_map/ppermute | solution.py:532
  107.8 5.1 %collective-permute-start.21 = (bf16[512,128]{1,0:T(8,128)(2,1)S(1)}, bf16[512,128]{1,0:T(8,128)(2,1)S(1)}, u32[]{:S(2)}, u32[]{:S(2)}) collective-permute-start(bf16[512,128]{1,0:T(8,128)(2,1)S(1)} %get-tuple-element.49.up), channel_id=1, source_target_pairs={{0,32},{8,40},{16,48},{24,56},{32,64},{40,72},{48,80},{56,88},{64,... | collective-permute-start | bytes 393224 | tf_op jit(solution)/shard_map/ppermute | solution.py:34
  109.1 4.7 %collective-permute-start.28 = (bf16[512,128]{1,0:T(8,128)(2,1)S(1)}, bf16[512,128]{1,0:T(8,128)(2,1)S(1)}, u32[]{:S(2)}, u32[]{:S(2)}) collective-permute-start(bf16[512,128]{1,0:T(8,128)(2,1)S(1)} %get-tuple-element.53), channel_id=1, source_target_pairs={{0,224},{8,232},{16,240},{24,248},{32,0},{40,8},{48,16},{56,24},{6... | collective-permute-start | bytes 393224 | tf_op jit(solution)/shard_map/ppermute | solution.py:34
  110.6 9.4 %collective-permute-start.24 = (bf16[1024,128]{1,0:T(8,128)(2,1)S(1)}, bf16[1024,128]{1,0:T(8,128)(2,1)S(1)}, u32[]{:S(2)}, u32[]{:S(2)}) collective-permute-start(bf16[1024,128]{1,0:T(8,128)(2,1)S(1)} %get-tuple-element.51), channel_id=1, source_target_pairs={{0,16},{8,24},{16,0},{24,8},{32,48},{40,56},{48,32},{56,40},{64,80... | collective-permute-start | bytes 786440 | tf_op jit(solution)/shard_map/ppermute | solution.py:30
  113.9 6.1 %collective-permute-start.23 = (bf16[768,128]{1,0:T(8,128)(2,1)S(1)}, bf16[768,128]{1,0:T(8,128)(2,1)S(1)}, u32[]{:S(2)}, u32[]{:S(2)}) collective-permute-start(bf16[768,128]{1,0:T(8,128)(2,1)S(1)} %pad_maximum_fusion.3), channel_id=1, source_target_pairs={{0,32},{8,40},{16,48},{24,56},{32,64},{40,72},{48,80},{56,88},{64,... | collective-permute-start | bytes 589832 | tf_op jit(solution)/shard_map/ppermute | solution.py:34
  115.5 4.9 %collective-permute-start.29 = (bf16[768,128]{1,0:T(8,128)(2,1)S(1)}, bf16[768,128]{1,0:T(8,128)(2,1)S(1)}, u32[]{:S(2)}, u32[]{:S(2)}) collective-permute-start(bf16[768,128]{1,0:T(8,128)(2,1)S(1)} %pad_maximum_fusion.6), channel_id=1, source_target_pairs={{0,224},{8,232},{16,240},{24,248},{32,0},{40,8},{48,16},{56,24},{6... | collective-permute-start | bytes 589832 | tf_op jit(solution)/shard_map/ppermute | solution.py:34
  116.7 10.1 %collective-permute-start.26 = (bf16[1024,128]{1,0:T(8,128)(2,1)S(1)}, bf16[1024,128]{1,0:T(8,128)(2,1)S(1)}, u32[]{:S(2)}, u32[]{:S(2)}) collective-permute-start(bf16[1024,128]{1,0:T(8,128)(2,1)S(1)} %get-tuple-element.52), channel_id=1, source_target_pairs={{0,16},{8,24},{16,0},{24,8},{32,48},{40,56},{48,32},{56,40},{64,80... | collective-permute-start | bytes 786440 | tf_op jit(solution)/shard_map/ppermute | solution.py:30
  120.5 6.3 %collective-permute-start.25 = (bf16[768,128]{1,0:T(8,128)(2,1)S(1)}, bf16[768,128]{1,0:T(8,128)(2,1)S(1)}, u32[]{:S(2)}, u32[]{:S(2)}) collective-permute-start(bf16[768,128]{1,0:T(8,128)(2,1)S(1)} %pad_maximum_fusion.4), channel_id=1, source_target_pairs={{0,32},{8,40},{16,48},{24,56},{32,64},{40,72},{48,80},{56,88},{64,... | collective-permute-start | bytes 589832 | tf_op jit(solution)/shard_map/ppermute | solution.py:34
  121.4 5.6 %collective-permute-start.30 = (bf16[768,128]{1,0:T(8,128)(2,1)S(1)}, bf16[768,128]{1,0:T(8,128)(2,1)S(1)}, u32[]{:S(2)}, u32[]{:S(2)}) collective-permute-start(bf16[768,128]{1,0:T(8,128)(2,1)S(1)} %pad_maximum_fusion.7), channel_id=1, source_target_pairs={{0,224},{8,232},{16,240},{24,248},{32,0},{40,8},{48,16},{56,24},{6... | collective-permute-start | bytes 589832 | tf_op jit(solution)/shard_map/ppermute | solution.py:34
  127.2 8.3 %collective-permute-start.27 = (bf16[768,128]{1,0:T(8,128)(2,1)S(1)}, bf16[768,128]{1,0:T(8,128)(2,1)S(1)}, u32[]{:S(2)}, u32[]{:S(2)}) collective-permute-start(bf16[768,128]{1,0:T(8,128)(2,1)S(1)} %pad_maximum_fusion.5), channel_id=1, source_target_pairs={{0,32},{8,40},{16,48},{24,56},{32,64},{40,72},{48,80},{56,88},{64,... | collective-permute-start | bytes 589832 | tf_op jit(solution)/shard_map/ppermute | solution.py:34
  129.0 5.3 %collective-permute-start.17 = (bf16[512,128]{1,0:T(8,128)(2,1)S(1)}, bf16[512,128]{1,0:T(8,128)(2,1)S(1)}, u32[]{:S(2)}, u32[]{:S(2)}) collective-permute-start(bf16[512,128]{1,0:T(8,128)(2,1)S(1)} %get-tuple-element.46), channel_id=1, source_target_pairs={{0,16},{8,24},{16,0},{24,8},{32,48},{40,56},{48,32},{56,40},{64,80... | collective-permute-start | bytes 393224 | tf_op jit(solution)/shard_map/ppermute | solution.py:30
  131.6 3.9 %collective-permute-start.31 = (bf16[512,128]{1,0:T(8,128)(2,1)S(1)}, bf16[512,128]{1,0:T(8,128)(2,1)S(1)}, u32[]{:S(2)}, u32[]{:S(2)}) collective-permute-start(bf16[512,128]{1,0:T(8,128)(2,1)S(1)} %get-tuple-element.59), channel_id=1, source_target_pairs={{0,224},{8,232},{16,240},{24,248},{32,0},{40,8},{48,16},{56,24},{6... | collective-permute-start | bytes 393224 | tf_op jit(solution)/shard_map/ppermute | solution.py:34
  135.7 10.4 %collective-permute-start.32 = (bf16[768,128]{1,0:T(8,128)(2,1)S(1)}, bf16[768,128]{1,0:T(8,128)(2,1)S(1)}, u32[]{:S(2)}, u32[]{:S(2)}) collective-permute-start(bf16[768,128]{1,0:T(8,128)(2,1)S(1)} %get-tuple-element.55), channel_id=1, source_target_pairs={{0,8},{8,0},{16,24},{24,16},{32,40},{40,32},{48,56},{56,48},{64,72... | collective-permute-start | bytes 589832 | tf_op jit(solution)/shard_map/ppermute | solution.py:30
  (7 other events, 92.7 us)

commit v8 on v6

--- a/solution.py
+++ b/solution.py
@@ -16,6 +16,7 @@
 SLOTS = 12
 W_ROWS = 128
 UNROLL = 4
+MOVES = (0, 6, 2, 5, 7, 1, 3, 4)
 
 
 def row_pairs(move):
@@ -28,6 +29,16 @@
 
 def quad_permute(x, flip):
     return lax.ppermute(x, "row", row_pairs(lambda z, q: (z, q ^ flip)))
+
+
+def col_move(x, k):
+    pairs = [(c, ((c >> 2) ^ (k >> 2)) * 4 + (c + k) % 4) for c in range(NCOL)]
+    return lax.ppermute(x, "col", pairs)
+
+
+def col_target(k, sign):
+    c = lax.axis_index("col")
+    return (((c >> 2) ^ (k >> 2)) << 2) + ((c + sign * (k & 3)) & 3)
 
 
 def z_shift(x, step):
@@ -138,7 +149,8 @@
 
 def forward_far_kernel(*refs):
     lists, refs = refs[:2], refs[2:]
-    adj0, adj1, near, far_a, far_b, out, acc, far, adj_vmem, rows, places, adj_sem = refs
+    adj0, adj1, near, far_a, far_b = refs[:5]
+    outs, (acc, far, adj_vmem, rows, places, adj_sem) = refs[5:13], refs[13:]
     n = list_slots(lists, (adj0, adj1), adj_vmem, adj_sem, rows, places, True, (16, 16))
     far[:2] = far_a[...]
     far[2:] = far_b[...]
@@ -151,21 +163,16 @@
         acc[rows[j]] += value
 
     slot_products(n, adj0, adj_vmem, adj_sem, product, add_to)
-    for row in range(8):
+    for k, out in zip(MOVES, outs):
+        row = col_target(k, 1)
         for i in range(2):
-            out[row, i] = acc[2 * row + i].astype(jnp.bfloat16)
-
-
-def backward_kernel(far, *refs):
-    lists, refs = refs[:2], refs[2:]
-    adj0, adj1, back = refs[:3]
-    acc, adj_vmem, rows, places, adj_sem = refs[-5:]
-    outs = refs[3:-5]
+            out[i] = acc[2 * row + i].astype(jnp.bfloat16)
+
+
+def backward_products(lists, adj_refs, back, acc, adj_vmem, rows, places, adj_sem, far):
     base = 16 if far else 0
     spare = acc.shape[0] - 1
-    n = list_slots(
-        lists, (adj0, adj1), adj_vmem, adj_sem, rows, places, far, (0, base + spare)
-    )
+    n = list_slots(lists, adj_refs, adj_vmem, adj_sem, rows, places, far, (0, base + spare))
     acc[...] = jnp.zeros_like(acc)
 
     def product(j):
@@ -180,18 +187,32 @@
     def add_to(j, value):
         acc[places[j] - base] += value
 
-    slot_products(n, adj0, adj_vmem, adj_sem, product, add_to)
-    if not far:
-        outs[0][...] = acc[:spare].astype(jnp.bfloat16)
-        return
+    slot_products(n, adj_refs[0], adj_vmem, adj_sem, product, add_to)
+
+
+def backward_far_kernel(*refs):
+    lists, adj_refs, received, refs = refs[:2], refs[2:4], refs[4:12], refs[12:]
+    up, down, back, acc, adj_vmem, rows, places, adj_sem, pieces = refs
+    for k, ref in zip(MOVES, received):
+        source = col_target(k, -1)
+        back[source] = ref[: 2 * TILE, :]
+        pieces[source] = ref[2 * TILE :, :]
+    backward_products(lists, adj_refs, back, acc, adj_vmem, rows, places, adj_sem, True)
     for k in range(QUAD):
-        rows = pl.ds((k & 1) * TILE, TILE)
-        outs[k >> 1][rows, :] = acc[k].astype(jnp.bfloat16)
-    piece = back[0, 2 * TILE :, :].astype(jnp.float32)
+        part = pl.ds((k & 1) * TILE, TILE)
+        (up, down)[k >> 1][part, :] = acc[k].astype(jnp.bfloat16)
+    piece = pieces[0].astype(jnp.float32)
     for c in range(1, NCOL):
-        piece = piece + back[c, 2 * TILE :, :].astype(jnp.float32)
-    for out in outs:
+        piece = piece + pieces[c].astype(jnp.float32)
+    for out in (up, down):
         out[2 * TILE :, :] = piece.astype(jnp.bfloat16)
+
+
+def backward_near_kernel(*refs):
+    lists, adj_refs, refs = refs[:2], refs[2:4], refs[4:]
+    back, out, acc, adj_vmem, rows, places, adj_sem = refs
+    backward_products(lists, adj_refs, back, acc, adj_vmem, rows, places, adj_sem, False)
+    out[...] = acc[: NZ * QUAD].astype(jnp.bfloat16)
 
 
 def split(x):
@@ -199,7 +220,7 @@
     return high, (x - high.astype(jnp.float32)).astype(jnp.bfloat16)
 
 
-def dense_kernel(agg_own, agg_other, weight, cot_own, cot_other, act_out, send_out):
+def dense_kernel(agg_own, agg_other, weight, cot_own, cot_other, act_out, send, send_x):
     first = (lax.axis_index("row") & 1) == 0
     own = agg_own[...]
     other = jnp.concatenate([agg_other[TILE:, :], agg_other[:TILE, :]], axis=0)
@@ -228,50 +249,54 @@
     rows = ((0,), (0,))
     w_part = (
         dot(own_hi, grad_hi, rows) + dot(own_lo, grad_hi, rows) + dot(own_hi, grad_lo, rows)
-    ).astype(jnp.bfloat16)
-    for c in range(NCOL):
-        send_out[c, : 2 * TILE, :] = back
-        piece = w_part[64 * (c // 4) : 64 * (c // 4) + 64]
-        send_out[c, 2 * TILE : 2 * TILE + 64, :] = piece[:, :HALF]
-        send_out[c, 2 * TILE + 64 :, :] = piece[:, HALF:]
+    )
+    x_lo = lax.axis_index("col") >> 2
+    for out, dest in ((send, x_lo), (send_x, 1 - x_lo)):
+        out[: 2 * TILE, :] = back
+        piece = jnp.where(dest == 0, w_part[:64], w_part[64:]).astype(jnp.bfloat16)
+        out[2 * TILE : 2 * TILE + 64, :] = piece[:, :HALF]
+        out[2 * TILE + 64 :, :] = piece[:, HALF:]
 
 
 def f32(ref, start, rows=TILE):
     return ref[start : start + rows, :].astype(jnp.float32)
 
 
-def away_kernel(parts, own, up1, up2, up3, up4, down1, down2, down3, down4, message, w_z):
+def ring_end_kernel(
+    parts, own, up1, up2, up3, up4, down1, down2, down3, down4, kept, message, by_step
+):
     z = lax.axis_index("row") >> 2
     half, size = 2 * TILE, QUAD * TILE
-    by_step = (
+    pieces = (
         (own, half),
         (down1, half),
         (down2, size),
         (down3, size),
-        (up4, half),
+        (up4, size),
         (up3, size),
         (up2, size),
         (up1, half),
     )
-    for k, (ref, start) in enumerate(by_step):
-        w_z[(k + z) & 7] = ref[start:, :]
-    w_sum = w_z[0].astype(jnp.float32)
+    for k, (ref, start) in enumerate(pieces):
+        by_step[(k + z) & 7] = ref[start:, :]
+    w_sum = by_step[0].astype(jnp.float32)
     for a in range(1, NZ):
-        w_sum = w_sum + w_z[a].astype(jnp.float32)
+        w_sum = w_sum + by_step[a].astype(jnp.float32)
     message[half:, :] = w_sum.astype(jnp.bfloat16)
-    for k in range(2):
+    for k in range(QUAD):
         start = k * TILE
-        total = parts[2 + k].astype(jnp.float32) + f32(up4, start) + f32(down4, start)
-        message[start : start + TILE, :] = total.astype(jnp.bfloat16)
-
-
-def middle_kernel(parts, up4, down4, sent, from_x, w_lo, w_both, mine, message, w_here):
+        total = parts[k].astype(jnp.float32) + f32(up4, start) + f32(down4, start)
+        if k < 2:
+            kept[k] = total
+        else:
+            message[start - half : start - half + TILE, :] = total.astype(jnp.bfloat16)
+
+
+def middle_kernel(kept, sent, from_x, w_lo, w_both, mine, message, w_here):
     x_lo = lax.axis_index("col") >> 2
     half = 2 * TILE
     for k, ref in enumerate((mine, message)):
-        start = k * TILE
-        total = parts[k].astype(jnp.float32) + f32(up4, start) + f32(down4, start)
-        ref[:TILE, :] = (total + f32(from_x, start)).astype(jnp.bfloat16)
+        ref[:TILE, :] = (kept[k] + f32(from_x, k * TILE)).astype(jnp.bfloat16)
     sums = (
         f32(sent, half, W_ROWS) + f32(from_x, half, W_ROWS),
         w_lo[...].astype(jnp.float32) + w_both[...].astype(jnp.float32),
@@ -388,7 +413,7 @@
 def forward_far(lists, adj0, adj1, near, far_a, far_b):
     return local(
         forward_far_kernel,
-        (shape(8, 2, TILE, HALF),),
+        (shape(2, TILE, HALF),) * NCOL,
         7,
         "forward_far",
         scalars=2,
@@ -400,43 +425,57 @@
         + SLOT_SCRATCH
         + [pltpu.SemaphoreType.DMA((LIST,))],
         cost=cost(3, 4),
-    )(*lists, adj0, adj1, near, far_a, far_b)[0]
-
-
-def backward_tiles(lists, adj0, adj1, back, far):
-    places = QUAD if far else NZ * QUAD
+    )(*lists, adj0, adj1, near, far_a, far_b)
+
+
+def backward_far(lists, adj0, adj1, received):
     message = shape(2 * TILE + W_ROWS, HALF)
     return local(
-        functools.partial(backward_kernel, far),
-        (message, message) if far else (shape(places, TILE, HALF),),
-        5,
-        "backward_far" if far else "backward_near",
+        backward_far_kernel,
+        (message, message, shape(NCOL, 2 * TILE, HALF)),
+        12,
+        "backward_far",
         scalars=2,
         any_in=2,
-        scratch=[pltpu.VMEM((places + 1, TILE, HALF), jnp.float32)]
+        scratch=[pltpu.VMEM((QUAD + 1, TILE, HALF), jnp.float32)]
+        + SLOT_SCRATCH
+        + [pltpu.SemaphoreType.DMA((LIST,)), pltpu.VMEM((NCOL, W_ROWS, HALF), jnp.bfloat16)],
+        cost=cost(3, 2),
+    )(*lists, adj0, adj1, *received)
+
+
+def backward_near(lists, adj0, adj1, back):
+    return local(
+        backward_near_kernel,
+        (shape(NZ * QUAD, TILE, HALF),),
+        5,
+        "backward_near",
+        scalars=2,
+        any_in=2,
+        scratch=[pltpu.VMEM((NZ * QUAD + 1, TILE, HALF), jnp.float32)]
         + SLOT_SCRATCH
         + [pltpu.SemaphoreType.DMA((LIST,))],
-        cost=cost(3, 2) if far else cost(21, 6),
-    )(*lists, adj0, adj1, back)
+        cost=cost(21, 6),
+    )(*lists, adj0, adj1, back)[0]
 
 
 def dense(agg_own, agg_other, weight, cot_own, cot_other):
     return local(
         dense_kernel,
-        (shape(TILE, 2 * HALF), shape(NCOL, 2 * TILE + W_ROWS, HALF)),
+        (shape(TILE, 2 * HALF),) + (shape(2 * TILE + W_ROWS, HALF),) * 2,
         5,
         "dense",
     )(agg_own, agg_other, weight, cot_own, cot_other)
 
 
-def away(parts, *messages):
-    return local(
-        away_kernel,
-        (shape(2 * TILE + W_ROWS, HALF),),
+def ring_end(parts, *messages):
+    return local(
+        ring_end_kernel,
+        (shape(2, TILE, HALF, dtype=jnp.float32), shape(2 * TILE + W_ROWS, HALF)),
         10,
-        "away",
+        "ring_end",
         scratch=[pltpu.VMEM((NZ, W_ROWS, HALF), jnp.bfloat16)],
-    )(parts, *messages)[0]
+    )(parts, *messages)
 
 
 def middle(*operands):
@@ -447,7 +486,7 @@
             shape(TILE + 4 * W_ROWS, HALF),
             shape(2, W_ROWS, HALF, dtype=jnp.float32),
         ),
-        7,
+        5,
         "middle",
     )(*operands)
 
@@ -484,17 +523,18 @@
     up3, down3 = z_shift(up2, 1), z_shift(down2, -1)
     far_a, far_b = z_shift(up3[:2], 1), z_shift(down3[2:], -1)
     near = forward_near(lists, adj0, adj1, [chunk, down1, down2, down3, up3, up2, up1])
-    partial = forward_far(lists, adj0, adj1, near, far_a, far_b)
-
-    shares = lax.all_to_all(partial, "col", 0, 0, tiled=True)
-    agg = shares.reshape(NCOL, 2 * TILE, HALF).astype(jnp.float32).sum(axis=0)
+    shares = forward_far(lists, adj0, adj1, near, far_a, far_b)
+    agg = sum(
+        (col_move(share, k) if k else share).astype(jnp.float32)
+        for k, share in zip(MOVES, shares)
+    ).reshape(2 * TILE, HALF)
     agg_other = quad_permute(agg, 1)
-    activated, send = dense(agg, agg_other, weight, cotangent, cot1)
-    received = lax.all_to_all(send, "col", 0, 0, tiled=True)
+    activated, send, send_x = dense(agg, agg_other, weight, cotangent, cot1)
+    received = [col_move(send if k < 4 else send_x, k) if k else send for k in MOVES]
 
     half, size = 2 * TILE, QUAD * TILE
-    own, own_down = backward_tiles(lists, adj0, adj1, received, True)
-    (blocks,) = backward_tiles(lists, adj0, adj1, received, False)
+    own, own_down, back = backward_far(lists, adj0, adj1, received)
+    blocks = backward_near(lists, adj0, adj1, back)
     parts = blocks.reshape(NZ, size, HALF)
     up1, down1 = z_shift(own, 1), z_shift(own_down, -1)
     up = [add(parts[3, :half], up1[:half]), parts[3, half:], up1[half:]]
@@ -503,13 +543,10 @@
     up = [add(parts[2], up2[:size]), up2[size:]]
     down = [add(parts[6], down2[:size]), down2[size:]]
     up3, down3 = z_shift(jnp.concatenate(up), 1), z_shift(jnp.concatenate(down), -1)
-    up = add(parts[1], up3[:size])
-    down = add(parts[7], down3[:size])
-    up4_away = z_shift(jnp.concatenate([up[half:], up3[size:]]), 1)
-    down4_away = z_shift(down[half:], -1)
-    up4, down4 = z_shift(up[:half], 1), z_shift(down[:half], -1)
-
-    to_x = away(blocks, own, up1, up2, up3, up4_away, down1, down2, down3, down4_away)
+    up4 = z_shift(jnp.concatenate([add(parts[1], up3[:size]), up3[size:]]), 1)
+    down4 = z_shift(add(parts[7], down3[:size]), -1)
+
+    kept, to_x = ring_end(blocks, own, up1, up2, up3, up4, down1, down2, down3, down4)
     w_send = to_x[half:]
     from_x = quad_permute(to_x, 2)
     w_lo = lax.ppermute(w_send, "col", [(c, c ^ 4) for c in range(NCOL)])
@@ -517,7 +554,7 @@
         (r * NCOL + c, (r ^ 2) * NCOL + (c ^ 4)) for r in range(NZ * QUAD) for c in range(NCOL)
     ]
     w_both = lax.ppermute(w_send, ("row", "col"), both)
-    mine, to_core, w_here = middle(blocks, up4, down4, to_x, from_x, w_lo, w_both)
+    mine, to_core, w_here = middle(kept, to_x, from_x, w_lo, w_both)
     grad, weight_grad = last(mine, quad_permute(to_core, 1), w_here)
     return (activated, weight_grad, grad[None])
 

time: 142 us -> 140 us (0.986); the launches traced: 142 us -> 138 us
  blocking collectives: 34.5 us -> 0 us
  starting transfers between devices: 54.8 us -> 70.9 us
  waiting for transfers between devices: 35.6 us -> 47.6 us
  Pallas kernels: 12.2 us -> 14.7 us
    all_to_all x2 -> x0, blocking collectives: 34.5 us -> none  [the longest x1 19.5 us: per_device(): received = lax.all_to_all(send, 'col', 0, 0, tiled=True)]
    ppermute x0 -> x14, starting transfers between devices: none -> 24.7 us  [col_move(): return lax.ppermute(x, 'col', pairs)]
    ppermute x0 -> x14, waiting for transfers between devices: none -> 12.6 us  [col_move(): return lax.ppermute(x, 'col', pairs)]
    ppermute x7, starting transfers between devices: 24.8 us -> 17.2 us  [quad_permute(): return lax.ppermute(x, 'row', row_pairs(lambda z, q: (z, q ^ flip)))]
    ppermute x18 -> x16, waiting for transfers between devices: 32.4 us -> 28.9 us  [z_shift(): return lax.ppermute(x, 'row', row_pairs(lambda z, q: (z + step, q)))]
    ppermute x18 -> x16, starting transfers between devices: 29.4 us -> 26.3 us  [z_shift(): return lax.ppermute(x, 'row', row_pairs(lambda z, q: (z + step, q)))]
    pallas_call x5, Pallas kernels: 7.66 us -> 9.41 us  [the longest x1 3.65 us: backward_near(): local(backward_near_kernel, (shape(NZ * QUAD, TILE, HALF),), 5, 'backward...]
    ppermute x1, waiting for transfers between devices: 0.01 us -> 1.65 us  [per_device(): w_both = lax.ppermute(w_send, ('row', 'col'), both)]
  transfers between devices with their start and end apart: 27 -> 39, of which waited for: 14 -> 19; matrix products, arithmetic and copies ran while one was open for 0% -> 0% of each run, Pallas kernels for 4% -> 6%
where the time goes in v8:
time: 140 us; the launch traced here: 138 us
  starting transfers between devices  70.9 us (51%)
  waiting for transfers between devices  47.6 us (34%)
  Pallas kernels  14.7 us (10%)
  local copies, waits for them, and re-layouts  2.4 us (2%)
  between operations  1.67 us (1%)
    ppermute x16, waiting for transfers between devices, z_shift(): return lax.ppermute(x, 'row', row_pairs(lambda z, q: (z + step, q)))  28.9 us
    ppermute x16, starting transfers between devices, z_shift(): return lax.ppermute(x, 'row', row_pairs(lambda z, q: (z + step, q)))  26.3 us
    ppermute x14, starting transfers between devices, col_move(): return lax.ppermute(x, 'col', pairs)  24.7 us
    ppermute x7, starting transfers between devices, quad_permute(): return lax.ppermute(x, 'row', row_pairs(lambda z, q: (z, q ^ flip)))  17.2 us
    ppermute x14, waiting for transfers between devices, col_move(): return lax.ppermute(x, 'col', pairs)  12.6 us
    pallas_call x1, Pallas kernels, backward_near(): local(backward_near_kernel, (shape(NZ * QUAD, TILE, HALF),), 5, 'backward...  3.65 us
    ppermute x7, waiting for transfers between devices, quad_permute(): return lax.ppermute(x, 'row', row_pairs(lambda z, q: (z, q ^ flip)))  3.3 us
    pallas_call x1, Pallas kernels, forward_near(): local(forward_near_kernel, (shape(17, TILE, HALF, dtype=jnp.float32),), 1...  3.24 us
  transfers between devices with their start and end apart: 39, of which 19 were waited for; matrix products, arithmetic and copies ran while one was open for 0% of the time, Pallas kernels for 6%

profile of v8, /device:TPU:1, one launch (start us, length us, event | category | flops | bytes accessed | tf_op | source)
XLA Modules:
  0.0 138.0 jit_solution(13916923086577611451)
XLA Ops:
  0.6 3.7 %collective-permute-start = (bf16[256,256]{1,0:T(8,128)(2,1)}, bf16[256,256]{1,0:T(8,128)(2,1)S(1)}, u32[]{:S(2)}, u32[]{:S(2)}) collective-permute-start(bf16[256,256]{1,0:T(8,128)(2,1)} %bitcast.51), channel_id=1, source_target_pairs={{0,16},{8,24},{16,0},{24,8},{32,48},{40,56},{48,32},{56,40},{64,80... | collective-permute-start | bytes 393224 | tf_op jit(solution)/shard_map/ppermute | solution.py:31
  11.8 4.7 %collective-permute-start.3 = (bf16[4,256,128]{2,1,0:T(8,128)(2,1)S(1)}, bf16[4,256,128]{2,1,0:T(8,128)(2,1)S(1)}, u32[]{:S(2)}, u32[]{:S(2)}) collective-permute-start(bf16[4,256,128]{2,1,0:T(8,128)(2,1)S(1)} %pad_maximum_fusion.5.refs_4_), channel_id=1, source_target_pairs={{0,224},{8,232},{16,240},{24,248},{32,0},{40,8},{48,16},{56,24},{6... | collective-permute-start | bytes 786440 | tf_op jit(solution)/shard_map/ppermute | solution.py:45
  16.5 5.6 %collective-permute-done.3.refs_5_ = bf16[4,256,128]{2,1,0:T(8,128)(2,1)S(1)} collective-permute-done((bf16[4,256,128]{2,1,0:T(8,128)(2,1)S(1)}, bf16[4,256,128]{2,1,0:T(8,128)(2,1)S(1)}, u32[]{:S(2)}, u32[]{:S(2)}) %collective-permute-start.3) | collective-permute-done | bytes 262176 | tf_op jit(solution)/shard_map/ppermute | solution.py:45
  22.1 3.4 %collective-permute-start.4 = (bf16[4,256,128]{2,1,0:T(8,128)(2,1)S(1)}, bf16[4,256,128]{2,1,0:T(8,128)(2,1)S(1)}, u32[]{:S(2)}, u32[]{:S(2)}) collective-permute-start(bf16[4,256,128]{2,1,0:T(8,128)(2,1)S(1)} %collective-permute-done.3.refs_5_), channel_id=1, source_target_pairs={{0,224},{8,232},{16,240},{24,248},{32,0},{40,8},{48,16},{56,24},{6... | collective-permute-start | bytes 786440 | tf_op jit(solution)/shard_map/ppermute | solution.py:45
  25.5 4.6 %collective-permute-done.4.refs_6_ = bf16[4,256,128]{2,1,0:T(8,128)(2,1)S(1)} collective-permute-done((bf16[4,256,128]{2,1,0:T(8,128)(2,1)S(1)}, bf16[4,256,128]{2,1,0:T(8,128)(2,1)S(1)}, u32[]{:S(2)}, u32[]{:S(2)}) %collective-permute-start.4) | collective-permute-done | bytes 262176 | tf_op jit(solution)/shard_map/ppermute | solution.py:45
  30.1 3.4 %collective-permute-start.5 = (bf16[4,256,128]{2,1,0:T(8,128)(2,1)S(1)}, bf16[4,256,128]{2,1,0:T(8,128)(2,1)S(1)}, u32[]{:S(2)}, u32[]{:S(2)}) collective-permute-start(bf16[4,256,128]{2,1,0:T(8,128)(2,1)S(1)} %collective-permute-done.4.refs_6_), channel_id=1, source_target_pairs={{0,224},{8,232},{16,240},{24,248},{32,0},{40,8},{48,16},{56,24},{6... | collective-permute-start | bytes 786440 | tf_op jit(solution)/shard_map/ppermute | solution.py:45
  33.6 3.7 %collective-permute-done.5.refs_7_ = bf16[4,256,128]{2,1,0:T(8,128)(2,1)S(1)} collective-permute-done((bf16[4,256,128]{2,1,0:T(8,128)(2,1)S(1)}, bf16[4,256,128]{2,1,0:T(8,128)(2,1)S(1)}, u32[]{:S(2)}, u32[]{:S(2)}) %collective-permute-start.5) | collective-permute-done | bytes 262176 | tf_op jit(solution)/shard_map/ppermute | solution.py:45
  37.3 3.5 %collective-permute-start.10 = (bf16[2,256,128]{2,1,0:T(8,128)(2,1)S(1)}, bf16[2,256,128]{2,1,0:T(8,128)(2,1)S(1)}, u32[]{:S(2)}, u32[]{:S(2)}) collective-permute-start(bf16[2,256,128]{2,1,0:T(8,128)(2,1)S(1)} %slice.127), channel_id=1, source_target_pairs={{0,224},{8,232},{16,240},{24,248},{32,0},{40,8},{48,16},{56,24},{6... | collective-permute-start | bytes 393224 | tf_op jit(solution)/shard_map/ppermute | solution.py:45
  40.9 3.2 %forward_near.1.refs_4_ = f32[17,256,128]{2,1,0:T(8,128)S(1)} custom-call(s32[25]{0:T(128)S(1)} %get-tuple-element.29.refs_0_, s32[25]{0:T(128)S(1)} %fusion.6.refs_1_, bf16[12,256,256]{2,1,0:T(8,128)(2,1)S(1)} %bitcast.43, bf16[12,256,256]{2,1,0:T(8,128)(2,1)S(1)} %collective-permute-done.2.refs_3_, bf16[4,256,128]{2,1,0:T(8,128)(2,1)S(1)} %pad_maximum_fusion.5.refs_4_, ...), custom_call_target="tpu_custom_call" | custom-call | flops 352321536 | bytes 6291456 | tf_op jit(solution)/shard_map/forward_near/pallas_call | solution.py:399
  45.9 2.0 %forward_far.1 = (bf16[2,256,128]{2,1,0:T(8,128)(2,1)S(1)}, bf16[2,256,128]{2,1,0:T(8,128)(2,1)S(1)}, bf16[2,256,128]{2,1,0:T(8,128)(2,1)S(1)}, bf16[2,256,128]{...) custom-call(s32[25]{0:T(128)S(1)} %get-tuple-element.29.refs_0_, ...), custom_call_target="tpu_custom_call" | custom-call | flops 50331648 | bytes 4194304 | tf_op jit(solution)/shard_map/forward_far/pallas_call | solution.py:414
  47.9 2.1 %collective-permute-start.11 = (bf16[2,256,128]{2,1,0:T(8,128)(2,1)S(1)}, bf16[2,256,128]{2,1,0:T(8,128)(2,1)S(1)}, u32[]{:S(2)}, u32[]{:S(2)}) collective-permute-start(bf16[2,256,128]{2,1,0:T(8,128)(2,1)S(1)} %get-tuple-element.35), channel_id=1, source_target_pairs={{0,6},{1,7},{2,4},{3,5},{4,2},{5,3},{6,0},{7,1},{8,14},{9,15},{10,... | collective-permute-start | bytes 393224 | tf_op jit(solution)/shard_map/ppermute | solution.py:36
  51.0 2.0 %collective-permute-start.13 = (bf16[2,256,128]{2,1,0:T(8,128)(2,1)S(1)}, bf16[2,256,128]{2,1,0:T(8,128)(2,1)S(1)}, u32[]{:S(2)}, u32[]{:S(2)}) collective-permute-start(bf16[2,256,128]{2,1,0:T(8,128)(2,1)S(1)} %get-tuple-element.37), channel_id=1, source_target_pairs={{0,5},{1,6},{2,7},{3,4},{4,1},{5,2},{6,3},{7,0},{8,13},{9,14},{10,... | collective-permute-start | bytes 393224 | tf_op jit(solution)/shard_map/ppermute | solution.py:36
  54.6 2.7 %collective-permute-start.16 = (bf16[2,256,128]{2,1,0:T(8,128)(2,1)S(1)}, bf16[2,256,128]{2,1,0:T(8,128)(2,1)S(1)}, u32[]{:S(2)}, u32[]{:S(2)}) collective-permute-start(bf16[2,256,128]{2,1,0:T(8,128)(2,1)S(1)} %get-tuple-element.40), channel_id=1, source_target_pairs={{0,3},{1,0},{2,1},{3,2},{4,7},{5,4},{6,5},{7,6},{8,11},{9,8},{10,9... | collective-permute-start | bytes 393224 | tf_op jit(solution)/shard_map/ppermute | solution.py:36
  57.3 3.2 %collective-permute-start.17 = (bf16[2,256,128]{2,1,0:T(8,128)(2,1)S(1)}, bf16[2,256,128]{2,1,0:T(8,128)(2,1)S(1)}, u32[]{:S(2)}, u32[]{:S(2)}) collective-permute-start(bf16[2,256,128]{2,1,0:T(8,128)(2,1)S(1)} %get-tuple-element.41), channel_id=1, source_target_pairs={{0,4},{1,5},{2,6},{3,7},{4,0},{5,1},{6,2},{7,3},{8,12},{9,13},{10,... | collective-permute-start | bytes 393224 | tf_op jit(solution)/shard_map/ppermute | solution.py:36
  60.5 3.0 %collective-permute-done.15 = bf16[2,256,128]{2,1,0:T(8,128)(2,1)S(1)} collective-permute-done((bf16[2,256,128]{2,1,0:T(8,128)(2,1)S(1)}, bf16[2,256,128]{2,1,0:T(8,128)(2,1)S(1)}, u32[]{:S(2)}, u32[]{:S(2)}) %collective-permute-start.15) | collective-permute-done | bytes 131104 | tf_op jit(solution)/shard_map/ppermute | solution.py:36
  63.8 4.4 %collective-permute-start.18 = (f32[512,128]{1,0:T(8,128)S(1)}, f32[512,128]{1,0:T(8,128)S(1)}, u32[]{:S(2)}, u32[]{:S(2)}) collective-permute-start(f32[512,128]{1,0:T(8,128)S(1)} %bitcast.49), channel_id=1, source_target_pairs={{0,8},{8,0},{16,24},{24,16},{32,40},{40,32},{48,56},{56,48},{64,72... | collective-permute-start | bytes 786440 | tf_op jit(solution)/shard_map/ppermute | solution.py:31
  71.1 3.1 %collective-permute-start.20 = (bf16[640,128]{1,0:T(8,128)(2,1)S(1)}, bf16[640,128]{1,0:T(8,128)(2,1)S(1)}, u32[]{:S(2)}, u32[]{:S(2)}) collective-permute-start(bf16[640,128]{1,0:T(8,128)(2,1)S(1)} %get-tuple-element.44), channel_id=1, source_target_pairs={{0,6},{1,7},{2,4},{3,5},{4,2},{5,3},{6,0},{7,1},{8,14},{9,15},{10,... | collective-permute-start | bytes 491528 | tf_op jit(solution)/shard_map/ppermute | solution.py:36
  76.2 2.6 %collective-permute-start.23 = (bf16[640,128]{1,0:T(8,128)(2,1)S(1)}, bf16[640,128]{1,0:T(8,128)(2,1)S(1)}, u32[]{:S(2)}, u32[]{:S(2)}) collective-permute-start(bf16[640,128]{1,0:T(8,128)(2,1)S(1)} %get-tuple-element.44), channel_id=1, source_target_pairs={{0,7},{1,4},{2,5},{3,6},{4,3},{5,0},{6,1},{7,2},{8,15},{9,12},{10,... | collective-permute-start | bytes 491528 | tf_op jit(solution)/shard_map/ppermute | solution.py:36
  79.0 2.5 %collective-permute-start.25 = (bf16[640,128]{1,0:T(8,128)(2,1)S(1)}, bf16[640,128]{1,0:T(8,128)(2,1)S(1)}, u32[]{:S(2)}, u32[]{:S(2)}) collective-permute-start(bf16[640,128]{1,0:T(8,128)(2,1)S(1)} %get-tuple-element.43.refs_4_), channel_id=1, source_target_pairs={{0,3},{1,0},{2,1},{3,2},{4,7},{5,4},{6,5},{7,6},{8,11},{9,8},{10,9... | collective-permute-start | bytes 491528 | tf_op jit(solution)/shard_map/ppermute | solution.py:36
  81.5 5.2 %collective-permute-done.21.refs_6_ = bf16[640,128]{1,0:T(8,128)(2,1)S(1)} collective-permute-done((bf16[640,128]{1,0:T(8,128)(2,1)S(1)}, bf16[640,128]{1,0:T(8,128)(2,1)S(1)}, u32[]{:S(2)}, u32[]{:S(2)}) %collective-permute-start.21) | collective-permute-done | bytes 163872 | tf_op jit(solution)/shard_map/ppermute | solution.py:36
  86.7 2.0 %collective-permute-start.26 = (bf16[640,128]{1,0:T(8,128)(2,1)S(1)}, bf16[640,128]{1,0:T(8,128)(2,1)S(1)}, u32[]{:S(2)}, u32[]{:S(2)}) collective-permute-start(bf16[640,128]{1,0:T(8,128)(2,1)S(1)} %get-tuple-element.44), channel_id=1, source_target_pairs={{0,4},{1,5},{2,6},{3,7},{4,0},{5,1},{6,2},{7,3},{8,12},{9,13},{10,... | collective-permute-start | bytes 491528 | tf_op jit(solution)/shard_map/ppermute | solution.py:36
  90.2 2.5 %collective-permute-done.26.refs_11_ = bf16[640,128]{1,0:T(8,128)(2,1)S(1)} collective-permute-done((bf16[640,128]{1,0:T(8,128)(2,1)S(1)}, bf16[640,128]{1,0:T(8,128)(2,1)S(1)}, u32[]{:S(2)}, u32[]{:S(2)}) %collective-permute-start.26) | collective-permute-done | bytes 163872 | tf_op jit(solution)/shard_map/ppermute | solution.py:36
  92.7 2.0 %backward_far.1 = (bf16[640,128]{1,0:T(8,128)(2,1)S(1)}, bf16[640,128]{1,0:T(8,128)(2,1)S(1)}, bf16[8,512,128]{2,1,0:T(8,128)(2,1)S(1)}) custom-call(s32[25]{0:T(128)S(1)} %get-tuple-element.29.refs_0_, s32[25]{0:T(128)S(1)} %fusion.6.refs_1_, bf16[12,256,256]{2,1,0:T(8,128)(2,1)S(1)} %bitcast.45, bf16[12,256,256]{2,1,0:T(8,128)(2,1)S(1)} %collective-permute-done.2.refs_3_, ...), custom_call_target="tpu_custom_call" | custom-call | flops 50331648 | bytes 2097152 | tf_op jit(solution)/shard_map/backward_far/pallas_call | solution.py:433
  94.8 2.7 %collective-permute-start.31 = (bf16[640,128]{1,0:T(8,128)(2,1)S(1)}, bf16[640,128]{1,0:T(8,128)(2,1)S(1)}, u32[]{:S(2)}, u32[]{:S(2)}) collective-permute-start(bf16[640,128]{1,0:T(8,128)(2,1)S(1)} %get-tuple-element.47), channel_id=1, source_target_pairs={{0,224},{8,232},{16,240},{24,248},{32,0},{40,8},{48,16},{56,24},{6... | collective-permute-start | bytes 491528 | tf_op jit(solution)/shard_map/ppermute | solution.py:45
  97.5 3.7 %backward_near.1.parts = bf16[32,256,128]{2,1,0:T(8,128)(2,1)S(1)} custom-call(s32[25]{0:T(128)S(1)} %get-tuple-element.29.refs_0_, s32[25]{0:T(128)S(1)} %fusion.6.refs_1_, bf16[12,256,256]{2,1,0:T(8,128)(2,1)S(1)} %bitcast.46, bf16[12,256,256]{2,1,0:T(8,128)(2,1)S(1)} %collective-permute-done.2.refs_3_, bf16[8,512,128]{2,1,0:T(8,128)(2,1)S(1)} %get-tuple-element.45.refs_4_), custom_call_target="tpu_custom_call" | custom-call | flops 352321536 | bytes 6291456 | tf_op jit(solution)/shard_map/backward_near/pallas_call | solution.py:448
  101.6 2.7 %collective-permute-start.32 = (bf16[1152,128]{1,0:T(8,128)(2,1)S(1)}, bf16[1152,128]{1,0:T(8,128)(2,1)S(1)}, u32[]{:S(2)}, u32[]{:S(2)}) collective-permute-start(bf16[1152,128]{1,0:T(8,128)(2,1)S(1)} %pad_maximum_fusion.3), channel_id=1, source_target_pairs={{0,224},{8,232},{16,240},{24,248},{32,0},{40,8},{48,16},{56,24},{6... | collective-permute-start | bytes 884744 | tf_op jit(solution)/shard_map/ppermute | solution.py:45
  104.3 5.1 %collective-permute-done.28.up2 = bf16[1152,128]{1,0:T(8,128)(2,1)S(1)} collective-permute-done((bf16[1152,128]{1,0:T(8,128)(2,1)S(1)}, bf16[1152,128]{1,0:T(8,128)(2,1)S(1)}, u32[]{:S(2)}, u32[]{:S(2)}) %collective-permute-start.28) | collective-permute-done | bytes 294944 | tf_op jit(solution)/shard_map/ppermute | solution.py:45
  109.8 2.7 %collective-permute-start.33 = (bf16[1152,128]{1,0:T(8,128)(2,1)S(1)}, bf16[1152,128]{1,0:T(8,128)(2,1)S(1)}, u32[]{:S(2)}, u32[]{:S(2)}) collective-permute-start(bf16[1152,128]{1,0:T(8,128)(2,1)S(1)} %pad_maximum_fusion.4), channel_id=1, source_target_pairs={{0,224},{8,232},{16,240},{24,248},{32,0},{40,8},{48,16},{56,24},{6... | collective-permute-start | bytes 884744 | tf_op jit(solution)/shard_map/ppermute | solution.py:45
  112.5 4.2 %collective-permute-done.29.up3 = bf16[1152,128]{1,0:T(8,128)(2,1)S(1)} collective-permute-done((bf16[1152,128]{1,0:T(8,128)(2,1)S(1)}, bf16[1152,128]{1,0:T(8,128)(2,1)S(1)}, u32[]{:S(2)}, u32[]{:S(2)}) %collective-permute-start.29) | collective-permute-done | bytes 294944 | tf_op jit(solution)/shard_map/ppermute | solution.py:45
  117.1 2.7 %collective-permute-start.34 = (bf16[1024,128]{1,0:T(8,128)(2,1)S(1)}, bf16[1024,128]{1,0:T(8,128)(2,1)S(1)}, u32[]{:S(2)}, u32[]{:S(2)}) collective-permute-start(bf16[1024,128]{1,0:T(8,128)(2,1)S(1)} %fusion), channel_id=1, source_target_pairs={{0,224},{8,232},{16,240},{24,248},{32,0},{40,8},{48,16},{56,24},{6... | collective-permute-start | bytes 786440 | tf_op jit(solution)/shard_map/ppermute | solution.py:45
  119.8 3.3 %collective-permute-done.34.down4 = bf16[1024,128]{1,0:T(8,128)(2,1)S(1)} collective-permute-done((bf16[1024,128]{1,0:T(8,128)(2,1)S(1)}, bf16[1024,128]{1,0:T(8,128)(2,1)S(1)}, u32[]{:S(2)}, u32[]{:S(2)}) %collective-permute-start.34) | collective-permute-done | bytes 262176 | tf_op jit(solution)/shard_map/ppermute | solution.py:45
  130.1 6.1 %collective-permute-start.38 = (bf16[768,128]{1,0:T(8,128)(2,1)S(1)}, bf16[768,128]{1,0:T(8,128)(2,1)S(1)}, u32[]{:S(2)}, u32[]{:S(2)}) collective-permute-start(bf16[768,128]{1,0:T(8,128)(2,1)S(1)} %get-tuple-element.51), channel_id=1, source_target_pairs={{0,8},{8,0},{16,24},{24,16},{32,40},{40,32},{48,56},{56,48},{64,72... | collective-permute-start | bytes 589832 | tf_op jit(solution)/shard_map/ppermute | solution.py:31
  (93 shorter events, 28.1 us)
Async XLA Ops:
  0.6 8.7 %collective-permute-start = (bf16[256,256]{1,0:T(8,128)(2,1)}, bf16[256,256]{1,0:T(8,128)(2,1)S(1)}, u32[]{:S(2)}, u32[]{:S(2)}) collective-permute-start(bf16[256,256]{1,0:T(8,128)(2,1)} %bitcast.51), channel_id=1, source_target_pairs={{0,16},{8,24},{16,0},{24,8},{32,48},{40,56},{48,32},{56,40},{64,80... | collective-permute-start | bytes 393224 | tf_op jit(solution)/shard_map/ppermute | solution.py:31
  4.3 36.6 %collective-permute-start.2 = (bf16[12,256,256]{2,1,0:T(8,128)(2,1)}, bf16[12,256,256]{2,1,0:T(8,128)(2,1)S(1)}, u32[]{:S(2)}, u32[]{:S(2)}) collective-permute-start(bf16[12,256,256]{2,1,0:T(8,128)(2,1)} %bitcast.42), channel_id=1, source_target_pairs={{0,8},{8,0},{16,24},{24,16},{32,40},{40,32},{48,56},{56,48},{64,72... | collective-permute-start | bytes 4718600 | tf_op jit(solution)/shard_map/ppermute | solution.py:31
  11.8 10.3 %collective-permute-start.3 = (bf16[4,256,128]{2,1,0:T(8,128)(2,1)S(1)}, bf16[4,256,128]{2,1,0:T(8,128)(2,1)S(1)}, u32[]{:S(2)}, u32[]{:S(2)}) collective-permute-start(bf16[4,256,128]{2,1,0:T(8,128)(2,1)S(1)} %pad_maximum_fusion.5.refs_4_), channel_id=1, source_target_pairs={{0,224},{8,232},{16,240},{24,248},{32,0},{40,8},{48,16},{56,24},{6... | collective-permute-start | bytes 786440 | tf_op jit(solution)/shard_map/ppermute | solution.py:45
  16.5 9.0 %collective-permute-start.6 = (bf16[4,256,128]{2,1,0:T(8,128)(2,1)S(1)}, bf16[4,256,128]{2,1,0:T(8,128)(2,1)S(1)}, u32[]{:S(2)}, u32[]{:S(2)}) collective-permute-start(bf16[4,256,128]{2,1,0:T(8,128)(2,1)S(1)} %pad_maximum_fusion.5.refs_4_), channel_id=1, source_target_pairs={{0,32},{8,40},{16,48},{24,56},{32,64},{40,72},{48,80},{56,88},{64,... | collective-permute-start | bytes 786440 | tf_op jit(solution)/shard_map/ppermute | solution.py:45
  22.1 8.1 %collective-permute-start.4 = (bf16[4,256,128]{2,1,0:T(8,128)(2,1)S(1)}, bf16[4,256,128]{2,1,0:T(8,128)(2,1)S(1)}, u32[]{:S(2)}, u32[]{:S(2)}) collective-permute-start(bf16[4,256,128]{2,1,0:T(8,128)(2,1)S(1)} %collective-permute-done.3.refs_5_), channel_id=1, source_target_pairs={{0,224},{8,232},{16,240},{24,248},{32,0},{40,8},{48,16},{56,24},{6... | collective-permute-start | bytes 786440 | tf_op jit(solution)/shard_map/ppermute | solution.py:45
  25.5 8.1 %collective-permute-start.7 = (bf16[4,256,128]{2,1,0:T(8,128)(2,1)S(1)}, bf16[4,256,128]{2,1,0:T(8,128)(2,1)S(1)}, u32[]{:S(2)}, u32[]{:S(2)}) collective-permute-start(bf16[4,256,128]{2,1,0:T(8,128)(2,1)S(1)} %collective-permute-done.6.refs_10_), channel_id=1, source_target_pairs={{0,32},{8,40},{16,48},{24,56},{32,64},{40,72},{48,80},{56,88},{64,... | collective-permute-start | bytes 786440 | tf_op jit(solution)/shard_map/ppermute | solution.py:45
  30.1 7.1 %collective-permute-start.5 = (bf16[4,256,128]{2,1,0:T(8,128)(2,1)S(1)}, bf16[4,256,128]{2,1,0:T(8,128)(2,1)S(1)}, u32[]{:S(2)}, u32[]{:S(2)}) collective-permute-start(bf16[4,256,128]{2,1,0:T(8,128)(2,1)S(1)} %collective-permute-done.4.refs_6_), channel_id=1, source_target_pairs={{0,224},{8,232},{16,240},{24,248},{32,0},{40,8},{48,16},{56,24},{6... | collective-permute-start | bytes 786440 | tf_op jit(solution)/shard_map/ppermute | solution.py:45
  33.6 7.2 %collective-permute-start.8 = (bf16[4,256,128]{2,1,0:T(8,128)(2,1)S(1)}, bf16[4,256,128]{2,1,0:T(8,128)(2,1)S(1)}, u32[]{:S(2)}, u32[]{:S(2)}) collective-permute-start(bf16[4,256,128]{2,1,0:T(8,128)(2,1)S(1)} %collective-permute-done.7.refs_9_), channel_id=1, source_target_pairs={{0,32},{8,40},{16,48},{24,56},{32,64},{40,72},{48,80},{56,88},{64,... | collective-permute-start | bytes 786440 | tf_op jit(solution)/shard_map/ppermute | solution.py:45
  37.3 6.9 %collective-permute-start.10 = (bf16[2,256,128]{2,1,0:T(8,128)(2,1)S(1)}, bf16[2,256,128]{2,1,0:T(8,128)(2,1)S(1)}, u32[]{:S(2)}, u32[]{:S(2)}) collective-permute-start(bf16[2,256,128]{2,1,0:T(8,128)(2,1)S(1)} %slice.127), channel_id=1, source_target_pairs={{0,224},{8,232},{16,240},{24,248},{32,0},{40,8},{48,16},{56,24},{6... | collective-permute-start | bytes 393224 | tf_op jit(solution)/shard_map/ppermute | solution.py:45
  47.9 6.7 %collective-permute-start.11 = (bf16[2,256,128]{2,1,0:T(8,128)(2,1)S(1)}, bf16[2,256,128]{2,1,0:T(8,128)(2,1)S(1)}, u32[]{:S(2)}, u32[]{:S(2)}) collective-permute-start(bf16[2,256,128]{2,1,0:T(8,128)(2,1)S(1)} %get-tuple-element.35), channel_id=1, source_target_pairs={{0,6},{1,7},{2,4},{3,5},{4,2},{5,3},{6,0},{7,1},{8,14},{9,15},{10,... | collective-permute-start | bytes 393224 | tf_op jit(solution)/shard_map/ppermute | solution.py:36
  50.0 7.3 %collective-permute-start.12 = (bf16[2,256,128]{2,1,0:T(8,128)(2,1)S(1)}, bf16[2,256,128]{2,1,0:T(8,128)(2,1)S(1)}, u32[]{:S(2)}, u32[]{:S(2)}) collective-permute-start(bf16[2,256,128]{2,1,0:T(8,128)(2,1)S(1)} %get-tuple-element.36), channel_id=1, source_target_pairs={{0,2},{1,3},{2,0},{3,1},{4,6},{5,7},{6,4},{7,5},{8,10},{9,11},{10,... | collective-permute-start | bytes 393224 | tf_op jit(solution)/shard_map/ppermute | solution.py:36
  51.0 9.4 %collective-permute-start.13 = (bf16[2,256,128]{2,1,0:T(8,128)(2,1)S(1)}, bf16[2,256,128]{2,1,0:T(8,128)(2,1)S(1)}, u32[]{:S(2)}, u32[]{:S(2)}) collective-permute-start(bf16[2,256,128]{2,1,0:T(8,128)(2,1)S(1)} %get-tuple-element.37), channel_id=1, source_target_pairs={{0,5},{1,6},{2,7},{3,4},{4,1},{5,2},{6,3},{7,0},{8,13},{9,14},{10,... | collective-permute-start | bytes 393224 | tf_op jit(solution)/shard_map/ppermute | solution.py:36
  53.0 7.4 %collective-permute-start.14 = (bf16[2,256,128]{2,1,0:T(8,128)(2,1)S(1)}, bf16[2,256,128]{2,1,0:T(8,128)(2,1)S(1)}, u32[]{:S(2)}, u32[]{:S(2)}) collective-permute-start(bf16[2,256,128]{2,1,0:T(8,128)(2,1)S(1)} %get-tuple-element.38), channel_id=1, source_target_pairs={{0,7},{1,4},{2,5},{3,6},{4,3},{5,0},{6,1},{7,2},{8,15},{9,12},{10,... | collective-permute-start | bytes 393224 | tf_op jit(solution)/shard_map/ppermute | solution.py:36
  54.6 8.9 %collective-permute-start.15 = (bf16[2,256,128]{2,1,0:T(8,128)(2,1)S(1)}, bf16[2,256,128]{2,1,0:T(8,128)(2,1)S(1)}, u32[]{:S(2)}, u32[]{:S(2)}) collective-permute-start(bf16[2,256,128]{2,1,0:T(8,128)(2,1)S(1)} %get-tuple-element.39), channel_id=1, source_target_pairs={{0,1},{1,2},{2,3},{3,0},{4,5},{5,6},{6,7},{7,4},{8,9},{9,10},{10,1... | collective-permute-start | bytes 393224 | tf_op jit(solution)/shard_map/ppermute | solution.py:36
  54.6 8.9 %collective-permute-start.16 = (bf16[2,256,128]{2,1,0:T(8,128)(2,1)S(1)}, bf16[2,256,128]{2,1,0:T(8,128)(2,1)S(1)}, u32[]{:S(2)}, u32[]{:S(2)}) collective-permute-start(bf16[2,256,128]{2,1,0:T(8,128)(2,1)S(1)} %get-tuple-element.40), channel_id=1, source_target_pairs={{0,3},{1,0},{2,1},{3,2},{4,7},{5,4},{6,5},{7,6},{8,11},{9,8},{10,9... | collective-permute-start | bytes 393224 | tf_op jit(solution)/shard_map/ppermute | solution.py:36
  57.3 6.4 %collective-permute-start.17 = (bf16[2,256,128]{2,1,0:T(8,128)(2,1)S(1)}, bf16[2,256,128]{2,1,0:T(8,128)(2,1)S(1)}, u32[]{:S(2)}, u32[]{:S(2)}) collective-permute-start(bf16[2,256,128]{2,1,0:T(8,128)(2,1)S(1)} %get-tuple-element.41), channel_id=1, source_target_pairs={{0,4},{1,5},{2,6},{3,7},{4,0},{5,1},{6,2},{7,3},{8,12},{9,13},{10,... | collective-permute-start | bytes 393224 | tf_op jit(solution)/shard_map/ppermute | solution.py:36
  71.1 7.8 %collective-permute-start.20 = (bf16[640,128]{1,0:T(8,128)(2,1)S(1)}, bf16[640,128]{1,0:T(8,128)(2,1)S(1)}, u32[]{:S(2)}, u32[]{:S(2)}) collective-permute-start(bf16[640,128]{1,0:T(8,128)(2,1)S(1)} %get-tuple-element.44), channel_id=1, source_target_pairs={{0,6},{1,7},{2,4},{3,5},{4,2},{5,3},{6,0},{7,1},{8,14},{9,15},{10,... | collective-permute-start | bytes 491528 | tf_op jit(solution)/shard_map/ppermute | solution.py:36
  74.2 12.5 %collective-permute-start.21 = (bf16[640,128]{1,0:T(8,128)(2,1)S(1)}, bf16[640,128]{1,0:T(8,128)(2,1)S(1)}, u32[]{:S(2)}, u32[]{:S(2)}) collective-permute-start(bf16[640,128]{1,0:T(8,128)(2,1)S(1)} %get-tuple-element.43.refs_4_), channel_id=1, source_target_pairs={{0,2},{1,3},{2,0},{3,1},{4,6},{5,7},{6,4},{7,5},{8,10},{9,11},{10,... | collective-permute-start | bytes 491528 | tf_op jit(solution)/shard_map/ppermute | solution.py:36
  75.2 13.4 %collective-permute-start.22 = (bf16[640,128]{1,0:T(8,128)(2,1)S(1)}, bf16[640,128]{1,0:T(8,128)(2,1)S(1)}, u32[]{:S(2)}, u32[]{:S(2)}) collective-permute-start(bf16[640,128]{1,0:T(8,128)(2,1)S(1)} %get-tuple-element.44), channel_id=1, source_target_pairs={{0,5},{1,6},{2,7},{3,4},{4,1},{5,2},{6,3},{7,0},{8,13},{9,14},{10,... | collective-permute-start | bytes 491528 | tf_op jit(solution)/shard_map/ppermute | solution.py:36
  76.2 12.4 %collective-permute-start.23 = (bf16[640,128]{1,0:T(8,128)(2,1)S(1)}, bf16[640,128]{1,0:T(8,128)(2,1)S(1)}, u32[]{:S(2)}, u32[]{:S(2)}) collective-permute-start(bf16[640,128]{1,0:T(8,128)(2,1)S(1)} %get-tuple-element.44), channel_id=1, source_target_pairs={{0,7},{1,4},{2,5},{3,6},{4,3},{5,0},{6,1},{7,2},{8,15},{9,12},{10,... | collective-permute-start | bytes 491528 | tf_op jit(solution)/shard_map/ppermute | solution.py:36
  78.8 11.4 %collective-permute-start.24 = (bf16[640,128]{1,0:T(8,128)(2,1)S(1)}, bf16[640,128]{1,0:T(8,128)(2,1)S(1)}, u32[]{:S(2)}, u32[]{:S(2)}) collective-permute-start(bf16[640,128]{1,0:T(8,128)(2,1)S(1)} %get-tuple-element.43.refs_4_), channel_id=1, source_target_pairs={{0,1},{1,2},{2,3},{3,0},{4,5},{5,6},{6,7},{7,4},{8,9},{9,10},{10,1... | collective-permute-start | bytes 491528 | tf_op jit(solution)/shard_map/ppermute | solution.py:36
  79.0 11.2 %collective-permute-start.25 = (bf16[640,128]{1,0:T(8,128)(2,1)S(1)}, bf16[640,128]{1,0:T(8,128)(2,1)S(1)}, u32[]{:S(2)}, u32[]{:S(2)}) collective-permute-start(bf16[640,128]{1,0:T(8,128)(2,1)S(1)} %get-tuple-element.43.refs_4_), channel_id=1, source_target_pairs={{0,3},{1,0},{2,1},{3,2},{4,7},{5,4},{6,5},{7,6},{8,11},{9,8},{10,9... | collective-permute-start | bytes 491528 | tf_op jit(solution)/shard_map/ppermute | solution.py:36
  94.7 6.4 %collective-permute-start.27 = (bf16[640,128]{1,0:T(8,128)(2,1)S(1)}, bf16[640,128]{1,0:T(8,128)(2,1)S(1)}, u32[]{:S(2)}, u32[]{:S(2)}) collective-permute-start(bf16[640,128]{1,0:T(8,128)(2,1)S(1)} %get-tuple-element.46.own), channel_id=1, source_target_pairs={{0,32},{8,40},{16,48},{24,56},{32,64},{40,72},{48,80},{56,88},{64,... | collective-permute-start | bytes 491528 | tf_op jit(solution)/shard_map/ppermute | solution.py:45
  94.8 6.4 %collective-permute-start.31 = (bf16[640,128]{1,0:T(8,128)(2,1)S(1)}, bf16[640,128]{1,0:T(8,128)(2,1)S(1)}, u32[]{:S(2)}, u32[]{:S(2)}) collective-permute-start(bf16[640,128]{1,0:T(8,128)(2,1)S(1)} %get-tuple-element.47), channel_id=1, source_target_pairs={{0,224},{8,232},{16,240},{24,248},{32,0},{40,8},{48,16},{56,24},{6... | collective-permute-start | bytes 491528 | tf_op jit(solution)/shard_map/ppermute | solution.py:45
  101.3 8.1 %collective-permute-start.28 = (bf16[1152,128]{1,0:T(8,128)(2,1)S(1)}, bf16[1152,128]{1,0:T(8,128)(2,1)S(1)}, u32[]{:S(2)}, u32[]{:S(2)}) collective-permute-start(bf16[1152,128]{1,0:T(8,128)(2,1)S(1)} %pad_maximum_fusion), channel_id=1, source_target_pairs={{0,32},{8,40},{16,48},{24,56},{32,64},{40,72},{48,80},{56,88},{64,... | collective-permute-start | bytes 884744 | tf_op jit(solution)/shard_map/ppermute | solution.py:45
  101.6 8.1 %collective-permute-start.32 = (bf16[1152,128]{1,0:T(8,128)(2,1)S(1)}, bf16[1152,128]{1,0:T(8,128)(2,1)S(1)}, u32[]{:S(2)}, u32[]{:S(2)}) collective-permute-start(bf16[1152,128]{1,0:T(8,128)(2,1)S(1)} %pad_maximum_fusion.3), channel_id=1, source_target_pairs={{0,224},{8,232},{16,240},{24,248},{32,0},{40,8},{48,16},{56,24},{6... | collective-permute-start | bytes 884744 | tf_op jit(solution)/shard_map/ppermute | solution.py:45
  109.6 7.2 %collective-permute-start.29 = (bf16[1152,128]{1,0:T(8,128)(2,1)S(1)}, bf16[1152,128]{1,0:T(8,128)(2,1)S(1)}, u32[]{:S(2)}, u32[]{:S(2)}) collective-permute-start(bf16[1152,128]{1,0:T(8,128)(2,1)S(1)} %pad_maximum_fusion.1), channel_id=1, source_target_pairs={{0,32},{8,40},{16,48},{24,56},{32,64},{40,72},{48,80},{56,88},{64,... | collective-permute-start | bytes 884744 | tf_op jit(solution)/shard_map/ppermute | solution.py:45
  109.8 7.2 %collective-permute-start.33 = (bf16[1152,128]{1,0:T(8,128)(2,1)S(1)}, bf16[1152,128]{1,0:T(8,128)(2,1)S(1)}, u32[]{:S(2)}, u32[]{:S(2)}) collective-permute-start(bf16[1152,128]{1,0:T(8,128)(2,1)S(1)} %pad_maximum_fusion.4), channel_id=1, source_target_pairs={{0,224},{8,232},{16,240},{24,248},{32,0},{40,8},{48,16},{56,24},{6... | collective-permute-start | bytes 884744 | tf_op jit(solution)/shard_map/ppermute | solution.py:45
  116.9 6.9 %collective-permute-start.30 = (bf16[1152,128]{1,0:T(8,128)(2,1)S(1)}, bf16[1152,128]{1,0:T(8,128)(2,1)S(1)}, u32[]{:S(2)}, u32[]{:S(2)}) collective-permute-start(bf16[1152,128]{1,0:T(8,128)(2,1)S(1)} %pad_maximum_fusion.2), channel_id=1, source_target_pairs={{0,32},{8,40},{16,48},{24,56},{32,64},{40,72},{48,80},{56,88},{64,... | collective-permute-start | bytes 884744 | tf_op jit(solution)/shard_map/ppermute | solution.py:45
  117.1 6.0 %collective-permute-start.34 = (bf16[1024,128]{1,0:T(8,128)(2,1)S(1)}, bf16[1024,128]{1,0:T(8,128)(2,1)S(1)}, u32[]{:S(2)}, u32[]{:S(2)}) collective-permute-start(bf16[1024,128]{1,0:T(8,128)(2,1)S(1)} %fusion), channel_id=1, source_target_pairs={{0,224},{8,232},{16,240},{24,248},{32,0},{40,8},{48,16},{56,24},{6... | collective-permute-start | bytes 786440 | tf_op jit(solution)/shard_map/ppermute | solution.py:45
  123.9 6.1 %collective-permute-start.35 = (bf16[640,128]{1,0:T(8,128)(2,1)S(1)}, bf16[640,128]{1,0:T(8,128)(2,1)S(1)}, u32[]{:S(2)}, u32[]{:S(2)}) collective-permute-start(bf16[640,128]{1,0:T(8,128)(2,1)S(1)} %get-tuple-element.49.sent), channel_id=1, source_target_pairs={{0,16},{8,24},{16,0},{24,8},{32,48},{40,56},{48,32},{56,40},{64,80... | collective-permute-start | bytes 491528 | tf_op jit(solution)/shard_map/ppermute | solution.py:31
  130.1 7.1 %collective-permute-start.38 = (bf16[768,128]{1,0:T(8,128)(2,1)S(1)}, bf16[768,128]{1,0:T(8,128)(2,1)S(1)}, u32[]{:S(2)}, u32[]{:S(2)}) collective-permute-start(bf16[768,128]{1,0:T(8,128)(2,1)S(1)} %get-tuple-element.51), channel_id=1, source_target_pairs={{0,8},{8,0},{16,24},{24,16},{32,40},{40,32},{48,56},{56,48},{64,72... | collective-permute-start | bytes 589832 | tf_op jit(solution)/shard_map/ppermute | solution.py:31
  (13 other events, 121.0 us)

commit v9 on v8

--- a/solution.py
+++ b/solution.py
@@ -16,6 +16,8 @@
 SLOTS = 12
 W_ROWS = 128
 UNROLL = 4
+PART = 16
+LIST = 4 * PART + 4
 MOVES = (0, 6, 2, 5, 7, 1, 3, 4)
 
 
@@ -83,135 +85,129 @@
         message[TILE + 16 :, :] = x_block[:, :HALF]
 
 
-def list_slots(lists, adj_refs, adj_vmem, adj_sem, rows, places, far, dummy):
+def list_slots(own, partner, lists):
     device = lax.axis_index("row")
     z, q = device >> 2, device & 3
-    n = jnp.int32(0)
-    for i in range(2):
-        count = lists[i][24]
+    for i, slots in enumerate((own, partner)):
+        near, far = jnp.int32(0), jnp.int32(0)
         for s in range(SLOTS):
-            tile = lists[i][12 + s]
-            row = lists[i][s]
+            tile = slots[12 + s]
             place = (((tile >> 2) - z) & 7) * QUAD + ((tile & 3) ^ q)
-            live = (s < count) & (((place >> 2) == 4) == far)
-            rows[n] = row * 2 + i
-            places[n] = place
-
-            @pl.when(live)
-            def _(i=i, s=s, n=n):
-                pltpu.make_async_copy(
-                    adj_refs[i].at[s], adj_vmem.at[n], adj_sem.at[n]
-                ).start()
-
-            n = n + live.astype(jnp.int32)
-    for u in range(UNROLL - 1):
-        rows[n + u], places[n + u] = dummy
-    return n
-
-
-def slot_products(n, adj_ref, adj_vmem, adj_sem, product, add_to):
-    @pl.loop(0, (n + UNROLL - 1) >> 2)
-    def _(step):
-        slots = [step * UNROLL + u for u in range(UNROLL)]
-        for j in slots:
-
-            @pl.when(j < n)
-            def _(j=j):
-                pltpu.make_async_copy(adj_ref.at[0], adj_vmem.at[j], adj_sem.at[j]).wait()
-
-        values = [product(j) for j in slots]
-        for j, value in zip(slots, values):
-            add_to(j, value)
-
-
-def forward_near_kernel(*refs):
-    lists, (adj0, adj1), refs = refs[:2], refs[2:4], refs[4:]
-    pieces, (acc, panel, adj_vmem, rows, places, panel_sem, adj_sem) = refs[:7], refs[7:]
+            live = (s < slots[24]).astype(jnp.int32)
+            is_far = ((place >> 2) == 4).astype(jnp.int32)
+            lists[i * PART + is_far * (2 * PART + far - near) + near] = (
+                s * 1024 + slots[s] * 64 + place
+            )
+            far = far + live * is_far
+            near = near + live * (1 - is_far)
+        for u in range(UNROLL - 1):
+            lists[i * PART + near + u] = 8 * 64 + 32
+        lists[4 * PART + i] = near
+        lists[4 * PART + 2 + i] = far
+
+
+def slot_products(lists, far, adj_refs, product, add_to):
+    unroll = 1 if far else UNROLL
+    for i, adj in enumerate(adj_refs):
+        part = 2 * far + i
+
+        @pl.loop(0, (lists[4 * PART + part] + unroll - 1) // unroll)
+        def _(step, i=i, adj=adj, part=part):
+            codes = [lists[part * PART + step * unroll + u] for u in range(unroll)]
+            places = [((code >> 6) & 15, i, code & 63) for code in codes]
+            values = [product(adj[code >> 10], *at) for code, at in zip(codes, places)]
+            for value, at in zip(values, places):
+                add_to(value, *at)
+
+
+def forward_near_kernel(own_any, partner_any, adj0, adj1, *refs):
+    pieces, (acc, lists, panel, own, partner, sems) = refs[:7], refs[7:]
     copies = [
-        pltpu.make_async_copy(piece, panel.at[pl.ds(place * QUAD, QUAD)], panel_sem.at[place])
-        for place, piece in zip((0, 1, 2, 3, 5, 6, 7), pieces)
+        pltpu.make_async_copy(own_any, own, sems.at[0]),
+        pltpu.make_async_copy(partner_any, partner, sems.at[1]),
     ]
     for copy in copies:
         copy.start()
-    n = list_slots(lists, (adj0, adj1), adj_vmem, adj_sem, rows, places, False, (16, 0))
+    for place, piece in zip((0, 1, 2, 3, 5, 6, 7), pieces):
+        panel[place * QUAD : (place + 1) * QUAD] = piece[...]
     acc[...] = jnp.zeros_like(acc)
     for copy in copies:
         copy.wait()
-
-    def product(j):
-        return jnp.dot(adj_vmem[j], panel[places[j]], preferred_element_type=jnp.float32)
-
-    def add_to(j, value):
-        acc[rows[j]] += value
-
-    slot_products(n, adj0, adj_vmem, adj_sem, product, add_to)
-
-
-def forward_far_kernel(*refs):
-    lists, refs = refs[:2], refs[2:]
-    adj0, adj1, near, far_a, far_b = refs[:5]
-    outs, (acc, far, adj_vmem, rows, places, adj_sem) = refs[5:13], refs[13:]
-    n = list_slots(lists, (adj0, adj1), adj_vmem, adj_sem, rows, places, True, (16, 16))
+    list_slots(own, partner, lists)
+
+    def product(tile, row, i, place):
+        return jnp.dot(tile, panel[place & 31], preferred_element_type=jnp.float32)
+
+    def add_to(value, row, i, place):
+        acc[2 * row + i] += value
+
+    slot_products(lists, False, (adj0, adj1), product, add_to)
+
+
+def forward_far_kernel(lists_any, adj0, adj1, near, far_a, far_b, *refs):
+    outs, (acc, far, lists, sem) = refs[:NCOL], refs[NCOL:]
+    copy = pltpu.make_async_copy(lists_any, lists, sem)
+    copy.start()
     far[:2] = far_a[...]
     far[2:] = far_b[...]
     acc[...] = near[...]
-
-    def product(j):
-        return jnp.dot(adj_vmem[j], far[places[j] - 16], preferred_element_type=jnp.float32)
-
-    def add_to(j, value):
-        acc[rows[j]] += value
-
-    slot_products(n, adj0, adj_vmem, adj_sem, product, add_to)
+    copy.wait()
+
+    def product(tile, row, i, place):
+        return jnp.dot(tile, far[place & 3], preferred_element_type=jnp.float32)
+
+    def add_to(value, row, i, place):
+        acc[2 * row + i] += value
+
+    slot_products(lists, True, (adj0, adj1), product, add_to)
     for k, out in zip(MOVES, outs):
         row = col_target(k, 1)
         for i in range(2):
             out[i] = acc[2 * row + i].astype(jnp.bfloat16)
 
 
-def backward_products(lists, adj_refs, back, acc, adj_vmem, rows, places, adj_sem, far):
-    base = 16 if far else 0
-    spare = acc.shape[0] - 1
-    n = list_slots(lists, adj_refs, adj_vmem, adj_sem, rows, places, far, (0, base + spare))
-    acc[...] = jnp.zeros_like(acc)
-
-    def product(j):
-        row = rows[j]
+def backward_products(lists, adj_refs, back, acc, far):
+    def product(tile, row, i, place):
         return lax.dot_general(
-            adj_vmem[j],
-            back[row >> 1, pl.ds((row & 1) * TILE, TILE), :],
+            tile,
+            back[row & 7, pl.ds(i * TILE, TILE), :],
             (((0,), (0,)), ((), ())),
             preferred_element_type=jnp.float32,
         )
 
-    def add_to(j, value):
-        acc[places[j] - base] += value
-
-    slot_products(n, adj_refs[0], adj_vmem, adj_sem, product, add_to)
-
-
-def backward_far_kernel(*refs):
-    lists, adj_refs, received, refs = refs[:2], refs[2:4], refs[4:12], refs[12:]
-    up, down, back, acc, adj_vmem, rows, places, adj_sem, pieces = refs
+    def add_to(value, row, i, place):
+        acc[place & 3 if far else place] += value
+
+    slot_products(lists, far, adj_refs, product, add_to)
+
+
+def backward_far_kernel(lists_any, adj0, adj1, *refs):
+    received, (up, down, back, acc, lists, sem, pieces) = refs[:NCOL], refs[NCOL:]
+    copy = pltpu.make_async_copy(lists_any, lists, sem)
+    copy.start()
     for k, ref in zip(MOVES, received):
         source = col_target(k, -1)
         back[source] = ref[: 2 * TILE, :]
         pieces[source] = ref[2 * TILE :, :]
-    backward_products(lists, adj_refs, back, acc, adj_vmem, rows, places, adj_sem, True)
-    for k in range(QUAD):
-        part = pl.ds((k & 1) * TILE, TILE)
-        (up, down)[k >> 1][part, :] = acc[k].astype(jnp.bfloat16)
+    acc[...] = jnp.zeros_like(acc)
     piece = pieces[0].astype(jnp.float32)
     for c in range(1, NCOL):
         piece = piece + pieces[c].astype(jnp.float32)
     for out in (up, down):
         out[2 * TILE :, :] = piece.astype(jnp.bfloat16)
-
-
-def backward_near_kernel(*refs):
-    lists, adj_refs, refs = refs[:2], refs[2:4], refs[4:]
-    back, out, acc, adj_vmem, rows, places, adj_sem = refs
-    backward_products(lists, adj_refs, back, acc, adj_vmem, rows, places, adj_sem, False)
+    copy.wait()
+    backward_products(lists, (adj0, adj1), back, acc, True)
+    for k in range(QUAD):
+        part = pl.ds((k & 1) * TILE, TILE)
+        (up, down)[k >> 1][part, :] = acc[k].astype(jnp.bfloat16)
+
+
+def backward_near_kernel(lists_any, adj0, adj1, back, out, acc, lists, sem):
+    copy = pltpu.make_async_copy(lists_any, lists, sem)
+    copy.start()
+    acc[...] = jnp.zeros_like(acc)
+    copy.wait()
+    backward_products(lists, (adj0, adj1), back, acc, False)
     out[...] = acc[: NZ * QUAD].astype(jnp.bfloat16)
 
 
@@ -344,12 +340,7 @@
     return pltpu.CompilerParams(vmem_limit_bytes=mib << 20)
 
 
-LIST = 2 * SLOTS + UNROLL
-SLOT_SCRATCH = [
-    pltpu.VMEM((LIST, TILE, TILE), jnp.bfloat16),
-    pltpu.SMEM((LIST,), jnp.int32),
-    pltpu.SMEM((LIST,), jnp.int32),
-]
+LIST_SCRATCH = [pltpu.SMEM((LIST,), jnp.int32), pltpu.SemaphoreType.DMA]
 
 
 def cost(slots, size):
@@ -395,37 +386,38 @@
     )(own_keep, own_message, x_block)
 
 
-def forward_near(lists, adj0, adj1, pieces):
+def forward_near(own, partner, adj0, adj1, pieces):
     return local(
         forward_near_kernel,
-        (shape(17, TILE, HALF, dtype=jnp.float32),),
+        (shape(18, TILE, HALF, dtype=jnp.float32), shape(LIST, dtype=jnp.int32)),
         11,
         "forward_near",
-        scalars=2,
-        any_in=9,
-        scratch=[pltpu.VMEM((NZ * QUAD, TILE, HALF), jnp.bfloat16)]
-        + SLOT_SCRATCH
-        + [pltpu.SemaphoreType.DMA((NZ,)), pltpu.SemaphoreType.DMA((LIST,))],
+        any_in=2,
+        scalar_out=1,
+        scratch=[
+            pltpu.VMEM((NZ * QUAD, TILE, HALF), jnp.bfloat16),
+            pltpu.SMEM((25,), jnp.int32),
+            pltpu.SMEM((25,), jnp.int32),
+            pltpu.SemaphoreType.DMA((2,)),
+        ],
         cost=cost(21, 6),
-    )(*lists, adj0, adj1, *pieces)[0]
+    )(own, partner, adj0, adj1, *pieces)
 
 
 def forward_far(lists, adj0, adj1, near, far_a, far_b):
     return local(
         forward_far_kernel,
         (shape(2, TILE, HALF),) * NCOL,
-        7,
+        6,
         "forward_far",
-        scalars=2,
-        any_in=2,
+        any_in=1,
         scratch=[
-            pltpu.VMEM((17, TILE, HALF), jnp.float32),
+            pltpu.VMEM((18, TILE, HALF), jnp.float32),
             pltpu.VMEM((QUAD, TILE, HALF), jnp.bfloat16),
         ]
-        + SLOT_SCRATCH
-        + [pltpu.SemaphoreType.DMA((LIST,))],
+        + LIST_SCRATCH,
         cost=cost(3, 4),
-    )(*lists, adj0, adj1, near, far_a, far_b)
+    )(lists, adj0, adj1, near, far_a, far_b)
 
 
 def backward_far(lists, adj0, adj1, received):
@@ -433,30 +425,26 @@
     return local(
         backward_far_kernel,
         (message, message, shape(NCOL, 2 * TILE, HALF)),
-        12,
+        11,
         "backward_far",
-        scalars=2,
-        any_in=2,
-        scratch=[pltpu.VMEM((QUAD + 1, TILE, HALF), jnp.float32)]
-        + SLOT_SCRATCH
-        + [pltpu.SemaphoreType.DMA((LIST,)), pltpu.VMEM((NCOL, W_ROWS, HALF), jnp.bfloat16)],
+        any_in=1,
+        scratch=[pltpu.VMEM((QUAD, TILE, HALF), jnp.float32)]
+        + LIST_SCRATCH
+        + [pltpu.VMEM((NCOL, W_ROWS, HALF), jnp.bfloat16)],
         cost=cost(3, 2),
-    )(*lists, adj0, adj1, *received)
+    )(lists, adj0, adj1, *received)
 
 
 def backward_near(lists, adj0, adj1, back):
     return local(
         backward_near_kernel,
         (shape(NZ * QUAD, TILE, HALF),),
-        5,
+        4,
         "backward_near",
-        scalars=2,
-        any_in=2,
-        scratch=[pltpu.VMEM((NZ * QUAD + 1, TILE, HALF), jnp.float32)]
-        + SLOT_SCRATCH
-        + [pltpu.SemaphoreType.DMA((LIST,))],
+        any_in=1,
+        scratch=[pltpu.VMEM((NZ * QUAD + 1, TILE, HALF), jnp.float32)] + LIST_SCRATCH,
         cost=cost(21, 6),
-    )(*lists, adj0, adj1, back)[0]
+    )(lists, adj0, adj1, back)[0]
 
 
 def dense(agg_own, agg_other, weight, cot_own, cot_other):
@@ -514,7 +502,7 @@
     from_core = quad_permute(message, 1)
     core_keep = from_core[16:].reshape(2, TILE, HALF)
     chunk = jnp.stack([keep[0], core_keep[0], keep[1], core_keep[1]])
-    lists = (own_lists, from_core[0, :25].astype(jnp.int32))
+    partner_lists = from_core[0, :25].astype(jnp.int32)
     adj1 = quad_permute(adj0, 1)
     cot1 = quad_permute(cotangent, 1)
 
@@ -522,7 +510,9 @@
     up2, down2 = z_shift(up1, 1), z_shift(down1, -1)
     up3, down3 = z_shift(up2, 1), z_shift(down2, -1)
     far_a, far_b = z_shift(up3[:2], 1), z_shift(down3[2:], -1)
-    near = forward_near(lists, adj0, adj1, [chunk, down1, down2, down3, up3, up2, up1])
+    near, lists = forward_near(
+        own_lists, partner_lists, adj0, adj1, [chunk, down1, down2, down3, up3, up2, up1]
+    )
     shares = forward_far(lists, adj0, adj1, near, far_a, far_b)
     agg = sum(
         (col_move(share, k) if k else share).astype(jnp.float32)

time: 140 us -> 136 us (0.971)
  Pallas kernels: 14.7 us -> 9.61 us
  waiting for transfers between devices: 47.6 us -> 51.8 us
  starting transfers between devices: 70.9 us -> 69.2 us
    ppermute x14, starting transfers between devices: 24.7 us -> 20.6 us  [col_move(): return lax.ppermute(x, 'col', pairs)]
    pallas_call x3, Pallas kernels: 8.89 us -> 4.96 us  [the longest x1 2.31 us: forward_near(): local(forward_near_kernel, (shape(18, TILE, HALF, dtype=jnp.float32), sha...]
    ppermute x7, starting transfers between devices: 17.2 us -> 21.1 us  [quad_permute(): return lax.ppermute(x, 'row', row_pairs(lambda z, q: (z, q ^ flip)))]
    ppermute x14, waiting for transfers between devices: 12.6 us -> 15.8 us  [col_move(): return lax.ppermute(x, 'col', pairs)]
  transfers between devices with their start and end apart: 39 -> 39, of which waited for: 19 -> 20; matrix products, arithmetic and copies ran while one was open for 0% -> 0% of each run, Pallas kernels for 6% -> 4%
where the time goes in v9:
time: 136 us; the launch traced here: 135 us
  starting transfers between devices  69.2 us (51%)
  waiting for transfers between devices  51.8 us (38%)
  Pallas kernels  9.61 us (7%)
  local copies, waits for them, and re-layouts  2.39 us (2%)
  between operations  1.63 us (1%)
    ppermute x16, waiting for transfers between devices, z_shift(): return lax.ppermute(x, 'row', row_pairs(lambda z, q: (z + step, q)))  29.6 us
    ppermute x16, starting transfers between devices, z_shift(): return lax.ppermute(x, 'row', row_pairs(lambda z, q: (z + step, q)))  26.5 us
    ppermute x7, starting transfers between devices, quad_permute(): return lax.ppermute(x, 'row', row_pairs(lambda z, q: (z, q ^ flip)))  21.1 us
    ppermute x14, starting transfers between devices, col_move(): return lax.ppermute(x, 'col', pairs)  20.6 us
    ppermute x14, waiting for transfers between devices, col_move(): return lax.ppermute(x, 'col', pairs)  15.8 us
    ppermute x7, waiting for transfers between devices, quad_permute(): return lax.ppermute(x, 'row', row_pairs(lambda z, q: (z, q ^ flip)))  3.3 us
  transfers between devices with their start and end apart: 39, of which 20 were waited for; matrix products, arithmetic and copies ran while one was open for 0% of the time, Pallas kernels for 4%

profile of v9, /device:TPU:1, one launch (start us, length us, event | category | flops | bytes accessed | tf_op | source)
XLA Modules:
  0.0 135.3 jit_solution(12131963897840456914)
XLA Ops:
  0.6 3.7 %collective-permute-start = (bf16[256,256]{1,0:T(8,128)(2,1)}, bf16[256,256]{1,0:T(8,128)(2,1)S(1)}, u32[]{:S(2)}, u32[]{:S(2)}) collective-permute-start(bf16[256,256]{1,0:T(8,128)(2,1)} %bitcast.51), channel_id=1, source_target_pairs={{0,16},{8,24},{16,0},{24,8},{32,48},{40,56},{48,32},{56,40},{64,80... | collective-permute-start | bytes 393224 | tf_op jit(solution)/shard_map/ppermute | solution.py:33
  11.8 4.7 %collective-permute-start.3 = (bf16[4,256,128]{2,1,0:T(8,128)(2,1)S(1)}, bf16[4,256,128]{2,1,0:T(8,128)(2,1)S(1)}, u32[]{:S(2)}, u32[]{:S(2)}) collective-permute-start(bf16[4,256,128]{2,1,0:T(8,128)(2,1)S(1)} %pad_maximum_fusion.5.refs_0_), channel_id=1, source_target_pairs={{0,224},{8,232},{16,240},{24,248},{32,0},{40,8},{48,16},{56,24},{6... | collective-permute-start | bytes 786440 | tf_op jit(solution)/shard_map/ppermute | solution.py:47
  16.5 5.6 %collective-permute-done.3.refs_1_ = bf16[4,256,128]{2,1,0:T(8,128)(2,1)S(1)} collective-permute-done((bf16[4,256,128]{2,1,0:T(8,128)(2,1)S(1)}, bf16[4,256,128]{2,1,0:T(8,128)(2,1)S(1)}, u32[]{:S(2)}, u32[]{:S(2)}) %collective-permute-start.3) | collective-permute-done | bytes 262176 | tf_op jit(solution)/shard_map/ppermute | solution.py:47
  22.1 3.4 %collective-permute-start.4 = (bf16[4,256,128]{2,1,0:T(8,128)(2,1)S(1)}, bf16[4,256,128]{2,1,0:T(8,128)(2,1)S(1)}, u32[]{:S(2)}, u32[]{:S(2)}) collective-permute-start(bf16[4,256,128]{2,1,0:T(8,128)(2,1)S(1)} %collective-permute-done.3.refs_1_), channel_id=1, source_target_pairs={{0,224},{8,232},{16,240},{24,248},{32,0},{40,8},{48,16},{56,24},{6... | collective-permute-start | bytes 786440 | tf_op jit(solution)/shard_map/ppermute | solution.py:47
  25.5 4.6 %collective-permute-done.4.refs_2_ = bf16[4,256,128]{2,1,0:T(8,128)(2,1)S(1)} collective-permute-done((bf16[4,256,128]{2,1,0:T(8,128)(2,1)S(1)}, bf16[4,256,128]{2,1,0:T(8,128)(2,1)S(1)}, u32[]{:S(2)}, u32[]{:S(2)}) %collective-permute-start.4) | collective-permute-done | bytes 262176 | tf_op jit(solution)/shard_map/ppermute | solution.py:47
  30.1 3.4 %collective-permute-start.5 = (bf16[4,256,128]{2,1,0:T(8,128)(2,1)S(1)}, bf16[4,256,128]{2,1,0:T(8,128)(2,1)S(1)}, u32[]{:S(2)}, u32[]{:S(2)}) collective-permute-start(bf16[4,256,128]{2,1,0:T(8,128)(2,1)S(1)} %collective-permute-done.4.refs_2_), channel_id=1, source_target_pairs={{0,224},{8,232},{16,240},{24,248},{32,0},{40,8},{48,16},{56,24},{6... | collective-permute-start | bytes 786440 | tf_op jit(solution)/shard_map/ppermute | solution.py:47
  33.6 3.7 %collective-permute-done.5.refs_3_ = bf16[4,256,128]{2,1,0:T(8,128)(2,1)S(1)} collective-permute-done((bf16[4,256,128]{2,1,0:T(8,128)(2,1)S(1)}, bf16[4,256,128]{2,1,0:T(8,128)(2,1)S(1)}, u32[]{:S(2)}, u32[]{:S(2)}) %collective-permute-start.5) | collective-permute-done | bytes 262176 | tf_op jit(solution)/shard_map/ppermute | solution.py:47
  37.3 3.5 %collective-permute-start.10 = (bf16[2,256,128]{2,1,0:T(8,128)(2,1)S(1)}, bf16[2,256,128]{2,1,0:T(8,128)(2,1)S(1)}, u32[]{:S(2)}, u32[]{:S(2)}) collective-permute-start(bf16[2,256,128]{2,1,0:T(8,128)(2,1)S(1)} %slice.127), channel_id=1, source_target_pairs={{0,224},{8,232},{16,240},{24,248},{32,0},{40,8},{48,16},{56,24},{6... | collective-permute-start | bytes 393224 | tf_op jit(solution)/shard_map/ppermute | solution.py:47
  40.9 2.3 %forward_near.1 = (f32[18,256,128]{2,1,0:T(8,128)S(1)}, s32[68]{0:T(128)S(1)}) custom-call(s32[25]{0:T(128)S(1)} %get-tuple-element.31.own_any, s32[25]{0:T(128)S(1)} %fusion.6.partner_any, bf16[12,256,256]{2,1,0:T(8,128)(2,1)S(1)} %bitcast.43, bf16[12,256,256]{2,1,0:T(8,128)(2,1)S(1)} %collective-permute-done.2.adj1, ...), custom_call_target="tpu_custom_call" | custom-call | flops 352321536 | bytes 6291456 | tf_op jit(solution)/shard_map/forward_near/pallas_call | solution.py:390
  43.3 2.7 %collective-permute-done.9.far_a = bf16[2,256,128]{2,1,0:T(8,128)(2,1)S(1)} collective-permute-done((bf16[2,256,128]{2,1,0:T(8,128)(2,1)S(1)}, bf16[2,256,128]{2,1,0:T(8,128)(2,1)S(1)}, u32[]{:S(2)}, u32[]{:S(2)}) %collective-permute-start.9) | collective-permute-done | bytes 131104 | tf_op jit(solution)/shard_map/ppermute | solution.py:47
  46.8 2.5 %collective-permute-start.11 = (bf16[2,256,128]{2,1,0:T(8,128)(2,1)S(1)}, bf16[2,256,128]{2,1,0:T(8,128)(2,1)S(1)}, u32[]{:S(2)}, u32[]{:S(2)}) collective-permute-start(bf16[2,256,128]{2,1,0:T(8,128)(2,1)S(1)} %get-tuple-element.39), channel_id=1, source_target_pairs={{0,6},{1,7},{2,4},{3,5},{4,2},{5,3},{6,0},{7,1},{8,14},{9,15},{10,... | collective-permute-start | bytes 393224 | tf_op jit(solution)/shard_map/ppermute | solution.py:38
  49.9 2.0 %collective-permute-start.13 = (bf16[2,256,128]{2,1,0:T(8,128)(2,1)S(1)}, bf16[2,256,128]{2,1,0:T(8,128)(2,1)S(1)}, u32[]{:S(2)}, u32[]{:S(2)}) collective-permute-start(bf16[2,256,128]{2,1,0:T(8,128)(2,1)S(1)} %get-tuple-element.41), channel_id=1, source_target_pairs={{0,5},{1,6},{2,7},{3,4},{4,1},{5,2},{6,3},{7,0},{8,13},{9,14},{10,... | collective-permute-start | bytes 393224 | tf_op jit(solution)/shard_map/ppermute | solution.py:38
  53.5 2.7 %collective-permute-start.16 = (bf16[2,256,128]{2,1,0:T(8,128)(2,1)S(1)}, bf16[2,256,128]{2,1,0:T(8,128)(2,1)S(1)}, u32[]{:S(2)}, u32[]{:S(2)}) collective-permute-start(bf16[2,256,128]{2,1,0:T(8,128)(2,1)S(1)} %get-tuple-element.44), channel_id=1, source_target_pairs={{0,3},{1,0},{2,1},{3,2},{4,7},{5,4},{6,5},{7,6},{8,11},{9,8},{10,9... | collective-permute-start | bytes 393224 | tf_op jit(solution)/shard_map/ppermute | solution.py:38
  57.8 4.7 %collective-permute-done.15 = bf16[2,256,128]{2,1,0:T(8,128)(2,1)S(1)} collective-permute-done((bf16[2,256,128]{2,1,0:T(8,128)(2,1)S(1)}, bf16[2,256,128]{2,1,0:T(8,128)(2,1)S(1)}, u32[]{:S(2)}, u32[]{:S(2)}) %collective-permute-start.15) | collective-permute-done | bytes 131104 | tf_op jit(solution)/shard_map/ppermute | solution.py:38
  62.6 5.2 %collective-permute-start.18 = (f32[512,128]{1,0:T(8,128)S(1)}, f32[512,128]{1,0:T(8,128)S(1)}, u32[]{:S(2)}, u32[]{:S(2)}) collective-permute-start(f32[512,128]{1,0:T(8,128)S(1)} %bitcast.49), channel_id=1, source_target_pairs={{0,8},{8,0},{16,24},{24,16},{32,40},{40,32},{48,56},{56,48},{64,72... | collective-permute-start | bytes 786440 | tf_op jit(solution)/shard_map/ppermute | solution.py:33
  72.4 1.9 %collective-permute-start.21 = (bf16[640,128]{1,0:T(8,128)(2,1)S(1)}, bf16[640,128]{1,0:T(8,128)(2,1)S(1)}, u32[]{:S(2)}, u32[]{:S(2)}) collective-permute-start(bf16[640,128]{1,0:T(8,128)(2,1)S(1)} %get-tuple-element.47.refs_0_), channel_id=1, source_target_pairs={{0,2},{1,3},{2,0},{3,1},{4,6},{5,7},{6,4},{7,5},{8,10},{9,11},{10,... | collective-permute-start | bytes 491528 | tf_op jit(solution)/shard_map/ppermute | solution.py:38
  75.5 2.3 %collective-permute-start.23 = (bf16[640,128]{1,0:T(8,128)(2,1)S(1)}, bf16[640,128]{1,0:T(8,128)(2,1)S(1)}, u32[]{:S(2)}, u32[]{:S(2)}) collective-permute-start(bf16[640,128]{1,0:T(8,128)(2,1)S(1)} %get-tuple-element.48), channel_id=1, source_target_pairs={{0,7},{1,4},{2,5},{3,6},{4,3},{5,0},{6,1},{7,2},{8,15},{9,12},{10,... | collective-permute-start | bytes 491528 | tf_op jit(solution)/shard_map/ppermute | solution.py:38
  78.5 2.0 %collective-permute-start.25 = (bf16[640,128]{1,0:T(8,128)(2,1)S(1)}, bf16[640,128]{1,0:T(8,128)(2,1)S(1)}, u32[]{:S(2)}, u32[]{:S(2)}) collective-permute-start(bf16[640,128]{1,0:T(8,128)(2,1)S(1)} %get-tuple-element.47.refs_0_), channel_id=1, source_target_pairs={{0,3},{1,0},{2,1},{3,2},{4,7},{5,4},{6,5},{7,6},{8,11},{9,8},{10,9... | collective-permute-start | bytes 491528 | tf_op jit(solution)/shard_map/ppermute | solution.py:38
  80.5 5.8 %collective-permute-done.21.refs_2_ = bf16[640,128]{1,0:T(8,128)(2,1)S(1)} collective-permute-done((bf16[640,128]{1,0:T(8,128)(2,1)S(1)}, bf16[640,128]{1,0:T(8,128)(2,1)S(1)}, u32[]{:S(2)}, u32[]{:S(2)}) %collective-permute-start.21) | collective-permute-done | bytes 163872 | tf_op jit(solution)/shard_map/ppermute | solution.py:38
  87.3 2.4 %collective-permute-done.24.refs_5_ = bf16[640,128]{1,0:T(8,128)(2,1)S(1)} collective-permute-done((bf16[640,128]{1,0:T(8,128)(2,1)S(1)}, bf16[640,128]{1,0:T(8,128)(2,1)S(1)}, u32[]{:S(2)}, u32[]{:S(2)}) %collective-permute-start.24) | collective-permute-done | bytes 163872 | tf_op jit(solution)/shard_map/ppermute | solution.py:38
  89.8 1.7 %collective-permute-done.26.refs_7_ = bf16[640,128]{1,0:T(8,128)(2,1)S(1)} collective-permute-done((bf16[640,128]{1,0:T(8,128)(2,1)S(1)}, bf16[640,128]{1,0:T(8,128)(2,1)S(1)}, u32[]{:S(2)}, u32[]{:S(2)}) %collective-permute-start.26) | collective-permute-done | bytes 163872 | tf_op jit(solution)/shard_map/ppermute | solution.py:38
  92.4 2.7 %collective-permute-start.31 = (bf16[640,128]{1,0:T(8,128)(2,1)S(1)}, bf16[640,128]{1,0:T(8,128)(2,1)S(1)}, u32[]{:S(2)}, u32[]{:S(2)}) collective-permute-start(bf16[640,128]{1,0:T(8,128)(2,1)S(1)} %get-tuple-element.51), channel_id=1, source_target_pairs={{0,224},{8,232},{16,240},{24,248},{32,0},{40,8},{48,16},{56,24},{6... | collective-permute-start | bytes 491528 | tf_op jit(solution)/shard_map/ppermute | solution.py:47
  95.0 1.8 %backward_near.1.parts = bf16[32,256,128]{2,1,0:T(8,128)(2,1)S(1)} custom-call(s32[68]{0:T(128)S(1)} %get-tuple-element.36.lists_any, bf16[12,256,256]{2,1,0:T(8,128)(2,1)S(1)} %bitcast.46, bf16[12,256,256]{2,1,0:T(8,128)(2,1)S(1)} %collective-permute-done.2.adj1, bf16[8,512,128]{2,1,0:T(8,128)(2,1)S(1)} %get-tuple-element.49.back), custom_call_target="tpu_custom_call" | custom-call | flops 352321536 | bytes 6291456 | tf_op jit(solution)/shard_map/backward_near/pallas_call | solution.py:439
  98.3 2.7 %collective-permute-start.32 = (bf16[1152,128]{1,0:T(8,128)(2,1)S(1)}, bf16[1152,128]{1,0:T(8,128)(2,1)S(1)}, u32[]{:S(2)}, u32[]{:S(2)}) collective-permute-start(bf16[1152,128]{1,0:T(8,128)(2,1)S(1)} %pad_maximum_fusion.3), channel_id=1, source_target_pairs={{0,224},{8,232},{16,240},{24,248},{32,0},{40,8},{48,16},{56,24},{6... | collective-permute-start | bytes 884744 | tf_op jit(solution)/shard_map/ppermute | solution.py:47
  101.0 4.2 %collective-permute-done.28.up2 = bf16[1152,128]{1,0:T(8,128)(2,1)S(1)} collective-permute-done((bf16[1152,128]{1,0:T(8,128)(2,1)S(1)}, bf16[1152,128]{1,0:T(8,128)(2,1)S(1)}, u32[]{:S(2)}, u32[]{:S(2)}) %collective-permute-start.28) | collective-permute-done | bytes 294944 | tf_op jit(solution)/shard_map/ppermute | solution.py:47
  105.6 2.7 %collective-permute-start.33 = (bf16[1152,128]{1,0:T(8,128)(2,1)S(1)}, bf16[1152,128]{1,0:T(8,128)(2,1)S(1)}, u32[]{:S(2)}, u32[]{:S(2)}) collective-permute-start(bf16[1152,128]{1,0:T(8,128)(2,1)S(1)} %pad_maximum_fusion.4), channel_id=1, source_target_pairs={{0,224},{8,232},{16,240},{24,248},{32,0},{40,8},{48,16},{56,24},{6... | collective-permute-start | bytes 884744 | tf_op jit(solution)/shard_map/ppermute | solution.py:47
  108.4 3.9 %collective-permute-done.29.up3 = bf16[1152,128]{1,0:T(8,128)(2,1)S(1)} collective-permute-done((bf16[1152,128]{1,0:T(8,128)(2,1)S(1)}, bf16[1152,128]{1,0:T(8,128)(2,1)S(1)}, u32[]{:S(2)}, u32[]{:S(2)}) %collective-permute-start.29) | collective-permute-done | bytes 294944 | tf_op jit(solution)/shard_map/ppermute | solution.py:47
  112.6 2.7 %collective-permute-start.34 = (bf16[1024,128]{1,0:T(8,128)(2,1)S(1)}, bf16[1024,128]{1,0:T(8,128)(2,1)S(1)}, u32[]{:S(2)}, u32[]{:S(2)}) collective-permute-start(bf16[1024,128]{1,0:T(8,128)(2,1)S(1)} %fusion), channel_id=1, source_target_pairs={{0,224},{8,232},{16,240},{24,248},{32,0},{40,8},{48,16},{56,24},{6... | collective-permute-start | bytes 786440 | tf_op jit(solution)/shard_map/ppermute | solution.py:47
  115.3 3.8 %collective-permute-done.34.down4 = bf16[1024,128]{1,0:T(8,128)(2,1)S(1)} collective-permute-done((bf16[1024,128]{1,0:T(8,128)(2,1)S(1)}, bf16[1024,128]{1,0:T(8,128)(2,1)S(1)}, u32[]{:S(2)}, u32[]{:S(2)}) %collective-permute-start.34) | collective-permute-done | bytes 262176 | tf_op jit(solution)/shard_map/ppermute | solution.py:47
  119.6 2.5 %collective-permute-start.35 = (bf16[640,128]{1,0:T(8,128)(2,1)S(1)}, bf16[640,128]{1,0:T(8,128)(2,1)S(1)}, u32[]{:S(2)}, u32[]{:S(2)}) collective-permute-start(bf16[640,128]{1,0:T(8,128)(2,1)S(1)} %get-tuple-element.53.sent), channel_id=1, source_target_pairs={{0,16},{8,24},{16,0},{24,8},{32,48},{40,56},{48,32},{56,40},{64,80... | collective-permute-start | bytes 491528 | tf_op jit(solution)/shard_map/ppermute | solution.py:33
  123.1 1.8 %collective-permute-done.36.w_lo = bf16[128,128]{1,0:T(8,128)(2,1)S(1)} collective-permute-done((bf16[128,128]{1,0:T(8,128)(2,1)S(1)}, bf16[128,128]{1,0:T(8,128)(2,1)S(1)}, u32[]{:S(2)}, u32[]{:S(2)}) %collective-permute-start.36) | collective-permute-done | bytes 32800 | tf_op jit(solution)/shard_map/ppermute | solution.py:542
  126.2 7.3 %collective-permute-start.38 = (bf16[768,128]{1,0:T(8,128)(2,1)S(1)}, bf16[768,128]{1,0:T(8,128)(2,1)S(1)}, u32[]{:S(2)}, u32[]{:S(2)}) collective-permute-start(bf16[768,128]{1,0:T(8,128)(2,1)S(1)} %get-tuple-element.55), channel_id=1, source_target_pairs={{0,8},{8,0},{16,24},{24,16},{32,40},{40,32},{48,56},{56,48},{64,72... | collective-permute-start | bytes 589832 | tf_op jit(solution)/shard_map/ppermute | solution.py:33
  (93 shorter events, 26.9 us)
Async XLA Ops:
  0.6 8.7 %collective-permute-start = (bf16[256,256]{1,0:T(8,128)(2,1)}, bf16[256,256]{1,0:T(8,128)(2,1)S(1)}, u32[]{:S(2)}, u32[]{:S(2)}) collective-permute-start(bf16[256,256]{1,0:T(8,128)(2,1)} %bitcast.51), channel_id=1, source_target_pairs={{0,16},{8,24},{16,0},{24,8},{32,48},{40,56},{48,32},{56,40},{64,80... | collective-permute-start | bytes 393224 | tf_op jit(solution)/shard_map/ppermute | solution.py:33
  4.3 36.6 %collective-permute-start.2 = (bf16[12,256,256]{2,1,0:T(8,128)(2,1)}, bf16[12,256,256]{2,1,0:T(8,128)(2,1)S(1)}, u32[]{:S(2)}, u32[]{:S(2)}) collective-permute-start(bf16[12,256,256]{2,1,0:T(8,128)(2,1)} %bitcast.42), channel_id=1, source_target_pairs={{0,8},{8,0},{16,24},{24,16},{32,40},{40,32},{48,56},{56,48},{64,72... | collective-permute-start | bytes 4718600 | tf_op jit(solution)/shard_map/ppermute | solution.py:33
  11.8 10.3 %collective-permute-start.3 = (bf16[4,256,128]{2,1,0:T(8,128)(2,1)S(1)}, bf16[4,256,128]{2,1,0:T(8,128)(2,1)S(1)}, u32[]{:S(2)}, u32[]{:S(2)}) collective-permute-start(bf16[4,256,128]{2,1,0:T(8,128)(2,1)S(1)} %pad_maximum_fusion.5.refs_0_), channel_id=1, source_target_pairs={{0,224},{8,232},{16,240},{24,248},{32,0},{40,8},{48,16},{56,24},{6... | collective-permute-start | bytes 786440 | tf_op jit(solution)/shard_map/ppermute | solution.py:47
  16.5 9.0 %collective-permute-start.6 = (bf16[4,256,128]{2,1,0:T(8,128)(2,1)S(1)}, bf16[4,256,128]{2,1,0:T(8,128)(2,1)S(1)}, u32[]{:S(2)}, u32[]{:S(2)}) collective-permute-start(bf16[4,256,128]{2,1,0:T(8,128)(2,1)S(1)} %pad_maximum_fusion.5.refs_0_), channel_id=1, source_target_pairs={{0,32},{8,40},{16,48},{24,56},{32,64},{40,72},{48,80},{56,88},{64,... | collective-permute-start | bytes 786440 | tf_op jit(solution)/shard_map/ppermute | solution.py:47
  22.1 8.1 %collective-permute-start.4 = (bf16[4,256,128]{2,1,0:T(8,128)(2,1)S(1)}, bf16[4,256,128]{2,1,0:T(8,128)(2,1)S(1)}, u32[]{:S(2)}, u32[]{:S(2)}) collective-permute-start(bf16[4,256,128]{2,1,0:T(8,128)(2,1)S(1)} %collective-permute-done.3.refs_1_), channel_id=1, source_target_pairs={{0,224},{8,232},{16,240},{24,248},{32,0},{40,8},{48,16},{56,24},{6... | collective-permute-start | bytes 786440 | tf_op jit(solution)/shard_map/ppermute | solution.py:47
  25.5 8.1 %collective-permute-start.7 = (bf16[4,256,128]{2,1,0:T(8,128)(2,1)S(1)}, bf16[4,256,128]{2,1,0:T(8,128)(2,1)S(1)}, u32[]{:S(2)}, u32[]{:S(2)}) collective-permute-start(bf16[4,256,128]{2,1,0:T(8,128)(2,1)S(1)} %collective-permute-done.6.refs_6_), channel_id=1, source_target_pairs={{0,32},{8,40},{16,48},{24,56},{32,64},{40,72},{48,80},{56,88},{64,... | collective-permute-start | bytes 786440 | tf_op jit(solution)/shard_map/ppermute | solution.py:47
  30.1 7.1 %collective-permute-start.5 = (bf16[4,256,128]{2,1,0:T(8,128)(2,1)S(1)}, bf16[4,256,128]{2,1,0:T(8,128)(2,1)S(1)}, u32[]{:S(2)}, u32[]{:S(2)}) collective-permute-start(bf16[4,256,128]{2,1,0:T(8,128)(2,1)S(1)} %collective-permute-done.4.refs_2_), channel_id=1, source_target_pairs={{0,224},{8,232},{16,240},{24,248},{32,0},{40,8},{48,16},{56,24},{6... | collective-permute-start | bytes 786440 | tf_op jit(solution)/shard_map/ppermute | solution.py:47
  33.6 7.2 %collective-permute-start.8 = (bf16[4,256,128]{2,1,0:T(8,128)(2,1)S(1)}, bf16[4,256,128]{2,1,0:T(8,128)(2,1)S(1)}, u32[]{:S(2)}, u32[]{:S(2)}) collective-permute-start(bf16[4,256,128]{2,1,0:T(8,128)(2,1)S(1)} %collective-permute-done.7.refs_5_), channel_id=1, source_target_pairs={{0,32},{8,40},{16,48},{24,56},{32,64},{40,72},{48,80},{56,88},{64,... | collective-permute-start | bytes 786440 | tf_op jit(solution)/shard_map/ppermute | solution.py:47
  37.3 6.0 %collective-permute-start.10 = (bf16[2,256,128]{2,1,0:T(8,128)(2,1)S(1)}, bf16[2,256,128]{2,1,0:T(8,128)(2,1)S(1)}, u32[]{:S(2)}, u32[]{:S(2)}) collective-permute-start(bf16[2,256,128]{2,1,0:T(8,128)(2,1)S(1)} %slice.127), channel_id=1, source_target_pairs={{0,224},{8,232},{16,240},{24,248},{32,0},{40,8},{48,16},{56,24},{6... | collective-permute-start | bytes 393224 | tf_op jit(solution)/shard_map/ppermute | solution.py:47
  46.8 6.7 %collective-permute-start.11 = (bf16[2,256,128]{2,1,0:T(8,128)(2,1)S(1)}, bf16[2,256,128]{2,1,0:T(8,128)(2,1)S(1)}, u32[]{:S(2)}, u32[]{:S(2)}) collective-permute-start(bf16[2,256,128]{2,1,0:T(8,128)(2,1)S(1)} %get-tuple-element.39), channel_id=1, source_target_pairs={{0,6},{1,7},{2,4},{3,5},{4,2},{5,3},{6,0},{7,1},{8,14},{9,15},{10,... | collective-permute-start | bytes 393224 | tf_op jit(solution)/shard_map/ppermute | solution.py:38
  49.3 6.8 %collective-permute-start.12 = (bf16[2,256,128]{2,1,0:T(8,128)(2,1)S(1)}, bf16[2,256,128]{2,1,0:T(8,128)(2,1)S(1)}, u32[]{:S(2)}, u32[]{:S(2)}) collective-permute-start(bf16[2,256,128]{2,1,0:T(8,128)(2,1)S(1)} %get-tuple-element.40), channel_id=1, source_target_pairs={{0,2},{1,3},{2,0},{3,1},{4,6},{5,7},{6,4},{7,5},{8,10},{9,11},{10,... | collective-permute-start | bytes 393224 | tf_op jit(solution)/shard_map/ppermute | solution.py:38
  49.9 7.4 %collective-permute-start.13 = (bf16[2,256,128]{2,1,0:T(8,128)(2,1)S(1)}, bf16[2,256,128]{2,1,0:T(8,128)(2,1)S(1)}, u32[]{:S(2)}, u32[]{:S(2)}) collective-permute-start(bf16[2,256,128]{2,1,0:T(8,128)(2,1)S(1)} %get-tuple-element.41), channel_id=1, source_target_pairs={{0,5},{1,6},{2,7},{3,4},{4,1},{5,2},{6,3},{7,0},{8,13},{9,14},{10,... | collective-permute-start | bytes 393224 | tf_op jit(solution)/shard_map/ppermute | solution.py:38
  51.9 5.9 %collective-permute-start.14 = (bf16[2,256,128]{2,1,0:T(8,128)(2,1)S(1)}, bf16[2,256,128]{2,1,0:T(8,128)(2,1)S(1)}, u32[]{:S(2)}, u32[]{:S(2)}) collective-permute-start(bf16[2,256,128]{2,1,0:T(8,128)(2,1)S(1)} %get-tuple-element.42), channel_id=1, source_target_pairs={{0,7},{1,4},{2,5},{3,6},{4,3},{5,0},{6,1},{7,2},{8,15},{9,12},{10,... | collective-permute-start | bytes 393224 | tf_op jit(solution)/shard_map/ppermute | solution.py:38
  53.4 9.0 %collective-permute-start.15 = (bf16[2,256,128]{2,1,0:T(8,128)(2,1)S(1)}, bf16[2,256,128]{2,1,0:T(8,128)(2,1)S(1)}, u32[]{:S(2)}, u32[]{:S(2)}) collective-permute-start(bf16[2,256,128]{2,1,0:T(8,128)(2,1)S(1)} %get-tuple-element.43), channel_id=1, source_target_pairs={{0,1},{1,2},{2,3},{3,0},{4,5},{5,6},{6,7},{7,4},{8,9},{9,10},{10,1... | collective-permute-start | bytes 393224 | tf_op jit(solution)/shard_map/ppermute | solution.py:38
  53.5 9.0 %collective-permute-start.16 = (bf16[2,256,128]{2,1,0:T(8,128)(2,1)S(1)}, bf16[2,256,128]{2,1,0:T(8,128)(2,1)S(1)}, u32[]{:S(2)}, u32[]{:S(2)}) collective-permute-start(bf16[2,256,128]{2,1,0:T(8,128)(2,1)S(1)} %get-tuple-element.44), channel_id=1, source_target_pairs={{0,3},{1,0},{2,1},{3,2},{4,7},{5,4},{6,5},{7,6},{8,11},{9,8},{10,9... | collective-permute-start | bytes 393224 | tf_op jit(solution)/shard_map/ppermute | solution.py:38
  56.1 6.3 %collective-permute-start.17 = (bf16[2,256,128]{2,1,0:T(8,128)(2,1)S(1)}, bf16[2,256,128]{2,1,0:T(8,128)(2,1)S(1)}, u32[]{:S(2)}, u32[]{:S(2)}) collective-permute-start(bf16[2,256,128]{2,1,0:T(8,128)(2,1)S(1)} %get-tuple-element.45), channel_id=1, source_target_pairs={{0,4},{1,5},{2,6},{3,7},{4,0},{5,1},{6,2},{7,3},{8,12},{9,13},{10,... | collective-permute-start | bytes 393224 | tf_op jit(solution)/shard_map/ppermute | solution.py:38
  62.6 6.5 %collective-permute-start.18 = (f32[512,128]{1,0:T(8,128)S(1)}, f32[512,128]{1,0:T(8,128)S(1)}, u32[]{:S(2)}, u32[]{:S(2)}) collective-permute-start(f32[512,128]{1,0:T(8,128)S(1)} %bitcast.49), channel_id=1, source_target_pairs={{0,8},{8,0},{16,24},{24,16},{32,40},{40,32},{48,56},{56,48},{64,72... | collective-permute-start | bytes 786440 | tf_op jit(solution)/shard_map/ppermute | solution.py:33
  70.7 7.9 %collective-permute-start.20 = (bf16[640,128]{1,0:T(8,128)(2,1)S(1)}, bf16[640,128]{1,0:T(8,128)(2,1)S(1)}, u32[]{:S(2)}, u32[]{:S(2)}) collective-permute-start(bf16[640,128]{1,0:T(8,128)(2,1)S(1)} %get-tuple-element.48), channel_id=1, source_target_pairs={{0,6},{1,7},{2,4},{3,5},{4,2},{5,3},{6,0},{7,1},{8,14},{9,15},{10,... | collective-permute-start | bytes 491528 | tf_op jit(solution)/shard_map/ppermute | solution.py:38
  72.4 13.9 %collective-permute-start.21 = (bf16[640,128]{1,0:T(8,128)(2,1)S(1)}, bf16[640,128]{1,0:T(8,128)(2,1)S(1)}, u32[]{:S(2)}, u32[]{:S(2)}) collective-permute-start(bf16[640,128]{1,0:T(8,128)(2,1)S(1)} %get-tuple-element.47.refs_0_), channel_id=1, source_target_pairs={{0,2},{1,3},{2,0},{3,1},{4,6},{5,7},{6,4},{7,5},{8,10},{9,11},{10,... | collective-permute-start | bytes 491528 | tf_op jit(solution)/shard_map/ppermute | solution.py:38
  74.3 13.1 %collective-permute-start.22 = (bf16[640,128]{1,0:T(8,128)(2,1)S(1)}, bf16[640,128]{1,0:T(8,128)(2,1)S(1)}, u32[]{:S(2)}, u32[]{:S(2)}) collective-permute-start(bf16[640,128]{1,0:T(8,128)(2,1)S(1)} %get-tuple-element.48), channel_id=1, source_target_pairs={{0,5},{1,6},{2,7},{3,4},{4,1},{5,2},{6,3},{7,0},{8,13},{9,14},{10,... | collective-permute-start | bytes 491528 | tf_op jit(solution)/shard_map/ppermute | solution.py:38
  75.5 11.8 %collective-permute-start.23 = (bf16[640,128]{1,0:T(8,128)(2,1)S(1)}, bf16[640,128]{1,0:T(8,128)(2,1)S(1)}, u32[]{:S(2)}, u32[]{:S(2)}) collective-permute-start(bf16[640,128]{1,0:T(8,128)(2,1)S(1)} %get-tuple-element.48), channel_id=1, source_target_pairs={{0,7},{1,4},{2,5},{3,6},{4,3},{5,0},{6,1},{7,2},{8,15},{9,12},{10,... | collective-permute-start | bytes 491528 | tf_op jit(solution)/shard_map/ppermute | solution.py:38
  77.8 11.9 %collective-permute-start.24 = (bf16[640,128]{1,0:T(8,128)(2,1)S(1)}, bf16[640,128]{1,0:T(8,128)(2,1)S(1)}, u32[]{:S(2)}, u32[]{:S(2)}) collective-permute-start(bf16[640,128]{1,0:T(8,128)(2,1)S(1)} %get-tuple-element.47.refs_0_), channel_id=1, source_target_pairs={{0,1},{1,2},{2,3},{3,0},{4,5},{5,6},{6,7},{7,4},{8,9},{9,10},{10,1... | collective-permute-start | bytes 491528 | tf_op jit(solution)/shard_map/ppermute | solution.py:38
  78.5 11.2 %collective-permute-start.25 = (bf16[640,128]{1,0:T(8,128)(2,1)S(1)}, bf16[640,128]{1,0:T(8,128)(2,1)S(1)}, u32[]{:S(2)}, u32[]{:S(2)}) collective-permute-start(bf16[640,128]{1,0:T(8,128)(2,1)S(1)} %get-tuple-element.47.refs_0_), channel_id=1, source_target_pairs={{0,3},{1,0},{2,1},{3,2},{4,7},{5,4},{6,5},{7,6},{8,11},{9,8},{10,9... | collective-permute-start | bytes 491528 | tf_op jit(solution)/shard_map/ppermute | solution.py:38
  92.3 5.5 %collective-permute-start.27 = (bf16[640,128]{1,0:T(8,128)(2,1)S(1)}, bf16[640,128]{1,0:T(8,128)(2,1)S(1)}, u32[]{:S(2)}, u32[]{:S(2)}) collective-permute-start(bf16[640,128]{1,0:T(8,128)(2,1)S(1)} %get-tuple-element.50.own), channel_id=1, source_target_pairs={{0,32},{8,40},{16,48},{24,56},{32,64},{40,72},{48,80},{56,88},{64,... | collective-permute-start | bytes 491528 | tf_op jit(solution)/shard_map/ppermute | solution.py:47
  97.9 7.4 %collective-permute-start.28 = (bf16[1152,128]{1,0:T(8,128)(2,1)S(1)}, bf16[1152,128]{1,0:T(8,128)(2,1)S(1)}, u32[]{:S(2)}, u32[]{:S(2)}) collective-permute-start(bf16[1152,128]{1,0:T(8,128)(2,1)S(1)} %pad_maximum_fusion), channel_id=1, source_target_pairs={{0,32},{8,40},{16,48},{24,56},{32,64},{40,72},{48,80},{56,88},{64,... | collective-permute-start | bytes 884744 | tf_op jit(solution)/shard_map/ppermute | solution.py:47
  98.3 7.2 %collective-permute-start.32 = (bf16[1152,128]{1,0:T(8,128)(2,1)S(1)}, bf16[1152,128]{1,0:T(8,128)(2,1)S(1)}, u32[]{:S(2)}, u32[]{:S(2)}) collective-permute-start(bf16[1152,128]{1,0:T(8,128)(2,1)S(1)} %pad_maximum_fusion.3), channel_id=1, source_target_pairs={{0,224},{8,232},{16,240},{24,248},{32,0},{40,8},{48,16},{56,24},{6... | collective-permute-start | bytes 884744 | tf_op jit(solution)/shard_map/ppermute | solution.py:47
  105.4 6.9 %collective-permute-start.29 = (bf16[1152,128]{1,0:T(8,128)(2,1)S(1)}, bf16[1152,128]{1,0:T(8,128)(2,1)S(1)}, u32[]{:S(2)}, u32[]{:S(2)}) collective-permute-start(bf16[1152,128]{1,0:T(8,128)(2,1)S(1)} %pad_maximum_fusion.1), channel_id=1, source_target_pairs={{0,32},{8,40},{16,48},{24,56},{32,64},{40,72},{48,80},{56,88},{64,... | collective-permute-start | bytes 884744 | tf_op jit(solution)/shard_map/ppermute | solution.py:47
  105.6 6.8 %collective-permute-start.33 = (bf16[1152,128]{1,0:T(8,128)(2,1)S(1)}, bf16[1152,128]{1,0:T(8,128)(2,1)S(1)}, u32[]{:S(2)}, u32[]{:S(2)}) collective-permute-start(bf16[1152,128]{1,0:T(8,128)(2,1)S(1)} %pad_maximum_fusion.4), channel_id=1, source_target_pairs={{0,224},{8,232},{16,240},{24,248},{32,0},{40,8},{48,16},{56,24},{6... | collective-permute-start | bytes 884744 | tf_op jit(solution)/shard_map/ppermute | solution.py:47
  112.4 7.0 %collective-permute-start.30 = (bf16[1152,128]{1,0:T(8,128)(2,1)S(1)}, bf16[1152,128]{1,0:T(8,128)(2,1)S(1)}, u32[]{:S(2)}, u32[]{:S(2)}) collective-permute-start(bf16[1152,128]{1,0:T(8,128)(2,1)S(1)} %pad_maximum_fusion.2), channel_id=1, source_target_pairs={{0,32},{8,40},{16,48},{24,56},{32,64},{40,72},{48,80},{56,88},{64,... | collective-permute-start | bytes 884744 | tf_op jit(solution)/shard_map/ppermute | solution.py:47
  112.6 6.5 %collective-permute-start.34 = (bf16[1024,128]{1,0:T(8,128)(2,1)S(1)}, bf16[1024,128]{1,0:T(8,128)(2,1)S(1)}, u32[]{:S(2)}, u32[]{:S(2)}) collective-permute-start(bf16[1024,128]{1,0:T(8,128)(2,1)S(1)} %fusion), channel_id=1, source_target_pairs={{0,224},{8,232},{16,240},{24,248},{32,0},{40,8},{48,16},{56,24},{6... | collective-permute-start | bytes 786440 | tf_op jit(solution)/shard_map/ppermute | solution.py:47
  119.6 6.5 %collective-permute-start.35 = (bf16[640,128]{1,0:T(8,128)(2,1)S(1)}, bf16[640,128]{1,0:T(8,128)(2,1)S(1)}, u32[]{:S(2)}, u32[]{:S(2)}) collective-permute-start(bf16[640,128]{1,0:T(8,128)(2,1)S(1)} %get-tuple-element.53.sent), channel_id=1, source_target_pairs={{0,16},{8,24},{16,0},{24,8},{32,48},{40,56},{48,32},{56,40},{64,80... | collective-permute-start | bytes 491528 | tf_op jit(solution)/shard_map/ppermute | solution.py:33
  126.2 8.3 %collective-permute-start.38 = (bf16[768,128]{1,0:T(8,128)(2,1)S(1)}, bf16[768,128]{1,0:T(8,128)(2,1)S(1)}, u32[]{:S(2)}, u32[]{:S(2)}) collective-permute-start(bf16[768,128]{1,0:T(8,128)(2,1)S(1)} %get-tuple-element.55), channel_id=1, source_target_pairs={{0,8},{8,0},{16,24},{24,16},{32,40},{40,32},{48,56},{56,48},{64,72... | collective-permute-start | bytes 589832 | tf_op jit(solution)/shard_map/ppermute | solution.py:33
  (13 other events, 113.7 us)

commit v10 on v9

--- a/solution.py
+++ b/solution.py
@@ -18,7 +18,7 @@
 UNROLL = 4
 PART = 16
 LIST = 4 * PART + 4
-MOVES = (0, 6, 2, 5, 7, 1, 3, 4)
+MOVES = (0, 4, 1, 6, 2, 3, 5, 7)
 
 
 def row_pairs(move):
@@ -120,7 +120,8 @@
                 add_to(value, *at)
 
 
-def forward_near_kernel(own_any, partner_any, adj0, adj1, *refs):
+def forward_near_kernel(own_any, partner_any, cotangent_any, adj0, adj1, *refs):
+    del cotangent_any
     pieces, (acc, lists, panel, own, partner, sems) = refs[:7], refs[7:]
     copies = [
         pltpu.make_async_copy(own_any, own, sems.at[0]),
@@ -386,13 +387,13 @@
     )(own_keep, own_message, x_block)
 
 
-def forward_near(own, partner, adj0, adj1, pieces):
+def forward_near(own, partner, cotangent, adj0, adj1, pieces):
     return local(
         forward_near_kernel,
         (shape(18, TILE, HALF, dtype=jnp.float32), shape(LIST, dtype=jnp.int32)),
-        11,
+        12,
         "forward_near",
-        any_in=2,
+        any_in=3,
         scalar_out=1,
         scratch=[
             pltpu.VMEM((NZ * QUAD, TILE, HALF), jnp.bfloat16),
@@ -401,7 +402,7 @@
             pltpu.SemaphoreType.DMA((2,)),
         ],
         cost=cost(21, 6),
-    )(own, partner, adj0, adj1, *pieces)
+    )(own, partner, cotangent, adj0, adj1, *pieces)
 
 
 def forward_far(lists, adj0, adj1, near, far_a, far_b):
@@ -511,7 +512,7 @@
     up3, down3 = z_shift(up2, 1), z_shift(down2, -1)
     far_a, far_b = z_shift(up3[:2], 1), z_shift(down3[2:], -1)
     near, lists = forward_near(
-        own_lists, partner_lists, adj0, adj1, [chunk, down1, down2, down3, up3, up2, up1]
+        own_lists, partner_lists, cot1, adj0, adj1, [chunk, down1, down2, down3, up3, up2, up1]
     )
     shares = forward_far(lists, adj0, adj1, near, far_a, far_b)
     agg = sum(

time: 136 us -> 142 us (1.044)
  the two profiles are of different devices: /device:TPU:1 before, /device:TPU:17 now
where the time goes in v10:
time: 142 us; the launch traced here: 141 us
  starting transfers between devices  72.6 us (51%)
  waiting for transfers between devices  54.2 us (38%)
  Pallas kernels  9.62 us (7%)
  local copies, waits for them, and re-layouts  2.4 us (2%)
  between operations  1.65 us (1%)
    ppermute x16, waiting for transfers between devices, z_shift(): return lax.ppermute(x, 'row', row_pairs(lambda z, q: (z + step, q)))  28.8 us
    ppermute x16, starting transfers between devices, z_shift(): return lax.ppermute(x, 'row', row_pairs(lambda z, q: (z + step, q)))  26.8 us
    ppermute x7, starting transfers between devices, quad_permute(): return lax.ppermute(x, 'row', row_pairs(lambda z, q: (z, q ^ flip)))  23 us
    ppermute x14, waiting for transfers between devices, col_move(): return lax.ppermute(x, 'col', pairs)  17.5 us
    ppermute x14, starting transfers between devices, col_move(): return lax.ppermute(x, 'col', pairs)  16.1 us
    ppermute x1, starting transfers between devices, per_device(): w_lo = lax.ppermute(w_send, 'col', [(c, c ^ 4) for c in range(NCOL)])  5.75 us
    ppermute x7, waiting for transfers between devices, quad_permute(): return lax.ppermute(x, 'row', row_pairs(lambda z, q: (z, q ^ flip)))  3.56 us
  transfers between devices with their start and end apart: 39, of which 20 were waited for; matrix products, arithmetic and copies ran while one was open for 0% of the time, Pallas kernels for 4%

profile of v10, /device:TPU:17, one launch (start us, length us, event | category | flops | bytes accessed | tf_op | source)
XLA Modules:
  0.0 141.2 jit_solution(2965244597237936567)
XLA Ops:
  0.6 2.8 %collective-permute-start = (bf16[256,256]{1,0:T(8,128)(2,1)}, bf16[256,256]{1,0:T(8,128)(2,1)S(1)}, u32[]{:S(2)}, u32[]{:S(2)}) collective-permute-start(bf16[256,256]{1,0:T(8,128)(2,1)} %bitcast.51), channel_id=1, source_target_pairs={{0,16},{8,24},{16,0},{24,8},{32,48},{40,56},{48,32},{56,40},{64,80... | collective-permute-start | bytes 393224 | tf_op jit(solution)/shard_map/ppermute | solution.py:33
  10.1 1.7 %collective-permute-start.7 = (bf16[4,256,128]{2,1,0:T(8,128)(2,1)S(1)}, bf16[4,256,128]{2,1,0:T(8,128)(2,1)S(1)}, u32[]{:S(2)}, u32[]{:S(2)}) collective-permute-start(bf16[4,256,128]{2,1,0:T(8,128)(2,1)S(1)} %pad_maximum_fusion.5.refs_0_), channel_id=1, source_target_pairs={{0,32},{8,40},{16,48},{24,56},{32,64},{40,72},{48,80},{56,88},{64,... | collective-permute-start | bytes 786440 | tf_op jit(solution)/shard_map/ppermute | solution.py:47
  11.8 4.0 %collective-permute-start.4 = (bf16[4,256,128]{2,1,0:T(8,128)(2,1)S(1)}, bf16[4,256,128]{2,1,0:T(8,128)(2,1)S(1)}, u32[]{:S(2)}, u32[]{:S(2)}) collective-permute-start(bf16[4,256,128]{2,1,0:T(8,128)(2,1)S(1)} %pad_maximum_fusion.5.refs_0_), channel_id=1, source_target_pairs={{0,224},{8,232},{16,240},{24,248},{32,0},{40,8},{48,16},{56,24},{6... | collective-permute-start | bytes 786440 | tf_op jit(solution)/shard_map/ppermute | solution.py:47
  15.8 6.4 %collective-permute-done.7.refs_6_ = bf16[4,256,128]{2,1,0:T(8,128)(2,1)S(1)} collective-permute-done((bf16[4,256,128]{2,1,0:T(8,128)(2,1)S(1)}, bf16[4,256,128]{2,1,0:T(8,128)(2,1)S(1)}, u32[]{:S(2)}, u32[]{:S(2)}) %collective-permute-start.7) | collective-permute-done | bytes 262176 | tf_op jit(solution)/shard_map/ppermute | solution.py:47
  22.3 2.7 %collective-permute-start.5 = (bf16[4,256,128]{2,1,0:T(8,128)(2,1)S(1)}, bf16[4,256,128]{2,1,0:T(8,128)(2,1)S(1)}, u32[]{:S(2)}, u32[]{:S(2)}) collective-permute-start(bf16[4,256,128]{2,1,0:T(8,128)(2,1)S(1)} %collective-permute-done.4.refs_1_), channel_id=1, source_target_pairs={{0,224},{8,232},{16,240},{24,248},{32,0},{40,8},{48,16},{56,24},{6... | collective-permute-start | bytes 786440 | tf_op jit(solution)/shard_map/ppermute | solution.py:47
  24.9 5.6 %collective-permute-done.8.refs_5_ = bf16[4,256,128]{2,1,0:T(8,128)(2,1)S(1)} collective-permute-done((bf16[4,256,128]{2,1,0:T(8,128)(2,1)S(1)}, bf16[4,256,128]{2,1,0:T(8,128)(2,1)S(1)}, u32[]{:S(2)}, u32[]{:S(2)}) %collective-permute-start.8) | collective-permute-done | bytes 262176 | tf_op jit(solution)/shard_map/ppermute | solution.py:47
  30.6 2.7 %collective-permute-start.6 = (bf16[4,256,128]{2,1,0:T(8,128)(2,1)S(1)}, bf16[4,256,128]{2,1,0:T(8,128)(2,1)S(1)}, u32[]{:S(2)}, u32[]{:S(2)}) collective-permute-start(bf16[4,256,128]{2,1,0:T(8,128)(2,1)S(1)} %collective-permute-done.5.refs_2_), channel_id=1, source_target_pairs={{0,224},{8,232},{16,240},{24,248},{32,0},{40,8},{48,16},{56,24},{6... | collective-permute-start | bytes 786440 | tf_op jit(solution)/shard_map/ppermute | solution.py:47
  33.3 2.2 %collective-permute-start.2 = (bf16[256,256]{1,0:T(8,128)(2,1)}, bf16[256,256]{1,0:T(8,128)(2,1)S(1)}, u32[]{:S(2)}, u32[]{:S(2)}) collective-permute-start(bf16[256,256]{1,0:T(8,128)(2,1)} %cot_own.1), channel_id=1, source_target_pairs={{0,8},{8,0},{16,24},{24,16},{32,40},{40,32},{48,56},{56,48},{64,72... | collective-permute-start | bytes 393224 | tf_op jit(solution)/shard_map/ppermute | solution.py:33
  35.4 2.6 %collective-permute-done.9.refs_4_ = bf16[4,256,128]{2,1,0:T(8,128)(2,1)S(1)} collective-permute-done((bf16[4,256,128]{2,1,0:T(8,128)(2,1)S(1)}, bf16[4,256,128]{2,1,0:T(8,128)(2,1)S(1)}, u32[]{:S(2)}, u32[]{:S(2)}) %collective-permute-start.9) | collective-permute-done | bytes 262176 | tf_op jit(solution)/shard_map/ppermute | solution.py:47
  38.1 2.7 %collective-permute-start.11 = (bf16[2,256,128]{2,1,0:T(8,128)(2,1)S(1)}, bf16[2,256,128]{2,1,0:T(8,128)(2,1)S(1)}, u32[]{:S(2)}, u32[]{:S(2)}) collective-permute-start(bf16[2,256,128]{2,1,0:T(8,128)(2,1)S(1)} %slice.127), channel_id=1, source_target_pairs={{0,224},{8,232},{16,240},{24,248},{32,0},{40,8},{48,16},{56,24},{6... | collective-permute-start | bytes 393224 | tf_op jit(solution)/shard_map/ppermute | solution.py:47
  40.9 2.3 %forward_near.1 = (f32[18,256,128]{2,1,0:T(8,128)S(1)}, s32[68]{0:T(128)S(1)}) custom-call(s32[25]{0:T(128)S(1)} %get-tuple-element.31.own_any, s32[25]{0:T(128)S(1)} %fusion.6.partner_any, bf16[256,256]{1,0:T(8,128)(2,1)S(1)} %collective-permute-done.2.cotangent_any.cot_other, bf16[12,256,256]{2,1,0:T(8,128)(2,1)S(1)} %bitcast.43, ...), custom_call_target="tpu_custom_call" | custom-call | flops 352321536 | bytes 6291456 | tf_op jit(solution)/shard_map/forward_near/pallas_call | solution.py:391
  45.2 1.8 %collective-permute-start.14 = (bf16[2,256,128]{2,1,0:T(8,128)(2,1)S(1)}, bf16[2,256,128]{2,1,0:T(8,128)(2,1)S(1)}, u32[]{:S(2)}, u32[]{:S(2)}) collective-permute-start(bf16[2,256,128]{2,1,0:T(8,128)(2,1)S(1)} %get-tuple-element.41), channel_id=1, source_target_pairs={{0,6},{1,7},{2,4},{3,5},{4,2},{5,3},{6,0},{7,1},{8,14},{9,15},{10,... | collective-permute-start | bytes 393224 | tf_op jit(solution)/shard_map/ppermute | solution.py:38
  47.1 2.2 %collective-permute-start.15 = (bf16[2,256,128]{2,1,0:T(8,128)(2,1)S(1)}, bf16[2,256,128]{2,1,0:T(8,128)(2,1)S(1)}, u32[]{:S(2)}, u32[]{:S(2)}) collective-permute-start(bf16[2,256,128]{2,1,0:T(8,128)(2,1)S(1)} %get-tuple-element.42), channel_id=1, source_target_pairs={{0,2},{1,3},{2,0},{3,1},{4,6},{5,7},{6,4},{7,5},{8,10},{9,11},{10,... | collective-permute-start | bytes 393224 | tf_op jit(solution)/shard_map/ppermute | solution.py:38
  50.6 1.6 %collective-permute-start.18 = (bf16[2,256,128]{2,1,0:T(8,128)(2,1)S(1)}, bf16[2,256,128]{2,1,0:T(8,128)(2,1)S(1)}, u32[]{:S(2)}, u32[]{:S(2)}) collective-permute-start(bf16[2,256,128]{2,1,0:T(8,128)(2,1)S(1)} %get-tuple-element.45), channel_id=1, source_target_pairs={{0,7},{1,4},{2,5},{3,6},{4,3},{5,0},{6,1},{7,2},{8,15},{9,12},{10,... | collective-permute-start | bytes 393224 | tf_op jit(solution)/shard_map/ppermute | solution.py:38
  52.6 4.9 %collective-permute-done.15 = bf16[2,256,128]{2,1,0:T(8,128)(2,1)S(1)} collective-permute-done((bf16[2,256,128]{2,1,0:T(8,128)(2,1)S(1)}, bf16[2,256,128]{2,1,0:T(8,128)(2,1)S(1)}, u32[]{:S(2)}, u32[]{:S(2)}) %collective-permute-start.15) | collective-permute-done | bytes 131104 | tf_op jit(solution)/shard_map/ppermute | solution.py:38
  58.6 5.6 %collective-permute-start.19 = (f32[512,128]{1,0:T(8,128)S(1)}, f32[512,128]{1,0:T(8,128)S(1)}, u32[]{:S(2)}, u32[]{:S(2)}) collective-permute-start(f32[512,128]{1,0:T(8,128)S(1)} %bitcast.49), channel_id=1, source_target_pairs={{0,8},{8,0},{16,24},{24,16},{32,40},{40,32},{48,56},{56,48},{64,72... | collective-permute-start | bytes 786440 | tf_op jit(solution)/shard_map/ppermute | solution.py:33
  65.4 1.6 %dense.1 = (bf16[256,256]{1,0:T(8,128)(2,1)}, bf16[640,128]{1,0:T(8,128)(2,1)S(1)}, bf16[640,128]{1,0:T(8,128)(2,1)S(1)}) custom-call(f32[512,128]{1,0:T(8,128)S(1)} %bitcast.50, f32[512,128]{1,0:T(8,128)S(1)} %collective-permute-done.19.agg_other, bf16[256,256]{1,0:T(8,128)(2,1)S(1)} %copy-done.2, bf16[256,256]{1,0:T(8,128)(2,1)S(1)} %copy-done.1, ...), custom_call_target="tpu_custom_call" | custom-call | tf_op jit(solution)/shard_map/dense/pallas_call | solution.py:452
  69.7 2.5 %collective-permute-start.23 = (bf16[640,128]{1,0:T(8,128)(2,1)S(1)}, bf16[640,128]{1,0:T(8,128)(2,1)S(1)}, u32[]{:S(2)}, u32[]{:S(2)}) collective-permute-start(bf16[640,128]{1,0:T(8,128)(2,1)S(1)} %get-tuple-element.47.refs_0_), channel_id=1, source_target_pairs={{0,2},{1,3},{2,0},{3,1},{4,6},{5,7},{6,4},{7,5},{8,10},{9,11},{10,... | collective-permute-start | bytes 491528 | tf_op jit(solution)/shard_map/ppermute | solution.py:38
  75.7 8.8 %collective-permute-done.23.refs_4_ = bf16[640,128]{1,0:T(8,128)(2,1)S(1)} collective-permute-done((bf16[640,128]{1,0:T(8,128)(2,1)S(1)}, bf16[640,128]{1,0:T(8,128)(2,1)S(1)}, u32[]{:S(2)}, u32[]{:S(2)}) %collective-permute-start.23) | collective-permute-done | bytes 163872 | tf_op jit(solution)/shard_map/ppermute | solution.py:38
  84.5 1.6 %collective-permute-done.24.refs_5_ = bf16[640,128]{1,0:T(8,128)(2,1)S(1)} collective-permute-done((bf16[640,128]{1,0:T(8,128)(2,1)S(1)}, bf16[640,128]{1,0:T(8,128)(2,1)S(1)}, u32[]{:S(2)}, u32[]{:S(2)}) %collective-permute-start.24) | collective-permute-done | bytes 163872 | tf_op jit(solution)/shard_map/ppermute | solution.py:38
  87.1 4.2 %collective-permute-start.31 = (bf16[640,128]{1,0:T(8,128)(2,1)S(1)}, bf16[640,128]{1,0:T(8,128)(2,1)S(1)}, u32[]{:S(2)}, u32[]{:S(2)}) collective-permute-start(bf16[640,128]{1,0:T(8,128)(2,1)S(1)} %get-tuple-element.51), channel_id=1, source_target_pairs={{0,224},{8,232},{16,240},{24,248},{32,0},{40,8},{48,16},{56,24},{6... | collective-permute-start | bytes 491528 | tf_op jit(solution)/shard_map/ppermute | solution.py:47
  91.3 1.8 %backward_near.1.parts = bf16[32,256,128]{2,1,0:T(8,128)(2,1)S(1)} custom-call(s32[68]{0:T(128)S(1)} %get-tuple-element.36.lists_any, bf16[12,256,256]{2,1,0:T(8,128)(2,1)S(1)} %bitcast.46, bf16[12,256,256]{2,1,0:T(8,128)(2,1)S(1)} %collective-permute-done.3.adj1, bf16[8,512,128]{2,1,0:T(8,128)(2,1)S(1)} %get-tuple-element.49.back), custom_call_target="tpu_custom_call" | custom-call | flops 352321536 | bytes 6291456 | tf_op jit(solution)/shard_map/backward_near/pallas_call | solution.py:440
  96.4 1.6 %collective-permute-start.32 = (bf16[1152,128]{1,0:T(8,128)(2,1)S(1)}, bf16[1152,128]{1,0:T(8,128)(2,1)S(1)}, u32[]{:S(2)}, u32[]{:S(2)}) collective-permute-start(bf16[1152,128]{1,0:T(8,128)(2,1)S(1)} %pad_maximum_fusion.3), channel_id=1, source_target_pairs={{0,224},{8,232},{16,240},{24,248},{32,0},{40,8},{48,16},{56,24},{6... | collective-permute-start | bytes 884744 | tf_op jit(solution)/shard_map/ppermute | solution.py:47
  98.0 4.7 %collective-permute-done.28.up2 = bf16[1152,128]{1,0:T(8,128)(2,1)S(1)} collective-permute-done((bf16[1152,128]{1,0:T(8,128)(2,1)S(1)}, bf16[1152,128]{1,0:T(8,128)(2,1)S(1)}, u32[]{:S(2)}, u32[]{:S(2)}) %collective-permute-start.28) | collective-permute-done | bytes 294944 | tf_op jit(solution)/shard_map/ppermute | solution.py:47
  103.0 2.7 %collective-permute-start.33 = (bf16[1152,128]{1,0:T(8,128)(2,1)S(1)}, bf16[1152,128]{1,0:T(8,128)(2,1)S(1)}, u32[]{:S(2)}, u32[]{:S(2)}) collective-permute-start(bf16[1152,128]{1,0:T(8,128)(2,1)S(1)} %pad_maximum_fusion.4), channel_id=1, source_target_pairs={{0,224},{8,232},{16,240},{24,248},{32,0},{40,8},{48,16},{56,24},{6... | collective-permute-start | bytes 884744 | tf_op jit(solution)/shard_map/ppermute | solution.py:47
  105.8 3.9 %collective-permute-done.29.up3 = bf16[1152,128]{1,0:T(8,128)(2,1)S(1)} collective-permute-done((bf16[1152,128]{1,0:T(8,128)(2,1)S(1)}, bf16[1152,128]{1,0:T(8,128)(2,1)S(1)}, u32[]{:S(2)}, u32[]{:S(2)}) %collective-permute-start.29) | collective-permute-done | bytes 294944 | tf_op jit(solution)/shard_map/ppermute | solution.py:47
  110.0 2.7 %collective-permute-start.34 = (bf16[1024,128]{1,0:T(8,128)(2,1)S(1)}, bf16[1024,128]{1,0:T(8,128)(2,1)S(1)}, u32[]{:S(2)}, u32[]{:S(2)}) collective-permute-start(bf16[1024,128]{1,0:T(8,128)(2,1)S(1)} %fusion), channel_id=1, source_target_pairs={{0,224},{8,232},{16,240},{24,248},{32,0},{40,8},{48,16},{56,24},{6... | collective-permute-start | bytes 786440 | tf_op jit(solution)/shard_map/ppermute | solution.py:47
  112.7 3.4 %collective-permute-done.34.down4 = bf16[1024,128]{1,0:T(8,128)(2,1)S(1)} collective-permute-done((bf16[1024,128]{1,0:T(8,128)(2,1)S(1)}, bf16[1024,128]{1,0:T(8,128)(2,1)S(1)}, u32[]{:S(2)}, u32[]{:S(2)}) %collective-permute-start.34) | collective-permute-done | bytes 262176 | tf_op jit(solution)/shard_map/ppermute | solution.py:47
  118.0 5.7 %collective-permute-start.36 = (bf16[128,128]{1,0:T(8,128)(2,1)S(1)}, bf16[128,128]{1,0:T(8,128)(2,1)S(1)}, u32[]{:S(2)}, u32[]{:S(2)}) collective-permute-start(bf16[128,128]{1,0:T(8,128)(2,1)S(1)} %slice.122), channel_id=1, source_target_pairs={{0,4},{1,5},{2,6},{3,7},{4,0},{5,1},{6,2},{7,3},{8,12},{9,13},{10,... | collective-permute-start | bytes 98312 | tf_op jit(solution)/shard_map/ppermute | solution.py:543
  124.8 2.4 %collective-permute-done.36.w_lo = bf16[128,128]{1,0:T(8,128)(2,1)S(1)} collective-permute-done((bf16[128,128]{1,0:T(8,128)(2,1)S(1)}, bf16[128,128]{1,0:T(8,128)(2,1)S(1)}, u32[]{:S(2)}, u32[]{:S(2)}) %collective-permute-start.36) | collective-permute-done | bytes 32800 | tf_op jit(solution)/shard_map/ppermute | solution.py:543
  127.1 2.0 %collective-permute-done.37.w_both = bf16[128,128]{1,0:T(8,128)(2,1)S(1)} collective-permute-done((bf16[128,128]{1,0:T(8,128)(2,1)S(1)}, bf16[128,128]{1,0:T(8,128)(2,1)S(1)}, u32[]{:S(2)}, u32[]{:S(2)}) %collective-permute-start.37) | collective-permute-done | bytes 32800 | tf_op jit(solution)/shard_map/ppermute | solution.py:547
  129.2 10.1 %collective-permute-start.38 = (bf16[768,128]{1,0:T(8,128)(2,1)S(1)}, bf16[768,128]{1,0:T(8,128)(2,1)S(1)}, u32[]{:S(2)}, u32[]{:S(2)}) collective-permute-start(bf16[768,128]{1,0:T(8,128)(2,1)S(1)} %get-tuple-element.55), channel_id=1, source_target_pairs={{0,8},{8,0},{16,24},{24,16},{32,40},{40,32},{48,56},{56,48},{64,72... | collective-permute-start | bytes 589832 | tf_op jit(solution)/shard_map/ppermute | solution.py:33
  (93 shorter events, 28.0 us)
Async XLA Ops:
  0.6 7.9 %collective-permute-start = (bf16[256,256]{1,0:T(8,128)(2,1)}, bf16[256,256]{1,0:T(8,128)(2,1)S(1)}, u32[]{:S(2)}, u32[]{:S(2)}) collective-permute-start(bf16[256,256]{1,0:T(8,128)(2,1)} %bitcast.51), channel_id=1, source_target_pairs={{0,16},{8,24},{16,0},{24,8},{32,48},{40,56},{48,32},{56,40},{64,80... | collective-permute-start | bytes 393224 | tf_op jit(solution)/shard_map/ppermute | solution.py:33
  3.5 37.4 %collective-permute-start.3 = (bf16[12,256,256]{2,1,0:T(8,128)(2,1)}, bf16[12,256,256]{2,1,0:T(8,128)(2,1)S(1)}, u32[]{:S(2)}, u32[]{:S(2)}) collective-permute-start(bf16[12,256,256]{2,1,0:T(8,128)(2,1)} %bitcast.42), channel_id=1, source_target_pairs={{0,8},{8,0},{16,24},{24,16},{32,40},{40,32},{48,56},{56,48},{64,72... | collective-permute-start | bytes 4718600 | tf_op jit(solution)/shard_map/ppermute | solution.py:33
  10.1 12.2 %collective-permute-start.7 = (bf16[4,256,128]{2,1,0:T(8,128)(2,1)S(1)}, bf16[4,256,128]{2,1,0:T(8,128)(2,1)S(1)}, u32[]{:S(2)}, u32[]{:S(2)}) collective-permute-start(bf16[4,256,128]{2,1,0:T(8,128)(2,1)S(1)} %pad_maximum_fusion.5.refs_0_), channel_id=1, source_target_pairs={{0,32},{8,40},{16,48},{24,56},{32,64},{40,72},{48,80},{56,88},{64,... | collective-permute-start | bytes 786440 | tf_op jit(solution)/shard_map/ppermute | solution.py:47
  11.8 10.5 %collective-permute-start.4 = (bf16[4,256,128]{2,1,0:T(8,128)(2,1)S(1)}, bf16[4,256,128]{2,1,0:T(8,128)(2,1)S(1)}, u32[]{:S(2)}, u32[]{:S(2)}) collective-permute-start(bf16[4,256,128]{2,1,0:T(8,128)(2,1)S(1)} %pad_maximum_fusion.5.refs_0_), channel_id=1, source_target_pairs={{0,224},{8,232},{16,240},{24,248},{32,0},{40,8},{48,16},{56,24},{6... | collective-permute-start | bytes 786440 | tf_op jit(solution)/shard_map/ppermute | solution.py:47
  22.2 8.3 %collective-permute-start.8 = (bf16[4,256,128]{2,1,0:T(8,128)(2,1)S(1)}, bf16[4,256,128]{2,1,0:T(8,128)(2,1)S(1)}, u32[]{:S(2)}, u32[]{:S(2)}) collective-permute-start(bf16[4,256,128]{2,1,0:T(8,128)(2,1)S(1)} %collective-permute-done.7.refs_6_), channel_id=1, source_target_pairs={{0,32},{8,40},{16,48},{24,56},{32,64},{40,72},{48,80},{56,88},{64,... | collective-permute-start | bytes 786440 | tf_op jit(solution)/shard_map/ppermute | solution.py:47
  22.3 8.3 %collective-permute-start.5 = (bf16[4,256,128]{2,1,0:T(8,128)(2,1)S(1)}, bf16[4,256,128]{2,1,0:T(8,128)(2,1)S(1)}, u32[]{:S(2)}, u32[]{:S(2)}) collective-permute-start(bf16[4,256,128]{2,1,0:T(8,128)(2,1)S(1)} %collective-permute-done.4.refs_1_), channel_id=1, source_target_pairs={{0,224},{8,232},{16,240},{24,248},{32,0},{40,8},{48,16},{56,24},{6... | collective-permute-start | bytes 786440 | tf_op jit(solution)/shard_map/ppermute | solution.py:47
  30.6 7.4 %collective-permute-start.9 = (bf16[4,256,128]{2,1,0:T(8,128)(2,1)S(1)}, bf16[4,256,128]{2,1,0:T(8,128)(2,1)S(1)}, u32[]{:S(2)}, u32[]{:S(2)}) collective-permute-start(bf16[4,256,128]{2,1,0:T(8,128)(2,1)S(1)} %collective-permute-done.8.refs_5_), channel_id=1, source_target_pairs={{0,32},{8,40},{16,48},{24,56},{32,64},{40,72},{48,80},{56,88},{64,... | collective-permute-start | bytes 786440 | tf_op jit(solution)/shard_map/ppermute | solution.py:47
  30.6 7.5 %collective-permute-start.6 = (bf16[4,256,128]{2,1,0:T(8,128)(2,1)S(1)}, bf16[4,256,128]{2,1,0:T(8,128)(2,1)S(1)}, u32[]{:S(2)}, u32[]{:S(2)}) collective-permute-start(bf16[4,256,128]{2,1,0:T(8,128)(2,1)S(1)} %collective-permute-done.5.refs_2_), channel_id=1, source_target_pairs={{0,224},{8,232},{16,240},{24,248},{32,0},{40,8},{48,16},{56,24},{6... | collective-permute-start | bytes 786440 | tf_op jit(solution)/shard_map/ppermute | solution.py:47
  33.3 7.6 %collective-permute-start.2 = (bf16[256,256]{1,0:T(8,128)(2,1)}, bf16[256,256]{1,0:T(8,128)(2,1)S(1)}, u32[]{:S(2)}, u32[]{:S(2)}) collective-permute-start(bf16[256,256]{1,0:T(8,128)(2,1)} %cot_own.1), channel_id=1, source_target_pairs={{0,8},{8,0},{16,24},{24,16},{32,40},{40,32},{48,56},{56,48},{64,72... | collective-permute-start | bytes 393224 | tf_op jit(solution)/shard_map/ppermute | solution.py:33
  44.3 6.3 %collective-permute-start.13 = (bf16[2,256,128]{2,1,0:T(8,128)(2,1)S(1)}, bf16[2,256,128]{2,1,0:T(8,128)(2,1)S(1)}, u32[]{:S(2)}, u32[]{:S(2)}) collective-permute-start(bf16[2,256,128]{2,1,0:T(8,128)(2,1)S(1)} %get-tuple-element.40), channel_id=1, source_target_pairs={{0,1},{1,2},{2,3},{3,0},{4,5},{5,6},{6,7},{7,4},{8,9},{9,10},{10,1... | collective-permute-start | bytes 393224 | tf_op jit(solution)/shard_map/ppermute | solution.py:38
  45.2 7.4 %collective-permute-start.14 = (bf16[2,256,128]{2,1,0:T(8,128)(2,1)S(1)}, bf16[2,256,128]{2,1,0:T(8,128)(2,1)S(1)}, u32[]{:S(2)}, u32[]{:S(2)}) collective-permute-start(bf16[2,256,128]{2,1,0:T(8,128)(2,1)S(1)} %get-tuple-element.41), channel_id=1, source_target_pairs={{0,6},{1,7},{2,4},{3,5},{4,2},{5,3},{6,0},{7,1},{8,14},{9,15},{10,... | collective-permute-start | bytes 393224 | tf_op jit(solution)/shard_map/ppermute | solution.py:38
  47.1 10.5 %collective-permute-start.15 = (bf16[2,256,128]{2,1,0:T(8,128)(2,1)S(1)}, bf16[2,256,128]{2,1,0:T(8,128)(2,1)S(1)}, u32[]{:S(2)}, u32[]{:S(2)}) collective-permute-start(bf16[2,256,128]{2,1,0:T(8,128)(2,1)S(1)} %get-tuple-element.42), channel_id=1, source_target_pairs={{0,2},{1,3},{2,0},{3,1},{4,6},{5,7},{6,4},{7,5},{8,10},{9,11},{10,... | collective-permute-start | bytes 393224 | tf_op jit(solution)/shard_map/ppermute | solution.py:38
  49.2 8.3 %collective-permute-start.16 = (bf16[2,256,128]{2,1,0:T(8,128)(2,1)S(1)}, bf16[2,256,128]{2,1,0:T(8,128)(2,1)S(1)}, u32[]{:S(2)}, u32[]{:S(2)}) collective-permute-start(bf16[2,256,128]{2,1,0:T(8,128)(2,1)S(1)} %get-tuple-element.43), channel_id=1, source_target_pairs={{0,3},{1,0},{2,1},{3,2},{4,7},{5,4},{6,5},{7,6},{8,11},{9,8},{10,9... | collective-permute-start | bytes 393224 | tf_op jit(solution)/shard_map/ppermute | solution.py:38
  49.8 7.7 %collective-permute-start.17 = (bf16[2,256,128]{2,1,0:T(8,128)(2,1)S(1)}, bf16[2,256,128]{2,1,0:T(8,128)(2,1)S(1)}, u32[]{:S(2)}, u32[]{:S(2)}) collective-permute-start(bf16[2,256,128]{2,1,0:T(8,128)(2,1)S(1)} %get-tuple-element.44), channel_id=1, source_target_pairs={{0,5},{1,6},{2,7},{3,4},{4,1},{5,2},{6,3},{7,0},{8,13},{9,14},{10,... | collective-permute-start | bytes 393224 | tf_op jit(solution)/shard_map/ppermute | solution.py:38
  50.6 7.9 %collective-permute-start.18 = (bf16[2,256,128]{2,1,0:T(8,128)(2,1)S(1)}, bf16[2,256,128]{2,1,0:T(8,128)(2,1)S(1)}, u32[]{:S(2)}, u32[]{:S(2)}) collective-permute-start(bf16[2,256,128]{2,1,0:T(8,128)(2,1)S(1)} %get-tuple-element.45), channel_id=1, source_target_pairs={{0,7},{1,4},{2,5},{3,6},{4,3},{5,0},{6,1},{7,2},{8,15},{9,12},{10,... | collective-permute-start | bytes 393224 | tf_op jit(solution)/shard_map/ppermute | solution.py:38
  58.6 6.8 %collective-permute-start.19 = (f32[512,128]{1,0:T(8,128)S(1)}, f32[512,128]{1,0:T(8,128)S(1)}, u32[]{:S(2)}, u32[]{:S(2)}) collective-permute-start(f32[512,128]{1,0:T(8,128)S(1)} %bitcast.49), channel_id=1, source_target_pairs={{0,8},{8,0},{16,24},{24,16},{32,40},{40,32},{48,56},{56,48},{64,72... | collective-permute-start | bytes 786440 | tf_op jit(solution)/shard_map/ppermute | solution.py:33
  67.6 6.2 %collective-permute-start.21 = (bf16[640,128]{1,0:T(8,128)(2,1)S(1)}, bf16[640,128]{1,0:T(8,128)(2,1)S(1)}, u32[]{:S(2)}, u32[]{:S(2)}) collective-permute-start(bf16[640,128]{1,0:T(8,128)(2,1)S(1)} %get-tuple-element.47.refs_0_), channel_id=1, source_target_pairs={{0,1},{1,2},{2,3},{3,0},{4,5},{5,6},{6,7},{7,4},{8,9},{9,10},{10,1... | collective-permute-start | bytes 491528 | tf_op jit(solution)/shard_map/ppermute | solution.py:38
  68.4 7.3 %collective-permute-start.22 = (bf16[640,128]{1,0:T(8,128)(2,1)S(1)}, bf16[640,128]{1,0:T(8,128)(2,1)S(1)}, u32[]{:S(2)}, u32[]{:S(2)}) collective-permute-start(bf16[640,128]{1,0:T(8,128)(2,1)S(1)} %get-tuple-element.48), channel_id=1, source_target_pairs={{0,6},{1,7},{2,4},{3,5},{4,2},{5,3},{6,0},{7,1},{8,14},{9,15},{10,... | collective-permute-start | bytes 491528 | tf_op jit(solution)/shard_map/ppermute | solution.py:38
  69.7 14.9 %collective-permute-start.23 = (bf16[640,128]{1,0:T(8,128)(2,1)S(1)}, bf16[640,128]{1,0:T(8,128)(2,1)S(1)}, u32[]{:S(2)}, u32[]{:S(2)}) collective-permute-start(bf16[640,128]{1,0:T(8,128)(2,1)S(1)} %get-tuple-element.47.refs_0_), channel_id=1, source_target_pairs={{0,2},{1,3},{2,0},{3,1},{4,6},{5,7},{6,4},{7,5},{8,10},{9,11},{10,... | collective-permute-start | bytes 491528 | tf_op jit(solution)/shard_map/ppermute | solution.py:38
  72.1 14.0 %collective-permute-start.24 = (bf16[640,128]{1,0:T(8,128)(2,1)S(1)}, bf16[640,128]{1,0:T(8,128)(2,1)S(1)}, u32[]{:S(2)}, u32[]{:S(2)}) collective-permute-start(bf16[640,128]{1,0:T(8,128)(2,1)S(1)} %get-tuple-element.47.refs_0_), channel_id=1, source_target_pairs={{0,3},{1,0},{2,1},{3,2},{4,7},{5,4},{6,5},{7,6},{8,11},{9,8},{10,9... | collective-permute-start | bytes 491528 | tf_op jit(solution)/shard_map/ppermute | solution.py:38
  72.6 13.6 %collective-permute-start.25 = (bf16[640,128]{1,0:T(8,128)(2,1)S(1)}, bf16[640,128]{1,0:T(8,128)(2,1)S(1)}, u32[]{:S(2)}, u32[]{:S(2)}) collective-permute-start(bf16[640,128]{1,0:T(8,128)(2,1)S(1)} %get-tuple-element.48), channel_id=1, source_target_pairs={{0,5},{1,6},{2,7},{3,4},{4,1},{5,2},{6,3},{7,0},{8,13},{9,14},{10,... | collective-permute-start | bytes 491528 | tf_op jit(solution)/shard_map/ppermute | solution.py:38
  73.8 12.4 %collective-permute-start.26 = (bf16[640,128]{1,0:T(8,128)(2,1)S(1)}, bf16[640,128]{1,0:T(8,128)(2,1)S(1)}, u32[]{:S(2)}, u32[]{:S(2)}) collective-permute-start(bf16[640,128]{1,0:T(8,128)(2,1)S(1)} %get-tuple-element.48), channel_id=1, source_target_pairs={{0,7},{1,4},{2,5},{3,6},{4,3},{5,0},{6,1},{7,2},{8,15},{9,12},{10,... | collective-permute-start | bytes 491528 | tf_op jit(solution)/shard_map/ppermute | solution.py:38
  87.0 7.6 %collective-permute-start.27 = (bf16[640,128]{1,0:T(8,128)(2,1)S(1)}, bf16[640,128]{1,0:T(8,128)(2,1)S(1)}, u32[]{:S(2)}, u32[]{:S(2)}) collective-permute-start(bf16[640,128]{1,0:T(8,128)(2,1)S(1)} %get-tuple-element.50.own), channel_id=1, source_target_pairs={{0,32},{8,40},{16,48},{24,56},{32,64},{40,72},{48,80},{56,88},{64,... | collective-permute-start | bytes 491528 | tf_op jit(solution)/shard_map/ppermute | solution.py:47
  87.1 7.6 %collective-permute-start.31 = (bf16[640,128]{1,0:T(8,128)(2,1)S(1)}, bf16[640,128]{1,0:T(8,128)(2,1)S(1)}, u32[]{:S(2)}, u32[]{:S(2)}) collective-permute-start(bf16[640,128]{1,0:T(8,128)(2,1)S(1)} %get-tuple-element.51), channel_id=1, source_target_pairs={{0,224},{8,232},{16,240},{24,248},{32,0},{40,8},{48,16},{56,24},{6... | collective-permute-start | bytes 491528 | tf_op jit(solution)/shard_map/ppermute | solution.py:47
  94.8 7.8 %collective-permute-start.28 = (bf16[1152,128]{1,0:T(8,128)(2,1)S(1)}, bf16[1152,128]{1,0:T(8,128)(2,1)S(1)}, u32[]{:S(2)}, u32[]{:S(2)}) collective-permute-start(bf16[1152,128]{1,0:T(8,128)(2,1)S(1)} %pad_maximum_fusion), channel_id=1, source_target_pairs={{0,32},{8,40},{16,48},{24,56},{32,64},{40,72},{48,80},{56,88},{64,... | collective-permute-start | bytes 884744 | tf_op jit(solution)/shard_map/ppermute | solution.py:47
  96.4 6.5 %collective-permute-start.32 = (bf16[1152,128]{1,0:T(8,128)(2,1)S(1)}, bf16[1152,128]{1,0:T(8,128)(2,1)S(1)}, u32[]{:S(2)}, u32[]{:S(2)}) collective-permute-start(bf16[1152,128]{1,0:T(8,128)(2,1)S(1)} %pad_maximum_fusion.3), channel_id=1, source_target_pairs={{0,224},{8,232},{16,240},{24,248},{32,0},{40,8},{48,16},{56,24},{6... | collective-permute-start | bytes 884744 | tf_op jit(solution)/shard_map/ppermute | solution.py:47
  102.8 6.9 %collective-permute-start.29 = (bf16[1152,128]{1,0:T(8,128)(2,1)S(1)}, bf16[1152,128]{1,0:T(8,128)(2,1)S(1)}, u32[]{:S(2)}, u32[]{:S(2)}) collective-permute-start(bf16[1152,128]{1,0:T(8,128)(2,1)S(1)} %pad_maximum_fusion.1), channel_id=1, source_target_pairs={{0,32},{8,40},{16,48},{24,56},{32,64},{40,72},{48,80},{56,88},{64,... | collective-permute-start | bytes 884744 | tf_op jit(solution)/shard_map/ppermute | solution.py:47
  103.0 6.8 %collective-permute-start.33 = (bf16[1152,128]{1,0:T(8,128)(2,1)S(1)}, bf16[1152,128]{1,0:T(8,128)(2,1)S(1)}, u32[]{:S(2)}, u32[]{:S(2)}) collective-permute-start(bf16[1152,128]{1,0:T(8,128)(2,1)S(1)} %pad_maximum_fusion.4), channel_id=1, source_target_pairs={{0,224},{8,232},{16,240},{24,248},{32,0},{40,8},{48,16},{56,24},{6... | collective-permute-start | bytes 884744 | tf_op jit(solution)/shard_map/ppermute | solution.py:47
  109.8 6.9 %collective-permute-start.30 = (bf16[1152,128]{1,0:T(8,128)(2,1)S(1)}, bf16[1152,128]{1,0:T(8,128)(2,1)S(1)}, u32[]{:S(2)}, u32[]{:S(2)}) collective-permute-start(bf16[1152,128]{1,0:T(8,128)(2,1)S(1)} %pad_maximum_fusion.2), channel_id=1, source_target_pairs={{0,32},{8,40},{16,48},{24,56},{32,64},{40,72},{48,80},{56,88},{64,... | collective-permute-start | bytes 884744 | tf_op jit(solution)/shard_map/ppermute | solution.py:47
  116.8 12.3 %collective-permute-start.35 = (bf16[640,128]{1,0:T(8,128)(2,1)S(1)}, bf16[640,128]{1,0:T(8,128)(2,1)S(1)}, u32[]{:S(2)}, u32[]{:S(2)}) collective-permute-start(bf16[640,128]{1,0:T(8,128)(2,1)S(1)} %get-tuple-element.53.sent), channel_id=1, source_target_pairs={{0,16},{8,24},{16,0},{24,8},{32,48},{40,56},{48,32},{56,40},{64,80... | collective-permute-start | bytes 491528 | tf_op jit(solution)/shard_map/ppermute | solution.py:33
  118.0 9.1 %collective-permute-start.36 = (bf16[128,128]{1,0:T(8,128)(2,1)S(1)}, bf16[128,128]{1,0:T(8,128)(2,1)S(1)}, u32[]{:S(2)}, u32[]{:S(2)}) collective-permute-start(bf16[128,128]{1,0:T(8,128)(2,1)S(1)} %slice.122), channel_id=1, source_target_pairs={{0,4},{1,5},{2,6},{3,7},{4,0},{5,1},{6,2},{7,3},{8,12},{9,13},{10,... | collective-permute-start | bytes 98312 | tf_op jit(solution)/shard_map/ppermute | solution.py:543
  129.2 11.2 %collective-permute-start.38 = (bf16[768,128]{1,0:T(8,128)(2,1)S(1)}, bf16[768,128]{1,0:T(8,128)(2,1)S(1)}, u32[]{:S(2)}, u32[]{:S(2)}) collective-permute-start(bf16[768,128]{1,0:T(8,128)(2,1)S(1)} %get-tuple-element.55), channel_id=1, source_target_pairs={{0,8},{8,0},{16,24},{24,16},{32,40},{40,32},{48,56},{56,48},{64,72... | collective-permute-start | bytes 589832 | tf_op jit(solution)/shard_map/ppermute | solution.py:33
  (13 other events, 121.2 us)

commit v11 on v9

--- a/solution.py
+++ b/solution.py
@@ -18,6 +18,7 @@
 UNROLL = 4
 PART = 16
 LIST = 4 * PART + 4
+NEAR_MOVES = (0, 1, 5, 3, 7, 4)
 MOVES = (0, 6, 2, 5, 7, 1, 3, 4)
 
 
@@ -185,10 +186,18 @@
     received, (up, down, back, acc, lists, sem, pieces) = refs[:NCOL], refs[NCOL:]
     copy = pltpu.make_async_copy(lists_any, lists, sem)
     copy.start()
-    for k, ref in zip(MOVES, received):
+    for k, ref in zip(NEAR_MOVES, received):
         source = col_target(k, -1)
         back[source] = ref[: 2 * TILE, :]
         pieces[source] = ref[2 * TILE :, :]
+    for h, ref in enumerate(received[len(NEAR_MOVES) :]):
+        for j, k in enumerate((2, 6)):
+            source = col_target(k, -1)
+            start = j * (TILE + W_ROWS // 2)
+            back[source, h * TILE : (h + 1) * TILE, :] = ref[start : start + TILE, :]
+            pieces[source, h * W_ROWS // 2 : (h + 1) * W_ROWS // 2, :] = ref[
+                start + TILE : start + TILE + W_ROWS // 2, :
+            ]
     acc[...] = jnp.zeros_like(acc)
     piece = pieces[0].astype(jnp.float32)
     for c in range(1, NCOL):
@@ -520,7 +529,15 @@
     ).reshape(2 * TILE, HALF)
     agg_other = quad_permute(agg, 1)
     activated, send, send_x = dense(agg, agg_other, weight, cotangent, cot1)
-    received = [col_move(send if k < 4 else send_x, k) if k else send for k in MOVES]
+    received = [col_move(send if k < 4 else send_x, k) if k else send for k in NEAR_MOVES]
+
+    def forward(near, across, h):
+        rows = [slice(h * TILE, (h + 1) * TILE)]
+        rows += [slice(2 * TILE + h * W_ROWS // 2, 2 * TILE + (h + 1) * W_ROWS // 2)]
+        message = jnp.concatenate([x[r] for x in (near, across) for r in rows])
+        return col_move(message, 3 if h else 1)
+
+    received += [forward(received[1], received[2], 0), forward(received[3], received[4], 1)]
 
     half, size = 2 * TILE, QUAD * TILE
     own, own_down, back = backward_far(lists, adj0, adj1, received)

time: 136 us -> 139 us (1.022)
  waiting for transfers between devices: 51.8 us -> 53.4 us
  starting transfers between devices: 69.2 us -> 70.7 us
    ppermute x16, waiting for transfers between devices: 29.6 us -> 33.4 us  [z_shift(): return lax.ppermute(x, 'row', row_pairs(lambda z, q: (z + step, q)))]
    ppermute x14, waiting for transfers between devices: 15.8 us -> 13.3 us  [col_move(): return lax.ppermute(x, 'col', pairs)]
    ppermute x7, starting transfers between devices: 21.1 us -> 23.5 us  [quad_permute(): return lax.ppermute(x, 'row', row_pairs(lambda z, q: (z, q ^ flip)))]
  transfers between devices with their start and end apart: 39 -> 39, of which waited for: 20 -> 19; matrix products, arithmetic and copies ran while one was open for 0% -> 1% of each run, Pallas kernels for 4% -> 4%
where the time goes in v11:
time: 139 us
  starting transfers between devices  70.7 us (51%)
  waiting for transfers between devices  53.4 us (38%)
  Pallas kernels  10.2 us (7%)
  local copies, waits for them, and re-layouts  2.42 us (2%)
  between operations  1.71 us (1%)
    ppermute x16, waiting for transfers between devices, z_shift(): return lax.ppermute(x, 'row', row_pairs(lambda z, q: (z + step, q)))  33.4 us
    ppermute x16, starting transfers between devices, z_shift(): return lax.ppermute(x, 'row', row_pairs(lambda z, q: (z + step, q)))  26.7 us
    ppermute x7, starting transfers between devices, quad_permute(): return lax.ppermute(x, 'row', row_pairs(lambda z, q: (z, q ^ flip)))  23.5 us
    ppermute x14, starting transfers between devices, col_move(): return lax.ppermute(x, 'col', pairs)  19.7 us
    ppermute x14, waiting for transfers between devices, col_move(): return lax.ppermute(x, 'col', pairs)  13.3 us
    ppermute x7, waiting for transfers between devices, quad_permute(): return lax.ppermute(x, 'row', row_pairs(lambda z, q: (z, q ^ flip)))  3.3 us
  transfers between devices with their start and end apart: 39, of which 19 were waited for; matrix products, arithmetic and copies ran while one was open for 1% of the time, Pallas kernels for 4%

profile of v11, /device:TPU:1, one launch (start us, length us, event | category | flops | bytes accessed | tf_op | source)
XLA Modules:
  0.0 139.1 jit_solution(6215054257653358596)
XLA Ops:
  0.6 3.7 %collective-permute-start = (bf16[256,256]{1,0:T(8,128)(2,1)}, bf16[256,256]{1,0:T(8,128)(2,1)S(1)}, u32[]{:S(2)}, u32[]{:S(2)}) collective-permute-start(bf16[256,256]{1,0:T(8,128)(2,1)} %bitcast.51), channel_id=1, source_target_pairs={{0,16},{8,24},{16,0},{24,8},{32,48},{40,56},{48,32},{56,40},{64,80... | collective-permute-start | bytes 393224 | tf_op jit(solution)/shard_map/ppermute | solution.py:34
  11.8 4.7 %collective-permute-start.3 = (bf16[4,256,128]{2,1,0:T(8,128)(2,1)S(1)}, bf16[4,256,128]{2,1,0:T(8,128)(2,1)S(1)}, u32[]{:S(2)}, u32[]{:S(2)}) collective-permute-start(bf16[4,256,128]{2,1,0:T(8,128)(2,1)S(1)} %pad_maximum_fusion.5.refs_0_), channel_id=1, source_target_pairs={{0,224},{8,232},{16,240},{24,248},{32,0},{40,8},{48,16},{56,24},{6... | collective-permute-start | bytes 786440 | tf_op jit(solution)/shard_map/ppermute | solution.py:48
  16.5 5.6 %collective-permute-done.3.refs_1_ = bf16[4,256,128]{2,1,0:T(8,128)(2,1)S(1)} collective-permute-done((bf16[4,256,128]{2,1,0:T(8,128)(2,1)S(1)}, bf16[4,256,128]{2,1,0:T(8,128)(2,1)S(1)}, u32[]{:S(2)}, u32[]{:S(2)}) %collective-permute-start.3) | collective-permute-done | bytes 262176 | tf_op jit(solution)/shard_map/ppermute | solution.py:48
  22.1 3.4 %collective-permute-start.4 = (bf16[4,256,128]{2,1,0:T(8,128)(2,1)S(1)}, bf16[4,256,128]{2,1,0:T(8,128)(2,1)S(1)}, u32[]{:S(2)}, u32[]{:S(2)}) collective-permute-start(bf16[4,256,128]{2,1,0:T(8,128)(2,1)S(1)} %collective-permute-done.3.refs_1_), channel_id=1, source_target_pairs={{0,224},{8,232},{16,240},{24,248},{32,0},{40,8},{48,16},{56,24},{6... | collective-permute-start | bytes 786440 | tf_op jit(solution)/shard_map/ppermute | solution.py:48
  25.5 4.6 %collective-permute-done.4.refs_2_ = bf16[4,256,128]{2,1,0:T(8,128)(2,1)S(1)} collective-permute-done((bf16[4,256,128]{2,1,0:T(8,128)(2,1)S(1)}, bf16[4,256,128]{2,1,0:T(8,128)(2,1)S(1)}, u32[]{:S(2)}, u32[]{:S(2)}) %collective-permute-start.4) | collective-permute-done | bytes 262176 | tf_op jit(solution)/shard_map/ppermute | solution.py:48
  30.1 3.4 %collective-permute-start.5 = (bf16[4,256,128]{2,1,0:T(8,128)(2,1)S(1)}, bf16[4,256,128]{2,1,0:T(8,128)(2,1)S(1)}, u32[]{:S(2)}, u32[]{:S(2)}) collective-permute-start(bf16[4,256,128]{2,1,0:T(8,128)(2,1)S(1)} %collective-permute-done.4.refs_2_), channel_id=1, source_target_pairs={{0,224},{8,232},{16,240},{24,248},{32,0},{40,8},{48,16},{56,24},{6... | collective-permute-start | bytes 786440 | tf_op jit(solution)/shard_map/ppermute | solution.py:48
  33.6 3.7 %collective-permute-done.5.refs_3_ = bf16[4,256,128]{2,1,0:T(8,128)(2,1)S(1)} collective-permute-done((bf16[4,256,128]{2,1,0:T(8,128)(2,1)S(1)}, bf16[4,256,128]{2,1,0:T(8,128)(2,1)S(1)}, u32[]{:S(2)}, u32[]{:S(2)}) %collective-permute-start.5) | collective-permute-done | bytes 262176 | tf_op jit(solution)/shard_map/ppermute | solution.py:48
  37.3 3.5 %collective-permute-start.10 = (bf16[2,256,128]{2,1,0:T(8,128)(2,1)S(1)}, bf16[2,256,128]{2,1,0:T(8,128)(2,1)S(1)}, u32[]{:S(2)}, u32[]{:S(2)}) collective-permute-start(bf16[2,256,128]{2,1,0:T(8,128)(2,1)S(1)} %slice.159), channel_id=1, source_target_pairs={{0,224},{8,232},{16,240},{24,248},{32,0},{40,8},{48,16},{56,24},{6... | collective-permute-start | bytes 393224 | tf_op jit(solution)/shard_map/ppermute | solution.py:48
  40.9 2.3 %forward_near.1 = (f32[18,256,128]{2,1,0:T(8,128)S(1)}, s32[68]{0:T(128)S(1)}) custom-call(s32[25]{0:T(128)S(1)} %get-tuple-element.31.own_any, s32[25]{0:T(128)S(1)} %fusion.6.partner_any, bf16[12,256,256]{2,1,0:T(8,128)(2,1)S(1)} %bitcast.43, bf16[12,256,256]{2,1,0:T(8,128)(2,1)S(1)} %collective-permute-done.2.adj1, ...), custom_call_target="tpu_custom_call" | custom-call | flops 352321536 | bytes 6291456 | tf_op jit(solution)/shard_map/forward_near/pallas_call | solution.py:399
  43.3 2.7 %collective-permute-done.9.far_a = bf16[2,256,128]{2,1,0:T(8,128)(2,1)S(1)} collective-permute-done((bf16[2,256,128]{2,1,0:T(8,128)(2,1)S(1)}, bf16[2,256,128]{2,1,0:T(8,128)(2,1)S(1)}, u32[]{:S(2)}, u32[]{:S(2)}) %collective-permute-start.9) | collective-permute-done | bytes 131104 | tf_op jit(solution)/shard_map/ppermute | solution.py:48
  46.9 2.4 %collective-permute-start.11 = (bf16[2,256,128]{2,1,0:T(8,128)(2,1)S(1)}, bf16[2,256,128]{2,1,0:T(8,128)(2,1)S(1)}, u32[]{:S(2)}, u32[]{:S(2)}) collective-permute-start(bf16[2,256,128]{2,1,0:T(8,128)(2,1)S(1)} %get-tuple-element.39), channel_id=1, source_target_pairs={{0,6},{1,7},{2,4},{3,5},{4,2},{5,3},{6,0},{7,1},{8,14},{9,15},{10,... | collective-permute-start | bytes 393224 | tf_op jit(solution)/shard_map/ppermute | solution.py:39
  49.9 2.0 %collective-permute-start.13 = (bf16[2,256,128]{2,1,0:T(8,128)(2,1)S(1)}, bf16[2,256,128]{2,1,0:T(8,128)(2,1)S(1)}, u32[]{:S(2)}, u32[]{:S(2)}) collective-permute-start(bf16[2,256,128]{2,1,0:T(8,128)(2,1)S(1)} %get-tuple-element.41), channel_id=1, source_target_pairs={{0,5},{1,6},{2,7},{3,4},{4,1},{5,2},{6,3},{7,0},{8,13},{9,14},{10,... | collective-permute-start | bytes 393224 | tf_op jit(solution)/shard_map/ppermute | solution.py:39
  51.9 1.8 %collective-permute-start.14 = (bf16[2,256,128]{2,1,0:T(8,128)(2,1)S(1)}, bf16[2,256,128]{2,1,0:T(8,128)(2,1)S(1)}, u32[]{:S(2)}, u32[]{:S(2)}) collective-permute-start(bf16[2,256,128]{2,1,0:T(8,128)(2,1)S(1)} %get-tuple-element.42), channel_id=1, source_target_pairs={{0,7},{1,4},{2,5},{3,6},{4,3},{5,0},{6,1},{7,2},{8,15},{9,12},{10,... | collective-permute-start | bytes 393224 | tf_op jit(solution)/shard_map/ppermute | solution.py:39
  53.6 2.7 %collective-permute-start.16 = (bf16[2,256,128]{2,1,0:T(8,128)(2,1)S(1)}, bf16[2,256,128]{2,1,0:T(8,128)(2,1)S(1)}, u32[]{:S(2)}, u32[]{:S(2)}) collective-permute-start(bf16[2,256,128]{2,1,0:T(8,128)(2,1)S(1)} %get-tuple-element.44), channel_id=1, source_target_pairs={{0,3},{1,0},{2,1},{3,2},{4,7},{5,4},{6,5},{7,6},{8,11},{9,8},{10,9... | collective-permute-start | bytes 393224 | tf_op jit(solution)/shard_map/ppermute | solution.py:39
  57.5 5.0 %collective-permute-done.15 = bf16[2,256,128]{2,1,0:T(8,128)(2,1)S(1)} collective-permute-done((bf16[2,256,128]{2,1,0:T(8,128)(2,1)S(1)}, bf16[2,256,128]{2,1,0:T(8,128)(2,1)S(1)}, u32[]{:S(2)}, u32[]{:S(2)}) %collective-permute-start.15) | collective-permute-done | bytes 131104 | tf_op jit(solution)/shard_map/ppermute | solution.py:39
  62.6 5.1 %collective-permute-start.18 = (f32[512,128]{1,0:T(8,128)S(1)}, f32[512,128]{1,0:T(8,128)S(1)}, u32[]{:S(2)}, u32[]{:S(2)}) collective-permute-start(f32[512,128]{1,0:T(8,128)S(1)} %bitcast.49), channel_id=1, source_target_pairs={{0,8},{8,0},{16,24},{24,16},{32,40},{40,32},{48,56},{56,48},{64,72... | collective-permute-start | bytes 786440 | tf_op jit(solution)/shard_map/ppermute | solution.py:34
  70.7 1.8 %collective-permute-start.22 = (bf16[640,128]{1,0:T(8,128)(2,1)S(1)}, bf16[640,128]{1,0:T(8,128)(2,1)S(1)}, u32[]{:S(2)}, u32[]{:S(2)}) collective-permute-start(bf16[640,128]{1,0:T(8,128)(2,1)S(1)} %get-tuple-element.47.refs_0_), channel_id=1, source_target_pairs={{0,3},{1,0},{2,1},{3,2},{4,7},{5,4},{6,5},{7,6},{8,11},{9,8},{10,9... | collective-permute-start | bytes 491528 | tf_op jit(solution)/shard_map/ppermute | solution.py:39
  76.1 2.9 %collective-permute-done.22.refs_3_ = bf16[640,128]{1,0:T(8,128)(2,1)S(1)} collective-permute-done((bf16[640,128]{1,0:T(8,128)(2,1)S(1)}, bf16[640,128]{1,0:T(8,128)(2,1)S(1)}, u32[]{:S(2)}, u32[]{:S(2)}) %collective-permute-start.22) | collective-permute-done | bytes 163872 | tf_op jit(solution)/shard_map/ppermute | solution.py:39
  79.0 3.7 %collective-permute-start.26 = (bf16[640,128]{1,0:T(8,128)(2,1)S(1)}, bf16[640,128]{1,0:T(8,128)(2,1)S(1)}, u32[]{:S(2)}, u32[]{:S(2)}) collective-permute-start(bf16[640,128]{1,0:T(8,128)(2,1)S(1)} %pad_maximum_fusion.7), channel_id=1, source_target_pairs={{0,3},{1,0},{2,1},{3,2},{4,7},{5,4},{6,5},{7,6},{8,11},{9,8},{10,9... | collective-permute-start | bytes 491528 | tf_op jit(solution)/shard_map/ppermute | solution.py:39
  82.9 1.9 %collective-permute-done.24.refs_5_ = bf16[640,128]{1,0:T(8,128)(2,1)S(1)} collective-permute-done((bf16[640,128]{1,0:T(8,128)(2,1)S(1)}, bf16[640,128]{1,0:T(8,128)(2,1)S(1)}, u32[]{:S(2)}, u32[]{:S(2)}) %collective-permute-start.24) | collective-permute-done | bytes 163872 | tf_op jit(solution)/shard_map/ppermute | solution.py:39
  85.0 3.3 %collective-permute-done.25.refs_6_ = bf16[640,128]{1,0:T(8,128)(2,1)S(1)} collective-permute-done((bf16[640,128]{1,0:T(8,128)(2,1)S(1)}, bf16[640,128]{1,0:T(8,128)(2,1)S(1)}, u32[]{:S(2)}, u32[]{:S(2)}) %collective-permute-start.25) | collective-permute-done | bytes 163872 | tf_op jit(solution)/shard_map/ppermute | solution.py:39
  89.4 2.7 %collective-permute-start.31 = (bf16[640,128]{1,0:T(8,128)(2,1)S(1)}, bf16[640,128]{1,0:T(8,128)(2,1)S(1)}, u32[]{:S(2)}, u32[]{:S(2)}) collective-permute-start(bf16[640,128]{1,0:T(8,128)(2,1)S(1)} %get-tuple-element.51), channel_id=1, source_target_pairs={{0,224},{8,232},{16,240},{24,248},{32,0},{40,8},{48,16},{56,24},{6... | collective-permute-start | bytes 491528 | tf_op jit(solution)/shard_map/ppermute | solution.py:48
  92.1 2.0 %backward_near.1.parts = bf16[32,256,128]{2,1,0:T(8,128)(2,1)S(1)} custom-call(s32[68]{0:T(128)S(1)} %get-tuple-element.36.lists_any, bf16[12,256,256]{2,1,0:T(8,128)(2,1)S(1)} %bitcast.46, bf16[12,256,256]{2,1,0:T(8,128)(2,1)S(1)} %collective-permute-done.2.adj1, bf16[8,512,128]{2,1,0:T(8,128)(2,1)S(1)} %get-tuple-element.49.back), custom_call_target="tpu_custom_call" | custom-call | flops 352321536 | bytes 6291456 | tf_op jit(solution)/shard_map/backward_near/pallas_call | solution.py:448
  95.2 2.7 %collective-permute-start.32 = (bf16[1152,128]{1,0:T(8,128)(2,1)S(1)}, bf16[1152,128]{1,0:T(8,128)(2,1)S(1)}, u32[]{:S(2)}, u32[]{:S(2)}) collective-permute-start(bf16[1152,128]{1,0:T(8,128)(2,1)S(1)} %pad_maximum_fusion.3), channel_id=1, source_target_pairs={{0,224},{8,232},{16,240},{24,248},{32,0},{40,8},{48,16},{56,24},{6... | collective-permute-start | bytes 884744 | tf_op jit(solution)/shard_map/ppermute | solution.py:48
  97.9 4.2 %collective-permute-done.28.up2 = bf16[1152,128]{1,0:T(8,128)(2,1)S(1)} collective-permute-done((bf16[1152,128]{1,0:T(8,128)(2,1)S(1)}, bf16[1152,128]{1,0:T(8,128)(2,1)S(1)}, u32[]{:S(2)}, u32[]{:S(2)}) %collective-permute-start.28) | collective-permute-done | bytes 294944 | tf_op jit(solution)/shard_map/ppermute | solution.py:48
  102.5 2.8 %collective-permute-start.33 = (bf16[1152,128]{1,0:T(8,128)(2,1)S(1)}, bf16[1152,128]{1,0:T(8,128)(2,1)S(1)}, u32[]{:S(2)}, u32[]{:S(2)}) collective-permute-start(bf16[1152,128]{1,0:T(8,128)(2,1)S(1)} %pad_maximum_fusion.4), channel_id=1, source_target_pairs={{0,224},{8,232},{16,240},{24,248},{32,0},{40,8},{48,16},{56,24},{6... | collective-permute-start | bytes 884744 | tf_op jit(solution)/shard_map/ppermute | solution.py:48
  105.3 5.3 %collective-permute-done.29.up3 = bf16[1152,128]{1,0:T(8,128)(2,1)S(1)} collective-permute-done((bf16[1152,128]{1,0:T(8,128)(2,1)S(1)}, bf16[1152,128]{1,0:T(8,128)(2,1)S(1)}, u32[]{:S(2)}, u32[]{:S(2)}) %collective-permute-start.29) | collective-permute-done | bytes 294944 | tf_op jit(solution)/shard_map/ppermute | solution.py:48
  111.0 3.0 %collective-permute-start.34 = (bf16[1024,128]{1,0:T(8,128)(2,1)S(1)}, bf16[1024,128]{1,0:T(8,128)(2,1)S(1)}, u32[]{:S(2)}, u32[]{:S(2)}) collective-permute-start(bf16[1024,128]{1,0:T(8,128)(2,1)S(1)} %fusion), channel_id=1, source_target_pairs={{0,224},{8,232},{16,240},{24,248},{32,0},{40,8},{48,16},{56,24},{6... | collective-permute-start | bytes 786440 | tf_op jit(solution)/shard_map/ppermute | solution.py:48
  114.0 6.1 %collective-permute-done.34.down4 = bf16[1024,128]{1,0:T(8,128)(2,1)S(1)} collective-permute-done((bf16[1024,128]{1,0:T(8,128)(2,1)S(1)}, bf16[1024,128]{1,0:T(8,128)(2,1)S(1)}, u32[]{:S(2)}, u32[]{:S(2)}) %collective-permute-start.34) | collective-permute-done | bytes 262176 | tf_op jit(solution)/shard_map/ppermute | solution.py:48
  120.7 2.4 %collective-permute-start.35 = (bf16[640,128]{1,0:T(8,128)(2,1)S(1)}, bf16[640,128]{1,0:T(8,128)(2,1)S(1)}, u32[]{:S(2)}, u32[]{:S(2)}) collective-permute-start(bf16[640,128]{1,0:T(8,128)(2,1)S(1)} %get-tuple-element.53.sent), channel_id=1, source_target_pairs={{0,16},{8,24},{16,0},{24,8},{32,48},{40,56},{48,32},{56,40},{64,80... | collective-permute-start | bytes 491528 | tf_op jit(solution)/shard_map/ppermute | solution.py:34
  124.1 2.1 %collective-permute-done.36.w_lo = bf16[128,128]{1,0:T(8,128)(2,1)S(1)} collective-permute-done((bf16[128,128]{1,0:T(8,128)(2,1)S(1)}, bf16[128,128]{1,0:T(8,128)(2,1)S(1)}, u32[]{:S(2)}, u32[]{:S(2)}) %collective-permute-start.36) | collective-permute-done | bytes 32800 | tf_op jit(solution)/shard_map/ppermute | solution.py:559
  127.5 9.8 %collective-permute-start.38 = (bf16[768,128]{1,0:T(8,128)(2,1)S(1)}, bf16[768,128]{1,0:T(8,128)(2,1)S(1)}, u32[]{:S(2)}, u32[]{:S(2)}) collective-permute-start(bf16[768,128]{1,0:T(8,128)(2,1)S(1)} %get-tuple-element.55), channel_id=1, source_target_pairs={{0,8},{8,0},{16,24},{24,16},{32,40},{40,32},{48,56},{56,48},{64,72... | collective-permute-start | bytes 589832 | tf_op jit(solution)/shard_map/ppermute | solution.py:34
  (103 shorter events, 24.2 us)
Async XLA Ops:
  0.6 8.7 %collective-permute-start = (bf16[256,256]{1,0:T(8,128)(2,1)}, bf16[256,256]{1,0:T(8,128)(2,1)S(1)}, u32[]{:S(2)}, u32[]{:S(2)}) collective-permute-start(bf16[256,256]{1,0:T(8,128)(2,1)} %bitcast.51), channel_id=1, source_target_pairs={{0,16},{8,24},{16,0},{24,8},{32,48},{40,56},{48,32},{56,40},{64,80... | collective-permute-start | bytes 393224 | tf_op jit(solution)/shard_map/ppermute | solution.py:34
  4.3 36.6 %collective-permute-start.2 = (bf16[12,256,256]{2,1,0:T(8,128)(2,1)}, bf16[12,256,256]{2,1,0:T(8,128)(2,1)S(1)}, u32[]{:S(2)}, u32[]{:S(2)}) collective-permute-start(bf16[12,256,256]{2,1,0:T(8,128)(2,1)} %bitcast.42), channel_id=1, source_target_pairs={{0,8},{8,0},{16,24},{24,16},{32,40},{40,32},{48,56},{56,48},{64,72... | collective-permute-start | bytes 4718600 | tf_op jit(solution)/shard_map/ppermute | solution.py:34
  11.8 10.3 %collective-permute-start.3 = (bf16[4,256,128]{2,1,0:T(8,128)(2,1)S(1)}, bf16[4,256,128]{2,1,0:T(8,128)(2,1)S(1)}, u32[]{:S(2)}, u32[]{:S(2)}) collective-permute-start(bf16[4,256,128]{2,1,0:T(8,128)(2,1)S(1)} %pad_maximum_fusion.5.refs_0_), channel_id=1, source_target_pairs={{0,224},{8,232},{16,240},{24,248},{32,0},{40,8},{48,16},{56,24},{6... | collective-permute-start | bytes 786440 | tf_op jit(solution)/shard_map/ppermute | solution.py:48
  16.5 9.0 %collective-permute-start.6 = (bf16[4,256,128]{2,1,0:T(8,128)(2,1)S(1)}, bf16[4,256,128]{2,1,0:T(8,128)(2,1)S(1)}, u32[]{:S(2)}, u32[]{:S(2)}) collective-permute-start(bf16[4,256,128]{2,1,0:T(8,128)(2,1)S(1)} %pad_maximum_fusion.5.refs_0_), channel_id=1, source_target_pairs={{0,32},{8,40},{16,48},{24,56},{32,64},{40,72},{48,80},{56,88},{64,... | collective-permute-start | bytes 786440 | tf_op jit(solution)/shard_map/ppermute | solution.py:48
  22.1 8.1 %collective-permute-start.4 = (bf16[4,256,128]{2,1,0:T(8,128)(2,1)S(1)}, bf16[4,256,128]{2,1,0:T(8,128)(2,1)S(1)}, u32[]{:S(2)}, u32[]{:S(2)}) collective-permute-start(bf16[4,256,128]{2,1,0:T(8,128)(2,1)S(1)} %collective-permute-done.3.refs_1_), channel_id=1, source_target_pairs={{0,224},{8,232},{16,240},{24,248},{32,0},{40,8},{48,16},{56,24},{6... | collective-permute-start | bytes 786440 | tf_op jit(solution)/shard_map/ppermute | solution.py:48
  25.5 8.1 %collective-permute-start.7 = (bf16[4,256,128]{2,1,0:T(8,128)(2,1)S(1)}, bf16[4,256,128]{2,1,0:T(8,128)(2,1)S(1)}, u32[]{:S(2)}, u32[]{:S(2)}) collective-permute-start(bf16[4,256,128]{2,1,0:T(8,128)(2,1)S(1)} %collective-permute-done.6.refs_6_), channel_id=1, source_target_pairs={{0,32},{8,40},{16,48},{24,56},{32,64},{40,72},{48,80},{56,88},{64,... | collective-permute-start | bytes 786440 | tf_op jit(solution)/shard_map/ppermute | solution.py:48
  30.1 7.1 %collective-permute-start.5 = (bf16[4,256,128]{2,1,0:T(8,128)(2,1)S(1)}, bf16[4,256,128]{2,1,0:T(8,128)(2,1)S(1)}, u32[]{:S(2)}, u32[]{:S(2)}) collective-permute-start(bf16[4,256,128]{2,1,0:T(8,128)(2,1)S(1)} %collective-permute-done.4.refs_2_), channel_id=1, source_target_pairs={{0,224},{8,232},{16,240},{24,248},{32,0},{40,8},{48,16},{56,24},{6... | collective-permute-start | bytes 786440 | tf_op jit(solution)/shard_map/ppermute | solution.py:48
  33.6 7.2 %collective-permute-start.8 = (bf16[4,256,128]{2,1,0:T(8,128)(2,1)S(1)}, bf16[4,256,128]{2,1,0:T(8,128)(2,1)S(1)}, u32[]{:S(2)}, u32[]{:S(2)}) collective-permute-start(bf16[4,256,128]{2,1,0:T(8,128)(2,1)S(1)} %collective-permute-done.7.refs_5_), channel_id=1, source_target_pairs={{0,32},{8,40},{16,48},{24,56},{32,64},{40,72},{48,80},{56,88},{64,... | collective-permute-start | bytes 786440 | tf_op jit(solution)/shard_map/ppermute | solution.py:48
  37.3 6.0 %collective-permute-start.10 = (bf16[2,256,128]{2,1,0:T(8,128)(2,1)S(1)}, bf16[2,256,128]{2,1,0:T(8,128)(2,1)S(1)}, u32[]{:S(2)}, u32[]{:S(2)}) collective-permute-start(bf16[2,256,128]{2,1,0:T(8,128)(2,1)S(1)} %slice.159), channel_id=1, source_target_pairs={{0,224},{8,232},{16,240},{24,248},{32,0},{40,8},{48,16},{56,24},{6... | collective-permute-start | bytes 393224 | tf_op jit(solution)/shard_map/ppermute | solution.py:48
  46.9 6.7 %collective-permute-start.11 = (bf16[2,256,128]{2,1,0:T(8,128)(2,1)S(1)}, bf16[2,256,128]{2,1,0:T(8,128)(2,1)S(1)}, u32[]{:S(2)}, u32[]{:S(2)}) collective-permute-start(bf16[2,256,128]{2,1,0:T(8,128)(2,1)S(1)} %get-tuple-element.39), channel_id=1, source_target_pairs={{0,6},{1,7},{2,4},{3,5},{4,2},{5,3},{6,0},{7,1},{8,14},{9,15},{10,... | collective-permute-start | bytes 393224 | tf_op jit(solution)/shard_map/ppermute | solution.py:39
  49.3 7.0 %collective-permute-start.12 = (bf16[2,256,128]{2,1,0:T(8,128)(2,1)S(1)}, bf16[2,256,128]{2,1,0:T(8,128)(2,1)S(1)}, u32[]{:S(2)}, u32[]{:S(2)}) collective-permute-start(bf16[2,256,128]{2,1,0:T(8,128)(2,1)S(1)} %get-tuple-element.40), channel_id=1, source_target_pairs={{0,2},{1,3},{2,0},{3,1},{4,6},{5,7},{6,4},{7,5},{8,10},{9,11},{10,... | collective-permute-start | bytes 393224 | tf_op jit(solution)/shard_map/ppermute | solution.py:39
  49.9 7.6 %collective-permute-start.13 = (bf16[2,256,128]{2,1,0:T(8,128)(2,1)S(1)}, bf16[2,256,128]{2,1,0:T(8,128)(2,1)S(1)}, u32[]{:S(2)}, u32[]{:S(2)}) collective-permute-start(bf16[2,256,128]{2,1,0:T(8,128)(2,1)S(1)} %get-tuple-element.41), channel_id=1, source_target_pairs={{0,5},{1,6},{2,7},{3,4},{4,1},{5,2},{6,3},{7,0},{8,13},{9,14},{10,... | collective-permute-start | bytes 393224 | tf_op jit(solution)/shard_map/ppermute | solution.py:39
  51.9 5.6 %collective-permute-start.14 = (bf16[2,256,128]{2,1,0:T(8,128)(2,1)S(1)}, bf16[2,256,128]{2,1,0:T(8,128)(2,1)S(1)}, u32[]{:S(2)}, u32[]{:S(2)}) collective-permute-start(bf16[2,256,128]{2,1,0:T(8,128)(2,1)S(1)} %get-tuple-element.42), channel_id=1, source_target_pairs={{0,7},{1,4},{2,5},{3,6},{4,3},{5,0},{6,1},{7,2},{8,15},{9,12},{10,... | collective-permute-start | bytes 393224 | tf_op jit(solution)/shard_map/ppermute | solution.py:39
  53.6 8.8 %collective-permute-start.15 = (bf16[2,256,128]{2,1,0:T(8,128)(2,1)S(1)}, bf16[2,256,128]{2,1,0:T(8,128)(2,1)S(1)}, u32[]{:S(2)}, u32[]{:S(2)}) collective-permute-start(bf16[2,256,128]{2,1,0:T(8,128)(2,1)S(1)} %get-tuple-element.43), channel_id=1, source_target_pairs={{0,1},{1,2},{2,3},{3,0},{4,5},{5,6},{6,7},{7,4},{8,9},{9,10},{10,1... | collective-permute-start | bytes 393224 | tf_op jit(solution)/shard_map/ppermute | solution.py:39
  53.6 8.8 %collective-permute-start.16 = (bf16[2,256,128]{2,1,0:T(8,128)(2,1)S(1)}, bf16[2,256,128]{2,1,0:T(8,128)(2,1)S(1)}, u32[]{:S(2)}, u32[]{:S(2)}) collective-permute-start(bf16[2,256,128]{2,1,0:T(8,128)(2,1)S(1)} %get-tuple-element.44), channel_id=1, source_target_pairs={{0,3},{1,0},{2,1},{3,2},{4,7},{5,4},{6,5},{7,6},{8,11},{9,8},{10,9... | collective-permute-start | bytes 393224 | tf_op jit(solution)/shard_map/ppermute | solution.py:39
  56.3 6.2 %collective-permute-start.17 = (bf16[2,256,128]{2,1,0:T(8,128)(2,1)S(1)}, bf16[2,256,128]{2,1,0:T(8,128)(2,1)S(1)}, u32[]{:S(2)}, u32[]{:S(2)}) collective-permute-start(bf16[2,256,128]{2,1,0:T(8,128)(2,1)S(1)} %get-tuple-element.45), channel_id=1, source_target_pairs={{0,4},{1,5},{2,6},{3,7},{4,0},{5,1},{6,2},{7,3},{8,12},{9,13},{10,... | collective-permute-start | bytes 393224 | tf_op jit(solution)/shard_map/ppermute | solution.py:39
  62.6 6.5 %collective-permute-start.18 = (f32[512,128]{1,0:T(8,128)S(1)}, f32[512,128]{1,0:T(8,128)S(1)}, u32[]{:S(2)}, u32[]{:S(2)}) collective-permute-start(f32[512,128]{1,0:T(8,128)S(1)} %bitcast.49), channel_id=1, source_target_pairs={{0,8},{8,0},{16,24},{24,16},{32,40},{40,32},{48,56},{56,48},{64,72... | collective-permute-start | bytes 786440 | tf_op jit(solution)/shard_map/ppermute | solution.py:34
  70.7 8.3 %collective-permute-start.22 = (bf16[640,128]{1,0:T(8,128)(2,1)S(1)}, bf16[640,128]{1,0:T(8,128)(2,1)S(1)}, u32[]{:S(2)}, u32[]{:S(2)}) collective-permute-start(bf16[640,128]{1,0:T(8,128)(2,1)S(1)} %get-tuple-element.47.refs_0_), channel_id=1, source_target_pairs={{0,3},{1,0},{2,1},{3,2},{4,7},{5,4},{6,5},{7,6},{8,11},{9,8},{10,9... | collective-permute-start | bytes 491528 | tf_op jit(solution)/shard_map/ppermute | solution.py:39
  72.5 6.5 %collective-permute-start.23 = (bf16[640,128]{1,0:T(8,128)(2,1)S(1)}, bf16[640,128]{1,0:T(8,128)(2,1)S(1)}, u32[]{:S(2)}, u32[]{:S(2)}) collective-permute-start(bf16[640,128]{1,0:T(8,128)(2,1)S(1)} %get-tuple-element.48), channel_id=1, source_target_pairs={{0,7},{1,4},{2,5},{3,6},{4,3},{5,0},{6,1},{7,2},{8,15},{9,12},{10,... | collective-permute-start | bytes 491528 | tf_op jit(solution)/shard_map/ppermute | solution.py:39
  73.4 9.3 %collective-permute-start.20 = (bf16[640,128]{1,0:T(8,128)(2,1)S(1)}, bf16[640,128]{1,0:T(8,128)(2,1)S(1)}, u32[]{:S(2)}, u32[]{:S(2)}) collective-permute-start(bf16[640,128]{1,0:T(8,128)(2,1)S(1)} %get-tuple-element.47.refs_0_), channel_id=1, source_target_pairs={{0,1},{1,2},{2,3},{3,0},{4,5},{5,6},{6,7},{7,4},{8,9},{9,10},{10,1... | collective-permute-start | bytes 491528 | tf_op jit(solution)/shard_map/ppermute | solution.py:39
  74.9 7.9 %collective-permute-start.21 = (bf16[640,128]{1,0:T(8,128)(2,1)S(1)}, bf16[640,128]{1,0:T(8,128)(2,1)S(1)}, u32[]{:S(2)}, u32[]{:S(2)}) collective-permute-start(bf16[640,128]{1,0:T(8,128)(2,1)S(1)} %get-tuple-element.48), channel_id=1, source_target_pairs={{0,5},{1,6},{2,7},{3,4},{4,1},{5,2},{6,3},{7,0},{8,13},{9,14},{10,... | collective-permute-start | bytes 491528 | tf_op jit(solution)/shard_map/ppermute | solution.py:39
  74.9 9.9 %collective-permute-start.24 = (bf16[640,128]{1,0:T(8,128)(2,1)S(1)}, bf16[640,128]{1,0:T(8,128)(2,1)S(1)}, u32[]{:S(2)}, u32[]{:S(2)}) collective-permute-start(bf16[640,128]{1,0:T(8,128)(2,1)S(1)} %get-tuple-element.48), channel_id=1, source_target_pairs={{0,4},{1,5},{2,6},{3,7},{4,0},{5,1},{6,2},{7,3},{8,12},{9,13},{10,... | collective-permute-start | bytes 491528 | tf_op jit(solution)/shard_map/ppermute | solution.py:39
  79.0 6.0 %collective-permute-start.26 = (bf16[640,128]{1,0:T(8,128)(2,1)S(1)}, bf16[640,128]{1,0:T(8,128)(2,1)S(1)}, u32[]{:S(2)}, u32[]{:S(2)}) collective-permute-start(bf16[640,128]{1,0:T(8,128)(2,1)S(1)} %pad_maximum_fusion.7), channel_id=1, source_target_pairs={{0,3},{1,0},{2,1},{3,2},{4,7},{5,4},{6,5},{7,6},{8,11},{9,8},{10,9... | collective-permute-start | bytes 491528 | tf_op jit(solution)/shard_map/ppermute | solution.py:39
  89.3 5.5 %collective-permute-start.27 = (bf16[640,128]{1,0:T(8,128)(2,1)S(1)}, bf16[640,128]{1,0:T(8,128)(2,1)S(1)}, u32[]{:S(2)}, u32[]{:S(2)}) collective-permute-start(bf16[640,128]{1,0:T(8,128)(2,1)S(1)} %get-tuple-element.50.own), channel_id=1, source_target_pairs={{0,32},{8,40},{16,48},{24,56},{32,64},{40,72},{48,80},{56,88},{64,... | collective-permute-start | bytes 491528 | tf_op jit(solution)/shard_map/ppermute | solution.py:48
  94.9 7.2 %collective-permute-start.28 = (bf16[1152,128]{1,0:T(8,128)(2,1)S(1)}, bf16[1152,128]{1,0:T(8,128)(2,1)S(1)}, u32[]{:S(2)}, u32[]{:S(2)}) collective-permute-start(bf16[1152,128]{1,0:T(8,128)(2,1)S(1)} %pad_maximum_fusion), channel_id=1, source_target_pairs={{0,32},{8,40},{16,48},{24,56},{32,64},{40,72},{48,80},{56,88},{64,... | collective-permute-start | bytes 884744 | tf_op jit(solution)/shard_map/ppermute | solution.py:48
  95.2 7.2 %collective-permute-start.32 = (bf16[1152,128]{1,0:T(8,128)(2,1)S(1)}, bf16[1152,128]{1,0:T(8,128)(2,1)S(1)}, u32[]{:S(2)}, u32[]{:S(2)}) collective-permute-start(bf16[1152,128]{1,0:T(8,128)(2,1)S(1)} %pad_maximum_fusion.3), channel_id=1, source_target_pairs={{0,224},{8,232},{16,240},{24,248},{32,0},{40,8},{48,16},{56,24},{6... | collective-permute-start | bytes 884744 | tf_op jit(solution)/shard_map/ppermute | solution.py:48
  102.3 8.4 %collective-permute-start.29 = (bf16[1152,128]{1,0:T(8,128)(2,1)S(1)}, bf16[1152,128]{1,0:T(8,128)(2,1)S(1)}, u32[]{:S(2)}, u32[]{:S(2)}) collective-permute-start(bf16[1152,128]{1,0:T(8,128)(2,1)S(1)} %pad_maximum_fusion.1), channel_id=1, source_target_pairs={{0,32},{8,40},{16,48},{24,56},{32,64},{40,72},{48,80},{56,88},{64,... | collective-permute-start | bytes 884744 | tf_op jit(solution)/shard_map/ppermute | solution.py:48
  102.5 8.3 %collective-permute-start.33 = (bf16[1152,128]{1,0:T(8,128)(2,1)S(1)}, bf16[1152,128]{1,0:T(8,128)(2,1)S(1)}, u32[]{:S(2)}, u32[]{:S(2)}) collective-permute-start(bf16[1152,128]{1,0:T(8,128)(2,1)S(1)} %pad_maximum_fusion.4), channel_id=1, source_target_pairs={{0,224},{8,232},{16,240},{24,248},{32,0},{40,8},{48,16},{56,24},{6... | collective-permute-start | bytes 884744 | tf_op jit(solution)/shard_map/ppermute | solution.py:48
  110.8 9.8 %collective-permute-start.30 = (bf16[1152,128]{1,0:T(8,128)(2,1)S(1)}, bf16[1152,128]{1,0:T(8,128)(2,1)S(1)}, u32[]{:S(2)}, u32[]{:S(2)}) collective-permute-start(bf16[1152,128]{1,0:T(8,128)(2,1)S(1)} %pad_maximum_fusion.2), channel_id=1, source_target_pairs={{0,32},{8,40},{16,48},{24,56},{32,64},{40,72},{48,80},{56,88},{64,... | collective-permute-start | bytes 884744 | tf_op jit(solution)/shard_map/ppermute | solution.py:48
  111.0 9.1 %collective-permute-start.34 = (bf16[1024,128]{1,0:T(8,128)(2,1)S(1)}, bf16[1024,128]{1,0:T(8,128)(2,1)S(1)}, u32[]{:S(2)}, u32[]{:S(2)}) collective-permute-start(bf16[1024,128]{1,0:T(8,128)(2,1)S(1)} %fusion), channel_id=1, source_target_pairs={{0,224},{8,232},{16,240},{24,248},{32,0},{40,8},{48,16},{56,24},{6... | collective-permute-start | bytes 786440 | tf_op jit(solution)/shard_map/ppermute | solution.py:48
  120.7 6.7 %collective-permute-start.35 = (bf16[640,128]{1,0:T(8,128)(2,1)S(1)}, bf16[640,128]{1,0:T(8,128)(2,1)S(1)}, u32[]{:S(2)}, u32[]{:S(2)}) collective-permute-start(bf16[640,128]{1,0:T(8,128)(2,1)S(1)} %get-tuple-element.53.sent), channel_id=1, source_target_pairs={{0,16},{8,24},{16,0},{24,8},{32,48},{40,56},{48,32},{56,40},{64,80... | collective-permute-start | bytes 491528 | tf_op jit(solution)/shard_map/ppermute | solution.py:34
  127.5 10.8 %collective-permute-start.38 = (bf16[768,128]{1,0:T(8,128)(2,1)S(1)}, bf16[768,128]{1,0:T(8,128)(2,1)S(1)}, u32[]{:S(2)}, u32[]{:S(2)}) collective-permute-start(bf16[768,128]{1,0:T(8,128)(2,1)S(1)} %get-tuple-element.55), channel_id=1, source_target_pairs={{0,8},{8,0},{16,24},{24,16},{32,40},{40,32},{48,56},{56,48},{64,72... | collective-permute-start | bytes 589832 | tf_op jit(solution)/shard_map/ppermute | solution.py:34
  (13 other events, 114.6 us)

commit v12 on v11

--- a/solution.py
+++ b/solution.py
@@ -182,7 +182,8 @@
     slot_products(lists, far, adj_refs, product, add_to)
 
 
-def backward_far_kernel(lists_any, adj0, adj1, *refs):
+def backward_far_kernel(lists_any, in_step_any, adj0, adj1, *refs):
+    del in_step_any
     received, (up, down, back, acc, lists, sem, pieces) = refs[:NCOL], refs[NCOL:]
     copy = pltpu.make_async_copy(lists_any, lists, sem)
     copy.start()
@@ -429,19 +430,19 @@
     )(lists, adj0, adj1, near, far_a, far_b)
 
 
-def backward_far(lists, adj0, adj1, received):
+def backward_far(lists, in_step, adj0, adj1, received):
     message = shape(2 * TILE + W_ROWS, HALF)
     return local(
         backward_far_kernel,
         (message, message, shape(NCOL, 2 * TILE, HALF)),
-        11,
+        12,
         "backward_far",
-        any_in=1,
+        any_in=2,
         scratch=[pltpu.VMEM((QUAD, TILE, HALF), jnp.float32)]
         + LIST_SCRATCH
         + [pltpu.VMEM((NCOL, W_ROWS, HALF), jnp.bfloat16)],
         cost=cost(3, 2),
-    )(lists, adj0, adj1, *received)
+    )(lists, in_step, adj0, adj1, *received)
 
 
 def backward_near(lists, adj0, adj1, back):
@@ -540,7 +541,8 @@
     received += [forward(received[1], received[2], 0), forward(received[3], received[4], 1)]
 
     half, size = 2 * TILE, QUAD * TILE
-    own, own_down, back = backward_far(lists, adj0, adj1, received)
+    in_step = quad_permute(received[4][:16], 1)
+    own, own_down, back = backward_far(lists, in_step, adj0, adj1, received)
     blocks = backward_near(lists, adj0, adj1, back)
     parts = blocks.reshape(NZ, size, HALF)
     up1, down1 = z_shift(own, 1), z_shift(own_down, -1)

time: 139 us -> 139 us (level)
  starting transfers between devices: 70.7 us -> 73.1 us
  Pallas kernels: 10.2 us -> 8.79 us
    ppermute x14, waiting for transfers between devices: 13.3 us -> 10.7 us  [col_move(): return lax.ppermute(x, 'col', pairs)]
    ppermute x1, starting transfers between devices: 0.01 us -> 2.23 us  [per_device(): w_lo = lax.ppermute(w_send, 'col', [(c, c ^ 4) for c in range(NCOL)])]
    ppermute x7 -> x8, waiting for transfers between devices: 3.3 us -> 4.12 us  [quad_permute(): return lax.ppermute(x, 'row', row_pairs(lambda z, q: (z, q ^ flip)))]
    ppermute x7 -> x8, starting transfers between devices: 23.5 us -> 23.9 us  [quad_permute(): return lax.ppermute(x, 'row', row_pairs(lambda z, q: (z, q ^ flip)))]
  transfers between devices with their start and end apart: 39 -> 40, of which waited for: 19 -> 19; matrix products, arithmetic and copies ran while one was open for 1% -> 1% of each run, Pallas kernels for 4% -> 4%
where the time goes in v12:
time: 139 us
  starting transfers between devices  73.1 us (53%)
  waiting for transfers between devices  52.2 us (38%)
  Pallas kernels  8.79 us (6%)
  local copies, waits for them, and re-layouts  2.43 us (2%)
  between operations  1.72 us (1%)
    ppermute x16, waiting for transfers between devices, z_shift(): return lax.ppermute(x, 'row', row_pairs(lambda z, q: (z + step, q)))  34.1 us
    ppermute x16, starting transfers between devices, z_shift(): return lax.ppermute(x, 'row', row_pairs(lambda z, q: (z + step, q)))  26.7 us
    ppermute x8, starting transfers between devices, quad_permute(): return lax.ppermute(x, 'row', row_pairs(lambda z, q: (z, q ^ flip)))  23.9 us
    ppermute x14, starting transfers between devices, col_move(): return lax.ppermute(x, 'col', pairs)  19.3 us
    ppermute x14, waiting for transfers between devices, col_move(): return lax.ppermute(x, 'col', pairs)  10.7 us
    ppermute x8, waiting for transfers between devices, quad_permute(): return lax.ppermute(x, 'row', row_pairs(lambda z, q: (z, q ^ flip)))  4.12 us
  transfers between devices with their start and end apart: 40, of which 19 were waited for; matrix products, arithmetic and copies ran while one was open for 1% of the time, Pallas kernels for 4%

profile of v12, /device:TPU:1, one launch (start us, length us, event | category | flops | bytes accessed | tf_op | source)
XLA Modules:
  0.0 139.0 jit_solution(2518971385183481057)
XLA Ops:
  0.6 3.7 %collective-permute-start = (bf16[256,256]{1,0:T(8,128)(2,1)}, bf16[256,256]{1,0:T(8,128)(2,1)S(1)}, u32[]{:S(2)}, u32[]{:S(2)}) collective-permute-start(bf16[256,256]{1,0:T(8,128)(2,1)} %bitcast.51), channel_id=1, source_target_pairs={{0,16},{8,24},{16,0},{24,8},{32,48},{40,56},{48,32},{56,40},{64,80... | collective-permute-start | bytes 393224 | tf_op jit(solution)/shard_map/ppermute | solution.py:34
  11.8 4.7 %collective-permute-start.3 = (bf16[4,256,128]{2,1,0:T(8,128)(2,1)S(1)}, bf16[4,256,128]{2,1,0:T(8,128)(2,1)S(1)}, u32[]{:S(2)}, u32[]{:S(2)}) collective-permute-start(bf16[4,256,128]{2,1,0:T(8,128)(2,1)S(1)} %pad_maximum_fusion.5.refs_0_), channel_id=1, source_target_pairs={{0,224},{8,232},{16,240},{24,248},{32,0},{40,8},{48,16},{56,24},{6... | collective-permute-start | bytes 786440 | tf_op jit(solution)/shard_map/ppermute | solution.py:48
  16.5 5.6 %collective-permute-done.3.refs_1_ = bf16[4,256,128]{2,1,0:T(8,128)(2,1)S(1)} collective-permute-done((bf16[4,256,128]{2,1,0:T(8,128)(2,1)S(1)}, bf16[4,256,128]{2,1,0:T(8,128)(2,1)S(1)}, u32[]{:S(2)}, u32[]{:S(2)}) %collective-permute-start.3) | collective-permute-done | bytes 262176 | tf_op jit(solution)/shard_map/ppermute | solution.py:48
  22.1 3.4 %collective-permute-start.4 = (bf16[4,256,128]{2,1,0:T(8,128)(2,1)S(1)}, bf16[4,256,128]{2,1,0:T(8,128)(2,1)S(1)}, u32[]{:S(2)}, u32[]{:S(2)}) collective-permute-start(bf16[4,256,128]{2,1,0:T(8,128)(2,1)S(1)} %collective-permute-done.3.refs_1_), channel_id=1, source_target_pairs={{0,224},{8,232},{16,240},{24,248},{32,0},{40,8},{48,16},{56,24},{6... | collective-permute-start | bytes 786440 | tf_op jit(solution)/shard_map/ppermute | solution.py:48
  25.5 4.6 %collective-permute-done.4.refs_2_ = bf16[4,256,128]{2,1,0:T(8,128)(2,1)S(1)} collective-permute-done((bf16[4,256,128]{2,1,0:T(8,128)(2,1)S(1)}, bf16[4,256,128]{2,1,0:T(8,128)(2,1)S(1)}, u32[]{:S(2)}, u32[]{:S(2)}) %collective-permute-start.4) | collective-permute-done | bytes 262176 | tf_op jit(solution)/shard_map/ppermute | solution.py:48
  30.1 3.4 %collective-permute-start.5 = (bf16[4,256,128]{2,1,0:T(8,128)(2,1)S(1)}, bf16[4,256,128]{2,1,0:T(8,128)(2,1)S(1)}, u32[]{:S(2)}, u32[]{:S(2)}) collective-permute-start(bf16[4,256,128]{2,1,0:T(8,128)(2,1)S(1)} %collective-permute-done.4.refs_2_), channel_id=1, source_target_pairs={{0,224},{8,232},{16,240},{24,248},{32,0},{40,8},{48,16},{56,24},{6... | collective-permute-start | bytes 786440 | tf_op jit(solution)/shard_map/ppermute | solution.py:48
  33.6 3.7 %collective-permute-done.5.refs_3_ = bf16[4,256,128]{2,1,0:T(8,128)(2,1)S(1)} collective-permute-done((bf16[4,256,128]{2,1,0:T(8,128)(2,1)S(1)}, bf16[4,256,128]{2,1,0:T(8,128)(2,1)S(1)}, u32[]{:S(2)}, u32[]{:S(2)}) %collective-permute-start.5) | collective-permute-done | bytes 262176 | tf_op jit(solution)/shard_map/ppermute | solution.py:48
  37.3 3.5 %collective-permute-start.10 = (bf16[2,256,128]{2,1,0:T(8,128)(2,1)S(1)}, bf16[2,256,128]{2,1,0:T(8,128)(2,1)S(1)}, u32[]{:S(2)}, u32[]{:S(2)}) collective-permute-start(bf16[2,256,128]{2,1,0:T(8,128)(2,1)S(1)} %slice.163), channel_id=1, source_target_pairs={{0,224},{8,232},{16,240},{24,248},{32,0},{40,8},{48,16},{56,24},{6... | collective-permute-start | bytes 393224 | tf_op jit(solution)/shard_map/ppermute | solution.py:48
  40.9 2.0 %forward_near.1 = (f32[18,256,128]{2,1,0:T(8,128)S(1)}, s32[68]{0:T(128)S(1)}) custom-call(s32[25]{0:T(128)S(1)} %get-tuple-element.31.own_any, s32[25]{0:T(128)S(1)} %fusion.6.partner_any, bf16[12,256,256]{2,1,0:T(8,128)(2,1)S(1)} %bitcast.43, bf16[12,256,256]{2,1,0:T(8,128)(2,1)S(1)} %collective-permute-done.2.adj1, ...), custom_call_target="tpu_custom_call" | custom-call | flops 352321536 | bytes 6291456 | tf_op jit(solution)/shard_map/forward_near/pallas_call | solution.py:400
  43.0 3.0 %collective-permute-done.9.far_a = bf16[2,256,128]{2,1,0:T(8,128)(2,1)S(1)} collective-permute-done((bf16[2,256,128]{2,1,0:T(8,128)(2,1)S(1)}, bf16[2,256,128]{2,1,0:T(8,128)(2,1)S(1)}, u32[]{:S(2)}, u32[]{:S(2)}) %collective-permute-start.9) | collective-permute-done | bytes 131104 | tf_op jit(solution)/shard_map/ppermute | solution.py:48
  46.6 2.9 %collective-permute-start.11 = (bf16[2,256,128]{2,1,0:T(8,128)(2,1)S(1)}, bf16[2,256,128]{2,1,0:T(8,128)(2,1)S(1)}, u32[]{:S(2)}, u32[]{:S(2)}) collective-permute-start(bf16[2,256,128]{2,1,0:T(8,128)(2,1)S(1)} %get-tuple-element.39), channel_id=1, source_target_pairs={{0,6},{1,7},{2,4},{3,5},{4,2},{5,3},{6,0},{7,1},{8,14},{9,15},{10,... | collective-permute-start | bytes 393224 | tf_op jit(solution)/shard_map/ppermute | solution.py:39
  49.9 2.2 %collective-permute-start.13 = (bf16[2,256,128]{2,1,0:T(8,128)(2,1)S(1)}, bf16[2,256,128]{2,1,0:T(8,128)(2,1)S(1)}, u32[]{:S(2)}, u32[]{:S(2)}) collective-permute-start(bf16[2,256,128]{2,1,0:T(8,128)(2,1)S(1)} %get-tuple-element.41), channel_id=1, source_target_pairs={{0,5},{1,6},{2,7},{3,4},{4,1},{5,2},{6,3},{7,0},{8,13},{9,14},{10,... | collective-permute-start | bytes 393224 | tf_op jit(solution)/shard_map/ppermute | solution.py:39
  52.0 1.8 %collective-permute-start.14 = (bf16[2,256,128]{2,1,0:T(8,128)(2,1)S(1)}, bf16[2,256,128]{2,1,0:T(8,128)(2,1)S(1)}, u32[]{:S(2)}, u32[]{:S(2)}) collective-permute-start(bf16[2,256,128]{2,1,0:T(8,128)(2,1)S(1)} %get-tuple-element.42), channel_id=1, source_target_pairs={{0,7},{1,4},{2,5},{3,6},{4,3},{5,0},{6,1},{7,2},{8,15},{9,12},{10,... | collective-permute-start | bytes 393224 | tf_op jit(solution)/shard_map/ppermute | solution.py:39
  53.8 2.7 %collective-permute-start.16 = (bf16[2,256,128]{2,1,0:T(8,128)(2,1)S(1)}, bf16[2,256,128]{2,1,0:T(8,128)(2,1)S(1)}, u32[]{:S(2)}, u32[]{:S(2)}) collective-permute-start(bf16[2,256,128]{2,1,0:T(8,128)(2,1)S(1)} %get-tuple-element.44), channel_id=1, source_target_pairs={{0,3},{1,0},{2,1},{3,2},{4,7},{5,4},{6,5},{7,6},{8,11},{9,8},{10,9... | collective-permute-start | bytes 393224 | tf_op jit(solution)/shard_map/ppermute | solution.py:39
  57.4 5.1 %collective-permute-done.15 = bf16[2,256,128]{2,1,0:T(8,128)(2,1)S(1)} collective-permute-done((bf16[2,256,128]{2,1,0:T(8,128)(2,1)S(1)}, bf16[2,256,128]{2,1,0:T(8,128)(2,1)S(1)}, u32[]{:S(2)}, u32[]{:S(2)}) %collective-permute-start.15) | collective-permute-done | bytes 131104 | tf_op jit(solution)/shard_map/ppermute | solution.py:39
  62.6 5.1 %collective-permute-start.18 = (f32[512,128]{1,0:T(8,128)S(1)}, f32[512,128]{1,0:T(8,128)S(1)}, u32[]{:S(2)}, u32[]{:S(2)}) collective-permute-start(f32[512,128]{1,0:T(8,128)S(1)} %bitcast.49), channel_id=1, source_target_pairs={{0,8},{8,0},{16,24},{24,16},{32,40},{40,32},{48,56},{56,48},{64,72... | collective-permute-start | bytes 786440 | tf_op jit(solution)/shard_map/ppermute | solution.py:34
  70.6 2.0 %collective-permute-start.24 = (bf16[640,128]{1,0:T(8,128)(2,1)S(1)}, bf16[640,128]{1,0:T(8,128)(2,1)S(1)}, u32[]{:S(2)}, u32[]{:S(2)}) collective-permute-start(bf16[640,128]{1,0:T(8,128)(2,1)S(1)} %get-tuple-element.48.refs_0_), channel_id=1, source_target_pairs={{0,3},{1,0},{2,1},{3,2},{4,7},{5,4},{6,5},{7,6},{8,11},{9,8},{10,9... | collective-permute-start | bytes 491528 | tf_op jit(solution)/shard_map/ppermute | solution.py:39
  76.1 3.5 %collective-permute-done.24.refs_3_ = bf16[640,128]{1,0:T(8,128)(2,1)S(1)} collective-permute-done((bf16[640,128]{1,0:T(8,128)(2,1)S(1)}, bf16[640,128]{1,0:T(8,128)(2,1)S(1)}, u32[]{:S(2)}, u32[]{:S(2)}) %collective-permute-start.24) | collective-permute-done | bytes 163872 | tf_op jit(solution)/shard_map/ppermute | solution.py:39
  79.7 3.1 %collective-permute-start.27 = (bf16[640,128]{1,0:T(8,128)(2,1)S(1)}, bf16[640,128]{1,0:T(8,128)(2,1)S(1)}, u32[]{:S(2)}, u32[]{:S(2)}) collective-permute-start(bf16[640,128]{1,0:T(8,128)(2,1)S(1)} %pad_maximum_fusion.7), channel_id=1, source_target_pairs={{0,3},{1,0},{2,1},{3,2},{4,7},{5,4},{6,5},{7,6},{8,11},{9,8},{10,9... | collective-permute-start | bytes 491528 | tf_op jit(solution)/shard_map/ppermute | solution.py:39
  83.0 2.6 %collective-permute-start.21 = (bf16[16,128]{1,0:T(8,128)(2,1)S(1)}, bf16[16,128]{1,0:T(8,128)(2,1)S(1)}, u32[]{:S(2)}, u32[]{:S(2)}) collective-permute-start(bf16[16,128]{1,0:T(8,128)(2,1)S(1)} %slice.164), channel_id=1, source_target_pairs={{0,8},{8,0},{16,24},{24,16},{32,40},{40,32},{48,56},{56,48},{64,72... | collective-permute-start | bytes 12296 | tf_op jit(solution)/shard_map/ppermute | solution.py:34
  86.4 1.9 %collective-permute-done.26.refs_6_ = bf16[640,128]{1,0:T(8,128)(2,1)S(1)} collective-permute-done((bf16[640,128]{1,0:T(8,128)(2,1)S(1)}, bf16[640,128]{1,0:T(8,128)(2,1)S(1)}, u32[]{:S(2)}, u32[]{:S(2)}) %collective-permute-start.26) | collective-permute-done | bytes 163872 | tf_op jit(solution)/shard_map/ppermute | solution.py:39
  89.0 2.7 %collective-permute-start.32 = (bf16[640,128]{1,0:T(8,128)(2,1)S(1)}, bf16[640,128]{1,0:T(8,128)(2,1)S(1)}, u32[]{:S(2)}, u32[]{:S(2)}) collective-permute-start(bf16[640,128]{1,0:T(8,128)(2,1)S(1)} %get-tuple-element.51), channel_id=1, source_target_pairs={{0,224},{8,232},{16,240},{24,248},{32,0},{40,8},{48,16},{56,24},{6... | collective-permute-start | bytes 491528 | tf_op jit(solution)/shard_map/ppermute | solution.py:48
  91.7 1.7 %backward_near.1.parts = bf16[32,256,128]{2,1,0:T(8,128)(2,1)S(1)} custom-call(s32[68]{0:T(128)S(1)} %get-tuple-element.36.lists_any, bf16[12,256,256]{2,1,0:T(8,128)(2,1)S(1)} %bitcast.46, bf16[12,256,256]{2,1,0:T(8,128)(2,1)S(1)} %collective-permute-done.2.adj1, bf16[8,512,128]{2,1,0:T(8,128)(2,1)S(1)} %get-tuple-element.49.back), custom_call_target="tpu_custom_call" | custom-call | flops 352321536 | bytes 6291456 | tf_op jit(solution)/shard_map/backward_near/pallas_call | solution.py:449
  94.8 2.7 %collective-permute-start.33 = (bf16[1152,128]{1,0:T(8,128)(2,1)S(1)}, bf16[1152,128]{1,0:T(8,128)(2,1)S(1)}, u32[]{:S(2)}, u32[]{:S(2)}) collective-permute-start(bf16[1152,128]{1,0:T(8,128)(2,1)S(1)} %pad_maximum_fusion.3), channel_id=1, source_target_pairs={{0,224},{8,232},{16,240},{24,248},{32,0},{40,8},{48,16},{56,24},{6... | collective-permute-start | bytes 884744 | tf_op jit(solution)/shard_map/ppermute | solution.py:48
  97.5 4.2 %collective-permute-done.29.up2 = bf16[1152,128]{1,0:T(8,128)(2,1)S(1)} collective-permute-done((bf16[1152,128]{1,0:T(8,128)(2,1)S(1)}, bf16[1152,128]{1,0:T(8,128)(2,1)S(1)}, u32[]{:S(2)}, u32[]{:S(2)}) %collective-permute-start.29) | collective-permute-done | bytes 294944 | tf_op jit(solution)/shard_map/ppermute | solution.py:48
  102.1 2.8 %collective-permute-start.34 = (bf16[1152,128]{1,0:T(8,128)(2,1)S(1)}, bf16[1152,128]{1,0:T(8,128)(2,1)S(1)}, u32[]{:S(2)}, u32[]{:S(2)}) collective-permute-start(bf16[1152,128]{1,0:T(8,128)(2,1)S(1)} %pad_maximum_fusion.4), channel_id=1, source_target_pairs={{0,224},{8,232},{16,240},{24,248},{32,0},{40,8},{48,16},{56,24},{6... | collective-permute-start | bytes 884744 | tf_op jit(solution)/shard_map/ppermute | solution.py:48
  104.9 5.3 %collective-permute-done.30.up3 = bf16[1152,128]{1,0:T(8,128)(2,1)S(1)} collective-permute-done((bf16[1152,128]{1,0:T(8,128)(2,1)S(1)}, bf16[1152,128]{1,0:T(8,128)(2,1)S(1)}, u32[]{:S(2)}, u32[]{:S(2)}) %collective-permute-start.30) | collective-permute-done | bytes 294944 | tf_op jit(solution)/shard_map/ppermute | solution.py:48
  110.5 3.0 %collective-permute-start.35 = (bf16[1024,128]{1,0:T(8,128)(2,1)S(1)}, bf16[1024,128]{1,0:T(8,128)(2,1)S(1)}, u32[]{:S(2)}, u32[]{:S(2)}) collective-permute-start(bf16[1024,128]{1,0:T(8,128)(2,1)S(1)} %fusion), channel_id=1, source_target_pairs={{0,224},{8,232},{16,240},{24,248},{32,0},{40,8},{48,16},{56,24},{6... | collective-permute-start | bytes 786440 | tf_op jit(solution)/shard_map/ppermute | solution.py:48
  113.5 6.1 %collective-permute-done.35.down4 = bf16[1024,128]{1,0:T(8,128)(2,1)S(1)} collective-permute-done((bf16[1024,128]{1,0:T(8,128)(2,1)S(1)}, bf16[1024,128]{1,0:T(8,128)(2,1)S(1)}, u32[]{:S(2)}, u32[]{:S(2)}) %collective-permute-start.35) | collective-permute-done | bytes 262176 | tf_op jit(solution)/shard_map/ppermute | solution.py:48
  120.5 2.2 %collective-permute-start.37 = (bf16[128,128]{1,0:T(8,128)(2,1)S(1)}, bf16[128,128]{1,0:T(8,128)(2,1)S(1)}, u32[]{:S(2)}, u32[]{:S(2)}) collective-permute-start(bf16[128,128]{1,0:T(8,128)(2,1)S(1)} %slice.158), channel_id=1, source_target_pairs={{0,4},{1,5},{2,6},{3,7},{4,0},{5,1},{6,2},{7,3},{8,12},{9,13},{10,... | collective-permute-start | bytes 98312 | tf_op jit(solution)/shard_map/ppermute | solution.py:561
  123.7 2.4 %collective-permute-done.37.w_lo = bf16[128,128]{1,0:T(8,128)(2,1)S(1)} collective-permute-done((bf16[128,128]{1,0:T(8,128)(2,1)S(1)}, bf16[128,128]{1,0:T(8,128)(2,1)S(1)}, u32[]{:S(2)}, u32[]{:S(2)}) %collective-permute-start.37) | collective-permute-done | bytes 32800 | tf_op jit(solution)/shard_map/ppermute | solution.py:561
  127.1 10.0 %collective-permute-start.39 = (bf16[768,128]{1,0:T(8,128)(2,1)S(1)}, bf16[768,128]{1,0:T(8,128)(2,1)S(1)}, u32[]{:S(2)}, u32[]{:S(2)}) collective-permute-start(bf16[768,128]{1,0:T(8,128)(2,1)S(1)} %get-tuple-element.55), channel_id=1, source_target_pairs={{0,8},{8,0},{16,24},{24,16},{32,40},{40,32},{48,56},{56,48},{64,72... | collective-permute-start | bytes 589832 | tf_op jit(solution)/shard_map/ppermute | solution.py:34
  (106 shorter events, 23.8 us)
Async XLA Ops:
  0.6 8.7 %collective-permute-start = (bf16[256,256]{1,0:T(8,128)(2,1)}, bf16[256,256]{1,0:T(8,128)(2,1)S(1)}, u32[]{:S(2)}, u32[]{:S(2)}) collective-permute-start(bf16[256,256]{1,0:T(8,128)(2,1)} %bitcast.51), channel_id=1, source_target_pairs={{0,16},{8,24},{16,0},{24,8},{32,48},{40,56},{48,32},{56,40},{64,80... | collective-permute-start | bytes 393224 | tf_op jit(solution)/shard_map/ppermute | solution.py:34
  4.3 36.6 %collective-permute-start.2 = (bf16[12,256,256]{2,1,0:T(8,128)(2,1)}, bf16[12,256,256]{2,1,0:T(8,128)(2,1)S(1)}, u32[]{:S(2)}, u32[]{:S(2)}) collective-permute-start(bf16[12,256,256]{2,1,0:T(8,128)(2,1)} %bitcast.42), channel_id=1, source_target_pairs={{0,8},{8,0},{16,24},{24,16},{32,40},{40,32},{48,56},{56,48},{64,72... | collective-permute-start | bytes 4718600 | tf_op jit(solution)/shard_map/ppermute | solution.py:34
  11.8 10.3 %collective-permute-start.3 = (bf16[4,256,128]{2,1,0:T(8,128)(2,1)S(1)}, bf16[4,256,128]{2,1,0:T(8,128)(2,1)S(1)}, u32[]{:S(2)}, u32[]{:S(2)}) collective-permute-start(bf16[4,256,128]{2,1,0:T(8,128)(2,1)S(1)} %pad_maximum_fusion.5.refs_0_), channel_id=1, source_target_pairs={{0,224},{8,232},{16,240},{24,248},{32,0},{40,8},{48,16},{56,24},{6... | collective-permute-start | bytes 786440 | tf_op jit(solution)/shard_map/ppermute | solution.py:48
  16.5 9.0 %collective-permute-start.6 = (bf16[4,256,128]{2,1,0:T(8,128)(2,1)S(1)}, bf16[4,256,128]{2,1,0:T(8,128)(2,1)S(1)}, u32[]{:S(2)}, u32[]{:S(2)}) collective-permute-start(bf16[4,256,128]{2,1,0:T(8,128)(2,1)S(1)} %pad_maximum_fusion.5.refs_0_), channel_id=1, source_target_pairs={{0,32},{8,40},{16,48},{24,56},{32,64},{40,72},{48,80},{56,88},{64,... | collective-permute-start | bytes 786440 | tf_op jit(solution)/shard_map/ppermute | solution.py:48
  22.1 8.1 %collective-permute-start.4 = (bf16[4,256,128]{2,1,0:T(8,128)(2,1)S(1)}, bf16[4,256,128]{2,1,0:T(8,128)(2,1)S(1)}, u32[]{:S(2)}, u32[]{:S(2)}) collective-permute-start(bf16[4,256,128]{2,1,0:T(8,128)(2,1)S(1)} %collective-permute-done.3.refs_1_), channel_id=1, source_target_pairs={{0,224},{8,232},{16,240},{24,248},{32,0},{40,8},{48,16},{56,24},{6... | collective-permute-start | bytes 786440 | tf_op jit(solution)/shard_map/ppermute | solution.py:48
  25.5 8.1 %collective-permute-start.7 = (bf16[4,256,128]{2,1,0:T(8,128)(2,1)S(1)}, bf16[4,256,128]{2,1,0:T(8,128)(2,1)S(1)}, u32[]{:S(2)}, u32[]{:S(2)}) collective-permute-start(bf16[4,256,128]{2,1,0:T(8,128)(2,1)S(1)} %collective-permute-done.6.refs_6_), channel_id=1, source_target_pairs={{0,32},{8,40},{16,48},{24,56},{32,64},{40,72},{48,80},{56,88},{64,... | collective-permute-start | bytes 786440 | tf_op jit(solution)/shard_map/ppermute | solution.py:48
  30.1 7.1 %collective-permute-start.5 = (bf16[4,256,128]{2,1,0:T(8,128)(2,1)S(1)}, bf16[4,256,128]{2,1,0:T(8,128)(2,1)S(1)}, u32[]{:S(2)}, u32[]{:S(2)}) collective-permute-start(bf16[4,256,128]{2,1,0:T(8,128)(2,1)S(1)} %collective-permute-done.4.refs_2_), channel_id=1, source_target_pairs={{0,224},{8,232},{16,240},{24,248},{32,0},{40,8},{48,16},{56,24},{6... | collective-permute-start | bytes 786440 | tf_op jit(solution)/shard_map/ppermute | solution.py:48
  33.6 7.2 %collective-permute-start.8 = (bf16[4,256,128]{2,1,0:T(8,128)(2,1)S(1)}, bf16[4,256,128]{2,1,0:T(8,128)(2,1)S(1)}, u32[]{:S(2)}, u32[]{:S(2)}) collective-permute-start(bf16[4,256,128]{2,1,0:T(8,128)(2,1)S(1)} %collective-permute-done.7.refs_5_), channel_id=1, source_target_pairs={{0,32},{8,40},{16,48},{24,56},{32,64},{40,72},{48,80},{56,88},{64,... | collective-permute-start | bytes 786440 | tf_op jit(solution)/shard_map/ppermute | solution.py:48
  37.3 5.6 %collective-permute-start.10 = (bf16[2,256,128]{2,1,0:T(8,128)(2,1)S(1)}, bf16[2,256,128]{2,1,0:T(8,128)(2,1)S(1)}, u32[]{:S(2)}, u32[]{:S(2)}) collective-permute-start(bf16[2,256,128]{2,1,0:T(8,128)(2,1)S(1)} %slice.163), channel_id=1, source_target_pairs={{0,224},{8,232},{16,240},{24,248},{32,0},{40,8},{48,16},{56,24},{6... | collective-permute-start | bytes 393224 | tf_op jit(solution)/shard_map/ppermute | solution.py:48
  46.6 7.2 %collective-permute-start.11 = (bf16[2,256,128]{2,1,0:T(8,128)(2,1)S(1)}, bf16[2,256,128]{2,1,0:T(8,128)(2,1)S(1)}, u32[]{:S(2)}, u32[]{:S(2)}) collective-permute-start(bf16[2,256,128]{2,1,0:T(8,128)(2,1)S(1)} %get-tuple-element.39), channel_id=1, source_target_pairs={{0,6},{1,7},{2,4},{3,5},{4,2},{5,3},{6,0},{7,1},{8,14},{9,15},{10,... | collective-permute-start | bytes 393224 | tf_op jit(solution)/shard_map/ppermute | solution.py:39
  49.5 7.0 %collective-permute-start.12 = (bf16[2,256,128]{2,1,0:T(8,128)(2,1)S(1)}, bf16[2,256,128]{2,1,0:T(8,128)(2,1)S(1)}, u32[]{:S(2)}, u32[]{:S(2)}) collective-permute-start(bf16[2,256,128]{2,1,0:T(8,128)(2,1)S(1)} %get-tuple-element.40), channel_id=1, source_target_pairs={{0,2},{1,3},{2,0},{3,1},{4,6},{5,7},{6,4},{7,5},{8,10},{9,11},{10,... | collective-permute-start | bytes 393224 | tf_op jit(solution)/shard_map/ppermute | solution.py:39
  49.9 7.3 %collective-permute-start.13 = (bf16[2,256,128]{2,1,0:T(8,128)(2,1)S(1)}, bf16[2,256,128]{2,1,0:T(8,128)(2,1)S(1)}, u32[]{:S(2)}, u32[]{:S(2)}) collective-permute-start(bf16[2,256,128]{2,1,0:T(8,128)(2,1)S(1)} %get-tuple-element.41), channel_id=1, source_target_pairs={{0,5},{1,6},{2,7},{3,4},{4,1},{5,2},{6,3},{7,0},{8,13},{9,14},{10,... | collective-permute-start | bytes 393224 | tf_op jit(solution)/shard_map/ppermute | solution.py:39
  53.8 8.6 %collective-permute-start.15 = (bf16[2,256,128]{2,1,0:T(8,128)(2,1)S(1)}, bf16[2,256,128]{2,1,0:T(8,128)(2,1)S(1)}, u32[]{:S(2)}, u32[]{:S(2)}) collective-permute-start(bf16[2,256,128]{2,1,0:T(8,128)(2,1)S(1)} %get-tuple-element.43), channel_id=1, source_target_pairs={{0,1},{1,2},{2,3},{3,0},{4,5},{5,6},{6,7},{7,4},{8,9},{9,10},{10,1... | collective-permute-start | bytes 393224 | tf_op jit(solution)/shard_map/ppermute | solution.py:39
  53.8 8.6 %collective-permute-start.16 = (bf16[2,256,128]{2,1,0:T(8,128)(2,1)S(1)}, bf16[2,256,128]{2,1,0:T(8,128)(2,1)S(1)}, u32[]{:S(2)}, u32[]{:S(2)}) collective-permute-start(bf16[2,256,128]{2,1,0:T(8,128)(2,1)S(1)} %get-tuple-element.44), channel_id=1, source_target_pairs={{0,3},{1,0},{2,1},{3,2},{4,7},{5,4},{6,5},{7,6},{8,11},{9,8},{10,9... | collective-permute-start | bytes 393224 | tf_op jit(solution)/shard_map/ppermute | solution.py:39
  56.5 5.9 %collective-permute-start.17 = (bf16[2,256,128]{2,1,0:T(8,128)(2,1)S(1)}, bf16[2,256,128]{2,1,0:T(8,128)(2,1)S(1)}, u32[]{:S(2)}, u32[]{:S(2)}) collective-permute-start(bf16[2,256,128]{2,1,0:T(8,128)(2,1)S(1)} %get-tuple-element.45), channel_id=1, source_target_pairs={{0,4},{1,5},{2,6},{3,7},{4,0},{5,1},{6,2},{7,3},{8,12},{9,13},{10,... | collective-permute-start | bytes 393224 | tf_op jit(solution)/shard_map/ppermute | solution.py:39
  62.6 6.4 %collective-permute-start.18 = (f32[512,128]{1,0:T(8,128)S(1)}, f32[512,128]{1,0:T(8,128)S(1)}, u32[]{:S(2)}, u32[]{:S(2)}) collective-permute-start(f32[512,128]{1,0:T(8,128)S(1)} %bitcast.49), channel_id=1, source_target_pairs={{0,8},{8,0},{16,24},{24,16},{32,40},{40,32},{48,56},{56,48},{64,72... | collective-permute-start | bytes 786440 | tf_op jit(solution)/shard_map/ppermute | solution.py:34
  70.6 9.1 %collective-permute-start.24 = (bf16[640,128]{1,0:T(8,128)(2,1)S(1)}, bf16[640,128]{1,0:T(8,128)(2,1)S(1)}, u32[]{:S(2)}, u32[]{:S(2)}) collective-permute-start(bf16[640,128]{1,0:T(8,128)(2,1)S(1)} %get-tuple-element.48.refs_0_), channel_id=1, source_target_pairs={{0,3},{1,0},{2,1},{3,2},{4,7},{5,4},{6,5},{7,6},{8,11},{9,8},{10,9... | collective-permute-start | bytes 491528 | tf_op jit(solution)/shard_map/ppermute | solution.py:39
  72.5 7.1 %collective-permute-start.20 = (bf16[640,128]{1,0:T(8,128)(2,1)S(1)}, bf16[640,128]{1,0:T(8,128)(2,1)S(1)}, u32[]{:S(2)}, u32[]{:S(2)}) collective-permute-start(bf16[640,128]{1,0:T(8,128)(2,1)S(1)} %get-tuple-element.47), channel_id=1, source_target_pairs={{0,7},{1,4},{2,5},{3,6},{4,3},{5,0},{6,1},{7,2},{8,15},{9,12},{10,... | collective-permute-start | bytes 491528 | tf_op jit(solution)/shard_map/ppermute | solution.py:39
  73.4 9.4 %collective-permute-start.22 = (bf16[640,128]{1,0:T(8,128)(2,1)S(1)}, bf16[640,128]{1,0:T(8,128)(2,1)S(1)}, u32[]{:S(2)}, u32[]{:S(2)}) collective-permute-start(bf16[640,128]{1,0:T(8,128)(2,1)S(1)} %get-tuple-element.48.refs_0_), channel_id=1, source_target_pairs={{0,1},{1,2},{2,3},{3,0},{4,5},{5,6},{6,7},{7,4},{8,9},{9,10},{10,1... | collective-permute-start | bytes 491528 | tf_op jit(solution)/shard_map/ppermute | solution.py:39
  74.9 7.9 %collective-permute-start.23 = (bf16[640,128]{1,0:T(8,128)(2,1)S(1)}, bf16[640,128]{1,0:T(8,128)(2,1)S(1)}, u32[]{:S(2)}, u32[]{:S(2)}) collective-permute-start(bf16[640,128]{1,0:T(8,128)(2,1)S(1)} %get-tuple-element.47), channel_id=1, source_target_pairs={{0,5},{1,6},{2,7},{3,4},{4,1},{5,2},{6,3},{7,0},{8,13},{9,14},{10,... | collective-permute-start | bytes 491528 | tf_op jit(solution)/shard_map/ppermute | solution.py:39
  74.9 10.7 %collective-permute-start.25 = (bf16[640,128]{1,0:T(8,128)(2,1)S(1)}, bf16[640,128]{1,0:T(8,128)(2,1)S(1)}, u32[]{:S(2)}, u32[]{:S(2)}) collective-permute-start(bf16[640,128]{1,0:T(8,128)(2,1)S(1)} %get-tuple-element.47), channel_id=1, source_target_pairs={{0,4},{1,5},{2,6},{3,7},{4,0},{5,1},{6,2},{7,3},{8,12},{9,13},{10,... | collective-permute-start | bytes 491528 | tf_op jit(solution)/shard_map/ppermute | solution.py:39
  79.7 6.7 %collective-permute-start.27 = (bf16[640,128]{1,0:T(8,128)(2,1)S(1)}, bf16[640,128]{1,0:T(8,128)(2,1)S(1)}, u32[]{:S(2)}, u32[]{:S(2)}) collective-permute-start(bf16[640,128]{1,0:T(8,128)(2,1)S(1)} %pad_maximum_fusion.7), channel_id=1, source_target_pairs={{0,3},{1,0},{2,1},{3,2},{4,7},{5,4},{6,5},{7,6},{8,11},{9,8},{10,9... | collective-permute-start | bytes 491528 | tf_op jit(solution)/shard_map/ppermute | solution.py:39
  88.9 5.5 %collective-permute-start.28 = (bf16[640,128]{1,0:T(8,128)(2,1)S(1)}, bf16[640,128]{1,0:T(8,128)(2,1)S(1)}, u32[]{:S(2)}, u32[]{:S(2)}) collective-permute-start(bf16[640,128]{1,0:T(8,128)(2,1)S(1)} %get-tuple-element.50.own), channel_id=1, source_target_pairs={{0,32},{8,40},{16,48},{24,56},{32,64},{40,72},{48,80},{56,88},{64,... | collective-permute-start | bytes 491528 | tf_op jit(solution)/shard_map/ppermute | solution.py:48
  94.5 7.2 %collective-permute-start.29 = (bf16[1152,128]{1,0:T(8,128)(2,1)S(1)}, bf16[1152,128]{1,0:T(8,128)(2,1)S(1)}, u32[]{:S(2)}, u32[]{:S(2)}) collective-permute-start(bf16[1152,128]{1,0:T(8,128)(2,1)S(1)} %pad_maximum_fusion), channel_id=1, source_target_pairs={{0,32},{8,40},{16,48},{24,56},{32,64},{40,72},{48,80},{56,88},{64,... | collective-permute-start | bytes 884744 | tf_op jit(solution)/shard_map/ppermute | solution.py:48
  94.8 7.2 %collective-permute-start.33 = (bf16[1152,128]{1,0:T(8,128)(2,1)S(1)}, bf16[1152,128]{1,0:T(8,128)(2,1)S(1)}, u32[]{:S(2)}, u32[]{:S(2)}) collective-permute-start(bf16[1152,128]{1,0:T(8,128)(2,1)S(1)} %pad_maximum_fusion.3), channel_id=1, source_target_pairs={{0,224},{8,232},{16,240},{24,248},{32,0},{40,8},{48,16},{56,24},{6... | collective-permute-start | bytes 884744 | tf_op jit(solution)/shard_map/ppermute | solution.py:48
  101.8 8.3 %collective-permute-start.30 = (bf16[1152,128]{1,0:T(8,128)(2,1)S(1)}, bf16[1152,128]{1,0:T(8,128)(2,1)S(1)}, u32[]{:S(2)}, u32[]{:S(2)}) collective-permute-start(bf16[1152,128]{1,0:T(8,128)(2,1)S(1)} %pad_maximum_fusion.1), channel_id=1, source_target_pairs={{0,32},{8,40},{16,48},{24,56},{32,64},{40,72},{48,80},{56,88},{64,... | collective-permute-start | bytes 884744 | tf_op jit(solution)/shard_map/ppermute | solution.py:48
  102.1 8.3 %collective-permute-start.34 = (bf16[1152,128]{1,0:T(8,128)(2,1)S(1)}, bf16[1152,128]{1,0:T(8,128)(2,1)S(1)}, u32[]{:S(2)}, u32[]{:S(2)}) collective-permute-start(bf16[1152,128]{1,0:T(8,128)(2,1)S(1)} %pad_maximum_fusion.4), channel_id=1, source_target_pairs={{0,224},{8,232},{16,240},{24,248},{32,0},{40,8},{48,16},{56,24},{6... | collective-permute-start | bytes 884744 | tf_op jit(solution)/shard_map/ppermute | solution.py:48
  110.3 9.9 %collective-permute-start.31 = (bf16[1152,128]{1,0:T(8,128)(2,1)S(1)}, bf16[1152,128]{1,0:T(8,128)(2,1)S(1)}, u32[]{:S(2)}, u32[]{:S(2)}) collective-permute-start(bf16[1152,128]{1,0:T(8,128)(2,1)S(1)} %pad_maximum_fusion.2), channel_id=1, source_target_pairs={{0,32},{8,40},{16,48},{24,56},{32,64},{40,72},{48,80},{56,88},{64,... | collective-permute-start | bytes 884744 | tf_op jit(solution)/shard_map/ppermute | solution.py:48
  110.5 9.1 %collective-permute-start.35 = (bf16[1024,128]{1,0:T(8,128)(2,1)S(1)}, bf16[1024,128]{1,0:T(8,128)(2,1)S(1)}, u32[]{:S(2)}, u32[]{:S(2)}) collective-permute-start(bf16[1024,128]{1,0:T(8,128)(2,1)S(1)} %fusion), channel_id=1, source_target_pairs={{0,224},{8,232},{16,240},{24,248},{32,0},{40,8},{48,16},{56,24},{6... | collective-permute-start | bytes 786440 | tf_op jit(solution)/shard_map/ppermute | solution.py:48
  120.4 6.6 %collective-permute-start.36 = (bf16[640,128]{1,0:T(8,128)(2,1)S(1)}, bf16[640,128]{1,0:T(8,128)(2,1)S(1)}, u32[]{:S(2)}, u32[]{:S(2)}) collective-permute-start(bf16[640,128]{1,0:T(8,128)(2,1)S(1)} %get-tuple-element.53.sent), channel_id=1, source_target_pairs={{0,16},{8,24},{16,0},{24,8},{32,48},{40,56},{48,32},{56,40},{64,80... | collective-permute-start | bytes 491528 | tf_op jit(solution)/shard_map/ppermute | solution.py:34
  120.5 5.6 %collective-permute-start.37 = (bf16[128,128]{1,0:T(8,128)(2,1)S(1)}, bf16[128,128]{1,0:T(8,128)(2,1)S(1)}, u32[]{:S(2)}, u32[]{:S(2)}) collective-permute-start(bf16[128,128]{1,0:T(8,128)(2,1)S(1)} %slice.158), channel_id=1, source_target_pairs={{0,4},{1,5},{2,6},{3,7},{4,0},{5,1},{6,2},{7,3},{8,12},{9,13},{10,... | collective-permute-start | bytes 98312 | tf_op jit(solution)/shard_map/ppermute | solution.py:561
  127.1 11.1 %collective-permute-start.39 = (bf16[768,128]{1,0:T(8,128)(2,1)S(1)}, bf16[768,128]{1,0:T(8,128)(2,1)S(1)}, u32[]{:S(2)}, u32[]{:S(2)}) collective-permute-start(bf16[768,128]{1,0:T(8,128)(2,1)S(1)} %get-tuple-element.55), channel_id=1, source_target_pairs={{0,8},{8,0},{16,24},{24,16},{32,40},{40,32},{48,56},{56,48},{64,72... | collective-permute-start | bytes 589832 | tf_op jit(solution)/shard_map/ppermute | solution.py:34
  (14 other events, 120.0 us)

commit v13 on v9

--- a/solution.py
+++ b/solution.py
@@ -44,7 +44,13 @@
 
 
 def z_shift(x, step):
-    return lax.ppermute(x, "row", row_pairs(lambda z, q: (z + step, q)))
+    return lax.ppermute(
+        x, "row", row_pairs(lambda z, q: (z + step * (1 - 2 * (q & 1)), q))
+    )
+
+
+def z_ahead(z, core, steps):
+    return (z + steps * (1 - 2 * core)) & 7
 
 
 def prepare_kernel(rows, cols, count, block, keep, message, own_lists):
@@ -92,7 +98,7 @@
         near, far = jnp.int32(0), jnp.int32(0)
         for s in range(SLOTS):
             tile = slots[12 + s]
-            place = (((tile >> 2) - z) & 7) * QUAD + ((tile & 3) ^ q)
+            place = z_ahead(0, q & 1, (tile >> 2) - z) * QUAD + ((tile & 3) ^ q)
             live = (s < slots[24]).astype(jnp.int32)
             is_far = ((place >> 2) == 4).astype(jnp.int32)
             lists[i * PART + is_far * (2 * PART + far - near) + near] = (
@@ -261,7 +267,8 @@
 def ring_end_kernel(
     parts, own, up1, up2, up3, up4, down1, down2, down3, down4, kept, message, by_step
 ):
-    z = lax.axis_index("row") >> 2
+    device = lax.axis_index("row")
+    z, core = device >> 2, device & 1
     half, size = 2 * TILE, QUAD * TILE
     pieces = (
         (own, half),
@@ -274,7 +281,7 @@
         (up1, half),
     )
     for k, (ref, start) in enumerate(pieces):
-        by_step[(k + z) & 7] = ref[start:, :]
+        by_step[z_ahead(z, core, k)] = ref[start:, :]
     w_sum = by_step[0].astype(jnp.float32)
     for a in range(1, NZ):
         w_sum = w_sum + by_step[a].astype(jnp.float32)

time: 136 us -> 142 us (1.044)
  starting transfers between devices: 69.2 us -> 76.1 us
    ppermute x7, starting transfers between devices: 21.1 us -> 28 us  [quad_permute(): return lax.ppermute(x, 'row', row_pairs(lambda z, q: (z, q ^ flip)))]
    ppermute x14, waiting for transfers between devices: 15.8 us -> 14.1 us  [col_move(): return lax.ppermute(x, 'col', pairs)]
  transfers between devices with their start and end apart: 39 -> 39, of which waited for: 20 -> 24; matrix products, arithmetic and copies ran while one was open for 0% -> 0% of each run, Pallas kernels for 4% -> 3%
where the time goes in v13:
time: 142 us
  starting transfers between devices  76.1 us (54%)
  waiting for transfers between devices  51.9 us (37%)
  Pallas kernels  8.97 us (6%)
  local copies, waits for them, and re-layouts  2.4 us (2%)
  between operations  1.59 us (1%)
    ppermute x16, waiting for transfers between devices, z_shift(): lax.ppermute(x, 'row', row_pairs(lambda z, q: (z + step * (1 - 2 * (q & 1...  30.4 us
    ppermute x7, starting transfers between devices, quad_permute(): return lax.ppermute(x, 'row', row_pairs(lambda z, q: (z, q ^ flip)))  28 us
    ppermute x16, starting transfers between devices, z_shift(): lax.ppermute(x, 'row', row_pairs(lambda z, q: (z + step * (1 - 2 * (q & 1...  26.8 us
    ppermute x14, starting transfers between devices, col_move(): return lax.ppermute(x, 'col', pairs)  20.4 us
    ppermute x14, waiting for transfers between devices, col_move(): return lax.ppermute(x, 'col', pairs)  14.1 us
    ppermute x7, waiting for transfers between devices, quad_permute(): return lax.ppermute(x, 'row', row_pairs(lambda z, q: (z, q ^ flip)))  3.3 us
    ppermute x1, waiting for transfers between devices, per_device(): w_lo = lax.ppermute(w_send, 'col', [(c, c ^ 4) for c in range(NCOL)])  3.05 us
  transfers between devices with their start and end apart: 39, of which 24 were waited for; matrix products, arithmetic and copies ran while one was open for 0% of the time, Pallas kernels for 3%

profile of v13, /device:TPU:1, one launch (start us, length us, event | category | flops | bytes accessed | tf_op | source)
XLA Modules:
  0.0 141.6 jit_solution(8898693096472620116)
XLA Ops:
  0.6 3.7 %collective-permute-start = (bf16[256,256]{1,0:T(8,128)(2,1)}, bf16[256,256]{1,0:T(8,128)(2,1)S(1)}, u32[]{:S(2)}, u32[]{:S(2)}) collective-permute-start(bf16[256,256]{1,0:T(8,128)(2,1)} %bitcast.51), channel_id=1, source_target_pairs={{0,16},{8,24},{16,0},{24,8},{32,48},{40,56},{48,32},{56,40},{64,80... | collective-permute-start | bytes 393224 | tf_op jit(solution)/shard_map/ppermute | solution.py:33
  12.6 4.0 %collective-permute-start.6 = (bf16[4,256,128]{2,1,0:T(8,128)(2,1)S(1)}, bf16[4,256,128]{2,1,0:T(8,128)(2,1)S(1)}, u32[]{:S(2)}, u32[]{:S(2)}) collective-permute-start(bf16[4,256,128]{2,1,0:T(8,128)(2,1)S(1)} %pad_maximum_fusion.5.refs_0_), channel_id=1, source_target_pairs={{0,32},{8,232},{16,48},{24,248},{32,64},{40,8},{48,80},{56,24},{64... | collective-permute-start | bytes 786440 | tf_op jit(solution)/shard_map/ppermute | solution.py:47
  16.6 3.7 %collective-permute-done.3.refs_1_ = bf16[4,256,128]{2,1,0:T(8,128)(2,1)S(1)} collective-permute-done((bf16[4,256,128]{2,1,0:T(8,128)(2,1)S(1)}, bf16[4,256,128]{2,1,0:T(8,128)(2,1)S(1)}, u32[]{:S(2)}, u32[]{:S(2)}) %collective-permute-start.3) | collective-permute-done | bytes 262176 | tf_op jit(solution)/shard_map/ppermute | solution.py:47
  20.3 2.0 %collective-permute-done.6.refs_6_ = bf16[4,256,128]{2,1,0:T(8,128)(2,1)S(1)} collective-permute-done((bf16[4,256,128]{2,1,0:T(8,128)(2,1)S(1)}, bf16[4,256,128]{2,1,0:T(8,128)(2,1)S(1)}, u32[]{:S(2)}, u32[]{:S(2)}) %collective-permute-start.6) | collective-permute-done | bytes 262176 | tf_op jit(solution)/shard_map/ppermute | solution.py:47
  22.3 3.4 %collective-permute-start.7 = (bf16[4,256,128]{2,1,0:T(8,128)(2,1)S(1)}, bf16[4,256,128]{2,1,0:T(8,128)(2,1)S(1)}, u32[]{:S(2)}, u32[]{:S(2)}) collective-permute-start(bf16[4,256,128]{2,1,0:T(8,128)(2,1)S(1)} %collective-permute-done.6.refs_6_), channel_id=1, source_target_pairs={{0,32},{8,232},{16,48},{24,248},{32,64},{40,8},{48,80},{56,24},{64... | collective-permute-start | bytes 786440 | tf_op jit(solution)/shard_map/ppermute | solution.py:47
  26.9 3.6 %collective-permute-done.7.refs_5_ = bf16[4,256,128]{2,1,0:T(8,128)(2,1)S(1)} collective-permute-done((bf16[4,256,128]{2,1,0:T(8,128)(2,1)S(1)}, bf16[4,256,128]{2,1,0:T(8,128)(2,1)S(1)}, u32[]{:S(2)}, u32[]{:S(2)}) %collective-permute-start.7) | collective-permute-done | bytes 262176 | tf_op jit(solution)/shard_map/ppermute | solution.py:47
  30.5 3.4 %collective-permute-start.8 = (bf16[4,256,128]{2,1,0:T(8,128)(2,1)S(1)}, bf16[4,256,128]{2,1,0:T(8,128)(2,1)S(1)}, u32[]{:S(2)}, u32[]{:S(2)}) collective-permute-start(bf16[4,256,128]{2,1,0:T(8,128)(2,1)S(1)} %collective-permute-done.7.refs_5_), channel_id=1, source_target_pairs={{0,32},{8,232},{16,48},{24,248},{32,64},{40,8},{48,80},{56,24},{64... | collective-permute-start | bytes 786440 | tf_op jit(solution)/shard_map/ppermute | solution.py:47
  33.9 2.3 %collective-permute-done.5.refs_3_ = bf16[4,256,128]{2,1,0:T(8,128)(2,1)S(1)} collective-permute-done((bf16[4,256,128]{2,1,0:T(8,128)(2,1)S(1)}, bf16[4,256,128]{2,1,0:T(8,128)(2,1)S(1)}, u32[]{:S(2)}, u32[]{:S(2)}) %collective-permute-start.5) | collective-permute-done | bytes 262176 | tf_op jit(solution)/shard_map/ppermute | solution.py:47
  37.8 3.5 %collective-permute-start.9 = (bf16[2,256,128]{2,1,0:T(8,128)(2,1)S(1)}, bf16[2,256,128]{2,1,0:T(8,128)(2,1)S(1)}, u32[]{:S(2)}, u32[]{:S(2)}) collective-permute-start(bf16[2,256,128]{2,1,0:T(8,128)(2,1)S(1)} %slice.126), channel_id=1, source_target_pairs={{0,32},{8,232},{16,48},{24,248},{32,64},{40,8},{48,80},{56,24},{64... | collective-permute-start | bytes 393224 | tf_op jit(solution)/shard_map/ppermute | solution.py:47
  41.3 2.0 %forward_near.1 = (f32[18,256,128]{2,1,0:T(8,128)S(1)}, s32[68]{0:T(128)S(1)}) custom-call(s32[25]{0:T(128)S(1)} %get-tuple-element.31.own_any, s32[25]{0:T(128)S(1)} %fusion.6.partner_any, bf16[12,256,256]{2,1,0:T(8,128)(2,1)S(1)} %bitcast.43, bf16[12,256,256]{2,1,0:T(8,128)(2,1)S(1)} %collective-permute-done.2.adj1, ...), custom_call_target="tpu_custom_call" | custom-call | flops 352321536 | bytes 6291456 | tf_op jit(solution)/shard_map/forward_near/pallas_call | solution.py:397
  44.2 2.4 %collective-permute-start.11 = (bf16[2,256,128]{2,1,0:T(8,128)(2,1)S(1)}, bf16[2,256,128]{2,1,0:T(8,128)(2,1)S(1)}, u32[]{:S(2)}, u32[]{:S(2)}) collective-permute-start(bf16[2,256,128]{2,1,0:T(8,128)(2,1)S(1)} %get-tuple-element.39), channel_id=1, source_target_pairs={{0,6},{1,7},{2,4},{3,5},{4,2},{5,3},{6,0},{7,1},{8,14},{9,15},{10,... | collective-permute-start | bytes 393224 | tf_op jit(solution)/shard_map/ppermute | solution.py:38
  47.3 2.6 %collective-permute-start.13 = (bf16[2,256,128]{2,1,0:T(8,128)(2,1)S(1)}, bf16[2,256,128]{2,1,0:T(8,128)(2,1)S(1)}, u32[]{:S(2)}, u32[]{:S(2)}) collective-permute-start(bf16[2,256,128]{2,1,0:T(8,128)(2,1)S(1)} %get-tuple-element.41), channel_id=1, source_target_pairs={{0,5},{1,6},{2,7},{3,4},{4,1},{5,2},{6,3},{7,0},{8,13},{9,14},{10,... | collective-permute-start | bytes 393224 | tf_op jit(solution)/shard_map/ppermute | solution.py:38
  51.0 2.6 %collective-permute-start.16 = (bf16[2,256,128]{2,1,0:T(8,128)(2,1)S(1)}, bf16[2,256,128]{2,1,0:T(8,128)(2,1)S(1)}, u32[]{:S(2)}, u32[]{:S(2)}) collective-permute-start(bf16[2,256,128]{2,1,0:T(8,128)(2,1)S(1)} %get-tuple-element.44), channel_id=1, source_target_pairs={{0,3},{1,0},{2,1},{3,2},{4,7},{5,4},{6,5},{7,6},{8,11},{9,8},{10,9... | collective-permute-start | bytes 393224 | tf_op jit(solution)/shard_map/ppermute | solution.py:38
  56.1 1.6 %collective-permute-done.17 = bf16[2,256,128]{2,1,0:T(8,128)(2,1)S(1)} collective-permute-done((bf16[2,256,128]{2,1,0:T(8,128)(2,1)S(1)}, bf16[2,256,128]{2,1,0:T(8,128)(2,1)S(1)}, u32[]{:S(2)}, u32[]{:S(2)}) %collective-permute-start.17) | collective-permute-done | bytes 131104 | tf_op jit(solution)/shard_map/ppermute | solution.py:38
  57.8 10.6 %collective-permute-start.18 = (f32[512,128]{1,0:T(8,128)S(1)}, f32[512,128]{1,0:T(8,128)S(1)}, u32[]{:S(2)}, u32[]{:S(2)}) collective-permute-start(f32[512,128]{1,0:T(8,128)S(1)} %bitcast.49), channel_id=1, source_target_pairs={{0,8},{8,0},{16,24},{24,16},{32,40},{40,32},{48,56},{56,48},{64,72... | collective-permute-start | bytes 786440 | tf_op jit(solution)/shard_map/ppermute | solution.py:33
  69.8 1.6 %dense.1 = (bf16[256,256]{1,0:T(8,128)(2,1)}, bf16[640,128]{1,0:T(8,128)(2,1)S(1)}, bf16[640,128]{1,0:T(8,128)(2,1)S(1)}) custom-call(f32[512,128]{1,0:T(8,128)S(1)} %bitcast.50, f32[512,128]{1,0:T(8,128)S(1)} %collective-permute-done.18.agg_other, bf16[256,256]{1,0:T(8,128)(2,1)S(1)} %copy-done.1, bf16[256,256]{1,0:T(8,128)(2,1)S(1)} %copy-done.2, ...), custom_call_target="tpu_custom_call" | custom-call | tf_op jit(solution)/shard_map/dense/pallas_call | solution.py:458
  72.5 2.5 %collective-permute-start.21 = (bf16[640,128]{1,0:T(8,128)(2,1)S(1)}, bf16[640,128]{1,0:T(8,128)(2,1)S(1)}, u32[]{:S(2)}, u32[]{:S(2)}) collective-permute-start(bf16[640,128]{1,0:T(8,128)(2,1)S(1)} %get-tuple-element.47.refs_0_), channel_id=1, source_target_pairs={{0,2},{1,3},{2,0},{3,1},{4,6},{5,7},{6,4},{7,5},{8,10},{9,11},{10,... | collective-permute-start | bytes 491528 | tf_op jit(solution)/shard_map/ppermute | solution.py:38
  74.9 3.6 %collective-permute-start.23 = (bf16[640,128]{1,0:T(8,128)(2,1)S(1)}, bf16[640,128]{1,0:T(8,128)(2,1)S(1)}, u32[]{:S(2)}, u32[]{:S(2)}) collective-permute-start(bf16[640,128]{1,0:T(8,128)(2,1)S(1)} %get-tuple-element.48), channel_id=1, source_target_pairs={{0,7},{1,4},{2,5},{3,6},{4,3},{5,0},{6,1},{7,2},{8,15},{9,12},{10,... | collective-permute-start | bytes 491528 | tf_op jit(solution)/shard_map/ppermute | solution.py:38
  79.2 2.0 %collective-permute-start.25 = (bf16[640,128]{1,0:T(8,128)(2,1)S(1)}, bf16[640,128]{1,0:T(8,128)(2,1)S(1)}, u32[]{:S(2)}, u32[]{:S(2)}) collective-permute-start(bf16[640,128]{1,0:T(8,128)(2,1)S(1)} %get-tuple-element.47.refs_0_), channel_id=1, source_target_pairs={{0,3},{1,0},{2,1},{3,2},{4,7},{5,4},{6,5},{7,6},{8,11},{9,8},{10,9... | collective-permute-start | bytes 491528 | tf_op jit(solution)/shard_map/ppermute | solution.py:38
  81.2 6.1 %collective-permute-done.21.refs_2_ = bf16[640,128]{1,0:T(8,128)(2,1)S(1)} collective-permute-done((bf16[640,128]{1,0:T(8,128)(2,1)S(1)}, bf16[640,128]{1,0:T(8,128)(2,1)S(1)}, u32[]{:S(2)}, u32[]{:S(2)}) %collective-permute-start.21) | collective-permute-done | bytes 163872 | tf_op jit(solution)/shard_map/ppermute | solution.py:38
  88.1 2.5 %collective-permute-done.24.refs_5_ = bf16[640,128]{1,0:T(8,128)(2,1)S(1)} collective-permute-done((bf16[640,128]{1,0:T(8,128)(2,1)S(1)}, bf16[640,128]{1,0:T(8,128)(2,1)S(1)}, u32[]{:S(2)}, u32[]{:S(2)}) %collective-permute-start.24) | collective-permute-done | bytes 163872 | tf_op jit(solution)/shard_map/ppermute | solution.py:38
  90.6 1.9 %collective-permute-done.26.refs_7_ = bf16[640,128]{1,0:T(8,128)(2,1)S(1)} collective-permute-done((bf16[640,128]{1,0:T(8,128)(2,1)S(1)}, bf16[640,128]{1,0:T(8,128)(2,1)S(1)}, u32[]{:S(2)}, u32[]{:S(2)}) %collective-permute-start.26) | collective-permute-done | bytes 163872 | tf_op jit(solution)/shard_map/ppermute | solution.py:38
  94.8 1.5 %backward_near.1.parts = bf16[32,256,128]{2,1,0:T(8,128)(2,1)S(1)} custom-call(s32[68]{0:T(128)S(1)} %get-tuple-element.36.lists_any, bf16[12,256,256]{2,1,0:T(8,128)(2,1)S(1)} %bitcast.46, bf16[12,256,256]{2,1,0:T(8,128)(2,1)S(1)} %collective-permute-done.2.adj1, bf16[8,512,128]{2,1,0:T(8,128)(2,1)S(1)} %get-tuple-element.49.back), custom_call_target="tpu_custom_call" | custom-call | flops 352321536 | bytes 6291456 | tf_op jit(solution)/shard_map/backward_near/pallas_call | solution.py:446
  99.4 2.1 %collective-permute-start.32 = (bf16[1152,128]{1,0:T(8,128)(2,1)S(1)}, bf16[1152,128]{1,0:T(8,128)(2,1)S(1)}, u32[]{:S(2)}, u32[]{:S(2)}) collective-permute-start(bf16[1152,128]{1,0:T(8,128)(2,1)S(1)} %pad_maximum_fusion.3), channel_id=1, source_target_pairs={{0,224},{8,40},{16,240},{24,56},{32,0},{40,72},{48,16},{56,88},{64... | collective-permute-start | bytes 884744 | tf_op jit(solution)/shard_map/ppermute | solution.py:47
  101.5 4.3 %collective-permute-done.28.up2 = bf16[1152,128]{1,0:T(8,128)(2,1)S(1)} collective-permute-done((bf16[1152,128]{1,0:T(8,128)(2,1)S(1)}, bf16[1152,128]{1,0:T(8,128)(2,1)S(1)}, u32[]{:S(2)}, u32[]{:S(2)}) %collective-permute-start.28) | collective-permute-done | bytes 294944 | tf_op jit(solution)/shard_map/ppermute | solution.py:47
  107.7 2.3 %collective-permute-start.33 = (bf16[1152,128]{1,0:T(8,128)(2,1)S(1)}, bf16[1152,128]{1,0:T(8,128)(2,1)S(1)}, u32[]{:S(2)}, u32[]{:S(2)}) collective-permute-start(bf16[1152,128]{1,0:T(8,128)(2,1)S(1)} %pad_maximum_fusion.4), channel_id=1, source_target_pairs={{0,224},{8,40},{16,240},{24,56},{32,0},{40,72},{48,16},{56,88},{64... | collective-permute-start | bytes 884744 | tf_op jit(solution)/shard_map/ppermute | solution.py:47
  110.0 3.0 %collective-permute-done.29.up3 = bf16[1152,128]{1,0:T(8,128)(2,1)S(1)} collective-permute-done((bf16[1152,128]{1,0:T(8,128)(2,1)S(1)}, bf16[1152,128]{1,0:T(8,128)(2,1)S(1)}, u32[]{:S(2)}, u32[]{:S(2)}) %collective-permute-start.29) | collective-permute-done | bytes 294944 | tf_op jit(solution)/shard_map/ppermute | solution.py:47
  113.1 3.2 %collective-permute-start.30 = (bf16[1152,128]{1,0:T(8,128)(2,1)S(1)}, bf16[1152,128]{1,0:T(8,128)(2,1)S(1)}, u32[]{:S(2)}, u32[]{:S(2)}) collective-permute-start(bf16[1152,128]{1,0:T(8,128)(2,1)S(1)} %pad_maximum_fusion.2), channel_id=1, source_target_pairs={{0,32},{8,232},{16,48},{24,248},{32,64},{40,8},{48,80},{56,24},{64... | collective-permute-start | bytes 884744 | tf_op jit(solution)/shard_map/ppermute | solution.py:47
  117.5 5.9 %collective-permute-done.34.down4 = bf16[1024,128]{1,0:T(8,128)(2,1)S(1)} collective-permute-done((bf16[1024,128]{1,0:T(8,128)(2,1)S(1)}, bf16[1024,128]{1,0:T(8,128)(2,1)S(1)}, u32[]{:S(2)}, u32[]{:S(2)}) %collective-permute-start.34) | collective-permute-done | bytes 262176 | tf_op jit(solution)/shard_map/ppermute | solution.py:47
  123.5 2.4 %collective-permute-start.35 = (bf16[640,128]{1,0:T(8,128)(2,1)S(1)}, bf16[640,128]{1,0:T(8,128)(2,1)S(1)}, u32[]{:S(2)}, u32[]{:S(2)}) collective-permute-start(bf16[640,128]{1,0:T(8,128)(2,1)S(1)} %get-tuple-element.53.sent), channel_id=1, source_target_pairs={{0,16},{8,24},{16,0},{24,8},{32,48},{40,56},{48,32},{56,40},{64,80... | collective-permute-start | bytes 491528 | tf_op jit(solution)/shard_map/ppermute | solution.py:33
  126.9 3.0 %collective-permute-done.36.w_lo = bf16[128,128]{1,0:T(8,128)(2,1)S(1)} collective-permute-done((bf16[128,128]{1,0:T(8,128)(2,1)S(1)}, bf16[128,128]{1,0:T(8,128)(2,1)S(1)}, u32[]{:S(2)}, u32[]{:S(2)}) %collective-permute-start.36) | collective-permute-done | bytes 32800 | tf_op jit(solution)/shard_map/ppermute | solution.py:549
  130.9 8.8 %collective-permute-start.38 = (bf16[768,128]{1,0:T(8,128)(2,1)S(1)}, bf16[768,128]{1,0:T(8,128)(2,1)S(1)}, u32[]{:S(2)}, u32[]{:S(2)}) collective-permute-start(bf16[768,128]{1,0:T(8,128)(2,1)S(1)} %get-tuple-element.55), channel_id=1, source_target_pairs={{0,8},{8,0},{16,24},{24,16},{32,40},{40,32},{48,56},{56,48},{64,72... | collective-permute-start | bytes 589832 | tf_op jit(solution)/shard_map/ppermute | solution.py:33
  (93 shorter events, 32.1 us)
Async XLA Ops:
  0.6 8.7 %collective-permute-start = (bf16[256,256]{1,0:T(8,128)(2,1)}, bf16[256,256]{1,0:T(8,128)(2,1)S(1)}, u32[]{:S(2)}, u32[]{:S(2)}) collective-permute-start(bf16[256,256]{1,0:T(8,128)(2,1)} %bitcast.51), channel_id=1, source_target_pairs={{0,16},{8,24},{16,0},{24,8},{32,48},{40,56},{48,32},{56,40},{64,80... | collective-permute-start | bytes 393224 | tf_op jit(solution)/shard_map/ppermute | solution.py:33
  4.3 37.0 %collective-permute-start.2 = (bf16[12,256,256]{2,1,0:T(8,128)(2,1)}, bf16[12,256,256]{2,1,0:T(8,128)(2,1)S(1)}, u32[]{:S(2)}, u32[]{:S(2)}) collective-permute-start(bf16[12,256,256]{2,1,0:T(8,128)(2,1)} %bitcast.42), channel_id=1, source_target_pairs={{0,8},{8,0},{16,24},{24,16},{32,40},{40,32},{48,56},{56,48},{64,72... | collective-permute-start | bytes 4718600 | tf_op jit(solution)/shard_map/ppermute | solution.py:33
  11.8 8.5 %collective-permute-start.3 = (bf16[4,256,128]{2,1,0:T(8,128)(2,1)S(1)}, bf16[4,256,128]{2,1,0:T(8,128)(2,1)S(1)}, u32[]{:S(2)}, u32[]{:S(2)}) collective-permute-start(bf16[4,256,128]{2,1,0:T(8,128)(2,1)S(1)} %pad_maximum_fusion.5.refs_0_), channel_id=1, source_target_pairs={{0,224},{8,40},{16,240},{24,56},{32,0},{40,72},{48,16},{56,88},{64... | collective-permute-start | bytes 786440 | tf_op jit(solution)/shard_map/ppermute | solution.py:47
  12.6 9.7 %collective-permute-start.6 = (bf16[4,256,128]{2,1,0:T(8,128)(2,1)S(1)}, bf16[4,256,128]{2,1,0:T(8,128)(2,1)S(1)}, u32[]{:S(2)}, u32[]{:S(2)}) collective-permute-start(bf16[4,256,128]{2,1,0:T(8,128)(2,1)S(1)} %pad_maximum_fusion.5.refs_0_), channel_id=1, source_target_pairs={{0,32},{8,232},{16,48},{24,248},{32,64},{40,8},{48,80},{56,24},{64... | collective-permute-start | bytes 786440 | tf_op jit(solution)/shard_map/ppermute | solution.py:47
  20.3 6.6 %collective-permute-start.4 = (bf16[4,256,128]{2,1,0:T(8,128)(2,1)S(1)}, bf16[4,256,128]{2,1,0:T(8,128)(2,1)S(1)}, u32[]{:S(2)}, u32[]{:S(2)}) collective-permute-start(bf16[4,256,128]{2,1,0:T(8,128)(2,1)S(1)} %collective-permute-done.3.refs_1_), channel_id=1, source_target_pairs={{0,224},{8,40},{16,240},{24,56},{32,0},{40,72},{48,16},{56,88},{64... | collective-permute-start | bytes 786440 | tf_op jit(solution)/shard_map/ppermute | solution.py:47
  22.3 8.2 %collective-permute-start.7 = (bf16[4,256,128]{2,1,0:T(8,128)(2,1)S(1)}, bf16[4,256,128]{2,1,0:T(8,128)(2,1)S(1)}, u32[]{:S(2)}, u32[]{:S(2)}) collective-permute-start(bf16[4,256,128]{2,1,0:T(8,128)(2,1)S(1)} %collective-permute-done.6.refs_6_), channel_id=1, source_target_pairs={{0,32},{8,232},{16,48},{24,248},{32,64},{40,8},{48,80},{56,24},{64... | collective-permute-start | bytes 786440 | tf_op jit(solution)/shard_map/ppermute | solution.py:47
  26.9 9.3 %collective-permute-start.5 = (bf16[4,256,128]{2,1,0:T(8,128)(2,1)S(1)}, bf16[4,256,128]{2,1,0:T(8,128)(2,1)S(1)}, u32[]{:S(2)}, u32[]{:S(2)}) collective-permute-start(bf16[4,256,128]{2,1,0:T(8,128)(2,1)S(1)} %collective-permute-done.4.refs_2_), channel_id=1, source_target_pairs={{0,224},{8,40},{16,240},{24,56},{32,0},{40,72},{48,16},{56,88},{64... | collective-permute-start | bytes 786440 | tf_op jit(solution)/shard_map/ppermute | solution.py:47
  30.5 7.3 %collective-permute-start.8 = (bf16[4,256,128]{2,1,0:T(8,128)(2,1)S(1)}, bf16[4,256,128]{2,1,0:T(8,128)(2,1)S(1)}, u32[]{:S(2)}, u32[]{:S(2)}) collective-permute-start(bf16[4,256,128]{2,1,0:T(8,128)(2,1)S(1)} %collective-permute-done.7.refs_5_), channel_id=1, source_target_pairs={{0,32},{8,232},{16,48},{24,248},{32,64},{40,8},{48,80},{56,24},{64... | collective-permute-start | bytes 786440 | tf_op jit(solution)/shard_map/ppermute | solution.py:47
  36.2 7.1 %collective-permute-start.10 = (bf16[2,256,128]{2,1,0:T(8,128)(2,1)S(1)}, bf16[2,256,128]{2,1,0:T(8,128)(2,1)S(1)}, u32[]{:S(2)}, u32[]{:S(2)}) collective-permute-start(bf16[2,256,128]{2,1,0:T(8,128)(2,1)S(1)} %slice.127), channel_id=1, source_target_pairs={{0,224},{8,40},{16,240},{24,56},{32,0},{40,72},{48,16},{56,88},{64... | collective-permute-start | bytes 393224 | tf_op jit(solution)/shard_map/ppermute | solution.py:47
  37.8 5.5 %collective-permute-start.9 = (bf16[2,256,128]{2,1,0:T(8,128)(2,1)S(1)}, bf16[2,256,128]{2,1,0:T(8,128)(2,1)S(1)}, u32[]{:S(2)}, u32[]{:S(2)}) collective-permute-start(bf16[2,256,128]{2,1,0:T(8,128)(2,1)S(1)} %slice.126), channel_id=1, source_target_pairs={{0,32},{8,232},{16,48},{24,248},{32,64},{40,8},{48,80},{56,24},{64... | collective-permute-start | bytes 393224 | tf_op jit(solution)/shard_map/ppermute | solution.py:47
  44.2 6.8 %collective-permute-start.11 = (bf16[2,256,128]{2,1,0:T(8,128)(2,1)S(1)}, bf16[2,256,128]{2,1,0:T(8,128)(2,1)S(1)}, u32[]{:S(2)}, u32[]{:S(2)}) collective-permute-start(bf16[2,256,128]{2,1,0:T(8,128)(2,1)S(1)} %get-tuple-element.39), channel_id=1, source_target_pairs={{0,6},{1,7},{2,4},{3,5},{4,2},{5,3},{6,0},{7,1},{8,14},{9,15},{10,... | collective-permute-start | bytes 393224 | tf_op jit(solution)/shard_map/ppermute | solution.py:38
  46.6 6.9 %collective-permute-start.12 = (bf16[2,256,128]{2,1,0:T(8,128)(2,1)S(1)}, bf16[2,256,128]{2,1,0:T(8,128)(2,1)S(1)}, u32[]{:S(2)}, u32[]{:S(2)}) collective-permute-start(bf16[2,256,128]{2,1,0:T(8,128)(2,1)S(1)} %get-tuple-element.40), channel_id=1, source_target_pairs={{0,2},{1,3},{2,0},{3,1},{4,6},{5,7},{6,4},{7,5},{8,10},{9,11},{10,... | collective-permute-start | bytes 393224 | tf_op jit(solution)/shard_map/ppermute | solution.py:38
  47.3 7.4 %collective-permute-start.13 = (bf16[2,256,128]{2,1,0:T(8,128)(2,1)S(1)}, bf16[2,256,128]{2,1,0:T(8,128)(2,1)S(1)}, u32[]{:S(2)}, u32[]{:S(2)}) collective-permute-start(bf16[2,256,128]{2,1,0:T(8,128)(2,1)S(1)} %get-tuple-element.41), channel_id=1, source_target_pairs={{0,5},{1,6},{2,7},{3,4},{4,1},{5,2},{6,3},{7,0},{8,13},{9,14},{10,... | collective-permute-start | bytes 393224 | tf_op jit(solution)/shard_map/ppermute | solution.py:38
  50.9 5.0 %collective-permute-start.15 = (bf16[2,256,128]{2,1,0:T(8,128)(2,1)S(1)}, bf16[2,256,128]{2,1,0:T(8,128)(2,1)S(1)}, u32[]{:S(2)}, u32[]{:S(2)}) collective-permute-start(bf16[2,256,128]{2,1,0:T(8,128)(2,1)S(1)} %get-tuple-element.43), channel_id=1, source_target_pairs={{0,1},{1,2},{2,3},{3,0},{4,5},{5,6},{6,7},{7,4},{8,9},{9,10},{10,1... | collective-permute-start | bytes 393224 | tf_op jit(solution)/shard_map/ppermute | solution.py:38
  51.0 5.1 %collective-permute-start.16 = (bf16[2,256,128]{2,1,0:T(8,128)(2,1)S(1)}, bf16[2,256,128]{2,1,0:T(8,128)(2,1)S(1)}, u32[]{:S(2)}, u32[]{:S(2)}) collective-permute-start(bf16[2,256,128]{2,1,0:T(8,128)(2,1)S(1)} %get-tuple-element.44), channel_id=1, source_target_pairs={{0,3},{1,0},{2,1},{3,2},{4,7},{5,4},{6,5},{7,6},{8,11},{9,8},{10,9... | collective-permute-start | bytes 393224 | tf_op jit(solution)/shard_map/ppermute | solution.py:38
  57.8 12.0 %collective-permute-start.18 = (f32[512,128]{1,0:T(8,128)S(1)}, f32[512,128]{1,0:T(8,128)S(1)}, u32[]{:S(2)}, u32[]{:S(2)}) collective-permute-start(f32[512,128]{1,0:T(8,128)S(1)} %bitcast.49), channel_id=1, source_target_pairs={{0,8},{8,0},{16,24},{24,16},{32,40},{40,32},{48,56},{56,48},{64,72... | collective-permute-start | bytes 786440 | tf_op jit(solution)/shard_map/ppermute | solution.py:33
  71.4 7.9 %collective-permute-start.20 = (bf16[640,128]{1,0:T(8,128)(2,1)S(1)}, bf16[640,128]{1,0:T(8,128)(2,1)S(1)}, u32[]{:S(2)}, u32[]{:S(2)}) collective-permute-start(bf16[640,128]{1,0:T(8,128)(2,1)S(1)} %get-tuple-element.48), channel_id=1, source_target_pairs={{0,6},{1,7},{2,4},{3,5},{4,2},{5,3},{6,0},{7,1},{8,14},{9,15},{10,... | collective-permute-start | bytes 491528 | tf_op jit(solution)/shard_map/ppermute | solution.py:38
  72.5 14.8 %collective-permute-start.21 = (bf16[640,128]{1,0:T(8,128)(2,1)S(1)}, bf16[640,128]{1,0:T(8,128)(2,1)S(1)}, u32[]{:S(2)}, u32[]{:S(2)}) collective-permute-start(bf16[640,128]{1,0:T(8,128)(2,1)S(1)} %get-tuple-element.47.refs_0_), channel_id=1, source_target_pairs={{0,2},{1,3},{2,0},{3,1},{4,6},{5,7},{6,4},{7,5},{8,10},{9,11},{10,... | collective-permute-start | bytes 491528 | tf_op jit(solution)/shard_map/ppermute | solution.py:38
  74.9 13.1 %collective-permute-start.22 = (bf16[640,128]{1,0:T(8,128)(2,1)S(1)}, bf16[640,128]{1,0:T(8,128)(2,1)S(1)}, u32[]{:S(2)}, u32[]{:S(2)}) collective-permute-start(bf16[640,128]{1,0:T(8,128)(2,1)S(1)} %get-tuple-element.48), channel_id=1, source_target_pairs={{0,5},{1,6},{2,7},{3,4},{4,1},{5,2},{6,3},{7,0},{8,13},{9,14},{10,... | collective-permute-start | bytes 491528 | tf_op jit(solution)/shard_map/ppermute | solution.py:38
  74.9 13.1 %collective-permute-start.23 = (bf16[640,128]{1,0:T(8,128)(2,1)S(1)}, bf16[640,128]{1,0:T(8,128)(2,1)S(1)}, u32[]{:S(2)}, u32[]{:S(2)}) collective-permute-start(bf16[640,128]{1,0:T(8,128)(2,1)S(1)} %get-tuple-element.48), channel_id=1, source_target_pairs={{0,7},{1,4},{2,5},{3,6},{4,3},{5,0},{6,1},{7,2},{8,15},{9,12},{10,... | collective-permute-start | bytes 491528 | tf_op jit(solution)/shard_map/ppermute | solution.py:38
  78.5 12.0 %collective-permute-start.24 = (bf16[640,128]{1,0:T(8,128)(2,1)S(1)}, bf16[640,128]{1,0:T(8,128)(2,1)S(1)}, u32[]{:S(2)}, u32[]{:S(2)}) collective-permute-start(bf16[640,128]{1,0:T(8,128)(2,1)S(1)} %get-tuple-element.47.refs_0_), channel_id=1, source_target_pairs={{0,1},{1,2},{2,3},{3,0},{4,5},{5,6},{6,7},{7,4},{8,9},{9,10},{10,1... | collective-permute-start | bytes 491528 | tf_op jit(solution)/shard_map/ppermute | solution.py:38
  79.2 11.3 %collective-permute-start.25 = (bf16[640,128]{1,0:T(8,128)(2,1)S(1)}, bf16[640,128]{1,0:T(8,128)(2,1)S(1)}, u32[]{:S(2)}, u32[]{:S(2)}) collective-permute-start(bf16[640,128]{1,0:T(8,128)(2,1)S(1)} %get-tuple-element.47.refs_0_), channel_id=1, source_target_pairs={{0,3},{1,0},{2,1},{3,2},{4,7},{5,4},{6,5},{7,6},{8,11},{9,8},{10,9... | collective-permute-start | bytes 491528 | tf_op jit(solution)/shard_map/ppermute | solution.py:38
  87.3 5.2 %collective-permute-start.26 = (bf16[640,128]{1,0:T(8,128)(2,1)S(1)}, bf16[640,128]{1,0:T(8,128)(2,1)S(1)}, u32[]{:S(2)}, u32[]{:S(2)}) collective-permute-start(bf16[640,128]{1,0:T(8,128)(2,1)S(1)} %get-tuple-element.48), channel_id=1, source_target_pairs={{0,4},{1,5},{2,6},{3,7},{4,0},{5,1},{6,2},{7,3},{8,12},{9,13},{10,... | collective-permute-start | bytes 491528 | tf_op jit(solution)/shard_map/ppermute | solution.py:38
  93.4 5.5 %collective-permute-start.31 = (bf16[640,128]{1,0:T(8,128)(2,1)S(1)}, bf16[640,128]{1,0:T(8,128)(2,1)S(1)}, u32[]{:S(2)}, u32[]{:S(2)}) collective-permute-start(bf16[640,128]{1,0:T(8,128)(2,1)S(1)} %get-tuple-element.51), channel_id=1, source_target_pairs={{0,224},{8,40},{16,240},{24,56},{32,0},{40,72},{48,16},{56,88},{64... | collective-permute-start | bytes 491528 | tf_op jit(solution)/shard_map/ppermute | solution.py:47
  98.9 6.8 %collective-permute-start.28 = (bf16[1152,128]{1,0:T(8,128)(2,1)S(1)}, bf16[1152,128]{1,0:T(8,128)(2,1)S(1)}, u32[]{:S(2)}, u32[]{:S(2)}) collective-permute-start(bf16[1152,128]{1,0:T(8,128)(2,1)S(1)} %pad_maximum_fusion), channel_id=1, source_target_pairs={{0,32},{8,232},{16,48},{24,248},{32,64},{40,8},{48,80},{56,24},{64... | collective-permute-start | bytes 884744 | tf_op jit(solution)/shard_map/ppermute | solution.py:47
  99.4 8.2 %collective-permute-start.32 = (bf16[1152,128]{1,0:T(8,128)(2,1)S(1)}, bf16[1152,128]{1,0:T(8,128)(2,1)S(1)}, u32[]{:S(2)}, u32[]{:S(2)}) collective-permute-start(bf16[1152,128]{1,0:T(8,128)(2,1)S(1)} %pad_maximum_fusion.3), channel_id=1, source_target_pairs={{0,224},{8,40},{16,240},{24,56},{32,0},{40,72},{48,16},{56,88},{64... | collective-permute-start | bytes 884744 | tf_op jit(solution)/shard_map/ppermute | solution.py:47
  105.9 7.0 %collective-permute-start.29 = (bf16[1152,128]{1,0:T(8,128)(2,1)S(1)}, bf16[1152,128]{1,0:T(8,128)(2,1)S(1)}, u32[]{:S(2)}, u32[]{:S(2)}) collective-permute-start(bf16[1152,128]{1,0:T(8,128)(2,1)S(1)} %pad_maximum_fusion.1), channel_id=1, source_target_pairs={{0,32},{8,232},{16,48},{24,248},{32,64},{40,8},{48,80},{56,24},{64... | collective-permute-start | bytes 884744 | tf_op jit(solution)/shard_map/ppermute | solution.py:47
  107.7 8.6 %collective-permute-start.33 = (bf16[1152,128]{1,0:T(8,128)(2,1)S(1)}, bf16[1152,128]{1,0:T(8,128)(2,1)S(1)}, u32[]{:S(2)}, u32[]{:S(2)}) collective-permute-start(bf16[1152,128]{1,0:T(8,128)(2,1)S(1)} %pad_maximum_fusion.4), channel_id=1, source_target_pairs={{0,224},{8,40},{16,240},{24,56},{32,0},{40,72},{48,16},{56,88},{64... | collective-permute-start | bytes 884744 | tf_op jit(solution)/shard_map/ppermute | solution.py:47
  113.1 10.2 %collective-permute-start.30 = (bf16[1152,128]{1,0:T(8,128)(2,1)S(1)}, bf16[1152,128]{1,0:T(8,128)(2,1)S(1)}, u32[]{:S(2)}, u32[]{:S(2)}) collective-permute-start(bf16[1152,128]{1,0:T(8,128)(2,1)S(1)} %pad_maximum_fusion.2), channel_id=1, source_target_pairs={{0,32},{8,232},{16,48},{24,248},{32,64},{40,8},{48,80},{56,24},{64... | collective-permute-start | bytes 884744 | tf_op jit(solution)/shard_map/ppermute | solution.py:47
  116.4 6.9 %collective-permute-start.34 = (bf16[1024,128]{1,0:T(8,128)(2,1)S(1)}, bf16[1024,128]{1,0:T(8,128)(2,1)S(1)}, u32[]{:S(2)}, u32[]{:S(2)}) collective-permute-start(bf16[1024,128]{1,0:T(8,128)(2,1)S(1)} %fusion), channel_id=1, source_target_pairs={{0,224},{8,40},{16,240},{24,56},{32,0},{40,72},{48,16},{56,88},{64... | collective-permute-start | bytes 786440 | tf_op jit(solution)/shard_map/ppermute | solution.py:47
  123.5 7.4 %collective-permute-start.35 = (bf16[640,128]{1,0:T(8,128)(2,1)S(1)}, bf16[640,128]{1,0:T(8,128)(2,1)S(1)}, u32[]{:S(2)}, u32[]{:S(2)}) collective-permute-start(bf16[640,128]{1,0:T(8,128)(2,1)S(1)} %get-tuple-element.53.sent), channel_id=1, source_target_pairs={{0,16},{8,24},{16,0},{24,8},{32,48},{40,56},{48,32},{56,40},{64,80... | collective-permute-start | bytes 491528 | tf_op jit(solution)/shard_map/ppermute | solution.py:33
  130.9 9.9 %collective-permute-start.38 = (bf16[768,128]{1,0:T(8,128)(2,1)S(1)}, bf16[768,128]{1,0:T(8,128)(2,1)S(1)}, u32[]{:S(2)}, u32[]{:S(2)}) collective-permute-start(bf16[768,128]{1,0:T(8,128)(2,1)S(1)} %get-tuple-element.55), channel_id=1, source_target_pairs={{0,8},{8,0},{16,24},{24,16},{32,40},{40,32},{48,56},{56,48},{64,72... | collective-permute-start | bytes 589832 | tf_op jit(solution)/shard_map/ppermute | solution.py:33
  (13 other events, 119.3 us)

commit v14 on v11

--- a/solution.py
+++ b/solution.py
@@ -465,6 +465,17 @@
     )(agg_own, agg_other, weight, cot_own, cot_other)
 
 
+def enter_kernel(in_step_any, up, down, up_out, down_out):
+    del in_step_any
+    up_out[...] = up[...]
+    down_out[...] = down[...]
+
+
+def enter(in_step, up, down):
+    message = shape(2 * TILE + W_ROWS, HALF)
+    return local(enter_kernel, (message, message), 3, "enter", any_in=1)(in_step, up, down)
+
+
 def ring_end(parts, *messages):
     return local(
         ring_end_kernel,
@@ -540,7 +551,9 @@
     received += [forward(received[1], received[2], 0), forward(received[3], received[4], 1)]
 
     half, size = 2 * TILE, QUAD * TILE
+    in_step = quad_permute(received[-1][:16], 1)
     own, own_down, back = backward_far(lists, adj0, adj1, received)
+    own, own_down = enter(in_step, own, own_down)
     blocks = backward_near(lists, adj0, adj1, back)
     parts = blocks.reshape(NZ, size, HALF)
     up1, down1 = z_shift(own, 1), z_shift(own_down, -1)

time: 139 us -> 140 us (level)
  starting transfers between devices: 70.7 us -> 72.9 us
  Pallas kernels: 10.2 us -> 8.6 us
    ppermute x16, waiting for transfers between devices: 33.4 us -> 35.9 us  [z_shift(): return lax.ppermute(x, 'row', row_pairs(lambda z, q: (z + step, q)))]
    ppermute x1, starting transfers between devices: 0.01 us -> 2.17 us  [per_device(): w_lo = lax.ppermute(w_send, 'col', [(c, c ^ 4) for c in range(NCOL)])]
    ppermute x14, waiting for transfers between devices: 13.3 us -> 11.9 us  [col_move(): return lax.ppermute(x, 'col', pairs)]
    ppermute x7 -> x8, starting transfers between devices: 23.5 us -> 23.7 us  [quad_permute(): return lax.ppermute(x, 'row', row_pairs(lambda z, q: (z, q ^ flip)))]
    ppermute x7 -> x8, waiting for transfers between devices: 3.3 us -> 3.3 us  [quad_permute(): return lax.ppermute(x, 'row', row_pairs(lambda z, q: (z, q ^ flip)))]
  transfers between devices with their start and end apart: 39 -> 40, of which waited for: 19 -> 19; matrix products, arithmetic and copies ran while one was open for 1% -> 1% of each run, Pallas kernels for 4% -> 4%
where the time goes in v14:
time: 140 us; the launch traced here: 141 us
  starting transfers between devices  72.9 us (52%)
  waiting for transfers between devices  54.4 us (39%)
  Pallas kernels  8.6 us (6%)
  local copies, waits for them, and re-layouts  2.42 us (2%)
  between operations  1.73 us (1%)
    ppermute x16, waiting for transfers between devices, z_shift(): return lax.ppermute(x, 'row', row_pairs(lambda z, q: (z + step, q)))  35.9 us
    ppermute x16, starting transfers between devices, z_shift(): return lax.ppermute(x, 'row', row_pairs(lambda z, q: (z + step, q)))  26.9 us
    ppermute x8, starting transfers between devices, quad_permute(): return lax.ppermute(x, 'row', row_pairs(lambda z, q: (z, q ^ flip)))  23.7 us
    ppermute x14, starting transfers between devices, col_move(): return lax.ppermute(x, 'col', pairs)  19.3 us
    ppermute x14, waiting for transfers between devices, col_move(): return lax.ppermute(x, 'col', pairs)  11.9 us
    ppermute x8, waiting for transfers between devices, quad_permute(): return lax.ppermute(x, 'row', row_pairs(lambda z, q: (z, q ^ flip)))  3.3 us
  transfers between devices with their start and end apart: 40, of which 19 were waited for; matrix products, arithmetic and copies ran while one was open for 1% of the time, Pallas kernels for 4%

profile of v14, /device:TPU:1, one launch (start us, length us, event | category | flops | bytes accessed | tf_op | source)
XLA Modules:
  0.0 140.8 jit_solution(13786477837358927067)
XLA Ops:
  0.6 3.7 %collective-permute-start = (bf16[256,256]{1,0:T(8,128)(2,1)}, bf16[256,256]{1,0:T(8,128)(2,1)S(1)}, u32[]{:S(2)}, u32[]{:S(2)}) collective-permute-start(bf16[256,256]{1,0:T(8,128)(2,1)} %bitcast.51), channel_id=1, source_target_pairs={{0,16},{8,24},{16,0},{24,8},{32,48},{40,56},{48,32},{56,40},{64,80... | collective-permute-start | bytes 393224 | tf_op jit(solution)/shard_map/ppermute | solution.py:34
  11.8 4.7 %collective-permute-start.3 = (bf16[4,256,128]{2,1,0:T(8,128)(2,1)S(1)}, bf16[4,256,128]{2,1,0:T(8,128)(2,1)S(1)}, u32[]{:S(2)}, u32[]{:S(2)}) collective-permute-start(bf16[4,256,128]{2,1,0:T(8,128)(2,1)S(1)} %pad_maximum_fusion.5.refs_0_), channel_id=1, source_target_pairs={{0,224},{8,232},{16,240},{24,248},{32,0},{40,8},{48,16},{56,24},{6... | collective-permute-start | bytes 786440 | tf_op jit(solution)/shard_map/ppermute | solution.py:48
  16.5 5.6 %collective-permute-done.3.refs_1_ = bf16[4,256,128]{2,1,0:T(8,128)(2,1)S(1)} collective-permute-done((bf16[4,256,128]{2,1,0:T(8,128)(2,1)S(1)}, bf16[4,256,128]{2,1,0:T(8,128)(2,1)S(1)}, u32[]{:S(2)}, u32[]{:S(2)}) %collective-permute-start.3) | collective-permute-done | bytes 262176 | tf_op jit(solution)/shard_map/ppermute | solution.py:48
  22.1 3.4 %collective-permute-start.4 = (bf16[4,256,128]{2,1,0:T(8,128)(2,1)S(1)}, bf16[4,256,128]{2,1,0:T(8,128)(2,1)S(1)}, u32[]{:S(2)}, u32[]{:S(2)}) collective-permute-start(bf16[4,256,128]{2,1,0:T(8,128)(2,1)S(1)} %collective-permute-done.3.refs_1_), channel_id=1, source_target_pairs={{0,224},{8,232},{16,240},{24,248},{32,0},{40,8},{48,16},{56,24},{6... | collective-permute-start | bytes 786440 | tf_op jit(solution)/shard_map/ppermute | solution.py:48
  25.5 4.6 %collective-permute-done.4.refs_2_ = bf16[4,256,128]{2,1,0:T(8,128)(2,1)S(1)} collective-permute-done((bf16[4,256,128]{2,1,0:T(8,128)(2,1)S(1)}, bf16[4,256,128]{2,1,0:T(8,128)(2,1)S(1)}, u32[]{:S(2)}, u32[]{:S(2)}) %collective-permute-start.4) | collective-permute-done | bytes 262176 | tf_op jit(solution)/shard_map/ppermute | solution.py:48
  30.1 3.4 %collective-permute-start.5 = (bf16[4,256,128]{2,1,0:T(8,128)(2,1)S(1)}, bf16[4,256,128]{2,1,0:T(8,128)(2,1)S(1)}, u32[]{:S(2)}, u32[]{:S(2)}) collective-permute-start(bf16[4,256,128]{2,1,0:T(8,128)(2,1)S(1)} %collective-permute-done.4.refs_2_), channel_id=1, source_target_pairs={{0,224},{8,232},{16,240},{24,248},{32,0},{40,8},{48,16},{56,24},{6... | collective-permute-start | bytes 786440 | tf_op jit(solution)/shard_map/ppermute | solution.py:48
  33.6 3.7 %collective-permute-done.5.refs_3_ = bf16[4,256,128]{2,1,0:T(8,128)(2,1)S(1)} collective-permute-done((bf16[4,256,128]{2,1,0:T(8,128)(2,1)S(1)}, bf16[4,256,128]{2,1,0:T(8,128)(2,1)S(1)}, u32[]{:S(2)}, u32[]{:S(2)}) %collective-permute-start.5) | collective-permute-done | bytes 262176 | tf_op jit(solution)/shard_map/ppermute | solution.py:48
  37.3 3.5 %collective-permute-start.10 = (bf16[2,256,128]{2,1,0:T(8,128)(2,1)S(1)}, bf16[2,256,128]{2,1,0:T(8,128)(2,1)S(1)}, u32[]{:S(2)}, u32[]{:S(2)}) collective-permute-start(bf16[2,256,128]{2,1,0:T(8,128)(2,1)S(1)} %slice.163), channel_id=1, source_target_pairs={{0,224},{8,232},{16,240},{24,248},{32,0},{40,8},{48,16},{56,24},{6... | collective-permute-start | bytes 393224 | tf_op jit(solution)/shard_map/ppermute | solution.py:48
  40.9 2.0 %forward_near.1 = (f32[18,256,128]{2,1,0:T(8,128)S(1)}, s32[68]{0:T(128)S(1)}) custom-call(s32[25]{0:T(128)S(1)} %get-tuple-element.33.own_any, s32[25]{0:T(128)S(1)} %fusion.6.partner_any, bf16[12,256,256]{2,1,0:T(8,128)(2,1)S(1)} %bitcast.43, bf16[12,256,256]{2,1,0:T(8,128)(2,1)S(1)} %collective-permute-done.2.adj1, ...), custom_call_target="tpu_custom_call" | custom-call | flops 352321536 | bytes 6291456 | tf_op jit(solution)/shard_map/forward_near/pallas_call | solution.py:399
  43.0 3.0 %collective-permute-done.9.far_a = bf16[2,256,128]{2,1,0:T(8,128)(2,1)S(1)} collective-permute-done((bf16[2,256,128]{2,1,0:T(8,128)(2,1)S(1)}, bf16[2,256,128]{2,1,0:T(8,128)(2,1)S(1)}, u32[]{:S(2)}, u32[]{:S(2)}) %collective-permute-start.9) | collective-permute-done | bytes 131104 | tf_op jit(solution)/shard_map/ppermute | solution.py:48
  46.6 2.7 %collective-permute-start.11 = (bf16[2,256,128]{2,1,0:T(8,128)(2,1)S(1)}, bf16[2,256,128]{2,1,0:T(8,128)(2,1)S(1)}, u32[]{:S(2)}, u32[]{:S(2)}) collective-permute-start(bf16[2,256,128]{2,1,0:T(8,128)(2,1)S(1)} %get-tuple-element.41), channel_id=1, source_target_pairs={{0,6},{1,7},{2,4},{3,5},{4,2},{5,3},{6,0},{7,1},{8,14},{9,15},{10,... | collective-permute-start | bytes 393224 | tf_op jit(solution)/shard_map/ppermute | solution.py:39
  49.7 2.2 %collective-permute-start.13 = (bf16[2,256,128]{2,1,0:T(8,128)(2,1)S(1)}, bf16[2,256,128]{2,1,0:T(8,128)(2,1)S(1)}, u32[]{:S(2)}, u32[]{:S(2)}) collective-permute-start(bf16[2,256,128]{2,1,0:T(8,128)(2,1)S(1)} %get-tuple-element.43), channel_id=1, source_target_pairs={{0,5},{1,6},{2,7},{3,4},{4,1},{5,2},{6,3},{7,0},{8,13},{9,14},{10,... | collective-permute-start | bytes 393224 | tf_op jit(solution)/shard_map/ppermute | solution.py:39
  51.9 2.0 %collective-permute-start.14 = (bf16[2,256,128]{2,1,0:T(8,128)(2,1)S(1)}, bf16[2,256,128]{2,1,0:T(8,128)(2,1)S(1)}, u32[]{:S(2)}, u32[]{:S(2)}) collective-permute-start(bf16[2,256,128]{2,1,0:T(8,128)(2,1)S(1)} %get-tuple-element.44), channel_id=1, source_target_pairs={{0,7},{1,4},{2,5},{3,6},{4,3},{5,0},{6,1},{7,2},{8,15},{9,12},{10,... | collective-permute-start | bytes 393224 | tf_op jit(solution)/shard_map/ppermute | solution.py:39
  53.8 2.7 %collective-permute-start.16 = (bf16[2,256,128]{2,1,0:T(8,128)(2,1)S(1)}, bf16[2,256,128]{2,1,0:T(8,128)(2,1)S(1)}, u32[]{:S(2)}, u32[]{:S(2)}) collective-permute-start(bf16[2,256,128]{2,1,0:T(8,128)(2,1)S(1)} %get-tuple-element.46), channel_id=1, source_target_pairs={{0,3},{1,0},{2,1},{3,2},{4,7},{5,4},{6,5},{7,6},{8,11},{9,8},{10,9... | collective-permute-start | bytes 393224 | tf_op jit(solution)/shard_map/ppermute | solution.py:39
  57.2 5.4 %collective-permute-done.15 = bf16[2,256,128]{2,1,0:T(8,128)(2,1)S(1)} collective-permute-done((bf16[2,256,128]{2,1,0:T(8,128)(2,1)S(1)}, bf16[2,256,128]{2,1,0:T(8,128)(2,1)S(1)}, u32[]{:S(2)}, u32[]{:S(2)}) %collective-permute-start.15) | collective-permute-done | bytes 131104 | tf_op jit(solution)/shard_map/ppermute | solution.py:39
  62.7 5.1 %collective-permute-start.18 = (f32[512,128]{1,0:T(8,128)S(1)}, f32[512,128]{1,0:T(8,128)S(1)}, u32[]{:S(2)}, u32[]{:S(2)}) collective-permute-start(f32[512,128]{1,0:T(8,128)S(1)} %bitcast.49), channel_id=1, source_target_pairs={{0,8},{8,0},{16,24},{24,16},{32,40},{40,32},{48,56},{56,48},{64,72... | collective-permute-start | bytes 786440 | tf_op jit(solution)/shard_map/ppermute | solution.py:34
  70.7 1.7 %collective-permute-start.22 = (bf16[640,128]{1,0:T(8,128)(2,1)S(1)}, bf16[640,128]{1,0:T(8,128)(2,1)S(1)}, u32[]{:S(2)}, u32[]{:S(2)}) collective-permute-start(bf16[640,128]{1,0:T(8,128)(2,1)S(1)} %get-tuple-element.49.refs_0_), channel_id=1, source_target_pairs={{0,3},{1,0},{2,1},{3,2},{4,7},{5,4},{6,5},{7,6},{8,11},{9,8},{10,9... | collective-permute-start | bytes 491528 | tf_op jit(solution)/shard_map/ppermute | solution.py:39
  75.9 3.2 %collective-permute-done.22.refs_3_ = bf16[640,128]{1,0:T(8,128)(2,1)S(1)} collective-permute-done((bf16[640,128]{1,0:T(8,128)(2,1)S(1)}, bf16[640,128]{1,0:T(8,128)(2,1)S(1)}, u32[]{:S(2)}, u32[]{:S(2)}) %collective-permute-start.22) | collective-permute-done | bytes 163872 | tf_op jit(solution)/shard_map/ppermute | solution.py:39
  79.1 3.5 %collective-permute-start.26 = (bf16[640,128]{1,0:T(8,128)(2,1)S(1)}, bf16[640,128]{1,0:T(8,128)(2,1)S(1)}, u32[]{:S(2)}, u32[]{:S(2)}) collective-permute-start(bf16[640,128]{1,0:T(8,128)(2,1)S(1)} %pad_maximum_fusion.7), channel_id=1, source_target_pairs={{0,3},{1,0},{2,1},{3,2},{4,7},{5,4},{6,5},{7,6},{8,11},{9,8},{10,9... | collective-permute-start | bytes 491528 | tf_op jit(solution)/shard_map/ppermute | solution.py:39
  82.8 2.1 %collective-permute-done.26.refs_7_ = bf16[640,128]{1,0:T(8,128)(2,1)S(1)} collective-permute-done((bf16[640,128]{1,0:T(8,128)(2,1)S(1)}, bf16[640,128]{1,0:T(8,128)(2,1)S(1)}, u32[]{:S(2)}, u32[]{:S(2)}) %collective-permute-start.26) | collective-permute-done | bytes 163872 | tf_op jit(solution)/shard_map/ppermute | solution.py:39
  84.9 2.1 %collective-permute-start.27 = (bf16[16,128]{1,0:T(8,128)(2,1)S(1)}, bf16[16,128]{1,0:T(8,128)(2,1)S(1)}, u32[]{:S(2)}, u32[]{:S(2)}) collective-permute-start(bf16[16,128]{1,0:T(8,128)(2,1)S(1)} %slice.172), channel_id=1, source_target_pairs={{0,8},{8,0},{16,24},{24,16},{32,40},{40,32},{48,56},{56,48},{64,72... | collective-permute-start | bytes 12296 | tf_op jit(solution)/shard_map/ppermute | solution.py:34
  90.6 2.7 %collective-permute-start.32 = (bf16[640,128]{1,0:T(8,128)(2,1)S(1)}, bf16[640,128]{1,0:T(8,128)(2,1)S(1)}, u32[]{:S(2)}, u32[]{:S(2)}) collective-permute-start(bf16[640,128]{1,0:T(8,128)(2,1)S(1)} %get-tuple-element.55), channel_id=1, source_target_pairs={{0,224},{8,232},{16,240},{24,248},{32,0},{40,8},{48,16},{56,24},{6... | collective-permute-start | bytes 491528 | tf_op jit(solution)/shard_map/ppermute | solution.py:48
  93.3 2.7 %collective-permute-done.28.up1 = bf16[640,128]{1,0:T(8,128)(2,1)S(1)} collective-permute-done((bf16[640,128]{1,0:T(8,128)(2,1)S(1)}, bf16[640,128]{1,0:T(8,128)(2,1)S(1)}, u32[]{:S(2)}, u32[]{:S(2)}) %collective-permute-start.28) | collective-permute-done | bytes 163872 | tf_op jit(solution)/shard_map/ppermute | solution.py:48
  96.3 2.7 %collective-permute-start.33 = (bf16[1152,128]{1,0:T(8,128)(2,1)S(1)}, bf16[1152,128]{1,0:T(8,128)(2,1)S(1)}, u32[]{:S(2)}, u32[]{:S(2)}) collective-permute-start(bf16[1152,128]{1,0:T(8,128)(2,1)S(1)} %pad_maximum_fusion.3), channel_id=1, source_target_pairs={{0,224},{8,232},{16,240},{24,248},{32,0},{40,8},{48,16},{56,24},{6... | collective-permute-start | bytes 884744 | tf_op jit(solution)/shard_map/ppermute | solution.py:48
  99.1 4.2 %collective-permute-done.29.up2 = bf16[1152,128]{1,0:T(8,128)(2,1)S(1)} collective-permute-done((bf16[1152,128]{1,0:T(8,128)(2,1)S(1)}, bf16[1152,128]{1,0:T(8,128)(2,1)S(1)}, u32[]{:S(2)}, u32[]{:S(2)}) %collective-permute-start.29) | collective-permute-done | bytes 294944 | tf_op jit(solution)/shard_map/ppermute | solution.py:48
  103.6 2.8 %collective-permute-start.34 = (bf16[1152,128]{1,0:T(8,128)(2,1)S(1)}, bf16[1152,128]{1,0:T(8,128)(2,1)S(1)}, u32[]{:S(2)}, u32[]{:S(2)}) collective-permute-start(bf16[1152,128]{1,0:T(8,128)(2,1)S(1)} %pad_maximum_fusion.4), channel_id=1, source_target_pairs={{0,224},{8,232},{16,240},{24,248},{32,0},{40,8},{48,16},{56,24},{6... | collective-permute-start | bytes 884744 | tf_op jit(solution)/shard_map/ppermute | solution.py:48
  106.4 5.2 %collective-permute-done.30.up3 = bf16[1152,128]{1,0:T(8,128)(2,1)S(1)} collective-permute-done((bf16[1152,128]{1,0:T(8,128)(2,1)S(1)}, bf16[1152,128]{1,0:T(8,128)(2,1)S(1)}, u32[]{:S(2)}, u32[]{:S(2)}) %collective-permute-start.30) | collective-permute-done | bytes 294944 | tf_op jit(solution)/shard_map/ppermute | solution.py:48
  112.0 3.0 %collective-permute-start.35 = (bf16[1024,128]{1,0:T(8,128)(2,1)S(1)}, bf16[1024,128]{1,0:T(8,128)(2,1)S(1)}, u32[]{:S(2)}, u32[]{:S(2)}) collective-permute-start(bf16[1024,128]{1,0:T(8,128)(2,1)S(1)} %fusion), channel_id=1, source_target_pairs={{0,224},{8,232},{16,240},{24,248},{32,0},{40,8},{48,16},{56,24},{6... | collective-permute-start | bytes 786440 | tf_op jit(solution)/shard_map/ppermute | solution.py:48
  115.0 6.1 %collective-permute-done.35.down4 = bf16[1024,128]{1,0:T(8,128)(2,1)S(1)} collective-permute-done((bf16[1024,128]{1,0:T(8,128)(2,1)S(1)}, bf16[1024,128]{1,0:T(8,128)(2,1)S(1)}, u32[]{:S(2)}, u32[]{:S(2)}) %collective-permute-start.35) | collective-permute-done | bytes 262176 | tf_op jit(solution)/shard_map/ppermute | solution.py:48
  122.4 2.2 %collective-permute-start.37 = (bf16[128,128]{1,0:T(8,128)(2,1)S(1)}, bf16[128,128]{1,0:T(8,128)(2,1)S(1)}, u32[]{:S(2)}, u32[]{:S(2)}) collective-permute-start(bf16[128,128]{1,0:T(8,128)(2,1)S(1)} %slice.158), channel_id=1, source_target_pairs={{0,4},{1,5},{2,6},{3,7},{4,0},{5,1},{6,2},{7,3},{8,12},{9,13},{10,... | collective-permute-start | bytes 98312 | tf_op jit(solution)/shard_map/ppermute | solution.py:572
  125.4 2.5 %collective-permute-done.37.w_lo = bf16[128,128]{1,0:T(8,128)(2,1)S(1)} collective-permute-done((bf16[128,128]{1,0:T(8,128)(2,1)S(1)}, bf16[128,128]{1,0:T(8,128)(2,1)S(1)}, u32[]{:S(2)}, u32[]{:S(2)}) %collective-permute-start.37) | collective-permute-done | bytes 32800 | tf_op jit(solution)/shard_map/ppermute | solution.py:572
  128.9 10.0 %collective-permute-start.39 = (bf16[768,128]{1,0:T(8,128)(2,1)S(1)}, bf16[768,128]{1,0:T(8,128)(2,1)S(1)}, u32[]{:S(2)}, u32[]{:S(2)}) collective-permute-start(bf16[768,128]{1,0:T(8,128)(2,1)S(1)} %get-tuple-element.59), channel_id=1, source_target_pairs={{0,8},{8,0},{16,24},{24,16},{32,40},{40,32},{48,56},{56,48},{64,72... | collective-permute-start | bytes 589832 | tf_op jit(solution)/shard_map/ppermute | solution.py:34
  (107 shorter events, 24.8 us)
Async XLA Ops:
  0.6 8.7 %collective-permute-start = (bf16[256,256]{1,0:T(8,128)(2,1)}, bf16[256,256]{1,0:T(8,128)(2,1)S(1)}, u32[]{:S(2)}, u32[]{:S(2)}) collective-permute-start(bf16[256,256]{1,0:T(8,128)(2,1)} %bitcast.51), channel_id=1, source_target_pairs={{0,16},{8,24},{16,0},{24,8},{32,48},{40,56},{48,32},{56,40},{64,80... | collective-permute-start | bytes 393224 | tf_op jit(solution)/shard_map/ppermute | solution.py:34
  4.3 36.6 %collective-permute-start.2 = (bf16[12,256,256]{2,1,0:T(8,128)(2,1)}, bf16[12,256,256]{2,1,0:T(8,128)(2,1)S(1)}, u32[]{:S(2)}, u32[]{:S(2)}) collective-permute-start(bf16[12,256,256]{2,1,0:T(8,128)(2,1)} %bitcast.42), channel_id=1, source_target_pairs={{0,8},{8,0},{16,24},{24,16},{32,40},{40,32},{48,56},{56,48},{64,72... | collective-permute-start | bytes 4718600 | tf_op jit(solution)/shard_map/ppermute | solution.py:34
  11.8 10.3 %collective-permute-start.3 = (bf16[4,256,128]{2,1,0:T(8,128)(2,1)S(1)}, bf16[4,256,128]{2,1,0:T(8,128)(2,1)S(1)}, u32[]{:S(2)}, u32[]{:S(2)}) collective-permute-start(bf16[4,256,128]{2,1,0:T(8,128)(2,1)S(1)} %pad_maximum_fusion.5.refs_0_), channel_id=1, source_target_pairs={{0,224},{8,232},{16,240},{24,248},{32,0},{40,8},{48,16},{56,24},{6... | collective-permute-start | bytes 786440 | tf_op jit(solution)/shard_map/ppermute | solution.py:48
  16.5 9.0 %collective-permute-start.6 = (bf16[4,256,128]{2,1,0:T(8,128)(2,1)S(1)}, bf16[4,256,128]{2,1,0:T(8,128)(2,1)S(1)}, u32[]{:S(2)}, u32[]{:S(2)}) collective-permute-start(bf16[4,256,128]{2,1,0:T(8,128)(2,1)S(1)} %pad_maximum_fusion.5.refs_0_), channel_id=1, source_target_pairs={{0,32},{8,40},{16,48},{24,56},{32,64},{40,72},{48,80},{56,88},{64,... | collective-permute-start | bytes 786440 | tf_op jit(solution)/shard_map/ppermute | solution.py:48
  22.1 8.1 %collective-permute-start.4 = (bf16[4,256,128]{2,1,0:T(8,128)(2,1)S(1)}, bf16[4,256,128]{2,1,0:T(8,128)(2,1)S(1)}, u32[]{:S(2)}, u32[]{:S(2)}) collective-permute-start(bf16[4,256,128]{2,1,0:T(8,128)(2,1)S(1)} %collective-permute-done.3.refs_1_), channel_id=1, source_target_pairs={{0,224},{8,232},{16,240},{24,248},{32,0},{40,8},{48,16},{56,24},{6... | collective-permute-start | bytes 786440 | tf_op jit(solution)/shard_map/ppermute | solution.py:48
  25.5 8.1 %collective-permute-start.7 = (bf16[4,256,128]{2,1,0:T(8,128)(2,1)S(1)}, bf16[4,256,128]{2,1,0:T(8,128)(2,1)S(1)}, u32[]{:S(2)}, u32[]{:S(2)}) collective-permute-start(bf16[4,256,128]{2,1,0:T(8,128)(2,1)S(1)} %collective-permute-done.6.refs_6_), channel_id=1, source_target_pairs={{0,32},{8,40},{16,48},{24,56},{32,64},{40,72},{48,80},{56,88},{64,... | collective-permute-start | bytes 786440 | tf_op jit(solution)/shard_map/ppermute | solution.py:48
  30.1 7.1 %collective-permute-start.5 = (bf16[4,256,128]{2,1,0:T(8,128)(2,1)S(1)}, bf16[4,256,128]{2,1,0:T(8,128)(2,1)S(1)}, u32[]{:S(2)}, u32[]{:S(2)}) collective-permute-start(bf16[4,256,128]{2,1,0:T(8,128)(2,1)S(1)} %collective-permute-done.4.refs_2_), channel_id=1, source_target_pairs={{0,224},{8,232},{16,240},{24,248},{32,0},{40,8},{48,16},{56,24},{6... | collective-permute-start | bytes 786440 | tf_op jit(solution)/shard_map/ppermute | solution.py:48
  33.6 7.2 %collective-permute-start.8 = (bf16[4,256,128]{2,1,0:T(8,128)(2,1)S(1)}, bf16[4,256,128]{2,1,0:T(8,128)(2,1)S(1)}, u32[]{:S(2)}, u32[]{:S(2)}) collective-permute-start(bf16[4,256,128]{2,1,0:T(8,128)(2,1)S(1)} %collective-permute-done.7.refs_5_), channel_id=1, source_target_pairs={{0,32},{8,40},{16,48},{24,56},{32,64},{40,72},{48,80},{56,88},{64,... | collective-permute-start | bytes 786440 | tf_op jit(solution)/shard_map/ppermute | solution.py:48
  37.3 5.6 %collective-permute-start.10 = (bf16[2,256,128]{2,1,0:T(8,128)(2,1)S(1)}, bf16[2,256,128]{2,1,0:T(8,128)(2,1)S(1)}, u32[]{:S(2)}, u32[]{:S(2)}) collective-permute-start(bf16[2,256,128]{2,1,0:T(8,128)(2,1)S(1)} %slice.163), channel_id=1, source_target_pairs={{0,224},{8,232},{16,240},{24,248},{32,0},{40,8},{48,16},{56,24},{6... | collective-permute-start | bytes 393224 | tf_op jit(solution)/shard_map/ppermute | solution.py:48
  46.6 7.2 %collective-permute-start.11 = (bf16[2,256,128]{2,1,0:T(8,128)(2,1)S(1)}, bf16[2,256,128]{2,1,0:T(8,128)(2,1)S(1)}, u32[]{:S(2)}, u32[]{:S(2)}) collective-permute-start(bf16[2,256,128]{2,1,0:T(8,128)(2,1)S(1)} %get-tuple-element.41), channel_id=1, source_target_pairs={{0,6},{1,7},{2,4},{3,5},{4,2},{5,3},{6,0},{7,1},{8,14},{9,15},{10,... | collective-permute-start | bytes 393224 | tf_op jit(solution)/shard_map/ppermute | solution.py:39
  49.3 7.2 %collective-permute-start.12 = (bf16[2,256,128]{2,1,0:T(8,128)(2,1)S(1)}, bf16[2,256,128]{2,1,0:T(8,128)(2,1)S(1)}, u32[]{:S(2)}, u32[]{:S(2)}) collective-permute-start(bf16[2,256,128]{2,1,0:T(8,128)(2,1)S(1)} %get-tuple-element.42), channel_id=1, source_target_pairs={{0,2},{1,3},{2,0},{3,1},{4,6},{5,7},{6,4},{7,5},{8,10},{9,11},{10,... | collective-permute-start | bytes 393224 | tf_op jit(solution)/shard_map/ppermute | solution.py:39
  49.7 7.4 %collective-permute-start.13 = (bf16[2,256,128]{2,1,0:T(8,128)(2,1)S(1)}, bf16[2,256,128]{2,1,0:T(8,128)(2,1)S(1)}, u32[]{:S(2)}, u32[]{:S(2)}) collective-permute-start(bf16[2,256,128]{2,1,0:T(8,128)(2,1)S(1)} %get-tuple-element.43), channel_id=1, source_target_pairs={{0,5},{1,6},{2,7},{3,4},{4,1},{5,2},{6,3},{7,0},{8,13},{9,14},{10,... | collective-permute-start | bytes 393224 | tf_op jit(solution)/shard_map/ppermute | solution.py:39
  53.8 8.7 %collective-permute-start.15 = (bf16[2,256,128]{2,1,0:T(8,128)(2,1)S(1)}, bf16[2,256,128]{2,1,0:T(8,128)(2,1)S(1)}, u32[]{:S(2)}, u32[]{:S(2)}) collective-permute-start(bf16[2,256,128]{2,1,0:T(8,128)(2,1)S(1)} %get-tuple-element.45), channel_id=1, source_target_pairs={{0,1},{1,2},{2,3},{3,0},{4,5},{5,6},{6,7},{7,4},{8,9},{9,10},{10,1... | collective-permute-start | bytes 393224 | tf_op jit(solution)/shard_map/ppermute | solution.py:39
  53.8 8.7 %collective-permute-start.16 = (bf16[2,256,128]{2,1,0:T(8,128)(2,1)S(1)}, bf16[2,256,128]{2,1,0:T(8,128)(2,1)S(1)}, u32[]{:S(2)}, u32[]{:S(2)}) collective-permute-start(bf16[2,256,128]{2,1,0:T(8,128)(2,1)S(1)} %get-tuple-element.46), channel_id=1, source_target_pairs={{0,3},{1,0},{2,1},{3,2},{4,7},{5,4},{6,5},{7,6},{8,11},{9,8},{10,9... | collective-permute-start | bytes 393224 | tf_op jit(solution)/shard_map/ppermute | solution.py:39
  56.5 6.1 %collective-permute-start.17 = (bf16[2,256,128]{2,1,0:T(8,128)(2,1)S(1)}, bf16[2,256,128]{2,1,0:T(8,128)(2,1)S(1)}, u32[]{:S(2)}, u32[]{:S(2)}) collective-permute-start(bf16[2,256,128]{2,1,0:T(8,128)(2,1)S(1)} %get-tuple-element.47), channel_id=1, source_target_pairs={{0,4},{1,5},{2,6},{3,7},{4,0},{5,1},{6,2},{7,3},{8,12},{9,13},{10,... | collective-permute-start | bytes 393224 | tf_op jit(solution)/shard_map/ppermute | solution.py:39
  62.7 6.4 %collective-permute-start.18 = (f32[512,128]{1,0:T(8,128)S(1)}, f32[512,128]{1,0:T(8,128)S(1)}, u32[]{:S(2)}, u32[]{:S(2)}) collective-permute-start(f32[512,128]{1,0:T(8,128)S(1)} %bitcast.49), channel_id=1, source_target_pairs={{0,8},{8,0},{16,24},{24,16},{32,40},{40,32},{48,56},{56,48},{64,72... | collective-permute-start | bytes 786440 | tf_op jit(solution)/shard_map/ppermute | solution.py:34
  70.7 8.4 %collective-permute-start.22 = (bf16[640,128]{1,0:T(8,128)(2,1)S(1)}, bf16[640,128]{1,0:T(8,128)(2,1)S(1)}, u32[]{:S(2)}, u32[]{:S(2)}) collective-permute-start(bf16[640,128]{1,0:T(8,128)(2,1)S(1)} %get-tuple-element.49.refs_0_), channel_id=1, source_target_pairs={{0,3},{1,0},{2,1},{3,2},{4,7},{5,4},{6,5},{7,6},{8,11},{9,8},{10,9... | collective-permute-start | bytes 491528 | tf_op jit(solution)/shard_map/ppermute | solution.py:39
  72.4 6.7 %collective-permute-start.23 = (bf16[640,128]{1,0:T(8,128)(2,1)S(1)}, bf16[640,128]{1,0:T(8,128)(2,1)S(1)}, u32[]{:S(2)}, u32[]{:S(2)}) collective-permute-start(bf16[640,128]{1,0:T(8,128)(2,1)S(1)} %get-tuple-element.50), channel_id=1, source_target_pairs={{0,7},{1,4},{2,5},{3,6},{4,3},{5,0},{6,1},{7,2},{8,15},{9,12},{10,... | collective-permute-start | bytes 491528 | tf_op jit(solution)/shard_map/ppermute | solution.py:39
  73.2 9.4 %collective-permute-start.20 = (bf16[640,128]{1,0:T(8,128)(2,1)S(1)}, bf16[640,128]{1,0:T(8,128)(2,1)S(1)}, u32[]{:S(2)}, u32[]{:S(2)}) collective-permute-start(bf16[640,128]{1,0:T(8,128)(2,1)S(1)} %get-tuple-element.49.refs_0_), channel_id=1, source_target_pairs={{0,1},{1,2},{2,3},{3,0},{4,5},{5,6},{6,7},{7,4},{8,9},{9,10},{10,1... | collective-permute-start | bytes 491528 | tf_op jit(solution)/shard_map/ppermute | solution.py:39
  74.7 8.0 %collective-permute-start.21 = (bf16[640,128]{1,0:T(8,128)(2,1)S(1)}, bf16[640,128]{1,0:T(8,128)(2,1)S(1)}, u32[]{:S(2)}, u32[]{:S(2)}) collective-permute-start(bf16[640,128]{1,0:T(8,128)(2,1)S(1)} %get-tuple-element.50), channel_id=1, source_target_pairs={{0,5},{1,6},{2,7},{3,4},{4,1},{5,2},{6,3},{7,0},{8,13},{9,14},{10,... | collective-permute-start | bytes 491528 | tf_op jit(solution)/shard_map/ppermute | solution.py:39
  74.7 12.3 %collective-permute-start.24 = (bf16[640,128]{1,0:T(8,128)(2,1)S(1)}, bf16[640,128]{1,0:T(8,128)(2,1)S(1)}, u32[]{:S(2)}, u32[]{:S(2)}) collective-permute-start(bf16[640,128]{1,0:T(8,128)(2,1)S(1)} %get-tuple-element.50), channel_id=1, source_target_pairs={{0,4},{1,5},{2,6},{3,7},{4,0},{5,1},{6,2},{7,3},{8,12},{9,13},{10,... | collective-permute-start | bytes 491528 | tf_op jit(solution)/shard_map/ppermute | solution.py:39
  79.1 5.8 %collective-permute-start.26 = (bf16[640,128]{1,0:T(8,128)(2,1)S(1)}, bf16[640,128]{1,0:T(8,128)(2,1)S(1)}, u32[]{:S(2)}, u32[]{:S(2)}) collective-permute-start(bf16[640,128]{1,0:T(8,128)(2,1)S(1)} %pad_maximum_fusion.7), channel_id=1, source_target_pairs={{0,3},{1,0},{2,1},{3,2},{4,7},{5,4},{6,5},{7,6},{8,11},{9,8},{10,9... | collective-permute-start | bytes 491528 | tf_op jit(solution)/shard_map/ppermute | solution.py:39
  90.3 5.7 %collective-permute-start.28 = (bf16[640,128]{1,0:T(8,128)(2,1)S(1)}, bf16[640,128]{1,0:T(8,128)(2,1)S(1)}, u32[]{:S(2)}, u32[]{:S(2)}) collective-permute-start(bf16[640,128]{1,0:T(8,128)(2,1)S(1)} %get-tuple-element.54.own), channel_id=1, source_target_pairs={{0,32},{8,40},{16,48},{24,56},{32,64},{40,72},{48,80},{56,88},{64,... | collective-permute-start | bytes 491528 | tf_op jit(solution)/shard_map/ppermute | solution.py:48
  96.1 7.2 %collective-permute-start.29 = (bf16[1152,128]{1,0:T(8,128)(2,1)S(1)}, bf16[1152,128]{1,0:T(8,128)(2,1)S(1)}, u32[]{:S(2)}, u32[]{:S(2)}) collective-permute-start(bf16[1152,128]{1,0:T(8,128)(2,1)S(1)} %pad_maximum_fusion), channel_id=1, source_target_pairs={{0,32},{8,40},{16,48},{24,56},{32,64},{40,72},{48,80},{56,88},{64,... | collective-permute-start | bytes 884744 | tf_op jit(solution)/shard_map/ppermute | solution.py:48
  96.3 7.1 %collective-permute-start.33 = (bf16[1152,128]{1,0:T(8,128)(2,1)S(1)}, bf16[1152,128]{1,0:T(8,128)(2,1)S(1)}, u32[]{:S(2)}, u32[]{:S(2)}) collective-permute-start(bf16[1152,128]{1,0:T(8,128)(2,1)S(1)} %pad_maximum_fusion.3), channel_id=1, source_target_pairs={{0,224},{8,232},{16,240},{24,248},{32,0},{40,8},{48,16},{56,24},{6... | collective-permute-start | bytes 884744 | tf_op jit(solution)/shard_map/ppermute | solution.py:48
  103.4 8.3 %collective-permute-start.30 = (bf16[1152,128]{1,0:T(8,128)(2,1)S(1)}, bf16[1152,128]{1,0:T(8,128)(2,1)S(1)}, u32[]{:S(2)}, u32[]{:S(2)}) collective-permute-start(bf16[1152,128]{1,0:T(8,128)(2,1)S(1)} %pad_maximum_fusion.1), channel_id=1, source_target_pairs={{0,32},{8,40},{16,48},{24,56},{32,64},{40,72},{48,80},{56,88},{64,... | collective-permute-start | bytes 884744 | tf_op jit(solution)/shard_map/ppermute | solution.py:48
  103.6 8.3 %collective-permute-start.34 = (bf16[1152,128]{1,0:T(8,128)(2,1)S(1)}, bf16[1152,128]{1,0:T(8,128)(2,1)S(1)}, u32[]{:S(2)}, u32[]{:S(2)}) collective-permute-start(bf16[1152,128]{1,0:T(8,128)(2,1)S(1)} %pad_maximum_fusion.4), channel_id=1, source_target_pairs={{0,224},{8,232},{16,240},{24,248},{32,0},{40,8},{48,16},{56,24},{6... | collective-permute-start | bytes 884744 | tf_op jit(solution)/shard_map/ppermute | solution.py:48
  111.8 10.1 %collective-permute-start.31 = (bf16[1152,128]{1,0:T(8,128)(2,1)S(1)}, bf16[1152,128]{1,0:T(8,128)(2,1)S(1)}, u32[]{:S(2)}, u32[]{:S(2)}) collective-permute-start(bf16[1152,128]{1,0:T(8,128)(2,1)S(1)} %pad_maximum_fusion.2), channel_id=1, source_target_pairs={{0,32},{8,40},{16,48},{24,56},{32,64},{40,72},{48,80},{56,88},{64,... | collective-permute-start | bytes 884744 | tf_op jit(solution)/shard_map/ppermute | solution.py:48
  112.0 9.1 %collective-permute-start.35 = (bf16[1024,128]{1,0:T(8,128)(2,1)S(1)}, bf16[1024,128]{1,0:T(8,128)(2,1)S(1)}, u32[]{:S(2)}, u32[]{:S(2)}) collective-permute-start(bf16[1024,128]{1,0:T(8,128)(2,1)S(1)} %fusion), channel_id=1, source_target_pairs={{0,224},{8,232},{16,240},{24,248},{32,0},{40,8},{48,16},{56,24},{6... | collective-permute-start | bytes 786440 | tf_op jit(solution)/shard_map/ppermute | solution.py:48
  122.1 6.8 %collective-permute-start.36 = (bf16[640,128]{1,0:T(8,128)(2,1)S(1)}, bf16[640,128]{1,0:T(8,128)(2,1)S(1)}, u32[]{:S(2)}, u32[]{:S(2)}) collective-permute-start(bf16[640,128]{1,0:T(8,128)(2,1)S(1)} %get-tuple-element.57.sent), channel_id=1, source_target_pairs={{0,16},{8,24},{16,0},{24,8},{32,48},{40,56},{48,32},{56,40},{64,80... | collective-permute-start | bytes 491528 | tf_op jit(solution)/shard_map/ppermute | solution.py:34
  122.4 5.5 %collective-permute-start.37 = (bf16[128,128]{1,0:T(8,128)(2,1)S(1)}, bf16[128,128]{1,0:T(8,128)(2,1)S(1)}, u32[]{:S(2)}, u32[]{:S(2)}) collective-permute-start(bf16[128,128]{1,0:T(8,128)(2,1)S(1)} %slice.158), channel_id=1, source_target_pairs={{0,4},{1,5},{2,6},{3,7},{4,0},{5,1},{6,2},{7,3},{8,12},{9,13},{10,... | collective-permute-start | bytes 98312 | tf_op jit(solution)/shard_map/ppermute | solution.py:572
  128.9 11.1 %collective-permute-start.39 = (bf16[768,128]{1,0:T(8,128)(2,1)S(1)}, bf16[768,128]{1,0:T(8,128)(2,1)S(1)}, u32[]{:S(2)}, u32[]{:S(2)}) collective-permute-start(bf16[768,128]{1,0:T(8,128)(2,1)S(1)} %get-tuple-element.59), channel_id=1, source_target_pairs={{0,8},{8,0},{16,24},{24,16},{32,40},{40,32},{48,56},{56,48},{64,72... | collective-permute-start | bytes 589832 | tf_op jit(solution)/shard_map/ppermute | solution.py:34
  (14 other events, 122.2 us)

commit v15 on v9

--- a/solution.py
+++ b/solution.py
@@ -181,18 +181,13 @@
     slot_products(lists, far, adj_refs, product, add_to)
 
 
-def backward_far_kernel(lists_any, adj0, adj1, *refs):
-    received, (up, down, back, acc, lists, sem, pieces) = refs[:NCOL], refs[NCOL:]
+def backward_far_kernel(lists_any, adj0, adj1, back, up, down, acc, lists, sem):
     copy = pltpu.make_async_copy(lists_any, lists, sem)
     copy.start()
-    for k, ref in zip(MOVES, received):
-        source = col_target(k, -1)
-        back[source] = ref[: 2 * TILE, :]
-        pieces[source] = ref[2 * TILE :, :]
     acc[...] = jnp.zeros_like(acc)
-    piece = pieces[0].astype(jnp.float32)
+    piece = back[0, 2 * TILE :, :].astype(jnp.float32)
     for c in range(1, NCOL):
-        piece = piece + pieces[c].astype(jnp.float32)
+        piece = piece + back[c, 2 * TILE :, :].astype(jnp.float32)
     for out in (up, down):
         out[2 * TILE :, :] = piece.astype(jnp.bfloat16)
     copy.wait()
@@ -216,7 +211,7 @@
     return high, (x - high.astype(jnp.float32)).astype(jnp.bfloat16)
 
 
-def dense_kernel(agg_own, agg_other, weight, cot_own, cot_other, act_out, send, send_x):
+def dense_kernel(agg_own, agg_other, weight, cot_own, cot_other, act_out, send):
     first = (lax.axis_index("row") & 1) == 0
     own = agg_own[...]
     other = jnp.concatenate([agg_other[TILE:, :], agg_other[:TILE, :]], axis=0)
@@ -246,12 +241,12 @@
     w_part = (
         dot(own_hi, grad_hi, rows) + dot(own_lo, grad_hi, rows) + dot(own_hi, grad_lo, rows)
     )
-    x_lo = lax.axis_index("col") >> 2
-    for out, dest in ((send, x_lo), (send_x, 1 - x_lo)):
-        out[: 2 * TILE, :] = back
-        piece = jnp.where(dest == 0, w_part[:64], w_part[64:]).astype(jnp.bfloat16)
-        out[2 * TILE : 2 * TILE + 64, :] = piece[:, :HALF]
-        out[2 * TILE + 64 :, :] = piece[:, HALF:]
+    w_part = w_part.astype(jnp.bfloat16)
+    for c in range(NCOL):
+        send[c, : 2 * TILE, :] = back
+        piece = w_part[64 * (c // 4) : 64 * (c // 4) + 64]
+        send[c, 2 * TILE : 2 * TILE + 64, :] = piece[:, :HALF]
+        send[c, 2 * TILE + 64 :, :] = piece[:, HALF:]
 
 
 def f32(ref, start, rows=TILE):
@@ -420,19 +415,17 @@
     )(lists, adj0, adj1, near, far_a, far_b)
 
 
-def backward_far(lists, adj0, adj1, received):
+def backward_far(lists, adj0, adj1, back):
     message = shape(2 * TILE + W_ROWS, HALF)
     return local(
         backward_far_kernel,
-        (message, message, shape(NCOL, 2 * TILE, HALF)),
-        11,
+        (message, message),
+        4,
         "backward_far",
         any_in=1,
-        scratch=[pltpu.VMEM((QUAD, TILE, HALF), jnp.float32)]
-        + LIST_SCRATCH
-        + [pltpu.VMEM((NCOL, W_ROWS, HALF), jnp.bfloat16)],
+        scratch=[pltpu.VMEM((QUAD, TILE, HALF), jnp.float32)] + LIST_SCRATCH,
         cost=cost(3, 2),
-    )(lists, adj0, adj1, *received)
+    )(lists, adj0, adj1, back)
 
 
 def backward_near(lists, adj0, adj1, back):
@@ -450,7 +443,7 @@
 def dense(agg_own, agg_other, weight, cot_own, cot_other):
     return local(
         dense_kernel,
-        (shape(TILE, 2 * HALF),) + (shape(2 * TILE + W_ROWS, HALF),) * 2,
+        (shape(TILE, 2 * HALF), shape(NCOL, 2 * TILE + W_ROWS, HALF)),
         5,
         "dense",
     )(agg_own, agg_other, weight, cot_own, cot_other)
@@ -519,12 +512,12 @@
         for k, share in zip(MOVES, shares)
     ).reshape(2 * TILE, HALF)
     agg_other = quad_permute(agg, 1)
-    activated, send, send_x = dense(agg, agg_other, weight, cotangent, cot1)
-    received = [col_move(send if k < 4 else send_x, k) if k else send for k in MOVES]
+    activated, send = dense(agg, agg_other, weight, cotangent, cot1)
+    received = lax.all_to_all(send, "col", 0, 0, tiled=True)
 
     half, size = 2 * TILE, QUAD * TILE
-    own, own_down, back = backward_far(lists, adj0, adj1, received)
-    blocks = backward_near(lists, adj0, adj1, back)
+    own, own_down = backward_far(lists, adj0, adj1, received)
+    blocks = backward_near(lists, adj0, adj1, received)
     parts = blocks.reshape(NZ, size, HALF)
     up1, down1 = z_shift(own, 1), z_shift(own_down, -1)
     up = [add(parts[3, :half], up1[:half]), parts[3, half:], up1[half:]]

time: 136 us -> 137 us (level)
  blocking collectives: 0 us -> 21.5 us
  waiting for transfers between devices: 51.8 us -> 40.7 us
  starting transfers between devices: 69.2 us -> 59.7 us
    all_to_all x0 -> x1, blocking collectives: none -> 21.5 us  [per_device(): received = lax.all_to_all(send, 'col', 0, 0, tiled=True)]
    ppermute x14 -> x7, waiting for transfers between devices: 15.8 us -> 5.06 us  [col_move(): return lax.ppermute(x, 'col', pairs)]
    ppermute x14 -> x7, starting transfers between devices: 20.6 us -> 10.5 us  [col_move(): return lax.ppermute(x, 'col', pairs)]
  transfers between devices with their start and end apart: 39 -> 32, of which waited for: 20 -> 16; matrix products, arithmetic and copies ran while one was open for 0% -> 0% of each run, Pallas kernels for 4% -> 4%
where the time goes in v15:
time: 137 us; the launch traced here: 136 us
  starting transfers between devices  59.7 us (44%)
  waiting for transfers between devices  40.7 us (30%)
  blocking collectives  21.5 us (16%)
  Pallas kernels  9.68 us (7%)
  local copies, waits for them, and re-layouts  2.39 us (2%)
  between operations  1.62 us (1%)
    ppermute x16, waiting for transfers between devices, z_shift(): return lax.ppermute(x, 'row', row_pairs(lambda z, q: (z + step, q)))  29.3 us
    ppermute x16, starting transfers between devices, z_shift(): return lax.ppermute(x, 'row', row_pairs(lambda z, q: (z + step, q)))  26.8 us
    all_to_all x1, blocking collectives, per_device(): received = lax.all_to_all(send, 'col', 0, 0, tiled=True)  21.5 us
    ppermute x7, starting transfers between devices, quad_permute(): return lax.ppermute(x, 'row', row_pairs(lambda z, q: (z, q ^ flip)))  20.7 us
    ppermute x7, starting transfers between devices, col_move(): return lax.ppermute(x, 'col', pairs)  10.5 us
    ppermute x7, waiting for transfers between devices, col_move(): return lax.ppermute(x, 'col', pairs)  5.06 us
    ppermute x7, waiting for transfers between devices, quad_permute(): return lax.ppermute(x, 'row', row_pairs(lambda z, q: (z, q ^ flip)))  3.3 us
  transfers between devices with their start and end apart: 32, of which 16 were waited for; matrix products, arithmetic and copies ran while one was open for 0% of the time, Pallas kernels for 4%

profile of v15, /device:TPU:1, one launch (start us, length us, event | category | flops | bytes accessed | tf_op | source)
XLA Modules:
  0.0 136.3 jit_solution(1593075849005724096)
XLA Ops:
  0.6 3.7 %collective-permute-start = (bf16[256,256]{1,0:T(8,128)(2,1)}, bf16[256,256]{1,0:T(8,128)(2,1)S(1)}, u32[]{:S(2)}, u32[]{:S(2)}) collective-permute-start(bf16[256,256]{1,0:T(8,128)(2,1)} %bitcast.51), channel_id=1, source_target_pairs={{0,16},{8,24},{16,0},{24,8},{32,48},{40,56},{48,32},{56,40},{64,80... | collective-permute-start | bytes 393224 | tf_op jit(solution)/shard_map/ppermute | solution.py:33
  9.4 1.4 %collective-permute-start.1 = (bf16[528,128]{1,0:T(8,128)(2,1)S(1)}, bf16[528,128]{1,0:T(8,128)(2,1)S(1)}, u32[]{:S(2)}, u32[]{:S(2)}) collective-permute-start(bf16[528,128]{1,0:T(8,128)(2,1)S(1)} %get-tuple-element.32), channel_id=1, source_target_pairs={{0,8},{8,0},{16,24},{24,16},{32,40},{40,32},{48,56},{56,48},{64,72... | collective-permute-start | bytes 405512 | tf_op jit(solution)/shard_map/ppermute | solution.py:33
  11.8 4.7 %collective-permute-start.3 = (bf16[4,256,128]{2,1,0:T(8,128)(2,1)S(1)}, bf16[4,256,128]{2,1,0:T(8,128)(2,1)S(1)}, u32[]{:S(2)}, u32[]{:S(2)}) collective-permute-start(bf16[4,256,128]{2,1,0:T(8,128)(2,1)S(1)} %pad_maximum_fusion.5.refs_0_), channel_id=1, source_target_pairs={{0,224},{8,232},{16,240},{24,248},{32,0},{40,8},{48,16},{56,24},{6... | collective-permute-start | bytes 786440 | tf_op jit(solution)/shard_map/ppermute | solution.py:47
  16.5 5.6 %collective-permute-done.3.refs_1_ = bf16[4,256,128]{2,1,0:T(8,128)(2,1)S(1)} collective-permute-done((bf16[4,256,128]{2,1,0:T(8,128)(2,1)S(1)}, bf16[4,256,128]{2,1,0:T(8,128)(2,1)S(1)}, u32[]{:S(2)}, u32[]{:S(2)}) %collective-permute-start.3) | collective-permute-done | bytes 262176 | tf_op jit(solution)/shard_map/ppermute | solution.py:47
  22.1 3.4 %collective-permute-start.4 = (bf16[4,256,128]{2,1,0:T(8,128)(2,1)S(1)}, bf16[4,256,128]{2,1,0:T(8,128)(2,1)S(1)}, u32[]{:S(2)}, u32[]{:S(2)}) collective-permute-start(bf16[4,256,128]{2,1,0:T(8,128)(2,1)S(1)} %collective-permute-done.3.refs_1_), channel_id=1, source_target_pairs={{0,224},{8,232},{16,240},{24,248},{32,0},{40,8},{48,16},{56,24},{6... | collective-permute-start | bytes 786440 | tf_op jit(solution)/shard_map/ppermute | solution.py:47
  25.5 4.6 %collective-permute-done.4.refs_2_ = bf16[4,256,128]{2,1,0:T(8,128)(2,1)S(1)} collective-permute-done((bf16[4,256,128]{2,1,0:T(8,128)(2,1)S(1)}, bf16[4,256,128]{2,1,0:T(8,128)(2,1)S(1)}, u32[]{:S(2)}, u32[]{:S(2)}) %collective-permute-start.4) | collective-permute-done | bytes 262176 | tf_op jit(solution)/shard_map/ppermute | solution.py:47
  30.1 3.4 %collective-permute-start.5 = (bf16[4,256,128]{2,1,0:T(8,128)(2,1)S(1)}, bf16[4,256,128]{2,1,0:T(8,128)(2,1)S(1)}, u32[]{:S(2)}, u32[]{:S(2)}) collective-permute-start(bf16[4,256,128]{2,1,0:T(8,128)(2,1)S(1)} %collective-permute-done.4.refs_2_), channel_id=1, source_target_pairs={{0,224},{8,232},{16,240},{24,248},{32,0},{40,8},{48,16},{56,24},{6... | collective-permute-start | bytes 786440 | tf_op jit(solution)/shard_map/ppermute | solution.py:47
  33.6 3.7 %collective-permute-done.5.refs_3_ = bf16[4,256,128]{2,1,0:T(8,128)(2,1)S(1)} collective-permute-done((bf16[4,256,128]{2,1,0:T(8,128)(2,1)S(1)}, bf16[4,256,128]{2,1,0:T(8,128)(2,1)S(1)}, u32[]{:S(2)}, u32[]{:S(2)}) %collective-permute-start.5) | collective-permute-done | bytes 262176 | tf_op jit(solution)/shard_map/ppermute | solution.py:47
  37.3 3.5 %collective-permute-start.10 = (bf16[2,256,128]{2,1,0:T(8,128)(2,1)S(1)}, bf16[2,256,128]{2,1,0:T(8,128)(2,1)S(1)}, u32[]{:S(2)}, u32[]{:S(2)}) collective-permute-start(bf16[2,256,128]{2,1,0:T(8,128)(2,1)S(1)} %slice.127), channel_id=1, source_target_pairs={{0,224},{8,232},{16,240},{24,248},{32,0},{40,8},{48,16},{56,24},{6... | collective-permute-start | bytes 393224 | tf_op jit(solution)/shard_map/ppermute | solution.py:47
  40.9 2.6 %forward_near.1 = (f32[18,256,128]{2,1,0:T(8,128)S(1)}, s32[68]{0:T(128)S(1)}) custom-call(s32[25]{0:T(128)S(1)} %get-tuple-element.29.own_any, s32[25]{0:T(128)S(1)} %fusion.6.partner_any, bf16[12,256,256]{2,1,0:T(8,128)(2,1)S(1)} %bitcast.43, bf16[12,256,256]{2,1,0:T(8,128)(2,1)S(1)} %collective-permute-done.2.adj1, ...), custom_call_target="tpu_custom_call" | custom-call | flops 352321536 | bytes 6291456 | tf_op jit(solution)/shard_map/forward_near/pallas_call | solution.py:385
  43.6 2.4 %collective-permute-done.9.far_a = bf16[2,256,128]{2,1,0:T(8,128)(2,1)S(1)} collective-permute-done((bf16[2,256,128]{2,1,0:T(8,128)(2,1)S(1)}, bf16[2,256,128]{2,1,0:T(8,128)(2,1)S(1)}, u32[]{:S(2)}, u32[]{:S(2)}) %collective-permute-start.9) | collective-permute-done | bytes 131104 | tf_op jit(solution)/shard_map/ppermute | solution.py:47
  46.6 2.9 %collective-permute-start.11 = (bf16[2,256,128]{2,1,0:T(8,128)(2,1)S(1)}, bf16[2,256,128]{2,1,0:T(8,128)(2,1)S(1)}, u32[]{:S(2)}, u32[]{:S(2)}) collective-permute-start(bf16[2,256,128]{2,1,0:T(8,128)(2,1)S(1)} %get-tuple-element.37), channel_id=1, source_target_pairs={{0,6},{1,7},{2,4},{3,5},{4,2},{5,3},{6,0},{7,1},{8,14},{9,15},{10,... | collective-permute-start | bytes 393224 | tf_op jit(solution)/shard_map/ppermute | solution.py:38
  49.7 2.3 %collective-permute-start.13 = (bf16[2,256,128]{2,1,0:T(8,128)(2,1)S(1)}, bf16[2,256,128]{2,1,0:T(8,128)(2,1)S(1)}, u32[]{:S(2)}, u32[]{:S(2)}) collective-permute-start(bf16[2,256,128]{2,1,0:T(8,128)(2,1)S(1)} %get-tuple-element.39), channel_id=1, source_target_pairs={{0,5},{1,6},{2,7},{3,4},{4,1},{5,2},{6,3},{7,0},{8,13},{9,14},{10,... | collective-permute-start | bytes 393224 | tf_op jit(solution)/shard_map/ppermute | solution.py:38
  52.0 1.3 collective-permute-start.14
  53.4 2.6 %collective-permute-start.16 = (bf16[2,256,128]{2,1,0:T(8,128)(2,1)S(1)}, bf16[2,256,128]{2,1,0:T(8,128)(2,1)S(1)}, u32[]{:S(2)}, u32[]{:S(2)}) collective-permute-start(bf16[2,256,128]{2,1,0:T(8,128)(2,1)S(1)} %get-tuple-element.42), channel_id=1, source_target_pairs={{0,3},{1,0},{2,1},{3,2},{4,7},{5,4},{6,5},{7,6},{8,11},{9,8},{10,9... | collective-permute-start | bytes 393224 | tf_op jit(solution)/shard_map/ppermute | solution.py:38
  57.5 4.7 %collective-permute-done.15 = bf16[2,256,128]{2,1,0:T(8,128)(2,1)S(1)} collective-permute-done((bf16[2,256,128]{2,1,0:T(8,128)(2,1)S(1)}, bf16[2,256,128]{2,1,0:T(8,128)(2,1)S(1)}, u32[]{:S(2)}, u32[]{:S(2)}) %collective-permute-start.15) | collective-permute-done | bytes 131104 | tf_op jit(solution)/shard_map/ppermute | solution.py:38
  62.3 5.0 %collective-permute-start.18 = (f32[512,128]{1,0:T(8,128)S(1)}, f32[512,128]{1,0:T(8,128)S(1)}, u32[]{:S(2)}, u32[]{:S(2)}) collective-permute-start(f32[512,128]{1,0:T(8,128)S(1)} %bitcast.49), channel_id=1, source_target_pairs={{0,8},{8,0},{16,24},{24,16},{32,40},{40,32},{48,56},{56,48},{64,72... | collective-permute-start | bytes 786440 | tf_op jit(solution)/shard_map/ppermute | solution.py:33
  68.7 1.4 %dense.1 = (bf16[256,256]{1,0:T(8,128)(2,1)}, bf16[8,640,128]{2,1,0:T(8,128)(2,1)S(1)}) custom-call(f32[512,128]{1,0:T(8,128)S(1)} %bitcast.50, f32[512,128]{1,0:T(8,128)S(1)} %collective-permute-done.18.agg_other, bf16[256,256]{1,0:T(8,128)(2,1)S(1)} %copy-done.1, bf16[256,256]{1,0:T(8,128)(2,1)S(1)} %copy-done.2, ...), custom_call_target="tpu_custom_call" | custom-call | tf_op jit(solution)/shard_map/dense/pallas_call | solution.py:444
  70.1 21.5 %all_to_all.5.back = bf16[8,640,128]{2,1,0:T(8,128)(2,1)S(1)} all-to-all(bf16[8,640,128]{2,1,0:T(8,128)(2,1)S(1)} %get-tuple-element.45), channel_id=1, replica_groups=mesh['row'=32,'col'=8] {'col'}, dimensions={0} | all-to-all | bytes 2621440 | tf_op jit(solution)/shard_map/all_to_all | solution.py:516
  92.2 2.7 %collective-permute-start.24 = (bf16[640,128]{1,0:T(8,128)(2,1)S(1)}, bf16[640,128]{1,0:T(8,128)(2,1)S(1)}, u32[]{:S(2)}, u32[]{:S(2)}) collective-permute-start(bf16[640,128]{1,0:T(8,128)(2,1)S(1)} %get-tuple-element.47), channel_id=1, source_target_pairs={{0,224},{8,232},{16,240},{24,248},{32,0},{40,8},{48,16},{56,24},{6... | collective-permute-start | bytes 491528 | tf_op jit(solution)/shard_map/ppermute | solution.py:47
  94.9 2.1 %backward_near.1.parts = bf16[32,256,128]{2,1,0:T(8,128)(2,1)S(1)} custom-call(s32[68]{0:T(128)S(1)} %get-tuple-element.34.lists_any, bf16[12,256,256]{2,1,0:T(8,128)(2,1)S(1)} %bitcast.46, bf16[12,256,256]{2,1,0:T(8,128)(2,1)S(1)} %collective-permute-done.2.adj1, bf16[8,640,128]{2,1,0:T(8,128)(2,1)S(1)} %all_to_all.5.back), custom_call_target="tpu_custom_call" | custom-call | flops 352321536 | bytes 6291456 | tf_op jit(solution)/shard_map/backward_near/pallas_call | solution.py:432
  98.0 2.7 %collective-permute-start.25 = (bf16[1152,128]{1,0:T(8,128)(2,1)S(1)}, bf16[1152,128]{1,0:T(8,128)(2,1)S(1)}, u32[]{:S(2)}, u32[]{:S(2)}) collective-permute-start(bf16[1152,128]{1,0:T(8,128)(2,1)S(1)} %pad_maximum_fusion.3), channel_id=1, source_target_pairs={{0,224},{8,232},{16,240},{24,248},{32,0},{40,8},{48,16},{56,24},{6... | collective-permute-start | bytes 884744 | tf_op jit(solution)/shard_map/ppermute | solution.py:47
  100.7 3.9 %collective-permute-done.21.up2 = bf16[1152,128]{1,0:T(8,128)(2,1)S(1)} collective-permute-done((bf16[1152,128]{1,0:T(8,128)(2,1)S(1)}, bf16[1152,128]{1,0:T(8,128)(2,1)S(1)}, u32[]{:S(2)}, u32[]{:S(2)}) %collective-permute-start.21) | collective-permute-done | bytes 294944 | tf_op jit(solution)/shard_map/ppermute | solution.py:47
  105.0 2.7 %collective-permute-start.26 = (bf16[1152,128]{1,0:T(8,128)(2,1)S(1)}, bf16[1152,128]{1,0:T(8,128)(2,1)S(1)}, u32[]{:S(2)}, u32[]{:S(2)}) collective-permute-start(bf16[1152,128]{1,0:T(8,128)(2,1)S(1)} %pad_maximum_fusion.4), channel_id=1, source_target_pairs={{0,224},{8,232},{16,240},{24,248},{32,0},{40,8},{48,16},{56,24},{6... | collective-permute-start | bytes 884744 | tf_op jit(solution)/shard_map/ppermute | solution.py:47
  107.7 3.9 %collective-permute-done.22.up3 = bf16[1152,128]{1,0:T(8,128)(2,1)S(1)} collective-permute-done((bf16[1152,128]{1,0:T(8,128)(2,1)S(1)}, bf16[1152,128]{1,0:T(8,128)(2,1)S(1)}, u32[]{:S(2)}, u32[]{:S(2)}) %collective-permute-start.22) | collective-permute-done | bytes 294944 | tf_op jit(solution)/shard_map/ppermute | solution.py:47
  111.9 3.2 %collective-permute-start.27 = (bf16[1024,128]{1,0:T(8,128)(2,1)S(1)}, bf16[1024,128]{1,0:T(8,128)(2,1)S(1)}, u32[]{:S(2)}, u32[]{:S(2)}) collective-permute-start(bf16[1024,128]{1,0:T(8,128)(2,1)S(1)} %fusion), channel_id=1, source_target_pairs={{0,224},{8,232},{16,240},{24,248},{32,0},{40,8},{48,16},{56,24},{6... | collective-permute-start | bytes 786440 | tf_op jit(solution)/shard_map/ppermute | solution.py:47
  115.1 4.4 %collective-permute-done.27.down4 = bf16[1024,128]{1,0:T(8,128)(2,1)S(1)} collective-permute-done((bf16[1024,128]{1,0:T(8,128)(2,1)S(1)}, bf16[1024,128]{1,0:T(8,128)(2,1)S(1)}, u32[]{:S(2)}, u32[]{:S(2)}) %collective-permute-start.27) | collective-permute-done | bytes 262176 | tf_op jit(solution)/shard_map/ppermute | solution.py:47
  120.0 1.6 %collective-permute-start.28 = (bf16[640,128]{1,0:T(8,128)(2,1)S(1)}, bf16[640,128]{1,0:T(8,128)(2,1)S(1)}, u32[]{:S(2)}, u32[]{:S(2)}) collective-permute-start(bf16[640,128]{1,0:T(8,128)(2,1)S(1)} %get-tuple-element.49.sent), channel_id=1, source_target_pairs={{0,16},{8,24},{16,0},{24,8},{32,48},{40,56},{48,32},{56,40},{64,80... | collective-permute-start | bytes 491528 | tf_op jit(solution)/shard_map/ppermute | solution.py:33
  121.6 1.7 %collective-permute-start.30 = (bf16[128,128]{1,0:T(8,128)(2,1)S(1)}, bf16[128,128]{1,0:T(8,128)(2,1)S(1)}, u32[]{:S(2)}, u32[]{:S(2)}) collective-permute-start(bf16[128,128]{1,0:T(8,128)(2,1)S(1)} %slice.122), channel_id=1, source_target_pairs={{0,20},{1,21},{2,22},{3,23},{4,16},{5,17},{6,18},{7,19},{8,28},{9,... | collective-permute-start | bytes 98312 | tf_op jit(solution)/shard_map/ppermute | solution.py:539
  123.3 1.3 collective-permute-done.29.w_lo
  124.7 1.7 %collective-permute-done.30.w_both = bf16[128,128]{1,0:T(8,128)(2,1)S(1)} collective-permute-done((bf16[128,128]{1,0:T(8,128)(2,1)S(1)}, bf16[128,128]{1,0:T(8,128)(2,1)S(1)}, u32[]{:S(2)}, u32[]{:S(2)}) %collective-permute-start.30) | collective-permute-done | bytes 32800 | tf_op jit(solution)/shard_map/ppermute | solution.py:539
  126.4 8.0 %collective-permute-start.31 = (bf16[768,128]{1,0:T(8,128)(2,1)S(1)}, bf16[768,128]{1,0:T(8,128)(2,1)S(1)}, u32[]{:S(2)}, u32[]{:S(2)}) collective-permute-start(bf16[768,128]{1,0:T(8,128)(2,1)S(1)} %get-tuple-element.51), channel_id=1, source_target_pairs={{0,8},{8,0},{16,24},{24,16},{32,40},{40,32},{48,56},{56,48},{64,72... | collective-permute-start | bytes 589832 | tf_op jit(solution)/shard_map/ppermute | solution.py:33
  (80 shorter events, 14.0 us)
Async XLA Ops:
  0.6 8.7 %collective-permute-start = (bf16[256,256]{1,0:T(8,128)(2,1)}, bf16[256,256]{1,0:T(8,128)(2,1)S(1)}, u32[]{:S(2)}, u32[]{:S(2)}) collective-permute-start(bf16[256,256]{1,0:T(8,128)(2,1)} %bitcast.51), channel_id=1, source_target_pairs={{0,16},{8,24},{16,0},{24,8},{32,48},{40,56},{48,32},{56,40},{64,80... | collective-permute-start | bytes 393224 | tf_op jit(solution)/shard_map/ppermute | solution.py:33
  4.3 36.6 %collective-permute-start.2 = (bf16[12,256,256]{2,1,0:T(8,128)(2,1)}, bf16[12,256,256]{2,1,0:T(8,128)(2,1)S(1)}, u32[]{:S(2)}, u32[]{:S(2)}) collective-permute-start(bf16[12,256,256]{2,1,0:T(8,128)(2,1)} %bitcast.42), channel_id=1, source_target_pairs={{0,8},{8,0},{16,24},{24,16},{32,40},{40,32},{48,56},{56,48},{64,72... | collective-permute-start | bytes 4718600 | tf_op jit(solution)/shard_map/ppermute | solution.py:33
  9.4 2.4 %collective-permute-start.1 = (bf16[528,128]{1,0:T(8,128)(2,1)S(1)}, bf16[528,128]{1,0:T(8,128)(2,1)S(1)}, u32[]{:S(2)}, u32[]{:S(2)}) collective-permute-start(bf16[528,128]{1,0:T(8,128)(2,1)S(1)} %get-tuple-element.32), channel_id=1, source_target_pairs={{0,8},{8,0},{16,24},{24,16},{32,40},{40,32},{48,56},{56,48},{64,72... | collective-permute-start | bytes 405512 | tf_op jit(solution)/shard_map/ppermute | solution.py:33
  11.8 10.3 %collective-permute-start.3 = (bf16[4,256,128]{2,1,0:T(8,128)(2,1)S(1)}, bf16[4,256,128]{2,1,0:T(8,128)(2,1)S(1)}, u32[]{:S(2)}, u32[]{:S(2)}) collective-permute-start(bf16[4,256,128]{2,1,0:T(8,128)(2,1)S(1)} %pad_maximum_fusion.5.refs_0_), channel_id=1, source_target_pairs={{0,224},{8,232},{16,240},{24,248},{32,0},{40,8},{48,16},{56,24},{6... | collective-permute-start | bytes 786440 | tf_op jit(solution)/shard_map/ppermute | solution.py:47
  16.5 9.0 %collective-permute-start.6 = (bf16[4,256,128]{2,1,0:T(8,128)(2,1)S(1)}, bf16[4,256,128]{2,1,0:T(8,128)(2,1)S(1)}, u32[]{:S(2)}, u32[]{:S(2)}) collective-permute-start(bf16[4,256,128]{2,1,0:T(8,128)(2,1)S(1)} %pad_maximum_fusion.5.refs_0_), channel_id=1, source_target_pairs={{0,32},{8,40},{16,48},{24,56},{32,64},{40,72},{48,80},{56,88},{64,... | collective-permute-start | bytes 786440 | tf_op jit(solution)/shard_map/ppermute | solution.py:47
  22.1 8.1 %collective-permute-start.4 = (bf16[4,256,128]{2,1,0:T(8,128)(2,1)S(1)}, bf16[4,256,128]{2,1,0:T(8,128)(2,1)S(1)}, u32[]{:S(2)}, u32[]{:S(2)}) collective-permute-start(bf16[4,256,128]{2,1,0:T(8,128)(2,1)S(1)} %collective-permute-done.3.refs_1_), channel_id=1, source_target_pairs={{0,224},{8,232},{16,240},{24,248},{32,0},{40,8},{48,16},{56,24},{6... | collective-permute-start | bytes 786440 | tf_op jit(solution)/shard_map/ppermute | solution.py:47
  25.5 8.1 %collective-permute-start.7 = (bf16[4,256,128]{2,1,0:T(8,128)(2,1)S(1)}, bf16[4,256,128]{2,1,0:T(8,128)(2,1)S(1)}, u32[]{:S(2)}, u32[]{:S(2)}) collective-permute-start(bf16[4,256,128]{2,1,0:T(8,128)(2,1)S(1)} %collective-permute-done.6.refs_6_), channel_id=1, source_target_pairs={{0,32},{8,40},{16,48},{24,56},{32,64},{40,72},{48,80},{56,88},{64,... | collective-permute-start | bytes 786440 | tf_op jit(solution)/shard_map/ppermute | solution.py:47
  30.1 7.1 %collective-permute-start.5 = (bf16[4,256,128]{2,1,0:T(8,128)(2,1)S(1)}, bf16[4,256,128]{2,1,0:T(8,128)(2,1)S(1)}, u32[]{:S(2)}, u32[]{:S(2)}) collective-permute-start(bf16[4,256,128]{2,1,0:T(8,128)(2,1)S(1)} %collective-permute-done.4.refs_2_), channel_id=1, source_target_pairs={{0,224},{8,232},{16,240},{24,248},{32,0},{40,8},{48,16},{56,24},{6... | collective-permute-start | bytes 786440 | tf_op jit(solution)/shard_map/ppermute | solution.py:47
  33.6 7.2 %collective-permute-start.8 = (bf16[4,256,128]{2,1,0:T(8,128)(2,1)S(1)}, bf16[4,256,128]{2,1,0:T(8,128)(2,1)S(1)}, u32[]{:S(2)}, u32[]{:S(2)}) collective-permute-start(bf16[4,256,128]{2,1,0:T(8,128)(2,1)S(1)} %collective-permute-done.7.refs_5_), channel_id=1, source_target_pairs={{0,32},{8,40},{16,48},{24,56},{32,64},{40,72},{48,80},{56,88},{64,... | collective-permute-start | bytes 786440 | tf_op jit(solution)/shard_map/ppermute | solution.py:47
  37.3 6.3 %collective-permute-start.10 = (bf16[2,256,128]{2,1,0:T(8,128)(2,1)S(1)}, bf16[2,256,128]{2,1,0:T(8,128)(2,1)S(1)}, u32[]{:S(2)}, u32[]{:S(2)}) collective-permute-start(bf16[2,256,128]{2,1,0:T(8,128)(2,1)S(1)} %slice.127), channel_id=1, source_target_pairs={{0,224},{8,232},{16,240},{24,248},{32,0},{40,8},{48,16},{56,24},{6... | collective-permute-start | bytes 393224 | tf_op jit(solution)/shard_map/ppermute | solution.py:47
  40.8 5.1 %collective-permute-start.9 = (bf16[2,256,128]{2,1,0:T(8,128)(2,1)S(1)}, bf16[2,256,128]{2,1,0:T(8,128)(2,1)S(1)}, u32[]{:S(2)}, u32[]{:S(2)}) collective-permute-start(bf16[2,256,128]{2,1,0:T(8,128)(2,1)S(1)} %slice.126), channel_id=1, source_target_pairs={{0,32},{8,40},{16,48},{24,56},{32,64},{40,72},{48,80},{56,88},{64,... | collective-permute-start | bytes 393224 | tf_op jit(solution)/shard_map/ppermute | solution.py:47
  46.6 6.8 %collective-permute-start.11 = (bf16[2,256,128]{2,1,0:T(8,128)(2,1)S(1)}, bf16[2,256,128]{2,1,0:T(8,128)(2,1)S(1)}, u32[]{:S(2)}, u32[]{:S(2)}) collective-permute-start(bf16[2,256,128]{2,1,0:T(8,128)(2,1)S(1)} %get-tuple-element.37), channel_id=1, source_target_pairs={{0,6},{1,7},{2,4},{3,5},{4,2},{5,3},{6,0},{7,1},{8,14},{9,15},{10,... | collective-permute-start | bytes 393224 | tf_op jit(solution)/shard_map/ppermute | solution.py:38
  49.5 6.5 %collective-permute-start.12 = (bf16[2,256,128]{2,1,0:T(8,128)(2,1)S(1)}, bf16[2,256,128]{2,1,0:T(8,128)(2,1)S(1)}, u32[]{:S(2)}, u32[]{:S(2)}) collective-permute-start(bf16[2,256,128]{2,1,0:T(8,128)(2,1)S(1)} %get-tuple-element.38), channel_id=1, source_target_pairs={{0,2},{1,3},{2,0},{3,1},{4,6},{5,7},{6,4},{7,5},{8,10},{9,11},{10,... | collective-permute-start | bytes 393224 | tf_op jit(solution)/shard_map/ppermute | solution.py:38
  49.7 7.4 %collective-permute-start.13 = (bf16[2,256,128]{2,1,0:T(8,128)(2,1)S(1)}, bf16[2,256,128]{2,1,0:T(8,128)(2,1)S(1)}, u32[]{:S(2)}, u32[]{:S(2)}) collective-permute-start(bf16[2,256,128]{2,1,0:T(8,128)(2,1)S(1)} %get-tuple-element.39), channel_id=1, source_target_pairs={{0,5},{1,6},{2,7},{3,4},{4,1},{5,2},{6,3},{7,0},{8,13},{9,14},{10,... | collective-permute-start | bytes 393224 | tf_op jit(solution)/shard_map/ppermute | solution.py:38
  52.0 5.4 %collective-permute-start.14 = (bf16[2,256,128]{2,1,0:T(8,128)(2,1)S(1)}, bf16[2,256,128]{2,1,0:T(8,128)(2,1)S(1)}, u32[]{:S(2)}, u32[]{:S(2)}) collective-permute-start(bf16[2,256,128]{2,1,0:T(8,128)(2,1)S(1)} %get-tuple-element.40), channel_id=1, source_target_pairs={{0,7},{1,4},{2,5},{3,6},{4,3},{5,0},{6,1},{7,2},{8,15},{9,12},{10,... | collective-permute-start | bytes 393224 | tf_op jit(solution)/shard_map/ppermute | solution.py:38
  53.3 8.9 %collective-permute-start.15 = (bf16[2,256,128]{2,1,0:T(8,128)(2,1)S(1)}, bf16[2,256,128]{2,1,0:T(8,128)(2,1)S(1)}, u32[]{:S(2)}, u32[]{:S(2)}) collective-permute-start(bf16[2,256,128]{2,1,0:T(8,128)(2,1)S(1)} %get-tuple-element.41), channel_id=1, source_target_pairs={{0,1},{1,2},{2,3},{3,0},{4,5},{5,6},{6,7},{7,4},{8,9},{9,10},{10,1... | collective-permute-start | bytes 393224 | tf_op jit(solution)/shard_map/ppermute | solution.py:38
  53.4 8.8 %collective-permute-start.16 = (bf16[2,256,128]{2,1,0:T(8,128)(2,1)S(1)}, bf16[2,256,128]{2,1,0:T(8,128)(2,1)S(1)}, u32[]{:S(2)}, u32[]{:S(2)}) collective-permute-start(bf16[2,256,128]{2,1,0:T(8,128)(2,1)S(1)} %get-tuple-element.42), channel_id=1, source_target_pairs={{0,3},{1,0},{2,1},{3,2},{4,7},{5,4},{6,5},{7,6},{8,11},{9,8},{10,9... | collective-permute-start | bytes 393224 | tf_op jit(solution)/shard_map/ppermute | solution.py:38
  56.0 6.2 %collective-permute-start.17 = (bf16[2,256,128]{2,1,0:T(8,128)(2,1)S(1)}, bf16[2,256,128]{2,1,0:T(8,128)(2,1)S(1)}, u32[]{:S(2)}, u32[]{:S(2)}) collective-permute-start(bf16[2,256,128]{2,1,0:T(8,128)(2,1)S(1)} %get-tuple-element.43), channel_id=1, source_target_pairs={{0,4},{1,5},{2,6},{3,7},{4,0},{5,1},{6,2},{7,3},{8,12},{9,13},{10,... | collective-permute-start | bytes 393224 | tf_op jit(solution)/shard_map/ppermute | solution.py:38
  62.3 6.4 %collective-permute-start.18 = (f32[512,128]{1,0:T(8,128)S(1)}, f32[512,128]{1,0:T(8,128)S(1)}, u32[]{:S(2)}, u32[]{:S(2)}) collective-permute-start(f32[512,128]{1,0:T(8,128)S(1)} %bitcast.49), channel_id=1, source_target_pairs={{0,8},{8,0},{16,24},{24,16},{32,40},{40,32},{48,56},{56,48},{64,72... | collective-permute-start | bytes 786440 | tf_op jit(solution)/shard_map/ppermute | solution.py:33
  67.3 1.3 collective-permute-start.19
  92.1 5.5 %collective-permute-start.20 = (bf16[640,128]{1,0:T(8,128)(2,1)S(1)}, bf16[640,128]{1,0:T(8,128)(2,1)S(1)}, u32[]{:S(2)}, u32[]{:S(2)}) collective-permute-start(bf16[640,128]{1,0:T(8,128)(2,1)S(1)} %get-tuple-element.46.own), channel_id=1, source_target_pairs={{0,32},{8,40},{16,48},{24,56},{32,64},{40,72},{48,80},{56,88},{64,... | collective-permute-start | bytes 491528 | tf_op jit(solution)/shard_map/ppermute | solution.py:47
  92.2 5.4 %collective-permute-start.24 = (bf16[640,128]{1,0:T(8,128)(2,1)S(1)}, bf16[640,128]{1,0:T(8,128)(2,1)S(1)}, u32[]{:S(2)}, u32[]{:S(2)}) collective-permute-start(bf16[640,128]{1,0:T(8,128)(2,1)S(1)} %get-tuple-element.47), channel_id=1, source_target_pairs={{0,224},{8,232},{16,240},{24,248},{32,0},{40,8},{48,16},{56,24},{6... | collective-permute-start | bytes 491528 | tf_op jit(solution)/shard_map/ppermute | solution.py:47
  97.7 6.9 %collective-permute-start.21 = (bf16[1152,128]{1,0:T(8,128)(2,1)S(1)}, bf16[1152,128]{1,0:T(8,128)(2,1)S(1)}, u32[]{:S(2)}, u32[]{:S(2)}) collective-permute-start(bf16[1152,128]{1,0:T(8,128)(2,1)S(1)} %pad_maximum_fusion), channel_id=1, source_target_pairs={{0,32},{8,40},{16,48},{24,56},{32,64},{40,72},{48,80},{56,88},{64,... | collective-permute-start | bytes 884744 | tf_op jit(solution)/shard_map/ppermute | solution.py:47
  98.0 6.9 %collective-permute-start.25 = (bf16[1152,128]{1,0:T(8,128)(2,1)S(1)}, bf16[1152,128]{1,0:T(8,128)(2,1)S(1)}, u32[]{:S(2)}, u32[]{:S(2)}) collective-permute-start(bf16[1152,128]{1,0:T(8,128)(2,1)S(1)} %pad_maximum_fusion.3), channel_id=1, source_target_pairs={{0,224},{8,232},{16,240},{24,248},{32,0},{40,8},{48,16},{56,24},{6... | collective-permute-start | bytes 884744 | tf_op jit(solution)/shard_map/ppermute | solution.py:47
  104.7 6.9 %collective-permute-start.22 = (bf16[1152,128]{1,0:T(8,128)(2,1)S(1)}, bf16[1152,128]{1,0:T(8,128)(2,1)S(1)}, u32[]{:S(2)}, u32[]{:S(2)}) collective-permute-start(bf16[1152,128]{1,0:T(8,128)(2,1)S(1)} %pad_maximum_fusion.1), channel_id=1, source_target_pairs={{0,32},{8,40},{16,48},{24,56},{32,64},{40,72},{48,80},{56,88},{64,... | collective-permute-start | bytes 884744 | tf_op jit(solution)/shard_map/ppermute | solution.py:47
  105.0 6.8 %collective-permute-start.26 = (bf16[1152,128]{1,0:T(8,128)(2,1)S(1)}, bf16[1152,128]{1,0:T(8,128)(2,1)S(1)}, u32[]{:S(2)}, u32[]{:S(2)}) collective-permute-start(bf16[1152,128]{1,0:T(8,128)(2,1)S(1)} %pad_maximum_fusion.4), channel_id=1, source_target_pairs={{0,224},{8,232},{16,240},{24,248},{32,0},{40,8},{48,16},{56,24},{6... | collective-permute-start | bytes 884744 | tf_op jit(solution)/shard_map/ppermute | solution.py:47
  111.7 8.1 %collective-permute-start.23 = (bf16[1152,128]{1,0:T(8,128)(2,1)S(1)}, bf16[1152,128]{1,0:T(8,128)(2,1)S(1)}, u32[]{:S(2)}, u32[]{:S(2)}) collective-permute-start(bf16[1152,128]{1,0:T(8,128)(2,1)S(1)} %pad_maximum_fusion.2), channel_id=1, source_target_pairs={{0,32},{8,40},{16,48},{24,56},{32,64},{40,72},{48,80},{56,88},{64,... | collective-permute-start | bytes 884744 | tf_op jit(solution)/shard_map/ppermute | solution.py:47
  111.9 7.6 %collective-permute-start.27 = (bf16[1024,128]{1,0:T(8,128)(2,1)S(1)}, bf16[1024,128]{1,0:T(8,128)(2,1)S(1)}, u32[]{:S(2)}, u32[]{:S(2)}) collective-permute-start(bf16[1024,128]{1,0:T(8,128)(2,1)S(1)} %fusion), channel_id=1, source_target_pairs={{0,224},{8,232},{16,240},{24,248},{32,0},{40,8},{48,16},{56,24},{6... | collective-permute-start | bytes 786440 | tf_op jit(solution)/shard_map/ppermute | solution.py:47
  120.0 6.4 %collective-permute-start.28 = (bf16[640,128]{1,0:T(8,128)(2,1)S(1)}, bf16[640,128]{1,0:T(8,128)(2,1)S(1)}, u32[]{:S(2)}, u32[]{:S(2)}) collective-permute-start(bf16[640,128]{1,0:T(8,128)(2,1)S(1)} %get-tuple-element.49.sent), channel_id=1, source_target_pairs={{0,16},{8,24},{16,0},{24,8},{32,48},{40,56},{48,32},{56,40},{64,80... | collective-permute-start | bytes 491528 | tf_op jit(solution)/shard_map/ppermute | solution.py:33
  121.6 3.1 %collective-permute-start.29 = (bf16[128,128]{1,0:T(8,128)(2,1)S(1)}, bf16[128,128]{1,0:T(8,128)(2,1)S(1)}, u32[]{:S(2)}, u32[]{:S(2)}) collective-permute-start(bf16[128,128]{1,0:T(8,128)(2,1)S(1)} %slice.122), channel_id=1, source_target_pairs={{0,4},{1,5},{2,6},{3,7},{4,0},{5,1},{6,2},{7,3},{8,12},{9,13},{10,... | collective-permute-start | bytes 98312 | tf_op jit(solution)/shard_map/ppermute | solution.py:535
  121.6 4.8 %collective-permute-start.30 = (bf16[128,128]{1,0:T(8,128)(2,1)S(1)}, bf16[128,128]{1,0:T(8,128)(2,1)S(1)}, u32[]{:S(2)}, u32[]{:S(2)}) collective-permute-start(bf16[128,128]{1,0:T(8,128)(2,1)S(1)} %slice.122), channel_id=1, source_target_pairs={{0,20},{1,21},{2,22},{3,23},{4,16},{5,17},{6,18},{7,19},{8,28},{9,... | collective-permute-start | bytes 98312 | tf_op jit(solution)/shard_map/ppermute | solution.py:539
  126.4 9.0 %collective-permute-start.31 = (bf16[768,128]{1,0:T(8,128)(2,1)S(1)}, bf16[768,128]{1,0:T(8,128)(2,1)S(1)}, u32[]{:S(2)}, u32[]{:S(2)}) collective-permute-start(bf16[768,128]{1,0:T(8,128)(2,1)S(1)} %get-tuple-element.51), channel_id=1, source_target_pairs={{0,8},{8,0},{16,24},{24,16},{32,40},{40,32},{48,56},{56,48},{64,72... | collective-permute-start | bytes 589832 | tf_op jit(solution)/shard_map/ppermute | solution.py:33
  (6 other events, 86.6 us)

commit v16 on v9

--- a/solution.py
+++ b/solution.py
@@ -202,7 +202,8 @@
         (up, down)[k >> 1][part, :] = acc[k].astype(jnp.bfloat16)
 
 
-def backward_near_kernel(lists_any, adj0, adj1, back, out, acc, lists, sem):
+def backward_near_kernel(lists_any, adj0, adj1, back, act, out, act_out, acc, lists, sem):
+    act_out[...] = act[...]
     copy = pltpu.make_async_copy(lists_any, lists, sem)
     copy.start()
     acc[...] = jnp.zeros_like(acc)
@@ -435,16 +436,16 @@
     )(lists, adj0, adj1, *received)
 
 
-def backward_near(lists, adj0, adj1, back):
+def backward_near(lists, adj0, adj1, back, act):
     return local(
         backward_near_kernel,
-        (shape(NZ * QUAD, TILE, HALF),),
-        4,
+        (shape(NZ * QUAD, TILE, HALF), shape(TILE, 2 * HALF)),
+        5,
         "backward_near",
         any_in=1,
         scratch=[pltpu.VMEM((NZ * QUAD + 1, TILE, HALF), jnp.float32)] + LIST_SCRATCH,
         cost=cost(21, 6),
-    )(lists, adj0, adj1, back)[0]
+    )(lists, adj0, adj1, back, act)
 
 
 def dense(agg_own, agg_other, weight, cot_own, cot_other):
@@ -524,7 +525,7 @@
 
     half, size = 2 * TILE, QUAD * TILE
     own, own_down, back = backward_far(lists, adj0, adj1, received)
-    blocks = backward_near(lists, adj0, adj1, back)
+    blocks, activated = backward_near(lists, adj0, adj1, back, activated)
     parts = blocks.reshape(NZ, size, HALF)
     up1, down1 = z_shift(own, 1), z_shift(own_down, -1)
     up = [add(parts[3, :half], up1[:half]), parts[3, half:], up1[half:]]

time: 136 us -> 136 us (level)
  no operation moved by 1% of the time
where the time goes in v16:
time: 136 us; the launch traced here: 135 us
  starting transfers between devices  68.7 us (51%)
  waiting for transfers between devices  52.2 us (38%)
  Pallas kernels  9.86 us (7%)
  local copies, waits for them, and re-layouts  2.39 us (2%)
  between operations  1.64 us (1%)
    ppermute x16, waiting for transfers between devices, z_shift(): return lax.ppermute(x, 'row', row_pairs(lambda z, q: (z + step, q)))  29.2 us
    ppermute x16, starting transfers between devices, z_shift(): return lax.ppermute(x, 'row', row_pairs(lambda z, q: (z + step, q)))  26.5 us
    ppermute x14, starting transfers between devices, col_move(): return lax.ppermute(x, 'col', pairs)  20.6 us
    ppermute x7, starting transfers between devices, quad_permute(): return lax.ppermute(x, 'row', row_pairs(lambda z, q: (z, q ^ flip)))  20.4 us
    ppermute x14, waiting for transfers between devices, col_move(): return lax.ppermute(x, 'col', pairs)  16.9 us
    ppermute x7, waiting for transfers between devices, quad_permute(): return lax.ppermute(x, 'row', row_pairs(lambda z, q: (z, q ^ flip)))  3.3 us
  transfers between devices with their start and end apart: 39, of which 20 were waited for; matrix products, arithmetic and copies ran while one was open for 0% of the time, Pallas kernels for 4%

profile of v16, /device:TPU:1, one launch (start us, length us, event | category | flops | bytes accessed | tf_op | source)
XLA Modules:
  0.0 135.5 jit_solution(14150267219494138679)
XLA Ops:
  0.6 3.7 %collective-permute-start = (bf16[256,256]{1,0:T(8,128)(2,1)}, bf16[256,256]{1,0:T(8,128)(2,1)S(1)}, u32[]{:S(2)}, u32[]{:S(2)}) collective-permute-start(bf16[256,256]{1,0:T(8,128)(2,1)} %bitcast.51), channel_id=1, source_target_pairs={{0,16},{8,24},{16,0},{24,8},{32,48},{40,56},{48,32},{56,40},{64,80... | collective-permute-start | bytes 393224 | tf_op jit(solution)/shard_map/ppermute | solution.py:33
  11.8 4.7 %collective-permute-start.3 = (bf16[4,256,128]{2,1,0:T(8,128)(2,1)S(1)}, bf16[4,256,128]{2,1,0:T(8,128)(2,1)S(1)}, u32[]{:S(2)}, u32[]{:S(2)}) collective-permute-start(bf16[4,256,128]{2,1,0:T(8,128)(2,1)S(1)} %pad_maximum_fusion.5.refs_0_), channel_id=1, source_target_pairs={{0,224},{8,232},{16,240},{24,248},{32,0},{40,8},{48,16},{56,24},{6... | collective-permute-start | bytes 786440 | tf_op jit(solution)/shard_map/ppermute | solution.py:47
  16.5 5.6 %collective-permute-done.3.refs_1_ = bf16[4,256,128]{2,1,0:T(8,128)(2,1)S(1)} collective-permute-done((bf16[4,256,128]{2,1,0:T(8,128)(2,1)S(1)}, bf16[4,256,128]{2,1,0:T(8,128)(2,1)S(1)}, u32[]{:S(2)}, u32[]{:S(2)}) %collective-permute-start.3) | collective-permute-done | bytes 262176 | tf_op jit(solution)/shard_map/ppermute | solution.py:47
  22.1 3.4 %collective-permute-start.4 = (bf16[4,256,128]{2,1,0:T(8,128)(2,1)S(1)}, bf16[4,256,128]{2,1,0:T(8,128)(2,1)S(1)}, u32[]{:S(2)}, u32[]{:S(2)}) collective-permute-start(bf16[4,256,128]{2,1,0:T(8,128)(2,1)S(1)} %collective-permute-done.3.refs_1_), channel_id=1, source_target_pairs={{0,224},{8,232},{16,240},{24,248},{32,0},{40,8},{48,16},{56,24},{6... | collective-permute-start | bytes 786440 | tf_op jit(solution)/shard_map/ppermute | solution.py:47
  25.5 4.6 %collective-permute-done.4.refs_2_ = bf16[4,256,128]{2,1,0:T(8,128)(2,1)S(1)} collective-permute-done((bf16[4,256,128]{2,1,0:T(8,128)(2,1)S(1)}, bf16[4,256,128]{2,1,0:T(8,128)(2,1)S(1)}, u32[]{:S(2)}, u32[]{:S(2)}) %collective-permute-start.4) | collective-permute-done | bytes 262176 | tf_op jit(solution)/shard_map/ppermute | solution.py:47
  30.1 3.4 %collective-permute-start.5 = (bf16[4,256,128]{2,1,0:T(8,128)(2,1)S(1)}, bf16[4,256,128]{2,1,0:T(8,128)(2,1)S(1)}, u32[]{:S(2)}, u32[]{:S(2)}) collective-permute-start(bf16[4,256,128]{2,1,0:T(8,128)(2,1)S(1)} %collective-permute-done.4.refs_2_), channel_id=1, source_target_pairs={{0,224},{8,232},{16,240},{24,248},{32,0},{40,8},{48,16},{56,24},{6... | collective-permute-start | bytes 786440 | tf_op jit(solution)/shard_map/ppermute | solution.py:47
  33.6 3.7 %collective-permute-done.5.refs_3_ = bf16[4,256,128]{2,1,0:T(8,128)(2,1)S(1)} collective-permute-done((bf16[4,256,128]{2,1,0:T(8,128)(2,1)S(1)}, bf16[4,256,128]{2,1,0:T(8,128)(2,1)S(1)}, u32[]{:S(2)}, u32[]{:S(2)}) %collective-permute-start.5) | collective-permute-done | bytes 262176 | tf_op jit(solution)/shard_map/ppermute | solution.py:47
  37.3 3.5 %collective-permute-start.10 = (bf16[2,256,128]{2,1,0:T(8,128)(2,1)S(1)}, bf16[2,256,128]{2,1,0:T(8,128)(2,1)S(1)}, u32[]{:S(2)}, u32[]{:S(2)}) collective-permute-start(bf16[2,256,128]{2,1,0:T(8,128)(2,1)S(1)} %slice.127), channel_id=1, source_target_pairs={{0,224},{8,232},{16,240},{24,248},{32,0},{40,8},{48,16},{56,24},{6... | collective-permute-start | bytes 393224 | tf_op jit(solution)/shard_map/ppermute | solution.py:47
  40.9 2.3 %forward_near.1 = (f32[18,256,128]{2,1,0:T(8,128)S(1)}, s32[68]{0:T(128)S(1)}) custom-call(s32[25]{0:T(128)S(1)} %get-tuple-element.33.own_any, s32[25]{0:T(128)S(1)} %fusion.6.partner_any, bf16[12,256,256]{2,1,0:T(8,128)(2,1)S(1)} %bitcast.43, bf16[12,256,256]{2,1,0:T(8,128)(2,1)S(1)} %collective-permute-done.2.adj1, ...), custom_call_target="tpu_custom_call" | custom-call | flops 352321536 | bytes 6291456 | tf_op jit(solution)/shard_map/forward_near/pallas_call | solution.py:391
  43.3 2.7 %collective-permute-done.9.far_a = bf16[2,256,128]{2,1,0:T(8,128)(2,1)S(1)} collective-permute-done((bf16[2,256,128]{2,1,0:T(8,128)(2,1)S(1)}, bf16[2,256,128]{2,1,0:T(8,128)(2,1)S(1)}, u32[]{:S(2)}, u32[]{:S(2)}) %collective-permute-start.9) | collective-permute-done | bytes 131104 | tf_op jit(solution)/shard_map/ppermute | solution.py:47
  46.8 2.5 %collective-permute-start.11 = (bf16[2,256,128]{2,1,0:T(8,128)(2,1)S(1)}, bf16[2,256,128]{2,1,0:T(8,128)(2,1)S(1)}, u32[]{:S(2)}, u32[]{:S(2)}) collective-permute-start(bf16[2,256,128]{2,1,0:T(8,128)(2,1)S(1)} %get-tuple-element.41), channel_id=1, source_target_pairs={{0,6},{1,7},{2,4},{3,5},{4,2},{5,3},{6,0},{7,1},{8,14},{9,15},{10,... | collective-permute-start | bytes 393224 | tf_op jit(solution)/shard_map/ppermute | solution.py:38
  49.9 2.2 %collective-permute-start.13 = (bf16[2,256,128]{2,1,0:T(8,128)(2,1)S(1)}, bf16[2,256,128]{2,1,0:T(8,128)(2,1)S(1)}, u32[]{:S(2)}, u32[]{:S(2)}) collective-permute-start(bf16[2,256,128]{2,1,0:T(8,128)(2,1)S(1)} %get-tuple-element.43), channel_id=1, source_target_pairs={{0,5},{1,6},{2,7},{3,4},{4,1},{5,2},{6,3},{7,0},{8,13},{9,14},{10,... | collective-permute-start | bytes 393224 | tf_op jit(solution)/shard_map/ppermute | solution.py:38
  52.0 1.8 %collective-permute-start.14 = (bf16[2,256,128]{2,1,0:T(8,128)(2,1)S(1)}, bf16[2,256,128]{2,1,0:T(8,128)(2,1)S(1)}, u32[]{:S(2)}, u32[]{:S(2)}) collective-permute-start(bf16[2,256,128]{2,1,0:T(8,128)(2,1)S(1)} %get-tuple-element.44), channel_id=1, source_target_pairs={{0,7},{1,4},{2,5},{3,6},{4,3},{5,0},{6,1},{7,2},{8,15},{9,12},{10,... | collective-permute-start | bytes 393224 | tf_op jit(solution)/shard_map/ppermute | solution.py:38
  53.8 2.7 %collective-permute-start.16 = (bf16[2,256,128]{2,1,0:T(8,128)(2,1)S(1)}, bf16[2,256,128]{2,1,0:T(8,128)(2,1)S(1)}, u32[]{:S(2)}, u32[]{:S(2)}) collective-permute-start(bf16[2,256,128]{2,1,0:T(8,128)(2,1)S(1)} %get-tuple-element.46), channel_id=1, source_target_pairs={{0,3},{1,0},{2,1},{3,2},{4,7},{5,4},{6,5},{7,6},{8,11},{9,8},{10,9... | collective-permute-start | bytes 393224 | tf_op jit(solution)/shard_map/ppermute | solution.py:38
  57.3 5.3 %collective-permute-done.15 = bf16[2,256,128]{2,1,0:T(8,128)(2,1)S(1)} collective-permute-done((bf16[2,256,128]{2,1,0:T(8,128)(2,1)S(1)}, bf16[2,256,128]{2,1,0:T(8,128)(2,1)S(1)}, u32[]{:S(2)}, u32[]{:S(2)}) %collective-permute-start.15) | collective-permute-done | bytes 131104 | tf_op jit(solution)/shard_map/ppermute | solution.py:38
  62.7 4.8 %collective-permute-start.18 = (f32[512,128]{1,0:T(8,128)S(1)}, f32[512,128]{1,0:T(8,128)S(1)}, u32[]{:S(2)}, u32[]{:S(2)}) collective-permute-start(f32[512,128]{1,0:T(8,128)S(1)} %bitcast.49), channel_id=1, source_target_pairs={{0,8},{8,0},{16,24},{24,16},{32,40},{40,32},{48,56},{56,48},{64,72... | collective-permute-start | bytes 786440 | tf_op jit(solution)/shard_map/ppermute | solution.py:33
  72.1 2.2 %collective-permute-start.21 = (bf16[640,128]{1,0:T(8,128)(2,1)S(1)}, bf16[640,128]{1,0:T(8,128)(2,1)S(1)}, u32[]{:S(2)}, u32[]{:S(2)}) collective-permute-start(bf16[640,128]{1,0:T(8,128)(2,1)S(1)} %get-tuple-element.48.refs_0_), channel_id=1, source_target_pairs={{0,2},{1,3},{2,0},{3,1},{4,6},{5,7},{6,4},{7,5},{8,10},{9,11},{10,... | collective-permute-start | bytes 491528 | tf_op jit(solution)/shard_map/ppermute | solution.py:38
  74.3 1.9 %collective-permute-start.22 = (bf16[640,128]{1,0:T(8,128)(2,1)S(1)}, bf16[640,128]{1,0:T(8,128)(2,1)S(1)}, u32[]{:S(2)}, u32[]{:S(2)}) collective-permute-start(bf16[640,128]{1,0:T(8,128)(2,1)S(1)} %get-tuple-element.49), channel_id=1, source_target_pairs={{0,5},{1,6},{2,7},{3,4},{4,1},{5,2},{6,3},{7,0},{8,13},{9,14},{10,... | collective-permute-start | bytes 491528 | tf_op jit(solution)/shard_map/ppermute | solution.py:38
  78.3 2.2 %collective-permute-start.25 = (bf16[640,128]{1,0:T(8,128)(2,1)S(1)}, bf16[640,128]{1,0:T(8,128)(2,1)S(1)}, u32[]{:S(2)}, u32[]{:S(2)}) collective-permute-start(bf16[640,128]{1,0:T(8,128)(2,1)S(1)} %get-tuple-element.48.refs_0_), channel_id=1, source_target_pairs={{0,3},{1,0},{2,1},{3,2},{4,7},{5,4},{6,5},{7,6},{8,11},{9,8},{10,9... | collective-permute-start | bytes 491528 | tf_op jit(solution)/shard_map/ppermute | solution.py:38
  80.5 6.3 %collective-permute-done.21.refs_2_ = bf16[640,128]{1,0:T(8,128)(2,1)S(1)} collective-permute-done((bf16[640,128]{1,0:T(8,128)(2,1)S(1)}, bf16[640,128]{1,0:T(8,128)(2,1)S(1)}, u32[]{:S(2)}, u32[]{:S(2)}) %collective-permute-start.21) | collective-permute-done | bytes 163872 | tf_op jit(solution)/shard_map/ppermute | solution.py:38
  87.2 3.1 %collective-permute-done.24.refs_5_ = bf16[640,128]{1,0:T(8,128)(2,1)S(1)} collective-permute-done((bf16[640,128]{1,0:T(8,128)(2,1)S(1)}, bf16[640,128]{1,0:T(8,128)(2,1)S(1)}, u32[]{:S(2)}, u32[]{:S(2)}) %collective-permute-start.24) | collective-permute-done | bytes 163872 | tf_op jit(solution)/shard_map/ppermute | solution.py:38
  92.9 2.7 %collective-permute-start.31 = (bf16[640,128]{1,0:T(8,128)(2,1)S(1)}, bf16[640,128]{1,0:T(8,128)(2,1)S(1)}, u32[]{:S(2)}, u32[]{:S(2)}) collective-permute-start(bf16[640,128]{1,0:T(8,128)(2,1)S(1)} %get-tuple-element.55), channel_id=1, source_target_pairs={{0,224},{8,232},{16,240},{24,248},{32,0},{40,8},{48,16},{56,24},{6... | collective-permute-start | bytes 491528 | tf_op jit(solution)/shard_map/ppermute | solution.py:47
  95.6 2.2 %backward_near.1 = (bf16[32,256,128]{2,1,0:T(8,128)(2,1)S(1)}, bf16[256,256]{1,0:T(8,128)(2,1)}) custom-call(s32[68]{0:T(128)S(1)} %get-tuple-element.38.lists_any, bf16[12,256,256]{2,1,0:T(8,128)(2,1)S(1)} %bitcast.46, bf16[12,256,256]{2,1,0:T(8,128)(2,1)S(1)} %collective-permute-done.2.adj1, bf16[8,512,128]{2,1,0:T(8,128)(2,1)S(1)} %get-tuple-element.50.back, ...), custom_call_target="tpu_custom_call" | custom-call | flops 352321536 | bytes 6291456 | tf_op jit(solution)/shard_map/backward_near/pallas_call | solution.py:440
  98.9 2.7 %collective-permute-start.32 = (bf16[1152,128]{1,0:T(8,128)(2,1)S(1)}, bf16[1152,128]{1,0:T(8,128)(2,1)S(1)}, u32[]{:S(2)}, u32[]{:S(2)}) collective-permute-start(bf16[1152,128]{1,0:T(8,128)(2,1)S(1)} %pad_maximum_fusion.3), channel_id=1, source_target_pairs={{0,224},{8,232},{16,240},{24,248},{32,0},{40,8},{48,16},{56,24},{6... | collective-permute-start | bytes 884744 | tf_op jit(solution)/shard_map/ppermute | solution.py:47
  101.6 4.2 %collective-permute-done.28.up2 = bf16[1152,128]{1,0:T(8,128)(2,1)S(1)} collective-permute-done((bf16[1152,128]{1,0:T(8,128)(2,1)S(1)}, bf16[1152,128]{1,0:T(8,128)(2,1)S(1)}, u32[]{:S(2)}, u32[]{:S(2)}) %collective-permute-start.28) | collective-permute-done | bytes 294944 | tf_op jit(solution)/shard_map/ppermute | solution.py:47
  106.2 2.7 %collective-permute-start.33 = (bf16[1152,128]{1,0:T(8,128)(2,1)S(1)}, bf16[1152,128]{1,0:T(8,128)(2,1)S(1)}, u32[]{:S(2)}, u32[]{:S(2)}) collective-permute-start(bf16[1152,128]{1,0:T(8,128)(2,1)S(1)} %pad_maximum_fusion.4), channel_id=1, source_target_pairs={{0,224},{8,232},{16,240},{24,248},{32,0},{40,8},{48,16},{56,24},{6... | collective-permute-start | bytes 884744 | tf_op jit(solution)/shard_map/ppermute | solution.py:47
  108.9 3.9 %collective-permute-done.29.up3 = bf16[1152,128]{1,0:T(8,128)(2,1)S(1)} collective-permute-done((bf16[1152,128]{1,0:T(8,128)(2,1)S(1)}, bf16[1152,128]{1,0:T(8,128)(2,1)S(1)}, u32[]{:S(2)}, u32[]{:S(2)}) %collective-permute-start.29) | collective-permute-done | bytes 294944 | tf_op jit(solution)/shard_map/ppermute | solution.py:47
  113.2 2.7 %collective-permute-start.34 = (bf16[1024,128]{1,0:T(8,128)(2,1)S(1)}, bf16[1024,128]{1,0:T(8,128)(2,1)S(1)}, u32[]{:S(2)}, u32[]{:S(2)}) collective-permute-start(bf16[1024,128]{1,0:T(8,128)(2,1)S(1)} %fusion), channel_id=1, source_target_pairs={{0,224},{8,232},{16,240},{24,248},{32,0},{40,8},{48,16},{56,24},{6... | collective-permute-start | bytes 786440 | tf_op jit(solution)/shard_map/ppermute | solution.py:47
  115.9 3.8 %collective-permute-done.34.down4 = bf16[1024,128]{1,0:T(8,128)(2,1)S(1)} collective-permute-done((bf16[1024,128]{1,0:T(8,128)(2,1)S(1)}, bf16[1024,128]{1,0:T(8,128)(2,1)S(1)}, u32[]{:S(2)}, u32[]{:S(2)}) %collective-permute-start.34) | collective-permute-done | bytes 262176 | tf_op jit(solution)/shard_map/ppermute | solution.py:47
  120.1 2.1 %collective-permute-start.35 = (bf16[640,128]{1,0:T(8,128)(2,1)S(1)}, bf16[640,128]{1,0:T(8,128)(2,1)S(1)}, u32[]{:S(2)}, u32[]{:S(2)}) collective-permute-start(bf16[640,128]{1,0:T(8,128)(2,1)S(1)} %get-tuple-element.57.sent), channel_id=1, source_target_pairs={{0,16},{8,24},{16,0},{24,8},{32,48},{40,56},{48,32},{56,40},{64,80... | collective-permute-start | bytes 491528 | tf_op jit(solution)/shard_map/ppermute | solution.py:33
  123.5 1.9 %collective-permute-done.36.w_lo = bf16[128,128]{1,0:T(8,128)(2,1)S(1)} collective-permute-done((bf16[128,128]{1,0:T(8,128)(2,1)S(1)}, bf16[128,128]{1,0:T(8,128)(2,1)S(1)}, u32[]{:S(2)}, u32[]{:S(2)}) %collective-permute-start.36) | collective-permute-done | bytes 32800 | tf_op jit(solution)/shard_map/ppermute | solution.py:543
  126.3 7.3 %collective-permute-start.38 = (bf16[768,128]{1,0:T(8,128)(2,1)S(1)}, bf16[768,128]{1,0:T(8,128)(2,1)S(1)}, u32[]{:S(2)}, u32[]{:S(2)}) collective-permute-start(bf16[768,128]{1,0:T(8,128)(2,1)S(1)} %get-tuple-element.59), channel_id=1, source_target_pairs={{0,8},{8,0},{16,24},{24,16},{32,40},{40,32},{48,56},{56,48},{64,72... | collective-permute-start | bytes 589832 | tf_op jit(solution)/shard_map/ppermute | solution.py:33
  (93 shorter events, 24.9 us)
Async XLA Ops:
  0.6 8.7 %collective-permute-start = (bf16[256,256]{1,0:T(8,128)(2,1)}, bf16[256,256]{1,0:T(8,128)(2,1)S(1)}, u32[]{:S(2)}, u32[]{:S(2)}) collective-permute-start(bf16[256,256]{1,0:T(8,128)(2,1)} %bitcast.51), channel_id=1, source_target_pairs={{0,16},{8,24},{16,0},{24,8},{32,48},{40,56},{48,32},{56,40},{64,80... | collective-permute-start | bytes 393224 | tf_op jit(solution)/shard_map/ppermute | solution.py:33
  4.3 36.6 %collective-permute-start.2 = (bf16[12,256,256]{2,1,0:T(8,128)(2,1)}, bf16[12,256,256]{2,1,0:T(8,128)(2,1)S(1)}, u32[]{:S(2)}, u32[]{:S(2)}) collective-permute-start(bf16[12,256,256]{2,1,0:T(8,128)(2,1)} %bitcast.42), channel_id=1, source_target_pairs={{0,8},{8,0},{16,24},{24,16},{32,40},{40,32},{48,56},{56,48},{64,72... | collective-permute-start | bytes 4718600 | tf_op jit(solution)/shard_map/ppermute | solution.py:33
  11.8 10.3 %collective-permute-start.3 = (bf16[4,256,128]{2,1,0:T(8,128)(2,1)S(1)}, bf16[4,256,128]{2,1,0:T(8,128)(2,1)S(1)}, u32[]{:S(2)}, u32[]{:S(2)}) collective-permute-start(bf16[4,256,128]{2,1,0:T(8,128)(2,1)S(1)} %pad_maximum_fusion.5.refs_0_), channel_id=1, source_target_pairs={{0,224},{8,232},{16,240},{24,248},{32,0},{40,8},{48,16},{56,24},{6... | collective-permute-start | bytes 786440 | tf_op jit(solution)/shard_map/ppermute | solution.py:47
  16.5 9.0 %collective-permute-start.6 = (bf16[4,256,128]{2,1,0:T(8,128)(2,1)S(1)}, bf16[4,256,128]{2,1,0:T(8,128)(2,1)S(1)}, u32[]{:S(2)}, u32[]{:S(2)}) collective-permute-start(bf16[4,256,128]{2,1,0:T(8,128)(2,1)S(1)} %pad_maximum_fusion.5.refs_0_), channel_id=1, source_target_pairs={{0,32},{8,40},{16,48},{24,56},{32,64},{40,72},{48,80},{56,88},{64,... | collective-permute-start | bytes 786440 | tf_op jit(solution)/shard_map/ppermute | solution.py:47
  22.1 8.1 %collective-permute-start.4 = (bf16[4,256,128]{2,1,0:T(8,128)(2,1)S(1)}, bf16[4,256,128]{2,1,0:T(8,128)(2,1)S(1)}, u32[]{:S(2)}, u32[]{:S(2)}) collective-permute-start(bf16[4,256,128]{2,1,0:T(8,128)(2,1)S(1)} %collective-permute-done.3.refs_1_), channel_id=1, source_target_pairs={{0,224},{8,232},{16,240},{24,248},{32,0},{40,8},{48,16},{56,24},{6... | collective-permute-start | bytes 786440 | tf_op jit(solution)/shard_map/ppermute | solution.py:47
  25.5 8.1 %collective-permute-start.7 = (bf16[4,256,128]{2,1,0:T(8,128)(2,1)S(1)}, bf16[4,256,128]{2,1,0:T(8,128)(2,1)S(1)}, u32[]{:S(2)}, u32[]{:S(2)}) collective-permute-start(bf16[4,256,128]{2,1,0:T(8,128)(2,1)S(1)} %collective-permute-done.6.refs_6_), channel_id=1, source_target_pairs={{0,32},{8,40},{16,48},{24,56},{32,64},{40,72},{48,80},{56,88},{64,... | collective-permute-start | bytes 786440 | tf_op jit(solution)/shard_map/ppermute | solution.py:47
  30.1 7.1 %collective-permute-start.5 = (bf16[4,256,128]{2,1,0:T(8,128)(2,1)S(1)}, bf16[4,256,128]{2,1,0:T(8,128)(2,1)S(1)}, u32[]{:S(2)}, u32[]{:S(2)}) collective-permute-start(bf16[4,256,128]{2,1,0:T(8,128)(2,1)S(1)} %collective-permute-done.4.refs_2_), channel_id=1, source_target_pairs={{0,224},{8,232},{16,240},{24,248},{32,0},{40,8},{48,16},{56,24},{6... | collective-permute-start | bytes 786440 | tf_op jit(solution)/shard_map/ppermute | solution.py:47
  33.6 7.2 %collective-permute-start.8 = (bf16[4,256,128]{2,1,0:T(8,128)(2,1)S(1)}, bf16[4,256,128]{2,1,0:T(8,128)(2,1)S(1)}, u32[]{:S(2)}, u32[]{:S(2)}) collective-permute-start(bf16[4,256,128]{2,1,0:T(8,128)(2,1)S(1)} %collective-permute-done.7.refs_5_), channel_id=1, source_target_pairs={{0,32},{8,40},{16,48},{24,56},{32,64},{40,72},{48,80},{56,88},{64,... | collective-permute-start | bytes 786440 | tf_op jit(solution)/shard_map/ppermute | solution.py:47
  37.3 6.0 %collective-permute-start.10 = (bf16[2,256,128]{2,1,0:T(8,128)(2,1)S(1)}, bf16[2,256,128]{2,1,0:T(8,128)(2,1)S(1)}, u32[]{:S(2)}, u32[]{:S(2)}) collective-permute-start(bf16[2,256,128]{2,1,0:T(8,128)(2,1)S(1)} %slice.127), channel_id=1, source_target_pairs={{0,224},{8,232},{16,240},{24,248},{32,0},{40,8},{48,16},{56,24},{6... | collective-permute-start | bytes 393224 | tf_op jit(solution)/shard_map/ppermute | solution.py:47
  46.8 7.0 %collective-permute-start.11 = (bf16[2,256,128]{2,1,0:T(8,128)(2,1)S(1)}, bf16[2,256,128]{2,1,0:T(8,128)(2,1)S(1)}, u32[]{:S(2)}, u32[]{:S(2)}) collective-permute-start(bf16[2,256,128]{2,1,0:T(8,128)(2,1)S(1)} %get-tuple-element.41), channel_id=1, source_target_pairs={{0,6},{1,7},{2,4},{3,5},{4,2},{5,3},{6,0},{7,1},{8,14},{9,15},{10,... | collective-permute-start | bytes 393224 | tf_op jit(solution)/shard_map/ppermute | solution.py:38
  49.3 7.2 %collective-permute-start.12 = (bf16[2,256,128]{2,1,0:T(8,128)(2,1)S(1)}, bf16[2,256,128]{2,1,0:T(8,128)(2,1)S(1)}, u32[]{:S(2)}, u32[]{:S(2)}) collective-permute-start(bf16[2,256,128]{2,1,0:T(8,128)(2,1)S(1)} %get-tuple-element.42), channel_id=1, source_target_pairs={{0,2},{1,3},{2,0},{3,1},{4,6},{5,7},{6,4},{7,5},{8,10},{9,11},{10,... | collective-permute-start | bytes 393224 | tf_op jit(solution)/shard_map/ppermute | solution.py:38
  49.9 7.4 %collective-permute-start.13 = (bf16[2,256,128]{2,1,0:T(8,128)(2,1)S(1)}, bf16[2,256,128]{2,1,0:T(8,128)(2,1)S(1)}, u32[]{:S(2)}, u32[]{:S(2)}) collective-permute-start(bf16[2,256,128]{2,1,0:T(8,128)(2,1)S(1)} %get-tuple-element.43), channel_id=1, source_target_pairs={{0,5},{1,6},{2,7},{3,4},{4,1},{5,2},{6,3},{7,0},{8,13},{9,14},{10,... | collective-permute-start | bytes 393224 | tf_op jit(solution)/shard_map/ppermute | solution.py:38
  53.8 8.8 %collective-permute-start.15 = (bf16[2,256,128]{2,1,0:T(8,128)(2,1)S(1)}, bf16[2,256,128]{2,1,0:T(8,128)(2,1)S(1)}, u32[]{:S(2)}, u32[]{:S(2)}) collective-permute-start(bf16[2,256,128]{2,1,0:T(8,128)(2,1)S(1)} %get-tuple-element.45), channel_id=1, source_target_pairs={{0,1},{1,2},{2,3},{3,0},{4,5},{5,6},{6,7},{7,4},{8,9},{9,10},{10,1... | collective-permute-start | bytes 393224 | tf_op jit(solution)/shard_map/ppermute | solution.py:38
  53.8 8.8 %collective-permute-start.16 = (bf16[2,256,128]{2,1,0:T(8,128)(2,1)S(1)}, bf16[2,256,128]{2,1,0:T(8,128)(2,1)S(1)}, u32[]{:S(2)}, u32[]{:S(2)}) collective-permute-start(bf16[2,256,128]{2,1,0:T(8,128)(2,1)S(1)} %get-tuple-element.46), channel_id=1, source_target_pairs={{0,3},{1,0},{2,1},{3,2},{4,7},{5,4},{6,5},{7,6},{8,11},{9,8},{10,9... | collective-permute-start | bytes 393224 | tf_op jit(solution)/shard_map/ppermute | solution.py:38
  56.5 6.1 %collective-permute-start.17 = (bf16[2,256,128]{2,1,0:T(8,128)(2,1)S(1)}, bf16[2,256,128]{2,1,0:T(8,128)(2,1)S(1)}, u32[]{:S(2)}, u32[]{:S(2)}) collective-permute-start(bf16[2,256,128]{2,1,0:T(8,128)(2,1)S(1)} %get-tuple-element.47), channel_id=1, source_target_pairs={{0,4},{1,5},{2,6},{3,7},{4,0},{5,1},{6,2},{7,3},{8,12},{9,13},{10,... | collective-permute-start | bytes 393224 | tf_op jit(solution)/shard_map/ppermute | solution.py:38
  62.7 6.2 %collective-permute-start.18 = (f32[512,128]{1,0:T(8,128)S(1)}, f32[512,128]{1,0:T(8,128)S(1)}, u32[]{:S(2)}, u32[]{:S(2)}) collective-permute-start(f32[512,128]{1,0:T(8,128)S(1)} %bitcast.49), channel_id=1, source_target_pairs={{0,8},{8,0},{16,24},{24,16},{32,40},{40,32},{48,56},{56,48},{64,72... | collective-permute-start | bytes 786440 | tf_op jit(solution)/shard_map/ppermute | solution.py:33
  70.3 7.9 %collective-permute-start.20 = (bf16[640,128]{1,0:T(8,128)(2,1)S(1)}, bf16[640,128]{1,0:T(8,128)(2,1)S(1)}, u32[]{:S(2)}, u32[]{:S(2)}) collective-permute-start(bf16[640,128]{1,0:T(8,128)(2,1)S(1)} %get-tuple-element.49), channel_id=1, source_target_pairs={{0,6},{1,7},{2,4},{3,5},{4,2},{5,3},{6,0},{7,1},{8,14},{9,15},{10,... | collective-permute-start | bytes 491528 | tf_op jit(solution)/shard_map/ppermute | solution.py:38
  72.1 14.8 %collective-permute-start.21 = (bf16[640,128]{1,0:T(8,128)(2,1)S(1)}, bf16[640,128]{1,0:T(8,128)(2,1)S(1)}, u32[]{:S(2)}, u32[]{:S(2)}) collective-permute-start(bf16[640,128]{1,0:T(8,128)(2,1)S(1)} %get-tuple-element.48.refs_0_), channel_id=1, source_target_pairs={{0,2},{1,3},{2,0},{3,1},{4,6},{5,7},{6,4},{7,5},{8,10},{9,11},{10,... | collective-permute-start | bytes 491528 | tf_op jit(solution)/shard_map/ppermute | solution.py:38
  74.3 12.9 %collective-permute-start.22 = (bf16[640,128]{1,0:T(8,128)(2,1)S(1)}, bf16[640,128]{1,0:T(8,128)(2,1)S(1)}, u32[]{:S(2)}, u32[]{:S(2)}) collective-permute-start(bf16[640,128]{1,0:T(8,128)(2,1)S(1)} %get-tuple-element.49), channel_id=1, source_target_pairs={{0,5},{1,6},{2,7},{3,4},{4,1},{5,2},{6,3},{7,0},{8,13},{9,14},{10,... | collective-permute-start | bytes 491528 | tf_op jit(solution)/shard_map/ppermute | solution.py:38
  76.2 11.0 %collective-permute-start.23 = (bf16[640,128]{1,0:T(8,128)(2,1)S(1)}, bf16[640,128]{1,0:T(8,128)(2,1)S(1)}, u32[]{:S(2)}, u32[]{:S(2)}) collective-permute-start(bf16[640,128]{1,0:T(8,128)(2,1)S(1)} %get-tuple-element.49), channel_id=1, source_target_pairs={{0,7},{1,4},{2,5},{3,6},{4,3},{5,0},{6,1},{7,2},{8,15},{9,12},{10,... | collective-permute-start | bytes 491528 | tf_op jit(solution)/shard_map/ppermute | solution.py:38
  77.9 12.5 %collective-permute-start.24 = (bf16[640,128]{1,0:T(8,128)(2,1)S(1)}, bf16[640,128]{1,0:T(8,128)(2,1)S(1)}, u32[]{:S(2)}, u32[]{:S(2)}) collective-permute-start(bf16[640,128]{1,0:T(8,128)(2,1)S(1)} %get-tuple-element.48.refs_0_), channel_id=1, source_target_pairs={{0,1},{1,2},{2,3},{3,0},{4,5},{5,6},{6,7},{7,4},{8,9},{9,10},{10,1... | collective-permute-start | bytes 491528 | tf_op jit(solution)/shard_map/ppermute | solution.py:38
  78.3 12.0 %collective-permute-start.25 = (bf16[640,128]{1,0:T(8,128)(2,1)S(1)}, bf16[640,128]{1,0:T(8,128)(2,1)S(1)}, u32[]{:S(2)}, u32[]{:S(2)}) collective-permute-start(bf16[640,128]{1,0:T(8,128)(2,1)S(1)} %get-tuple-element.48.refs_0_), channel_id=1, source_target_pairs={{0,3},{1,0},{2,1},{3,2},{4,7},{5,4},{6,5},{7,6},{8,11},{9,8},{10,9... | collective-permute-start | bytes 491528 | tf_op jit(solution)/shard_map/ppermute | solution.py:38
  92.8 5.5 %collective-permute-start.27 = (bf16[640,128]{1,0:T(8,128)(2,1)S(1)}, bf16[640,128]{1,0:T(8,128)(2,1)S(1)}, u32[]{:S(2)}, u32[]{:S(2)}) collective-permute-start(bf16[640,128]{1,0:T(8,128)(2,1)S(1)} %get-tuple-element.54.own), channel_id=1, source_target_pairs={{0,32},{8,40},{16,48},{24,56},{32,64},{40,72},{48,80},{56,88},{64,... | collective-permute-start | bytes 491528 | tf_op jit(solution)/shard_map/ppermute | solution.py:47
  92.9 5.4 %collective-permute-start.31 = (bf16[640,128]{1,0:T(8,128)(2,1)S(1)}, bf16[640,128]{1,0:T(8,128)(2,1)S(1)}, u32[]{:S(2)}, u32[]{:S(2)}) collective-permute-start(bf16[640,128]{1,0:T(8,128)(2,1)S(1)} %get-tuple-element.55), channel_id=1, source_target_pairs={{0,224},{8,232},{16,240},{24,248},{32,0},{40,8},{48,16},{56,24},{6... | collective-permute-start | bytes 491528 | tf_op jit(solution)/shard_map/ppermute | solution.py:47
  98.4 7.4 %collective-permute-start.28 = (bf16[1152,128]{1,0:T(8,128)(2,1)S(1)}, bf16[1152,128]{1,0:T(8,128)(2,1)S(1)}, u32[]{:S(2)}, u32[]{:S(2)}) collective-permute-start(bf16[1152,128]{1,0:T(8,128)(2,1)S(1)} %pad_maximum_fusion), channel_id=1, source_target_pairs={{0,32},{8,40},{16,48},{24,56},{32,64},{40,72},{48,80},{56,88},{64,... | collective-permute-start | bytes 884744 | tf_op jit(solution)/shard_map/ppermute | solution.py:47
  98.9 7.2 %collective-permute-start.32 = (bf16[1152,128]{1,0:T(8,128)(2,1)S(1)}, bf16[1152,128]{1,0:T(8,128)(2,1)S(1)}, u32[]{:S(2)}, u32[]{:S(2)}) collective-permute-start(bf16[1152,128]{1,0:T(8,128)(2,1)S(1)} %pad_maximum_fusion.3), channel_id=1, source_target_pairs={{0,224},{8,232},{16,240},{24,248},{32,0},{40,8},{48,16},{56,24},{6... | collective-permute-start | bytes 884744 | tf_op jit(solution)/shard_map/ppermute | solution.py:47
  106.0 6.9 %collective-permute-start.29 = (bf16[1152,128]{1,0:T(8,128)(2,1)S(1)}, bf16[1152,128]{1,0:T(8,128)(2,1)S(1)}, u32[]{:S(2)}, u32[]{:S(2)}) collective-permute-start(bf16[1152,128]{1,0:T(8,128)(2,1)S(1)} %pad_maximum_fusion.1), channel_id=1, source_target_pairs={{0,32},{8,40},{16,48},{24,56},{32,64},{40,72},{48,80},{56,88},{64,... | collective-permute-start | bytes 884744 | tf_op jit(solution)/shard_map/ppermute | solution.py:47
  106.2 6.8 %collective-permute-start.33 = (bf16[1152,128]{1,0:T(8,128)(2,1)S(1)}, bf16[1152,128]{1,0:T(8,128)(2,1)S(1)}, u32[]{:S(2)}, u32[]{:S(2)}) collective-permute-start(bf16[1152,128]{1,0:T(8,128)(2,1)S(1)} %pad_maximum_fusion.4), channel_id=1, source_target_pairs={{0,224},{8,232},{16,240},{24,248},{32,0},{40,8},{48,16},{56,24},{6... | collective-permute-start | bytes 884744 | tf_op jit(solution)/shard_map/ppermute | solution.py:47
  113.0 7.0 %collective-permute-start.30 = (bf16[1152,128]{1,0:T(8,128)(2,1)S(1)}, bf16[1152,128]{1,0:T(8,128)(2,1)S(1)}, u32[]{:S(2)}, u32[]{:S(2)}) collective-permute-start(bf16[1152,128]{1,0:T(8,128)(2,1)S(1)} %pad_maximum_fusion.2), channel_id=1, source_target_pairs={{0,32},{8,40},{16,48},{24,56},{32,64},{40,72},{48,80},{56,88},{64,... | collective-permute-start | bytes 884744 | tf_op jit(solution)/shard_map/ppermute | solution.py:47
  113.2 6.5 %collective-permute-start.34 = (bf16[1024,128]{1,0:T(8,128)(2,1)S(1)}, bf16[1024,128]{1,0:T(8,128)(2,1)S(1)}, u32[]{:S(2)}, u32[]{:S(2)}) collective-permute-start(bf16[1024,128]{1,0:T(8,128)(2,1)S(1)} %fusion), channel_id=1, source_target_pairs={{0,224},{8,232},{16,240},{24,248},{32,0},{40,8},{48,16},{56,24},{6... | collective-permute-start | bytes 786440 | tf_op jit(solution)/shard_map/ppermute | solution.py:47
  120.1 6.1 %collective-permute-start.35 = (bf16[640,128]{1,0:T(8,128)(2,1)S(1)}, bf16[640,128]{1,0:T(8,128)(2,1)S(1)}, u32[]{:S(2)}, u32[]{:S(2)}) collective-permute-start(bf16[640,128]{1,0:T(8,128)(2,1)S(1)} %get-tuple-element.57.sent), channel_id=1, source_target_pairs={{0,16},{8,24},{16,0},{24,8},{32,48},{40,56},{48,32},{56,40},{64,80... | collective-permute-start | bytes 491528 | tf_op jit(solution)/shard_map/ppermute | solution.py:33
  126.3 8.3 %collective-permute-start.38 = (bf16[768,128]{1,0:T(8,128)(2,1)S(1)}, bf16[768,128]{1,0:T(8,128)(2,1)S(1)}, u32[]{:S(2)}, u32[]{:S(2)}) collective-permute-start(bf16[768,128]{1,0:T(8,128)(2,1)S(1)} %get-tuple-element.59), channel_id=1, source_target_pairs={{0,8},{8,0},{16,24},{24,16},{32,40},{40,32},{48,56},{56,48},{64,72... | collective-permute-start | bytes 589832 | tf_op jit(solution)/shard_map/ppermute | solution.py:33
  (13 other events, 113.6 us)
